TPU v7x, 32 devices: a whole 2x2x4 slice. The times are simulated.
32 devices in a mesh: seq: 8 (over y, x, core), tp: 4 (over z).
Axes of the slice: x: 2, y: 2, z: 4, core: 2. Of those that a mesh axis runs over, the one named last changes fastest.
Arguments:
- tokens: bfloat16 [4096, 4096], P(('seq', 'tp')), may hold values from -6 to 6
- norm_gain: float32 [4096], replicated, may hold values from 0.1 to 1.9
- in_weight: bfloat16 [3, 4096, 4096], P(None, 'seq', 'tp'), may hold values from -0.09375 to 0.09375
- filters: float32 [7, 256], P(None, 'tp'), may hold values from -4 to 4
- out_weight: bfloat16 [4096, 4096], P('tp', 'seq'), may hold values from -0.09375 to 0.09375
- keep_mask: int32 [4096, 4096], P(('seq', 'tp')), may hold values 0 or 1
Outputs:
- block_out: bfloat16 [4096, 4096], P(('seq', 'tp'))
All inputs are finite; a program needn't handle non-finite values. No bound on the sum of `keep_mask` on one device may be relied on, other than what follows from the above.
Results may differ from a plain program's by a relative error of at most 0.013.
Values may be sent and summed in bfloat16 or wider, within the bound.
No kernel may reach another device: no remote copies, remote signals or barrier semaphores. Data moves between devices by JAX's collectives and lax.ppermute only.
A program may use at most 128 MiB of HBM per device.

v0:
```python
import jax
import jax.numpy as jnp
from jax import lax
from jax.sharding import PartitionSpec as P


def shifted(block, axis, distance):
    devices = range(lax.axis_size(axis))
    route = [(i - distance, i) for i in devices if i - distance in devices]
    return lax.ppermute(block, axis, route)


def on_device(tokens, norm_gain, in_weight, filters, out_weight, keep_mask):
    widened = tokens.astype(jnp.float32)
    mean_sq = jnp.mean(widened * widened, axis=1, keepdims=True)
    normed = (widened * lax.rsqrt(mean_sq + 1e-06) * norm_gain).astype(jnp.bfloat16)
    gathered = lax.all_gather(normed, "tp", axis=0, tiled=True)
    length = gathered.shape[0]
    channels = in_weight.shape[2]
    stacked = jnp.einsum(
        "ld,pdc->plc",
        gathered,
        lax.all_gather(in_weight, "seq", axis=1, tiled=True),
        preferred_element_type=jnp.float32,
    )
    projected = [stacked[index].astype(jnp.bfloat16) for index in range(3)]
    query, key_rows, value_rows = projected
    reach = filters.shape[0] - 1
    tails = jnp.stack([key_rows[length - reach :], value_rows[length - reach :]])
    rim_rows = shifted(tails, "seq", 1)
    keys_ext = jnp.concatenate([rim_rows[0], key_rows], axis=0)
    values_ext = jnp.concatenate([rim_rows[1], value_rows], axis=0)
    product = keys_ext.astype(jnp.float32) * values_ext.astype(jnp.float32)
    tap_weights = jnp.repeat(filters, channels // filters.shape[1], axis=1)
    filtered = jnp.zeros((length, channels), jnp.float32)
    for offset in range(reach + 1):
        filtered = (
            filtered + tap_weights[offset] * product[reach - offset : reach - offset + length]
        )
    gated = (query.astype(jnp.float32) * filtered).astype(jnp.bfloat16)
    terms = jnp.dot(
        gated,
        lax.all_gather(out_weight, "seq", axis=1, tiled=True),
        preferred_element_type=jnp.float32,
    )
    mixed = lax.psum_scatter(
        terms.astype(jnp.bfloat16), "tp", scatter_dimension=0, tiled=True
    ).astype(jnp.float32)
    return (widened + keep_mask.astype(jnp.float32) * mixed * (1.0 / 0.9)).astype(jnp.bfloat16)


def solution(mesh):
    in_specs = (
        P(("seq", "tp"), None),
        P(),
        P(None, "seq", "tp"),
        P(None, "tp"),
        P("tp", "seq"),
        P(("seq", "tp"), None),
    )
    out_specs = P(("seq", "tp"), None)
    return jax.shard_map(
        on_device, mesh=mesh, in_specs=in_specs, out_specs=out_specs, check_vma=False
    )
```

profile of v0, /device:TPU:0, one launch (start us, length us, event | category | flops | bytes accessed | tf_op | source)
XLA Modules:
  0.0 375.6 jit_solution(9495244907731836936)
XLA Ops:
  6.5 0.0 all-gather.4.cloned.1.call-start
  6.5 1.5 fusion.4
  8.1 2.5 fusion.6
  10.6 0.0 all-gather.4.cloned.1.call-update
  10.6 0.0 copy-start.3
  10.6 0.0 all-gather.6.cloned.1.call-start
  10.7 0.7 all-gather.6.cloned.1.call-update
  11.4 0.0 all-gather.8.cloned.1.call-start
  11.4 0.7 all-gather.8.cloned.1.call-update
  12.1 0.0 reduce-scatter.2.cloned.1.call-start
  12.2 0.0 copy-done.3
  12.2 0.1 broadcast_in_dim.31
  12.3 0.1 broadcast_in_dim.32
  12.3 0.1 broadcast_in_dim.33
  12.4 0.1 broadcast_in_dim.34
  12.5 0.1 broadcast_in_dim.35
  12.6 0.1 broadcast_in_dim.36
  12.6 0.1 broadcast_in_dim.37
  12.7 0.1 broadcast_in_dim.38
  12.8 0.1 broadcast_in_dim.39
  12.9 0.1 broadcast_in_dim.40
  13.0 0.1 broadcast_in_dim.41
  13.0 0.1 broadcast_in_dim.42
  13.1 0.1 broadcast_in_dim.43
  13.2 0.1 broadcast_in_dim.44
  13.3 81.0 %all-gather.4.cloned.1.call-done = bf16[512,4096]{1,0:T(8,128)(2,1)} async-done(((bf16[128,4096]{1,0:T(8,128)(2,1)}), bf16[512,4096]{1,0:T(8,128)(2,1)}) %all-gather.4.cloned.1.call-update) | async-done | bytes 4194320 | tf_op jit(solution)/shard_map/all_gather | solution.py:17
  94.2 125.8 %all-gather.6.cloned.1.call-done = bf16[3,4096,1024]{2,1,0:T(8,128)(2,1)} async-done(((bf16[3,512,1024]{2,1,0:T(8,128)(2,1)}), bf16[3,4096,1024]{2,1,0:T(8,128)(2,1)}) %all-gather.6.cloned.1.call-update) | async-done | bytes 25165840 | tf_op jit(solution)/shard_map/all_gather | solution.py:23
  220.0 18.1 %convert_bitcast_fusion = bf16[3,512,1024]{2,1,0:T(8,128)(2,1)S(1)} fusion(bf16[3,4096,1024]{2,1,0:T(8,128)(2,1)} %all-gather.6.cloned.1.call-done, bf16[512,4096]{1,0:T(8,128)(2,1)} %all-gather.4.cloned.1.call-done), kind=kOutput, calls=%fused_computation.3 | convolution fusion | flops 12886474752 | bytes 32505856 | tf_op jit(solution)/shard_map/ld,pdc->plc/dot_general | solution.py:20
  238.1 0.0 copy-start.2
  238.2 2.2 collective-permute-start
  240.3 0.2 slice_bitcast_fusion
  240.5 0.0 copy-done.2
  240.5 0.7 collective-permute-done
  241.2 0.5 convert_multiply_fusion.2
  241.7 36.2 %all-gather.8.cloned.1.call-done = bf16[1024,4096]{1,0:T(8,128)(2,1)} async-done(((bf16[1024,512]{1,0:T(8,128)(2,1)}), bf16[1024,4096]{1,0:T(8,128)(2,1)}) %all-gather.8.cloned.1.call-update) | async-done | bytes 8388624 | tf_op jit(solution)/shard_map/all_gather | solution.py:43
  277.9 11.6 %convolution_convert_fusion = bf16[512,4096]{1,0:T(8,128)(2,1)} fusion(bf16[1024,4096]{1,0:T(8,128)(2,1)} %all-gather.8.cloned.1.call-done, f32[518,1024]{1,0:T(8,128)S(1)} %convert_multiply_fusion.2, bf16[3,512,1024]{2,1,0:T(8,128)(2,1)} %copy-done.2, f32[1024]{0:T(1024)S(1)} %broadcast_in_dim.44, f32[1024]{0:T(1024)S(1)} %broadcast_in_dim.42, ...), kind=kOutput, calls=%fused_computation | convolution fusion | flops 4305453056 | bytes 28340224 | tf_op jit(solution)/shard_map/dot_general | solution.py:41
  289.5 0.0 copy-start
  289.5 0.0 copy-start.1
  289.5 0.0 reduce-scatter.2.cloned.1.call-update
  289.5 76.9 %reduce-scatter.2.cloned.1.call-done = bf16[128,4096]{1,0:T(8,128)(2,1)} async-done(((bf16[512,4096]{1,0:T(8,128)(2,1)}), bf16[128,4096]{1,0:T(8,128)(2,1)}) %reduce-scatter.2.cloned.1.call-update) | async-done | bytes 1048592 | tf_op jit(solution)/shard_map/reduce_scatter | solution.py:46
  366.4 0.0 copy-done
  366.4 0.0 copy-done.1
  366.4 2.6 fusion.7
  (4 shorter events, 0.0 us)
Async XLA Ops:
  6.5 87.7 %all-gather.4.cloned.1.call-start = ((), (), s32[]{:S(2)}) async-start(), calls=%async_computation.1 | async-start | bytes 5242880 | tf_op jit(solution)/shard_map/all_gather | solution.py:17
  10.6 1.5 copy-start.3
  10.6 209.4 %all-gather.6.cloned.1.call-start = ((), (), s32[]{:S(2)}) async-start(), calls=%async_computation.2 | async-start | bytes 28311552 | tf_op jit(solution)/shard_map/all_gather | solution.py:23
  11.4 266.5 %all-gather.8.cloned.1.call-start = ((), (), s32[]{:S(2)}) async-start(), calls=%async_computation.3 | async-start | bytes 9437184 | tf_op jit(solution)/shard_map/all_gather | solution.py:43
  12.1 354.3 %reduce-scatter.2.cloned.1.call-start = ((), (), s32[]{:S(2)}) async-start(), calls=%async_computation.4 | async-start | bytes 5242880 | tf_op jit(solution)/shard_map/reduce_scatter | solution.py:46
  238.1 2.4 copy-start.2
  238.2 3.0 collective-permute-start
  289.5 77.0 %copy-start = (bf16[128,4096]{1,0:T(8,128)(2,1)S(1)}, bf16[128,4096]{1,0:T(8,128)(2,1)}, u32[]{:S(2)}) copy-start(bf16[128,4096]{1,0:T(8,128)(2,1)} %param.6) | copy-start | bytes 3145732
  289.5 77.0 %copy-start.1 = (s32[128,4096]{1,0:T(8,128)S(1)}, s32[128,4096]{1,0:T(8,128)}, u32[]{:S(2)}) copy-start(s32[128,4096]{1,0:T(8,128)} %param.11) | copy-start | bytes 6291460
Sparse Core Ops, SparseCore 0:
  10.7 83.4 all-gather.3
  96.1 123.8 all-gather.5
  221.9 55.9 all-gather.7
  289.6 76.7 reduce-scatter.1
where the time goes:
time: 376 us
  waiting for transfers between devices  322 us (86%)
  matrix products  29.7 us (8%)
  between operations  13.2 us (4%)
  other arithmetic  7.2 us (2%)
    all_gather x1, waiting for transfers between devices, on_device(): lax.all_gather(in_weight, 'seq', axis=1, tiled=True)  126 us
    all_gather x1, waiting for transfers between devices, on_device(): gathered = lax.all_gather(normed, 'tp', axis=0, tiled=True)  81 us
    reduce_scatter x1, waiting for transfers between devices, on_device(): lax.psum_scatter(terms.astype(jnp.bfloat16), 'tp', scatter_dimension=0, t...  76.9 us
    all_gather x1, waiting for transfers between devices, on_device(): lax.all_gather(out_weight, 'seq', axis=1, tiled=True)  36.2 us
    dot_general x1, matrix products, on_device(): jnp.einsum('ld,pdc->plc', gathered, lax.all_gather(in_weight, 'seq', axis...  18.1 us
    dot_general x1, matrix products, on_device(): jnp.dot(gated, lax.all_gather(out_weight, 'seq', axis=1, tiled=True), pre...  11.6 us
  transfers between devices with their start and end apart: 5, of which 5 were waited for; matrix products, arithmetic and copies ran while one was open for 5% of the time, Pallas kernels for 0%

commit v1 on v0

v1 whole, which is shorter than its diff:
```python
import math

import jax
import jax.numpy as jnp
from jax import lax
from jax.sharding import PartitionSpec as P

F32 = jnp.float32
BF16 = jnp.bfloat16


def grid_of(chips):
    ny = max(d for d in range(1, math.isqrt(chips) + 1) if chips % d == 0)
    return ny, chips // ny


def on_device(tokens, norm_gain, in_weight, filters, out_weight, keep_mask):
    n_seq, n_tp = lax.axis_size("seq"), lax.axis_size("tp")
    chips = n_seq // 2
    ny, nx = grid_of(chips)
    seq = lax.axis_index("seq")
    core, here = seq % 2, seq // 2
    my_y, my_x = here // nx, here % nx
    rows, model = tokens.shape
    length = rows * n_tp
    deep, channels = in_weight.shape[1:]
    half = channels // 2
    wide = out_weight.shape[1]

    def place(y, x, c):
        return ((y % ny) * nx + x % nx) * 2 + c

    def from_chip(block, dy, dx):
        route = [
            (place(y + dy, x + dx, c), place(y, x, c))
            for y in range(ny)
            for x in range(nx)
            for c in range(2)
        ]
        return lax.ppermute(block, "seq", route)

    def from_partner(block):
        return lax.ppermute(block, "seq", [(s, s ^ 1) for s in range(n_seq)])

    def by_core(mine, other, axis):
        return jnp.where(
            core == 0,
            jnp.concatenate([mine, other], axis=axis),
            jnp.concatenate([other, mine], axis=axis),
        )

    def spread(block):
        cut = block.shape[0] // 2
        along_x = [block] + [from_chip(block, 0, dx) for dx in range(1, nx)]
        along_y = [block] + [from_chip(block, dy, 0) for dy in range(1, ny)]
        found = {(0, dx): [along_x[dx]] for dx in range(nx)}
        found.update({(dy, 0): [along_y[dy]] for dy in range(1, ny)})
        for dy in range(1, ny):
            for dx in range(1, nx):
                found[dy, dx] = [
                    from_chip(along_x[dx][:cut], dy, 0),
                    from_chip(along_y[dy][cut:], 0, dx),
                ]
        return found

    def turned(array, sign):
        parts = array.reshape(array.shape[0], ny, nx, -1)
        parts = jnp.roll(parts, (sign * my_y, sign * my_x), axis=(1, 2))
        return parts.reshape(array.shape)

    widened = tokens.astype(F32)
    mean_sq = jnp.mean(widened * widened, axis=1, keepdims=True)
    normed = (widened * lax.rsqrt(mean_sq + 1e-06) * norm_gain).astype(BF16)
    own_rows = lax.all_gather(turned(normed, -1), "tp", axis=0, tiled=True)
    other_rows = from_partner(own_rows)

    mine = lax.dynamic_slice_in_dim(in_weight, core * half, half, axis=2)
    away = lax.dynamic_slice_in_dim(in_weight, (1 - core) * half, half, axis=2)
    brought = from_partner(away)
    projected = {}
    for index in (1, 2, 0):
        chip_block = by_core(mine[index], brought[index], 0)
        found = spread(chip_block)
        totals = [jnp.zeros((length, half), F32)] * 2
        for (dy, dx), pieces in found.items():
            at = (dy * nx + dx) * 2 * deep
            for piece in pieces:
                depth = piece.shape[0]
                totals = [
                    total
                    + jnp.dot(
                        block[:, at : at + depth], piece, preferred_element_type=F32
                    )
                    for total, block in zip(totals, (own_rows, other_rows))
                ]
                at += depth
        projected[index] = by_core(totals[0].astype(BF16), totals[1].astype(BF16), 0)
    query, key, value = projected[0], projected[1], projected[2]

    reach = filters.shape[0] - 1
    groups = filters.shape[1] // 2
    product = key.astype(F32) * value.astype(F32)
    tail = product[2 * length - reach :]
    rim = lax.ppermute(
        tail, "seq", [(2 * i + c, 2 * i + 2 + c) for i in range(chips - 1) for c in range(2)]
    )
    product = jnp.concatenate([rim, product], axis=0)
    taps = jnp.repeat(
        lax.dynamic_slice_in_dim(filters, core * groups, groups, axis=1), half // groups, axis=1
    )
    filtered = jnp.zeros((2 * length, half), F32)
    for offset in range(reach + 1):
        filtered = filtered + taps[offset] * product[reach - offset : reach - offset + 2 * length]
    gated = (query.astype(F32) * filtered).astype(BF16)

    stays = lax.dynamic_slice_in_dim(gated, core * length, length, axis=0)
    leaves = lax.dynamic_slice_in_dim(gated, (1 - core) * length, length, axis=0)
    gated = by_core(stays, from_partner(leaves), 1)

    out_found = spread(out_weight)
    position = lax.axis_index("tp")
    up = [(i, i + 1) for i in range(n_tp - 1)]
    down = [(i + 1, i) for i in range(n_tp - 1)]

    def summed(terms):
        terms = terms.reshape(n_tp, rows, -1)

        def rows_of(where):
            where = jnp.clip(where, 0, n_tp - 1)
            return lax.dynamic_index_in_dim(terms, where, 0, keepdims=False)

        rising = falling = None
        for step in range(n_tp - 1):
            ahead = n_tp - 1 - step
            send_up, send_down = rows_of(position + ahead), rows_of(position - ahead)
            if step:
                send_up = (send_up.astype(F32) + rising.astype(F32)).astype(BF16)
                send_down = (send_down.astype(F32) + falling.astype(F32)).astype(BF16)
            rising = lax.ppermute(send_up, "tp", up)
            falling = lax.ppermute(send_down, "tp", down)
        total = rows_of(position).astype(F32)
        return total + rising.astype(F32) + falling.astype(F32)

    result = jnp.zeros((rows, model), BF16)
    for (dy, dx), pieces in out_found.items():
        sides = []
        for side in (pieces, [from_partner(piece) for piece in pieces]):
            total, at = 0.0, 0
            for piece in side:
                depth = piece.shape[0]
                total = total + jnp.dot(
                    gated[:, at : at + depth], piece, preferred_element_type=F32
                )
                at += depth
            sides.append(total.astype(BF16))
        mixed = summed(by_core(sides[0], sides[1], 1))
        chip = ((my_y + dy) % ny) * nx + (my_x + dx) % nx
        at = chip * 2 * wide
        kept = lax.dynamic_slice_in_dim(keep_mask, at, 2 * wide, axis=1).astype(F32)
        base = lax.dynamic_slice_in_dim(tokens, at, 2 * wide, axis=1).astype(F32)
        part = (base + kept * mixed * (1.0 / 0.9)).astype(BF16)
        result = lax.dynamic_update_slice_in_dim(result, part, at, axis=1)
    return result


def solution(mesh):
    in_specs = (
        P(("seq", "tp"), None),
        P(),
        P(None, "seq", "tp"),
        P(None, "tp"),
        P("tp", "seq"),
        P(("seq", "tp"), None),
    )
    out_specs = P(("seq", "tp"), None)
    return jax.shard_map(
        on_device, mesh=mesh, in_specs=in_specs, out_specs=out_specs, check_vma=False
    )
```

time: 376 us -> 321 us (0.85)
  waiting for transfers between devices: 322 us -> 119 us
  starting transfers between devices: 2.29 us -> 93.9 us
  local copies, waits for them, and re-layouts: 1.29 us -> 23.9 us
  matrix products: 29.7 us -> 49.3 us
  other arithmetic: 7.2 us -> 18.2 us
    all_gather x3 -> x1, waiting for transfers between devices: 243 us -> 0.01 us  [on_device(): own_rows = lax.all_gather(turned(normed, -1), 'tp', axis=0, tiled=True)]
    ppermute x1 -> x49, waiting for transfers between devices: 0.65 us -> 119 us  [the longest x16 95.8 us: from_chip(): return lax.ppermute(block, 'seq', route)]
    ppermute x1 -> x49, starting transfers between devices: 2.17 us -> 93.9 us  [the longest x12 50.6 us: summed(): rising = lax.ppermute(send_up, 'tp', up)]
    reduce_scatter x1 -> x0, waiting for transfers between devices: 76.9 us -> none  [on_device(): lax.psum_scatter(terms.astype(jnp.bfloat16), 'tp', scatter_dimension=0, t...]
    dot_general x2 -> x40, matrix products: 29.7 us -> 49.3 us  [the longest x30 37.6 us: on_device(): jnp.dot(block[:, at:at + depth], piece, preferred_element_type=F32)]
    slice x1 -> x10, local copies, waits for them, and re-layouts: 0.01 us -> 14 us  [the longest x4 7.48 us: spread(): along_x[dx][:cut]]
    concatenate x0 -> x2, other arithmetic: none -> 6.48 us  [turned(): parts = jnp.roll(parts, (sign * my_y, sign * my_x), axis=(1, 2))]
  transfers between devices with their start and end apart: 5 -> 50, of which waited for: 5 -> 19; matrix products, arithmetic and copies ran while one was open for 5% -> 24% of each run, Pallas kernels for 0% -> 0%
where the time goes in v1:
time: 321 us; the launch traced here: 319 us
  waiting for transfers between devices  119 us (37%)
  starting transfers between devices  93.9 us (29%)
  matrix products  49.3 us (15%)
  local copies, waits for them, and re-layouts  23.9 us (7%)
  other arithmetic  18.2 us (6%)
  between operations  14.4 us (4%)
    ppermute x16, waiting for transfers between devices, from_chip(): return lax.ppermute(block, 'seq', route)  95.8 us
    ppermute x12, starting transfers between devices, summed(): rising = lax.ppermute(send_up, 'tp', up)  50.6 us
    dot_general x30, matrix products, on_device(): jnp.dot(block[:, at:at + depth], piece, preferred_element_type=F32)  37.6 us
    ppermute x16, starting transfers between devices, from_chip(): return lax.ppermute(block, 'seq', route)  23.3 us
    ppermute x12, starting transfers between devices, summed(): falling = lax.ppermute(send_down, 'tp', down)  15.8 us
    ppermute x12, waiting for transfers between devices, summed(): falling = lax.ppermute(send_down, 'tp', down)  15.2 us
    dot_general x10, matrix products, on_device(): jnp.dot(gated[:, at:at + depth], piece, preferred_element_type=F32)  11.8 us
    slice x4, local copies, waits for them, and re-layouts, spread(): along_x[dx][:cut]  7.48 us
  transfers between devices with their start and end apart: 50, of which 19 were waited for; matrix products, arithmetic and copies ran while one was open for 24% of the time, Pallas kernels for 0%

profile of v1, /device:TPU:0, one launch (start us, length us, event | category | flops | bytes accessed | tf_op | source)
XLA Modules:
  0.0 318.5 jit_solution(753251932309509210)
XLA Ops:
  6.5 1.5 fusion
  8.1 1.6 fusion.2
  10.5 2.6 fusion.45
  13.1 3.8 %fusion.46 = bf16[128,2,2,1024]{3,2,1,0:T(2,128)(2,1)S(1)} fusion(s32[]{:T(128)S(6)} %select_n.195, bf16[128,2,2,1024]{3,2,1,0:T(2,128)(2,1)S(1)} %fusion.45), kind=kLoop, calls=%fused_computation.79 | loop fusion | flops 2097152 | bytes 2097156 | tf_op jit(solution)/shard_map/jit(_roll_dynamic)/concatenate | solution.py:68
  17.0 1.6 reshape.105
  18.6 2.9 constant_dynamic-slice_fusion.3
  21.9 2.5 collective-permute-start.31
  28.1 2.1 collective-permute-start.2
  32.7 16.0 %collective-permute-done.31 = bf16[1024,512]{1,0:T(8,128)(2,1)} collective-permute-done((bf16[1024,512]{1,0:T(8,128)(2,1)}, bf16[1024,512]{1,0:T(8,128)(2,1)}, u32[]{:S(2)}, u32[]{:S(2)}) %collective-permute-start.31) | collective-permute-done | bytes 1048608 | tf_op jit(solution)/shard_map/ppermute | solution.py:40
  48.8 1.9 collective-permute-start.10
  51.2 1.6 collective-permute-start.7
  52.8 18.4 %collective-permute-done.2 = bf16[1024,512]{1,0:T(8,128)(2,1)S(1)} collective-permute-done((bf16[1024,512]{1,0:T(8,128)(2,1)S(1)}, bf16[1024,512]{1,0:T(8,128)(2,1)S(1)}, u32[]{:S(2)}, u32[]{:S(2)}) %collective-permute-start.2) | collective-permute-done | bytes 1048608 | tf_op jit(solution)/shard_map/ppermute | solution.py:40
  71.1 1.9 collective-permute-start.6
  75.7 1.9 slice.222
  77.5 16.2 %collective-permute-done.11 = bf16[1024,512]{1,0:T(8,128)(2,1)} collective-permute-done((bf16[1024,512]{1,0:T(8,128)(2,1)S(1)}, bf16[1024,512]{1,0:T(8,128)(2,1)}, u32[]{:S(2)}, u32[]{:S(2)}) %collective-permute-start.11) | collective-permute-done | bytes 1048608 | tf_op jit(solution)/shard_map/ppermute | solution.py:40
  93.7 1.9 collective-permute-start.3
  96.8 1.9 slice.250
  98.7 1.9 slice.248
  100.6 1.9 slice.235
  103.9 1.9 slice.234
  105.8 10.4 %collective-permute-done.7 = bf16[1024,512]{1,0:T(8,128)(2,1)} collective-permute-done((bf16[1024,512]{1,0:T(8,128)(2,1)S(1)}, bf16[1024,512]{1,0:T(8,128)(2,1)}, u32[]{:S(2)}, u32[]{:S(2)}) %collective-permute-start.7) | collective-permute-done | bytes 1048608 | tf_op jit(solution)/shard_map/ppermute | solution.py:40
  116.2 1.9 collective-permute-start.39
  118.1 1.9 slice.232
  121.5 1.9 slice.231
  123.4 6.0 %collective-permute-done.4 = bf16[512,512]{1,0:T(8,128)(2,1)} collective-permute-done((bf16[512,512]{1,0:T(8,128)(2,1)}, bf16[512,512]{1,0:T(8,128)(2,1)}, u32[]{:S(2)}, u32[]{:S(2)}) %collective-permute-start.4) | collective-permute-done | bytes 524320 | tf_op jit(solution)/shard_map/ppermute | solution.py:40
  129.4 1.8 fusion.132
  131.3 1.7 fusion.138
  133.0 18.2 %collective-permute-done.13 = bf16[512,512]{1,0:T(8,128)(2,1)} collective-permute-done((bf16[512,512]{1,0:T(8,128)(2,1)}, bf16[512,512]{1,0:T(8,128)(2,1)}, u32[]{:S(2)}, u32[]{:S(2)}) %collective-permute-start.13) | collective-permute-done | bytes 524320 | tf_op jit(solution)/shard_map/ppermute | solution.py:40
  152.7 1.6 fusion.128
  156.4 8.2 %collective-permute-done.9 = bf16[512,512]{1,0:T(8,128)(2,1)S(1)} collective-permute-done((bf16[512,512]{1,0:T(8,128)(2,1)}, bf16[512,512]{1,0:T(8,128)(2,1)S(1)}, u32[]{:S(2)}, u32[]{:S(2)}) %collective-permute-start.9) | collective-permute-done | bytes 524320 | tf_op jit(solution)/shard_map/ppermute | solution.py:40
  165.1 2.3 collective-permute-done.8
  171.2 1.9 convolution_add_fusion.4
  173.1 2.0 convolution_add_fusion.7
  175.9 1.9 fusion.40
  177.9 1.9 fusion.41
  182.8 1.9 fusion.47
  184.8 1.9 fusion.53
  186.7 1.9 fusion.55
  188.6 1.9 fusion.49
  193.9 2.4 collective-permute-start.14
  201.6 2.1 fusion.8
  209.1 2.0 collective-permute-done.42
  212.8 3.5 %collective-permute-start.43 = (bf16[128,1024]{1,0:T(8,128)(2,1)S(1)}, bf16[128,1024]{1,0:T(8,128)(2,1)S(1)}, u32[]{:S(2)}, u32[]{:S(2)}) collective-permute-start(bf16[128,1024]{1,0:T(8,128)(2,1)S(1)} %get-tuple-element.13), channel_id=1, source_target_pairs={{0,1},{1,2},{2,3},{4,5},{5,6},{6,7},{8,9},{9,10},{10,11},{12,13},{... | collective-permute-start | bytes 786440 | tf_op jit(solution)/shard_map/ppermute | solution.py:139
  217.5 1.9 convolution_convert_fusion.1
  220.6 4.6 %collective-permute-start.33 = (bf16[128,1024]{1,0:T(8,128)(2,1)S(1)}, bf16[128,1024]{1,0:T(8,128)(2,1)S(1)}, u32[]{:S(2)}, u32[]{:S(2)}) collective-permute-start(bf16[128,1024]{1,0:T(8,128)(2,1)S(1)} %get-tuple-element.17), channel_id=1, source_target_pairs={{0,1},{1,2},{2,3},{4,5},{5,6},{6,7},{8,9},{9,10},{10,11},{12,13},{... | collective-permute-start | bytes 786440 | tf_op jit(solution)/shard_map/ppermute | solution.py:139
  225.2 1.9 convolution_convert_fusion.3
  229.5 1.9 convolution_convert_fusion.5
  231.5 4.6 %collective-permute-start.25 = (bf16[128,1024]{1,0:T(8,128)(2,1)S(1)}, bf16[128,1024]{1,0:T(8,128)(2,1)S(1)}, u32[]{:S(2)}, u32[]{:S(2)}) collective-permute-start(bf16[128,1024]{1,0:T(8,128)(2,1)S(1)} %get-tuple-element.21), channel_id=1, source_target_pairs={{0,1},{1,2},{2,3},{4,5},{5,6},{6,7},{8,9},{9,10},{10,11},{12,13},{... | collective-permute-start | bytes 786440 | tf_op jit(solution)/shard_map/ppermute | solution.py:139
  238.5 4.6 %collective-permute-start.17 = (bf16[128,1024]{1,0:T(8,128)(2,1)S(1)}, bf16[128,1024]{1,0:T(8,128)(2,1)S(1)}, u32[]{:S(2)}, u32[]{:S(2)}) collective-permute-start(bf16[128,1024]{1,0:T(8,128)(2,1)S(1)} %get-tuple-element.25), channel_id=1, source_target_pairs={{0,1},{1,2},{2,3},{4,5},{5,6},{6,7},{8,9},{9,10},{10,11},{12,13},{... | collective-permute-start | bytes 786440 | tf_op jit(solution)/shard_map/ppermute | solution.py:139
  243.2 3.5 %collective-permute-start.44 = (bf16[128,1024]{1,0:T(8,128)(2,1)S(1)}, bf16[128,1024]{1,0:T(8,128)(2,1)S(1)}, u32[]{:S(2)}, u32[]{:S(2)}) collective-permute-start(bf16[128,1024]{1,0:T(8,128)(2,1)S(1)} %fusion.76), channel_id=1, source_target_pairs={{0,1},{1,2},{2,3},{4,5},{5,6},{6,7},{8,9},{9,10},{10,11},{12,13},{... | collective-permute-start | bytes 786440 | tf_op jit(solution)/shard_map/ppermute | solution.py:139
  246.7 2.9 collective-permute-done.17
  249.6 4.4 %collective-permute-start.34 = (bf16[128,1024]{1,0:T(8,128)(2,1)S(1)}, bf16[128,1024]{1,0:T(8,128)(2,1)S(1)}, u32[]{:S(2)}, u32[]{:S(2)}) collective-permute-start(bf16[128,1024]{1,0:T(8,128)(2,1)S(1)} %fusion.85), channel_id=1, source_target_pairs={{0,1},{1,2},{2,3},{4,5},{5,6},{6,7},{8,9},{9,10},{10,11},{12,13},{... | collective-permute-start | bytes 786440 | tf_op jit(solution)/shard_map/ppermute | solution.py:139
  254.1 1.6 collective-permute-start.20
  255.7 4.6 %collective-permute-start.18 = (bf16[128,1024]{1,0:T(8,128)(2,1)S(1)}, bf16[128,1024]{1,0:T(8,128)(2,1)S(1)}, u32[]{:S(2)}, u32[]{:S(2)}) collective-permute-start(bf16[128,1024]{1,0:T(8,128)(2,1)S(1)} %fusion.103), channel_id=1, source_target_pairs={{0,1},{1,2},{2,3},{4,5},{5,6},{6,7},{8,9},{9,10},{10,11},{12,13},{... | collective-permute-start | bytes 786440 | tf_op jit(solution)/shard_map/ppermute | solution.py:139
  260.5 3.3 %collective-permute-start.26 = (bf16[128,1024]{1,0:T(8,128)(2,1)S(1)}, bf16[128,1024]{1,0:T(8,128)(2,1)S(1)}, u32[]{:S(2)}, u32[]{:S(2)}) collective-permute-start(bf16[128,1024]{1,0:T(8,128)(2,1)S(1)} %fusion.94), channel_id=1, source_target_pairs={{0,1},{1,2},{2,3},{4,5},{5,6},{6,7},{8,9},{9,10},{10,11},{12,13},{... | collective-permute-start | bytes 786440 | tf_op jit(solution)/shard_map/ppermute | solution.py:139
  265.4 4.6 %collective-permute-start.45 = (bf16[128,1024]{1,0:T(8,128)(2,1)S(1)}, bf16[128,1024]{1,0:T(8,128)(2,1)S(1)}, u32[]{:S(2)}, u32[]{:S(2)}) collective-permute-start(bf16[128,1024]{1,0:T(8,128)(2,1)S(1)} %get-tuple-element.11), channel_id=1, source_target_pairs={{0,1},{1,2},{2,3},{4,5},{5,6},{6,7},{8,9},{9,10},{10,11},{12,13},{... | collective-permute-start | bytes 786440 | tf_op jit(solution)/shard_map/ppermute | solution.py:139
  274.9 5.5 %collective-permute-start.27 = (bf16[128,1024]{1,0:T(8,128)(2,1)S(1)}, bf16[128,1024]{1,0:T(8,128)(2,1)S(1)}, u32[]{:S(2)}, u32[]{:S(2)}) collective-permute-start(bf16[128,1024]{1,0:T(8,128)(2,1)S(1)} %get-tuple-element.19), channel_id=1, source_target_pairs={{0,1},{1,2},{2,3},{4,5},{5,6},{6,7},{8,9},{9,10},{10,11},{12,13},{... | collective-permute-start | bytes 786440 | tf_op jit(solution)/shard_map/ppermute | solution.py:139
  280.5 4.6 %collective-permute-done.21 = bf16[128,1024]{1,0:T(8,128)(2,1)S(1)} collective-permute-done((bf16[128,1024]{1,0:T(8,128)(2,1)S(1)}, bf16[128,1024]{1,0:T(8,128)(2,1)S(1)}, u32[]{:S(2)}, u32[]{:S(2)}) %collective-permute-start.21) | collective-permute-done | bytes 262176 | tf_op jit(solution)/shard_map/ppermute | solution.py:140
  285.1 3.3 %collective-permute-start.19 = (bf16[128,1024]{1,0:T(8,128)(2,1)S(1)}, bf16[128,1024]{1,0:T(8,128)(2,1)S(1)}, u32[]{:S(2)}, u32[]{:S(2)}) collective-permute-start(bf16[128,1024]{1,0:T(8,128)(2,1)S(1)} %get-tuple-element.23), channel_id=1, source_target_pairs={{0,1},{1,2},{2,3},{4,5},{5,6},{6,7},{8,9},{9,10},{10,11},{12,13},{... | collective-permute-start | bytes 786440 | tf_op jit(solution)/shard_map/ppermute | solution.py:139
  291.2 1.8 collective-permute-done.19
  293.0 4.4 %collective-permute-start.35 = (bf16[128,1024]{1,0:T(8,128)(2,1)S(1)}, bf16[128,1024]{1,0:T(8,128)(2,1)S(1)}, u32[]{:S(2)}, u32[]{:S(2)}) collective-permute-start(bf16[128,1024]{1,0:T(8,128)(2,1)S(1)} %get-tuple-element.15), channel_id=1, source_target_pairs={{0,1},{1,2},{2,3},{4,5},{5,6},{6,7},{8,9},{9,10},{10,11},{12,13},{... | collective-permute-start | bytes 786440 | tf_op jit(solution)/shard_map/ppermute | solution.py:139
  300.8 2.7 collective-permute-done.30
  303.7 4.2 %collective-permute-done.38 = bf16[128,1024]{1,0:T(8,128)(2,1)S(1)} collective-permute-done((bf16[128,1024]{1,0:T(8,128)(2,1)S(1)}, bf16[128,1024]{1,0:T(8,128)(2,1)S(1)}, u32[]{:S(2)}, u32[]{:S(2)}) %collective-permute-start.38) | collective-permute-done | bytes 262176 | tf_op jit(solution)/shard_map/ppermute | solution.py:140
  308.2 2.6 collective-permute-done.48
  (168 shorter events, 63.3 us)
Async XLA Ops:
  6.5 89.1 %copy-start = (f32[7,64]{1,0:T(8,128)S(1)}, f32[7,64]{1,0:T(8,128)}, u32[]{:S(2)}) copy-start(f32[7,64]{1,0:T(8,128)} %param.9) | copy-start | bytes 5380
  6.5 122.9 %all-gather.2.cloned.1.call-start = ((), (), s32[]{:S(2)}) async-start(), calls=%async_computation | async-start | bytes 5242880 | tf_op jit(solution)/shard_map/all_gather | solution.py:74
  18.6 7.4 %copy-start.4 = (bf16[3,512,1024]{2,1,0:T(8,128)(2,1)S(1)}, bf16[3,512,1024]{2,1,0:T(8,128)(2,1)}, u32[]{:S(2)}) copy-start(bf16[3,512,1024]{2,1,0:T(8,128)(2,1)} %param.8) | copy-start | bytes 9437188
  21.5 4.6 %collective-permute-start = (bf16[3,512,512]{2,1,0:T(8,128)(2,1)}, bf16[3,512,512]{2,1,0:T(8,128)(2,1)}, u32[]{:S(2)}, u32[]{:S(2)}) collective-permute-start(bf16[3,512,512]{2,1,0:T(8,128)(2,1)} %constant_dynamic-slice_fusion.3), channel_id=1, source_target_pairs={{0,4},{4,0},{8,12},{12,8},{16,20},{20,16},{24,28},{28,24},{1,5},{5... | collective-permute-start | bytes 4718600 | tf_op jit(solution)/shard_map/ppermute | solution.py:43
  21.9 26.8 %collective-permute-start.31 = (bf16[1024,512]{1,0:T(8,128)(2,1)}, bf16[1024,512]{1,0:T(8,128)(2,1)}, u32[]{:S(2)}, u32[]{:S(2)}) collective-permute-start(bf16[1024,512]{1,0:T(8,128)(2,1)} %param.10), channel_id=1, source_target_pairs={{16,0},{20,4},{24,8},{28,12},{0,16},{4,20},{8,24},{12,28},{17,1},{... | collective-permute-start | bytes 3145736 | tf_op jit(solution)/shard_map/ppermute | solution.py:40
  24.5 26.7 %collective-permute-start.23 = (bf16[1024,512]{1,0:T(8,128)(2,1)}, bf16[1024,512]{1,0:T(8,128)(2,1)}, u32[]{:S(2)}, u32[]{:S(2)}) collective-permute-start(bf16[1024,512]{1,0:T(8,128)(2,1)} %param.10), channel_id=1, source_target_pairs={{8,0},{12,4},{0,8},{4,12},{24,16},{28,20},{16,24},{20,28},{9,1},{1... | collective-permute-start | bytes 3145736 | tf_op jit(solution)/shard_map/ppermute | solution.py:40
  28.1 43.1 %collective-permute-start.2 = (bf16[1024,512]{1,0:T(8,128)(2,1)S(1)}, bf16[1024,512]{1,0:T(8,128)(2,1)S(1)}, u32[]{:S(2)}, u32[]{:S(2)}) collective-permute-start(bf16[1024,512]{1,0:T(8,128)(2,1)S(1)} %maximum_select_fusion), channel_id=1, source_target_pairs={{16,0},{20,4},{24,8},{28,12},{0,16},{4,20},{8,24},{12,28},{17,1},{... | collective-permute-start | bytes 3145736 | tf_op jit(solution)/shard_map/ppermute | solution.py:40
  30.2 43.7 %collective-permute-start.1 = (bf16[1024,512]{1,0:T(8,128)(2,1)S(1)}, bf16[1024,512]{1,0:T(8,128)(2,1)S(1)}, u32[]{:S(2)}, u32[]{:S(2)}) collective-permute-start(bf16[1024,512]{1,0:T(8,128)(2,1)S(1)} %maximum_select_fusion), channel_id=1, source_target_pairs={{8,0},{12,4},{0,8},{4,12},{24,16},{28,20},{16,24},{20,28},{9,1},{1... | collective-permute-start | bytes 3145736 | tf_op jit(solution)/shard_map/ppermute | solution.py:40
  32.2 61.5 %collective-permute-start.11 = (bf16[1024,512]{1,0:T(8,128)(2,1)S(1)}, bf16[1024,512]{1,0:T(8,128)(2,1)}, u32[]{:S(2)}, u32[]{:S(2)}) collective-permute-start(bf16[1024,512]{1,0:T(8,128)(2,1)S(1)} %maximum_select_fusion.4), channel_id=1, source_target_pairs={{16,0},{20,4},{24,8},{28,12},{0,16},{4,20},{8,24},{12,28},{17,1},{... | collective-permute-start | bytes 3145736 | tf_op jit(solution)/shard_map/ppermute | solution.py:40
  48.8 53.7 %collective-permute-start.10 = (bf16[1024,512]{1,0:T(8,128)(2,1)S(1)}, bf16[1024,512]{1,0:T(8,128)(2,1)}, u32[]{:S(2)}, u32[]{:S(2)}) collective-permute-start(bf16[1024,512]{1,0:T(8,128)(2,1)S(1)} %maximum_select_fusion.4), channel_id=1, source_target_pairs={{8,0},{12,4},{0,8},{4,12},{24,16},{28,20},{16,24},{20,28},{9,1},{1... | collective-permute-start | bytes 3145736 | tf_op jit(solution)/shard_map/ppermute | solution.py:40
  51.2 65.0 %collective-permute-start.7 = (bf16[1024,512]{1,0:T(8,128)(2,1)S(1)}, bf16[1024,512]{1,0:T(8,128)(2,1)}, u32[]{:S(2)}, u32[]{:S(2)}) collective-permute-start(bf16[1024,512]{1,0:T(8,128)(2,1)S(1)} %maximum_select_fusion.2), channel_id=1, source_target_pairs={{16,0},{20,4},{24,8},{28,12},{0,16},{4,20},{8,24},{12,28},{17,1},{... | collective-permute-start | bytes 3145736 | tf_op jit(solution)/shard_map/ppermute | solution.py:40
  71.1 2.8 copy-start.5
  71.1 48.9 %collective-permute-start.6 = (bf16[1024,512]{1,0:T(8,128)(2,1)S(1)}, bf16[1024,512]{1,0:T(8,128)(2,1)}, u32[]{:S(2)}, u32[]{:S(2)}) collective-permute-start(bf16[1024,512]{1,0:T(8,128)(2,1)S(1)} %maximum_select_fusion.2), channel_id=1, source_target_pairs={{8,0},{12,4},{0,8},{4,12},{24,16},{28,20},{16,24},{20,28},{9,1},{1... | collective-permute-start | bytes 3145736 | tf_op jit(solution)/shard_map/ppermute | solution.py:40
  73.9 1.0 copy-start.7
  75.0 54.5 %collective-permute-start.4 = (bf16[512,512]{1,0:T(8,128)(2,1)}, bf16[512,512]{1,0:T(8,128)(2,1)}, u32[]{:S(2)}, u32[]{:S(2)}) collective-permute-start(bf16[512,512]{1,0:T(8,128)(2,1)} %slice.224), channel_id=1, source_target_pairs={{8,0},{12,4},{0,8},{4,12},{24,16},{28,20},{16,24},{20,28},{9,1},{1... | collective-permute-start | bytes 1572872 | tf_op jit(solution)/shard_map/ppermute | solution.py:40
  93.7 37.5 %collective-permute-start.3 = (bf16[512,512]{1,0:T(8,128)(2,1)}, bf16[512,512]{1,0:T(8,128)(2,1)}, u32[]{:S(2)}, u32[]{:S(2)}) collective-permute-start(bf16[512,512]{1,0:T(8,128)(2,1)} %slice.222), channel_id=1, source_target_pairs={{16,0},{20,4},{24,8},{28,12},{0,16},{4,20},{8,24},{12,28},{17,1},{... | collective-permute-start | bytes 1572872 | tf_op jit(solution)/shard_map/ppermute | solution.py:40
  102.5 102.0 %collective-permute-start.40 = (bf16[512,512]{1,0:T(8,128)(2,1)}, bf16[512,512]{1,0:T(8,128)(2,1)}, u32[]{:S(2)}, u32[]{:S(2)}) collective-permute-start(bf16[512,512]{1,0:T(8,128)(2,1)} %slice.250), channel_id=1, source_target_pairs={{8,0},{12,4},{0,8},{4,12},{24,16},{28,20},{16,24},{20,28},{9,1},{1... | collective-permute-start | bytes 1572872 | tf_op jit(solution)/shard_map/ppermute | solution.py:40
  116.2 88.7 %collective-permute-start.39 = (bf16[512,512]{1,0:T(8,128)(2,1)}, bf16[512,512]{1,0:T(8,128)(2,1)}, u32[]{:S(2)}, u32[]{:S(2)}) collective-permute-start(bf16[512,512]{1,0:T(8,128)(2,1)} %slice.248), channel_id=1, source_target_pairs={{16,0},{20,4},{24,8},{28,12},{0,16},{4,20},{8,24},{12,28},{17,1},{... | collective-permute-start | bytes 1572872 | tf_op jit(solution)/shard_map/ppermute | solution.py:40
  120.0 31.2 %collective-permute-start.13 = (bf16[512,512]{1,0:T(8,128)(2,1)}, bf16[512,512]{1,0:T(8,128)(2,1)}, u32[]{:S(2)}, u32[]{:S(2)}) collective-permute-start(bf16[512,512]{1,0:T(8,128)(2,1)} %slice.235), channel_id=1, source_target_pairs={{8,0},{12,4},{0,8},{4,12},{24,16},{28,20},{16,24},{20,28},{9,1},{1... | collective-permute-start | bytes 1572872 | tf_op jit(solution)/shard_map/ppermute | solution.py:40
  129.4 24.9 %collective-permute-start.12 = (bf16[512,512]{1,0:T(8,128)(2,1)}, bf16[512,512]{1,0:T(8,128)(2,1)}, u32[]{:S(2)}, u32[]{:S(2)}) collective-permute-start(bf16[512,512]{1,0:T(8,128)(2,1)} %slice.234), channel_id=1, source_target_pairs={{16,0},{20,4},{24,8},{28,12},{0,16},{4,20},{8,24},{12,28},{17,1},{... | collective-permute-start | bytes 1572872 | tf_op jit(solution)/shard_map/ppermute | solution.py:40
  129.4 25.5 %copy-start.2 = (bf16[512,4096]{1,0:T(8,128)(2,1)S(1)}, bf16[512,4096]{1,0:T(8,128)(2,1)}, u32[]{:S(2)}) copy-start(bf16[512,4096]{1,0:T(8,128)(2,1)} %all-gather.2.cloned.1.call-done) | copy-start | bytes 12582916
  131.2 23.1 %copy-start.11 = (bf16[512,512]{1,0:T(8,128)(2,1)S(1)}, bf16[512,512]{1,0:T(8,128)(2,1)}, u32[]{:S(2)}) copy-start(bf16[512,512]{1,0:T(8,128)(2,1)} %slice.231) | copy-start | bytes 1572868
  131.2 48.6 %collective-permute-start.5 = (bf16[512,4096]{1,0:T(8,128)(2,1)}, bf16[512,4096]{1,0:T(8,128)(2,1)S(1)}, u32[]{:S(2)}, u32[]{:S(2)}) collective-permute-start(bf16[512,4096]{1,0:T(8,128)(2,1)} %all-gather.2.cloned.1.call-done), channel_id=1, source_target_pairs={{0,4},{4,0},{8,12},{12,8},{16,20},{20,16},{24,28},{28,24},{1,5},{5... | collective-permute-start | bytes 12582920 | tf_op jit(solution)/shard_map/ppermute | solution.py:43
  151.2 13.4 %collective-permute-start.9 = (bf16[512,512]{1,0:T(8,128)(2,1)}, bf16[512,512]{1,0:T(8,128)(2,1)S(1)}, u32[]{:S(2)}, u32[]{:S(2)}) collective-permute-start(bf16[512,512]{1,0:T(8,128)(2,1)} %slice.232), channel_id=1, source_target_pairs={{8,0},{12,4},{0,8},{4,12},{24,16},{28,20},{16,24},{20,28},{9,1},{1... | collective-permute-start | bytes 1572872 | tf_op jit(solution)/shard_map/ppermute | solution.py:40
  154.3 13.0 %collective-permute-start.8 = (bf16[512,512]{1,0:T(8,128)(2,1)S(1)}, bf16[512,512]{1,0:T(8,128)(2,1)S(1)}, u32[]{:S(2)}, u32[]{:S(2)}) collective-permute-start(bf16[512,512]{1,0:T(8,128)(2,1)S(1)} %copy-done.11), channel_id=1, source_target_pairs={{16,0},{20,4},{24,8},{28,12},{0,16},{4,20},{8,24},{12,28},{17,1},{... | collective-permute-start | bytes 1572872 | tf_op jit(solution)/shard_map/ppermute | solution.py:40
  169.2 1.2 copy-start.8
  173.1 2.0 copy-start.6
  193.9 7.7 %collective-permute-start.14 = (f32[6,512]{1,0:T(8,128)S(1)}, f32[6,512]{1,0:T(8,128)S(1)}, u32[]{:S(2)}, u32[]{:S(2)}) collective-permute-start(f32[6,512]{1,0:T(8,128)S(1)} %slice.236), channel_id=1, source_target_pairs={{0,8},{4,12},{8,16},{12,20},{16,24},{20,28},{1,9},{5,13},{9,17},{1... | collective-permute-start | bytes 36872 | tf_op jit(solution)/shard_map/ppermute | solution.py:104
  203.7 2.0 collective-permute-start.15
  203.8 27.6 %collective-permute-start.16 = (bf16[1024,512]{1,0:T(8,128)(2,1)}, bf16[1024,512]{1,0:T(8,128)(2,1)S(1)}, u32[]{:S(2)}, u32[]{:S(2)}) collective-permute-start(bf16[1024,512]{1,0:T(8,128)(2,1)} %param.10), channel_id=1, source_target_pairs={{0,4},{4,0},{8,12},{12,8},{16,20},{20,16},{24,28},{28,24},{1,5},{5... | collective-permute-start | bytes 3145736 | tf_op jit(solution)/shard_map/ppermute | solution.py:43
  204.3 15.2 %collective-permute-start.32 = (bf16[1024,512]{1,0:T(8,128)(2,1)}, bf16[1024,512]{1,0:T(8,128)(2,1)S(1)}, u32[]{:S(2)}, u32[]{:S(2)}) collective-permute-start(bf16[1024,512]{1,0:T(8,128)(2,1)} %collective-permute-done.31), channel_id=1, source_target_pairs={{0,4},{4,0},{8,12},{12,8},{16,20},{20,16},{24,28},{28,24},{1,5},{5... | collective-permute-start | bytes 3145736 | tf_op jit(solution)/shard_map/ppermute | solution.py:43
  204.4 22.7 %collective-permute-start.24 = (bf16[1024,512]{1,0:T(8,128)(2,1)}, bf16[1024,512]{1,0:T(8,128)(2,1)S(1)}, u32[]{:S(2)}, u32[]{:S(2)}) collective-permute-start(bf16[1024,512]{1,0:T(8,128)(2,1)} %collective-permute-done.23), channel_id=1, source_target_pairs={{0,4},{4,0},{8,12},{12,8},{16,20},{20,16},{24,28},{28,24},{1,5},{5... | collective-permute-start | bytes 3145736 | tf_op jit(solution)/shard_map/ppermute | solution.py:43
  204.8 6.3 %collective-permute-start.42 = (bf16[512,512]{1,0:T(8,128)(2,1)}, bf16[512,512]{1,0:T(8,128)(2,1)S(1)}, u32[]{:S(2)}, u32[]{:S(2)}) collective-permute-start(bf16[512,512]{1,0:T(8,128)(2,1)} %collective-permute-done.40), channel_id=1, source_target_pairs={{0,4},{4,0},{8,12},{12,8},{16,20},{20,16},{24,28},{28,24},{1,5},{5... | collective-permute-start | bytes 1572872 | tf_op jit(solution)/shard_map/ppermute | solution.py:43
  205.7 6.2 %collective-permute-start.41 = (bf16[512,512]{1,0:T(8,128)(2,1)}, bf16[512,512]{1,0:T(8,128)(2,1)S(1)}, u32[]{:S(2)}, u32[]{:S(2)}) collective-permute-start(bf16[512,512]{1,0:T(8,128)(2,1)} %collective-permute-done.39), channel_id=1, source_target_pairs={{0,4},{4,0},{8,12},{12,8},{16,20},{20,16},{24,28},{28,24},{1,5},{5... | collective-permute-start | bytes 1572872 | tf_op jit(solution)/shard_map/ppermute | solution.py:43
  212.8 24.4 %collective-permute-start.43 = (bf16[128,1024]{1,0:T(8,128)(2,1)S(1)}, bf16[128,1024]{1,0:T(8,128)(2,1)S(1)}, u32[]{:S(2)}, u32[]{:S(2)}) collective-permute-start(bf16[128,1024]{1,0:T(8,128)(2,1)S(1)} %get-tuple-element.13), channel_id=1, source_target_pairs={{0,1},{1,2},{2,3},{4,5},{5,6},{6,7},{8,9},{9,10},{10,11},{12,13},{... | collective-permute-start | bytes 786440 | tf_op jit(solution)/shard_map/ppermute | solution.py:139
  216.2 37.9 %collective-permute-start.46 = (bf16[128,1024]{1,0:T(8,128)(2,1)S(1)}, bf16[128,1024]{1,0:T(8,128)(2,1)S(1)}, u32[]{:S(2)}, u32[]{:S(2)}) collective-permute-start(bf16[128,1024]{1,0:T(8,128)(2,1)S(1)} %get-tuple-element.14), channel_id=1, source_target_pairs={{1,0},{2,1},{3,2},{5,4},{6,5},{7,6},{9,8},{10,9},{11,10},{13,12},{... | collective-permute-start | bytes 786440 | tf_op jit(solution)/shard_map/ppermute | solution.py:140
  220.6 17.9 %collective-permute-start.33 = (bf16[128,1024]{1,0:T(8,128)(2,1)S(1)}, bf16[128,1024]{1,0:T(8,128)(2,1)S(1)}, u32[]{:S(2)}, u32[]{:S(2)}) collective-permute-start(bf16[128,1024]{1,0:T(8,128)(2,1)S(1)} %get-tuple-element.17), channel_id=1, source_target_pairs={{0,1},{1,2},{2,3},{4,5},{5,6},{6,7},{8,9},{9,10},{10,11},{12,13},{... | collective-permute-start | bytes 786440 | tf_op jit(solution)/shard_map/ppermute | solution.py:139
  227.1 33.4 %collective-permute-start.36 = (bf16[128,1024]{1,0:T(8,128)(2,1)S(1)}, bf16[128,1024]{1,0:T(8,128)(2,1)S(1)}, u32[]{:S(2)}, u32[]{:S(2)}) collective-permute-start(bf16[128,1024]{1,0:T(8,128)(2,1)S(1)} %get-tuple-element.18), channel_id=1, source_target_pairs={{1,0},{2,1},{3,2},{5,4},{6,5},{7,6},{9,8},{10,9},{11,10},{13,12},{... | collective-permute-start | bytes 786440 | tf_op jit(solution)/shard_map/ppermute | solution.py:140
  231.5 11.7 %collective-permute-start.25 = (bf16[128,1024]{1,0:T(8,128)(2,1)S(1)}, bf16[128,1024]{1,0:T(8,128)(2,1)S(1)}, u32[]{:S(2)}, u32[]{:S(2)}) collective-permute-start(bf16[128,1024]{1,0:T(8,128)(2,1)S(1)} %get-tuple-element.21), channel_id=1, source_target_pairs={{0,1},{1,2},{2,3},{4,5},{5,6},{6,7},{8,9},{9,10},{10,11},{12,13},{... | collective-permute-start | bytes 786440 | tf_op jit(solution)/shard_map/ppermute | solution.py:139
  237.1 34.3 %collective-permute-start.28 = (bf16[128,1024]{1,0:T(8,128)(2,1)S(1)}, bf16[128,1024]{1,0:T(8,128)(2,1)S(1)}, u32[]{:S(2)}, u32[]{:S(2)}) collective-permute-start(bf16[128,1024]{1,0:T(8,128)(2,1)S(1)} %get-tuple-element.22), channel_id=1, source_target_pairs={{1,0},{2,1},{3,2},{5,4},{6,5},{7,6},{9,8},{10,9},{11,10},{13,12},{... | collective-permute-start | bytes 786440 | tf_op jit(solution)/shard_map/ppermute | solution.py:140
  238.5 11.1 %collective-permute-start.17 = (bf16[128,1024]{1,0:T(8,128)(2,1)S(1)}, bf16[128,1024]{1,0:T(8,128)(2,1)S(1)}, u32[]{:S(2)}, u32[]{:S(2)}) collective-permute-start(bf16[128,1024]{1,0:T(8,128)(2,1)S(1)} %get-tuple-element.25), channel_id=1, source_target_pairs={{0,1},{1,2},{2,3},{4,5},{5,6},{6,7},{8,9},{9,10},{10,11},{12,13},{... | collective-permute-start | bytes 786440 | tf_op jit(solution)/shard_map/ppermute | solution.py:139
  243.2 12.5 %collective-permute-start.44 = (bf16[128,1024]{1,0:T(8,128)(2,1)S(1)}, bf16[128,1024]{1,0:T(8,128)(2,1)S(1)}, u32[]{:S(2)}, u32[]{:S(2)}) collective-permute-start(bf16[128,1024]{1,0:T(8,128)(2,1)S(1)} %fusion.76), channel_id=1, source_target_pairs={{0,1},{1,2},{2,3},{4,5},{5,6},{6,7},{8,9},{9,10},{10,11},{12,13},{... | collective-permute-start | bytes 786440 | tf_op jit(solution)/shard_map/ppermute | solution.py:139
  249.6 14.2 %collective-permute-start.34 = (bf16[128,1024]{1,0:T(8,128)(2,1)S(1)}, bf16[128,1024]{1,0:T(8,128)(2,1)S(1)}, u32[]{:S(2)}, u32[]{:S(2)}) collective-permute-start(bf16[128,1024]{1,0:T(8,128)(2,1)S(1)} %fusion.85), channel_id=1, source_target_pairs={{0,1},{1,2},{2,3},{4,5},{5,6},{6,7},{8,9},{9,10},{10,11},{12,13},{... | collective-permute-start | bytes 786440 | tf_op jit(solution)/shard_map/ppermute | solution.py:139
  254.1 11.2 %collective-permute-start.20 = (bf16[128,1024]{1,0:T(8,128)(2,1)S(1)}, bf16[128,1024]{1,0:T(8,128)(2,1)S(1)}, u32[]{:S(2)}, u32[]{:S(2)}) collective-permute-start(bf16[128,1024]{1,0:T(8,128)(2,1)S(1)} %get-tuple-element.26), channel_id=1, source_target_pairs={{1,0},{2,1},{3,2},{5,4},{6,5},{7,6},{9,8},{10,9},{11,10},{13,12},{... | collective-permute-start | bytes 786440 | tf_op jit(solution)/shard_map/ppermute | solution.py:140
  255.7 14.2 %collective-permute-start.18 = (bf16[128,1024]{1,0:T(8,128)(2,1)S(1)}, bf16[128,1024]{1,0:T(8,128)(2,1)S(1)}, u32[]{:S(2)}, u32[]{:S(2)}) collective-permute-start(bf16[128,1024]{1,0:T(8,128)(2,1)S(1)} %fusion.103), channel_id=1, source_target_pairs={{0,1},{1,2},{2,3},{4,5},{5,6},{6,7},{8,9},{9,10},{10,11},{12,13},{... | collective-permute-start | bytes 786440 | tf_op jit(solution)/shard_map/ppermute | solution.py:139
  260.5 12.3 %collective-permute-start.26 = (bf16[128,1024]{1,0:T(8,128)(2,1)S(1)}, bf16[128,1024]{1,0:T(8,128)(2,1)S(1)}, u32[]{:S(2)}, u32[]{:S(2)}) collective-permute-start(bf16[128,1024]{1,0:T(8,128)(2,1)S(1)} %fusion.94), channel_id=1, source_target_pairs={{0,1},{1,2},{2,3},{4,5},{5,6},{6,7},{8,9},{9,10},{10,11},{12,13},{... | collective-permute-start | bytes 786440 | tf_op jit(solution)/shard_map/ppermute | solution.py:139
  263.9 11.1 %collective-permute-start.47 = (bf16[128,1024]{1,0:T(8,128)(2,1)S(1)}, bf16[128,1024]{1,0:T(8,128)(2,1)S(1)}, u32[]{:S(2)}, u32[]{:S(2)}) collective-permute-start(bf16[128,1024]{1,0:T(8,128)(2,1)S(1)} %get-tuple-element.12), channel_id=1, source_target_pairs={{1,0},{2,1},{3,2},{5,4},{6,5},{7,6},{9,8},{10,9},{11,10},{13,12},{... | collective-permute-start | bytes 786440 | tf_op jit(solution)/shard_map/ppermute | solution.py:140
  265.4 42.8 %collective-permute-start.45 = (bf16[128,1024]{1,0:T(8,128)(2,1)S(1)}, bf16[128,1024]{1,0:T(8,128)(2,1)S(1)}, u32[]{:S(2)}, u32[]{:S(2)}) collective-permute-start(bf16[128,1024]{1,0:T(8,128)(2,1)S(1)} %get-tuple-element.11), channel_id=1, source_target_pairs={{0,1},{1,2},{2,3},{4,5},{5,6},{6,7},{8,9},{9,10},{10,11},{12,13},{... | collective-permute-start | bytes 786440 | tf_op jit(solution)/shard_map/ppermute | solution.py:139
  269.9 19.9 %collective-permute-start.37 = (bf16[128,1024]{1,0:T(8,128)(2,1)S(1)}, bf16[128,1024]{1,0:T(8,128)(2,1)S(1)}, u32[]{:S(2)}, u32[]{:S(2)}) collective-permute-start(bf16[128,1024]{1,0:T(8,128)(2,1)S(1)} %get-tuple-element.16), channel_id=1, source_target_pairs={{1,0},{2,1},{3,2},{5,4},{6,5},{7,6},{9,8},{10,9},{11,10},{13,12},{... | collective-permute-start | bytes 786440 | tf_op jit(solution)/shard_map/ppermute | solution.py:140
  271.5 13.6 %collective-permute-start.21 = (bf16[128,1024]{1,0:T(8,128)(2,1)S(1)}, bf16[128,1024]{1,0:T(8,128)(2,1)S(1)}, u32[]{:S(2)}, u32[]{:S(2)}) collective-permute-start(bf16[128,1024]{1,0:T(8,128)(2,1)S(1)} %get-tuple-element.24), channel_id=1, source_target_pairs={{1,0},{2,1},{3,2},{5,4},{6,5},{7,6},{9,8},{10,9},{11,10},{13,12},{... | collective-permute-start | bytes 786440 | tf_op jit(solution)/shard_map/ppermute | solution.py:140
  273.0 15.5 %collective-permute-start.29 = (bf16[128,1024]{1,0:T(8,128)(2,1)S(1)}, bf16[128,1024]{1,0:T(8,128)(2,1)S(1)}, u32[]{:S(2)}, u32[]{:S(2)}) collective-permute-start(bf16[128,1024]{1,0:T(8,128)(2,1)S(1)} %get-tuple-element.20), channel_id=1, source_target_pairs={{1,0},{2,1},{3,2},{5,4},{6,5},{7,6},{9,8},{10,9},{11,10},{13,12},{... | collective-permute-start | bytes 786440 | tf_op jit(solution)/shard_map/ppermute | solution.py:140
  274.9 24.3 %copy-start.3 = (bf16[128,4096]{1,0:T(8,128)(2,1)S(1)}, bf16[128,4096]{1,0:T(8,128)(2,1)}, u32[]{:S(2)}) copy-start(bf16[128,4096]{1,0:T(8,128)(2,1)} %param.6) | copy-start | bytes 3145732
  274.9 24.4 %copy-start.9 = (s32[128,4096]{1,0:T(8,128)S(1)}, s32[128,4096]{1,0:T(8,128)}, u32[]{:S(2)}) copy-start(s32[128,4096]{1,0:T(8,128)} %param.11) | copy-start | bytes 6291460
  274.9 24.6 %collective-permute-start.27 = (bf16[128,1024]{1,0:T(8,128)(2,1)S(1)}, bf16[128,1024]{1,0:T(8,128)(2,1)S(1)}, u32[]{:S(2)}, u32[]{:S(2)}) collective-permute-start(bf16[128,1024]{1,0:T(8,128)(2,1)S(1)} %get-tuple-element.19), channel_id=1, source_target_pairs={{0,1},{1,2},{2,3},{4,5},{5,6},{6,7},{8,9},{9,10},{10,11},{12,13},{... | collective-permute-start | bytes 786440 | tf_op jit(solution)/shard_map/ppermute | solution.py:139
  285.1 7.9 %collective-permute-start.19 = (bf16[128,1024]{1,0:T(8,128)(2,1)S(1)}, bf16[128,1024]{1,0:T(8,128)(2,1)S(1)}, u32[]{:S(2)}, u32[]{:S(2)}) collective-permute-start(bf16[128,1024]{1,0:T(8,128)(2,1)S(1)} %get-tuple-element.23), channel_id=1, source_target_pairs={{0,1},{1,2},{2,3},{4,5},{5,6},{6,7},{8,9},{9,10},{10,11},{12,13},{... | collective-permute-start | bytes 786440 | tf_op jit(solution)/shard_map/ppermute | solution.py:139
  288.5 9.4 %collective-permute-start.22 = (bf16[128,1024]{1,0:T(8,128)(2,1)S(1)}, bf16[128,1024]{1,0:T(8,128)(2,1)S(1)}, u32[]{:S(2)}, u32[]{:S(2)}) collective-permute-start(bf16[128,1024]{1,0:T(8,128)(2,1)S(1)} %fusion.102), channel_id=1, source_target_pairs={{1,0},{2,1},{3,2},{5,4},{6,5},{7,6},{9,8},{10,9},{11,10},{13,12},{... | collective-permute-start | bytes 786440 | tf_op jit(solution)/shard_map/ppermute | solution.py:140
  289.9 13.6 %collective-permute-start.30 = (bf16[128,1024]{1,0:T(8,128)(2,1)S(1)}, bf16[128,1024]{1,0:T(8,128)(2,1)S(1)}, u32[]{:S(2)}, u32[]{:S(2)}) collective-permute-start(bf16[128,1024]{1,0:T(8,128)(2,1)S(1)} %fusion.93), channel_id=1, source_target_pairs={{1,0},{2,1},{3,2},{5,4},{6,5},{7,6},{9,8},{10,9},{11,10},{13,12},{... | collective-permute-start | bytes 786440 | tf_op jit(solution)/shard_map/ppermute | solution.py:140
  293.0 10.7 %collective-permute-start.35 = (bf16[128,1024]{1,0:T(8,128)(2,1)S(1)}, bf16[128,1024]{1,0:T(8,128)(2,1)S(1)}, u32[]{:S(2)}, u32[]{:S(2)}) collective-permute-start(bf16[128,1024]{1,0:T(8,128)(2,1)S(1)} %get-tuple-element.15), channel_id=1, source_target_pairs={{0,1},{1,2},{2,3},{4,5},{5,6},{6,7},{8,9},{9,10},{10,11},{12,13},{... | collective-permute-start | bytes 786440 | tf_op jit(solution)/shard_map/ppermute | solution.py:139
  297.9 10.1 %collective-permute-start.38 = (bf16[128,1024]{1,0:T(8,128)(2,1)S(1)}, bf16[128,1024]{1,0:T(8,128)(2,1)S(1)}, u32[]{:S(2)}, u32[]{:S(2)}) collective-permute-start(bf16[128,1024]{1,0:T(8,128)(2,1)S(1)} %fusion.84), channel_id=1, source_target_pairs={{1,0},{2,1},{3,2},{5,4},{6,5},{7,6},{9,8},{10,9},{11,10},{13,12},{... | collective-permute-start | bytes 786440 | tf_op jit(solution)/shard_map/ppermute | solution.py:140
  299.5 11.2 %collective-permute-start.48 = (bf16[128,1024]{1,0:T(8,128)(2,1)S(1)}, bf16[128,1024]{1,0:T(8,128)(2,1)S(1)}, u32[]{:S(2)}, u32[]{:S(2)}) collective-permute-start(bf16[128,1024]{1,0:T(8,128)(2,1)S(1)} %fusion.75), channel_id=1, source_target_pairs={{1,0},{2,1},{3,2},{5,4},{6,5},{7,6},{9,8},{10,9},{11,10},{13,12},{... | collective-permute-start | bytes 786440 | tf_op jit(solution)/shard_map/ppermute | solution.py:140
  303.5 8.2 %copy-start.1 = (f32[7,64]{1,0:T(8,128)S(1)}, f32[7,64]{1,0:T(8,128)}, u32[]{:S(2)}) copy-start(f32[7,64]{1,0:T(8,128)} %param.9) | copy-start | bytes 5380
  308.2 2.6 copy-start.10
Sparse Core Ops, SparseCore 0:
  18.7 83.4 all-gather.1

commit v2 on v0

v2 whole, which is shorter than its diff:
```python
import functools
import math

import jax
import jax.numpy as jnp
from jax import lax
from jax.experimental import pallas as pl
from jax.experimental.pallas import tpu as pltpu
from jax.sharding import PartitionSpec as P

F32 = jnp.float32
BF16 = jnp.bfloat16
MIB = 1 << 20
WHOLE = pl.BlockSpec(memory_space=pltpu.VMEM)


def grid_of(chips):
    ny = max(d for d in range(1, math.isqrt(chips) + 1) if chips % d == 0)
    return ny, chips // ny


def dot(a, b):
    return jnp.dot(a, b, preferred_element_type=F32)


def cost(flops, *arrays):
    moved = sum(math.prod(a.shape) * a.dtype.itemsize for a in arrays)
    return pl.CostEstimate(flops=flops, bytes_accessed=moved, transcendentals=0)


def columns_of(x_ref, at_ref, index, deep):
    return x_ref[:, pl.ds(pl.multiple_of(at_ref[index], deep), deep)]


def product_kernel(at_ref, x_ref, *refs):
    pieces, out_ref = refs[:-1], refs[-1]
    deep = pieces[0].shape[1]
    key = value = None
    for index, piece in enumerate(pieces):
        x = columns_of(x_ref, at_ref, index, deep)
        new_key, new_value = dot(x, piece[0]), dot(x, piece[1])
        key = new_key if key is None else key + new_key
        value = new_value if value is None else value + new_value
    out_ref[...] = key.astype(BF16).astype(F32) * value.astype(BF16).astype(F32)


def gate_kernel(at_ref, x_ref, filtered_ref, *refs):
    pieces, out_ref = refs[:-1], refs[-1]
    deep = pieces[0].shape[0]
    query = None
    for index, piece in enumerate(pieces):
        new = dot(columns_of(x_ref, at_ref, index, deep), piece[...])
        query = new if query is None else query + new
    out_ref[...] = (query.astype(BF16).astype(F32) * filtered_ref[...]).astype(BF16)


def project(kernel, at, x, extra, pieces, out_dtype):
    length, model = x.shape
    half = pieces[0].shape[-1]
    tile = math.gcd(half, 256)
    lead = pieces[0].shape[:-1]
    count = 2 if len(lead) == 2 else 1
    out = jax.ShapeDtypeStruct((length, half), out_dtype)
    by_tile = pl.BlockSpec((length, tile), lambda j, at: (0, j))
    return pl.pallas_call(
        kernel,
        out_shape=out,
        grid_spec=pltpu.PrefetchScalarGridSpec(
            num_scalar_prefetch=1,
            grid=(half // tile,),
            in_specs=[pl.BlockSpec((length, model), lambda j, at: (0, 0))]
            + [by_tile] * len(extra)
            + [
                pl.BlockSpec(lead + (tile,), lambda j, at: (0,) * len(lead) + (j,))
                for _ in pieces
            ],
            out_specs=by_tile,
        ),
        compiler_params=pltpu.CompilerParams(vmem_limit_bytes=36 * MIB),
        cost_estimate=cost(2 * count * length * model * half, x, out, *extra, *pieces),
    )(at, x, *extra, *pieces)


def filter_kernel(product_ref, halo_ref, taps_ref, out_ref, held):
    length, pad = product_ref.shape[0], halo_ref.shape[0]
    held[:pad] = halo_ref[...]
    held[pad:] = product_ref[...]
    total = None
    for offset in range(taps_ref.shape[0]):
        term = taps_ref[offset : offset + 1] * held[pad - offset : pad - offset + length]
        total = term if total is None else total + term
    out_ref[...] = total


def causal_filter(product, halo, taps):
    length, half = product.shape
    pad = halo.shape[0]
    tile = math.gcd(half, 256)
    return pl.pallas_call(
        filter_kernel,
        out_shape=jax.ShapeDtypeStruct(product.shape, F32),
        grid=(half // tile,),
        in_specs=[
            pl.BlockSpec((rows, tile), lambda j: (0, j)) for rows in (length, pad, taps.shape[0])
        ],
        out_specs=pl.BlockSpec((length, tile), lambda j: (0, j)),
        scratch_shapes=[pltpu.VMEM((pad + length, tile), F32)],
        compiler_params=pltpu.CompilerParams(vmem_limit_bytes=16 * MIB),
        cost_estimate=cost(14 * length * half, product, product),
    )(product, halo, taps)


def terms_kernel(count, n_tp, z_ref, gated_ref, *refs):
    pieces, refs = refs[:count], refs[count:]
    given, outs, held = (refs[0], refs[1:-1], refs[-1]) if len(refs) > 2 else (None, refs[:1], refs[-1])
    length = gated_ref.shape[0]
    rows = length // n_tp
    for slot in range(n_tp):
        owner = lax.rem(z_ref[0] + slot, n_tp)
        held[slot * rows : (slot + 1) * rows] = gated_ref[
            pl.ds(pl.multiple_of(owner * rows, rows), rows)
        ]
    wide = pieces[0].shape[1]
    for index, piece in enumerate(pieces):
        at = slice(index * wide, (index + 1) * wide)
        total = dot(held[...], piece[...])
        if given is None:
            outs[0][:, at] = total.astype(BF16)
        else:
            total = total + given[:, at].astype(F32)
            for slot in range(n_tp):
                outs[slot][:, at] = total[slot * rows : (slot + 1) * rows].astype(BF16)


def terms(n_tp, z, gated, pieces, given=None):
    length, half = gated.shape
    cols = len(pieces) * pieces[0].shape[1]
    if given is None:
        out = [jax.ShapeDtypeStruct((length, cols), BF16)]
    else:
        out = [jax.ShapeDtypeStruct((length // n_tp, cols), BF16)] * n_tp
    extra = [] if given is None else [given]
    result = pl.pallas_call(
        functools.partial(terms_kernel, len(pieces), n_tp),
        out_shape=out,
        in_specs=[pl.BlockSpec(memory_space=pltpu.SMEM)]
        + [WHOLE] * (1 + len(pieces) + len(extra)),
        out_specs=[WHOLE] * len(out),
        scratch_shapes=[pltpu.VMEM((length, half), BF16)],
        compiler_params=pltpu.CompilerParams(vmem_limit_bytes=36 * MIB),
        cost_estimate=cost(2 * length * half * cols, gated, *pieces, *extra, *out),
    )(z, gated, *pieces, *extra)
    return result[0] if given is None else result


def on_device(tokens, norm_gain, in_weight, filters, out_weight, keep_mask):
    n_seq, n_tp = lax.axis_size("seq"), lax.axis_size("tp")
    chips = n_seq // 2
    ny, nx = grid_of(chips)
    seq = lax.axis_index("seq")
    core, here = seq % 2, seq // 2
    my_y, my_x = here // nx, here % nx
    rows, model = tokens.shape
    length = rows * n_tp
    deep, channels = in_weight.shape[1:]
    half = channels // 2
    wide = out_weight.shape[1]

    def place(y, x, c):
        return ((y % ny) * nx + x % nx) * 2 + c

    def from_chip(block, dy, dx):
        route = [
            (place(y + dy, x + dx, c), place(y, x, c))
            for y in range(ny)
            for x in range(nx)
            for c in range(2)
        ]
        return lax.ppermute(block, "seq", route)

    def from_partner(block):
        return lax.ppermute(block, "seq", [(s, s ^ 1) for s in range(n_seq)])

    def direct(mine, brought):
        along_x = [(mine, brought)]
        along_y = [(mine, brought)]
        along_x += [tuple(from_chip(b, 0, dx) for b in (mine, brought)) for dx in range(1, nx)]
        along_y += [tuple(from_chip(b, dy, 0) for b in (mine, brought)) for dy in range(1, ny)]
        return along_x, along_y

    def onward(along_x, along_y):
        return {
            (dy, dx): (from_chip(along_x[dx][0], dy, 0), from_chip(along_y[dy][1], 0, dx))
            for dy in range(1, ny)
            for dx in range(1, nx)
        }

    def listed(along_x, along_y, rest):
        found = {(0, dx): pair for dx, pair in enumerate(along_x)}
        found.update({(dy, 0): pair for dy, pair in enumerate(along_y)})
        found.update(rest)
        return found

    def halves(array, axis, at):
        size = array.shape[axis] // 2
        return lax.dynamic_slice_in_dim(array, at * size, size, axis=axis)

    def columns(array, first, count, at):
        return lax.dynamic_slice(array, (first, 0, at * half), (count, deep, half))

    mine_kv = columns(in_weight, 1, 2, core)
    away_kv = columns(in_weight, 1, 2, 1 - core)
    brought_kv = from_partner(away_kv)
    kv_x, kv_y = direct(mine_kv, brought_kv)

    tokens_then, _ = lax.optimization_barrier((tokens, away_kv))
    widened = tokens_then.astype(F32)
    mean_sq = jnp.mean(widened * widened, axis=1, keepdims=True)
    normed = (widened * lax.rsqrt(mean_sq + 1e-06) * norm_gain).astype(BF16)
    own_rows = lax.all_gather(normed, "tp", axis=0, tiled=True)
    in_weight_then, out_weight_then, _ = lax.optimization_barrier((in_weight, out_weight, normed))
    mine_q = columns(in_weight_then, 0, 1, core)[0]
    brought_q = from_partner(columns(in_weight_then, 0, 1, 1 - core)[0])
    mine_o = halves(out_weight_then, 0, core)
    brought_o = from_partner(halves(out_weight_then, 0, 1 - core))

    kv_rest = onward(kv_x, kv_y)
    mine_q, brought_q, _ = lax.optimization_barrier((mine_q, brought_q, (kv_x[1:], kv_y[1:])))
    q_x, q_y = direct(mine_q, brought_q)
    q_x, q_y, kv_rest = lax.optimization_barrier((q_x, q_y, kv_rest))
    q_rest = onward(q_x, q_y)
    mine_o, brought_o, _ = lax.optimization_barrier((mine_o, brought_o, q_rest))
    o_x, o_y = direct(mine_o, brought_o)
    o_rest = onward(o_x, o_y)

    own_rows, _ = lax.optimization_barrier((own_rows, kv_rest))
    other_rows = from_partner(own_rows)
    kv = listed(kv_x, kv_y, kv_rest)
    q = listed(q_x, q_y, q_rest)
    order = list(kv)
    at = jnp.stack(
        [place(my_y + dy, my_x + dx, core ^ rc) * deep for dy, dx in order for rc in range(2)]
    ).astype(jnp.int32)
    kv_pieces = [piece for key in order for piece in kv[key]]
    q_pieces = [piece for key in order for piece in q[key]]

    reach = filters.shape[0] - 1
    pad = -(-reach // 8) * 8
    own_product = project(product_kernel, at, own_rows, [], kv_pieces, F32)
    other_product = project(product_kernel, at, other_rows, [], kv_pieces, F32)
    own_tail, other_tail = own_product[length - pad :], other_product[length - pad :]
    first_tail = jnp.where(core == 0, own_tail, other_tail)
    last_tail = jnp.where(core == 0, other_tail, own_tail)
    rim = lax.ppermute(
        last_tail,
        "seq",
        [(2 * i + c, 2 * i + 2 + c) for i in range(chips - 1) for c in range(2)],
    )
    groups = filters.shape[1] // 2
    taps = jnp.repeat(
        lax.dynamic_slice_in_dim(filters, core * groups, groups, axis=1), half // groups, axis=1
    )
    own_filtered = causal_filter(own_product, jnp.where(core == 0, rim, first_tail), taps)
    other_filtered = causal_filter(other_product, jnp.where(core == 0, first_tail, rim), taps)
    other_gated = project(gate_kernel, at, other_rows, [other_filtered], q_pieces, BF16)
    own_gated = project(gate_kernel, at, own_rows, [own_filtered], q_pieces, BF16)

    position = lax.axis_index("tp")
    z = position.astype(jnp.int32).reshape(1)
    up = [(i, i + 1) for i in range(n_tp - 1)]
    down = [(i + 1, i) for i in range(n_tp - 1)]

    def plus(a, b):
        return (a.astype(F32) + b.astype(F32)).astype(BF16)

    def summed(pairs, own_gated, other_gated):
        pieces = [piece for pair in pairs for piece in pair]
        leaving = terms(n_tp, z, other_gated, [piece for pair in pairs for piece in pair[::-1]])
        slots = terms(n_tp, z, own_gated, pieces, from_partner(leaving))
        rising = falling = None
        for step in range(n_tp - 1):
            send_up, send_down = slots[n_tp - 1 - step], slots[step + 1]
            if step:
                send_up, send_down = plus(send_up, rising), plus(send_down, falling)
            rising = lax.ppermute(send_up, "tp", up)
            falling = lax.ppermute(send_down, "tp", down)
        return slots[0].astype(F32) + rising.astype(F32) + falling.astype(F32), slots[0]

    groups_of = [[(0, 0)], [key for key in order if (key[0] == 0) != (key[1] == 0)], list(o_rest)]
    out_pieces = listed(o_x, o_y, o_rest)
    result = jnp.zeros((rows, model), BF16)
    for keys in groups_of:
        mixed, done = summed([out_pieces[key] for key in keys], own_gated, other_gated)
        own_gated, other_gated, _ = lax.optimization_barrier((own_gated, other_gated, done))
        for index, (dy, dx) in enumerate(keys):
            start = place(my_y + dy, my_x + dx, 0) * wide
            pair = mixed[:, index * 2 * wide : (index + 1) * 2 * wide]
            swapped = jnp.concatenate([pair[:, wide:], pair[:, :wide]], axis=1)
            kept = lax.dynamic_slice_in_dim(keep_mask, start, 2 * wide, axis=1).astype(F32)
            base = lax.dynamic_slice_in_dim(tokens, start, 2 * wide, axis=1).astype(F32)
            pair = jnp.where(core == 0, pair, swapped)
            part = (base + kept * pair * (1.0 / 0.9)).astype(BF16)
            result = lax.dynamic_update_slice_in_dim(result, part, start, axis=1)
    return result


def solution(mesh):
    in_specs = (
        P(("seq", "tp"), None),
        P(),
        P(None, "seq", "tp"),
        P(None, "tp"),
        P("tp", "seq"),
        P(("seq", "tp"), None),
    )
    out_specs = P(("seq", "tp"), None)
    return jax.shard_map(
        on_device, mesh=mesh, in_specs=in_specs, out_specs=out_specs, check_vma=False
    )
```

time: 376 us -> 300 us (0.80)
  waiting for transfers between devices: 322 us -> 129 us
  starting transfers between devices: 2.29 us -> 79.2 us
  Pallas kernels: 0 us -> 39.2 us
  matrix products: 29.7 us -> 0 us
  local copies, waits for them, and re-layouts: 1.29 us -> 30 us
    all_gather x3 -> x1, waiting for transfers between devices: 243 us -> 0.01 us  [on_device(): own_rows = lax.all_gather(normed, 'tp', axis=0, tiled=True)]
    ppermute x1 -> x44, waiting for transfers between devices: 0.65 us -> 129 us  [the longest x18 88.5 us: from_chip(): return lax.ppermute(block, 'seq', route)]
    ppermute x1 -> x44, starting transfers between devices: 2.17 us -> 79.2 us  [the longest x9 36.2 us: summed(): rising = lax.ppermute(send_up, 'tp', up)]
    reduce_scatter x1 -> x0, waiting for transfers between devices: 76.9 us -> none  [on_device(): lax.psum_scatter(terms.astype(jnp.bfloat16), 'tp', scatter_dimension=0, t...]
    pallas_call x0 -> x12, Pallas kernels: none -> 39.2 us  [the longest x4 23.8 us: project(): pl.pallas_call(kernel, out_shape=out, grid_spec=pltpu.PrefetchScalarGridS...]
    dot_general x2 -> x0, matrix products: 29.7 us -> none  [the longest x1 18.1 us: on_device(): jnp.einsum('ld,pdc->plc', gathered, lax.all_gather(in_weight, 'seq', axis...]
    unnamed x8 -> x86, local copies, waits for them, and re-layouts: 0.02 us -> 24.3 us
    dynamic_slice x0 -> x3, local copies, waits for them, and re-layouts: none -> 3.9 us  [the longest x1 2.06 us: halves(): return lax.dynamic_slice_in_dim(array, at * size, size, axis=axis)]
  transfers between devices with their start and end apart: 5 -> 45, of which waited for: 5 -> 21; matrix products, arithmetic and copies ran while one was open for 5% -> 3% of each run, Pallas kernels for 0% -> 9%
where the time goes in v2:
time: 300 us; the launch traced here: 299 us
  waiting for transfers between devices  129 us (43%)
  starting transfers between devices  79.2 us (26%)
  Pallas kernels  39.2 us (13%)
  local copies, waits for them, and re-layouts  30 us (10%)
  between operations  14.2 us (5%)
  other arithmetic  6.98 us (2%)
    ppermute x18, waiting for transfers between devices, from_chip(): return lax.ppermute(block, 'seq', route)  88.5 us
    ppermute x9, starting transfers between devices, summed(): rising = lax.ppermute(send_up, 'tp', up)  36.2 us
    ppermute x9, waiting for transfers between devices, summed(): falling = lax.ppermute(send_down, 'tp', down)  28.8 us
    ppermute x18, starting transfers between devices, from_chip(): return lax.ppermute(block, 'seq', route)  27.5 us
    unnamed x86, local copies, waits for them, and re-layouts  24.3 us
    pallas_call x4, Pallas kernels, project(): pl.pallas_call(kernel, out_shape=out, grid_spec=pltpu.PrefetchScalarGridS...  23.8 us
    pallas_call x6, Pallas kernels, terms(): pl.pallas_call(functools.partial(terms_kernel, len(pieces), n_tp), out_sh...  12.1 us
    ppermute x9, starting transfers between devices, summed(): falling = lax.ppermute(send_down, 'tp', down)  11.6 us
  transfers between devices with their start and end apart: 45, of which 21 were waited for; matrix products, arithmetic and copies ran while one was open for 3% of the time, Pallas kernels for 9%

profile of v2, /device:TPU:0, one launch (start us, length us, event | category | flops | bytes accessed | tf_op | source)
XLA Modules:
  0.0 298.5 jit_solution(1010739598062132988)
XLA Ops:
  6.5 1.8 constant_dynamic-slice_fusion.3
  8.7 1.3 fusion.2
  10.6 2.6 collective-permute-start.1
  13.1 2.6 collective-permute-start.5
  15.8 1.9 collective-permute-start.3
  17.7 19.4 %collective-permute-done.1.refs_2_ = bf16[2,512,512]{2,1,0:T(8,128)(2,1)S(1)} collective-permute-done((bf16[2,512,512]{2,1,0:T(8,128)(2,1)S(1)}, bf16[2,512,512]{2,1,0:T(8,128)(2,1)S(1)}, u32[]{:S(2)}, u32[]{:S(2)}) %collective-permute-start.1) | collective-permute-done | bytes 1048608 | tf_op jit(solution)/shard_map/ppermute | solution.py:179
  37.1 2.0 collective-permute-start.10
  39.1 1.3 dynamic-slice_bitcast_fusion
  40.5 1.6 collective-permute-start.11
  43.0 19.1 %collective-permute-done.4.refs_4_ = bf16[2,512,512]{2,1,0:T(8,128)(2,1)S(1)} collective-permute-done((bf16[2,512,512]{2,1,0:T(8,128)(2,1)S(1)}, bf16[2,512,512]{2,1,0:T(8,128)(2,1)S(1)}, u32[]{:S(2)}, u32[]{:S(2)}) %collective-permute-start.4) | collective-permute-done | bytes 1048608 | tf_op jit(solution)/shard_map/ppermute | solution.py:179
  64.1 2.0 collective-permute-start.6
  66.1 1.5 collective-permute-start.8
  68.2 16.4 %collective-permute-done.10.refs_6_ = bf16[2,512,512]{2,1,0:T(8,128)(2,1)S(1)} collective-permute-done((bf16[2,512,512]{2,1,0:T(8,128)(2,1)S(1)}, bf16[2,512,512]{2,1,0:T(8,128)(2,1)S(1)}, u32[]{:S(2)}, u32[]{:S(2)}) %collective-permute-start.10) | collective-permute-done | bytes 1048608 | tf_op jit(solution)/shard_map/ppermute | solution.py:179
  85.6 2.1 collective-permute-start.9
  87.7 5.6 %collective-permute-done.6.refs_2_ = bf16[512,512]{1,0:T(8,128)(2,1)S(1)} collective-permute-done((bf16[512,512]{1,0:T(8,128)(2,1)S(1)}, bf16[512,512]{1,0:T(8,128)(2,1)S(1)}, u32[]{:S(2)}, u32[]{:S(2)}) %collective-permute-start.6) | collective-permute-done | bytes 524320 | tf_op jit(solution)/shard_map/ppermute | solution.py:179
  93.3 11.0 %collective-permute-done.7.refs_3_ = bf16[512,512]{1,0:T(8,128)(2,1)S(1)} collective-permute-done((bf16[512,512]{1,0:T(8,128)(2,1)S(1)}, bf16[512,512]{1,0:T(8,128)(2,1)S(1)}, u32[]{:S(2)}, u32[]{:S(2)}) %collective-permute-start.7) | collective-permute-done | bytes 524320 | tf_op jit(solution)/shard_map/ppermute | solution.py:179
  105.1 1.5 collective-permute-done.9.refs_5_
  107.6 2.1 constant_dynamic-slice_fusion
  110.3 1.7 collective-permute-start.14
  112.0 1.5 collective-permute-start.15
  113.5 2.2 copy-done.2
  125.5 5.9 %shard_map.64.product_ref = f32[512,512]{1,0:T(8,128)S(1)} custom-call(s32[8]{0:T(128)S(1)} %stack.35.at_ref, bf16[512,4096]{1,0:T(8,128)(2,1)S(1)} %copy-done.2, bf16[2,512,512]{2,1,0:T(8,128)(2,1)S(1)} %copy-done.19, bf16[2,512,512]{2,1,0:T(8,128)(2,1)S(1)} %copy-done.25, bf16[2,512,512]{2,1,0:T(8,128)(2,1)S(1)} %copy-done.27, ...), custom_call_target="tpu_custom_call" | custom-call | flops 4294967296 | bytes 13631488 | tf_op jit(solution)/shard_map/pallas_call | solution.py:65
  131.5 7.8 %shard_map.65.product_ref = f32[512,512]{1,0:T(8,128)S(1)} custom-call(s32[8]{0:T(128)S(1)} %stack.35.at_ref, bf16[512,4096]{1,0:T(8,128)(2,1)} %collective-permute-done.12.x_ref, bf16[2,512,512]{2,1,0:T(8,128)(2,1)S(1)} %copy-done.19, bf16[2,512,512]{2,1,0:T(8,128)(2,1)S(1)} %copy-done.25, bf16[2,512,512]{2,1,0:T(8,128)(2,1)S(1)} %copy-done.27, ...), custom_call_target="tpu_custom_call" | custom-call | flops 4294967296 | bytes 13631488 | tf_op jit(solution)/shard_map/pallas_call | solution.py:65
  140.3 2.6 collective-permute-start.13
  146.1 1.7 shard_map.68.filtered_ref
  149.9 5.7 %shard_map.69.gated_ref = bf16[512,512]{1,0:T(8,128)(2,1)S(1)} custom-call(s32[8]{0:T(128)S(1)} %stack.35.at_ref, bf16[512,4096]{1,0:T(8,128)(2,1)} %collective-permute-done.12.x_ref, f32[512,512]{1,0:T(8,128)S(1)} %shard_map.68.filtered_ref, bf16[512,512]{1,0:T(8,128)(2,1)S(1)} %get-tuple-element.44.refs_0_, ...), custom_call_target="tpu_custom_call" | custom-call | flops 2147483648 | bytes 9961472 | tf_op jit(solution)/shard_map/pallas_call | solution.py:65
  155.6 1.9 shard_map.70
  157.6 2.4 collective-permute-start.24
  160.0 2.8 collective-permute-start.26
  162.9 1.7 shard_map.66.filtered_ref
  164.6 4.3 %shard_map.67.gated_ref = bf16[512,512]{1,0:T(8,128)(2,1)S(1)} custom-call(s32[8]{0:T(128)S(1)} %stack.35.at_ref, bf16[512,4096]{1,0:T(8,128)(2,1)S(1)} %copy-done.3, f32[512,512]{1,0:T(8,128)S(1)} %shard_map.66.filtered_ref, bf16[512,512]{1,0:T(8,128)(2,1)S(1)} %get-tuple-element.44.refs_0_, bf16[512,512]{1,0:T(8,128)(2,1)S(1)} %collective-permute-done.refs_1_, ...), custom_call_target="tpu_custom_call" | custom-call | flops 2147483648 | bytes 9961472 | tf_op jit(solution)/shard_map/pallas_call | solution.py:65
  168.9 1.8 shard_map.71
  170.7 2.1 collective-permute-done.24.refs_1_.refs_0_
  172.8 10.9 %collective-permute-done.25.refs_0_.refs_1_ = bf16[512,512]{1,0:T(8,128)(2,1)S(1)} collective-permute-done((bf16[512,512]{1,0:T(8,128)(2,1)}, bf16[512,512]{1,0:T(8,128)(2,1)S(1)}, u32[]{:S(2)}, u32[]{:S(2)}) %collective-permute-start.25) | collective-permute-done | bytes 524320 | tf_op jit(solution)/shard_map/ppermute | solution.py:179
  183.7 2.4 collective-permute-done.27.refs_2_.refs_3_
  186.2 3.8 %shard_map.72 = bf16[512,2048]{1,0:T(8,128)(2,1)} custom-call(s32[1]{0:T(128)} %bitcast.z_ref, bf16[512,512]{1,0:T(8,128)(2,1)S(1)} %shard_map.69.gated_ref, bf16[512,512]{1,0:T(8,128)(2,1)S(1)} %collective-permute-done.25.refs_0_.refs_1_, bf16[512,512]{1,0:T(8,128)(2,1)} %collective-permute-done.24.refs_1_.refs_0_, ...), custom_call_target="tpu_custom_call" | custom-call | flops 1073741824 | bytes 4718592 | tf_op jit(solution)/shard_map/pallas_call | solution.py:143
  190.0 3.5 %collective-permute-start.18 = (bf16[128,1024]{1,0:T(8,128)(2,1)S(1)}, bf16[128,1024]{1,0:T(8,128)(2,1)S(1)}, u32[]{:S(2)}, u32[]{:S(2)}) collective-permute-start(bf16[128,1024]{1,0:T(8,128)(2,1)S(1)} %get-tuple-element.56), channel_id=1, source_target_pairs={{0,1},{1,2},{2,3},{4,5},{5,6},{6,7},{8,9},{9,10},{10,11},{12,13},{... | collective-permute-start | bytes 786440 | tf_op jit(solution)/shard_map/ppermute | solution.py:285
  193.5 1.3 collective-permute-start.21
  194.8 1.8 collective-permute-start.35
  196.9 2.8 collective-permute-done.18
  199.7 4.1 %collective-permute-done.21 = bf16[128,1024]{1,0:T(8,128)(2,1)S(1)} collective-permute-done((bf16[128,1024]{1,0:T(8,128)(2,1)S(1)}, bf16[128,1024]{1,0:T(8,128)(2,1)S(1)}, u32[]{:S(2)}, u32[]{:S(2)}) %collective-permute-start.21) | collective-permute-done | bytes 262176 | tf_op jit(solution)/shard_map/ppermute | solution.py:286
  204.7 4.2 %collective-permute-start.19 = (bf16[128,1024]{1,0:T(8,128)(2,1)}, bf16[128,1024]{1,0:T(8,128)(2,1)}, u32[]{:S(2)}, u32[]{:S(2)}) collective-permute-start(bf16[128,1024]{1,0:T(8,128)(2,1)} %get-tuple-element.89), channel_id=1, source_target_pairs={{0,1},{1,2},{2,3},{4,5},{5,6},{6,7},{8,9},{9,10},{10,11},{12,13},{... | collective-permute-start | bytes 786440 | tf_op jit(solution)/shard_map/ppermute | solution.py:285
  208.9 1.3 collective-permute-start.22
  212.3 3.2 %shard_map.73 = (bf16[128,2048]{1,0:T(8,128)(2,1)S(1)}, bf16[128,2048]{1,0:T(8,128)(2,1)S(1)}, bf16[128,2048]{1,0:T(8,128)(2,1)S(1)}, bf16[128,2048]{1,0:T(8,128)(2,1)S(1)}) custom-call(s32[1]{0:T(128)} %bitcast.z_ref, bf16[512,512]{1,0:T(8,128)(2,1)S(1)} %shard_map.67.gated_ref, bf16[512,512]{1,0:T(8,128)(2,1)} %collective-permute-done.24.refs_1_.refs_0_, ...), custom_call_target="tpu_custom_call" | custom-call | flops 1073741824 | bytes 6815744 | tf_op jit(solution)/shard_map/pallas_call | solution.py:143
  215.5 4.7 %collective-permute-start.29 = (bf16[128,2048]{1,0:T(8,128)(2,1)S(1)}, bf16[128,2048]{1,0:T(8,128)(2,1)S(1)}, u32[]{:S(2)}, u32[]{:S(2)}) collective-permute-start(bf16[128,2048]{1,0:T(8,128)(2,1)S(1)} %get-tuple-element.62), channel_id=1, source_target_pairs={{0,1},{1,2},{2,3},{4,5},{5,6},{6,7},{8,9},{9,10},{10,11},{12,13},{... | collective-permute-start | bytes 1572872 | tf_op jit(solution)/shard_map/ppermute | solution.py:285
  220.2 1.3 collective-permute-start.32
  222.6 4.6 %collective-permute-start.20 = (bf16[128,1024]{1,0:T(8,128)(2,1)S(1)}, bf16[128,1024]{1,0:T(8,128)(2,1)S(1)}, u32[]{:S(2)}, u32[]{:S(2)}) collective-permute-start(bf16[128,1024]{1,0:T(8,128)(2,1)S(1)} %add_convert_fusion.5), channel_id=1, source_target_pairs={{0,1},{1,2},{2,3},{4,5},{5,6},{6,7},{8,9},{9,10},{10,11},{12,13},{... | collective-permute-start | bytes 786440 | tf_op jit(solution)/shard_map/ppermute | solution.py:285
  228.1 1.3 collective-permute-start.23
  229.4 3.2 %collective-permute-done.29 = bf16[128,2048]{1,0:T(8,128)(2,1)S(1)} collective-permute-done((bf16[128,2048]{1,0:T(8,128)(2,1)S(1)}, bf16[128,2048]{1,0:T(8,128)(2,1)S(1)}, u32[]{:S(2)}, u32[]{:S(2)}) %collective-permute-start.29) | collective-permute-done | bytes 524320 | tf_op jit(solution)/shard_map/ppermute | solution.py:285
  232.6 3.3 %collective-permute-done.32 = bf16[128,2048]{1,0:T(8,128)(2,1)S(1)} collective-permute-done((bf16[128,2048]{1,0:T(8,128)(2,1)S(1)}, bf16[128,2048]{1,0:T(8,128)(2,1)S(1)}, u32[]{:S(2)}, u32[]{:S(2)}) %collective-permute-start.32) | collective-permute-done | bytes 524320 | tf_op jit(solution)/shard_map/ppermute | solution.py:286
  236.2 2.8 collective-permute-start.30
  240.3 1.3 collective-permute-start.33
  242.3 4.6 %collective-permute-start.38 = (bf16[128,1024]{1,0:T(8,128)(2,1)S(1)}, bf16[128,1024]{1,0:T(8,128)(2,1)S(1)}, u32[]{:S(2)}, u32[]{:S(2)}) collective-permute-start(bf16[128,1024]{1,0:T(8,128)(2,1)S(1)} %get-tuple-element.68), channel_id=1, source_target_pairs={{0,1},{1,2},{2,3},{4,5},{5,6},{6,7},{8,9},{9,10},{10,11},{12,13},{... | collective-permute-start | bytes 786440 | tf_op jit(solution)/shard_map/ppermute | solution.py:285
  246.9 1.3 collective-permute-start.41
  249.1 4.7 %collective-permute-start.31 = (bf16[128,2048]{1,0:T(8,128)(2,1)S(1)}, bf16[128,2048]{1,0:T(8,128)(2,1)S(1)}, u32[]{:S(2)}, u32[]{:S(2)}) collective-permute-start(bf16[128,2048]{1,0:T(8,128)(2,1)S(1)} %add_convert_fusion.1), channel_id=1, source_target_pairs={{0,1},{1,2},{2,3},{4,5},{5,6},{6,7},{8,9},{9,10},{10,11},{12,13},{... | collective-permute-start | bytes 1572872 | tf_op jit(solution)/shard_map/ppermute | solution.py:285
  254.4 5.9 %collective-permute-done.41 = bf16[128,1024]{1,0:T(8,128)(2,1)S(1)} collective-permute-done((bf16[128,1024]{1,0:T(8,128)(2,1)S(1)}, bf16[128,1024]{1,0:T(8,128)(2,1)S(1)}, u32[]{:S(2)}, u32[]{:S(2)}) %collective-permute-start.41) | collective-permute-done | bytes 262176 | tf_op jit(solution)/shard_map/ppermute | solution.py:286
  260.5 2.8 collective-permute-start.39
  263.4 1.3 collective-permute-start.34
  264.7 1.3 collective-permute-start.42
  266.3 3.3 %collective-permute-done.39 = bf16[128,1024]{1,0:T(8,128)(2,1)S(1)} collective-permute-done((bf16[128,1024]{1,0:T(8,128)(2,1)S(1)}, bf16[128,1024]{1,0:T(8,128)(2,1)S(1)}, u32[]{:S(2)}, u32[]{:S(2)}) %collective-permute-start.39) | collective-permute-done | bytes 262176 | tf_op jit(solution)/shard_map/ppermute | solution.py:285
  269.7 4.4 %collective-permute-start.40 = (bf16[128,1024]{1,0:T(8,128)(2,1)S(1)}, bf16[128,1024]{1,0:T(8,128)(2,1)S(1)}, u32[]{:S(2)}, u32[]{:S(2)}) collective-permute-start(bf16[128,1024]{1,0:T(8,128)(2,1)S(1)} %add_convert_fusion.3), channel_id=1, source_target_pairs={{0,1},{1,2},{2,3},{4,5},{5,6},{6,7},{8,9},{9,10},{10,11},{12,13},{... | collective-permute-start | bytes 786440 | tf_op jit(solution)/shard_map/ppermute | solution.py:285
  274.1 8.1 %collective-permute-done.42 = bf16[128,1024]{1,0:T(8,128)(2,1)S(1)} collective-permute-done((bf16[128,1024]{1,0:T(8,128)(2,1)S(1)}, bf16[128,1024]{1,0:T(8,128)(2,1)S(1)}, u32[]{:S(2)}, u32[]{:S(2)}) %collective-permute-start.42) | collective-permute-done | bytes 262176 | tf_op jit(solution)/shard_map/ppermute | solution.py:286
  282.4 1.3 collective-permute-start.43
  284.4 6.3 %collective-permute-done.43 = bf16[128,1024]{1,0:T(8,128)(2,1)S(1)} collective-permute-done((bf16[128,1024]{1,0:T(8,128)(2,1)S(1)}, bf16[128,1024]{1,0:T(8,128)(2,1)S(1)}, u32[]{:S(2)}, u32[]{:S(2)}) %collective-permute-start.43) | collective-permute-done | bytes 262176 | tf_op jit(solution)/shard_map/ppermute | solution.py:286
  (157 shorter events, 35.5 us)
Async XLA Ops:
  6.5 136.4 %copy-start = (f32[7,64]{1,0:T(8,128)S(1)}, f32[7,64]{1,0:T(8,128)}, u32[]{:S(2)}) copy-start(f32[7,64]{1,0:T(8,128)} %param.9) | copy-start | bytes 5380
  6.5 101.1 %all-gather.2.cloned.1.call-start = ((), (), s32[]{:S(2)}) async-start(), calls=%async_computation | async-start | bytes 5242880 | tf_op jit(solution)/shard_map/all_gather | solution.py:220
  8.3 7.4 %copy-start.18 = (bf16[2,512,512]{2,1,0:T(8,128)(2,1)}, bf16[2,512,512]{2,1,0:T(8,128)(2,1)S(1)}, u32[]{:S(2)}) copy-start(bf16[2,512,512]{2,1,0:T(8,128)(2,1)S(1)} %get-tuple-element.69.refs_0_) | copy-start | bytes 3145732
  10.0 3.1 %collective-permute-start.2 = (bf16[2,512,512]{2,1,0:T(8,128)(2,1)S(1)}, bf16[2,512,512]{2,1,0:T(8,128)(2,1)S(1)}, u32[]{:S(2)}, u32[]{:S(2)}) collective-permute-start(bf16[2,512,512]{2,1,0:T(8,128)(2,1)S(1)} %get-tuple-element.70), channel_id=1, source_target_pairs={{0,4},{4,0},{8,12},{12,8},{16,20},{20,16},{24,28},{28,24},{1,5},{5... | collective-permute-start | bytes 3145736 | tf_op jit(solution)/shard_map/ppermute | solution.py:182
  10.6 26.6 %collective-permute-start.1 = (bf16[2,512,512]{2,1,0:T(8,128)(2,1)S(1)}, bf16[2,512,512]{2,1,0:T(8,128)(2,1)S(1)}, u32[]{:S(2)}, u32[]{:S(2)}) collective-permute-start(bf16[2,512,512]{2,1,0:T(8,128)(2,1)S(1)} %get-tuple-element.69.refs_0_), channel_id=1, source_target_pairs={{8,0},{12,4},{0,8},{4,12},{24,16},{28,20},{16,24},{20,28},{9,1},{1... | collective-permute-start | bytes 3145736 | tf_op jit(solution)/shard_map/ppermute | solution.py:179
  13.1 93.5 %copy-start.24 = (bf16[2,512,512]{2,1,0:T(8,128)(2,1)}, bf16[2,512,512]{2,1,0:T(8,128)(2,1)S(1)}, u32[]{:S(2)}) copy-start(bf16[2,512,512]{2,1,0:T(8,128)(2,1)S(1)} %collective-permute-done.2.refs_1_) | copy-start | bytes 3145732
  13.1 27.3 %collective-permute-start.5 = (bf16[2,512,512]{2,1,0:T(8,128)(2,1)S(1)}, bf16[2,512,512]{2,1,0:T(8,128)(2,1)S(1)}, u32[]{:S(2)}, u32[]{:S(2)}) collective-permute-start(bf16[2,512,512]{2,1,0:T(8,128)(2,1)S(1)} %collective-permute-done.2.refs_1_), channel_id=1, source_target_pairs={{16,0},{20,4},{24,8},{28,12},{0,16},{4,20},{8,24},{12,28},{17,1},{... | collective-permute-start | bytes 3145736 | tf_op jit(solution)/shard_map/ppermute | solution.py:179
  15.7 46.4 %collective-permute-start.4 = (bf16[2,512,512]{2,1,0:T(8,128)(2,1)S(1)}, bf16[2,512,512]{2,1,0:T(8,128)(2,1)S(1)}, u32[]{:S(2)}, u32[]{:S(2)}) collective-permute-start(bf16[2,512,512]{2,1,0:T(8,128)(2,1)S(1)} %get-tuple-element.69.refs_0_), channel_id=1, source_target_pairs={{16,0},{20,4},{24,8},{28,12},{0,16},{4,20},{8,24},{12,28},{17,1},{... | collective-permute-start | bytes 3145736 | tf_op jit(solution)/shard_map/ppermute | solution.py:179
  15.8 47.3 %collective-permute-start.3 = (bf16[2,512,512]{2,1,0:T(8,128)(2,1)S(1)}, bf16[2,512,512]{2,1,0:T(8,128)(2,1)S(1)}, u32[]{:S(2)}, u32[]{:S(2)}) collective-permute-start(bf16[2,512,512]{2,1,0:T(8,128)(2,1)S(1)} %collective-permute-done.2.refs_1_), channel_id=1, source_target_pairs={{8,0},{12,4},{0,8},{4,12},{24,16},{28,20},{16,24},{20,28},{9,1},{1... | collective-permute-start | bytes 3145736 | tf_op jit(solution)/shard_map/ppermute | solution.py:179
  37.1 69.5 %copy-start.26 = (bf16[2,512,512]{2,1,0:T(8,128)(2,1)}, bf16[2,512,512]{2,1,0:T(8,128)(2,1)S(1)}, u32[]{:S(2)}) copy-start(bf16[2,512,512]{2,1,0:T(8,128)(2,1)S(1)} %collective-permute-done.1.refs_2_) | copy-start | bytes 3145732
  37.1 47.5 %collective-permute-start.10 = (bf16[2,512,512]{2,1,0:T(8,128)(2,1)S(1)}, bf16[2,512,512]{2,1,0:T(8,128)(2,1)S(1)}, u32[]{:S(2)}, u32[]{:S(2)}) collective-permute-start(bf16[2,512,512]{2,1,0:T(8,128)(2,1)S(1)} %collective-permute-done.1.refs_2_), channel_id=1, source_target_pairs={{16,0},{20,4},{24,8},{28,12},{0,16},{4,20},{8,24},{12,28},{17,1},{... | collective-permute-start | bytes 3145736 | tf_op jit(solution)/shard_map/ppermute | solution.py:179
  40.4 2.6 collective-permute-start
  40.5 66.1 %collective-permute-start.11 = (bf16[2,512,512]{2,1,0:T(8,128)(2,1)S(1)}, bf16[2,512,512]{2,1,0:T(8,128)(2,1)S(1)}, u32[]{:S(2)}, u32[]{:S(2)}) collective-permute-start(bf16[2,512,512]{2,1,0:T(8,128)(2,1)S(1)} %collective-permute-done.5.refs_5_), channel_id=1, source_target_pairs={{8,0},{12,4},{0,8},{4,12},{24,16},{28,20},{16,24},{20,28},{9,1},{1... | collective-permute-start | bytes 3145736 | tf_op jit(solution)/shard_map/ppermute | solution.py:179
  64.1 29.2 %collective-permute-start.6 = (bf16[512,512]{1,0:T(8,128)(2,1)S(1)}, bf16[512,512]{1,0:T(8,128)(2,1)S(1)}, u32[]{:S(2)}, u32[]{:S(2)}) collective-permute-start(bf16[512,512]{1,0:T(8,128)(2,1)S(1)} %get-tuple-element.44.refs_0_), channel_id=1, source_target_pairs={{8,0},{12,4},{0,8},{4,12},{24,16},{28,20},{16,24},{20,28},{9,1},{1... | collective-permute-start | bytes 1572872 | tf_op jit(solution)/shard_map/ppermute | solution.py:179
  66.1 39.0 %collective-permute-start.8 = (bf16[512,512]{1,0:T(8,128)(2,1)S(1)}, bf16[512,512]{1,0:T(8,128)(2,1)S(1)}, u32[]{:S(2)}, u32[]{:S(2)}) collective-permute-start(bf16[512,512]{1,0:T(8,128)(2,1)S(1)} %get-tuple-element.44.refs_0_), channel_id=1, source_target_pairs={{16,0},{20,4},{24,8},{28,12},{0,16},{4,20},{8,24},{12,28},{17,1},{... | collective-permute-start | bytes 1572872 | tf_op jit(solution)/shard_map/ppermute | solution.py:179
  67.7 36.6 %collective-permute-start.7 = (bf16[512,512]{1,0:T(8,128)(2,1)S(1)}, bf16[512,512]{1,0:T(8,128)(2,1)S(1)}, u32[]{:S(2)}, u32[]{:S(2)}) collective-permute-start(bf16[512,512]{1,0:T(8,128)(2,1)S(1)} %collective-permute-done.refs_1_), channel_id=1, source_target_pairs={{8,0},{12,4},{0,8},{4,12},{24,16},{28,20},{16,24},{20,28},{9,1},{1... | collective-permute-start | bytes 1572872 | tf_op jit(solution)/shard_map/ppermute | solution.py:179
  85.6 21.0 %collective-permute-start.9 = (bf16[512,512]{1,0:T(8,128)(2,1)S(1)}, bf16[512,512]{1,0:T(8,128)(2,1)S(1)}, u32[]{:S(2)}, u32[]{:S(2)}) collective-permute-start(bf16[512,512]{1,0:T(8,128)(2,1)S(1)} %collective-permute-done.refs_1_), channel_id=1, source_target_pairs={{16,0},{20,4},{24,8},{28,12},{0,16},{4,20},{8,24},{12,28},{17,1},{... | collective-permute-start | bytes 1572872 | tf_op jit(solution)/shard_map/ppermute | solution.py:179
  105.1 42.7 %copy-start.4 = (bf16[512,512]{1,0:T(8,128)(2,1)}, bf16[512,512]{1,0:T(8,128)(2,1)S(1)}, u32[]{:S(2)}) copy-start(bf16[512,512]{1,0:T(8,128)(2,1)S(1)} %collective-permute-done.8.refs_4_) | copy-start | bytes 1572868
  106.6 24.8 %copy-start.8 = (bf16[512,512]{1,0:T(8,128)(2,1)}, bf16[512,512]{1,0:T(8,128)(2,1)S(1)}, u32[]{:S(2)}) copy-start(bf16[512,512]{1,0:T(8,128)(2,1)S(1)} %collective-permute-done.9.refs_5_) | copy-start | bytes 1572868
  107.6 23.8 %collective-permute-start.12 = (bf16[512,4096]{1,0:T(8,128)(2,1)}, bf16[512,4096]{1,0:T(8,128)(2,1)}, u32[]{:S(2)}, u32[]{:S(2)}) collective-permute-start(bf16[512,4096]{1,0:T(8,128)(2,1)} %all-gather.2.cloned.1.call-done.x_ref), channel_id=1, source_target_pairs={{0,4},{4,0},{8,12},{12,8},{16,20},{20,16},{24,28},{28,24},{1,5},{5... | collective-permute-start | bytes 12582920 | tf_op jit(solution)/shard_map/ppermute | solution.py:182
  109.7 33.5 %collective-permute-start.16 = (bf16[512,512]{1,0:T(8,128)(2,1)}, bf16[512,512]{1,0:T(8,128)(2,1)}, u32[]{:S(2)}, u32[]{:S(2)}) collective-permute-start(bf16[512,512]{1,0:T(8,128)(2,1)} %get-tuple-element.79), channel_id=1, source_target_pairs={{0,4},{4,0},{8,12},{12,8},{16,20},{20,16},{24,28},{28,24},{1,5},{5... | collective-permute-start | bytes 1572872 | tf_op jit(solution)/shard_map/ppermute | solution.py:182
  110.3 32.9 %collective-permute-start.14 = (bf16[512,512]{1,0:T(8,128)(2,1)S(1)}, bf16[512,512]{1,0:T(8,128)(2,1)}, u32[]{:S(2)}, u32[]{:S(2)}) collective-permute-start(bf16[512,512]{1,0:T(8,128)(2,1)S(1)} %collective-permute-done.6.refs_2_), channel_id=1, source_target_pairs={{16,0},{20,4},{24,8},{28,12},{0,16},{4,20},{8,24},{12,28},{17,1},{... | collective-permute-start | bytes 1572872 | tf_op jit(solution)/shard_map/ppermute | solution.py:179
  112.0 31.2 %collective-permute-start.15 = (bf16[512,512]{1,0:T(8,128)(2,1)S(1)}, bf16[512,512]{1,0:T(8,128)(2,1)}, u32[]{:S(2)}, u32[]{:S(2)}) collective-permute-start(bf16[512,512]{1,0:T(8,128)(2,1)S(1)} %collective-permute-done.9.refs_5_), channel_id=1, source_target_pairs={{8,0},{12,4},{0,8},{4,12},{24,16},{28,20},{16,24},{20,28},{9,1},{1... | collective-permute-start | bytes 1572872 | tf_op jit(solution)/shard_map/ppermute | solution.py:179
  131.4 7.9 %copy-start.14 = (f32[512,512]{1,0:T(8,128)}, f32[512,512]{1,0:T(8,128)S(1)}, u32[]{:S(2)}) copy-start(f32[512,512]{1,0:T(8,128)S(1)} %shard_map.64.product_ref) | copy-start | bytes 3145732
  140.3 3.9 %collective-permute-start.13 = (f32[8,512]{1,0:T(8,128)S(1)}, f32[8,512]{1,0:T(8,128)S(1)}, u32[]{:S(2)}, u32[]{:S(2)}) collective-permute-start(f32[8,512]{1,0:T(8,128)S(1)} %slice_select_fusion.3), channel_id=1, source_target_pairs={{0,8},{4,12},{8,16},{12,20},{16,24},{20,28},{1,9},{5,13},{9,17},{1... | collective-permute-start | bytes 49160 | tf_op jit(solution)/shard_map/ppermute | solution.py:254
  149.9 13.0 %copy-start.15 = (f32[512,512]{1,0:T(8,128)S(1)}, f32[512,512]{1,0:T(8,128)}, u32[]{:S(2)}) copy-start(f32[512,512]{1,0:T(8,128)} %copy-done.14) | copy-start | bytes 3145732
  155.6 9.0 %copy-start.3 = (bf16[512,4096]{1,0:T(8,128)(2,1)S(1)}, bf16[512,4096]{1,0:T(8,128)(2,1)}, u32[]{:S(2)}) copy-start(bf16[512,4096]{1,0:T(8,128)(2,1)} %all-gather.2.cloned.1.call-done.x_ref) | copy-start | bytes 12582916
  155.6 9.0 %copy-start.5 = (bf16[512,512]{1,0:T(8,128)(2,1)S(1)}, bf16[512,512]{1,0:T(8,128)(2,1)}, u32[]{:S(2)}) copy-start(bf16[512,512]{1,0:T(8,128)(2,1)} %copy-done.4) | copy-start | bytes 1572868
  157.5 11.4 %collective-permute-start.17 = (bf16[512,1024]{1,0:T(8,128)(2,1)S(1)}, bf16[512,1024]{1,0:T(8,128)(2,1)S(1)}, u32[]{:S(2)}, u32[]{:S(2)}) collective-permute-start(bf16[512,1024]{1,0:T(8,128)(2,1)S(1)} %shard_map.70), channel_id=1, source_target_pairs={{0,4},{4,0},{8,12},{12,8},{16,20},{20,16},{24,28},{28,24},{1,5},{5... | collective-permute-start | bytes 3145736 | tf_op jit(solution)/shard_map/ppermute | solution.py:182
  157.6 15.2 %collective-permute-start.24 = (bf16[512,512]{1,0:T(8,128)(2,1)S(1)}, bf16[512,512]{1,0:T(8,128)(2,1)}, u32[]{:S(2)}, u32[]{:S(2)}) collective-permute-start(bf16[512,512]{1,0:T(8,128)(2,1)S(1)} %get-tuple-element.51.refs_1_.refs_0_), channel_id=1, source_target_pairs={{8,0},{12,4},{0,8},{4,12},{24,16},{28,20},{16,24},{20,28},{9,1},{1... | collective-permute-start | bytes 1572872 | tf_op jit(solution)/shard_map/ppermute | solution.py:179
  160.0 23.8 %collective-permute-start.25 = (bf16[512,512]{1,0:T(8,128)(2,1)}, bf16[512,512]{1,0:T(8,128)(2,1)S(1)}, u32[]{:S(2)}, u32[]{:S(2)}) collective-permute-start(bf16[512,512]{1,0:T(8,128)(2,1)} %collective-permute-done.16.refs_0_.refs_1_), channel_id=1, source_target_pairs={{8,0},{12,4},{0,8},{4,12},{24,16},{28,20},{16,24},{20,28},{9,1},{1... | collective-permute-start | bytes 1572872 | tf_op jit(solution)/shard_map/ppermute | solution.py:179
  160.0 23.7 %collective-permute-start.26 = (bf16[512,512]{1,0:T(8,128)(2,1)S(1)}, bf16[512,512]{1,0:T(8,128)(2,1)S(1)}, u32[]{:S(2)}, u32[]{:S(2)}) collective-permute-start(bf16[512,512]{1,0:T(8,128)(2,1)S(1)} %get-tuple-element.51.refs_1_.refs_0_), channel_id=1, source_target_pairs={{16,0},{20,4},{24,8},{28,12},{0,16},{4,20},{8,24},{12,28},{17,1},{... | collective-permute-start | bytes 1572872 | tf_op jit(solution)/shard_map/ppermute | solution.py:179
  162.9 23.3 %collective-permute-start.27 = (bf16[512,512]{1,0:T(8,128)(2,1)}, bf16[512,512]{1,0:T(8,128)(2,1)}, u32[]{:S(2)}, u32[]{:S(2)}) collective-permute-start(bf16[512,512]{1,0:T(8,128)(2,1)} %collective-permute-done.16.refs_0_.refs_1_), channel_id=1, source_target_pairs={{16,0},{20,4},{24,8},{28,12},{0,16},{4,20},{8,24},{12,28},{17,1},{... | collective-permute-start | bytes 1572872 | tf_op jit(solution)/shard_map/ppermute | solution.py:179
  170.7 19.3 %copy-start.20 = (bf16[128,1024]{1,0:T(8,128)(2,1)}, bf16[128,1024]{1,0:T(8,128)(2,1)S(1)}, u32[]{:S(2)}) copy-start(bf16[128,1024]{1,0:T(8,128)(2,1)S(1)} %get-tuple-element.56) | copy-start | bytes 786436
  170.7 22.8 %copy-start.22 = (bf16[128,1024]{1,0:T(8,128)(2,1)}, bf16[128,1024]{1,0:T(8,128)(2,1)S(1)}, u32[]{:S(2)}) copy-start(bf16[128,1024]{1,0:T(8,128)(2,1)S(1)} %get-tuple-element.54) | copy-start | bytes 786436
  183.7 6.3 %copy-start.10 = (bf16[512,512]{1,0:T(8,128)(2,1)}, bf16[512,512]{1,0:T(8,128)(2,1)S(1)}, u32[]{:S(2)}) copy-start(bf16[512,512]{1,0:T(8,128)(2,1)S(1)} %collective-permute-done.25.refs_0_.refs_1_) | copy-start | bytes 1572868
  183.7 6.3 %copy-start.12 = (bf16[512,512]{1,0:T(8,128)(2,1)}, bf16[512,512]{1,0:T(8,128)(2,1)S(1)}, u32[]{:S(2)}) copy-start(bf16[512,512]{1,0:T(8,128)(2,1)S(1)} %collective-permute-done.26.refs_3_.refs_2_) | copy-start | bytes 1572868
  190.0 20.2 %collective-permute-start.28 = (bf16[512,2048]{1,0:T(8,128)(2,1)}, bf16[512,2048]{1,0:T(8,128)(2,1)}, u32[]{:S(2)}, u32[]{:S(2)}) collective-permute-start(bf16[512,2048]{1,0:T(8,128)(2,1)} %shard_map.72), channel_id=1, source_target_pairs={{0,4},{4,0},{8,12},{12,8},{16,20},{20,16},{24,28},{28,24},{1,5},{5... | collective-permute-start | bytes 6291464 | tf_op jit(solution)/shard_map/ppermute | solution.py:182
  190.0 9.7 %collective-permute-start.18 = (bf16[128,1024]{1,0:T(8,128)(2,1)S(1)}, bf16[128,1024]{1,0:T(8,128)(2,1)S(1)}, u32[]{:S(2)}, u32[]{:S(2)}) collective-permute-start(bf16[128,1024]{1,0:T(8,128)(2,1)S(1)} %get-tuple-element.56), channel_id=1, source_target_pairs={{0,1},{1,2},{2,3},{4,5},{5,6},{6,7},{8,9},{9,10},{10,11},{12,13},{... | collective-permute-start | bytes 786440 | tf_op jit(solution)/shard_map/ppermute | solution.py:285
  193.5 10.3 %collective-permute-start.21 = (bf16[128,1024]{1,0:T(8,128)(2,1)S(1)}, bf16[128,1024]{1,0:T(8,128)(2,1)S(1)}, u32[]{:S(2)}, u32[]{:S(2)}) collective-permute-start(bf16[128,1024]{1,0:T(8,128)(2,1)S(1)} %get-tuple-element.54), channel_id=1, source_target_pairs={{1,0},{2,1},{3,2},{5,4},{6,5},{7,6},{9,8},{10,9},{11,10},{13,12},{... | collective-permute-start | bytes 786440 | tf_op jit(solution)/shard_map/ppermute | solution.py:286
  194.8 27.8 %collective-permute-start.35 = (bf16[512,512]{1,0:T(8,128)(2,1)}, bf16[512,512]{1,0:T(8,128)(2,1)S(1)}, u32[]{:S(2)}, u32[]{:S(2)}) collective-permute-start(bf16[512,512]{1,0:T(8,128)(2,1)} %collective-permute-done.24.refs_1_.refs_0_), channel_id=1, source_target_pairs={{16,0},{20,4},{24,8},{28,12},{0,16},{4,20},{8,24},{12,28},{17,1},{... | collective-permute-start | bytes 1572872 | tf_op jit(solution)/shard_map/ppermute | solution.py:179
  196.6 30.6 %collective-permute-start.36 = (bf16[512,512]{1,0:T(8,128)(2,1)}, bf16[512,512]{1,0:T(8,128)(2,1)S(1)}, u32[]{:S(2)}, u32[]{:S(2)}) collective-permute-start(bf16[512,512]{1,0:T(8,128)(2,1)} %collective-permute-done.27.refs_2_.refs_3_), channel_id=1, source_target_pairs={{8,0},{12,4},{0,8},{4,12},{24,16},{28,20},{16,24},{20,28},{9,1},{1... | collective-permute-start | bytes 1572872 | tf_op jit(solution)/shard_map/ppermute | solution.py:179
  204.7 15.5 %collective-permute-start.19 = (bf16[128,1024]{1,0:T(8,128)(2,1)}, bf16[128,1024]{1,0:T(8,128)(2,1)}, u32[]{:S(2)}, u32[]{:S(2)}) collective-permute-start(bf16[128,1024]{1,0:T(8,128)(2,1)} %get-tuple-element.89), channel_id=1, source_target_pairs={{0,1},{1,2},{2,3},{4,5},{5,6},{6,7},{8,9},{9,10},{10,11},{12,13},{... | collective-permute-start | bytes 786440 | tf_op jit(solution)/shard_map/ppermute | solution.py:285
  208.9 19.1 %collective-permute-start.22 = (bf16[128,1024]{1,0:T(8,128)(2,1)S(1)}, bf16[128,1024]{1,0:T(8,128)(2,1)S(1)}, u32[]{:S(2)}, u32[]{:S(2)}) collective-permute-start(bf16[128,1024]{1,0:T(8,128)(2,1)S(1)} %get-tuple-element.90), channel_id=1, source_target_pairs={{1,0},{2,1},{3,2},{5,4},{6,5},{7,6},{9,8},{10,9},{11,10},{13,12},{... | collective-permute-start | bytes 786440 | tf_op jit(solution)/shard_map/ppermute | solution.py:286
  212.2 9.3 %copy-start.23 = (bf16[128,1024]{1,0:T(8,128)(2,1)S(1)}, bf16[128,1024]{1,0:T(8,128)(2,1)}, u32[]{:S(2)}) copy-start(bf16[128,1024]{1,0:T(8,128)(2,1)} %copy-done.22) | copy-start | bytes 786436
  215.5 12.5 %copy-start.21 = (bf16[128,1024]{1,0:T(8,128)(2,1)S(1)}, bf16[128,1024]{1,0:T(8,128)(2,1)}, u32[]{:S(2)}) copy-start(bf16[128,1024]{1,0:T(8,128)(2,1)} %copy-done.20) | copy-start | bytes 786436
  215.5 17.1 %collective-permute-start.29 = (bf16[128,2048]{1,0:T(8,128)(2,1)S(1)}, bf16[128,2048]{1,0:T(8,128)(2,1)S(1)}, u32[]{:S(2)}, u32[]{:S(2)}) collective-permute-start(bf16[128,2048]{1,0:T(8,128)(2,1)S(1)} %get-tuple-element.62), channel_id=1, source_target_pairs={{0,1},{1,2},{2,3},{4,5},{5,6},{6,7},{8,9},{9,10},{10,11},{12,13},{... | collective-permute-start | bytes 1572872 | tf_op jit(solution)/shard_map/ppermute | solution.py:285
  220.2 15.7 %collective-permute-start.32 = (bf16[128,2048]{1,0:T(8,128)(2,1)S(1)}, bf16[128,2048]{1,0:T(8,128)(2,1)S(1)}, u32[]{:S(2)}, u32[]{:S(2)}) collective-permute-start(bf16[128,2048]{1,0:T(8,128)(2,1)S(1)} %get-tuple-element.60), channel_id=1, source_target_pairs={{1,0},{2,1},{3,2},{5,4},{6,5},{7,6},{9,8},{10,9},{11,10},{13,12},{... | collective-permute-start | bytes 1572872 | tf_op jit(solution)/shard_map/ppermute | solution.py:286
  222.6 16.5 %collective-permute-start.20 = (bf16[128,1024]{1,0:T(8,128)(2,1)S(1)}, bf16[128,1024]{1,0:T(8,128)(2,1)S(1)}, u32[]{:S(2)}, u32[]{:S(2)}) collective-permute-start(bf16[128,1024]{1,0:T(8,128)(2,1)S(1)} %add_convert_fusion.5), channel_id=1, source_target_pairs={{0,1},{1,2},{2,3},{4,5},{5,6},{6,7},{8,9},{9,10},{10,11},{12,13},{... | collective-permute-start | bytes 786440 | tf_op jit(solution)/shard_map/ppermute | solution.py:285
  227.9 13.7 %collective-permute-start.37 = (bf16[512,1024]{1,0:T(8,128)(2,1)S(1)}, bf16[512,1024]{1,0:T(8,128)(2,1)S(1)}, u32[]{:S(2)}, u32[]{:S(2)}) collective-permute-start(bf16[512,1024]{1,0:T(8,128)(2,1)S(1)} %shard_map.74), channel_id=1, source_target_pairs={{0,4},{4,0},{8,12},{12,8},{16,20},{20,16},{24,28},{28,24},{1,5},{5... | collective-permute-start | bytes 3145736 | tf_op jit(solution)/shard_map/ppermute | solution.py:182
  228.1 12.0 %collective-permute-start.23 = (bf16[128,1024]{1,0:T(8,128)(2,1)S(1)}, bf16[128,1024]{1,0:T(8,128)(2,1)S(1)}, u32[]{:S(2)}, u32[]{:S(2)}) collective-permute-start(bf16[128,1024]{1,0:T(8,128)(2,1)S(1)} %add_convert_fusion.4), channel_id=1, source_target_pairs={{1,0},{2,1},{3,2},{5,4},{6,5},{7,6},{9,8},{10,9},{11,10},{13,12},{... | collective-permute-start | bytes 786440 | tf_op jit(solution)/shard_map/ppermute | solution.py:286
  236.2 12.7 %collective-permute-start.30 = (bf16[128,2048]{1,0:T(8,128)(2,1)S(1)}, bf16[128,2048]{1,0:T(8,128)(2,1)S(1)}, u32[]{:S(2)}, u32[]{:S(2)}) collective-permute-start(bf16[128,2048]{1,0:T(8,128)(2,1)S(1)} %get-tuple-element.83), channel_id=1, source_target_pairs={{0,1},{1,2},{2,3},{4,5},{5,6},{6,7},{8,9},{9,10},{10,11},{12,13},{... | collective-permute-start | bytes 1572872 | tf_op jit(solution)/shard_map/ppermute | solution.py:285
  240.3 23.0 %collective-permute-start.33 = (bf16[128,2048]{1,0:T(8,128)(2,1)S(1)}, bf16[128,2048]{1,0:T(8,128)(2,1)S(1)}, u32[]{:S(2)}, u32[]{:S(2)}) collective-permute-start(bf16[128,2048]{1,0:T(8,128)(2,1)S(1)} %get-tuple-element.84), channel_id=1, source_target_pairs={{1,0},{2,1},{3,2},{5,4},{6,5},{7,6},{9,8},{10,9},{11,10},{13,12},{... | collective-permute-start | bytes 1572872 | tf_op jit(solution)/shard_map/ppermute | solution.py:286
  242.3 12.1 %collective-permute-start.38 = (bf16[128,1024]{1,0:T(8,128)(2,1)S(1)}, bf16[128,1024]{1,0:T(8,128)(2,1)S(1)}, u32[]{:S(2)}, u32[]{:S(2)}) collective-permute-start(bf16[128,1024]{1,0:T(8,128)(2,1)S(1)} %get-tuple-element.68), channel_id=1, source_target_pairs={{0,1},{1,2},{2,3},{4,5},{5,6},{6,7},{8,9},{9,10},{10,11},{12,13},{... | collective-permute-start | bytes 786440 | tf_op jit(solution)/shard_map/ppermute | solution.py:285
  246.9 13.5 %collective-permute-start.41 = (bf16[128,1024]{1,0:T(8,128)(2,1)S(1)}, bf16[128,1024]{1,0:T(8,128)(2,1)S(1)}, u32[]{:S(2)}, u32[]{:S(2)}) collective-permute-start(bf16[128,1024]{1,0:T(8,128)(2,1)S(1)} %get-tuple-element.66), channel_id=1, source_target_pairs={{1,0},{2,1},{3,2},{5,4},{6,5},{7,6},{9,8},{10,9},{11,10},{13,12},{... | collective-permute-start | bytes 786440 | tf_op jit(solution)/shard_map/ppermute | solution.py:286
  249.1 17.1 %copy-start.39 = (bf16[128,4096]{1,0:T(8,128)(2,1)S(1)}, bf16[128,4096]{1,0:T(8,128)(2,1)}, u32[]{:S(2)}) copy-start(bf16[128,4096]{1,0:T(8,128)(2,1)} %param.6) | copy-start | bytes 3145732
  249.1 17.1 %copy-start.40 = (s32[128,4096]{1,0:T(8,128)S(1)}, s32[128,4096]{1,0:T(8,128)}, u32[]{:S(2)}) copy-start(s32[128,4096]{1,0:T(8,128)} %param.11) | copy-start | bytes 6291460
  249.1 34.6 %collective-permute-start.31 = (bf16[128,2048]{1,0:T(8,128)(2,1)S(1)}, bf16[128,2048]{1,0:T(8,128)(2,1)S(1)}, u32[]{:S(2)}, u32[]{:S(2)}) collective-permute-start(bf16[128,2048]{1,0:T(8,128)(2,1)S(1)} %add_convert_fusion.1), channel_id=1, source_target_pairs={{0,1},{1,2},{2,3},{4,5},{5,6},{6,7},{8,9},{9,10},{10,11},{12,13},{... | collective-permute-start | bytes 1572872 | tf_op jit(solution)/shard_map/ppermute | solution.py:285
  260.5 9.2 %collective-permute-start.39 = (bf16[128,1024]{1,0:T(8,128)(2,1)S(1)}, bf16[128,1024]{1,0:T(8,128)(2,1)S(1)}, u32[]{:S(2)}, u32[]{:S(2)}) collective-permute-start(bf16[128,1024]{1,0:T(8,128)(2,1)S(1)} %get-tuple-element.87), channel_id=1, source_target_pairs={{0,1},{1,2},{2,3},{4,5},{5,6},{6,7},{8,9},{9,10},{10,11},{12,13},{... | collective-permute-start | bytes 786440 | tf_op jit(solution)/shard_map/ppermute | solution.py:285
  263.4 20.2 %collective-permute-start.34 = (bf16[128,2048]{1,0:T(8,128)(2,1)S(1)}, bf16[128,2048]{1,0:T(8,128)(2,1)S(1)}, u32[]{:S(2)}, u32[]{:S(2)}) collective-permute-start(bf16[128,2048]{1,0:T(8,128)(2,1)S(1)} %add_convert_fusion), channel_id=1, source_target_pairs={{1,0},{2,1},{3,2},{5,4},{6,5},{7,6},{9,8},{10,9},{11,10},{13,12},{... | collective-permute-start | bytes 1572872 | tf_op jit(solution)/shard_map/ppermute | solution.py:286
  264.7 17.5 %collective-permute-start.42 = (bf16[128,1024]{1,0:T(8,128)(2,1)S(1)}, bf16[128,1024]{1,0:T(8,128)(2,1)S(1)}, u32[]{:S(2)}, u32[]{:S(2)}) collective-permute-start(bf16[128,1024]{1,0:T(8,128)(2,1)S(1)} %get-tuple-element.88), channel_id=1, source_target_pairs={{1,0},{2,1},{3,2},{5,4},{6,5},{7,6},{9,8},{10,9},{11,10},{13,12},{... | collective-permute-start | bytes 786440 | tf_op jit(solution)/shard_map/ppermute | solution.py:286
  269.7 14.6 %collective-permute-start.40 = (bf16[128,1024]{1,0:T(8,128)(2,1)S(1)}, bf16[128,1024]{1,0:T(8,128)(2,1)S(1)}, u32[]{:S(2)}, u32[]{:S(2)}) collective-permute-start(bf16[128,1024]{1,0:T(8,128)(2,1)S(1)} %add_convert_fusion.3), channel_id=1, source_target_pairs={{0,1},{1,2},{2,3},{4,5},{5,6},{6,7},{8,9},{9,10},{10,11},{12,13},{... | collective-permute-start | bytes 786440 | tf_op jit(solution)/shard_map/ppermute | solution.py:285
  282.4 8.3 %collective-permute-start.43 = (bf16[128,1024]{1,0:T(8,128)(2,1)S(1)}, bf16[128,1024]{1,0:T(8,128)(2,1)S(1)}, u32[]{:S(2)}, u32[]{:S(2)}) collective-permute-start(bf16[128,1024]{1,0:T(8,128)(2,1)S(1)} %add_convert_fusion.2), channel_id=1, source_target_pairs={{1,0},{2,1},{3,2},{5,4},{6,5},{7,6},{9,8},{10,9},{11,10},{13,12},{... | collective-permute-start | bytes 786440 | tf_op jit(solution)/shard_map/ppermute | solution.py:286
  284.3 6.4 %copy-start.41 = (bf16[128,4096]{1,0:T(8,128)(2,1)}, bf16[128,4096]{1,0:T(8,128)(2,1)S(1)}, u32[]{:S(2)}) copy-start(bf16[128,4096]{1,0:T(8,128)(2,1)S(1)} %fusion.28) | copy-start | bytes 3145732
  (24 other events, 29.2 us)
Sparse Core Ops, SparseCore 0:
  10.2 83.4 all-gather.1

commit v3 on v2

--- a/solution.py
+++ b/solution.py
@@ -10,8 +10,7 @@
 
 F32 = jnp.float32
 BF16 = jnp.bfloat16
-MIB = 1 << 20
-WHOLE = pl.BlockSpec(memory_space=pltpu.VMEM)
+GRANT = 58 << 20
 
 
 def grid_of(chips):
@@ -19,13 +18,17 @@
     return ny, chips // ny
 
 
+def whole(array):
+    return pl.BlockSpec(array.shape, lambda *_: (0,) * len(array.shape))
+
+
 def dot(a, b):
     return jnp.dot(a, b, preferred_element_type=F32)
 
 
 def cost(flops, *arrays):
     moved = sum(math.prod(a.shape) * a.dtype.itemsize for a in arrays)
-    return pl.CostEstimate(flops=flops, bytes_accessed=moved, transcendentals=0)
+    return pl.CostEstimate(flops=1, bytes_accessed=1, transcendentals=0)
 
 
 def columns_of(x_ref, at_ref, index, deep):
@@ -44,13 +47,22 @@
     out_ref[...] = key.astype(BF16).astype(F32) * value.astype(BF16).astype(F32)
 
 
-def gate_kernel(at_ref, x_ref, filtered_ref, *refs):
+def query_kernel(at_ref, x_ref, *refs):
+    pairs, out_ref = refs[:-1], refs[-1]
+    deep = pairs[0].shape[1]
+    query = None
+    for index in range(2 * len(pairs)):
+        new = dot(columns_of(x_ref, at_ref, index, deep), pairs[index // 2][index % 2])
+        query = new if query is None else query + new
+    out_ref[...] = query
+
+
+def gate_kernel(at_ref, x_ref, filtered_ref, partial_ref, *refs):
     pieces, out_ref = refs[:-1], refs[-1]
     deep = pieces[0].shape[0]
-    query = None
+    query = partial_ref[...]
     for index, piece in enumerate(pieces):
-        new = dot(columns_of(x_ref, at_ref, index, deep), piece[...])
-        query = new if query is None else query + new
+        query = query + dot(columns_of(x_ref, at_ref, index, deep), piece[...])
     out_ref[...] = (query.astype(BF16).astype(F32) * filtered_ref[...]).astype(BF16)
 
 
@@ -76,7 +88,7 @@
             ],
             out_specs=by_tile,
         ),
-        compiler_params=pltpu.CompilerParams(vmem_limit_bytes=36 * MIB),
+        compiler_params=pltpu.CompilerParams(vmem_limit_bytes=GRANT),
         cost_estimate=cost(2 * count * length * model * half, x, out, *extra, *pieces),
     )(at, x, *extra, *pieces)
 
@@ -105,14 +117,14 @@
         ],
         out_specs=pl.BlockSpec((length, tile), lambda j: (0, j)),
         scratch_shapes=[pltpu.VMEM((pad + length, tile), F32)],
-        compiler_params=pltpu.CompilerParams(vmem_limit_bytes=16 * MIB),
+        compiler_params=pltpu.CompilerParams(vmem_limit_bytes=GRANT),
         cost_estimate=cost(14 * length * half, product, product),
     )(product, halo, taps)
 
 
-def terms_kernel(count, n_tp, z_ref, gated_ref, *refs):
-    pieces, refs = refs[:count], refs[count:]
-    given, outs, held = (refs[0], refs[1:-1], refs[-1]) if len(refs) > 2 else (None, refs[:1], refs[-1])
+def terms_kernel(count, order, n_tp, z_ref, gated_ref, *refs):
+    pairs, refs, held = refs[:count], refs[count:-1], refs[-1]
+    given, outs = (refs[0], refs[1:]) if len(refs) > 1 else (None, refs)
     length = gated_ref.shape[0]
     rows = length // n_tp
     for slot in range(n_tp):
@@ -120,10 +132,10 @@
         held[slot * rows : (slot + 1) * rows] = gated_ref[
             pl.ds(pl.multiple_of(owner * rows, rows), rows)
         ]
-    wide = pieces[0].shape[1]
-    for index, piece in enumerate(pieces):
+    wide = pairs[0].shape[2]
+    for index, (pair, side) in enumerate((p, s) for p in pairs for s in order):
         at = slice(index * wide, (index + 1) * wide)
-        total = dot(held[...], piece[...])
+        total = dot(held[...], pair[side])
         if given is None:
             outs[0][:, at] = total.astype(BF16)
         else:
@@ -132,24 +144,25 @@
                 outs[slot][:, at] = total[slot * rows : (slot + 1) * rows].astype(BF16)
 
 
-def terms(n_tp, z, gated, pieces, given=None):
+def terms(n_tp, z, gated, pairs, order, given=None):
     length, half = gated.shape
-    cols = len(pieces) * pieces[0].shape[1]
+    cols = len(pairs) * 2 * pairs[0].shape[2]
     if given is None:
         out = [jax.ShapeDtypeStruct((length, cols), BF16)]
     else:
         out = [jax.ShapeDtypeStruct((length // n_tp, cols), BF16)] * n_tp
     extra = [] if given is None else [given]
     result = pl.pallas_call(
-        functools.partial(terms_kernel, len(pieces), n_tp),
+        functools.partial(terms_kernel, len(pairs), order, n_tp),
         out_shape=out,
+        grid=(1,),
         in_specs=[pl.BlockSpec(memory_space=pltpu.SMEM)]
-        + [WHOLE] * (1 + len(pieces) + len(extra)),
-        out_specs=[WHOLE] * len(out),
+        + [whole(a) for a in (gated, *pairs, *extra)],
+        out_specs=[whole(a) for a in out],
         scratch_shapes=[pltpu.VMEM((length, half), BF16)],
-        compiler_params=pltpu.CompilerParams(vmem_limit_bytes=36 * MIB),
-        cost_estimate=cost(2 * length * half * cols, gated, *pieces, *extra, *out),
-    )(z, gated, *pieces, *extra)
+        compiler_params=pltpu.CompilerParams(vmem_limit_bytes=GRANT),
+        cost_estimate=cost(2 * length * half * cols, gated, *pairs, *extra, *out),
+    )(z, gated, *pairs, *extra)
     return result[0] if given is None else result
 
 
@@ -220,34 +233,38 @@
     own_rows = lax.all_gather(normed, "tp", axis=0, tiled=True)
     in_weight_then, out_weight_then, _ = lax.optimization_barrier((in_weight, out_weight, normed))
     mine_q = columns(in_weight_then, 0, 1, core)[0]
-    brought_q = from_partner(columns(in_weight_then, 0, 1, 1 - core)[0])
+    both_q = jnp.stack([mine_q, from_partner(columns(in_weight_then, 0, 1, 1 - core)[0])])
     mine_o = halves(out_weight_then, 0, core)
-    brought_o = from_partner(halves(out_weight_then, 0, 1 - core))
-
+    both_o = jnp.stack([mine_o, from_partner(halves(out_weight_then, 0, 1 - core))])
+
+    kv_x, kv_y, both_q = lax.optimization_barrier((kv_x, kv_y, both_q))
     kv_rest = onward(kv_x, kv_y)
-    mine_q, brought_q, _ = lax.optimization_barrier((mine_q, brought_q, (kv_x[1:], kv_y[1:])))
-    q_x, q_y = direct(mine_q, brought_q)
-    q_x, q_y, kv_rest = lax.optimization_barrier((q_x, q_y, kv_rest))
-    q_rest = onward(q_x, q_y)
-    mine_o, brought_o, _ = lax.optimization_barrier((mine_o, brought_o, q_rest))
-    o_x, o_y = direct(mine_o, brought_o)
-    o_rest = onward(o_x, o_y)
-
-    own_rows, _ = lax.optimization_barrier((own_rows, kv_rest))
-    other_rows = from_partner(own_rows)
+    q_x = {(0, dx): from_chip(both_q, 0, dx) for dx in range(1, nx)}
+    q_y = {(dy, 0): from_chip(both_q, dy, 0) for dy in range(1, ny)}
+    arrived = (kv_x, kv_y, kv_rest, q_x, q_y)
+    own_rows, arrived = lax.optimization_barrier((own_rows, arrived))
+    kv_x, kv_y, kv_rest, q_x, q_y = arrived
     kv = listed(kv_x, kv_y, kv_rest)
-    q = listed(q_x, q_y, q_rest)
     order = list(kv)
+    kv_pieces = [piece for key in order for piece in kv[key]]
     at = jnp.stack(
         [place(my_y + dy, my_x + dx, core ^ rc) * deep for dy, dx in order for rc in range(2)]
     ).astype(jnp.int32)
-    kv_pieces = [piece for key in order for piece in kv[key]]
-    q_pieces = [piece for key in order for piece in q[key]]
+    early = 2 * (ny + nx - 1)
+
+    other_rows = from_partner(own_rows)
+    own_product = project(product_kernel, at, own_rows, [], kv_pieces, F32)
+    q_rest = {
+        (dy, dx): (from_chip(q_x[0, dx][0], dy, 0), from_chip(q_y[dy, 0][1], 0, dx))
+        for dy, _ in q_y
+        for _, dx in q_x
+    }
+    q_pairs = {(0, 0): both_q, **q_x, **q_y}
+    q_early = [q_pairs[key] for key in order if key in q_pairs]
+    other_product = project(product_kernel, at, other_rows, [], kv_pieces, F32)
 
     reach = filters.shape[0] - 1
     pad = -(-reach // 8) * 8
-    own_product = project(product_kernel, at, own_rows, [], kv_pieces, F32)
-    other_product = project(product_kernel, at, other_rows, [], kv_pieces, F32)
     own_tail, other_tail = own_product[length - pad :], other_product[length - pad :]
     first_tail = jnp.where(core == 0, own_tail, other_tail)
     last_tail = jnp.where(core == 0, other_tail, own_tail)
@@ -256,14 +273,25 @@
         "seq",
         [(2 * i + c, 2 * i + 2 + c) for i in range(chips - 1) for c in range(2)],
     )
+    other_query = project(query_kernel, at, other_rows, [], q_early, F32)
+    own_query = project(query_kernel, at, own_rows, [], q_early, F32)
     groups = filters.shape[1] // 2
     taps = jnp.repeat(
         lax.dynamic_slice_in_dim(filters, core * groups, groups, axis=1), half // groups, axis=1
     )
     own_filtered = causal_filter(own_product, jnp.where(core == 0, rim, first_tail), taps)
     other_filtered = causal_filter(other_product, jnp.where(core == 0, first_tail, rim), taps)
-    other_gated = project(gate_kernel, at, other_rows, [other_filtered], q_pieces, BF16)
-    own_gated = project(gate_kernel, at, own_rows, [own_filtered], q_pieces, BF16)
+
+    ready = (own_filtered, other_filtered, own_query, other_query)
+    both_o, q_rest, ready = lax.optimization_barrier((both_o, q_rest, ready))
+    own_filtered, other_filtered, own_query, other_query = ready
+    o_x = {(0, dx): from_chip(both_o, 0, dx) for dx in range(1, nx)}
+    o_y = {(dy, 0): from_chip(both_o, dy, 0) for dy in range(1, ny)}
+    late = [piece for pair in q_rest.values() for piece in pair]
+    other_gated = project(
+        gate_kernel, at[early:], other_rows, [other_filtered, other_query], late, BF16
+    )
+    own_gated = project(gate_kernel, at[early:], own_rows, [own_filtered, own_query], late, BF16)
 
     position = lax.axis_index("tp")
     z = position.astype(jnp.int32).reshape(1)
@@ -274,23 +302,23 @@
         return (a.astype(F32) + b.astype(F32)).astype(BF16)
 
     def summed(pairs, own_gated, other_gated):
-        pieces = [piece for pair in pairs for piece in pair]
-        leaving = terms(n_tp, z, other_gated, [piece for pair in pairs for piece in pair[::-1]])
-        slots = terms(n_tp, z, own_gated, pieces, from_partner(leaving))
-        rising = falling = None
+        leaving = terms(n_tp, z, other_gated, pairs, (1, 0))
+        slots = terms(n_tp, z, own_gated, pairs, (0, 1), from_partner(leaving))
+        rising = falling = first = None
         for step in range(n_tp - 1):
             send_up, send_down = slots[n_tp - 1 - step], slots[step + 1]
             if step:
                 send_up, send_down = plus(send_up, rising), plus(send_down, falling)
             rising = lax.ppermute(send_up, "tp", up)
             falling = lax.ppermute(send_down, "tp", down)
-        return slots[0].astype(F32) + rising.astype(F32) + falling.astype(F32), slots[0]
-
-    groups_of = [[(0, 0)], [key for key in order if (key[0] == 0) != (key[1] == 0)], list(o_rest)]
-    out_pieces = listed(o_x, o_y, o_rest)
+            first = (rising, falling) if step == 0 else first
+        return slots[0].astype(F32) + rising.astype(F32) + falling.astype(F32), first
+
+    o_rest = {(dy, dx): from_chip(o_x[0, dx], dy, 0) for dy, _ in o_y for _, dx in o_x}
+    out_pairs = {(0, 0): both_o, **o_x, **o_y, **o_rest}
     result = jnp.zeros((rows, model), BF16)
-    for keys in groups_of:
-        mixed, done = summed([out_pieces[key] for key in keys], own_gated, other_gated)
+    for keys in ([(0, 0)], [*o_x, *o_y], list(o_rest)):
+        mixed, done = summed([out_pairs[key] for key in keys], own_gated, other_gated)
         own_gated, other_gated, _ = lax.optimization_barrier((own_gated, other_gated, done))
         for index, (dy, dx) in enumerate(keys):
             start = place(my_y + dy, my_x + dx, 0) * wide

time: 300 us -> 326 us (1.087)
  Pallas kernels: 39.2 us -> 73.4 us
  local copies, waits for them, and re-layouts: 30 us -> 15.4 us
  starting transfers between devices: 79.2 us -> 68.3 us
  waiting for transfers between devices: 129 us -> 138 us
  other arithmetic: 6.98 us -> 15.9 us
    pallas_call x4 -> x6, Pallas kernels: 23.8 us -> 44.7 us  [project(): pl.pallas_call(kernel, out_shape=out, grid_spec=pltpu.PrefetchScalarGridS...]
    unnamed x86 -> x80, local copies, waits for them, and re-layouts: 24.3 us -> 6.99 us
    ppermute x18 -> x13, starting transfers between devices: 27.5 us -> 14.9 us  [from_chip(): return lax.ppermute(block, 'seq', route)]
    pallas_call x6, Pallas kernels: 12.1 us -> 21.9 us  [terms(): pl.pallas_call(functools.partial(terms_kernel, len(pairs), order, n_tp),...]
    ppermute x9, waiting for transfers between devices: 10.7 us -> 19.6 us  [summed(): rising = lax.ppermute(send_up, 'tp', up)]
    ppermute x7, waiting for transfers between devices: 0.02 us -> 6.27 us  [from_partner(): return lax.ppermute(block, 'seq', [(s, s ^ 1) for s in range(n_seq)])]
    pallas_call x2, Pallas kernels: 3.33 us -> 6.77 us  [causal_filter(): pl.pallas_call(filter_kernel, out_shape=jax.ShapeDtypeStruct(product.shap...]
    ppermute x9, waiting for transfers between devices: 28.8 us -> 25.5 us  [summed(): falling = lax.ppermute(send_down, 'tp', down)]
  transfers between devices with their start and end apart: 45 -> 40, of which waited for: 21 -> 23; matrix products, arithmetic and copies ran while one was open for 3% -> 6% of each run, Pallas kernels for 9% -> 17%
where the time goes in v3:
time: 326 us; the launch traced here: 325 us
  waiting for transfers between devices  138 us (42%)
  Pallas kernels  73.4 us (23%)
  starting transfers between devices  68.3 us (21%)
  other arithmetic  15.9 us (5%)
  local copies, waits for them, and re-layouts  15.4 us (5%)
  between operations  14.1 us (4%)
    ppermute x13, waiting for transfers between devices, from_chip(): return lax.ppermute(block, 'seq', route)  86.5 us
    pallas_call x6, Pallas kernels, project(): pl.pallas_call(kernel, out_shape=out, grid_spec=pltpu.PrefetchScalarGridS...  44.7 us
    ppermute x9, starting transfers between devices, summed(): rising = lax.ppermute(send_up, 'tp', up)  37 us
    ppermute x9, waiting for transfers between devices, summed(): falling = lax.ppermute(send_down, 'tp', down)  25.5 us
    pallas_call x6, Pallas kernels, terms(): pl.pallas_call(functools.partial(terms_kernel, len(pairs), order, n_tp),...  21.9 us
    ppermute x9, waiting for transfers between devices, summed(): rising = lax.ppermute(send_up, 'tp', up)  19.6 us
    ppermute x13, starting transfers between devices, from_chip(): return lax.ppermute(block, 'seq', route)  14.9 us
    ppermute x9, starting transfers between devices, summed(): falling = lax.ppermute(send_down, 'tp', down)  12.3 us
  transfers between devices with their start and end apart: 40, of which 23 were waited for; matrix products, arithmetic and copies ran while one was open for 6% of the time, Pallas kernels for 17%

profile of v3, /device:TPU:0, one launch (start us, length us, event | category | flops | bytes accessed | tf_op | source)
XLA Modules:
  0.0 324.9 jit_solution(4860590254891155894)
XLA Ops:
  6.5 1.8 constant_dynamic-slice_fusion.3
  8.7 1.3 fusion.2
  10.6 2.6 collective-permute-start.1
  13.1 1.5 collective-permute-start.3
  15.7 1.5 collective-permute-start.4
  18.6 1.9 collective-permute-done.5
  20.6 16.5 %collective-permute-done.1.refs_2_ = bf16[2,512,512]{2,1,0:T(8,128)(2,1)S(1)} collective-permute-done((bf16[2,512,512]{2,1,0:T(8,128)(2,1)S(1)}, bf16[2,512,512]{2,1,0:T(8,128)(2,1)S(1)}, u32[]{:S(2)}, u32[]{:S(2)}) %collective-permute-start.1) | collective-permute-done | bytes 1048608 | tf_op jit(solution)/shard_map/ppermute | solution.py:192
  37.1 2.0 collective-permute-done.3.refs_4_
  39.1 20.2 %collective-permute-done.2.refs_3_ = bf16[2,512,512]{2,1,0:T(8,128)(2,1)S(1)} collective-permute-done((bf16[2,512,512]{2,1,0:T(8,128)(2,1)S(1)}, bf16[2,512,512]{2,1,0:T(8,128)(2,1)S(1)}, u32[]{:S(2)}, u32[]{:S(2)}) %collective-permute-start.2) | collective-permute-done | bytes 1048608 | tf_op jit(solution)/shard_map/ppermute | solution.py:192
  59.3 1.5 collective-permute-done.4.refs_5_
  60.8 1.5 collective-permute-start.6
  62.9 1.5 collective-permute-start.8
  64.9 22.0 %collective-permute-done.6.refs_6_ = bf16[2,512,512]{2,1,0:T(8,128)(2,1)S(1)} collective-permute-done((bf16[2,512,512]{2,1,0:T(8,128)(2,1)S(1)}, bf16[2,512,512]{2,1,0:T(8,128)(2,1)S(1)}, u32[]{:S(2)}, u32[]{:S(2)}) %collective-permute-start.6) | collective-permute-done | bytes 1048608 | tf_op jit(solution)/shard_map/ppermute | solution.py:192
  86.9 1.5 collective-permute-done.7.refs_7_
  88.4 20.6 %collective-permute-done.8.refs_1_ = bf16[2,512,512]{2,1,0:T(8,128)(2,1)S(1)} collective-permute-done((bf16[2,512,512]{2,1,0:T(8,128)(2,1)S(1)}, bf16[2,512,512]{2,1,0:T(8,128)(2,1)S(1)}, u32[]{:S(2)}, u32[]{:S(2)}) %collective-permute-start.8) | collective-permute-done | bytes 1048608 | tf_op jit(solution)/shard_map/ppermute | solution.py:192
  109.2 2.5 dynamic-slice_bitcast_fusion
  116.5 10.3 %shard_map.64.product_ref = f32[512,512]{1,0:T(8,128)} custom-call(s32[8]{0:T(128)} %stack.58.at_ref, bf16[512,4096]{1,0:T(8,128)(2,1)} %all-gather.2.cloned.1.call-done.x_ref, bf16[2,512,512]{2,1,0:T(8,128)(2,1)} %copy-done.5, bf16[2,512,512]{2,1,0:T(8,128)(2,1)} %copy-done.11, bf16[2,512,512]{2,1,0:T(8,128)(2,1)} %copy-done.12, ...), custom_call_target="tpu_custom_call" | custom-call | flops 1 | bytes 1 | tf_op jit(solution)/shard_map/pallas_call | solution.py:77
  126.8 10.5 %shard_map.65.product_ref = f32[512,512]{1,0:T(8,128)} custom-call(s32[8]{0:T(128)} %stack.58.at_ref, bf16[512,4096]{1,0:T(8,128)(2,1)} %collective-permute-done.13.x_ref, bf16[2,512,512]{2,1,0:T(8,128)(2,1)} %copy-done.5, bf16[2,512,512]{2,1,0:T(8,128)(2,1)} %copy-done.11, bf16[2,512,512]{2,1,0:T(8,128)(2,1)} %copy-done.12, ...), custom_call_target="tpu_custom_call" | custom-call | flops 1 | bytes 1 | tf_op jit(solution)/shard_map/pallas_call | solution.py:77
  138.1 3.3 %collective-permute-start.14 = (f32[8,512]{1,0:T(8,128)S(1)}, f32[8,512]{1,0:T(8,128)S(1)}, u32[]{:S(2)}, u32[]{:S(2)}) collective-permute-start(f32[8,512]{1,0:T(8,128)S(1)} %slice_select_fusion.3), channel_id=1, source_target_pairs={{0,8},{4,12},{8,16},{12,20},{16,24},{20,28},{1,9},{5,13},{9,17},{1... | collective-permute-start | bytes 49160 | tf_op jit(solution)/shard_map/ppermute | solution.py:271
  141.4 2.2 pad_maximum_fusion.1.refs_0_
  143.5 6.5 %shard_map.68.partial_ref = f32[512,512]{1,0:T(8,128)} custom-call(s32[8]{0:T(128)} %stack.58.at_ref, bf16[512,4096]{1,0:T(8,128)(2,1)} %all-gather.2.cloned.1.call-done.x_ref, bf16[2,512,512]{2,1,0:T(8,128)(2,1)} %copy-done.2, bf16[2,512,512]{2,1,0:T(8,128)(2,1)} %copy-done.6, bf16[2,512,512]{2,1,0:T(8,128)(2,1)} %collective-permute-done.9.refs_2_), custom_call_target="tpu_custom_call" | custom-call | flops 1 | bytes 1 | tf_op jit(solution)/shard_map/pallas_call | solution.py:77
  150.1 6.5 %shard_map.69.partial_ref = f32[512,512]{1,0:T(8,128)} custom-call(s32[8]{0:T(128)} %stack.58.at_ref, bf16[512,4096]{1,0:T(8,128)(2,1)} %collective-permute-done.13.x_ref, bf16[2,512,512]{2,1,0:T(8,128)(2,1)} %copy-done.2, bf16[2,512,512]{2,1,0:T(8,128)(2,1)} %copy-done.6, bf16[2,512,512]{2,1,0:T(8,128)(2,1)} %collective-permute-done.9.refs_2_), custom_call_target="tpu_custom_call" | custom-call | flops 1 | bytes 1 | tf_op jit(solution)/shard_map/pallas_call | solution.py:77
  156.6 1.4 broadcast_select_fusion
  158.0 3.4 %shard_map.67.filtered_ref = f32[512,512]{1,0:T(8,128)} custom-call(f32[512,512]{1,0:T(8,128)} %shard_map.65.product_ref, f32[8,512]{1,0:T(8,128)} %get-tuple-element.97.halo_ref, f32[7,512]{1,0:T(8,128)} %reshape.16.taps_ref), custom_call_target="tpu_custom_call" | custom-call | flops 1 | bytes 1 | tf_op jit(solution)/shard_map/pallas_call | solution.py:111
  161.3 3.4 %shard_map.66.filtered_ref = f32[512,512]{1,0:T(8,128)} custom-call(f32[512,512]{1,0:T(8,128)} %shard_map.64.product_ref, f32[8,512]{1,0:T(8,128)} %get-tuple-element.98.halo_ref, f32[7,512]{1,0:T(8,128)} %reshape.16.taps_ref), custom_call_target="tpu_custom_call" | custom-call | flops 1 | bytes 1 | tf_op jit(solution)/shard_map/pallas_call | solution.py:111
  166.4 5.4 %shard_map.71.gated_ref = bf16[512,512]{1,0:T(8,128)(2,1)} custom-call(s32[2]{0:T(128)} %pad_add_fusion.at_ref, bf16[512,4096]{1,0:T(8,128)(2,1)} %collective-permute-done.13.x_ref, f32[512,512]{1,0:T(8,128)} %shard_map.67.filtered_ref, f32[512,512]{1,0:T(8,128)} %shard_map.69.partial_ref, bf16[512,512]{1,0:T(8,128)(2,1)} %copy-done.18, ...), custom_call_target="tpu_custom_call" | custom-call | flops 1 | bytes 1 | tf_op jit(solution)/shard_map/pallas_call | solution.py:77
  171.8 3.2 shard_map.72
  174.9 1.6 collective-permute-start.22
  176.5 5.4 %shard_map.70.gated_ref = bf16[512,512]{1,0:T(8,128)(2,1)} custom-call(s32[2]{0:T(128)} %pad_add_fusion.at_ref, bf16[512,4096]{1,0:T(8,128)(2,1)} %all-gather.2.cloned.1.call-done.x_ref, f32[512,512]{1,0:T(8,128)} %shard_map.66.filtered_ref, f32[512,512]{1,0:T(8,128)} %shard_map.68.partial_ref, bf16[512,512]{1,0:T(8,128)(2,1)} %copy-done.18, ...), custom_call_target="tpu_custom_call" | custom-call | flops 1 | bytes 1 | tf_op jit(solution)/shard_map/pallas_call | solution.py:77
  182.9 3.3 %shard_map.73 = (bf16[128,1024]{1,0:T(8,128)(2,1)}, bf16[128,1024]{1,0:T(8,128)(2,1)}, bf16[128,1024]{1,0:T(8,128)(2,1)}, bf16[128,1024]{1,0:T(8,128)(2,1)}) custom-call(s32[1]{0:T(128)} %bitcast.z_ref, bf16[512,512]{1,0:T(8,128)(2,1)} %shard_map.70.gated_ref, bf16[2,512,512]{2,1,0:T(8,128)(2,1)} %pad_maximum_fusion.1.refs_0_, bf16[512,1024]{1,0:T(8,128)(2,1)} %copy-done.24), custom_call_target="tpu_custom_call" | custom-call | flops 1 | bytes 1 | tf_op jit(solution)/shard_map/pallas_call | solution.py:155
  186.2 3.5 %collective-permute-start.16 = (bf16[128,1024]{1,0:T(8,128)(2,1)}, bf16[128,1024]{1,0:T(8,128)(2,1)S(1)}, u32[]{:S(2)}, u32[]{:S(2)}) collective-permute-start(bf16[128,1024]{1,0:T(8,128)(2,1)} %get-tuple-element.80), channel_id=1, source_target_pairs={{0,1},{1,2},{2,3},{4,5},{5,6},{6,7},{8,9},{9,10},{10,11},{12,13},{... | collective-permute-start | bytes 786440 | tf_op jit(solution)/shard_map/ppermute | solution.py:312
  189.7 1.5 collective-permute-start.19
  191.1 4.8 %collective-permute-done.16 = bf16[128,1024]{1,0:T(8,128)(2,1)S(1)} collective-permute-done((bf16[128,1024]{1,0:T(8,128)(2,1)}, bf16[128,1024]{1,0:T(8,128)(2,1)S(1)}, u32[]{:S(2)}, u32[]{:S(2)}) %collective-permute-start.16) | collective-permute-done | bytes 262176 | tf_op jit(solution)/shard_map/ppermute | solution.py:312
  195.9 4.0 %collective-permute-done.19 = bf16[128,1024]{1,0:T(8,128)(2,1)S(1)} collective-permute-done((bf16[128,1024]{1,0:T(8,128)(2,1)}, bf16[128,1024]{1,0:T(8,128)(2,1)S(1)}, u32[]{:S(2)}, u32[]{:S(2)}) %collective-permute-start.19) | collective-permute-done | bytes 262176 | tf_op jit(solution)/shard_map/ppermute | solution.py:313
  200.5 1.3 collective-permute-done.23.refs_1_
  202.8 4.3 %shard_map.74 = bf16[512,2048]{1,0:T(8,128)(2,1)} custom-call(s32[1]{0:T(128)} %bitcast.z_ref, bf16[512,512]{1,0:T(8,128)(2,1)} %shard_map.71.gated_ref, bf16[2,512,512]{2,1,0:T(8,128)(2,1)} %copy-done.7, bf16[2,512,512]{2,1,0:T(8,128)(2,1)} %copy-done.9), custom_call_target="tpu_custom_call" | custom-call | flops 1 | bytes 1 | tf_op jit(solution)/shard_map/pallas_call | solution.py:155
  207.1 4.4 %collective-permute-done.24.refs_2_ = bf16[512,2048]{1,0:T(8,128)(2,1)S(1)} collective-permute-done((bf16[512,2048]{1,0:T(8,128)(2,1)}, bf16[512,2048]{1,0:T(8,128)(2,1)S(1)}, u32[]{:S(2)}, u32[]{:S(2)}) %collective-permute-start.24) | collective-permute-done | bytes 2097184 | tf_op jit(solution)/shard_map/ppermute | solution.py:195
  211.4 1.3 copy-done.20
  212.7 4.9 %shard_map.75 = (bf16[128,2048]{1,0:T(8,128)(2,1)}, bf16[128,2048]{1,0:T(8,128)(2,1)}, bf16[128,2048]{1,0:T(8,128)(2,1)}, bf16[128,2048]{1,0:T(8,128)(2,1)}) custom-call(s32[1]{0:T(128)} %bitcast.z_ref, bf16[512,512]{1,0:T(8,128)(2,1)} %shard_map.70.gated_ref, bf16[2,512,512]{2,1,0:T(8,128)(2,1)} %copy-done.7, bf16[2,512,512]{2,1,0:T(8,128)(2,1)} %copy-done.9, ...), custom_call_target="tpu_custom_call" | custom-call | flops 1 | bytes 1 | tf_op jit(solution)/shard_map/pallas_call | solution.py:155
  217.6 3.6 %collective-permute-start.25 = (bf16[128,2048]{1,0:T(8,128)(2,1)}, bf16[128,2048]{1,0:T(8,128)(2,1)S(1)}, u32[]{:S(2)}, u32[]{:S(2)}) collective-permute-start(bf16[128,2048]{1,0:T(8,128)(2,1)} %get-tuple-element.86), channel_id=1, source_target_pairs={{0,1},{1,2},{2,3},{4,5},{5,6},{6,7},{8,9},{9,10},{10,11},{12,13},{... | collective-permute-start | bytes 1572872 | tf_op jit(solution)/shard_map/ppermute | solution.py:312
  221.3 1.3 collective-permute-start.28
  222.7 4.6 %collective-permute-start.17 = (bf16[128,1024]{1,0:T(8,128)(2,1)S(1)}, bf16[128,1024]{1,0:T(8,128)(2,1)S(1)}, u32[]{:S(2)}, u32[]{:S(2)}) collective-permute-start(bf16[128,1024]{1,0:T(8,128)(2,1)S(1)} %get-tuple-element.113), channel_id=1, source_target_pairs={{0,1},{1,2},{2,3},{4,5},{5,6},{6,7},{8,9},{9,10},{10,11},{12,13},{... | collective-permute-start | bytes 786440 | tf_op jit(solution)/shard_map/ppermute | solution.py:312
  229.8 8.7 %collective-permute-done.17 = bf16[128,1024]{1,0:T(8,128)(2,1)S(1)} collective-permute-done((bf16[128,1024]{1,0:T(8,128)(2,1)S(1)}, bf16[128,1024]{1,0:T(8,128)(2,1)S(1)}, u32[]{:S(2)}, u32[]{:S(2)}) %collective-permute-start.17) | collective-permute-done | bytes 262176 | tf_op jit(solution)/shard_map/ppermute | solution.py:312
  239.3 5.1 %collective-permute-start.18 = (bf16[128,1024]{1,0:T(8,128)(2,1)}, bf16[128,1024]{1,0:T(8,128)(2,1)}, u32[]{:S(2)}, u32[]{:S(2)}) collective-permute-start(bf16[128,1024]{1,0:T(8,128)(2,1)} %add_convert_fusion.5), channel_id=1, source_target_pairs={{0,1},{1,2},{2,3},{4,5},{5,6},{6,7},{8,9},{9,10},{10,11},{12,13},{... | collective-permute-start | bytes 786440 | tf_op jit(solution)/shard_map/ppermute | solution.py:312
  244.4 1.3 fusion.3
  245.7 3.8 %collective-permute-start.26 = (bf16[128,2048]{1,0:T(8,128)(2,1)}, bf16[128,2048]{1,0:T(8,128)(2,1)}, u32[]{:S(2)}, u32[]{:S(2)}) collective-permute-start(bf16[128,2048]{1,0:T(8,128)(2,1)} %get-tuple-element.107), channel_id=1, source_target_pairs={{0,1},{1,2},{2,3},{4,5},{5,6},{6,7},{8,9},{9,10},{10,11},{12,13},{... | collective-permute-start | bytes 1572872 | tf_op jit(solution)/shard_map/ppermute | solution.py:312
  252.7 3.1 shard_map.76
  255.8 1.4 collective-permute-start.29
  257.2 2.2 collective-permute-done.21
  261.8 4.1 %collective-permute-start.27 = (bf16[128,2048]{1,0:T(8,128)(2,1)S(1)}, bf16[128,2048]{1,0:T(8,128)(2,1)S(1)}, u32[]{:S(2)}, u32[]{:S(2)}) collective-permute-start(bf16[128,2048]{1,0:T(8,128)(2,1)S(1)} %add_convert_fusion.1), channel_id=1, source_target_pairs={{0,1},{1,2},{2,3},{4,5},{5,6},{6,7},{8,9},{9,10},{10,11},{12,13},{... | collective-permute-start | bytes 1572872 | tf_op jit(solution)/shard_map/ppermute | solution.py:312
  265.9 6.8 %collective-permute-done.29 = bf16[128,2048]{1,0:T(8,128)(2,1)S(1)} collective-permute-done((bf16[128,2048]{1,0:T(8,128)(2,1)S(1)}, bf16[128,2048]{1,0:T(8,128)(2,1)S(1)}, u32[]{:S(2)}, u32[]{:S(2)}) %collective-permute-start.29) | collective-permute-done | bytes 524320 | tf_op jit(solution)/shard_map/ppermute | solution.py:313
  273.7 1.4 collective-permute-start.30
  276.1 3.3 %shard_map.77 = (bf16[128,1024]{1,0:T(8,128)(2,1)}, bf16[128,1024]{1,0:T(8,128)(2,1)}, bf16[128,1024]{1,0:T(8,128)(2,1)}, bf16[128,1024]{1,0:T(8,128)(2,1)}) custom-call(s32[1]{0:T(128)} %bitcast.z_ref, bf16[512,512]{1,0:T(8,128)(2,1)} %shard_map.70.gated_ref, bf16[2,512,512]{2,1,0:T(8,128)(2,1)} %copy-done.10, bf16[512,1024]{1,0:T(8,128)(2,1)} %copy-done.23), custom_call_target="tpu_custom_call" | custom-call | flops 1 | bytes 1 | tf_op jit(solution)/shard_map/pallas_call | solution.py:155
  279.4 4.5 %collective-permute-start.33 = (bf16[128,1024]{1,0:T(8,128)(2,1)}, bf16[128,1024]{1,0:T(8,128)(2,1)S(1)}, u32[]{:S(2)}, u32[]{:S(2)}) collective-permute-start(bf16[128,1024]{1,0:T(8,128)(2,1)} %get-tuple-element.92), channel_id=1, source_target_pairs={{0,1},{1,2},{2,3},{4,5},{5,6},{6,7},{8,9},{9,10},{10,11},{12,13},{... | collective-permute-start | bytes 786440 | tf_op jit(solution)/shard_map/ppermute | solution.py:312
  283.9 1.4 collective-permute-start.36
  285.7 3.7 %collective-permute-done.33 = bf16[128,1024]{1,0:T(8,128)(2,1)S(1)} collective-permute-done((bf16[128,1024]{1,0:T(8,128)(2,1)}, bf16[128,1024]{1,0:T(8,128)(2,1)S(1)}, u32[]{:S(2)}, u32[]{:S(2)}) %collective-permute-start.33) | collective-permute-done | bytes 262176 | tf_op jit(solution)/shard_map/ppermute | solution.py:312
  289.4 5.7 %collective-permute-done.36 = bf16[128,1024]{1,0:T(8,128)(2,1)S(1)} collective-permute-done((bf16[128,1024]{1,0:T(8,128)(2,1)}, bf16[128,1024]{1,0:T(8,128)(2,1)S(1)}, u32[]{:S(2)}, u32[]{:S(2)}) %collective-permute-start.36) | collective-permute-done | bytes 262176 | tf_op jit(solution)/shard_map/ppermute | solution.py:313
  295.3 3.4 %collective-permute-start.34 = (bf16[128,1024]{1,0:T(8,128)(2,1)S(1)}, bf16[128,1024]{1,0:T(8,128)(2,1)S(1)}, u32[]{:S(2)}, u32[]{:S(2)}) collective-permute-start(bf16[128,1024]{1,0:T(8,128)(2,1)S(1)} %get-tuple-element.111), channel_id=1, source_target_pairs={{0,1},{1,2},{2,3},{4,5},{5,6},{6,7},{8,9},{9,10},{10,11},{12,13},{... | collective-permute-start | bytes 786440 | tf_op jit(solution)/shard_map/ppermute | solution.py:312
  298.8 1.3 convert_add_fusion.2
  300.1 1.4 collective-permute-start.37
  301.6 1.4 collective-permute-done.34
  303.1 4.4 %collective-permute-start.35 = (bf16[128,1024]{1,0:T(8,128)(2,1)S(1)}, bf16[128,1024]{1,0:T(8,128)(2,1)S(1)}, u32[]{:S(2)}, u32[]{:S(2)}) collective-permute-start(bf16[128,1024]{1,0:T(8,128)(2,1)S(1)} %add_convert_fusion.3), channel_id=1, source_target_pairs={{0,1},{1,2},{2,3},{4,5},{5,6},{6,7},{8,9},{9,10},{10,11},{12,13},{... | collective-permute-start | bytes 786440 | tf_op jit(solution)/shard_map/ppermute | solution.py:312
  308.8 1.3 collective-permute-start.38
  311.4 5.6 %collective-permute-done.38 = bf16[128,1024]{1,0:T(8,128)(2,1)S(1)} collective-permute-done((bf16[128,1024]{1,0:T(8,128)(2,1)S(1)}, bf16[128,1024]{1,0:T(8,128)(2,1)S(1)}, u32[]{:S(2)}, u32[]{:S(2)}) %collective-permute-start.38) | collective-permute-done | bytes 262176 | tf_op jit(solution)/shard_map/ppermute | solution.py:313
  (148 shorter events, 29.3 us)
Async XLA Ops:
  6.5 105.4 %copy-start = (f32[7,64]{1,0:T(8,128)S(1)}, f32[7,64]{1,0:T(8,128)}, u32[]{:S(2)}) copy-start(f32[7,64]{1,0:T(8,128)} %param.9) | copy-start | bytes 5380
  6.5 102.6 %all-gather.2.cloned.1.call-start = ((), (), s32[]{:S(2)}) async-start(), calls=%async_computation | async-start | bytes 5242880 | tf_op jit(solution)/shard_map/all_gather | solution.py:233
  10.0 4.6 %collective-permute-start = (bf16[2,512,512]{2,1,0:T(8,128)(2,1)S(1)}, bf16[2,512,512]{2,1,0:T(8,128)(2,1)S(1)}, u32[]{:S(2)}, u32[]{:S(2)}) collective-permute-start(bf16[2,512,512]{2,1,0:T(8,128)(2,1)S(1)} %get-tuple-element.96), channel_id=1, source_target_pairs={{0,4},{4,0},{8,12},{12,8},{16,20},{20,16},{24,28},{28,24},{1,5},{5... | collective-permute-start | bytes 3145736 | tf_op jit(solution)/shard_map/ppermute | solution.py:195
  10.6 26.6 %collective-permute-start.1 = (bf16[2,512,512]{2,1,0:T(8,128)(2,1)S(1)}, bf16[2,512,512]{2,1,0:T(8,128)(2,1)S(1)}, u32[]{:S(2)}, u32[]{:S(2)}) collective-permute-start(bf16[2,512,512]{2,1,0:T(8,128)(2,1)S(1)} %get-tuple-element.62.refs_0_), channel_id=1, source_target_pairs={{8,0},{12,4},{0,8},{4,12},{24,16},{28,20},{16,24},{20,28},{9,1},{1... | collective-permute-start | bytes 3145736 | tf_op jit(solution)/shard_map/ppermute | solution.py:192
  13.1 26.0 %collective-permute-start.3 = (bf16[2,512,512]{2,1,0:T(8,128)(2,1)S(1)}, bf16[2,512,512]{2,1,0:T(8,128)(2,1)S(1)}, u32[]{:S(2)}, u32[]{:S(2)}) collective-permute-start(bf16[2,512,512]{2,1,0:T(8,128)(2,1)S(1)} %get-tuple-element.62.refs_0_), channel_id=1, source_target_pairs={{16,0},{20,4},{24,8},{28,12},{0,16},{4,20},{8,24},{12,28},{17,1},{... | collective-permute-start | bytes 3145736 | tf_op jit(solution)/shard_map/ppermute | solution.py:192
  14.6 44.7 %collective-permute-start.2 = (bf16[2,512,512]{2,1,0:T(8,128)(2,1)S(1)}, bf16[2,512,512]{2,1,0:T(8,128)(2,1)S(1)}, u32[]{:S(2)}, u32[]{:S(2)}) collective-permute-start(bf16[2,512,512]{2,1,0:T(8,128)(2,1)S(1)} %collective-permute-done.refs_1_), channel_id=1, source_target_pairs={{8,0},{12,4},{0,8},{4,12},{24,16},{28,20},{16,24},{20,28},{9,1},{1... | collective-permute-start | bytes 3145736 | tf_op jit(solution)/shard_map/ppermute | solution.py:192
  15.7 45.1 %collective-permute-start.4 = (bf16[2,512,512]{2,1,0:T(8,128)(2,1)S(1)}, bf16[2,512,512]{2,1,0:T(8,128)(2,1)S(1)}, u32[]{:S(2)}, u32[]{:S(2)}) collective-permute-start(bf16[2,512,512]{2,1,0:T(8,128)(2,1)S(1)} %collective-permute-done.refs_1_), channel_id=1, source_target_pairs={{16,0},{20,4},{24,8},{28,12},{0,16},{4,20},{8,24},{12,28},{17,1},{... | collective-permute-start | bytes 3145736 | tf_op jit(solution)/shard_map/ppermute | solution.py:192
  18.5 2.0 collective-permute-start.5
  20.6 95.2 %copy-start.2 = (bf16[2,512,512]{2,1,0:T(8,128)(2,1)}, bf16[2,512,512]{2,1,0:T(8,128)(2,1)S(1)}, u32[]{:S(2)}) copy-start(bf16[2,512,512]{2,1,0:T(8,128)(2,1)S(1)} %pad_maximum_fusion.refs_0_) | copy-start | bytes 3145732
  37.1 71.9 %copy-start.12 = (bf16[2,512,512]{2,1,0:T(8,128)(2,1)}, bf16[2,512,512]{2,1,0:T(8,128)(2,1)S(1)}, u32[]{:S(2)}) copy-start(bf16[2,512,512]{2,1,0:T(8,128)(2,1)S(1)} %collective-permute-done.1.refs_2_) | copy-start | bytes 3145732
  39.1 69.9 %copy-start.13 = (bf16[2,512,512]{2,1,0:T(8,128)(2,1)}, bf16[2,512,512]{2,1,0:T(8,128)(2,1)S(1)}, u32[]{:S(2)}) copy-start(bf16[2,512,512]{2,1,0:T(8,128)(2,1)S(1)} %collective-permute-done.3.refs_4_) | copy-start | bytes 3145732
  59.3 49.7 %copy-start.14 = (bf16[2,512,512]{2,1,0:T(8,128)(2,1)}, bf16[2,512,512]{2,1,0:T(8,128)(2,1)S(1)}, u32[]{:S(2)}) copy-start(bf16[2,512,512]{2,1,0:T(8,128)(2,1)S(1)} %collective-permute-done.2.refs_3_) | copy-start | bytes 3145732
  60.8 48.2 %copy-start.15 = (bf16[2,512,512]{2,1,0:T(8,128)(2,1)}, bf16[2,512,512]{2,1,0:T(8,128)(2,1)S(1)}, u32[]{:S(2)}) copy-start(bf16[2,512,512]{2,1,0:T(8,128)(2,1)S(1)} %collective-permute-done.4.refs_5_) | copy-start | bytes 3145732
  60.8 26.1 %collective-permute-start.6 = (bf16[2,512,512]{2,1,0:T(8,128)(2,1)S(1)}, bf16[2,512,512]{2,1,0:T(8,128)(2,1)S(1)}, u32[]{:S(2)}, u32[]{:S(2)}) collective-permute-start(bf16[2,512,512]{2,1,0:T(8,128)(2,1)S(1)} %collective-permute-done.1.refs_2_), channel_id=1, source_target_pairs={{16,0},{20,4},{24,8},{28,12},{0,16},{4,20},{8,24},{12,28},{17,1},{... | collective-permute-start | bytes 3145736 | tf_op jit(solution)/shard_map/ppermute | solution.py:192
  62.3 26.1 %collective-permute-start.7 = (bf16[2,512,512]{2,1,0:T(8,128)(2,1)S(1)}, bf16[2,512,512]{2,1,0:T(8,128)(2,1)S(1)}, u32[]{:S(2)}, u32[]{:S(2)}) collective-permute-start(bf16[2,512,512]{2,1,0:T(8,128)(2,1)S(1)} %collective-permute-done.4.refs_5_), channel_id=1, source_target_pairs={{8,0},{12,4},{0,8},{4,12},{24,16},{28,20},{16,24},{20,28},{9,1},{1... | collective-permute-start | bytes 3145736 | tf_op jit(solution)/shard_map/ppermute | solution.py:192
  62.9 46.1 %collective-permute-start.8 = (bf16[2,512,512]{2,1,0:T(8,128)(2,1)S(1)}, bf16[2,512,512]{2,1,0:T(8,128)(2,1)S(1)}, u32[]{:S(2)}, u32[]{:S(2)}) collective-permute-start(bf16[2,512,512]{2,1,0:T(8,128)(2,1)S(1)} %pad_maximum_fusion.refs_0_), channel_id=1, source_target_pairs={{8,0},{12,4},{0,8},{4,12},{24,16},{28,20},{16,24},{20,28},{9,1},{1... | collective-permute-start | bytes 3145736 | tf_op jit(solution)/shard_map/ppermute | solution.py:192
  64.4 44.7 %collective-permute-start.9 = (bf16[2,512,512]{2,1,0:T(8,128)(2,1)S(1)}, bf16[2,512,512]{2,1,0:T(8,128)(2,1)}, u32[]{:S(2)}, u32[]{:S(2)}) collective-permute-start(bf16[2,512,512]{2,1,0:T(8,128)(2,1)S(1)} %pad_maximum_fusion.refs_0_), channel_id=1, source_target_pairs={{16,0},{20,4},{24,8},{28,12},{0,16},{4,20},{8,24},{12,28},{17,1},{... | collective-permute-start | bytes 3145736 | tf_op jit(solution)/shard_map/ppermute | solution.py:192
  86.9 22.1 %copy-start.16 = (bf16[2,512,512]{2,1,0:T(8,128)(2,1)}, bf16[2,512,512]{2,1,0:T(8,128)(2,1)S(1)}, u32[]{:S(2)}) copy-start(bf16[2,512,512]{2,1,0:T(8,128)(2,1)S(1)} %collective-permute-done.6.refs_6_) | copy-start | bytes 3145732
  88.4 20.6 %copy-start.17 = (bf16[2,512,512]{2,1,0:T(8,128)(2,1)}, bf16[2,512,512]{2,1,0:T(8,128)(2,1)S(1)}, u32[]{:S(2)}) copy-start(bf16[2,512,512]{2,1,0:T(8,128)(2,1)S(1)} %collective-permute-done.7.refs_7_) | copy-start | bytes 3145732
  109.1 6.7 %copy-start.6 = (bf16[2,512,512]{2,1,0:T(8,128)(2,1)}, bf16[2,512,512]{2,1,0:T(8,128)(2,1)S(1)}, u32[]{:S(2)}) copy-start(bf16[2,512,512]{2,1,0:T(8,128)(2,1)S(1)} %collective-permute-done.8.refs_1_) | copy-start | bytes 3145732
  109.1 17.7 %collective-permute-start.13 = (bf16[512,4096]{1,0:T(8,128)(2,1)}, bf16[512,4096]{1,0:T(8,128)(2,1)}, u32[]{:S(2)}, u32[]{:S(2)}) collective-permute-start(bf16[512,4096]{1,0:T(8,128)(2,1)} %all-gather.2.cloned.1.call-done.x_ref), channel_id=1, source_target_pairs={{0,4},{4,0},{8,12},{12,8},{16,20},{20,16},{24,28},{28,24},{1,5},{5... | collective-permute-start | bytes 12582920 | tf_op jit(solution)/shard_map/ppermute | solution.py:195
  111.7 29.6 %collective-permute-start.10 = (bf16[512,512]{1,0:T(8,128)(2,1)}, bf16[512,512]{1,0:T(8,128)(2,1)}, u32[]{:S(2)}, u32[]{:S(2)}) collective-permute-start(bf16[512,512]{1,0:T(8,128)(2,1)} %get-tuple-element.104), channel_id=1, source_target_pairs={{0,4},{4,0},{8,12},{12,8},{16,20},{20,16},{24,28},{28,24},{1,5},{5... | collective-permute-start | bytes 1572872 | tf_op jit(solution)/shard_map/ppermute | solution.py:195
  114.1 50.7 %collective-permute-start.11 = (bf16[512,512]{1,0:T(8,128)(2,1)S(1)}, bf16[512,512]{1,0:T(8,128)(2,1)S(1)}, u32[]{:S(2)}, u32[]{:S(2)}) collective-permute-start(bf16[512,512]{1,0:T(8,128)(2,1)S(1)} %slice_bitcast_fusion.1), channel_id=1, source_target_pairs={{16,0},{20,4},{24,8},{28,12},{0,16},{4,20},{8,24},{12,28},{17,1},{... | collective-permute-start | bytes 1572872 | tf_op jit(solution)/shard_map/ppermute | solution.py:192
  115.8 49.0 %collective-permute-start.12 = (bf16[512,512]{1,0:T(8,128)(2,1)S(1)}, bf16[512,512]{1,0:T(8,128)(2,1)S(1)}, u32[]{:S(2)}, u32[]{:S(2)}) collective-permute-start(bf16[512,512]{1,0:T(8,128)(2,1)S(1)} %slice_bitcast_fusion), channel_id=1, source_target_pairs={{8,0},{12,4},{0,8},{4,12},{24,16},{28,20},{16,24},{20,28},{9,1},{1... | collective-permute-start | bytes 1572872 | tf_op jit(solution)/shard_map/ppermute | solution.py:192
  126.8 14.6 %copy-start.22 = (bf16[1,512,512]{2,1,0:T(8,128)(2,1)S(1)}, bf16[1,512,512]{2,1,0:T(8,128)(2,1)}, u32[]{:S(2)}) copy-start(bf16[1,512,512]{2,1,0:T(8,128)(2,1)} %get-tuple-element.103) | copy-start | bytes 1572868
  138.1 18.5 %collective-permute-start.14 = (f32[8,512]{1,0:T(8,128)S(1)}, f32[8,512]{1,0:T(8,128)S(1)}, u32[]{:S(2)}, u32[]{:S(2)}) collective-permute-start(f32[8,512]{1,0:T(8,128)S(1)} %slice_select_fusion.3), channel_id=1, source_target_pairs={{0,8},{4,12},{8,16},{12,20},{16,24},{20,28},{1,9},{5,13},{9,17},{1... | collective-permute-start | bytes 49160 | tf_op jit(solution)/shard_map/ppermute | solution.py:271
  174.9 7.0 %collective-permute-start.15 = (bf16[512,1024]{1,0:T(8,128)(2,1)}, bf16[512,1024]{1,0:T(8,128)(2,1)S(1)}, u32[]{:S(2)}, u32[]{:S(2)}) collective-permute-start(bf16[512,1024]{1,0:T(8,128)(2,1)} %shard_map.72), channel_id=1, source_target_pairs={{0,4},{4,0},{8,12},{12,8},{16,20},{20,16},{24,28},{28,24},{1,5},{5... | collective-permute-start | bytes 3145736 | tf_op jit(solution)/shard_map/ppermute | solution.py:195
  174.9 25.6 %collective-permute-start.22 = (bf16[2,512,512]{2,1,0:T(8,128)(2,1)S(1)}, bf16[2,512,512]{2,1,0:T(8,128)(2,1)S(1)}, u32[]{:S(2)}, u32[]{:S(2)}) collective-permute-start(bf16[2,512,512]{2,1,0:T(8,128)(2,1)S(1)} %copy-done.3), channel_id=1, source_target_pairs={{8,0},{12,4},{0,8},{4,12},{24,16},{28,20},{16,24},{20,28},{9,1},{1... | collective-permute-start | bytes 3145736 | tf_op jit(solution)/shard_map/ppermute | solution.py:192
  176.5 25.3 %collective-permute-start.23 = (bf16[2,512,512]{2,1,0:T(8,128)(2,1)S(1)}, bf16[2,512,512]{2,1,0:T(8,128)(2,1)S(1)}, u32[]{:S(2)}, u32[]{:S(2)}) collective-permute-start(bf16[2,512,512]{2,1,0:T(8,128)(2,1)S(1)} %copy-done.3), channel_id=1, source_target_pairs={{16,0},{20,4},{24,8},{28,12},{0,16},{4,20},{8,24},{12,28},{17,1},{... | collective-permute-start | bytes 3145736 | tf_op jit(solution)/shard_map/ppermute | solution.py:192
  186.2 9.7 %collective-permute-start.16 = (bf16[128,1024]{1,0:T(8,128)(2,1)}, bf16[128,1024]{1,0:T(8,128)(2,1)S(1)}, u32[]{:S(2)}, u32[]{:S(2)}) collective-permute-start(bf16[128,1024]{1,0:T(8,128)(2,1)} %get-tuple-element.80), channel_id=1, source_target_pairs={{0,1},{1,2},{2,3},{4,5},{5,6},{6,7},{8,9},{9,10},{10,11},{12,13},{... | collective-permute-start | bytes 786440 | tf_op jit(solution)/shard_map/ppermute | solution.py:312
  189.7 10.3 %collective-permute-start.19 = (bf16[128,1024]{1,0:T(8,128)(2,1)}, bf16[128,1024]{1,0:T(8,128)(2,1)S(1)}, u32[]{:S(2)}, u32[]{:S(2)}) collective-permute-start(bf16[128,1024]{1,0:T(8,128)(2,1)} %get-tuple-element.78), channel_id=1, source_target_pairs={{1,0},{2,1},{3,2},{5,4},{6,5},{7,6},{9,8},{10,9},{11,10},{13,12},{... | collective-permute-start | bytes 786440 | tf_op jit(solution)/shard_map/ppermute | solution.py:313
  207.1 15.5 %copy-start.37 = (bf16[128,1024]{1,0:T(8,128)(2,1)S(1)}, bf16[128,1024]{1,0:T(8,128)(2,1)}, u32[]{:S(2)}) copy-start(bf16[128,1024]{1,0:T(8,128)(2,1)} %get-tuple-element.79) | copy-start | bytes 786436
  207.1 20.2 %copy-start.8 = (bf16[2,512,512]{2,1,0:T(8,128)(2,1)S(1)}, bf16[2,512,512]{2,1,0:T(8,128)(2,1)}, u32[]{:S(2)}) copy-start(bf16[2,512,512]{2,1,0:T(8,128)(2,1)} %copy-done.7) | copy-start | bytes 3145732
  207.1 31.5 %copy-start.35 = (bf16[128,1024]{1,0:T(8,128)(2,1)S(1)}, bf16[128,1024]{1,0:T(8,128)(2,1)}, u32[]{:S(2)}) copy-start(bf16[128,1024]{1,0:T(8,128)(2,1)} %get-tuple-element.78) | copy-start | bytes 786436
  207.1 4.4 %collective-permute-start.24 = (bf16[512,2048]{1,0:T(8,128)(2,1)}, bf16[512,2048]{1,0:T(8,128)(2,1)S(1)}, u32[]{:S(2)}, u32[]{:S(2)}) collective-permute-start(bf16[512,2048]{1,0:T(8,128)(2,1)} %shard_map.74), channel_id=1, source_target_pairs={{0,4},{4,0},{8,12},{12,8},{16,20},{20,16},{24,28},{28,24},{1,5},{5... | collective-permute-start | bytes 6291464 | tf_op jit(solution)/shard_map/ppermute | solution.py:195
  217.6 26.8 %copy-start.30 = (bf16[128,2048]{1,0:T(8,128)(2,1)S(1)}, bf16[128,2048]{1,0:T(8,128)(2,1)}, u32[]{:S(2)}) copy-start(bf16[128,2048]{1,0:T(8,128)(2,1)} %get-tuple-element.85) | copy-start | bytes 1572868
  217.6 26.7 %collective-permute-start.25 = (bf16[128,2048]{1,0:T(8,128)(2,1)}, bf16[128,2048]{1,0:T(8,128)(2,1)S(1)}, u32[]{:S(2)}, u32[]{:S(2)}) collective-permute-start(bf16[128,2048]{1,0:T(8,128)(2,1)} %get-tuple-element.86), channel_id=1, source_target_pairs={{0,1},{1,2},{2,3},{4,5},{5,6},{6,7},{8,9},{9,10},{10,11},{12,13},{... | collective-permute-start | bytes 1572872 | tf_op jit(solution)/shard_map/ppermute | solution.py:312
  221.3 23.1 %collective-permute-start.28 = (bf16[128,2048]{1,0:T(8,128)(2,1)}, bf16[128,2048]{1,0:T(8,128)(2,1)S(1)}, u32[]{:S(2)}, u32[]{:S(2)}) collective-permute-start(bf16[128,2048]{1,0:T(8,128)(2,1)} %get-tuple-element.84), channel_id=1, source_target_pairs={{1,0},{2,1},{3,2},{5,4},{6,5},{7,6},{9,8},{10,9},{11,10},{13,12},{... | collective-permute-start | bytes 1572872 | tf_op jit(solution)/shard_map/ppermute | solution.py:313
  222.6 26.9 %copy-start.33 = (bf16[128,1024]{1,0:T(8,128)(2,1)S(1)}, bf16[128,1024]{1,0:T(8,128)(2,1)}, u32[]{:S(2)}) copy-start(bf16[128,1024]{1,0:T(8,128)(2,1)} %get-tuple-element.80) | copy-start | bytes 786436
  222.7 15.8 %collective-permute-start.17 = (bf16[128,1024]{1,0:T(8,128)(2,1)S(1)}, bf16[128,1024]{1,0:T(8,128)(2,1)S(1)}, u32[]{:S(2)}, u32[]{:S(2)}) collective-permute-start(bf16[128,1024]{1,0:T(8,128)(2,1)S(1)} %get-tuple-element.113), channel_id=1, source_target_pairs={{0,1},{1,2},{2,3},{4,5},{5,6},{6,7},{8,9},{9,10},{10,11},{12,13},{... | collective-permute-start | bytes 786440 | tf_op jit(solution)/shard_map/ppermute | solution.py:312
  227.3 24.4 %collective-permute-start.31 = (bf16[2,512,512]{2,1,0:T(8,128)(2,1)S(1)}, bf16[2,512,512]{2,1,0:T(8,128)(2,1)S(1)}, u32[]{:S(2)}, u32[]{:S(2)}) collective-permute-start(bf16[2,512,512]{2,1,0:T(8,128)(2,1)S(1)} %copy-done.8), channel_id=1, source_target_pairs={{16,0},{20,4},{24,8},{28,12},{0,16},{4,20},{8,24},{12,28},{17,1},{... | collective-permute-start | bytes 3145736 | tf_op jit(solution)/shard_map/ppermute | solution.py:192
  228.5 20.9 %collective-permute-start.20 = (bf16[128,1024]{1,0:T(8,128)(2,1)S(1)}, bf16[128,1024]{1,0:T(8,128)(2,1)S(1)}, u32[]{:S(2)}, u32[]{:S(2)}) collective-permute-start(bf16[128,1024]{1,0:T(8,128)(2,1)S(1)} %get-tuple-element.114), channel_id=1, source_target_pairs={{1,0},{2,1},{3,2},{5,4},{6,5},{7,6},{9,8},{10,9},{11,10},{13,12},{... | collective-permute-start | bytes 786440 | tf_op jit(solution)/shard_map/ppermute | solution.py:313
  239.3 17.9 %collective-permute-start.18 = (bf16[128,1024]{1,0:T(8,128)(2,1)}, bf16[128,1024]{1,0:T(8,128)(2,1)}, u32[]{:S(2)}, u32[]{:S(2)}) collective-permute-start(bf16[128,1024]{1,0:T(8,128)(2,1)} %add_convert_fusion.5), channel_id=1, source_target_pairs={{0,1},{1,2},{2,3},{4,5},{5,6},{6,7},{8,9},{9,10},{10,11},{12,13},{... | collective-permute-start | bytes 786440 | tf_op jit(solution)/shard_map/ppermute | solution.py:312
  245.7 13.7 %copy-start.31 = (bf16[128,1024]{1,0:T(8,128)(2,1)S(1)}, bf16[128,1024]{1,0:T(8,128)(2,1)}, u32[]{:S(2)}) copy-start(bf16[128,1024]{1,0:T(8,128)(2,1)} %get-tuple-element.77) | copy-start | bytes 786436
  245.7 14.9 %collective-permute-start.26 = (bf16[128,2048]{1,0:T(8,128)(2,1)}, bf16[128,2048]{1,0:T(8,128)(2,1)}, u32[]{:S(2)}, u32[]{:S(2)}) collective-permute-start(bf16[128,2048]{1,0:T(8,128)(2,1)} %get-tuple-element.107), channel_id=1, source_target_pairs={{0,1},{1,2},{2,3},{4,5},{5,6},{6,7},{8,9},{9,10},{10,11},{12,13},{... | collective-permute-start | bytes 1572872 | tf_op jit(solution)/shard_map/ppermute | solution.py:312
  250.2 9.2 %collective-permute-start.21 = (bf16[128,1024]{1,0:T(8,128)(2,1)}, bf16[128,1024]{1,0:T(8,128)(2,1)}, u32[]{:S(2)}, u32[]{:S(2)}) collective-permute-start(bf16[128,1024]{1,0:T(8,128)(2,1)} %add_convert_fusion.4), channel_id=1, source_target_pairs={{1,0},{2,1},{3,2},{5,4},{6,5},{7,6},{9,8},{10,9},{11,10},{13,12},{... | collective-permute-start | bytes 786440 | tf_op jit(solution)/shard_map/ppermute | solution.py:313
  251.6 9.0 %copy-start.28 = (bf16[128,2048]{1,0:T(8,128)(2,1)S(1)}, bf16[128,2048]{1,0:T(8,128)(2,1)}, u32[]{:S(2)}) copy-start(bf16[128,2048]{1,0:T(8,128)(2,1)} %get-tuple-element.84) | copy-start | bytes 1572868
  255.8 17.0 %copy-start.27 = (bf16[128,2048]{1,0:T(8,128)(2,1)S(1)}, bf16[128,2048]{1,0:T(8,128)(2,1)}, u32[]{:S(2)}) copy-start(bf16[128,2048]{1,0:T(8,128)(2,1)} %get-tuple-element.86) | copy-start | bytes 1572868
  255.8 19.3 %collective-permute-start.32 = (bf16[512,1024]{1,0:T(8,128)(2,1)}, bf16[512,1024]{1,0:T(8,128)(2,1)S(1)}, u32[]{:S(2)}, u32[]{:S(2)}) collective-permute-start(bf16[512,1024]{1,0:T(8,128)(2,1)} %shard_map.76), channel_id=1, source_target_pairs={{0,4},{4,0},{8,12},{12,8},{16,20},{20,16},{24,28},{28,24},{1,5},{5... | collective-permute-start | bytes 3145736 | tf_op jit(solution)/shard_map/ppermute | solution.py:195
  255.8 17.0 %collective-permute-start.29 = (bf16[128,2048]{1,0:T(8,128)(2,1)S(1)}, bf16[128,2048]{1,0:T(8,128)(2,1)S(1)}, u32[]{:S(2)}, u32[]{:S(2)}) collective-permute-start(bf16[128,2048]{1,0:T(8,128)(2,1)S(1)} %copy-done.29), channel_id=1, source_target_pairs={{1,0},{2,1},{3,2},{5,4},{6,5},{7,6},{9,8},{10,9},{11,10},{13,12},{... | collective-permute-start | bytes 1572872 | tf_op jit(solution)/shard_map/ppermute | solution.py:313
  261.8 36.9 %collective-permute-start.27 = (bf16[128,2048]{1,0:T(8,128)(2,1)S(1)}, bf16[128,2048]{1,0:T(8,128)(2,1)S(1)}, u32[]{:S(2)}, u32[]{:S(2)}) collective-permute-start(bf16[128,2048]{1,0:T(8,128)(2,1)S(1)} %add_convert_fusion.1), channel_id=1, source_target_pairs={{0,1},{1,2},{2,3},{4,5},{5,6},{6,7},{8,9},{9,10},{10,11},{12,13},{... | collective-permute-start | bytes 1572872 | tf_op jit(solution)/shard_map/ppermute | solution.py:312
  273.7 11.8 %copy-start.21 = (s32[128,4096]{1,0:T(8,128)S(1)}, s32[128,4096]{1,0:T(8,128)}, u32[]{:S(2)}) copy-start(s32[128,4096]{1,0:T(8,128)} %param.11) | copy-start | bytes 6291460
  273.7 25.1 %collective-permute-start.30 = (bf16[128,2048]{1,0:T(8,128)(2,1)}, bf16[128,2048]{1,0:T(8,128)(2,1)}, u32[]{:S(2)}, u32[]{:S(2)}) collective-permute-start(bf16[128,2048]{1,0:T(8,128)(2,1)} %add_convert_fusion), channel_id=1, source_target_pairs={{1,0},{2,1},{3,2},{5,4},{6,5},{7,6},{9,8},{10,9},{11,10},{13,12},{... | collective-permute-start | bytes 1572872 | tf_op jit(solution)/shard_map/ppermute | solution.py:313
  279.4 10.1 %collective-permute-start.33 = (bf16[128,1024]{1,0:T(8,128)(2,1)}, bf16[128,1024]{1,0:T(8,128)(2,1)S(1)}, u32[]{:S(2)}, u32[]{:S(2)}) collective-permute-start(bf16[128,1024]{1,0:T(8,128)(2,1)} %get-tuple-element.92), channel_id=1, source_target_pairs={{0,1},{1,2},{2,3},{4,5},{5,6},{6,7},{8,9},{9,10},{10,11},{12,13},{... | collective-permute-start | bytes 786440 | tf_op jit(solution)/shard_map/ppermute | solution.py:312
  283.9 11.2 %copy-start.38 = (bf16[128,1024]{1,0:T(8,128)(2,1)S(1)}, bf16[128,1024]{1,0:T(8,128)(2,1)}, u32[]{:S(2)}) copy-start(bf16[128,1024]{1,0:T(8,128)(2,1)} %get-tuple-element.91) | copy-start | bytes 786436
  283.9 11.2 %collective-permute-start.36 = (bf16[128,1024]{1,0:T(8,128)(2,1)}, bf16[128,1024]{1,0:T(8,128)(2,1)S(1)}, u32[]{:S(2)}, u32[]{:S(2)}) collective-permute-start(bf16[128,1024]{1,0:T(8,128)(2,1)} %get-tuple-element.90), channel_id=1, source_target_pairs={{1,0},{2,1},{3,2},{5,4},{6,5},{7,6},{9,8},{10,9},{11,10},{13,12},{... | collective-permute-start | bytes 786440 | tf_op jit(solution)/shard_map/ppermute | solution.py:313
  285.4 13.3 %copy-start.26 = (bf16[128,2048]{1,0:T(8,128)(2,1)S(1)}, bf16[128,2048]{1,0:T(8,128)(2,1)}, u32[]{:S(2)}) copy-start(bf16[128,2048]{1,0:T(8,128)(2,1)} %get-tuple-element.83) | copy-start | bytes 1572868
  295.3 7.8 %collective-permute-start.34 = (bf16[128,1024]{1,0:T(8,128)(2,1)S(1)}, bf16[128,1024]{1,0:T(8,128)(2,1)S(1)}, u32[]{:S(2)}, u32[]{:S(2)}) collective-permute-start(bf16[128,1024]{1,0:T(8,128)(2,1)S(1)} %get-tuple-element.111), channel_id=1, source_target_pairs={{0,1},{1,2},{2,3},{4,5},{5,6},{6,7},{8,9},{9,10},{10,11},{12,13},{... | collective-permute-start | bytes 786440 | tf_op jit(solution)/shard_map/ppermute | solution.py:312
  300.1 8.6 %copy-start.34 = (bf16[128,1024]{1,0:T(8,128)(2,1)S(1)}, bf16[128,1024]{1,0:T(8,128)(2,1)}, u32[]{:S(2)}) copy-start(bf16[128,1024]{1,0:T(8,128)(2,1)} %get-tuple-element.92) | copy-start | bytes 786436
  300.1 8.6 %collective-permute-start.37 = (bf16[128,1024]{1,0:T(8,128)(2,1)S(1)}, bf16[128,1024]{1,0:T(8,128)(2,1)S(1)}, u32[]{:S(2)}, u32[]{:S(2)}) collective-permute-start(bf16[128,1024]{1,0:T(8,128)(2,1)S(1)} %get-tuple-element.112), channel_id=1, source_target_pairs={{1,0},{2,1},{3,2},{5,4},{6,5},{7,6},{9,8},{10,9},{11,10},{13,12},{... | collective-permute-start | bytes 786440 | tf_op jit(solution)/shard_map/ppermute | solution.py:313
  303.1 8.3 %collective-permute-start.35 = (bf16[128,1024]{1,0:T(8,128)(2,1)S(1)}, bf16[128,1024]{1,0:T(8,128)(2,1)S(1)}, u32[]{:S(2)}, u32[]{:S(2)}) collective-permute-start(bf16[128,1024]{1,0:T(8,128)(2,1)S(1)} %add_convert_fusion.3), channel_id=1, source_target_pairs={{0,1},{1,2},{2,3},{4,5},{5,6},{6,7},{8,9},{9,10},{10,11},{12,13},{... | collective-permute-start | bytes 786440 | tf_op jit(solution)/shard_map/ppermute | solution.py:312
  308.8 8.3 %collective-permute-start.38 = (bf16[128,1024]{1,0:T(8,128)(2,1)S(1)}, bf16[128,1024]{1,0:T(8,128)(2,1)S(1)}, u32[]{:S(2)}, u32[]{:S(2)}) collective-permute-start(bf16[128,1024]{1,0:T(8,128)(2,1)S(1)} %add_convert_fusion.2), channel_id=1, source_target_pairs={{1,0},{2,1},{3,2},{5,4},{6,5},{7,6},{9,8},{10,9},{11,10},{13,12},{... | collective-permute-start | bytes 786440 | tf_op jit(solution)/shard_map/ppermute | solution.py:313
  310.1 7.0 %copy-start.32 = (bf16[128,1024]{1,0:T(8,128)(2,1)S(1)}, bf16[128,1024]{1,0:T(8,128)(2,1)}, u32[]{:S(2)}) copy-start(bf16[128,1024]{1,0:T(8,128)(2,1)} %get-tuple-element.89) | copy-start | bytes 786436
  310.4 6.8 %copy-start.25 = (bf16[128,4096]{1,0:T(8,128)(2,1)}, bf16[128,4096]{1,0:T(8,128)(2,1)S(1)}, u32[]{:S(2)}) copy-start(bf16[128,4096]{1,0:T(8,128)(2,1)S(1)} %fusion.28) | copy-start | bytes 3145732
  (16 other events, 35.6 us)
Sparse Core Ops, SparseCore 0:
  10.2 83.4 all-gather.1

commit v4 on v3

--- a/solution.py
+++ b/solution.py
@@ -10,7 +10,8 @@
 
 F32 = jnp.float32
 BF16 = jnp.bfloat16
-GRANT = 58 << 20
+GRANT = 16 << 20
+WHOLE = pl.BlockSpec(memory_space=pltpu.VMEM)
 
 
 def grid_of(chips):
@@ -18,152 +19,125 @@
     return ny, chips // ny
 
 
-def whole(array):
-    return pl.BlockSpec(array.shape, lambda *_: (0,) * len(array.shape))
-
-
 def dot(a, b):
     return jnp.dot(a, b, preferred_element_type=F32)
 
 
-def cost(flops, *arrays):
-    moved = sum(math.prod(a.shape) * a.dtype.itemsize for a in arrays)
-    return pl.CostEstimate(flops=1, bytes_accessed=1, transcendentals=0)
-
-
 def columns_of(x_ref, at_ref, index, deep):
     return x_ref[:, pl.ds(pl.multiple_of(at_ref[index], deep), deep)]
+
+
+def tiles_of(out_ref):
+    tile = math.gcd(out_ref.shape[1], 256)
+    return [slice(at, at + tile) for at in range(0, out_ref.shape[1], tile)]
 
 
 def product_kernel(at_ref, x_ref, *refs):
     pieces, out_ref = refs[:-1], refs[-1]
     deep = pieces[0].shape[1]
-    key = value = None
-    for index, piece in enumerate(pieces):
-        x = columns_of(x_ref, at_ref, index, deep)
-        new_key, new_value = dot(x, piece[0]), dot(x, piece[1])
-        key = new_key if key is None else key + new_key
-        value = new_value if value is None else value + new_value
-    out_ref[...] = key.astype(BF16).astype(F32) * value.astype(BF16).astype(F32)
+    for tile in tiles_of(out_ref):
+        key = value = None
+        for index, piece in enumerate(pieces):
+            x = columns_of(x_ref, at_ref, index, deep)
+            new_key, new_value = dot(x, piece[0, :, tile]), dot(x, piece[1, :, tile])
+            key = new_key if key is None else key + new_key
+            value = new_value if value is None else value + new_value
+        out_ref[:, tile] = key.astype(BF16).astype(F32) * value.astype(BF16).astype(F32)
 
 
 def query_kernel(at_ref, x_ref, *refs):
     pairs, out_ref = refs[:-1], refs[-1]
     deep = pairs[0].shape[1]
-    query = None
-    for index in range(2 * len(pairs)):
-        new = dot(columns_of(x_ref, at_ref, index, deep), pairs[index // 2][index % 2])
-        query = new if query is None else query + new
-    out_ref[...] = query
+    for tile in tiles_of(out_ref):
+        query = None
+        for index in range(2 * len(pairs)):
+            x = columns_of(x_ref, at_ref, index, deep)
+            new = dot(x, pairs[index // 2][index % 2, :, tile])
+            query = new if query is None else query + new
+        out_ref[:, tile] = query
 
 
 def gate_kernel(at_ref, x_ref, filtered_ref, partial_ref, *refs):
     pieces, out_ref = refs[:-1], refs[-1]
     deep = pieces[0].shape[0]
-    query = partial_ref[...]
-    for index, piece in enumerate(pieces):
-        query = query + dot(columns_of(x_ref, at_ref, index, deep), piece[...])
-    out_ref[...] = (query.astype(BF16).astype(F32) * filtered_ref[...]).astype(BF16)
-
-
-def project(kernel, at, x, extra, pieces, out_dtype):
-    length, model = x.shape
-    half = pieces[0].shape[-1]
-    tile = math.gcd(half, 256)
-    lead = pieces[0].shape[:-1]
-    count = 2 if len(lead) == 2 else 1
-    out = jax.ShapeDtypeStruct((length, half), out_dtype)
-    by_tile = pl.BlockSpec((length, tile), lambda j, at: (0, j))
+    for tile in tiles_of(out_ref):
+        query = partial_ref[:, tile]
+        for index, piece in enumerate(pieces):
+            query = query + dot(columns_of(x_ref, at_ref, index, deep), piece[:, tile])
+        out_ref[:, tile] = (query.astype(BF16).astype(F32) * filtered_ref[:, tile]).astype(BF16)
+
+
+def call(kernel, scalars, operands, out, scratch=()):
     return pl.pallas_call(
         kernel,
         out_shape=out,
-        grid_spec=pltpu.PrefetchScalarGridSpec(
-            num_scalar_prefetch=1,
-            grid=(half // tile,),
-            in_specs=[pl.BlockSpec((length, model), lambda j, at: (0, 0))]
-            + [by_tile] * len(extra)
-            + [
-                pl.BlockSpec(lead + (tile,), lambda j, at: (0,) * len(lead) + (j,))
-                for _ in pieces
-            ],
-            out_specs=by_tile,
-        ),
+        in_specs=[pl.BlockSpec(memory_space=pltpu.SMEM)] + [WHOLE] * len(operands),
+        out_specs=jax.tree.map(lambda _: WHOLE, out),
+        scratch_shapes=scratch,
         compiler_params=pltpu.CompilerParams(vmem_limit_bytes=GRANT),
-        cost_estimate=cost(2 * count * length * model * half, x, out, *extra, *pieces),
-    )(at, x, *extra, *pieces)
-
-
-def filter_kernel(product_ref, halo_ref, taps_ref, out_ref, held):
+        cost_estimate=pl.CostEstimate(flops=1, bytes_accessed=1, transcendentals=0),
+    )(scalars, *operands)
+
+
+def project(kernel, at, x, extra, pieces, out_dtype):
+    half = pieces[0].shape[-1]
+    out = jax.ShapeDtypeStruct((x.shape[0], half), out_dtype)
+    return call(kernel, at, (x, *extra, *pieces), out)
+
+
+def filter_kernel(_, product_ref, halo_ref, taps_ref, out_ref, held):
     length, pad = product_ref.shape[0], halo_ref.shape[0]
     held[:pad] = halo_ref[...]
     held[pad:] = product_ref[...]
-    total = None
-    for offset in range(taps_ref.shape[0]):
-        term = taps_ref[offset : offset + 1] * held[pad - offset : pad - offset + length]
-        total = term if total is None else total + term
-    out_ref[...] = total
-
-
-def causal_filter(product, halo, taps):
+    for tile in tiles_of(out_ref):
+        total = None
+        for offset in range(taps_ref.shape[0]):
+            term = taps_ref[offset : offset + 1, tile] * held[pad - offset : pad - offset + length, tile]
+            total = term if total is None else total + term
+        out_ref[:, tile] = total
+
+
+def causal_filter(at, product, halo, taps):
     length, half = product.shape
-    pad = halo.shape[0]
-    tile = math.gcd(half, 256)
-    return pl.pallas_call(
-        filter_kernel,
-        out_shape=jax.ShapeDtypeStruct(product.shape, F32),
-        grid=(half // tile,),
-        in_specs=[
-            pl.BlockSpec((rows, tile), lambda j: (0, j)) for rows in (length, pad, taps.shape[0])
-        ],
-        out_specs=pl.BlockSpec((length, tile), lambda j: (0, j)),
-        scratch_shapes=[pltpu.VMEM((pad + length, tile), F32)],
-        compiler_params=pltpu.CompilerParams(vmem_limit_bytes=GRANT),
-        cost_estimate=cost(14 * length * half, product, product),
-    )(product, halo, taps)
-
-
-def terms_kernel(count, order, n_tp, z_ref, gated_ref, *refs):
-    pairs, refs, held = refs[:count], refs[count:-1], refs[-1]
-    given, outs = (refs[0], refs[1:]) if len(refs) > 1 else (None, refs)
+    out = jax.ShapeDtypeStruct(product.shape, F32)
+    scratch = [pltpu.VMEM((halo.shape[0] + length, half), F32)]
+    return call(filter_kernel, at, (product, halo, taps), out, scratch)
+
+
+def terms_kernel(count, order, turned, n_tp, z_ref, gated_ref, *refs):
+    pairs, refs = refs[:count], refs[count:]
     length = gated_ref.shape[0]
     rows = length // n_tp
-    for slot in range(n_tp):
-        owner = lax.rem(z_ref[0] + slot, n_tp)
-        held[slot * rows : (slot + 1) * rows] = gated_ref[
-            pl.ds(pl.multiple_of(owner * rows, rows), rows)
-        ]
+    held = gated_ref
+    if turned:
+        refs, held = refs[:-1], refs[-1]
+        for slot in range(n_tp):
+            owner = lax.rem(z_ref[0] + slot, n_tp)
+            held[slot * rows : (slot + 1) * rows] = gated_ref[
+                pl.ds(pl.multiple_of(owner * rows, rows), rows)
+            ]
+    given, outs = (refs[0], refs[1:]) if len(refs) > 1 else (None, refs)
     wide = pairs[0].shape[2]
     for index, (pair, side) in enumerate((p, s) for p in pairs for s in order):
         at = slice(index * wide, (index + 1) * wide)
         total = dot(held[...], pair[side])
-        if given is None:
-            outs[0][:, at] = total.astype(BF16)
-        else:
+        if given is not None:
             total = total + given[:, at].astype(F32)
-            for slot in range(n_tp):
-                outs[slot][:, at] = total[slot * rows : (slot + 1) * rows].astype(BF16)
-
-
-def terms(n_tp, z, gated, pairs, order, given=None):
+        share = length // len(outs)
+        for slot, out in enumerate(outs):
+            out[:, at] = total[slot * share : (slot + 1) * share].astype(BF16)
+
+
+def terms(n_tp, z, gated, pairs, order, turned, given=None):
     length, half = gated.shape
     cols = len(pairs) * 2 * pairs[0].shape[2]
-    if given is None:
-        out = [jax.ShapeDtypeStruct((length, cols), BF16)]
-    else:
-        out = [jax.ShapeDtypeStruct((length // n_tp, cols), BF16)] * n_tp
-    extra = [] if given is None else [given]
-    result = pl.pallas_call(
-        functools.partial(terms_kernel, len(pairs), order, n_tp),
-        out_shape=out,
-        grid=(1,),
-        in_specs=[pl.BlockSpec(memory_space=pltpu.SMEM)]
-        + [whole(a) for a in (gated, *pairs, *extra)],
-        out_specs=[whole(a) for a in out],
-        scratch_shapes=[pltpu.VMEM((length, half), BF16)],
-        compiler_params=pltpu.CompilerParams(vmem_limit_bytes=GRANT),
-        cost_estimate=cost(2 * length * half * cols, gated, *pairs, *extra, *out),
-    )(z, gated, *pairs, *extra)
-    return result[0] if given is None else result
+    slots = n_tp if turned and given is not None else 1
+    out = [jax.ShapeDtypeStruct((length // slots, cols), BF16)] * slots
+    kernel = functools.partial(terms_kernel, len(pairs), order, turned, n_tp)
+    extra = () if given is None else (given,)
+    scratch = [pltpu.VMEM((length, half), BF16)] if turned else []
+    result = call(kernel, z, (gated, *pairs, *extra), out, scratch)
+    return result if slots > 1 else result[0]
 
 
 def on_device(tokens, norm_gain, in_weight, filters, out_weight, keep_mask):
@@ -279,8 +253,8 @@
     taps = jnp.repeat(
         lax.dynamic_slice_in_dim(filters, core * groups, groups, axis=1), half // groups, axis=1
     )
-    own_filtered = causal_filter(own_product, jnp.where(core == 0, rim, first_tail), taps)
-    other_filtered = causal_filter(other_product, jnp.where(core == 0, first_tail, rim), taps)
+    own_filtered = causal_filter(at, own_product, jnp.where(core == 0, rim, first_tail), taps)
+    other_filtered = causal_filter(at, other_product, jnp.where(core == 0, first_tail, rim), taps)
 
     ready = (own_filtered, other_filtered, own_query, other_query)
     both_o, q_rest, ready = lax.optimization_barrier((both_o, q_rest, ready))
@@ -301,25 +275,35 @@
     def plus(a, b):
         return (a.astype(F32) + b.astype(F32)).astype(BF16)
 
-    def summed(pairs, own_gated, other_gated):
-        leaving = terms(n_tp, z, other_gated, pairs, (1, 0))
-        slots = terms(n_tp, z, own_gated, pairs, (0, 1), from_partner(leaving))
-        rising = falling = first = None
+    def terms_of(pairs, gates, turned):
+        own, other = gates
+        leaving = terms(n_tp, z, other, pairs, (1, 0), turned)
+        return terms(n_tp, z, own, pairs, (0, 1), turned, from_partner(leaving))
+
+    def chained(slots):
+        rising = falling = hop = None
         for step in range(n_tp - 1):
             send_up, send_down = slots[n_tp - 1 - step], slots[step + 1]
             if step:
                 send_up, send_down = plus(send_up, rising), plus(send_down, falling)
             rising = lax.ppermute(send_up, "tp", up)
             falling = lax.ppermute(send_down, "tp", down)
-            first = (rising, falling) if step == 0 else first
-        return slots[0].astype(F32) + rising.astype(F32) + falling.astype(F32), first
+            hop = hop or (rising, falling)
+        total = slots[0].astype(F32) + rising.astype(F32) + falling.astype(F32)
+        return total, hop
 
     o_rest = {(dy, dx): from_chip(o_x[0, dx], dy, 0) for dy, _ in o_y for _, dx in o_x}
     out_pairs = {(0, 0): both_o, **o_x, **o_y, **o_rest}
     result = jnp.zeros((rows, model), BF16)
-    for keys in ([(0, 0)], [*o_x, *o_y], list(o_rest)):
-        mixed, done = summed([out_pairs[key] for key in keys], own_gated, other_gated)
-        own_gated, other_gated, _ = lax.optimization_barrier((own_gated, other_gated, done))
+    gates = (own_gated, other_gated)
+    sets = [(0, 0)], [*o_x, *o_y], list(o_rest)
+    first_sum, hop = chained(terms_of([out_pairs[key] for key in sets[0]], gates, True))
+    gates, _ = lax.optimization_barrier((gates, hop))
+    middle = terms_of([out_pairs[key] for key in sets[1]], gates, False)
+    gates, middle = lax.optimization_barrier((gates, middle))
+    middle_sum = lax.psum_scatter(middle, "tp", scatter_dimension=0, tiled=True).astype(F32)
+    last_sum, _ = chained(terms_of([out_pairs[key] for key in sets[2]], gates, True))
+    for keys, mixed in zip(sets, (first_sum, middle_sum, last_sum)):
         for index, (dy, dx) in enumerate(keys):
             start = place(my_y + dy, my_x + dx, 0) * wide
             pair = mixed[:, index * 2 * wide : (index + 1) * 2 * wide]

time: 326 us -> 280 us (0.86)
  Pallas kernels: 73.4 us -> 34.1 us
  starting transfers between devices: 68.3 us -> 54.5 us
  other arithmetic: 15.9 us -> 6.95 us
  local copies, waits for them, and re-layouts: 15.4 us -> 24.2 us
  waiting for transfers between devices: 138 us -> 145 us
    pallas_call x14, Pallas kernels: 73.4 us -> 34.1 us  [call(): pl.pallas_call(kernel, out_shape=out, in_specs=[pl.BlockSpec(memory_space...]
    ppermute x13, waiting for transfers between devices: 86.5 us -> 108 us  [from_chip(): return lax.ppermute(block, 'seq', route)]
    ppermute x18 -> x12, starting transfers between devices: 49.3 us -> 34.8 us  [the longest x6 27.1 us: chained(): rising = lax.ppermute(send_up, 'tp', up)]
    ppermute x18 -> x12, waiting for transfers between devices: 45.1 us -> 31.5 us  [the longest x6 16.9 us: chained(): rising = lax.ppermute(send_up, 'tp', up)]
    unnamed x80 -> x70, local copies, waits for them, and re-layouts: 6.99 us -> 15.8 us
    convert_element_type x9 -> x6, other arithmetic: 5.43 us -> 1.28 us  [plus(): return (a.astype(F32) + b.astype(F32)).astype(BF16)]
  transfers between devices with their start and end apart: 40 -> 35, of which waited for: 23 -> 22; matrix products, arithmetic and copies ran while one was open for 6% -> 3% of each run, Pallas kernels for 17% -> 10%
where the time goes in v4:
time: 280 us; the launch traced here: 279 us
  waiting for transfers between devices  145 us (52%)
  starting transfers between devices  54.5 us (19%)
  Pallas kernels  34.1 us (12%)
  local copies, waits for them, and re-layouts  24.2 us (9%)
  between operations  14.2 us (5%)
  other arithmetic  6.95 us (2%)
    ppermute x13, waiting for transfers between devices, from_chip(): return lax.ppermute(block, 'seq', route)  108 us
    pallas_call x14, Pallas kernels, call(): pl.pallas_call(kernel, out_shape=out, in_specs=[pl.BlockSpec(memory_space...  34.1 us
    ppermute x6, starting transfers between devices, chained(): rising = lax.ppermute(send_up, 'tp', up)  27.1 us
    ppermute x6, waiting for transfers between devices, chained(): rising = lax.ppermute(send_up, 'tp', up)  16.9 us
    unnamed x70, local copies, waits for them, and re-layouts  15.8 us
    ppermute x13, starting transfers between devices, from_chip(): return lax.ppermute(block, 'seq', route)  15.7 us
    ppermute x6, waiting for transfers between devices, chained(): falling = lax.ppermute(send_down, 'tp', down)  14.5 us
    ppermute x6, starting transfers between devices, chained(): falling = lax.ppermute(send_down, 'tp', down)  7.75 us
  transfers between devices with their start and end apart: 35, of which 22 were waited for; matrix products, arithmetic and copies ran while one was open for 3% of the time, Pallas kernels for 10%

profile of v4, /device:TPU:0, one launch (start us, length us, event | category | flops | bytes accessed | tf_op | source)
XLA Modules:
  0.0 279.2 jit_solution(11824320520717292027)
XLA Ops:
  6.5 1.8 constant_dynamic-slice_fusion.3
  8.7 1.3 fusion.2
  10.6 2.6 collective-permute-start.1
  13.2 1.5 collective-permute-start.3
  15.8 1.5 collective-permute-start.4
  17.3 1.3 constant_dynamic-slice_fusion.2
  18.6 1.9 collective-permute-done.5
  20.6 16.5 %collective-permute-done.1.refs_2_ = bf16[2,512,512]{2,1,0:T(8,128)(2,1)S(1)} collective-permute-done((bf16[2,512,512]{2,1,0:T(8,128)(2,1)S(1)}, bf16[2,512,512]{2,1,0:T(8,128)(2,1)S(1)}, u32[]{:S(2)}, u32[]{:S(2)}) %collective-permute-start.1) | collective-permute-done | bytes 1048608 | tf_op jit(solution)/shard_map/ppermute | solution.py:166
  37.2 2.0 collective-permute-done.3.refs_4_
  40.2 19.2 %collective-permute-done.2.refs_3_ = bf16[2,512,512]{2,1,0:T(8,128)(2,1)S(1)} collective-permute-done((bf16[2,512,512]{2,1,0:T(8,128)(2,1)S(1)}, bf16[2,512,512]{2,1,0:T(8,128)(2,1)S(1)}, u32[]{:S(2)}, u32[]{:S(2)}) %collective-permute-start.2) | collective-permute-done | bytes 1048608 | tf_op jit(solution)/shard_map/ppermute | solution.py:166
  60.9 1.5 collective-permute-start.6
  63.4 1.3 collective-permute-start.7
  66.9 20.1 %collective-permute-done.6.refs_6_ = bf16[2,512,512]{2,1,0:T(8,128)(2,1)S(1)} collective-permute-done((bf16[2,512,512]{2,1,0:T(8,128)(2,1)S(1)}, bf16[2,512,512]{2,1,0:T(8,128)(2,1)S(1)}, u32[]{:S(2)}, u32[]{:S(2)}) %collective-permute-start.6) | collective-permute-done | bytes 1048608 | tf_op jit(solution)/shard_map/ppermute | solution.py:166
  88.0 1.5 collective-permute-done.7.refs_7_
  90.5 19.7 %collective-permute-done.8.refs_1_ = bf16[2,512,512]{2,1,0:T(8,128)(2,1)S(1)} collective-permute-done((bf16[2,512,512]{2,1,0:T(8,128)(2,1)S(1)}, bf16[2,512,512]{2,1,0:T(8,128)(2,1)S(1)}, u32[]{:S(2)}, u32[]{:S(2)}) %collective-permute-start.8) | collective-permute-done | bytes 1048608 | tf_op jit(solution)/shard_map/ppermute | solution.py:166
  110.2 2.3 dynamic-slice_bitcast_fusion
  114.0 1.1 slice_bitcast_fusion
  115.1 1.6 collective-permute-start.12
  116.7 2.2 copy-done.2
  118.9 1.2 copy-done.9
  120.1 1.2 copy-done.11
  121.3 1.2 copy-done.13
  122.5 1.2 copy-done.15
  123.8 1.2 copy-done.17
  125.0 5.0 %shard_map.64.product_ref = f32[512,512]{1,0:T(8,128)S(1)} custom-call(s32[8]{0:T(128)S(1)} %stack.58.at_ref._, bf16[512,4096]{1,0:T(8,128)(2,1)S(1)} %copy-done.2, bf16[2,512,512]{2,1,0:T(8,128)(2,1)S(1)} %get-tuple-element.59.refs_0_, bf16[2,512,512]{2,1,0:T(8,128)(2,1)S(1)} %copy-done.5, bf16[2,512,512]{2,1,0:T(8,128)(2,1)S(1)} %copy-done.7, ...), custom_call_target="tpu_custom_call" | custom-call | flops 1 | bytes 1 | tf_op jit(solution)/shard_map/pallas_call | solution.py:71
  130.0 6.8 %shard_map.65.product_ref = f32[512,512]{1,0:T(8,128)S(1)} custom-call(s32[8]{0:T(128)S(1)} %stack.58.at_ref._, bf16[512,4096]{1,0:T(8,128)(2,1)} %collective-permute-done.13.x_ref, bf16[2,512,512]{2,1,0:T(8,128)(2,1)S(1)} %get-tuple-element.59.refs_0_, bf16[2,512,512]{2,1,0:T(8,128)(2,1)S(1)} %copy-done.5, bf16[2,512,512]{2,1,0:T(8,128)(2,1)S(1)} %copy-done.7, ...), custom_call_target="tpu_custom_call" | custom-call | flops 1 | bytes 1 | tf_op jit(solution)/shard_map/pallas_call | solution.py:71
  136.9 2.6 collective-permute-start.14
  139.5 1.1 pad_maximum_fusion.1.refs_0_
  140.7 3.0 %shard_map.68.partial_ref = f32[512,512]{1,0:T(8,128)S(1)} custom-call(s32[8]{0:T(128)S(1)} %stack.58.at_ref._, bf16[512,4096]{1,0:T(8,128)(2,1)S(1)} %copy-done.3, bf16[2,512,512]{2,1,0:T(8,128)(2,1)S(1)} %pad_maximum_fusion.refs_0_, bf16[2,512,512]{2,1,0:T(8,128)(2,1)S(1)} %collective-permute-done.8.refs_1_, ...), custom_call_target="tpu_custom_call" | custom-call | flops 1 | bytes 1 | tf_op jit(solution)/shard_map/pallas_call | solution.py:71
  143.7 4.3 %shard_map.69.partial_ref = f32[512,512]{1,0:T(8,128)S(1)} custom-call(s32[8]{0:T(128)S(1)} %stack.58.at_ref._, bf16[512,4096]{1,0:T(8,128)(2,1)} %collective-permute-done.13.x_ref, bf16[2,512,512]{2,1,0:T(8,128)(2,1)S(1)} %pad_maximum_fusion.refs_0_, bf16[2,512,512]{2,1,0:T(8,128)(2,1)S(1)} %collective-permute-done.8.refs_1_, ...), custom_call_target="tpu_custom_call" | custom-call | flops 1 | bytes 1 | tf_op jit(solution)/shard_map/pallas_call | solution.py:71
  148.0 2.0 shard_map.67.filtered_ref
  150.1 2.0 shard_map.66.filtered_ref
  152.1 2.9 %shard_map.71.gated_ref = bf16[512,512]{1,0:T(8,128)(2,1)S(1)} custom-call(s32[2]{0:T(128)S(1)} %pad_add_fusion.at_ref, bf16[512,4096]{1,0:T(8,128)(2,1)} %collective-permute-done.13.x_ref, f32[512,512]{1,0:T(8,128)S(1)} %shard_map.67.filtered_ref, f32[512,512]{1,0:T(8,128)S(1)} %shard_map.69.partial_ref, ...), custom_call_target="tpu_custom_call" | custom-call | flops 1 | bytes 1 | tf_op jit(solution)/shard_map/pallas_call | solution.py:71
  155.9 2.6 collective-permute-start.22
  158.4 1.3 shard_map.70.gated_ref
  160.4 3.5 %collective-permute-start.16 = (bf16[128,1024]{1,0:T(8,128)(2,1)S(1)}, bf16[128,1024]{1,0:T(8,128)(2,1)S(1)}, u32[]{:S(2)}, u32[]{:S(2)}) collective-permute-start(bf16[128,1024]{1,0:T(8,128)(2,1)S(1)} %get-tuple-element.77), channel_id=1, source_target_pairs={{0,1},{1,2},{2,3},{4,5},{5,6},{6,7},{8,9},{9,10},{10,11},{12,13},{... | collective-permute-start | bytes 786440 | tf_op jit(solution)/shard_map/ppermute | solution.py:289
  163.9 1.3 collective-permute-start.19
  165.2 4.6 %collective-permute-done.16 = bf16[128,1024]{1,0:T(8,128)(2,1)S(1)} collective-permute-done((bf16[128,1024]{1,0:T(8,128)(2,1)S(1)}, bf16[128,1024]{1,0:T(8,128)(2,1)S(1)}, u32[]{:S(2)}, u32[]{:S(2)}) %collective-permute-start.16) | collective-permute-done | bytes 262176 | tf_op jit(solution)/shard_map/ppermute | solution.py:289
  169.8 4.1 %collective-permute-done.19 = bf16[128,1024]{1,0:T(8,128)(2,1)S(1)} collective-permute-done((bf16[128,1024]{1,0:T(8,128)(2,1)S(1)}, bf16[128,1024]{1,0:T(8,128)(2,1)S(1)}, u32[]{:S(2)}, u32[]{:S(2)}) %collective-permute-start.19) | collective-permute-done | bytes 262176 | tf_op jit(solution)/shard_map/ppermute | solution.py:290
  173.9 8.2 %collective-permute-done.22.refs_0_ = bf16[2,512,512]{2,1,0:T(8,128)(2,1)S(1)} collective-permute-done((bf16[2,512,512]{2,1,0:T(8,128)(2,1)S(1)}, bf16[2,512,512]{2,1,0:T(8,128)(2,1)S(1)}, u32[]{:S(2)}, u32[]{:S(2)}) %collective-permute-start.22) | collective-permute-done | bytes 1048608 | tf_op jit(solution)/shard_map/ppermute | solution.py:166
  182.2 1.5 collective-permute-done.23.refs_1_
  183.6 1.3 shard_map.74
  185.4 3.8 %collective-permute-done.24.refs_2_ = bf16[512,2048]{1,0:T(8,128)(2,1)S(1)} collective-permute-done((bf16[512,2048]{1,0:T(8,128)(2,1)S(1)}, bf16[512,2048]{1,0:T(8,128)(2,1)S(1)}, u32[]{:S(2)}, u32[]{:S(2)}) %collective-permute-start.24) | collective-permute-done | bytes 2097184 | tf_op jit(solution)/shard_map/ppermute | solution.py:169
  189.2 2.6 shard_map.75
  191.8 18.8 %collective-permute-done.25.refs_0_ = bf16[2,512,512]{2,1,0:T(8,128)(2,1)S(1)} collective-permute-done((bf16[2,512,512]{2,1,0:T(8,128)(2,1)S(1)}, bf16[2,512,512]{2,1,0:T(8,128)(2,1)S(1)}, u32[]{:S(2)}, u32[]{:S(2)}) %collective-permute-start.25) | collective-permute-done | bytes 1048608 | tf_op jit(solution)/shard_map/ppermute | solution.py:166
  211.6 3.5 %collective-permute-start.17 = (bf16[128,1024]{1,0:T(8,128)(2,1)S(1)}, bf16[128,1024]{1,0:T(8,128)(2,1)S(1)}, u32[]{:S(2)}, u32[]{:S(2)}) collective-permute-start(bf16[128,1024]{1,0:T(8,128)(2,1)S(1)} %get-tuple-element.105), channel_id=1, source_target_pairs={{0,1},{1,2},{2,3},{4,5},{5,6},{6,7},{8,9},{9,10},{10,11},{12,13},{... | collective-permute-start | bytes 786440 | tf_op jit(solution)/shard_map/ppermute | solution.py:289
  215.1 1.3 collective-permute-start.20
  217.1 4.6 %collective-permute-start.27 = (bf16[128,1024]{1,0:T(8,128)(2,1)S(1)}, bf16[128,1024]{1,0:T(8,128)(2,1)S(1)}, u32[]{:S(2)}, u32[]{:S(2)}) collective-permute-start(bf16[128,1024]{1,0:T(8,128)(2,1)S(1)} %get-tuple-element.86), channel_id=1, source_target_pairs={{0,1},{1,2},{2,3},{4,5},{5,6},{6,7},{8,9},{9,10},{10,11},{12,13},{... | collective-permute-start | bytes 786440 | tf_op jit(solution)/shard_map/ppermute | solution.py:289
  221.7 1.3 collective-permute-start.30
  223.0 4.4 %collective-permute-done.17 = bf16[128,1024]{1,0:T(8,128)(2,1)S(1)} collective-permute-done((bf16[128,1024]{1,0:T(8,128)(2,1)S(1)}, bf16[128,1024]{1,0:T(8,128)(2,1)S(1)}, u32[]{:S(2)}, u32[]{:S(2)}) %collective-permute-start.17) | collective-permute-done | bytes 262176 | tf_op jit(solution)/shard_map/ppermute | solution.py:289
  227.5 7.3 %collective-permute-start.18 = (bf16[128,1024]{1,0:T(8,128)(2,1)S(1)}, bf16[128,1024]{1,0:T(8,128)(2,1)S(1)}, u32[]{:S(2)}, u32[]{:S(2)}) collective-permute-start(bf16[128,1024]{1,0:T(8,128)(2,1)S(1)} %add_convert_fusion.3), channel_id=1, source_target_pairs={{0,1},{1,2},{2,3},{4,5},{5,6},{6,7},{8,9},{9,10},{10,11},{12,13},{... | collective-permute-start | bytes 786440 | tf_op jit(solution)/shard_map/ppermute | solution.py:289
  234.8 1.1 collective-permute-done.20
  236.0 1.3 collective-permute-start.21
  237.3 1.4 collective-permute-done.27
  238.6 5.0 %collective-permute-done.30 = bf16[128,1024]{1,0:T(8,128)(2,1)S(1)} collective-permute-done((bf16[128,1024]{1,0:T(8,128)(2,1)S(1)}, bf16[128,1024]{1,0:T(8,128)(2,1)S(1)}, u32[]{:S(2)}, u32[]{:S(2)}) %collective-permute-start.30) | collective-permute-done | bytes 262176 | tf_op jit(solution)/shard_map/ppermute | solution.py:290
  244.5 3.9 %collective-permute-start.28 = (bf16[128,1024]{1,0:T(8,128)(2,1)}, bf16[128,1024]{1,0:T(8,128)(2,1)S(1)}, u32[]{:S(2)}, u32[]{:S(2)}) collective-permute-start(bf16[128,1024]{1,0:T(8,128)(2,1)} %get-tuple-element.103), channel_id=1, source_target_pairs={{0,1},{1,2},{2,3},{4,5},{5,6},{6,7},{8,9},{9,10},{10,11},{12,13},{... | collective-permute-start | bytes 786440 | tf_op jit(solution)/shard_map/ppermute | solution.py:289
  248.4 1.3 collective-permute-start.31
  250.0 4.5 %collective-permute-done.28 = bf16[128,1024]{1,0:T(8,128)(2,1)S(1)} collective-permute-done((bf16[128,1024]{1,0:T(8,128)(2,1)}, bf16[128,1024]{1,0:T(8,128)(2,1)S(1)}, u32[]{:S(2)}, u32[]{:S(2)}) %collective-permute-start.28) | collective-permute-done | bytes 262176 | tf_op jit(solution)/shard_map/ppermute | solution.py:289
  254.5 4.3 %collective-permute-start.29 = (bf16[128,1024]{1,0:T(8,128)(2,1)S(1)}, bf16[128,1024]{1,0:T(8,128)(2,1)S(1)}, u32[]{:S(2)}, u32[]{:S(2)}) collective-permute-start(bf16[128,1024]{1,0:T(8,128)(2,1)S(1)} %add_convert_fusion.1), channel_id=1, source_target_pairs={{0,1},{1,2},{2,3},{4,5},{5,6},{6,7},{8,9},{9,10},{10,11},{12,13},{... | collective-permute-start | bytes 786440 | tf_op jit(solution)/shard_map/ppermute | solution.py:289
  258.9 1.3 collective-permute-start.32
  260.4 1.2 fusion.24
  261.6 2.1 collective-permute-done.29
  263.8 4.2 %collective-permute-done.32 = bf16[128,1024]{1,0:T(8,128)(2,1)S(1)} collective-permute-done((bf16[128,1024]{1,0:T(8,128)(2,1)S(1)}, bf16[128,1024]{1,0:T(8,128)(2,1)S(1)}, u32[]{:S(2)}, u32[]{:S(2)}) %collective-permute-start.32) | collective-permute-done | bytes 262176 | tf_op jit(solution)/shard_map/ppermute | solution.py:290
  268.2 1.4 fusion.28
  (126 shorter events, 19.4 us)
Async XLA Ops:
  6.5 106.4 %copy-start = (f32[7,64]{1,0:T(8,128)S(1)}, f32[7,64]{1,0:T(8,128)}, u32[]{:S(2)}) copy-start(f32[7,64]{1,0:T(8,128)} %param.9) | copy-start | bytes 5380
  6.5 103.6 %all-gather.2.cloned.1.call-start = ((), (), s32[]{:S(2)}) async-start(), calls=%async_computation.1 | async-start | bytes 5242880 | tf_op jit(solution)/shard_map/all_gather | solution.py:207
  6.5 1.9 copy-start.24
  6.5 2.2 copy-start.34
  10.0 258.1 %reduce-scatter.2.cloned.1.call-start = ((), (), s32[]{:S(2)}) async-start(), calls=%async_computation.2 | async-start | bytes 2621440 | tf_op jit(solution)/shard_map/reduce_scatter | solution.py:304
  10.1 4.6 %collective-permute-start = (bf16[2,512,512]{2,1,0:T(8,128)(2,1)S(1)}, bf16[2,512,512]{2,1,0:T(8,128)(2,1)S(1)}, u32[]{:S(2)}, u32[]{:S(2)}) collective-permute-start(bf16[2,512,512]{2,1,0:T(8,128)(2,1)S(1)} %get-tuple-element.90), channel_id=1, source_target_pairs={{0,4},{4,0},{8,12},{12,8},{16,20},{20,16},{24,28},{28,24},{1,5},{5... | collective-permute-start | bytes 3145736 | tf_op jit(solution)/shard_map/ppermute | solution.py:169
  10.6 26.6 %collective-permute-start.1 = (bf16[2,512,512]{2,1,0:T(8,128)(2,1)S(1)}, bf16[2,512,512]{2,1,0:T(8,128)(2,1)S(1)}, u32[]{:S(2)}, u32[]{:S(2)}) collective-permute-start(bf16[2,512,512]{2,1,0:T(8,128)(2,1)S(1)} %get-tuple-element.59.refs_0_), channel_id=1, source_target_pairs={{8,0},{12,4},{0,8},{4,12},{24,16},{28,20},{16,24},{20,28},{9,1},{1... | collective-permute-start | bytes 3145736 | tf_op jit(solution)/shard_map/ppermute | solution.py:166
  13.2 26.0 %collective-permute-start.3 = (bf16[2,512,512]{2,1,0:T(8,128)(2,1)S(1)}, bf16[2,512,512]{2,1,0:T(8,128)(2,1)S(1)}, u32[]{:S(2)}, u32[]{:S(2)}) collective-permute-start(bf16[2,512,512]{2,1,0:T(8,128)(2,1)S(1)} %get-tuple-element.59.refs_0_), channel_id=1, source_target_pairs={{16,0},{20,4},{24,8},{28,12},{0,16},{4,20},{8,24},{12,28},{17,1},{... | collective-permute-start | bytes 3145736 | tf_op jit(solution)/shard_map/ppermute | solution.py:166
  14.7 5.9 %copy-start.4 = (bf16[2,512,512]{2,1,0:T(8,128)(2,1)}, bf16[2,512,512]{2,1,0:T(8,128)(2,1)S(1)}, u32[]{:S(2)}) copy-start(bf16[2,512,512]{2,1,0:T(8,128)(2,1)S(1)} %collective-permute-done.refs_1_) | copy-start | bytes 3145732
  14.7 44.7 %collective-permute-start.2 = (bf16[2,512,512]{2,1,0:T(8,128)(2,1)S(1)}, bf16[2,512,512]{2,1,0:T(8,128)(2,1)S(1)}, u32[]{:S(2)}, u32[]{:S(2)}) collective-permute-start(bf16[2,512,512]{2,1,0:T(8,128)(2,1)S(1)} %collective-permute-done.refs_1_), channel_id=1, source_target_pairs={{8,0},{12,4},{0,8},{4,12},{24,16},{28,20},{16,24},{20,28},{9,1},{1... | collective-permute-start | bytes 3145736 | tf_op jit(solution)/shard_map/ppermute | solution.py:166
  15.8 45.1 %collective-permute-start.4 = (bf16[2,512,512]{2,1,0:T(8,128)(2,1)S(1)}, bf16[2,512,512]{2,1,0:T(8,128)(2,1)S(1)}, u32[]{:S(2)}, u32[]{:S(2)}) collective-permute-start(bf16[2,512,512]{2,1,0:T(8,128)(2,1)S(1)} %collective-permute-done.refs_1_), channel_id=1, source_target_pairs={{16,0},{20,4},{24,8},{28,12},{0,16},{4,20},{8,24},{12,28},{17,1},{... | collective-permute-start | bytes 3145736 | tf_op jit(solution)/shard_map/ppermute | solution.py:166
  18.5 2.0 collective-permute-start.5
  39.2 1.0 copy-start.8
  60.9 26.1 %collective-permute-start.6 = (bf16[2,512,512]{2,1,0:T(8,128)(2,1)S(1)}, bf16[2,512,512]{2,1,0:T(8,128)(2,1)S(1)}, u32[]{:S(2)}, u32[]{:S(2)}) collective-permute-start(bf16[2,512,512]{2,1,0:T(8,128)(2,1)S(1)} %collective-permute-done.1.refs_2_), channel_id=1, source_target_pairs={{16,0},{20,4},{24,8},{28,12},{0,16},{4,20},{8,24},{12,28},{17,1},{... | collective-permute-start | bytes 3145736 | tf_op jit(solution)/shard_map/ppermute | solution.py:166
  63.4 26.1 %collective-permute-start.7 = (bf16[2,512,512]{2,1,0:T(8,128)(2,1)S(1)}, bf16[2,512,512]{2,1,0:T(8,128)(2,1)S(1)}, u32[]{:S(2)}, u32[]{:S(2)}) collective-permute-start(bf16[2,512,512]{2,1,0:T(8,128)(2,1)S(1)} %collective-permute-done.4.refs_5_), channel_id=1, source_target_pairs={{8,0},{12,4},{0,8},{4,12},{24,16},{28,20},{16,24},{20,28},{9,1},{1... | collective-permute-start | bytes 3145736 | tf_op jit(solution)/shard_map/ppermute | solution.py:166
  65.6 44.6 %collective-permute-start.8 = (bf16[2,512,512]{2,1,0:T(8,128)(2,1)S(1)}, bf16[2,512,512]{2,1,0:T(8,128)(2,1)S(1)}, u32[]{:S(2)}, u32[]{:S(2)}) collective-permute-start(bf16[2,512,512]{2,1,0:T(8,128)(2,1)S(1)} %pad_maximum_fusion.refs_0_), channel_id=1, source_target_pairs={{8,0},{12,4},{0,8},{4,12},{24,16},{28,20},{16,24},{20,28},{9,1},{1... | collective-permute-start | bytes 3145736 | tf_op jit(solution)/shard_map/ppermute | solution.py:166
  66.4 43.8 %collective-permute-start.9 = (bf16[2,512,512]{2,1,0:T(8,128)(2,1)S(1)}, bf16[2,512,512]{2,1,0:T(8,128)(2,1)}, u32[]{:S(2)}, u32[]{:S(2)}) collective-permute-start(bf16[2,512,512]{2,1,0:T(8,128)(2,1)S(1)} %pad_maximum_fusion.refs_0_), channel_id=1, source_target_pairs={{16,0},{20,4},{24,8},{28,12},{0,16},{4,20},{8,24},{12,28},{17,1},{... | collective-permute-start | bytes 3145736 | tf_op jit(solution)/shard_map/ppermute | solution.py:166
  110.2 19.9 %collective-permute-start.13 = (bf16[512,4096]{1,0:T(8,128)(2,1)}, bf16[512,4096]{1,0:T(8,128)(2,1)}, u32[]{:S(2)}, u32[]{:S(2)}) collective-permute-start(bf16[512,4096]{1,0:T(8,128)(2,1)} %all-gather.2.cloned.1.call-done.x_ref), channel_id=1, source_target_pairs={{0,4},{4,0},{8,12},{12,8},{16,20},{20,16},{24,28},{28,24},{1,5},{5... | collective-permute-start | bytes 12582920 | tf_op jit(solution)/shard_map/ppermute | solution.py:169
  112.5 27.0 %collective-permute-start.10 = (bf16[512,512]{1,0:T(8,128)(2,1)}, bf16[512,512]{1,0:T(8,128)(2,1)}, u32[]{:S(2)}, u32[]{:S(2)}) collective-permute-start(bf16[512,512]{1,0:T(8,128)(2,1)} %get-tuple-element.94), channel_id=1, source_target_pairs={{0,4},{4,0},{8,12},{12,8},{16,20},{20,16},{24,28},{28,24},{1,5},{5... | collective-permute-start | bytes 1572872 | tf_op jit(solution)/shard_map/ppermute | solution.py:169
  113.3 3.3 %copy-start.5 = (bf16[2,512,512]{2,1,0:T(8,128)(2,1)S(1)}, bf16[2,512,512]{2,1,0:T(8,128)(2,1)}, u32[]{:S(2)}) copy-start(bf16[2,512,512]{2,1,0:T(8,128)(2,1)} %copy-done.4) | copy-start | bytes 3145732
  113.3 3.3 %copy-start.7 = (bf16[2,512,512]{2,1,0:T(8,128)(2,1)S(1)}, bf16[2,512,512]{2,1,0:T(8,128)(2,1)}, u32[]{:S(2)}) copy-start(bf16[2,512,512]{2,1,0:T(8,128)(2,1)} %copy-done.6) | copy-start | bytes 3145732
  113.5 38.7 %collective-permute-start.11 = (bf16[512,512]{1,0:T(8,128)(2,1)S(1)}, bf16[512,512]{1,0:T(8,128)(2,1)S(1)}, u32[]{:S(2)}, u32[]{:S(2)}) collective-permute-start(bf16[512,512]{1,0:T(8,128)(2,1)S(1)} %slice_bitcast_fusion.1), channel_id=1, source_target_pairs={{16,0},{20,4},{24,8},{28,12},{0,16},{4,20},{8,24},{12,28},{17,1},{... | collective-permute-start | bytes 1572872 | tf_op jit(solution)/shard_map/ppermute | solution.py:166
  115.1 37.1 %collective-permute-start.12 = (bf16[512,512]{1,0:T(8,128)(2,1)S(1)}, bf16[512,512]{1,0:T(8,128)(2,1)S(1)}, u32[]{:S(2)}, u32[]{:S(2)}) collective-permute-start(bf16[512,512]{1,0:T(8,128)(2,1)S(1)} %slice_bitcast_fusion), channel_id=1, source_target_pairs={{8,0},{12,4},{0,8},{4,12},{24,16},{28,20},{16,24},{20,28},{9,1},{1... | collective-permute-start | bytes 1572872 | tf_op jit(solution)/shard_map/ppermute | solution.py:166
  116.7 2.2 copy-start.2
  118.9 1.2 copy-start.9
  120.1 1.2 copy-start.11
  121.3 1.2 copy-start.13
  122.5 1.2 copy-start.15
  123.8 1.2 copy-start.17
  130.0 9.5 %copy-start.28 = (bf16[1,512,512]{2,1,0:T(8,128)(2,1)S(1)}, bf16[1,512,512]{2,1,0:T(8,128)(2,1)}, u32[]{:S(2)}) copy-start(bf16[1,512,512]{2,1,0:T(8,128)(2,1)} %get-tuple-element.93) | copy-start | bytes 1572868
  130.0 10.6 %copy-start.3 = (bf16[512,4096]{1,0:T(8,128)(2,1)S(1)}, bf16[512,4096]{1,0:T(8,128)(2,1)}, u32[]{:S(2)}) copy-start(bf16[512,4096]{1,0:T(8,128)(2,1)} %all-gather.2.cloned.1.call-done.x_ref) | copy-start | bytes 12582916
  136.9 11.1 %collective-permute-start.14 = (f32[8,512]{1,0:T(8,128)S(1)}, f32[8,512]{1,0:T(8,128)S(1)}, u32[]{:S(2)}, u32[]{:S(2)}) collective-permute-start(f32[8,512]{1,0:T(8,128)S(1)} %slice_select_fusion.3), channel_id=1, source_target_pairs={{0,8},{4,12},{8,16},{12,20},{16,24},{20,28},{1,9},{5,13},{9,17},{1... | collective-permute-start | bytes 49160 | tf_op jit(solution)/shard_map/ppermute | solution.py:245
  155.8 3.9 %collective-permute-start.15 = (bf16[512,1024]{1,0:T(8,128)(2,1)S(1)}, bf16[512,1024]{1,0:T(8,128)(2,1)S(1)}, u32[]{:S(2)}, u32[]{:S(2)}) collective-permute-start(bf16[512,1024]{1,0:T(8,128)(2,1)S(1)} %shard_map.72), channel_id=1, source_target_pairs={{0,4},{4,0},{8,12},{12,8},{16,20},{20,16},{24,28},{28,24},{1,5},{5... | collective-permute-start | bytes 3145736 | tf_op jit(solution)/shard_map/ppermute | solution.py:169
  155.9 26.3 %collective-permute-start.22 = (bf16[2,512,512]{2,1,0:T(8,128)(2,1)S(1)}, bf16[2,512,512]{2,1,0:T(8,128)(2,1)S(1)}, u32[]{:S(2)}, u32[]{:S(2)}) collective-permute-start(bf16[2,512,512]{2,1,0:T(8,128)(2,1)S(1)} %pad_maximum_fusion.1.refs_0_), channel_id=1, source_target_pairs={{8,0},{12,4},{0,8},{4,12},{24,16},{28,20},{16,24},{20,28},{9,1},{1... | collective-permute-start | bytes 3145736 | tf_op jit(solution)/shard_map/ppermute | solution.py:166
  158.4 25.2 %collective-permute-start.23 = (bf16[2,512,512]{2,1,0:T(8,128)(2,1)S(1)}, bf16[2,512,512]{2,1,0:T(8,128)(2,1)S(1)}, u32[]{:S(2)}, u32[]{:S(2)}) collective-permute-start(bf16[2,512,512]{2,1,0:T(8,128)(2,1)S(1)} %pad_maximum_fusion.1.refs_0_), channel_id=1, source_target_pairs={{16,0},{20,4},{24,8},{28,12},{0,16},{4,20},{8,24},{12,28},{17,1},{... | collective-permute-start | bytes 3145736 | tf_op jit(solution)/shard_map/ppermute | solution.py:166
  160.4 24.5 %copy-start.18 = (bf16[128,1024]{1,0:T(8,128)(2,1)}, bf16[128,1024]{1,0:T(8,128)(2,1)S(1)}, u32[]{:S(2)}) copy-start(bf16[128,1024]{1,0:T(8,128)(2,1)S(1)} %get-tuple-element.77) | copy-start | bytes 786436
  160.4 24.5 %copy-start.20 = (bf16[128,1024]{1,0:T(8,128)(2,1)}, bf16[128,1024]{1,0:T(8,128)(2,1)S(1)}, u32[]{:S(2)}) copy-start(bf16[128,1024]{1,0:T(8,128)(2,1)S(1)} %get-tuple-element.75) | copy-start | bytes 786436
  160.4 24.5 %copy-start.22 = (bf16[128,1024]{1,0:T(8,128)(2,1)}, bf16[128,1024]{1,0:T(8,128)(2,1)S(1)}, u32[]{:S(2)}) copy-start(bf16[128,1024]{1,0:T(8,128)(2,1)S(1)} %get-tuple-element.76) | copy-start | bytes 786436
  160.4 9.4 %collective-permute-start.16 = (bf16[128,1024]{1,0:T(8,128)(2,1)S(1)}, bf16[128,1024]{1,0:T(8,128)(2,1)S(1)}, u32[]{:S(2)}, u32[]{:S(2)}) collective-permute-start(bf16[128,1024]{1,0:T(8,128)(2,1)S(1)} %get-tuple-element.77), channel_id=1, source_target_pairs={{0,1},{1,2},{2,3},{4,5},{5,6},{6,7},{8,9},{9,10},{10,11},{12,13},{... | collective-permute-start | bytes 786440 | tf_op jit(solution)/shard_map/ppermute | solution.py:289
  163.9 10.0 %collective-permute-start.19 = (bf16[128,1024]{1,0:T(8,128)(2,1)S(1)}, bf16[128,1024]{1,0:T(8,128)(2,1)S(1)}, u32[]{:S(2)}, u32[]{:S(2)}) collective-permute-start(bf16[128,1024]{1,0:T(8,128)(2,1)S(1)} %get-tuple-element.75), channel_id=1, source_target_pairs={{1,0},{2,1},{3,2},{5,4},{6,5},{7,6},{9,8},{10,9},{11,10},{13,12},{... | collective-permute-start | bytes 786440 | tf_op jit(solution)/shard_map/ppermute | solution.py:290
  169.8 15.1 %copy-start.30 = (bf16[128,1024]{1,0:T(8,128)(2,1)}, bf16[128,1024]{1,0:T(8,128)(2,1)S(1)}, u32[]{:S(2)}) copy-start(bf16[128,1024]{1,0:T(8,128)(2,1)S(1)} %collective-permute-done.16) | copy-start | bytes 786436
  173.9 11.0 %copy-start.32 = (bf16[128,1024]{1,0:T(8,128)(2,1)}, bf16[128,1024]{1,0:T(8,128)(2,1)S(1)}, u32[]{:S(2)}) copy-start(bf16[128,1024]{1,0:T(8,128)(2,1)S(1)} %collective-permute-done.19) | copy-start | bytes 786436
  185.0 4.2 %collective-permute-start.24 = (bf16[512,2048]{1,0:T(8,128)(2,1)S(1)}, bf16[512,2048]{1,0:T(8,128)(2,1)S(1)}, u32[]{:S(2)}, u32[]{:S(2)}) collective-permute-start(bf16[512,2048]{1,0:T(8,128)(2,1)S(1)} %shard_map.74), channel_id=1, source_target_pairs={{0,4},{4,0},{8,12},{12,8},{16,20},{20,16},{24,28},{28,24},{1,5},{5... | collective-permute-start | bytes 6291464 | tf_op jit(solution)/shard_map/ppermute | solution.py:169
  185.0 25.6 %collective-permute-start.25 = (bf16[2,512,512]{2,1,0:T(8,128)(2,1)S(1)}, bf16[2,512,512]{2,1,0:T(8,128)(2,1)S(1)}, u32[]{:S(2)}, u32[]{:S(2)}) collective-permute-start(bf16[2,512,512]{2,1,0:T(8,128)(2,1)S(1)} %collective-permute-done.22.refs_0_), channel_id=1, source_target_pairs={{16,0},{20,4},{24,8},{28,12},{0,16},{4,20},{8,24},{12,28},{17,1},{... | collective-permute-start | bytes 3145736 | tf_op jit(solution)/shard_map/ppermute | solution.py:166
  191.8 19.6 %copy-start.23 = (bf16[128,1024]{1,0:T(8,128)(2,1)S(1)}, bf16[128,1024]{1,0:T(8,128)(2,1)}, u32[]{:S(2)}) copy-start(bf16[128,1024]{1,0:T(8,128)(2,1)} %copy-done.22) | copy-start | bytes 786436
  191.8 19.6 %copy-start.31 = (bf16[128,1024]{1,0:T(8,128)(2,1)S(1)}, bf16[128,1024]{1,0:T(8,128)(2,1)}, u32[]{:S(2)}) copy-start(bf16[128,1024]{1,0:T(8,128)(2,1)} %copy-done.30) | copy-start | bytes 786436
  191.8 19.6 %copy-start.33 = (bf16[128,1024]{1,0:T(8,128)(2,1)S(1)}, bf16[128,1024]{1,0:T(8,128)(2,1)}, u32[]{:S(2)}) copy-start(bf16[128,1024]{1,0:T(8,128)(2,1)} %copy-done.32) | copy-start | bytes 786436
  211.3 16.1 %copy-start.21 = (bf16[128,1024]{1,0:T(8,128)(2,1)S(1)}, bf16[128,1024]{1,0:T(8,128)(2,1)}, u32[]{:S(2)}) copy-start(bf16[128,1024]{1,0:T(8,128)(2,1)} %copy-done.20) | copy-start | bytes 786436
  211.3 5.1 %collective-permute-start.26 = (bf16[512,1024]{1,0:T(8,128)(2,1)S(1)}, bf16[512,1024]{1,0:T(8,128)(2,1)S(1)}, u32[]{:S(2)}, u32[]{:S(2)}) collective-permute-start(bf16[512,1024]{1,0:T(8,128)(2,1)S(1)} %shard_map.76), channel_id=1, source_target_pairs={{0,4},{4,0},{8,12},{12,8},{16,20},{20,16},{24,28},{28,24},{1,5},{5... | collective-permute-start | bytes 3145736 | tf_op jit(solution)/shard_map/ppermute | solution.py:169
  211.4 24.4 %copy-start.19 = (bf16[128,1024]{1,0:T(8,128)(2,1)S(1)}, bf16[128,1024]{1,0:T(8,128)(2,1)}, u32[]{:S(2)}) copy-start(bf16[128,1024]{1,0:T(8,128)(2,1)} %copy-done.18) | copy-start | bytes 786436
  211.6 15.8 %collective-permute-start.17 = (bf16[128,1024]{1,0:T(8,128)(2,1)S(1)}, bf16[128,1024]{1,0:T(8,128)(2,1)S(1)}, u32[]{:S(2)}, u32[]{:S(2)}) collective-permute-start(bf16[128,1024]{1,0:T(8,128)(2,1)S(1)} %get-tuple-element.105), channel_id=1, source_target_pairs={{0,1},{1,2},{2,3},{4,5},{5,6},{6,7},{8,9},{9,10},{10,11},{12,13},{... | collective-permute-start | bytes 786440 | tf_op jit(solution)/shard_map/ppermute | solution.py:289
  215.1 20.8 %collective-permute-start.20 = (bf16[128,1024]{1,0:T(8,128)(2,1)S(1)}, bf16[128,1024]{1,0:T(8,128)(2,1)S(1)}, u32[]{:S(2)}, u32[]{:S(2)}) collective-permute-start(bf16[128,1024]{1,0:T(8,128)(2,1)S(1)} %get-tuple-element.106), channel_id=1, source_target_pairs={{1,0},{2,1},{3,2},{5,4},{6,5},{7,6},{9,8},{10,9},{11,10},{13,12},{... | collective-permute-start | bytes 786440 | tf_op jit(solution)/shard_map/ppermute | solution.py:290
  217.1 21.5 %collective-permute-start.27 = (bf16[128,1024]{1,0:T(8,128)(2,1)S(1)}, bf16[128,1024]{1,0:T(8,128)(2,1)S(1)}, u32[]{:S(2)}, u32[]{:S(2)}) collective-permute-start(bf16[128,1024]{1,0:T(8,128)(2,1)S(1)} %get-tuple-element.86), channel_id=1, source_target_pairs={{0,1},{1,2},{2,3},{4,5},{5,6},{6,7},{8,9},{9,10},{10,11},{12,13},{... | collective-permute-start | bytes 786440 | tf_op jit(solution)/shard_map/ppermute | solution.py:289
  221.7 21.9 %collective-permute-start.30 = (bf16[128,1024]{1,0:T(8,128)(2,1)S(1)}, bf16[128,1024]{1,0:T(8,128)(2,1)S(1)}, u32[]{:S(2)}, u32[]{:S(2)}) collective-permute-start(bf16[128,1024]{1,0:T(8,128)(2,1)S(1)} %get-tuple-element.84), channel_id=1, source_target_pairs={{1,0},{2,1},{3,2},{5,4},{6,5},{7,6},{9,8},{10,9},{11,10},{13,12},{... | collective-permute-start | bytes 786440 | tf_op jit(solution)/shard_map/ppermute | solution.py:290
  227.5 22.3 %collective-permute-start.18 = (bf16[128,1024]{1,0:T(8,128)(2,1)S(1)}, bf16[128,1024]{1,0:T(8,128)(2,1)S(1)}, u32[]{:S(2)}, u32[]{:S(2)}) collective-permute-start(bf16[128,1024]{1,0:T(8,128)(2,1)S(1)} %add_convert_fusion.3), channel_id=1, source_target_pairs={{0,1},{1,2},{2,3},{4,5},{5,6},{6,7},{8,9},{9,10},{10,11},{12,13},{... | collective-permute-start | bytes 786440 | tf_op jit(solution)/shard_map/ppermute | solution.py:289
  236.0 13.9 %collective-permute-start.21 = (bf16[128,1024]{1,0:T(8,128)(2,1)S(1)}, bf16[128,1024]{1,0:T(8,128)(2,1)S(1)}, u32[]{:S(2)}, u32[]{:S(2)}) collective-permute-start(bf16[128,1024]{1,0:T(8,128)(2,1)S(1)} %add_convert_fusion.2), channel_id=1, source_target_pairs={{1,0},{2,1},{3,2},{5,4},{6,5},{7,6},{9,8},{10,9},{11,10},{13,12},{... | collective-permute-start | bytes 786440 | tf_op jit(solution)/shard_map/ppermute | solution.py:290
  244.5 10.0 %collective-permute-start.28 = (bf16[128,1024]{1,0:T(8,128)(2,1)}, bf16[128,1024]{1,0:T(8,128)(2,1)S(1)}, u32[]{:S(2)}, u32[]{:S(2)}) collective-permute-start(bf16[128,1024]{1,0:T(8,128)(2,1)} %get-tuple-element.103), channel_id=1, source_target_pairs={{0,1},{1,2},{2,3},{4,5},{5,6},{6,7},{8,9},{9,10},{10,11},{12,13},{... | collective-permute-start | bytes 786440 | tf_op jit(solution)/shard_map/ppermute | solution.py:289
  248.4 10.4 %collective-permute-start.31 = (bf16[128,1024]{1,0:T(8,128)(2,1)S(1)}, bf16[128,1024]{1,0:T(8,128)(2,1)S(1)}, u32[]{:S(2)}, u32[]{:S(2)}) collective-permute-start(bf16[128,1024]{1,0:T(8,128)(2,1)S(1)} %get-tuple-element.104), channel_id=1, source_target_pairs={{1,0},{2,1},{3,2},{5,4},{6,5},{7,6},{9,8},{10,9},{11,10},{13,12},{... | collective-permute-start | bytes 786440 | tf_op jit(solution)/shard_map/ppermute | solution.py:290
  249.9 10.4 %copy-start.25 = (bf16[128,4096]{1,0:T(8,128)(2,1)S(1)}, bf16[128,4096]{1,0:T(8,128)(2,1)}, u32[]{:S(2)}) copy-start(bf16[128,4096]{1,0:T(8,128)(2,1)} %param.6) | copy-start | bytes 3145732
  254.5 9.2 %collective-permute-start.29 = (bf16[128,1024]{1,0:T(8,128)(2,1)S(1)}, bf16[128,1024]{1,0:T(8,128)(2,1)S(1)}, u32[]{:S(2)}, u32[]{:S(2)}) collective-permute-start(bf16[128,1024]{1,0:T(8,128)(2,1)S(1)} %add_convert_fusion.1), channel_id=1, source_target_pairs={{0,1},{1,2},{2,3},{4,5},{5,6},{6,7},{8,9},{9,10},{10,11},{12,13},{... | collective-permute-start | bytes 786440 | tf_op jit(solution)/shard_map/ppermute | solution.py:289
  258.9 9.1 %collective-permute-start.32 = (bf16[128,1024]{1,0:T(8,128)(2,1)S(1)}, bf16[128,1024]{1,0:T(8,128)(2,1)S(1)}, u32[]{:S(2)}, u32[]{:S(2)}) collective-permute-start(bf16[128,1024]{1,0:T(8,128)(2,1)S(1)} %add_convert_fusion), channel_id=1, source_target_pairs={{1,0},{2,1},{3,2},{5,4},{6,5},{7,6},{9,8},{10,9},{11,10},{13,12},{... | collective-permute-start | bytes 786440 | tf_op jit(solution)/shard_map/ppermute | solution.py:290
  268.2 1.4 copy-start.26
  268.2 2.0 copy-start.27
  270.4 2.0 copy-start.1
  (6 other events, 5.9 us)
Sparse Core Ops, SparseCore 0:
  10.2 83.4 all-gather.1
  191.9 55.4 reduce-scatter.1

commit v5 on v4

--- a/solution.py
+++ b/solution.py
@@ -32,39 +32,49 @@
     return [slice(at, at + tile) for at in range(0, out_ref.shape[1], tile)]
 
 
-def product_kernel(at_ref, x_ref, *refs):
-    pieces, out_ref = refs[:-1], refs[-1]
+def blocks_of(xs, out_ref):
+    tile = math.gcd(out_ref.shape[1], 256)
+    size = xs[0].shape[0]
+    for at in range(0, out_ref.shape[1], tile):
+        for index, x_ref in enumerate(xs):
+            yield x_ref, slice(index * size, (index + 1) * size), slice(at, at + tile)
+
+
+def product_kernel(parts, at_ref, *refs):
+    xs, pieces, out_ref = refs[:parts], refs[parts:-1], refs[-1]
     deep = pieces[0].shape[1]
-    for tile in tiles_of(out_ref):
+    for x_ref, rows, tile in blocks_of(xs, out_ref):
         key = value = None
         for index, piece in enumerate(pieces):
             x = columns_of(x_ref, at_ref, index, deep)
             new_key, new_value = dot(x, piece[0, :, tile]), dot(x, piece[1, :, tile])
             key = new_key if key is None else key + new_key
             value = new_value if value is None else value + new_value
-        out_ref[:, tile] = key.astype(BF16).astype(F32) * value.astype(BF16).astype(F32)
-
-
-def query_kernel(at_ref, x_ref, *refs):
-    pairs, out_ref = refs[:-1], refs[-1]
+        out_ref[rows, tile] = key.astype(BF16).astype(F32) * value.astype(BF16).astype(F32)
+
+
+def query_kernel(parts, at_ref, *refs):
+    xs, pairs, out_ref = refs[:parts], refs[parts:-1], refs[-1]
     deep = pairs[0].shape[1]
-    for tile in tiles_of(out_ref):
+    for x_ref, rows, tile in blocks_of(xs, out_ref):
         query = None
         for index in range(2 * len(pairs)):
             x = columns_of(x_ref, at_ref, index, deep)
             new = dot(x, pairs[index // 2][index % 2, :, tile])
             query = new if query is None else query + new
-        out_ref[:, tile] = query
-
-
-def gate_kernel(at_ref, x_ref, filtered_ref, partial_ref, *refs):
-    pieces, out_ref = refs[:-1], refs[-1]
+        out_ref[rows, tile] = query
+
+
+def gate_kernel(parts, at_ref, *refs):
+    xs, refs = refs[:parts], refs[parts:]
+    filtered_ref, partial_ref, pieces, out_ref = refs[0], refs[1], refs[2:-1], refs[-1]
     deep = pieces[0].shape[0]
-    for tile in tiles_of(out_ref):
-        query = partial_ref[:, tile]
+    for x_ref, rows, tile in blocks_of(xs, out_ref):
+        query = partial_ref[rows, tile]
         for index, piece in enumerate(pieces):
             query = query + dot(columns_of(x_ref, at_ref, index, deep), piece[:, tile])
-        out_ref[:, tile] = (query.astype(BF16).astype(F32) * filtered_ref[:, tile]).astype(BF16)
+        gated = query.astype(BF16).astype(F32) * filtered_ref[rows, tile]
+        out_ref[rows, tile] = gated.astype(BF16)
 
 
 def call(kernel, scalars, operands, out, scratch=()):
@@ -79,10 +89,10 @@
     )(scalars, *operands)
 
 
-def project(kernel, at, x, extra, pieces, out_dtype):
-    half = pieces[0].shape[-1]
-    out = jax.ShapeDtypeStruct((x.shape[0], half), out_dtype)
-    return call(kernel, at, (x, *extra, *pieces), out)
+def project(kernel, at, xs, extra, pieces, out_dtype):
+    rows = sum(x.shape[0] for x in xs)
+    out = jax.ShapeDtypeStruct((rows, pieces[0].shape[-1]), out_dtype)
+    return call(functools.partial(kernel, len(xs)), at, (*xs, *extra, *pieces), out)
 
 
 def filter_kernel(_, product_ref, halo_ref, taps_ref, out_ref, held):
@@ -215,9 +225,9 @@
     kv_rest = onward(kv_x, kv_y)
     q_x = {(0, dx): from_chip(both_q, 0, dx) for dx in range(1, nx)}
     q_y = {(dy, 0): from_chip(both_q, dy, 0) for dy in range(1, ny)}
-    arrived = (kv_x, kv_y, kv_rest, q_x, q_y)
+    arrived = (kv_x, kv_y, kv_rest)
     own_rows, arrived = lax.optimization_barrier((own_rows, arrived))
-    kv_x, kv_y, kv_rest, q_x, q_y = arrived
+    kv_x, kv_y, kv_rest = arrived
     kv = listed(kv_x, kv_y, kv_rest)
     order = list(kv)
     kv_pieces = [piece for key in order for piece in kv[key]]
@@ -226,8 +236,9 @@
     ).astype(jnp.int32)
     early = 2 * (ny + nx - 1)
 
-    other_rows = from_partner(own_rows)
-    own_product = project(product_kernel, at, own_rows, [], kv_pieces, F32)
+    own_product = project(product_kernel, at, [own_rows], [], kv_pieces, F32)
+    rows_then, q_x, q_y, own_product = lax.optimization_barrier((own_rows, q_x, q_y, own_product))
+    other_rows = from_partner(rows_then)
     q_rest = {
         (dy, dx): (from_chip(q_x[0, dx][0], dy, 0), from_chip(q_y[dy, 0][1], 0, dx))
         for dy, _ in q_y
@@ -235,7 +246,9 @@
     }
     q_pairs = {(0, 0): both_q, **q_x, **q_y}
     q_early = [q_pairs[key] for key in order if key in q_pairs]
-    other_product = project(product_kernel, at, other_rows, [], kv_pieces, F32)
+    own_query = project(query_kernel, at, [own_rows], [], q_early, F32)
+    other_rows, own_query = lax.optimization_barrier((other_rows, own_query))
+    other_product = project(product_kernel, at, [other_rows], [], kv_pieces, F32)
 
     reach = filters.shape[0] - 1
     pad = -(-reach // 8) * 8
@@ -247,8 +260,7 @@
         "seq",
         [(2 * i + c, 2 * i + 2 + c) for i in range(chips - 1) for c in range(2)],
     )
-    other_query = project(query_kernel, at, other_rows, [], q_early, F32)
-    own_query = project(query_kernel, at, own_rows, [], q_early, F32)
+    other_query = project(query_kernel, at, [other_rows], [], q_early, F32)
     groups = filters.shape[1] // 2
     taps = jnp.repeat(
         lax.dynamic_slice_in_dim(filters, core * groups, groups, axis=1), half // groups, axis=1
@@ -263,9 +275,9 @@
     o_y = {(dy, 0): from_chip(both_o, dy, 0) for dy in range(1, ny)}
     late = [piece for pair in q_rest.values() for piece in pair]
     other_gated = project(
-        gate_kernel, at[early:], other_rows, [other_filtered, other_query], late, BF16
-    )
-    own_gated = project(gate_kernel, at[early:], own_rows, [own_filtered, own_query], late, BF16)
+        gate_kernel, at[early:], [other_rows], [other_filtered, other_query], late, BF16
+    )
+    own_gated = project(gate_kernel, at[early:], [own_rows], [own_filtered, own_query], late, BF16)
 
     position = lax.axis_index("tp")
     z = position.astype(jnp.int32).reshape(1)

time: 280 us -> 267 us (0.954)
  waiting for transfers between devices: 145 us -> 134 us
  local copies, waits for them, and re-layouts: 24.2 us -> 16.1 us
  Pallas kernels: 34.1 us -> 41.3 us
    ppermute x13, waiting for transfers between devices: 108 us -> 91.5 us  [from_chip(): return lax.ppermute(block, 'seq', route)]
    pallas_call x14, Pallas kernels: 34.1 us -> 41.3 us  [call(): pl.pallas_call(kernel, out_shape=out, in_specs=[pl.BlockSpec(memory_space...]
    unnamed x70 -> x62, local copies, waits for them, and re-layouts: 15.8 us -> 8.94 us
    all_gather x1, waiting for transfers between devices: 0.01 us -> 4.74 us  [on_device(): own_rows = lax.all_gather(normed, 'tp', axis=0, tiled=True)]
  transfers between devices with their start and end apart: 35 -> 35, of which waited for: 22 -> 24; matrix products, arithmetic and copies ran while one was open for 3% -> 3% of each run, Pallas kernels for 10% -> 14%
where the time goes in v5:
time: 267 us; the launch traced here: 266 us
  waiting for transfers between devices  134 us (50%)
  starting transfers between devices  54.7 us (20%)
  Pallas kernels  41.3 us (15%)
  local copies, waits for them, and re-layouts  16.1 us (6%)
  between operations  14.2 us (5%)
  other arithmetic  6.22 us (2%)
    ppermute x13, waiting for transfers between devices, from_chip(): return lax.ppermute(block, 'seq', route)  91.5 us
    pallas_call x14, Pallas kernels, call(): pl.pallas_call(kernel, out_shape=out, in_specs=[pl.BlockSpec(memory_space...  41.3 us
    ppermute x6, starting transfers between devices, chained(): rising = lax.ppermute(send_up, 'tp', up)  27.2 us
    ppermute x6, waiting for transfers between devices, chained(): rising = lax.ppermute(send_up, 'tp', up)  16.1 us
    ppermute x13, starting transfers between devices, from_chip(): return lax.ppermute(block, 'seq', route)  15.8 us
    ppermute x6, waiting for transfers between devices, chained(): falling = lax.ppermute(send_down, 'tp', down)  15.7 us
    unnamed x62, local copies, waits for them, and re-layouts  8.94 us
    ppermute x6, starting transfers between devices, chained(): falling = lax.ppermute(send_down, 'tp', down)  7.75 us
  transfers between devices with their start and end apart: 35, of which 24 were waited for; matrix products, arithmetic and copies ran while one was open for 3% of the time, Pallas kernels for 14%

profile of v5, /device:TPU:0, one launch (start us, length us, event | category | flops | bytes accessed | tf_op | source)
XLA Modules:
  0.0 266.2 jit_solution(14880766526704185624)
XLA Ops:
  6.5 1.8 constant_dynamic-slice_fusion.3
  8.7 1.3 fusion.2
  10.6 2.6 collective-permute-start.1
  13.2 1.5 collective-permute-start.3
  14.7 1.1 collective-permute-start.2
  15.8 1.5 collective-permute-start.4
  17.3 1.3 constant_dynamic-slice_fusion.2
  18.6 1.9 collective-permute-done.5
  20.6 16.7 %collective-permute-done.1.refs_3_ = bf16[2,512,512]{2,1,0:T(8,128)(2,1)} collective-permute-done((bf16[2,512,512]{2,1,0:T(8,128)(2,1)S(1)}, bf16[2,512,512]{2,1,0:T(8,128)(2,1)}, u32[]{:S(2)}, u32[]{:S(2)}) %collective-permute-start.1) | collective-permute-done | bytes 1048608 | tf_op jit(solution)/shard_map/ppermute | solution.py:176
  37.3 1.9 collective-permute-done.3.refs_5_
  40.2 19.2 %collective-permute-done.2.refs_4_ = bf16[2,512,512]{2,1,0:T(8,128)(2,1)S(1)} collective-permute-done((bf16[2,512,512]{2,1,0:T(8,128)(2,1)S(1)}, bf16[2,512,512]{2,1,0:T(8,128)(2,1)S(1)}, u32[]{:S(2)}, u32[]{:S(2)}) %collective-permute-start.2) | collective-permute-done | bytes 1048608 | tf_op jit(solution)/shard_map/ppermute | solution.py:176
  61.0 1.5 collective-permute-start.6
  62.5 1.1 collective-permute-start.7
  65.1 22.3 %collective-permute-done.6.refs_7_ = bf16[2,512,512]{2,1,0:T(8,128)(2,1)} collective-permute-done((bf16[2,512,512]{2,1,0:T(8,128)(2,1)}, bf16[2,512,512]{2,1,0:T(8,128)(2,1)}, u32[]{:S(2)}, u32[]{:S(2)}) %collective-permute-start.6) | collective-permute-done | bytes 1048608 | tf_op jit(solution)/shard_map/ppermute | solution.py:176
  87.4 1.5 collective-permute-done.7.refs_8_
  88.9 4.7 %all-gather.2.cloned.1.call-done.refs_0_ = bf16[512,4096]{1,0:T(8,128)(2,1)} async-done(((bf16[128,4096]{1,0:T(8,128)(2,1)}), bf16[512,4096]{1,0:T(8,128)(2,1)}) %all-gather.2.cloned.1.call-update) | async-done | bytes 4194320 | tf_op jit(solution)/shard_map/all_gather | solution.py:217
  93.7 1.2 copy-done.5
  94.9 1.2 copy-done.8
  96.1 1.2 copy-done.11
  97.3 8.0 %shard_map.64.product_ref = f32[512,512]{1,0:T(8,128)S(1)} custom-call(s32[8]{0:T(128)S(1)} %stack.58.at_ref._, bf16[512,4096]{1,0:T(8,128)(2,1)} %all-gather.2.cloned.1.call-done.refs_0_, bf16[2,512,512]{2,1,0:T(8,128)(2,1)S(1)} %get-tuple-element.61.refs_1_, bf16[2,512,512]{2,1,0:T(8,128)(2,1)S(1)} %copy-done.5, ...), custom_call_target="tpu_custom_call" | custom-call | flops 1 | bytes 1 | tf_op jit(solution)/shard_map/pallas_call | solution.py:81
  106.3 1.8 collective-permute-done.10.refs_3_
  108.1 1.4 collective-permute-done.9.refs_2_
  109.5 1.1 dynamic-slice_bitcast_fusion
  111.4 1.1 slice_bitcast_fusion.1
  112.6 4.5 %shard_map.65.refs_2_ = f32[512,512]{1,0:T(8,128)S(1)} custom-call(s32[8]{0:T(128)S(1)} %stack.58.at_ref._, bf16[512,4096]{1,0:T(8,128)(2,1)} %all-gather.2.cloned.1.call-done.refs_0_, bf16[2,512,512]{2,1,0:T(8,128)(2,1)S(1)} %pad_maximum_fusion.refs_1_, bf16[2,512,512]{2,1,0:T(8,128)(2,1)} %collective-permute-done.9.refs_2_, ...), custom_call_target="tpu_custom_call" | custom-call | flops 1 | bytes 1 | tf_op jit(solution)/shard_map/pallas_call | solution.py:81
  117.6 1.6 collective-permute-start.12
  119.2 7.9 %shard_map.66.product_ref = f32[512,512]{1,0:T(8,128)S(1)} custom-call(s32[8]{0:T(128)S(1)} %stack.58.at_ref._, bf16[512,4096]{1,0:T(8,128)(2,1)} %collective-permute-done.13.refs_0_, bf16[2,512,512]{2,1,0:T(8,128)(2,1)S(1)} %get-tuple-element.61.refs_1_, bf16[2,512,512]{2,1,0:T(8,128)(2,1)S(1)} %copy-done.6, ...), custom_call_target="tpu_custom_call" | custom-call | flops 1 | bytes 1 | tf_op jit(solution)/shard_map/pallas_call | solution.py:81
  127.2 2.5 collective-permute-start.14
  129.7 1.1 pad_maximum_fusion.1.refs_0_
  130.9 4.3 %shard_map.69.refs_2_ = f32[512,512]{1,0:T(8,128)S(1)} custom-call(s32[8]{0:T(128)S(1)} %stack.58.at_ref._, bf16[512,4096]{1,0:T(8,128)(2,1)} %collective-permute-done.13.refs_0_, bf16[2,512,512]{2,1,0:T(8,128)(2,1)S(1)} %pad_maximum_fusion.refs_1_, bf16[2,512,512]{2,1,0:T(8,128)(2,1)} %collective-permute-done.9.refs_2_, ...), custom_call_target="tpu_custom_call" | custom-call | flops 1 | bytes 1 | tf_op jit(solution)/shard_map/pallas_call | solution.py:81
  135.2 2.0 shard_map.68.refs_1_
  137.3 2.0 shard_map.67.refs_1_
  139.3 2.9 %shard_map.71.gated_ref = bf16[512,512]{1,0:T(8,128)(2,1)S(1)} custom-call(s32[2]{0:T(128)S(1)} %pad_add_fusion.at_ref, bf16[512,4096]{1,0:T(8,128)(2,1)} %collective-permute-done.13.refs_0_, f32[512,512]{1,0:T(8,128)S(1)} %shard_map.68.refs_1_, f32[512,512]{1,0:T(8,128)S(1)} %shard_map.69.refs_2_, bf16[512,512]{1,0:T(8,128)(2,1)S(1)} %collective-permute-done.11.refs_3_, ...), custom_call_target="tpu_custom_call" | custom-call | flops 1 | bytes 1 | tf_op jit(solution)/shard_map/pallas_call | solution.py:81
  143.1 2.6 collective-permute-start.22
  145.7 2.9 %shard_map.70.gated_ref = bf16[512,512]{1,0:T(8,128)(2,1)S(1)} custom-call(s32[2]{0:T(128)S(1)} %pad_add_fusion.at_ref, bf16[512,4096]{1,0:T(8,128)(2,1)} %all-gather.2.cloned.1.call-done.refs_0_, f32[512,512]{1,0:T(8,128)S(1)} %shard_map.67.refs_1_, f32[512,512]{1,0:T(8,128)S(1)} %shard_map.65.refs_2_, ...), custom_call_target="tpu_custom_call" | custom-call | flops 1 | bytes 1 | tf_op jit(solution)/shard_map/pallas_call | solution.py:81
  150.0 3.5 %collective-permute-start.16 = (bf16[128,1024]{1,0:T(8,128)(2,1)S(1)}, bf16[128,1024]{1,0:T(8,128)(2,1)S(1)}, u32[]{:S(2)}, u32[]{:S(2)}) collective-permute-start(bf16[128,1024]{1,0:T(8,128)(2,1)S(1)} %get-tuple-element.85), channel_id=1, source_target_pairs={{0,1},{1,2},{2,3},{4,5},{5,6},{6,7},{8,9},{9,10},{10,11},{12,13},{... | collective-permute-start | bytes 786440 | tf_op jit(solution)/shard_map/ppermute | solution.py:301
  153.5 1.3 collective-permute-start.19
  154.8 4.6 %collective-permute-done.16 = bf16[128,1024]{1,0:T(8,128)(2,1)S(1)} collective-permute-done((bf16[128,1024]{1,0:T(8,128)(2,1)S(1)}, bf16[128,1024]{1,0:T(8,128)(2,1)S(1)}, u32[]{:S(2)}, u32[]{:S(2)}) %collective-permute-start.16) | collective-permute-done | bytes 262176 | tf_op jit(solution)/shard_map/ppermute | solution.py:301
  159.4 4.1 %collective-permute-done.19 = bf16[128,1024]{1,0:T(8,128)(2,1)S(1)} collective-permute-done((bf16[128,1024]{1,0:T(8,128)(2,1)S(1)}, bf16[128,1024]{1,0:T(8,128)(2,1)S(1)}, u32[]{:S(2)}, u32[]{:S(2)}) %collective-permute-start.19) | collective-permute-done | bytes 262176 | tf_op jit(solution)/shard_map/ppermute | solution.py:302
  163.5 5.9 %collective-permute-done.22.refs_0_ = bf16[2,512,512]{2,1,0:T(8,128)(2,1)S(1)} collective-permute-done((bf16[2,512,512]{2,1,0:T(8,128)(2,1)S(1)}, bf16[2,512,512]{2,1,0:T(8,128)(2,1)S(1)}, u32[]{:S(2)}, u32[]{:S(2)}) %collective-permute-start.22) | collective-permute-done | bytes 1048608 | tf_op jit(solution)/shard_map/ppermute | solution.py:176
  169.4 1.5 collective-permute-done.23.refs_1_
  170.9 1.3 shard_map.74
  172.6 3.8 %collective-permute-done.24.refs_2_ = bf16[512,2048]{1,0:T(8,128)(2,1)S(1)} collective-permute-done((bf16[512,2048]{1,0:T(8,128)(2,1)S(1)}, bf16[512,2048]{1,0:T(8,128)(2,1)S(1)}, u32[]{:S(2)}, u32[]{:S(2)}) %collective-permute-start.24) | collective-permute-done | bytes 2097184 | tf_op jit(solution)/shard_map/ppermute | solution.py:179
  176.4 2.6 shard_map.75
  179.0 18.8 %collective-permute-done.25.refs_0_ = bf16[2,512,512]{2,1,0:T(8,128)(2,1)S(1)} collective-permute-done((bf16[2,512,512]{2,1,0:T(8,128)(2,1)S(1)}, bf16[2,512,512]{2,1,0:T(8,128)(2,1)S(1)}, u32[]{:S(2)}, u32[]{:S(2)}) %collective-permute-start.25) | collective-permute-done | bytes 1048608 | tf_op jit(solution)/shard_map/ppermute | solution.py:176
  198.8 3.5 %collective-permute-start.17 = (bf16[128,1024]{1,0:T(8,128)(2,1)S(1)}, bf16[128,1024]{1,0:T(8,128)(2,1)S(1)}, u32[]{:S(2)}, u32[]{:S(2)}) collective-permute-start(bf16[128,1024]{1,0:T(8,128)(2,1)S(1)} %get-tuple-element.113), channel_id=1, source_target_pairs={{0,1},{1,2},{2,3},{4,5},{5,6},{6,7},{8,9},{9,10},{10,11},{12,13},{... | collective-permute-start | bytes 786440 | tf_op jit(solution)/shard_map/ppermute | solution.py:301
  202.3 1.3 collective-permute-start.20
  204.4 4.6 %collective-permute-start.27 = (bf16[128,1024]{1,0:T(8,128)(2,1)S(1)}, bf16[128,1024]{1,0:T(8,128)(2,1)S(1)}, u32[]{:S(2)}, u32[]{:S(2)}) collective-permute-start(bf16[128,1024]{1,0:T(8,128)(2,1)S(1)} %get-tuple-element.94), channel_id=1, source_target_pairs={{0,1},{1,2},{2,3},{4,5},{5,6},{6,7},{8,9},{9,10},{10,11},{12,13},{... | collective-permute-start | bytes 786440 | tf_op jit(solution)/shard_map/ppermute | solution.py:301
  208.9 1.3 collective-permute-start.30
  210.2 4.4 %collective-permute-done.17 = bf16[128,1024]{1,0:T(8,128)(2,1)S(1)} collective-permute-done((bf16[128,1024]{1,0:T(8,128)(2,1)S(1)}, bf16[128,1024]{1,0:T(8,128)(2,1)S(1)}, u32[]{:S(2)}, u32[]{:S(2)}) %collective-permute-start.17) | collective-permute-done | bytes 262176 | tf_op jit(solution)/shard_map/ppermute | solution.py:301
  214.7 7.3 %collective-permute-start.18 = (bf16[128,1024]{1,0:T(8,128)(2,1)S(1)}, bf16[128,1024]{1,0:T(8,128)(2,1)S(1)}, u32[]{:S(2)}, u32[]{:S(2)}) collective-permute-start(bf16[128,1024]{1,0:T(8,128)(2,1)S(1)} %add_convert_fusion.3), channel_id=1, source_target_pairs={{0,1},{1,2},{2,3},{4,5},{5,6},{6,7},{8,9},{9,10},{10,11},{12,13},{... | collective-permute-start | bytes 786440 | tf_op jit(solution)/shard_map/ppermute | solution.py:301
  222.0 1.1 collective-permute-done.20
  223.2 1.3 collective-permute-start.21
  224.5 1.4 collective-permute-done.27
  225.8 5.0 %collective-permute-done.30 = bf16[128,1024]{1,0:T(8,128)(2,1)S(1)} collective-permute-done((bf16[128,1024]{1,0:T(8,128)(2,1)S(1)}, bf16[128,1024]{1,0:T(8,128)(2,1)S(1)}, u32[]{:S(2)}, u32[]{:S(2)}) %collective-permute-start.30) | collective-permute-done | bytes 262176 | tf_op jit(solution)/shard_map/ppermute | solution.py:302
  231.0 4.0 %collective-permute-start.28 = (bf16[128,1024]{1,0:T(8,128)(2,1)S(1)}, bf16[128,1024]{1,0:T(8,128)(2,1)S(1)}, u32[]{:S(2)}, u32[]{:S(2)}) collective-permute-start(bf16[128,1024]{1,0:T(8,128)(2,1)S(1)} %get-tuple-element.111), channel_id=1, source_target_pairs={{0,1},{1,2},{2,3},{4,5},{5,6},{6,7},{8,9},{9,10},{10,11},{12,13},{... | collective-permute-start | bytes 786440 | tf_op jit(solution)/shard_map/ppermute | solution.py:301
  235.0 1.3 collective-permute-start.31
  237.2 3.6 %collective-permute-done.28 = bf16[128,1024]{1,0:T(8,128)(2,1)S(1)} collective-permute-done((bf16[128,1024]{1,0:T(8,128)(2,1)S(1)}, bf16[128,1024]{1,0:T(8,128)(2,1)S(1)}, u32[]{:S(2)}, u32[]{:S(2)}) %collective-permute-start.28) | collective-permute-done | bytes 262176 | tf_op jit(solution)/shard_map/ppermute | solution.py:301
  240.8 4.4 %collective-permute-start.29 = (bf16[128,1024]{1,0:T(8,128)(2,1)S(1)}, bf16[128,1024]{1,0:T(8,128)(2,1)S(1)}, u32[]{:S(2)}, u32[]{:S(2)}) collective-permute-start(bf16[128,1024]{1,0:T(8,128)(2,1)S(1)} %add_convert_fusion.1), channel_id=1, source_target_pairs={{0,1},{1,2},{2,3},{4,5},{5,6},{6,7},{8,9},{9,10},{10,11},{12,13},{... | collective-permute-start | bytes 786440 | tf_op jit(solution)/shard_map/ppermute | solution.py:301
  245.3 1.3 collective-permute-start.32
  246.8 1.2 fusion.24
  248.0 2.2 collective-permute-done.29
  250.2 4.8 %collective-permute-done.32 = bf16[128,1024]{1,0:T(8,128)(2,1)S(1)} collective-permute-done((bf16[128,1024]{1,0:T(8,128)(2,1)S(1)}, bf16[128,1024]{1,0:T(8,128)(2,1)S(1)}, u32[]{:S(2)}, u32[]{:S(2)}) %collective-permute-start.32) | collective-permute-done | bytes 262176 | tf_op jit(solution)/shard_map/ppermute | solution.py:302
  255.2 1.4 fusion.28
  (118 shorter events, 16.3 us)
Async XLA Ops:
  6.5 104.5 %copy-start = (f32[7,64]{1,0:T(8,128)S(1)}, f32[7,64]{1,0:T(8,128)}, u32[]{:S(2)}) copy-start(f32[7,64]{1,0:T(8,128)} %param.9) | copy-start | bytes 5380
  6.5 87.1 %all-gather.2.cloned.1.call-start = ((), (), s32[]{:S(2)}) async-start(), calls=%async_computation.1 | async-start | bytes 5242880 | tf_op jit(solution)/shard_map/all_gather | solution.py:217
  6.5 1.9 copy-start.19
  6.5 2.2 copy-start.30
  10.0 245.1 %reduce-scatter.2.cloned.1.call-start = ((), (), s32[]{:S(2)}) async-start(), calls=%async_computation.2 | async-start | bytes 2621440 | tf_op jit(solution)/shard_map/reduce_scatter | solution.py:316
  10.1 4.6 %collective-permute-start = (bf16[2,512,512]{2,1,0:T(8,128)(2,1)S(1)}, bf16[2,512,512]{2,1,0:T(8,128)(2,1)S(1)}, u32[]{:S(2)}, u32[]{:S(2)}) collective-permute-start(bf16[2,512,512]{2,1,0:T(8,128)(2,1)S(1)} %get-tuple-element.98), channel_id=1, source_target_pairs={{0,4},{4,0},{8,12},{12,8},{16,20},{20,16},{24,28},{28,24},{1,5},{5... | collective-permute-start | bytes 3145736 | tf_op jit(solution)/shard_map/ppermute | solution.py:179
  10.6 26.7 %collective-permute-start.1 = (bf16[2,512,512]{2,1,0:T(8,128)(2,1)S(1)}, bf16[2,512,512]{2,1,0:T(8,128)(2,1)}, u32[]{:S(2)}, u32[]{:S(2)}) collective-permute-start(bf16[2,512,512]{2,1,0:T(8,128)(2,1)S(1)} %get-tuple-element.61.refs_1_), channel_id=1, source_target_pairs={{8,0},{12,4},{0,8},{4,12},{24,16},{28,20},{16,24},{20,28},{9,1},{1... | collective-permute-start | bytes 3145736 | tf_op jit(solution)/shard_map/ppermute | solution.py:176
  13.2 26.0 %collective-permute-start.3 = (bf16[2,512,512]{2,1,0:T(8,128)(2,1)S(1)}, bf16[2,512,512]{2,1,0:T(8,128)(2,1)S(1)}, u32[]{:S(2)}, u32[]{:S(2)}) collective-permute-start(bf16[2,512,512]{2,1,0:T(8,128)(2,1)S(1)} %get-tuple-element.61.refs_1_), channel_id=1, source_target_pairs={{16,0},{20,4},{24,8},{28,12},{0,16},{4,20},{8,24},{12,28},{17,1},{... | collective-permute-start | bytes 3145736 | tf_op jit(solution)/shard_map/ppermute | solution.py:176
  14.7 5.9 %copy-start.4 = (bf16[2,512,512]{2,1,0:T(8,128)(2,1)}, bf16[2,512,512]{2,1,0:T(8,128)(2,1)S(1)}, u32[]{:S(2)}) copy-start(bf16[2,512,512]{2,1,0:T(8,128)(2,1)S(1)} %collective-permute-done.refs_2_) | copy-start | bytes 3145732
  14.7 44.7 %collective-permute-start.2 = (bf16[2,512,512]{2,1,0:T(8,128)(2,1)S(1)}, bf16[2,512,512]{2,1,0:T(8,128)(2,1)S(1)}, u32[]{:S(2)}, u32[]{:S(2)}) collective-permute-start(bf16[2,512,512]{2,1,0:T(8,128)(2,1)S(1)} %collective-permute-done.refs_2_), channel_id=1, source_target_pairs={{8,0},{12,4},{0,8},{4,12},{24,16},{28,20},{16,24},{20,28},{9,1},{1... | collective-permute-start | bytes 3145736 | tf_op jit(solution)/shard_map/ppermute | solution.py:176
  15.8 45.2 %collective-permute-start.4 = (bf16[2,512,512]{2,1,0:T(8,128)(2,1)S(1)}, bf16[2,512,512]{2,1,0:T(8,128)(2,1)}, u32[]{:S(2)}, u32[]{:S(2)}) collective-permute-start(bf16[2,512,512]{2,1,0:T(8,128)(2,1)S(1)} %collective-permute-done.refs_2_), channel_id=1, source_target_pairs={{16,0},{20,4},{24,8},{28,12},{0,16},{4,20},{8,24},{12,28},{17,1},{... | collective-permute-start | bytes 3145736 | tf_op jit(solution)/shard_map/ppermute | solution.py:176
  18.5 2.0 collective-permute-start.5
  39.2 1.0 copy-start.7
  61.0 26.4 %collective-permute-start.6 = (bf16[2,512,512]{2,1,0:T(8,128)(2,1)}, bf16[2,512,512]{2,1,0:T(8,128)(2,1)}, u32[]{:S(2)}, u32[]{:S(2)}) collective-permute-start(bf16[2,512,512]{2,1,0:T(8,128)(2,1)} %collective-permute-done.1.refs_3_), channel_id=1, source_target_pairs={{16,0},{20,4},{24,8},{28,12},{0,16},{4,20},{8,24},{12,28},{17,1},{... | collective-permute-start | bytes 3145736 | tf_op jit(solution)/shard_map/ppermute | solution.py:176
  62.5 26.4 %collective-permute-start.7 = (bf16[2,512,512]{2,1,0:T(8,128)(2,1)}, bf16[2,512,512]{2,1,0:T(8,128)(2,1)}, u32[]{:S(2)}, u32[]{:S(2)}) collective-permute-start(bf16[2,512,512]{2,1,0:T(8,128)(2,1)} %collective-permute-done.4.refs_6_), channel_id=1, source_target_pairs={{8,0},{12,4},{0,8},{4,12},{24,16},{28,20},{16,24},{20,28},{9,1},{1... | collective-permute-start | bytes 3145736 | tf_op jit(solution)/shard_map/ppermute | solution.py:176
  63.6 44.4 %collective-permute-start.10 = (bf16[2,512,512]{2,1,0:T(8,128)(2,1)S(1)}, bf16[2,512,512]{2,1,0:T(8,128)(2,1)S(1)}, u32[]{:S(2)}, u32[]{:S(2)}) collective-permute-start(bf16[2,512,512]{2,1,0:T(8,128)(2,1)S(1)} %pad_maximum_fusion.refs_1_), channel_id=1, source_target_pairs={{16,0},{20,4},{24,8},{28,12},{0,16},{4,20},{8,24},{12,28},{17,1},{... | collective-permute-start | bytes 3145736 | tf_op jit(solution)/shard_map/ppermute | solution.py:176
  64.2 45.3 %collective-permute-start.9 = (bf16[2,512,512]{2,1,0:T(8,128)(2,1)S(1)}, bf16[2,512,512]{2,1,0:T(8,128)(2,1)}, u32[]{:S(2)}, u32[]{:S(2)}) collective-permute-start(bf16[2,512,512]{2,1,0:T(8,128)(2,1)S(1)} %pad_maximum_fusion.refs_1_), channel_id=1, source_target_pairs={{8,0},{12,4},{0,8},{4,12},{24,16},{28,20},{16,24},{20,28},{9,1},{1... | collective-permute-start | bytes 3145736 | tf_op jit(solution)/shard_map/ppermute | solution.py:176
  93.7 1.2 copy-start.5
  94.9 1.2 copy-start.8
  96.1 1.2 copy-start.11
  97.3 12.2 %copy-start.25 = (bf16[1024,512]{1,0:T(8,128)(2,1)S(1)}, bf16[1024,512]{1,0:T(8,128)(2,1)}, u32[]{:S(2)}) copy-start(bf16[1024,512]{1,0:T(8,128)(2,1)} %param.10) | copy-start | bytes 3145732
  105.3 1.0 copy-start.2
  109.5 9.7 %collective-permute-start.13 = (bf16[512,4096]{1,0:T(8,128)(2,1)}, bf16[512,4096]{1,0:T(8,128)(2,1)}, u32[]{:S(2)}, u32[]{:S(2)}) collective-permute-start(bf16[512,4096]{1,0:T(8,128)(2,1)} %all-gather.2.cloned.1.call-done.refs_0_), channel_id=1, source_target_pairs={{0,4},{4,0},{8,12},{12,8},{16,20},{20,16},{24,28},{28,24},{1,5},{5... | collective-permute-start | bytes 12582920 | tf_op jit(solution)/shard_map/ppermute | solution.py:179
  110.6 19.1 %collective-permute-start.8 = (bf16[512,512]{1,0:T(8,128)(2,1)}, bf16[512,512]{1,0:T(8,128)(2,1)}, u32[]{:S(2)}, u32[]{:S(2)}) collective-permute-start(bf16[512,512]{1,0:T(8,128)(2,1)} %get-tuple-element.102), channel_id=1, source_target_pairs={{0,4},{4,0},{8,12},{12,8},{16,20},{20,16},{24,28},{28,24},{1,5},{5... | collective-permute-start | bytes 1572872 | tf_op jit(solution)/shard_map/ppermute | solution.py:179
  112.5 6.7 %copy-start.6 = (bf16[2,512,512]{2,1,0:T(8,128)(2,1)S(1)}, bf16[2,512,512]{2,1,0:T(8,128)(2,1)}, u32[]{:S(2)}) copy-start(bf16[2,512,512]{2,1,0:T(8,128)(2,1)} %copy-done.4) | copy-start | bytes 3145732
  112.5 6.7 %copy-start.9 = (bf16[2,512,512]{2,1,0:T(8,128)(2,1)S(1)}, bf16[2,512,512]{2,1,0:T(8,128)(2,1)}, u32[]{:S(2)}) copy-start(bf16[2,512,512]{2,1,0:T(8,128)(2,1)} %copy-done.7) | copy-start | bytes 3145732
  112.5 6.7 %copy-start.12 = (bf16[2,512,512]{2,1,0:T(8,128)(2,1)S(1)}, bf16[2,512,512]{2,1,0:T(8,128)(2,1)}, u32[]{:S(2)}) copy-start(bf16[2,512,512]{2,1,0:T(8,128)(2,1)} %copy-done.10) | copy-start | bytes 3145732
  117.0 22.3 %collective-permute-start.11 = (bf16[512,512]{1,0:T(8,128)(2,1)S(1)}, bf16[512,512]{1,0:T(8,128)(2,1)S(1)}, u32[]{:S(2)}, u32[]{:S(2)}) collective-permute-start(bf16[512,512]{1,0:T(8,128)(2,1)S(1)} %slice_bitcast_fusion.1), channel_id=1, source_target_pairs={{16,0},{20,4},{24,8},{28,12},{0,16},{4,20},{8,24},{12,28},{17,1},{... | collective-permute-start | bytes 1572872 | tf_op jit(solution)/shard_map/ppermute | solution.py:176
  117.6 9.6 %copy-start.3 = (f32[512,512]{1,0:T(8,128)S(1)}, f32[512,512]{1,0:T(8,128)}, u32[]{:S(2)}) copy-start(f32[512,512]{1,0:T(8,128)} %copy-done.2) | copy-start | bytes 3145732
  117.6 12.2 %copy-start.23 = (bf16[1,512,512]{2,1,0:T(8,128)(2,1)S(1)}, bf16[1,512,512]{2,1,0:T(8,128)(2,1)}, u32[]{:S(2)}) copy-start(bf16[1,512,512]{2,1,0:T(8,128)(2,1)} %get-tuple-element.101) | copy-start | bytes 1572868
  117.6 21.7 %collective-permute-start.12 = (bf16[512,512]{1,0:T(8,128)(2,1)S(1)}, bf16[512,512]{1,0:T(8,128)(2,1)S(1)}, u32[]{:S(2)}, u32[]{:S(2)}) collective-permute-start(bf16[512,512]{1,0:T(8,128)(2,1)S(1)} %slice_bitcast_fusion), channel_id=1, source_target_pairs={{8,0},{12,4},{0,8},{4,12},{24,16},{28,20},{16,24},{20,28},{9,1},{1... | collective-permute-start | bytes 1572872 | tf_op jit(solution)/shard_map/ppermute | solution.py:176
  127.2 8.0 %collective-permute-start.14 = (f32[8,512]{1,0:T(8,128)S(1)}, f32[8,512]{1,0:T(8,128)S(1)}, u32[]{:S(2)}, u32[]{:S(2)}) collective-permute-start(f32[8,512]{1,0:T(8,128)S(1)} %slice_select_fusion.3), channel_id=1, source_target_pairs={{0,8},{4,12},{8,16},{12,20},{16,24},{20,28},{1,9},{5,13},{9,17},{1... | collective-permute-start | bytes 49160 | tf_op jit(solution)/shard_map/ppermute | solution.py:258
  143.0 5.6 %collective-permute-start.15 = (bf16[512,1024]{1,0:T(8,128)(2,1)S(1)}, bf16[512,1024]{1,0:T(8,128)(2,1)S(1)}, u32[]{:S(2)}, u32[]{:S(2)}) collective-permute-start(bf16[512,1024]{1,0:T(8,128)(2,1)S(1)} %shard_map.72), channel_id=1, source_target_pairs={{0,4},{4,0},{8,12},{12,8},{16,20},{20,16},{24,28},{28,24},{1,5},{5... | collective-permute-start | bytes 3145736 | tf_op jit(solution)/shard_map/ppermute | solution.py:179
  143.1 26.3 %collective-permute-start.22 = (bf16[2,512,512]{2,1,0:T(8,128)(2,1)S(1)}, bf16[2,512,512]{2,1,0:T(8,128)(2,1)S(1)}, u32[]{:S(2)}, u32[]{:S(2)}) collective-permute-start(bf16[2,512,512]{2,1,0:T(8,128)(2,1)S(1)} %pad_maximum_fusion.1.refs_0_), channel_id=1, source_target_pairs={{8,0},{12,4},{0,8},{4,12},{24,16},{28,20},{16,24},{20,28},{9,1},{1... | collective-permute-start | bytes 3145736 | tf_op jit(solution)/shard_map/ppermute | solution.py:176
  145.6 25.2 %collective-permute-start.23 = (bf16[2,512,512]{2,1,0:T(8,128)(2,1)S(1)}, bf16[2,512,512]{2,1,0:T(8,128)(2,1)S(1)}, u32[]{:S(2)}, u32[]{:S(2)}) collective-permute-start(bf16[2,512,512]{2,1,0:T(8,128)(2,1)S(1)} %pad_maximum_fusion.1.refs_0_), channel_id=1, source_target_pairs={{16,0},{20,4},{24,8},{28,12},{0,16},{4,20},{8,24},{12,28},{17,1},{... | collective-permute-start | bytes 3145736 | tf_op jit(solution)/shard_map/ppermute | solution.py:176
  150.0 22.1 %copy-start.13 = (bf16[128,1024]{1,0:T(8,128)(2,1)}, bf16[128,1024]{1,0:T(8,128)(2,1)S(1)}, u32[]{:S(2)}) copy-start(bf16[128,1024]{1,0:T(8,128)(2,1)S(1)} %get-tuple-element.85) | copy-start | bytes 786436
  150.0 22.1 %copy-start.15 = (bf16[128,1024]{1,0:T(8,128)(2,1)}, bf16[128,1024]{1,0:T(8,128)(2,1)S(1)}, u32[]{:S(2)}) copy-start(bf16[128,1024]{1,0:T(8,128)(2,1)S(1)} %get-tuple-element.83) | copy-start | bytes 786436
  150.0 9.4 %collective-permute-start.16 = (bf16[128,1024]{1,0:T(8,128)(2,1)S(1)}, bf16[128,1024]{1,0:T(8,128)(2,1)S(1)}, u32[]{:S(2)}, u32[]{:S(2)}) collective-permute-start(bf16[128,1024]{1,0:T(8,128)(2,1)S(1)} %get-tuple-element.85), channel_id=1, source_target_pairs={{0,1},{1,2},{2,3},{4,5},{5,6},{6,7},{8,9},{9,10},{10,11},{12,13},{... | collective-permute-start | bytes 786440 | tf_op jit(solution)/shard_map/ppermute | solution.py:301
  153.5 10.0 %collective-permute-start.19 = (bf16[128,1024]{1,0:T(8,128)(2,1)S(1)}, bf16[128,1024]{1,0:T(8,128)(2,1)S(1)}, u32[]{:S(2)}, u32[]{:S(2)}) collective-permute-start(bf16[128,1024]{1,0:T(8,128)(2,1)S(1)} %get-tuple-element.83), channel_id=1, source_target_pairs={{1,0},{2,1},{3,2},{5,4},{6,5},{7,6},{9,8},{10,9},{11,10},{13,12},{... | collective-permute-start | bytes 786440 | tf_op jit(solution)/shard_map/ppermute | solution.py:302
  159.4 12.8 %copy-start.26 = (bf16[128,1024]{1,0:T(8,128)(2,1)}, bf16[128,1024]{1,0:T(8,128)(2,1)S(1)}, u32[]{:S(2)}) copy-start(bf16[128,1024]{1,0:T(8,128)(2,1)S(1)} %collective-permute-done.16) | copy-start | bytes 786436
  163.5 8.7 %copy-start.28 = (bf16[128,1024]{1,0:T(8,128)(2,1)}, bf16[128,1024]{1,0:T(8,128)(2,1)S(1)}, u32[]{:S(2)}) copy-start(bf16[128,1024]{1,0:T(8,128)(2,1)S(1)} %collective-permute-done.19) | copy-start | bytes 786436
  172.2 4.2 %collective-permute-start.24 = (bf16[512,2048]{1,0:T(8,128)(2,1)S(1)}, bf16[512,2048]{1,0:T(8,128)(2,1)S(1)}, u32[]{:S(2)}, u32[]{:S(2)}) collective-permute-start(bf16[512,2048]{1,0:T(8,128)(2,1)S(1)} %shard_map.74), channel_id=1, source_target_pairs={{0,4},{4,0},{8,12},{12,8},{16,20},{20,16},{24,28},{28,24},{1,5},{5... | collective-permute-start | bytes 6291464 | tf_op jit(solution)/shard_map/ppermute | solution.py:179
  172.3 25.6 %collective-permute-start.25 = (bf16[2,512,512]{2,1,0:T(8,128)(2,1)S(1)}, bf16[2,512,512]{2,1,0:T(8,128)(2,1)S(1)}, u32[]{:S(2)}, u32[]{:S(2)}) collective-permute-start(bf16[2,512,512]{2,1,0:T(8,128)(2,1)S(1)} %collective-permute-done.22.refs_0_), channel_id=1, source_target_pairs={{16,0},{20,4},{24,8},{28,12},{0,16},{4,20},{8,24},{12,28},{17,1},{... | collective-permute-start | bytes 3145736 | tf_op jit(solution)/shard_map/ppermute | solution.py:176
  179.0 19.6 %copy-start.18 = (bf16[128,1024]{1,0:T(8,128)(2,1)S(1)}, bf16[128,1024]{1,0:T(8,128)(2,1)}, u32[]{:S(2)}) copy-start(bf16[128,1024]{1,0:T(8,128)(2,1)} %copy-done.17) | copy-start | bytes 786436
  179.0 19.6 %copy-start.27 = (bf16[128,1024]{1,0:T(8,128)(2,1)S(1)}, bf16[128,1024]{1,0:T(8,128)(2,1)}, u32[]{:S(2)}) copy-start(bf16[128,1024]{1,0:T(8,128)(2,1)} %copy-done.26) | copy-start | bytes 786436
  179.0 19.6 %copy-start.29 = (bf16[128,1024]{1,0:T(8,128)(2,1)S(1)}, bf16[128,1024]{1,0:T(8,128)(2,1)}, u32[]{:S(2)}) copy-start(bf16[128,1024]{1,0:T(8,128)(2,1)} %copy-done.28) | copy-start | bytes 786436
  198.5 16.1 %copy-start.16 = (bf16[128,1024]{1,0:T(8,128)(2,1)S(1)}, bf16[128,1024]{1,0:T(8,128)(2,1)}, u32[]{:S(2)}) copy-start(bf16[128,1024]{1,0:T(8,128)(2,1)} %copy-done.15) | copy-start | bytes 786436
  198.6 5.1 %collective-permute-start.26 = (bf16[512,1024]{1,0:T(8,128)(2,1)S(1)}, bf16[512,1024]{1,0:T(8,128)(2,1)S(1)}, u32[]{:S(2)}, u32[]{:S(2)}) collective-permute-start(bf16[512,1024]{1,0:T(8,128)(2,1)S(1)} %shard_map.76), channel_id=1, source_target_pairs={{0,4},{4,0},{8,12},{12,8},{16,20},{20,16},{24,28},{28,24},{1,5},{5... | collective-permute-start | bytes 3145736 | tf_op jit(solution)/shard_map/ppermute | solution.py:179
  198.7 24.4 %copy-start.14 = (bf16[128,1024]{1,0:T(8,128)(2,1)S(1)}, bf16[128,1024]{1,0:T(8,128)(2,1)}, u32[]{:S(2)}) copy-start(bf16[128,1024]{1,0:T(8,128)(2,1)} %copy-done.13) | copy-start | bytes 786436
  198.8 15.8 %collective-permute-start.17 = (bf16[128,1024]{1,0:T(8,128)(2,1)S(1)}, bf16[128,1024]{1,0:T(8,128)(2,1)S(1)}, u32[]{:S(2)}, u32[]{:S(2)}) collective-permute-start(bf16[128,1024]{1,0:T(8,128)(2,1)S(1)} %get-tuple-element.113), channel_id=1, source_target_pairs={{0,1},{1,2},{2,3},{4,5},{5,6},{6,7},{8,9},{9,10},{10,11},{12,13},{... | collective-permute-start | bytes 786440 | tf_op jit(solution)/shard_map/ppermute | solution.py:301
  202.3 20.8 %collective-permute-start.20 = (bf16[128,1024]{1,0:T(8,128)(2,1)S(1)}, bf16[128,1024]{1,0:T(8,128)(2,1)S(1)}, u32[]{:S(2)}, u32[]{:S(2)}) collective-permute-start(bf16[128,1024]{1,0:T(8,128)(2,1)S(1)} %get-tuple-element.114), channel_id=1, source_target_pairs={{1,0},{2,1},{3,2},{5,4},{6,5},{7,6},{9,8},{10,9},{11,10},{13,12},{... | collective-permute-start | bytes 786440 | tf_op jit(solution)/shard_map/ppermute | solution.py:302
  204.4 21.5 %collective-permute-start.27 = (bf16[128,1024]{1,0:T(8,128)(2,1)S(1)}, bf16[128,1024]{1,0:T(8,128)(2,1)S(1)}, u32[]{:S(2)}, u32[]{:S(2)}) collective-permute-start(bf16[128,1024]{1,0:T(8,128)(2,1)S(1)} %get-tuple-element.94), channel_id=1, source_target_pairs={{0,1},{1,2},{2,3},{4,5},{5,6},{6,7},{8,9},{9,10},{10,11},{12,13},{... | collective-permute-start | bytes 786440 | tf_op jit(solution)/shard_map/ppermute | solution.py:301
  208.9 21.9 %collective-permute-start.30 = (bf16[128,1024]{1,0:T(8,128)(2,1)S(1)}, bf16[128,1024]{1,0:T(8,128)(2,1)S(1)}, u32[]{:S(2)}, u32[]{:S(2)}) collective-permute-start(bf16[128,1024]{1,0:T(8,128)(2,1)S(1)} %get-tuple-element.92), channel_id=1, source_target_pairs={{1,0},{2,1},{3,2},{5,4},{6,5},{7,6},{9,8},{10,9},{11,10},{13,12},{... | collective-permute-start | bytes 786440 | tf_op jit(solution)/shard_map/ppermute | solution.py:302
  214.7 21.6 %collective-permute-start.18 = (bf16[128,1024]{1,0:T(8,128)(2,1)S(1)}, bf16[128,1024]{1,0:T(8,128)(2,1)S(1)}, u32[]{:S(2)}, u32[]{:S(2)}) collective-permute-start(bf16[128,1024]{1,0:T(8,128)(2,1)S(1)} %add_convert_fusion.3), channel_id=1, source_target_pairs={{0,1},{1,2},{2,3},{4,5},{5,6},{6,7},{8,9},{9,10},{10,11},{12,13},{... | collective-permute-start | bytes 786440 | tf_op jit(solution)/shard_map/ppermute | solution.py:301
  223.2 13.9 %collective-permute-start.21 = (bf16[128,1024]{1,0:T(8,128)(2,1)S(1)}, bf16[128,1024]{1,0:T(8,128)(2,1)S(1)}, u32[]{:S(2)}, u32[]{:S(2)}) collective-permute-start(bf16[128,1024]{1,0:T(8,128)(2,1)S(1)} %add_convert_fusion.2), channel_id=1, source_target_pairs={{1,0},{2,1},{3,2},{5,4},{6,5},{7,6},{9,8},{10,9},{11,10},{13,12},{... | collective-permute-start | bytes 786440 | tf_op jit(solution)/shard_map/ppermute | solution.py:302
  231.0 9.8 %collective-permute-start.28 = (bf16[128,1024]{1,0:T(8,128)(2,1)S(1)}, bf16[128,1024]{1,0:T(8,128)(2,1)S(1)}, u32[]{:S(2)}, u32[]{:S(2)}) collective-permute-start(bf16[128,1024]{1,0:T(8,128)(2,1)S(1)} %get-tuple-element.111), channel_id=1, source_target_pairs={{0,1},{1,2},{2,3},{4,5},{5,6},{6,7},{8,9},{9,10},{10,11},{12,13},{... | collective-permute-start | bytes 786440 | tf_op jit(solution)/shard_map/ppermute | solution.py:301
  235.0 10.3 %collective-permute-start.31 = (bf16[128,1024]{1,0:T(8,128)(2,1)S(1)}, bf16[128,1024]{1,0:T(8,128)(2,1)S(1)}, u32[]{:S(2)}, u32[]{:S(2)}) collective-permute-start(bf16[128,1024]{1,0:T(8,128)(2,1)S(1)} %get-tuple-element.112), channel_id=1, source_target_pairs={{1,0},{2,1},{3,2},{5,4},{6,5},{7,6},{9,8},{10,9},{11,10},{13,12},{... | collective-permute-start | bytes 786440 | tf_op jit(solution)/shard_map/ppermute | solution.py:302
  237.2 9.6 %copy-start.20 = (bf16[128,4096]{1,0:T(8,128)(2,1)S(1)}, bf16[128,4096]{1,0:T(8,128)(2,1)}, u32[]{:S(2)}) copy-start(bf16[128,4096]{1,0:T(8,128)(2,1)} %param.6) | copy-start | bytes 3145732
  240.8 9.4 %collective-permute-start.29 = (bf16[128,1024]{1,0:T(8,128)(2,1)S(1)}, bf16[128,1024]{1,0:T(8,128)(2,1)S(1)}, u32[]{:S(2)}, u32[]{:S(2)}) collective-permute-start(bf16[128,1024]{1,0:T(8,128)(2,1)S(1)} %add_convert_fusion.1), channel_id=1, source_target_pairs={{0,1},{1,2},{2,3},{4,5},{5,6},{6,7},{8,9},{9,10},{10,11},{12,13},{... | collective-permute-start | bytes 786440 | tf_op jit(solution)/shard_map/ppermute | solution.py:301
  245.3 9.7 %collective-permute-start.32 = (bf16[128,1024]{1,0:T(8,128)(2,1)S(1)}, bf16[128,1024]{1,0:T(8,128)(2,1)S(1)}, u32[]{:S(2)}, u32[]{:S(2)}) collective-permute-start(bf16[128,1024]{1,0:T(8,128)(2,1)S(1)} %add_convert_fusion), channel_id=1, source_target_pairs={{1,0},{2,1},{3,2},{5,4},{6,5},{7,6},{9,8},{10,9},{11,10},{13,12},{... | collective-permute-start | bytes 786440 | tf_op jit(solution)/shard_map/ppermute | solution.py:302
  255.2 1.4 copy-start.21
  255.2 2.0 copy-start.22
  257.4 2.0 copy-start.1
  257.6 1.0 copy-start.24
  (2 other events, 1.7 us)
Sparse Core Ops, SparseCore 0:
  10.2 83.4 all-gather.1
  179.1 55.4 reduce-scatter.1

commit v6 on v5

--- a/solution.py
+++ b/solution.py
@@ -114,8 +114,9 @@
     return call(filter_kernel, at, (product, halo, taps), out, scratch)
 
 
-def terms_kernel(count, order, turned, n_tp, z_ref, gated_ref, *refs):
-    pairs, refs = refs[:count], refs[count:]
+def terms_kernel(plan, turned, n_tp, z_ref, gated_ref, *refs):
+    count = 1 + max(which for which, _ in plan)
+    weights, refs = refs[:count], refs[count:]
     length = gated_ref.shape[0]
     rows = length // n_tp
     held = gated_ref
@@ -127,10 +128,11 @@
                 pl.ds(pl.multiple_of(owner * rows, rows), rows)
             ]
     given, outs = (refs[0], refs[1:]) if len(refs) > 1 else (None, refs)
-    wide = pairs[0].shape[2]
-    for index, (pair, side) in enumerate((p, s) for p in pairs for s in order):
+    wide = weights[0].shape[-1]
+    for index, (which, side) in enumerate(plan):
         at = slice(index * wide, (index + 1) * wide)
-        total = dot(held[...], pair[side])
+        weight = weights[which]
+        total = dot(held[...], weight[...] if side is None else weight[side])
         if given is not None:
             total = total + given[:, at].astype(F32)
         share = length // len(outs)
@@ -140,13 +142,21 @@
 
 def terms(n_tp, z, gated, pairs, order, turned, given=None):
     length, half = gated.shape
-    cols = len(pairs) * 2 * pairs[0].shape[2]
+    weights, plan = [], []
+    for pair in pairs:
+        if isinstance(pair, tuple):
+            plan += [(len(weights) + side, None) for side in order]
+            weights += pair
+        else:
+            plan += [(len(weights), side) for side in order]
+            weights.append(pair)
+    cols = len(plan) * weights[0].shape[-1]
     slots = n_tp if turned and given is not None else 1
     out = [jax.ShapeDtypeStruct((length // slots, cols), BF16)] * slots
-    kernel = functools.partial(terms_kernel, len(pairs), order, turned, n_tp)
+    kernel = functools.partial(terms_kernel, plan, turned, n_tp)
     extra = () if given is None else (given,)
     scratch = [pltpu.VMEM((length, half), BF16)] if turned else []
-    result = call(kernel, z, (gated, *pairs, *extra), out, scratch)
+    result = call(kernel, z, (gated, *weights, *extra), out, scratch)
     return result if slots > 1 else result[0]
 
 
@@ -192,6 +202,13 @@
             for dx in range(1, nx)
         }
 
+    def crossed(along_x, along_y):
+        return {
+            (dy, dx): (from_chip(along_x[0, dx][0], dy, 0), from_chip(along_y[dy, 0][1], 0, dx))
+            for dy, _ in along_y
+            for _, dx in along_x
+        }
+
     def listed(along_x, along_y, rest):
         found = {(0, dx): pair for dx, pair in enumerate(along_x)}
         found.update({(dy, 0): pair for dy, pair in enumerate(along_y)})
@@ -221,7 +238,7 @@
     mine_o = halves(out_weight_then, 0, core)
     both_o = jnp.stack([mine_o, from_partner(halves(out_weight_then, 0, 1 - core))])
 
-    kv_x, kv_y, both_q = lax.optimization_barrier((kv_x, kv_y, both_q))
+    kv_x, kv_y, both_q, both_o = lax.optimization_barrier((kv_x, kv_y, both_q, both_o))
     kv_rest = onward(kv_x, kv_y)
     q_x = {(0, dx): from_chip(both_q, 0, dx) for dx in range(1, nx)}
     q_y = {(dy, 0): from_chip(both_q, dy, 0) for dy in range(1, ny)}
@@ -239,11 +256,7 @@
     own_product = project(product_kernel, at, [own_rows], [], kv_pieces, F32)
     rows_then, q_x, q_y, own_product = lax.optimization_barrier((own_rows, q_x, q_y, own_product))
     other_rows = from_partner(rows_then)
-    q_rest = {
-        (dy, dx): (from_chip(q_x[0, dx][0], dy, 0), from_chip(q_y[dy, 0][1], 0, dx))
-        for dy, _ in q_y
-        for _, dx in q_x
-    }
+    q_rest = crossed(q_x, q_y)
     q_pairs = {(0, 0): both_q, **q_x, **q_y}
     q_early = [q_pairs[key] for key in order if key in q_pairs]
     own_query = project(query_kernel, at, [own_rows], [], q_early, F32)
@@ -260,7 +273,6 @@
         "seq",
         [(2 * i + c, 2 * i + 2 + c) for i in range(chips - 1) for c in range(2)],
     )
-    other_query = project(query_kernel, at, [other_rows], [], q_early, F32)
     groups = filters.shape[1] // 2
     taps = jnp.repeat(
         lax.dynamic_slice_in_dim(filters, core * groups, groups, axis=1), half // groups, axis=1
@@ -268,16 +280,20 @@
     own_filtered = causal_filter(at, own_product, jnp.where(core == 0, rim, first_tail), taps)
     other_filtered = causal_filter(at, other_product, jnp.where(core == 0, first_tail, rim), taps)
 
-    ready = (own_filtered, other_filtered, own_query, other_query)
-    both_o, q_rest, ready = lax.optimization_barrier((both_o, q_rest, ready))
-    own_filtered, other_filtered, own_query, other_query = ready
+    other_rows, own_filtered, other_filtered = lax.optimization_barrier(
+        (other_rows, own_filtered, other_filtered)
+    )
+    other_query = project(query_kernel, at, [other_rows], [], q_early, F32)
+    both_o, q_x, q_y = lax.optimization_barrier((both_o, q_x, q_y))
     o_x = {(0, dx): from_chip(both_o, 0, dx) for dx in range(1, nx)}
     o_y = {(dy, 0): from_chip(both_o, dy, 0) for dy in range(1, ny)}
     late = [piece for pair in q_rest.values() for piece in pair]
     other_gated = project(
         gate_kernel, at[early:], [other_rows], [other_filtered, other_query], late, BF16
     )
-    own_gated = project(gate_kernel, at[early:], [own_rows], [own_filtered, own_query], late, BF16)
+    own_gated = project(
+        gate_kernel, at[early:], [own_rows], [own_filtered, own_query], late, BF16
+    )
 
     position = lax.axis_index("tp")
     z = position.astype(jnp.int32).reshape(1)
@@ -287,35 +303,34 @@
     def plus(a, b):
         return (a.astype(F32) + b.astype(F32)).astype(BF16)
 
-    def terms_of(pairs, gates, turned):
-        own, other = gates
-        leaving = terms(n_tp, z, other, pairs, (1, 0), turned)
-        return terms(n_tp, z, own, pairs, (0, 1), turned, from_partner(leaving))
+    def leaving_of(pairs, gates, turned):
+        return from_partner(terms(n_tp, z, gates[1], pairs, (1, 0), turned))
+
+    def terms_of(pairs, gates, turned, given):
+        return terms(n_tp, z, gates[0], pairs, (0, 1), turned, given)
 
     def chained(slots):
-        rising = falling = hop = None
+        rising = falling = None
         for step in range(n_tp - 1):
             send_up, send_down = slots[n_tp - 1 - step], slots[step + 1]
             if step:
                 send_up, send_down = plus(send_up, rising), plus(send_down, falling)
             rising = lax.ppermute(send_up, "tp", up)
             falling = lax.ppermute(send_down, "tp", down)
-            hop = hop or (rising, falling)
         total = slots[0].astype(F32) + rising.astype(F32) + falling.astype(F32)
-        return total, hop
-
-    o_rest = {(dy, dx): from_chip(o_x[0, dx], dy, 0) for dy, _ in o_y for _, dx in o_x}
+        return total
+
+    o_rest = crossed(o_x, o_y)
     out_pairs = {(0, 0): both_o, **o_x, **o_y, **o_rest}
     result = jnp.zeros((rows, model), BF16)
     gates = (own_gated, other_gated)
-    sets = [(0, 0)], [*o_x, *o_y], list(o_rest)
-    first_sum, hop = chained(terms_of([out_pairs[key] for key in sets[0]], gates, True))
-    gates, _ = lax.optimization_barrier((gates, hop))
-    middle = terms_of([out_pairs[key] for key in sets[1]], gates, False)
-    gates, middle = lax.optimization_barrier((gates, middle))
-    middle_sum = lax.psum_scatter(middle, "tp", scatter_dimension=0, tiled=True).astype(F32)
-    last_sum, _ = chained(terms_of([out_pairs[key] for key in sets[2]], gates, True))
-    for keys, mixed in zip(sets, (first_sum, middle_sum, last_sum)):
+    sets = [(0, 0), *o_x, *o_y], list(o_rest)
+    first, last = ([out_pairs[key] for key in keys] for keys in sets)
+    found = terms_of(first, gates, False, leaving_of(first, gates, False))
+    gates, found = lax.optimization_barrier((gates, found))
+    first_sum = lax.psum_scatter(found, "tp", scatter_dimension=0, tiled=True).astype(F32)
+    last_sum = chained(terms_of(last, gates, True, leaving_of(last, gates, True)))
+    for keys, mixed in zip(sets, (first_sum, last_sum)):
         for index, (dy, dx) in enumerate(keys):
             start = place(my_y + dy, my_x + dx, 0) * wide
             pair = mixed[:, index * 2 * wide : (index + 1) * 2 * wide]

time: 267 us -> 274 us (1.026)
  starting transfers between devices: 54.7 us -> 38.9 us
  waiting for transfers between devices: 134 us -> 146 us
  local copies, waits for them, and re-layouts: 16.1 us -> 23.7 us
  Pallas kernels: 41.3 us -> 45.4 us
    ppermute x1, waiting for transfers between devices: 0.01 us -> 14.9 us  [on_device(): lax.ppermute(last_tail, 'seq', [(2 * i + c, 2 * i + 2 + c) for i in range...]
    ppermute x6 -> x3, starting transfers between devices: 27.2 us -> 14 us  [chained(): rising = lax.ppermute(send_up, 'tp', up)]
    ppermute x6 -> x3, waiting for transfers between devices: 15.7 us -> 27.4 us  [chained(): falling = lax.ppermute(send_down, 'tp', down)]
    ppermute x13 -> x14, waiting for transfers between devices: 91.5 us -> 81.1 us  [from_chip(): return lax.ppermute(block, 'seq', route)]
    squeeze x2 -> x4, local copies, waits for them, and re-layouts: 1.11 us -> 5.91 us  [the longest x2 2.96 us: crossed(): along_x[0, dx][0]]
    pallas_call x14 -> x12, Pallas kernels: 41.3 us -> 45.4 us  [call(): pl.pallas_call(kernel, out_shape=out, in_specs=[pl.BlockSpec(memory_space...]
    ppermute x6 -> x3, starting transfers between devices: 7.75 us -> 3.88 us  [chained(): falling = lax.ppermute(send_down, 'tp', down)]
    ppermute x6 -> x3, waiting for transfers between devices: 16.1 us -> 12.3 us  [chained(): rising = lax.ppermute(send_up, 'tp', up)]
  transfers between devices with their start and end apart: 35 -> 29, of which waited for: 24 -> 19; matrix products, arithmetic and copies ran while one was open for 3% -> 4% of each run, Pallas kernels for 14% -> 14%
where the time goes in v6:
time: 274 us; the launch traced here: 273 us
  waiting for transfers between devices  146 us (53%)
  Pallas kernels  45.4 us (17%)
  starting transfers between devices  38.9 us (14%)
  local copies, waits for them, and re-layouts  23.7 us (9%)
  between operations  13.9 us (5%)
  other arithmetic  5.29 us (2%)
    ppermute x14, waiting for transfers between devices, from_chip(): return lax.ppermute(block, 'seq', route)  81.1 us
    pallas_call x12, Pallas kernels, call(): pl.pallas_call(kernel, out_shape=out, in_specs=[pl.BlockSpec(memory_space...  45.4 us
    ppermute x3, waiting for transfers between devices, chained(): falling = lax.ppermute(send_down, 'tp', down)  27.4 us
    ppermute x14, starting transfers between devices, from_chip(): return lax.ppermute(block, 'seq', route)  16.6 us
    ppermute x1, waiting for transfers between devices, on_device(): lax.ppermute(last_tail, 'seq', [(2 * i + c, 2 * i + 2 + c) for i in range...  14.9 us
    ppermute x3, starting transfers between devices, chained(): rising = lax.ppermute(send_up, 'tp', up)  14 us
    ppermute x3, waiting for transfers between devices, chained(): rising = lax.ppermute(send_up, 'tp', up)  12.3 us
    unnamed x46, local copies, waits for them, and re-layouts  11.5 us
  transfers between devices with their start and end apart: 29, of which 19 were waited for; matrix products, arithmetic and copies ran while one was open for 4% of the time, Pallas kernels for 14%

profile of v6, /device:TPU:0, one launch (start us, length us, event | category | flops | bytes accessed | tf_op | source)
XLA Modules:
  0.0 273.1 jit_solution(16123719192402566868)
XLA Ops:
  6.5 1.8 constant_dynamic-slice_fusion.3
  8.7 1.3 fusion.2
  10.6 1.3 constant_dynamic-slice_fusion.2
  12.0 2.9 %collective-permute-start.1 = (bf16[2,512,512]{2,1,0:T(8,128)(2,1)S(1)}, bf16[2,512,512]{2,1,0:T(8,128)(2,1)}, u32[]{:S(2)}, u32[]{:S(2)}) collective-permute-start(bf16[2,512,512]{2,1,0:T(8,128)(2,1)S(1)} %get-tuple-element.53.refs_1_), channel_id=1, source_target_pairs={{8,0},{12,4},{0,8},{4,12},{24,16},{28,20},{16,24},{20,28},{9,1},{1... | collective-permute-start | bytes 3145736 | tf_op jit(solution)/shard_map/ppermute | solution.py:186
  14.9 1.5 collective-permute-start.3
  17.3 1.3 dynamic-slice_bitcast_fusion
  18.8 1.8 collective-permute-done.6
  20.6 18.4 %collective-permute-done.1.refs_3_ = bf16[2,512,512]{2,1,0:T(8,128)(2,1)} collective-permute-done((bf16[2,512,512]{2,1,0:T(8,128)(2,1)S(1)}, bf16[2,512,512]{2,1,0:T(8,128)(2,1)}, u32[]{:S(2)}, u32[]{:S(2)}) %collective-permute-start.1) | collective-permute-done | bytes 1048608 | tf_op jit(solution)/shard_map/ppermute | solution.py:186
  39.0 2.0 collective-permute-done.3.refs_5_
  41.0 1.0 copy-done.11
  42.0 18.9 %collective-permute-done.2.refs_4_ = bf16[2,512,512]{2,1,0:T(8,128)(2,1)S(1)} collective-permute-done((bf16[2,512,512]{2,1,0:T(8,128)(2,1)S(1)}, bf16[2,512,512]{2,1,0:T(8,128)(2,1)S(1)}, u32[]{:S(2)}, u32[]{:S(2)}) %collective-permute-start.2) | collective-permute-done | bytes 1048608 | tf_op jit(solution)/shard_map/ppermute | solution.py:186
  60.8 1.0 copy-done.14
  62.4 1.5 collective-permute-start.7
  63.9 1.2 collective-permute-start.8
  65.1 0.9 collective-permute-start.9
  66.5 22.3 %collective-permute-done.7.refs_7_ = bf16[2,512,512]{2,1,0:T(8,128)(2,1)} collective-permute-done((bf16[2,512,512]{2,1,0:T(8,128)(2,1)}, bf16[2,512,512]{2,1,0:T(8,128)(2,1)}, u32[]{:S(2)}, u32[]{:S(2)}) %collective-permute-start.7) | collective-permute-done | bytes 1048608 | tf_op jit(solution)/shard_map/ppermute | solution.py:186
  88.8 1.5 collective-permute-done.8.refs_8_
  90.3 3.3 %all-gather.2.cloned.1.call-done.refs_0_ = bf16[512,4096]{1,0:T(8,128)(2,1)} async-done(((bf16[128,4096]{1,0:T(8,128)(2,1)}), bf16[512,4096]{1,0:T(8,128)(2,1)}) %all-gather.2.cloned.1.call-update) | async-done | bytes 4194320 | tf_op jit(solution)/shard_map/all_gather | solution.py:234
  93.7 1.2 copy-done.9
  94.9 1.2 copy-done.12
  96.1 1.2 copy-done.15
  97.3 7.9 %shard_map.64.product_ref = f32[512,512]{1,0:T(8,128)S(1)} custom-call(s32[8]{0:T(128)S(1)} %stack.58.at_ref._, bf16[512,4096]{1,0:T(8,128)(2,1)} %all-gather.2.cloned.1.call-done.refs_0_, bf16[2,512,512]{2,1,0:T(8,128)(2,1)S(1)} %get-tuple-element.53.refs_1_, bf16[2,512,512]{2,1,0:T(8,128)(2,1)S(1)} %copy-done.9, ...), custom_call_target="tpu_custom_call" | custom-call | flops 1 | bytes 1 | tf_op jit(solution)/shard_map/pallas_call | solution.py:81
  105.2 1.0 copy-done.2
  106.2 4.3 %collective-permute-done.9.refs_2_ = bf16[2,512,512]{2,1,0:T(8,128)(2,1)} collective-permute-done((bf16[2,512,512]{2,1,0:T(8,128)(2,1)S(1)}, bf16[2,512,512]{2,1,0:T(8,128)(2,1)}, u32[]{:S(2)}, u32[]{:S(2)}) %collective-permute-start.9) | collective-permute-done | bytes 1048608 | tf_op jit(solution)/shard_map/ppermute | solution.py:186
  110.6 4.7 %shard_map.65.refs_2_ = f32[512,512]{1,0:T(8,128)S(1)} custom-call(s32[8]{0:T(128)S(1)} %stack.58.at_ref._, bf16[512,4096]{1,0:T(8,128)(2,1)} %all-gather.2.cloned.1.call-done.refs_0_, bf16[2,512,512]{2,1,0:T(8,128)(2,1)S(1)} %pad_maximum_fusion.refs_1_, bf16[2,512,512]{2,1,0:T(8,128)(2,1)} %collective-permute-done.9.refs_2_, ...), custom_call_target="tpu_custom_call" | custom-call | flops 1 | bytes 1 | tf_op jit(solution)/shard_map/pallas_call | solution.py:81
  115.3 1.6 collective-permute-start.15
  117.4 1.9 slice_bitcast_fusion.3
  119.2 1.5 collective-permute-start.13
  120.8 1.9 slice_bitcast_fusion.2
  123.2 7.9 %shard_map.66.product_ref = f32[512,512]{1,0:T(8,128)S(1)} custom-call(s32[8]{0:T(128)S(1)} %stack.58.at_ref._, bf16[512,4096]{1,0:T(8,128)(2,1)} %collective-permute-done.11.refs_0_, bf16[2,512,512]{2,1,0:T(8,128)(2,1)S(1)} %get-tuple-element.53.refs_1_, bf16[2,512,512]{2,1,0:T(8,128)(2,1)S(1)} %copy-done.10, ...), custom_call_target="tpu_custom_call" | custom-call | flops 1 | bytes 1 | tf_op jit(solution)/shard_map/pallas_call | solution.py:81
  131.1 1.0 copy-done.4
  132.8 3.6 %collective-permute-start.12 = (f32[8,512]{1,0:T(8,128)S(1)}, f32[8,512]{1,0:T(8,128)S(1)}, u32[]{:S(2)}, u32[]{:S(2)}) collective-permute-start(f32[8,512]{1,0:T(8,128)S(1)} %slice_select_fusion.4), channel_id=1, source_target_pairs={{0,8},{4,12},{8,16},{12,20},{16,24},{20,28},{1,9},{5,13},{9,17},{1... | collective-permute-start | bytes 49160 | tf_op jit(solution)/shard_map/ppermute | solution.py:271
  136.7 14.9 %collective-permute-done.12 = f32[8,512]{1,0:T(8,128)S(1)} collective-permute-done((f32[8,512]{1,0:T(8,128)S(1)}, f32[8,512]{1,0:T(8,128)S(1)}, u32[]{:S(2)}, u32[]{:S(2)}) %collective-permute-start.12) | collective-permute-done | bytes 16416 | tf_op jit(solution)/shard_map/ppermute | solution.py:271
  151.5 0.7 broadcast_select_fusion
  152.3 1.2 copy-done.3
  153.5 2.0 shard_map.67.refs_1_
  155.5 2.0 shard_map.68.refs_1_
  157.6 4.6 %shard_map.70.refs_2_ = f32[512,512]{1,0:T(8,128)S(1)} custom-call(s32[8]{0:T(128)S(1)} %stack.58.at_ref._, bf16[512,4096]{1,0:T(8,128)(2,1)} %collective-permute-done.11.refs_0_, bf16[2,512,512]{2,1,0:T(8,128)(2,1)S(1)} %pad_maximum_fusion.refs_1_, bf16[2,512,512]{2,1,0:T(8,128)(2,1)} %collective-permute-done.9.refs_2_, ...), custom_call_target="tpu_custom_call" | custom-call | flops 1 | bytes 1 | tf_op jit(solution)/shard_map/pallas_call | solution.py:81
  162.2 3.2 %shard_map.71.gated_ref = bf16[512,512]{1,0:T(8,128)(2,1)S(1)} custom-call(s32[2]{0:T(128)S(1)} %pad_add_fusion.at_ref, bf16[512,4096]{1,0:T(8,128)(2,1)} %collective-permute-done.11.refs_0_, f32[512,512]{1,0:T(8,128)S(1)} %shard_map.68.refs_1_, f32[512,512]{1,0:T(8,128)S(1)} %shard_map.70.refs_2_, bf16[512,512]{1,0:T(8,128)(2,1)} %collective-permute-done.13.refs_3_, ...), custom_call_target="tpu_custom_call" | custom-call | flops 1 | bytes 1 | tf_op jit(solution)/shard_map/pallas_call | solution.py:81
  165.4 3.4 %shard_map.72 = bf16[512,3072]{1,0:T(8,128)(2,1)S(1)} custom-call(s32[1]{0:T(128)} %bitcast.14.z_ref, bf16[512,512]{1,0:T(8,128)(2,1)S(1)} %shard_map.71.gated_ref, bf16[2,512,512]{2,1,0:T(8,128)(2,1)S(1)} %pad_maximum_fusion.1.refs_0_, bf16[2,512,512]{2,1,0:T(8,128)(2,1)} %collective-permute-done.15.refs_1_, ...), custom_call_target="tpu_custom_call" | custom-call | flops 1 | bytes 1 | tf_op jit(solution)/shard_map/pallas_call | solution.py:81
  169.0 3.2 %shard_map.69.gated_ref = bf16[512,512]{1,0:T(8,128)(2,1)S(1)} custom-call(s32[2]{0:T(128)S(1)} %pad_add_fusion.at_ref, bf16[512,4096]{1,0:T(8,128)(2,1)} %all-gather.2.cloned.1.call-done.refs_0_, f32[512,512]{1,0:T(8,128)S(1)} %shard_map.67.refs_1_, f32[512,512]{1,0:T(8,128)S(1)} %copy-done.7, bf16[512,512]{1,0:T(8,128)(2,1)} %collective-permute-done.13.refs_3_, ...), custom_call_target="tpu_custom_call" | custom-call | flops 1 | bytes 1 | tf_op jit(solution)/shard_map/pallas_call | solution.py:81
  172.2 2.4 collective-permute-done.17.refs_3_
  174.6 5.0 %shard_map.73 = bf16[512,3072]{1,0:T(8,128)(2,1)} custom-call(s32[1]{0:T(128)} %bitcast.14.z_ref, bf16[512,512]{1,0:T(8,128)(2,1)S(1)} %shard_map.69.gated_ref, bf16[2,512,512]{2,1,0:T(8,128)(2,1)S(1)} %pad_maximum_fusion.1.refs_0_, bf16[2,512,512]{2,1,0:T(8,128)(2,1)} %collective-permute-done.15.refs_1_, ...), custom_call_target="tpu_custom_call" | custom-call | flops 1 | bytes 1 | tf_op jit(solution)/shard_map/pallas_call | solution.py:81
  179.7 1.1 slice_bitcast_fusion.1
  180.7 2.6 collective-permute-start.18
  183.4 1.1 slice_bitcast_fusion
  184.9 10.7 %collective-permute-done.18.refs_0_ = bf16[512,512]{1,0:T(8,128)(2,1)S(1)} collective-permute-done((bf16[512,512]{1,0:T(8,128)(2,1)S(1)}, bf16[512,512]{1,0:T(8,128)(2,1)S(1)}, u32[]{:S(2)}, u32[]{:S(2)}) %collective-permute-start.18) | collective-permute-done | bytes 524320 | tf_op jit(solution)/shard_map/ppermute | solution.py:186
  195.6 2.6 collective-permute-done.19.refs_1_
  199.0 2.6 collective-permute-done.20.refs_2_
  202.3 3.5 %collective-permute-start.21 = (bf16[128,1024]{1,0:T(8,128)(2,1)S(1)}, bf16[128,1024]{1,0:T(8,128)(2,1)S(1)}, u32[]{:S(2)}, u32[]{:S(2)}) collective-permute-start(bf16[128,1024]{1,0:T(8,128)(2,1)S(1)} %get-tuple-element.78), channel_id=1, source_target_pairs={{0,1},{1,2},{2,3},{4,5},{5,6},{6,7},{8,9},{9,10},{10,11},{12,13},{... | collective-permute-start | bytes 786440 | tf_op jit(solution)/shard_map/ppermute | solution.py:318
  205.9 1.3 collective-permute-start.24
  207.2 10.8 %collective-permute-done.21 = bf16[128,1024]{1,0:T(8,128)(2,1)S(1)} collective-permute-done((bf16[128,1024]{1,0:T(8,128)(2,1)S(1)}, bf16[128,1024]{1,0:T(8,128)(2,1)S(1)}, u32[]{:S(2)}, u32[]{:S(2)}) %collective-permute-start.21) | collective-permute-done | bytes 262176 | tf_op jit(solution)/shard_map/ppermute | solution.py:318
  217.9 10.4 %collective-permute-done.24 = bf16[128,1024]{1,0:T(8,128)(2,1)S(1)} collective-permute-done((bf16[128,1024]{1,0:T(8,128)(2,1)S(1)}, bf16[128,1024]{1,0:T(8,128)(2,1)S(1)}, u32[]{:S(2)}, u32[]{:S(2)}) %collective-permute-start.24) | collective-permute-done | bytes 262176 | tf_op jit(solution)/shard_map/ppermute | solution.py:319
  228.5 1.3 collective-permute-start.25
  229.8 4.6 %collective-permute-start.22 = (bf16[128,1024]{1,0:T(8,128)(2,1)S(1)}, bf16[128,1024]{1,0:T(8,128)(2,1)S(1)}, u32[]{:S(2)}, u32[]{:S(2)}) collective-permute-start(bf16[128,1024]{1,0:T(8,128)(2,1)S(1)} %get-tuple-element.95), channel_id=1, source_target_pairs={{0,1},{1,2},{2,3},{4,5},{5,6},{6,7},{8,9},{9,10},{10,11},{12,13},{... | collective-permute-start | bytes 786440 | tf_op jit(solution)/shard_map/ppermute | solution.py:318
  234.4 14.6 %collective-permute-done.25 = bf16[128,1024]{1,0:T(8,128)(2,1)S(1)} collective-permute-done((bf16[128,1024]{1,0:T(8,128)(2,1)S(1)}, bf16[128,1024]{1,0:T(8,128)(2,1)S(1)}, u32[]{:S(2)}, u32[]{:S(2)}) %collective-permute-start.25) | collective-permute-done | bytes 262176 | tf_op jit(solution)/shard_map/ppermute | solution.py:319
  249.1 1.3 collective-permute-start.26
  250.5 6.0 %collective-permute-start.23 = (bf16[128,1024]{1,0:T(8,128)(2,1)S(1)}, bf16[128,1024]{1,0:T(8,128)(2,1)S(1)}, u32[]{:S(2)}, u32[]{:S(2)}) collective-permute-start(bf16[128,1024]{1,0:T(8,128)(2,1)S(1)} %add_convert_fusion.1), channel_id=1, source_target_pairs={{0,1},{1,2},{2,3},{4,5},{5,6},{6,7},{8,9},{9,10},{10,11},{12,13},{... | collective-permute-start | bytes 786440 | tf_op jit(solution)/shard_map/ppermute | solution.py:318
  256.5 2.3 collective-permute-done.26
  258.8 1.5 collective-permute-done.23
  260.5 1.4 fusion.25
  262.2 1.0 copy-done.18
  264.5 1.0 copy-done.21
  265.4 0.9 fusion.21
  (85 shorter events, 9.5 us)
Async XLA Ops:
  6.5 104.0 %copy-start = (f32[7,64]{1,0:T(8,128)S(1)}, f32[7,64]{1,0:T(8,128)}, u32[]{:S(2)}) copy-start(f32[7,64]{1,0:T(8,128)} %param.9) | copy-start | bytes 5380
  6.5 87.1 %all-gather.2.cloned.1.call-start = ((), (), s32[]{:S(2)}) async-start(), calls=%async_computation.1 | async-start | bytes 5242880 | tf_op jit(solution)/shard_map/all_gather | solution.py:234
  6.5 1.9 copy-start.17
  6.5 2.2 copy-start.22
  10.0 250.4 %reduce-scatter.2.cloned.1.call-start = ((), (), s32[]{:S(2)}) async-start(), calls=%async_computation.2 | async-start | bytes 3932160 | tf_op jit(solution)/shard_map/reduce_scatter | solution.py:331
  10.1 6.4 %collective-permute-start = (bf16[2,512,512]{2,1,0:T(8,128)(2,1)S(1)}, bf16[2,512,512]{2,1,0:T(8,128)(2,1)S(1)}, u32[]{:S(2)}, u32[]{:S(2)}) collective-permute-start(bf16[2,512,512]{2,1,0:T(8,128)(2,1)S(1)} %get-tuple-element.82), channel_id=1, source_target_pairs={{0,4},{4,0},{8,12},{12,8},{16,20},{20,16},{24,28},{28,24},{1,5},{5... | collective-permute-start | bytes 3145736 | tf_op jit(solution)/shard_map/ppermute | solution.py:189
  11.9 6.7 %collective-permute-start.5 = (bf16[512,512]{1,0:T(8,128)(2,1)S(1)}, bf16[512,512]{1,0:T(8,128)(2,1)S(1)}, u32[]{:S(2)}, u32[]{:S(2)}) collective-permute-start(bf16[512,512]{1,0:T(8,128)(2,1)S(1)} %get-tuple-element.80), channel_id=1, source_target_pairs={{0,4},{4,0},{8,12},{12,8},{16,20},{20,16},{24,28},{28,24},{1,5},{5... | collective-permute-start | bytes 1572872 | tf_op jit(solution)/shard_map/ppermute | solution.py:189
  12.0 27.0 %collective-permute-start.1 = (bf16[2,512,512]{2,1,0:T(8,128)(2,1)S(1)}, bf16[2,512,512]{2,1,0:T(8,128)(2,1)}, u32[]{:S(2)}, u32[]{:S(2)}) collective-permute-start(bf16[2,512,512]{2,1,0:T(8,128)(2,1)S(1)} %get-tuple-element.53.refs_1_), channel_id=1, source_target_pairs={{8,0},{12,4},{0,8},{4,12},{24,16},{28,20},{16,24},{20,28},{9,1},{1... | collective-permute-start | bytes 3145736 | tf_op jit(solution)/shard_map/ppermute | solution.py:186
  14.9 26.1 %collective-permute-start.3 = (bf16[2,512,512]{2,1,0:T(8,128)(2,1)S(1)}, bf16[2,512,512]{2,1,0:T(8,128)(2,1)S(1)}, u32[]{:S(2)}, u32[]{:S(2)}) collective-permute-start(bf16[2,512,512]{2,1,0:T(8,128)(2,1)S(1)} %get-tuple-element.53.refs_1_), channel_id=1, source_target_pairs={{16,0},{20,4},{24,8},{28,12},{0,16},{4,20},{8,24},{12,28},{17,1},{... | collective-permute-start | bytes 3145736 | tf_op jit(solution)/shard_map/ppermute | solution.py:186
  16.5 2.3 copy-start.8
  16.5 44.3 %collective-permute-start.2 = (bf16[2,512,512]{2,1,0:T(8,128)(2,1)S(1)}, bf16[2,512,512]{2,1,0:T(8,128)(2,1)S(1)}, u32[]{:S(2)}, u32[]{:S(2)}) collective-permute-start(bf16[2,512,512]{2,1,0:T(8,128)(2,1)S(1)} %collective-permute-done.refs_2_), channel_id=1, source_target_pairs={{8,0},{12,4},{0,8},{4,12},{24,16},{28,20},{16,24},{20,28},{9,1},{1... | collective-permute-start | bytes 3145736 | tf_op jit(solution)/shard_map/ppermute | solution.py:186
  17.0 45.4 %collective-permute-start.4 = (bf16[2,512,512]{2,1,0:T(8,128)(2,1)S(1)}, bf16[2,512,512]{2,1,0:T(8,128)(2,1)}, u32[]{:S(2)}, u32[]{:S(2)}) collective-permute-start(bf16[2,512,512]{2,1,0:T(8,128)(2,1)S(1)} %collective-permute-done.refs_2_), channel_id=1, source_target_pairs={{16,0},{20,4},{24,8},{28,12},{0,16},{4,20},{8,24},{12,28},{17,1},{... | collective-permute-start | bytes 3145736 | tf_op jit(solution)/shard_map/ppermute | solution.py:186
  18.6 2.0 collective-permute-start.6
  41.0 1.0 copy-start.11
  60.8 1.0 copy-start.14
  62.4 26.4 %collective-permute-start.7 = (bf16[2,512,512]{2,1,0:T(8,128)(2,1)}, bf16[2,512,512]{2,1,0:T(8,128)(2,1)}, u32[]{:S(2)}, u32[]{:S(2)}) collective-permute-start(bf16[2,512,512]{2,1,0:T(8,128)(2,1)} %collective-permute-done.1.refs_3_), channel_id=1, source_target_pairs={{16,0},{20,4},{24,8},{28,12},{0,16},{4,20},{8,24},{12,28},{17,1},{... | collective-permute-start | bytes 3145736 | tf_op jit(solution)/shard_map/ppermute | solution.py:186
  63.9 26.4 %collective-permute-start.8 = (bf16[2,512,512]{2,1,0:T(8,128)(2,1)}, bf16[2,512,512]{2,1,0:T(8,128)(2,1)}, u32[]{:S(2)}, u32[]{:S(2)}) collective-permute-start(bf16[2,512,512]{2,1,0:T(8,128)(2,1)} %collective-permute-done.4.refs_6_), channel_id=1, source_target_pairs={{8,0},{12,4},{0,8},{4,12},{24,16},{28,20},{16,24},{20,28},{9,1},{1... | collective-permute-start | bytes 3145736 | tf_op jit(solution)/shard_map/ppermute | solution.py:186
  65.1 45.4 %collective-permute-start.9 = (bf16[2,512,512]{2,1,0:T(8,128)(2,1)S(1)}, bf16[2,512,512]{2,1,0:T(8,128)(2,1)}, u32[]{:S(2)}, u32[]{:S(2)}) collective-permute-start(bf16[2,512,512]{2,1,0:T(8,128)(2,1)S(1)} %pad_maximum_fusion.refs_1_), channel_id=1, source_target_pairs={{8,0},{12,4},{0,8},{4,12},{24,16},{28,20},{16,24},{20,28},{9,1},{1... | collective-permute-start | bytes 3145736 | tf_op jit(solution)/shard_map/ppermute | solution.py:186
  65.9 44.6 %collective-permute-start.10 = (bf16[2,512,512]{2,1,0:T(8,128)(2,1)S(1)}, bf16[2,512,512]{2,1,0:T(8,128)(2,1)}, u32[]{:S(2)}, u32[]{:S(2)}) collective-permute-start(bf16[2,512,512]{2,1,0:T(8,128)(2,1)S(1)} %pad_maximum_fusion.refs_1_), channel_id=1, source_target_pairs={{16,0},{20,4},{24,8},{28,12},{0,16},{4,20},{8,24},{12,28},{17,1},{... | collective-permute-start | bytes 3145736 | tf_op jit(solution)/shard_map/ppermute | solution.py:186
  93.7 1.2 copy-start.9
  94.9 1.2 copy-start.12
  96.1 1.2 copy-start.15
  105.2 1.0 copy-start.2
  110.5 12.7 %collective-permute-start.11 = (bf16[512,4096]{1,0:T(8,128)(2,1)}, bf16[512,4096]{1,0:T(8,128)(2,1)}, u32[]{:S(2)}, u32[]{:S(2)}) collective-permute-start(bf16[512,4096]{1,0:T(8,128)(2,1)} %all-gather.2.cloned.1.call-done.refs_0_), channel_id=1, source_target_pairs={{0,4},{4,0},{8,12},{12,8},{16,20},{20,16},{24,28},{28,24},{1,5},{5... | collective-permute-start | bytes 12582920 | tf_op jit(solution)/shard_map/ppermute | solution.py:189
  110.6 12.6 %copy-start.16 = (bf16[2,512,512]{2,1,0:T(8,128)(2,1)S(1)}, bf16[2,512,512]{2,1,0:T(8,128)(2,1)}, u32[]{:S(2)}) copy-start(bf16[2,512,512]{2,1,0:T(8,128)(2,1)} %copy-done.14) | copy-start | bytes 3145732
  115.3 7.9 %copy-start.6 = (f32[512,512]{1,0:T(8,128)}, f32[512,512]{1,0:T(8,128)S(1)}, u32[]{:S(2)}) copy-start(f32[512,512]{1,0:T(8,128)S(1)} %shard_map.65.refs_2_) | copy-start | bytes 3145732
  115.3 7.9 %copy-start.10 = (bf16[2,512,512]{2,1,0:T(8,128)(2,1)S(1)}, bf16[2,512,512]{2,1,0:T(8,128)(2,1)}, u32[]{:S(2)}) copy-start(bf16[2,512,512]{2,1,0:T(8,128)(2,1)} %copy-done.8) | copy-start | bytes 3145732
  115.3 7.9 %copy-start.13 = (bf16[2,512,512]{2,1,0:T(8,128)(2,1)S(1)}, bf16[2,512,512]{2,1,0:T(8,128)(2,1)}, u32[]{:S(2)}) copy-start(bf16[2,512,512]{2,1,0:T(8,128)(2,1)} %copy-done.11) | copy-start | bytes 3145732
  115.3 50.1 %collective-permute-start.15 = (bf16[2,512,512]{2,1,0:T(8,128)(2,1)S(1)}, bf16[2,512,512]{2,1,0:T(8,128)(2,1)}, u32[]{:S(2)}, u32[]{:S(2)}) collective-permute-start(bf16[2,512,512]{2,1,0:T(8,128)(2,1)S(1)} %pad_maximum_fusion.1.refs_0_), channel_id=1, source_target_pairs={{8,0},{12,4},{0,8},{4,12},{24,16},{28,20},{16,24},{20,28},{9,1},{1... | collective-permute-start | bytes 3145736 | tf_op jit(solution)/shard_map/ppermute | solution.py:186
  116.8 48.6 %collective-permute-start.16 = (bf16[2,512,512]{2,1,0:T(8,128)(2,1)S(1)}, bf16[2,512,512]{2,1,0:T(8,128)(2,1)}, u32[]{:S(2)}, u32[]{:S(2)}) collective-permute-start(bf16[2,512,512]{2,1,0:T(8,128)(2,1)S(1)} %pad_maximum_fusion.1.refs_0_), channel_id=1, source_target_pairs={{16,0},{20,4},{24,8},{28,12},{0,16},{4,20},{8,24},{12,28},{17,1},{... | collective-permute-start | bytes 3145736 | tf_op jit(solution)/shard_map/ppermute | solution.py:186
  119.2 42.9 %collective-permute-start.13 = (bf16[512,512]{1,0:T(8,128)(2,1)}, bf16[512,512]{1,0:T(8,128)(2,1)}, u32[]{:S(2)}, u32[]{:S(2)}) collective-permute-start(bf16[512,512]{1,0:T(8,128)(2,1)} %slice_bitcast_fusion.3), channel_id=1, source_target_pairs={{16,0},{20,4},{24,8},{28,12},{0,16},{4,20},{8,24},{12,28},{17,1},{... | collective-permute-start | bytes 1572872 | tf_op jit(solution)/shard_map/ppermute | solution.py:186
  122.6 39.6 %collective-permute-start.14 = (bf16[512,512]{1,0:T(8,128)(2,1)}, bf16[512,512]{1,0:T(8,128)(2,1)}, u32[]{:S(2)}, u32[]{:S(2)}) collective-permute-start(bf16[512,512]{1,0:T(8,128)(2,1)} %slice_bitcast_fusion.2), channel_id=1, source_target_pairs={{8,0},{12,4},{0,8},{4,12},{24,16},{28,20},{16,24},{20,28},{9,1},{1... | collective-permute-start | bytes 1572872 | tf_op jit(solution)/shard_map/ppermute | solution.py:186
  131.1 1.0 copy-start.4
  132.8 18.7 %collective-permute-start.12 = (f32[8,512]{1,0:T(8,128)S(1)}, f32[8,512]{1,0:T(8,128)S(1)}, u32[]{:S(2)}, u32[]{:S(2)}) collective-permute-start(f32[8,512]{1,0:T(8,128)S(1)} %slice_select_fusion.4), channel_id=1, source_target_pairs={{0,8},{4,12},{8,16},{12,20},{16,24},{20,28},{1,9},{5,13},{9,17},{1... | collective-permute-start | bytes 49160 | tf_op jit(solution)/shard_map/ppermute | solution.py:271
  152.3 1.2 copy-start.3
  153.5 2.0 copy-start.5
  165.4 3.5 %copy-start.7 = (f32[512,512]{1,0:T(8,128)S(1)}, f32[512,512]{1,0:T(8,128)}, u32[]{:S(2)}) copy-start(f32[512,512]{1,0:T(8,128)} %copy-done.6) | copy-start | bytes 3145732
  168.9 5.7 %collective-permute-start.17 = (bf16[512,3072]{1,0:T(8,128)(2,1)S(1)}, bf16[512,3072]{1,0:T(8,128)(2,1)S(1)}, u32[]{:S(2)}, u32[]{:S(2)}) collective-permute-start(bf16[512,3072]{1,0:T(8,128)(2,1)S(1)} %shard_map.72), channel_id=1, source_target_pairs={{0,4},{4,0},{8,12},{12,8},{16,20},{20,16},{24,28},{28,24},{1,5},{5... | collective-permute-start | bytes 9437192 | tf_op jit(solution)/shard_map/ppermute | solution.py:189
  180.7 14.8 %collective-permute-start.18 = (bf16[512,512]{1,0:T(8,128)(2,1)S(1)}, bf16[512,512]{1,0:T(8,128)(2,1)S(1)}, u32[]{:S(2)}, u32[]{:S(2)}) collective-permute-start(bf16[512,512]{1,0:T(8,128)(2,1)S(1)} %slice_bitcast_fusion.1), channel_id=1, source_target_pairs={{16,0},{20,4},{24,8},{28,12},{0,16},{4,20},{8,24},{12,28},{17,1},{... | collective-permute-start | bytes 1572872 | tf_op jit(solution)/shard_map/ppermute | solution.py:186
  184.4 13.8 %collective-permute-start.19 = (bf16[512,512]{1,0:T(8,128)(2,1)S(1)}, bf16[512,512]{1,0:T(8,128)(2,1)S(1)}, u32[]{:S(2)}, u32[]{:S(2)}) collective-permute-start(bf16[512,512]{1,0:T(8,128)(2,1)S(1)} %slice_bitcast_fusion), channel_id=1, source_target_pairs={{8,0},{12,4},{0,8},{4,12},{24,16},{28,20},{16,24},{20,28},{9,1},{1... | collective-permute-start | bytes 1572872 | tf_op jit(solution)/shard_map/ppermute | solution.py:186
  198.9 2.7 collective-permute-start.20
  202.3 15.6 %collective-permute-start.21 = (bf16[128,1024]{1,0:T(8,128)(2,1)S(1)}, bf16[128,1024]{1,0:T(8,128)(2,1)S(1)}, u32[]{:S(2)}, u32[]{:S(2)}) collective-permute-start(bf16[128,1024]{1,0:T(8,128)(2,1)S(1)} %get-tuple-element.78), channel_id=1, source_target_pairs={{0,1},{1,2},{2,3},{4,5},{5,6},{6,7},{8,9},{9,10},{10,11},{12,13},{... | collective-permute-start | bytes 786440 | tf_op jit(solution)/shard_map/ppermute | solution.py:318
  205.9 22.5 %collective-permute-start.24 = (bf16[128,1024]{1,0:T(8,128)(2,1)S(1)}, bf16[128,1024]{1,0:T(8,128)(2,1)S(1)}, u32[]{:S(2)}, u32[]{:S(2)}) collective-permute-start(bf16[128,1024]{1,0:T(8,128)(2,1)S(1)} %get-tuple-element.76), channel_id=1, source_target_pairs={{1,0},{2,1},{3,2},{5,4},{6,5},{7,6},{9,8},{10,9},{11,10},{13,12},{... | collective-permute-start | bytes 786440 | tf_op jit(solution)/shard_map/ppermute | solution.py:319
  228.5 20.5 %collective-permute-start.25 = (bf16[128,1024]{1,0:T(8,128)(2,1)S(1)}, bf16[128,1024]{1,0:T(8,128)(2,1)S(1)}, u32[]{:S(2)}, u32[]{:S(2)}) collective-permute-start(bf16[128,1024]{1,0:T(8,128)(2,1)S(1)} %get-tuple-element.96), channel_id=1, source_target_pairs={{1,0},{2,1},{3,2},{5,4},{6,5},{7,6},{9,8},{10,9},{11,10},{13,12},{... | collective-permute-start | bytes 786440 | tf_op jit(solution)/shard_map/ppermute | solution.py:319
  229.8 20.6 %collective-permute-start.22 = (bf16[128,1024]{1,0:T(8,128)(2,1)S(1)}, bf16[128,1024]{1,0:T(8,128)(2,1)S(1)}, u32[]{:S(2)}, u32[]{:S(2)}) collective-permute-start(bf16[128,1024]{1,0:T(8,128)(2,1)S(1)} %get-tuple-element.95), channel_id=1, source_target_pairs={{0,1},{1,2},{2,3},{4,5},{5,6},{6,7},{8,9},{9,10},{10,11},{12,13},{... | collective-permute-start | bytes 786440 | tf_op jit(solution)/shard_map/ppermute | solution.py:318
  249.1 9.7 %collective-permute-start.26 = (bf16[128,1024]{1,0:T(8,128)(2,1)S(1)}, bf16[128,1024]{1,0:T(8,128)(2,1)S(1)}, u32[]{:S(2)}, u32[]{:S(2)}) collective-permute-start(bf16[128,1024]{1,0:T(8,128)(2,1)S(1)} %add_convert_fusion), channel_id=1, source_target_pairs={{1,0},{2,1},{3,2},{5,4},{6,5},{7,6},{9,8},{10,9},{11,10},{13,12},{... | collective-permute-start | bytes 786440 | tf_op jit(solution)/shard_map/ppermute | solution.py:319
  250.5 9.8 %collective-permute-start.23 = (bf16[128,1024]{1,0:T(8,128)(2,1)S(1)}, bf16[128,1024]{1,0:T(8,128)(2,1)S(1)}, u32[]{:S(2)}, u32[]{:S(2)}) collective-permute-start(bf16[128,1024]{1,0:T(8,128)(2,1)S(1)} %add_convert_fusion.1), channel_id=1, source_target_pairs={{0,1},{1,2},{2,3},{4,5},{5,6},{6,7},{8,9},{9,10},{10,11},{12,13},{... | collective-permute-start | bytes 786440 | tf_op jit(solution)/shard_map/ppermute | solution.py:318
  260.5 1.5 copy-start.19
  262.0 1.2 copy-start.18
  262.0 1.9 copy-start.20
  264.2 2.1 copy-start.1
  264.4 1.0 copy-start.21
Sparse Core Ops, SparseCore 0:
  10.2 83.4 all-gather.1
  179.8 72.6 reduce-scatter.1

commit v7 on v6

--- a/solution.py
+++ b/solution.py
@@ -53,6 +53,24 @@
         out_ref[rows, tile] = key.astype(BF16).astype(F32) * value.astype(BF16).astype(F32)
 
 
+def joined_kernel(at_ref, before_ref, x_ref, *refs):
+    pieces, (rim_ref, out_ref, joined) = refs[:-3], refs[-3:]
+    pad = before_ref.shape[0]
+    joined[:pad] = before_ref[...]
+    joined[pad:] = x_ref[...]
+    deep = pieces[0].shape[1]
+    for _, _, tile in blocks_of([x_ref], out_ref):
+        key = value = None
+        for index, piece in enumerate(pieces):
+            x = columns_of(joined, at_ref, index, deep)
+            new_key, new_value = dot(x, piece[0, :, tile]), dot(x, piece[1, :, tile])
+            key = new_key if key is None else key + new_key
+            value = new_value if value is None else value + new_value
+        product = key.astype(BF16).astype(F32) * value.astype(BF16).astype(F32)
+        rim_ref[:, tile] = product[:pad]
+        out_ref[:, tile] = product[pad:]
+
+
 def query_kernel(parts, at_ref, *refs):
     xs, pairs, out_ref = refs[:parts], refs[parts:-1], refs[-1]
     deep = pairs[0].shape[1]
@@ -93,6 +111,14 @@
     rows = sum(x.shape[0] for x in xs)
     out = jax.ShapeDtypeStruct((rows, pieces[0].shape[-1]), out_dtype)
     return call(functools.partial(kernel, len(xs)), at, (*xs, *extra, *pieces), out)
+
+
+def project_joined(at, before, x, pieces):
+    half = pieces[0].shape[-1]
+    pad, length = before.shape[0], x.shape[0]
+    out = [jax.ShapeDtypeStruct((rows, half), F32) for rows in (pad, length)]
+    scratch = [pltpu.VMEM((pad + length, x.shape[1]), BF16)]
+    return call(joined_kernel, at, (before, x, *pieces), out, scratch)
 
 
 def filter_kernel(_, product_ref, halo_ref, taps_ref, out_ref, held):
@@ -254,25 +280,24 @@
     early = 2 * (ny + nx - 1)
 
     own_product = project(product_kernel, at, [own_rows], [], kv_pieces, F32)
-    rows_then, q_x, q_y, own_product = lax.optimization_barrier((own_rows, q_x, q_y, own_product))
+    reach = filters.shape[0] - 1
+    pad = -(-reach // 16) * 16
+    ends = [
+        lax.ppermute(own_rows[length - pad :], "seq", [(2 * i + 1, 2 * i + 2 + c) for i in range(chips - 1)])
+        for c in range(2)
+    ]
+    before = jnp.where(core == 0, ends[0], ends[1])
+    ready = (own_rows, q_x, q_y, own_product, before)
+    rows_then, q_x, q_y, own_product, before = lax.optimization_barrier(ready)
     other_rows = from_partner(rows_then)
     q_rest = crossed(q_x, q_y)
     q_pairs = {(0, 0): both_q, **q_x, **q_y}
     q_early = [q_pairs[key] for key in order if key in q_pairs]
     own_query = project(query_kernel, at, [own_rows], [], q_early, F32)
     other_rows, own_query = lax.optimization_barrier((other_rows, own_query))
-    other_product = project(product_kernel, at, [other_rows], [], kv_pieces, F32)
-
-    reach = filters.shape[0] - 1
-    pad = -(-reach // 8) * 8
+    rim, other_product = project_joined(at, before, other_rows, kv_pieces)
     own_tail, other_tail = own_product[length - pad :], other_product[length - pad :]
     first_tail = jnp.where(core == 0, own_tail, other_tail)
-    last_tail = jnp.where(core == 0, other_tail, own_tail)
-    rim = lax.ppermute(
-        last_tail,
-        "seq",
-        [(2 * i + c, 2 * i + 2 + c) for i in range(chips - 1) for c in range(2)],
-    )
     groups = filters.shape[1] // 2
     taps = jnp.repeat(
         lax.dynamic_slice_in_dim(filters, core * groups, groups, axis=1), half // groups, axis=1

time: 274 us -> 265 us (0.967)
  waiting for transfers between devices: 146 us -> 134 us
  local copies, waits for them, and re-layouts: 23.7 us -> 31 us
    ppermute x1 -> x2, waiting for transfers between devices: 14.9 us -> 0.01 us  [on_device(): lax.ppermute(own_rows[length - pad:], 'seq', [(2 * i + 1, 2 * i + 2 + c)...]
    unnamed x46 -> x66, local copies, waits for them, and re-layouts: 11.5 us -> 18.5 us
    ppermute x6, starting transfers between devices: 0.86 us -> 5.45 us  [from_partner(): return lax.ppermute(block, 'seq', [(s, s ^ 1) for s in range(n_seq)])]
    ppermute x14, waiting for transfers between devices: 81.1 us -> 84.8 us  [from_chip(): return lax.ppermute(block, 'seq', route)]
  transfers between devices with their start and end apart: 29 -> 30, of which waited for: 19 -> 19; matrix products, arithmetic and copies ran while one was open for 4% -> 4% of each run, Pallas kernels for 14% -> 13%
where the time goes in v7:
time: 265 us; the launch traced here: 264 us
  waiting for transfers between devices  134 us (51%)
  Pallas kernels  43.7 us (16%)
  starting transfers between devices  37 us (14%)
  local copies, waits for them, and re-layouts  31 us (12%)
  between operations  14.1 us (5%)
  other arithmetic  3.88 us (1%)
    ppermute x14, waiting for transfers between devices, from_chip(): return lax.ppermute(block, 'seq', route)  84.8 us
    pallas_call x12, Pallas kernels, call(): pl.pallas_call(kernel, out_shape=out, in_specs=[pl.BlockSpec(memory_space...  43.7 us
    ppermute x3, waiting for transfers between devices, chained(): falling = lax.ppermute(send_down, 'tp', down)  28.9 us
    unnamed x66, local copies, waits for them, and re-layouts  18.5 us
    ppermute x14, starting transfers between devices, from_chip(): return lax.ppermute(block, 'seq', route)  14.3 us
    ppermute x3, waiting for transfers between devices, chained(): rising = lax.ppermute(send_up, 'tp', up)  12.1 us
    ppermute x3, starting transfers between devices, chained(): rising = lax.ppermute(send_up, 'tp', up)  11.8 us
    ppermute x6, waiting for transfers between devices, from_partner(): return lax.ppermute(block, 'seq', [(s, s ^ 1) for s in range(n_seq)])  6.86 us
  transfers between devices with their start and end apart: 30, of which 19 were waited for; matrix products, arithmetic and copies ran while one was open for 4% of the time, Pallas kernels for 13%

profile of v7, /device:TPU:0, one launch (start us, length us, event | category | flops | bytes accessed | tf_op | source)
XLA Modules:
  0.0 264.1 jit_solution(18226416287585549559)
XLA Ops:
  6.5 1.8 constant_dynamic-slice_fusion.3
  8.7 1.3 fusion.2
  10.6 1.3 constant_dynamic-slice_fusion.2
  12.1 2.8 %collective-permute-start.1 = (bf16[2,512,512]{2,1,0:T(8,128)(2,1)S(1)}, bf16[2,512,512]{2,1,0:T(8,128)(2,1)S(1)}, u32[]{:S(2)}, u32[]{:S(2)}) collective-permute-start(bf16[2,512,512]{2,1,0:T(8,128)(2,1)S(1)} %get-tuple-element.56.refs_1_.refs_0_), channel_id=1, source_target_pairs={{8,0},{12,4},{0,8},{4,12},{24,16},{28,20},{16,24},{20,28},{9,1},{1... | collective-permute-start | bytes 3145736 | tf_op jit(solution)/shard_map/ppermute | solution.py:212
  14.9 1.5 collective-permute-start.3
  17.6 1.8 collective-permute-done.6
  19.4 19.4 %collective-permute-done.1.refs_3_.refs_2_ = bf16[2,512,512]{2,1,0:T(8,128)(2,1)S(1)} collective-permute-done((bf16[2,512,512]{2,1,0:T(8,128)(2,1)S(1)}, bf16[2,512,512]{2,1,0:T(8,128)(2,1)S(1)}, u32[]{:S(2)}, u32[]{:S(2)}) %collective-permute-start.1) | collective-permute-done | bytes 1048608 | tf_op jit(solution)/shard_map/ppermute | solution.py:212
  38.9 2.1 collective-permute-done.3.refs_5_.refs_4_
  41.0 1.0 copy-done.10
  42.0 18.8 %collective-permute-done.2.refs_4_.refs_3_ = bf16[2,512,512]{2,1,0:T(8,128)(2,1)S(1)} collective-permute-done((bf16[2,512,512]{2,1,0:T(8,128)(2,1)S(1)}, bf16[2,512,512]{2,1,0:T(8,128)(2,1)S(1)}, u32[]{:S(2)}, u32[]{:S(2)}) %collective-permute-start.2) | collective-permute-done | bytes 1048608 | tf_op jit(solution)/shard_map/ppermute | solution.py:212
  60.8 1.0 copy-done.13
  62.3 1.5 collective-permute-start.7
  63.8 1.0 copy-done.7
  64.8 1.3 collective-permute-start.8
  66.1 1.0 copy-done.16
  68.3 20.1 %collective-permute-done.7.refs_7_.refs_6_ = bf16[2,512,512]{2,1,0:T(8,128)(2,1)S(1)} collective-permute-done((bf16[2,512,512]{2,1,0:T(8,128)(2,1)S(1)}, bf16[2,512,512]{2,1,0:T(8,128)(2,1)S(1)}, u32[]{:S(2)}, u32[]{:S(2)}) %collective-permute-start.7) | collective-permute-done | bytes 1048608 | tf_op jit(solution)/shard_map/ppermute | solution.py:212
  88.4 1.0 copy-done.19
  89.4 1.5 collective-permute-done.8.refs_8_.refs_7_
  90.9 1.0 copy-done.22
  91.9 1.7 all-gather.2.cloned.1.call-done.refs_0_
  96.3 1.2 copy-done.5
  97.5 1.2 copy-done.8
  98.8 1.2 copy-done.11
  100.0 1.2 copy-done.14
  101.2 1.2 copy-done.17
  102.4 1.2 copy-done.20
  103.7 1.2 copy-done.23
  104.9 6.7 %shard_map.64.product_ref = f32[512,512]{1,0:T(8,128)S(1)} custom-call(s32[8]{0:T(128)S(1)} %stack.58.at_ref._, bf16[512,4096]{1,0:T(8,128)(2,1)} %all-gather.2.cloned.1.call-done.refs_0_, bf16[2,512,512]{2,1,0:T(8,128)(2,1)S(1)} %get-tuple-element.56.refs_1_.refs_0_, bf16[2,512,512]{2,1,0:T(8,128)(2,1)S(1)} %copy-done.5, ...), custom_call_target="tpu_custom_call" | custom-call | flops 1 | bytes 1 | tf_op jit(solution)/shard_map/pallas_call | solution.py:99
  111.6 1.0 copy-done.2
  113.5 4.5 %collective-permute-start.13 = (bf16[512,4096]{1,0:T(8,128)(2,1)}, bf16[512,4096]{1,0:T(8,128)(2,1)}, u32[]{:S(2)}, u32[]{:S(2)}) collective-permute-start(bf16[512,4096]{1,0:T(8,128)(2,1)} %all-gather.2.cloned.1.call-done.refs_0_), channel_id=1, source_target_pairs={{0,4},{4,0},{8,12},{12,8},{16,20},{20,16},{24,28},{28,24},{1,5},{5... | collective-permute-start | bytes 12582920 | tf_op jit(solution)/shard_map/ppermute | solution.py:215
  118.0 1.5 collective-permute-start.16
  119.4 1.9 slice_bitcast_fusion.3
  121.3 1.9 slice_bitcast_fusion.2
  123.2 2.0 collective-permute-start.14
  126.2 4.8 %shard_map.65.refs_2_ = f32[512,512]{1,0:T(8,128)S(1)} custom-call(s32[8]{0:T(128)S(1)} %stack.58.at_ref._, bf16[512,4096]{1,0:T(8,128)(2,1)} %all-gather.2.cloned.1.call-done.refs_0_, bf16[2,512,512]{2,1,0:T(8,128)(2,1)S(1)} %pad_maximum_fusion.refs_1_, bf16[2,512,512]{2,1,0:T(8,128)(2,1)} %collective-permute-done.9.refs_2_, ...), custom_call_target="tpu_custom_call" | custom-call | flops 1 | bytes 1 | tf_op jit(solution)/shard_map/pallas_call | solution.py:99
  131.1 7.2 %shard_map.66 = (f32[16,512]{1,0:T(8,128)S(1)}, f32[512,512]{1,0:T(8,128)S(1)}) custom-call(s32[8]{0:T(128)S(1)} %stack.58.at_ref._, bf16[16,4096]{1,0:T(8,128)(2,1)S(1)} %broadcast_select_fusion.before_ref, bf16[512,4096]{1,0:T(8,128)(2,1)} %collective-permute-done.13.x_ref.refs_0_, bf16[2,512,512]{2,1,0:T(8,128)(2,1)S(1)} %get-tuple-element.56.refs_1_.refs_0_, ...), custom_call_target="tpu_custom_call" | custom-call | flops 1 | bytes 1 | tf_op jit(solution)/shard_map/pallas_call | solution.py:99
  138.3 2.0 shard_map.67.refs_1_
  140.4 2.0 shard_map.68.refs_1_
  142.4 4.8 %shard_map.70.refs_2_ = f32[512,512]{1,0:T(8,128)S(1)} custom-call(s32[8]{0:T(128)S(1)} %stack.58.at_ref._, bf16[512,4096]{1,0:T(8,128)(2,1)} %collective-permute-done.13.x_ref.refs_0_, bf16[2,512,512]{2,1,0:T(8,128)(2,1)S(1)} %pad_maximum_fusion.refs_1_, bf16[2,512,512]{2,1,0:T(8,128)(2,1)} %collective-permute-done.9.refs_2_, ...), custom_call_target="tpu_custom_call" | custom-call | flops 1 | bytes 1 | tf_op jit(solution)/shard_map/pallas_call | solution.py:99
  147.2 8.4 %collective-permute-done.14.refs_3_ = bf16[512,512]{1,0:T(8,128)(2,1)} collective-permute-done((bf16[512,512]{1,0:T(8,128)(2,1)}, bf16[512,512]{1,0:T(8,128)(2,1)}, u32[]{:S(2)}, u32[]{:S(2)}) %collective-permute-start.14) | collective-permute-done | bytes 524320 | tf_op jit(solution)/shard_map/ppermute | solution.py:212
  155.6 3.2 %shard_map.71.gated_ref = bf16[512,512]{1,0:T(8,128)(2,1)S(1)} custom-call(s32[2]{0:T(128)S(1)} %pad_add_fusion.at_ref, bf16[512,4096]{1,0:T(8,128)(2,1)} %collective-permute-done.13.x_ref.refs_0_, f32[512,512]{1,0:T(8,128)S(1)} %shard_map.68.refs_1_, f32[512,512]{1,0:T(8,128)S(1)} %shard_map.70.refs_2_, bf16[512,512]{1,0:T(8,128)(2,1)} %collective-permute-done.14.refs_3_, ...), custom_call_target="tpu_custom_call" | custom-call | flops 1 | bytes 1 | tf_op jit(solution)/shard_map/pallas_call | solution.py:99
  158.9 3.3 %shard_map.72 = bf16[512,3072]{1,0:T(8,128)(2,1)S(1)} custom-call(s32[1]{0:T(128)} %bitcast.14.z_ref, bf16[512,512]{1,0:T(8,128)(2,1)S(1)} %shard_map.71.gated_ref, bf16[2,512,512]{2,1,0:T(8,128)(2,1)S(1)} %pad_maximum_fusion.1.refs_0_, bf16[2,512,512]{2,1,0:T(8,128)(2,1)} %collective-permute-done.16.refs_1_, ...), custom_call_target="tpu_custom_call" | custom-call | flops 1 | bytes 1 | tf_op jit(solution)/shard_map/pallas_call | solution.py:99
  162.3 3.2 %shard_map.69.gated_ref = bf16[512,512]{1,0:T(8,128)(2,1)S(1)} custom-call(s32[2]{0:T(128)S(1)} %pad_add_fusion.at_ref, bf16[512,4096]{1,0:T(8,128)(2,1)} %all-gather.2.cloned.1.call-done.refs_0_, f32[512,512]{1,0:T(8,128)S(1)} %shard_map.67.refs_1_, f32[512,512]{1,0:T(8,128)S(1)} %shard_map.65.refs_2_, bf16[512,512]{1,0:T(8,128)(2,1)} %collective-permute-done.14.refs_3_, ...), custom_call_target="tpu_custom_call" | custom-call | flops 1 | bytes 1 | tf_op jit(solution)/shard_map/pallas_call | solution.py:99
  165.5 2.4 collective-permute-done.18.refs_3_
  167.9 5.0 %shard_map.73 = bf16[512,3072]{1,0:T(8,128)(2,1)} custom-call(s32[1]{0:T(128)} %bitcast.14.z_ref, bf16[512,512]{1,0:T(8,128)(2,1)S(1)} %shard_map.69.gated_ref, bf16[2,512,512]{2,1,0:T(8,128)(2,1)S(1)} %pad_maximum_fusion.1.refs_0_, bf16[2,512,512]{2,1,0:T(8,128)(2,1)} %collective-permute-done.16.refs_1_, ...), custom_call_target="tpu_custom_call" | custom-call | flops 1 | bytes 1 | tf_op jit(solution)/shard_map/pallas_call | solution.py:99
  172.9 1.1 slice_bitcast_fusion.1
  174.4 1.1 slice_bitcast_fusion
  176.1 12.0 %collective-permute-done.19.refs_0_ = bf16[512,512]{1,0:T(8,128)(2,1)S(1)} collective-permute-done((bf16[512,512]{1,0:T(8,128)(2,1)S(1)}, bf16[512,512]{1,0:T(8,128)(2,1)S(1)}, u32[]{:S(2)}, u32[]{:S(2)}) %collective-permute-start.19) | collective-permute-done | bytes 524320 | tf_op jit(solution)/shard_map/ppermute | solution.py:212
  188.1 1.2 collective-permute-done.20.refs_1_
  190.0 2.6 %collective-permute-done.21.refs_2_ = bf16[512,1024]{1,0:T(8,128)(2,1)S(1)} collective-permute-done((bf16[512,1024]{1,0:T(8,128)(2,1)S(1)}, bf16[512,1024]{1,0:T(8,128)(2,1)S(1)}, u32[]{:S(2)}, u32[]{:S(2)}) %collective-permute-start.21) | collective-permute-done | bytes 1048608 | tf_op jit(solution)/shard_map/ppermute | solution.py:215
  193.4 1.3 collective-permute-start.22
  194.7 1.3 collective-permute-start.25
  196.0 10.9 %collective-permute-done.22 = bf16[128,1024]{1,0:T(8,128)(2,1)S(1)} collective-permute-done((bf16[128,1024]{1,0:T(8,128)(2,1)S(1)}, bf16[128,1024]{1,0:T(8,128)(2,1)S(1)}, u32[]{:S(2)}, u32[]{:S(2)}) %collective-permute-start.22) | collective-permute-done | bytes 262176 | tf_op jit(solution)/shard_map/ppermute | solution.py:343
  206.8 10.7 %collective-permute-done.25 = bf16[128,1024]{1,0:T(8,128)(2,1)S(1)} collective-permute-done((bf16[128,1024]{1,0:T(8,128)(2,1)S(1)}, bf16[128,1024]{1,0:T(8,128)(2,1)S(1)}, u32[]{:S(2)}, u32[]{:S(2)}) %collective-permute-start.25) | collective-permute-done | bytes 262176 | tf_op jit(solution)/shard_map/ppermute | solution.py:344
  217.7 1.3 collective-permute-start.26
  219.0 4.6 %collective-permute-start.23 = (bf16[128,1024]{1,0:T(8,128)(2,1)S(1)}, bf16[128,1024]{1,0:T(8,128)(2,1)S(1)}, u32[]{:S(2)}, u32[]{:S(2)}) collective-permute-start(bf16[128,1024]{1,0:T(8,128)(2,1)S(1)} %get-tuple-element.101), channel_id=1, source_target_pairs={{0,1},{1,2},{2,3},{4,5},{5,6},{6,7},{8,9},{9,10},{10,11},{12,13},{... | collective-permute-start | bytes 786440 | tf_op jit(solution)/shard_map/ppermute | solution.py:343
  223.6 14.0 %collective-permute-done.26 = bf16[128,1024]{1,0:T(8,128)(2,1)S(1)} collective-permute-done((bf16[128,1024]{1,0:T(8,128)(2,1)S(1)}, bf16[128,1024]{1,0:T(8,128)(2,1)S(1)}, u32[]{:S(2)}, u32[]{:S(2)}) %collective-permute-start.26) | collective-permute-done | bytes 262176 | tf_op jit(solution)/shard_map/ppermute | solution.py:344
  237.7 1.3 collective-permute-start.27
  239.1 6.0 %collective-permute-start.24 = (bf16[128,1024]{1,0:T(8,128)(2,1)S(1)}, bf16[128,1024]{1,0:T(8,128)(2,1)S(1)}, u32[]{:S(2)}, u32[]{:S(2)}) collective-permute-start(bf16[128,1024]{1,0:T(8,128)(2,1)S(1)} %add_convert_fusion.1), channel_id=1, source_target_pairs={{0,1},{1,2},{2,3},{4,5},{5,6},{6,7},{8,9},{9,10},{10,11},{12,13},{... | collective-permute-start | bytes 786440 | tf_op jit(solution)/shard_map/ppermute | solution.py:343
  245.1 4.2 %collective-permute-done.27 = bf16[128,1024]{1,0:T(8,128)(2,1)S(1)} collective-permute-done((bf16[128,1024]{1,0:T(8,128)(2,1)S(1)}, bf16[128,1024]{1,0:T(8,128)(2,1)S(1)}, u32[]{:S(2)}, u32[]{:S(2)}) %collective-permute-start.27) | collective-permute-done | bytes 262176 | tf_op jit(solution)/shard_map/ppermute | solution.py:344
  249.3 1.3 collective-permute-done.24
  251.4 1.4 fusion.25
  253.2 1.0 copy-done.26
  255.4 1.0 copy-done.29
  (108 shorter events, 14.7 us)
Async XLA Ops:
  6.5 119.2 %copy-start = (f32[7,64]{1,0:T(8,128)S(1)}, f32[7,64]{1,0:T(8,128)}, u32[]{:S(2)}) copy-start(f32[7,64]{1,0:T(8,128)} %param.9) | copy-start | bytes 5380
  6.5 87.1 %all-gather.2.cloned.1.call-start = ((), (), s32[]{:S(2)}) async-start(), calls=%async_computation.1 | async-start | bytes 5242880 | tf_op jit(solution)/shard_map/all_gather | solution.py:260
  6.5 1.9 copy-start.25
  6.5 2.2 copy-start.32
  10.0 7.3 %copy-start.30 = (bf16[1024,512]{1,0:T(8,128)(2,1)S(1)}, bf16[1024,512]{1,0:T(8,128)(2,1)}, u32[]{:S(2)}) copy-start(bf16[1024,512]{1,0:T(8,128)(2,1)} %param.10) | copy-start | bytes 3145732
  10.0 241.4 %reduce-scatter.2.cloned.1.call-start = ((), (), s32[]{:S(2)}) async-start(), calls=%async_computation.2 | async-start | bytes 3932160 | tf_op jit(solution)/shard_map/reduce_scatter | solution.py:356
  10.1 6.4 %collective-permute-start = (bf16[2,512,512]{2,1,0:T(8,128)(2,1)S(1)}, bf16[2,512,512]{2,1,0:T(8,128)(2,1)S(1)}, u32[]{:S(2)}, u32[]{:S(2)}) collective-permute-start(bf16[2,512,512]{2,1,0:T(8,128)(2,1)S(1)} %get-tuple-element.88), channel_id=1, source_target_pairs={{0,4},{4,0},{8,12},{12,8},{16,20},{20,16},{24,28},{28,24},{1,5},{5... | collective-permute-start | bytes 3145736 | tf_op jit(solution)/shard_map/ppermute | solution.py:215
  11.9 5.5 %collective-permute-start.5 = (bf16[512,512]{1,0:T(8,128)(2,1)S(1)}, bf16[512,512]{1,0:T(8,128)(2,1)S(1)}, u32[]{:S(2)}, u32[]{:S(2)}) collective-permute-start(bf16[512,512]{1,0:T(8,128)(2,1)S(1)} %get-tuple-element.86), channel_id=1, source_target_pairs={{0,4},{4,0},{8,12},{12,8},{16,20},{20,16},{24,28},{28,24},{1,5},{5... | collective-permute-start | bytes 1572872 | tf_op jit(solution)/shard_map/ppermute | solution.py:215
  12.1 26.8 %collective-permute-start.1 = (bf16[2,512,512]{2,1,0:T(8,128)(2,1)S(1)}, bf16[2,512,512]{2,1,0:T(8,128)(2,1)S(1)}, u32[]{:S(2)}, u32[]{:S(2)}) collective-permute-start(bf16[2,512,512]{2,1,0:T(8,128)(2,1)S(1)} %get-tuple-element.56.refs_1_.refs_0_), channel_id=1, source_target_pairs={{8,0},{12,4},{0,8},{4,12},{24,16},{28,20},{16,24},{20,28},{9,1},{1... | collective-permute-start | bytes 3145736 | tf_op jit(solution)/shard_map/ppermute | solution.py:212
  14.9 26.0 %collective-permute-start.3 = (bf16[2,512,512]{2,1,0:T(8,128)(2,1)S(1)}, bf16[2,512,512]{2,1,0:T(8,128)(2,1)S(1)}, u32[]{:S(2)}, u32[]{:S(2)}) collective-permute-start(bf16[2,512,512]{2,1,0:T(8,128)(2,1)S(1)} %get-tuple-element.56.refs_1_.refs_0_), channel_id=1, source_target_pairs={{16,0},{20,4},{24,8},{28,12},{0,16},{4,20},{8,24},{12,28},{17,1},{... | collective-permute-start | bytes 3145736 | tf_op jit(solution)/shard_map/ppermute | solution.py:212
  16.5 1.1 copy-start.4
  16.5 44.4 %collective-permute-start.2 = (bf16[2,512,512]{2,1,0:T(8,128)(2,1)S(1)}, bf16[2,512,512]{2,1,0:T(8,128)(2,1)S(1)}, u32[]{:S(2)}, u32[]{:S(2)}) collective-permute-start(bf16[2,512,512]{2,1,0:T(8,128)(2,1)S(1)} %collective-permute-done.refs_2_.refs_1_), channel_id=1, source_target_pairs={{8,0},{12,4},{0,8},{4,12},{24,16},{28,20},{16,24},{20,28},{9,1},{1... | collective-permute-start | bytes 3145736 | tf_op jit(solution)/shard_map/ppermute | solution.py:212
  17.0 45.3 %collective-permute-start.4 = (bf16[2,512,512]{2,1,0:T(8,128)(2,1)S(1)}, bf16[2,512,512]{2,1,0:T(8,128)(2,1)S(1)}, u32[]{:S(2)}, u32[]{:S(2)}) collective-permute-start(bf16[2,512,512]{2,1,0:T(8,128)(2,1)S(1)} %collective-permute-done.refs_2_.refs_1_), channel_id=1, source_target_pairs={{16,0},{20,4},{24,8},{28,12},{0,16},{4,20},{8,24},{12,28},{17,1},{... | collective-permute-start | bytes 3145736 | tf_op jit(solution)/shard_map/ppermute | solution.py:212
  17.4 2.0 collective-permute-start.6
  41.0 1.0 copy-start.10
  60.8 1.0 copy-start.13
  62.3 26.1 %collective-permute-start.7 = (bf16[2,512,512]{2,1,0:T(8,128)(2,1)S(1)}, bf16[2,512,512]{2,1,0:T(8,128)(2,1)S(1)}, u32[]{:S(2)}, u32[]{:S(2)}) collective-permute-start(bf16[2,512,512]{2,1,0:T(8,128)(2,1)S(1)} %collective-permute-done.1.refs_3_.refs_2_), channel_id=1, source_target_pairs={{16,0},{20,4},{24,8},{28,12},{0,16},{4,20},{8,24},{12,28},{17,1},{... | collective-permute-start | bytes 3145736 | tf_op jit(solution)/shard_map/ppermute | solution.py:212
  63.8 1.0 copy-start.7
  64.8 26.1 %collective-permute-start.8 = (bf16[2,512,512]{2,1,0:T(8,128)(2,1)S(1)}, bf16[2,512,512]{2,1,0:T(8,128)(2,1)S(1)}, u32[]{:S(2)}, u32[]{:S(2)}) collective-permute-start(bf16[2,512,512]{2,1,0:T(8,128)(2,1)S(1)} %collective-permute-done.4.refs_6_.refs_5_), channel_id=1, source_target_pairs={{8,0},{12,4},{0,8},{4,12},{24,16},{28,20},{16,24},{20,28},{9,1},{1... | collective-permute-start | bytes 3145736 | tf_op jit(solution)/shard_map/ppermute | solution.py:212
  66.1 1.0 copy-start.16
  67.1 46.4 %collective-permute-start.9 = (bf16[2,512,512]{2,1,0:T(8,128)(2,1)S(1)}, bf16[2,512,512]{2,1,0:T(8,128)(2,1)}, u32[]{:S(2)}, u32[]{:S(2)}) collective-permute-start(bf16[2,512,512]{2,1,0:T(8,128)(2,1)S(1)} %pad_maximum_fusion.refs_1_), channel_id=1, source_target_pairs={{8,0},{12,4},{0,8},{4,12},{24,16},{28,20},{16,24},{20,28},{9,1},{1... | collective-permute-start | bytes 3145736 | tf_op jit(solution)/shard_map/ppermute | solution.py:212
  67.8 45.6 %collective-permute-start.10 = (bf16[2,512,512]{2,1,0:T(8,128)(2,1)S(1)}, bf16[2,512,512]{2,1,0:T(8,128)(2,1)}, u32[]{:S(2)}, u32[]{:S(2)}) collective-permute-start(bf16[2,512,512]{2,1,0:T(8,128)(2,1)S(1)} %pad_maximum_fusion.refs_1_), channel_id=1, source_target_pairs={{16,0},{20,4},{24,8},{28,12},{0,16},{4,20},{8,24},{12,28},{17,1},{... | collective-permute-start | bytes 3145736 | tf_op jit(solution)/shard_map/ppermute | solution.py:212
  88.4 1.0 copy-start.19
  90.9 1.0 copy-start.22
  94.6 18.0 %collective-permute-start.11 = (bf16[16,4096]{1,0:T(8,128)(2,1)S(1)}, bf16[16,4096]{1,0:T(8,128)(2,1)S(1)}, u32[]{:S(2)}, u32[]{:S(2)}) collective-permute-start(bf16[16,4096]{1,0:T(8,128)(2,1)S(1)} %slice.64), channel_id=1, source_target_pairs={{4,8},{12,16},{20,24},{5,9},{13,17},{21,25},{6,10},{14,18},{22,26}... | collective-permute-start | bytes 393224 | tf_op jit(solution)/shard_map/ppermute | solution.py:286
  95.2 17.3 %collective-permute-start.12 = (bf16[16,4096]{1,0:T(8,128)(2,1)S(1)}, bf16[16,4096]{1,0:T(8,128)(2,1)S(1)}, u32[]{:S(2)}, u32[]{:S(2)}) collective-permute-start(bf16[16,4096]{1,0:T(8,128)(2,1)S(1)} %slice.64), channel_id=1, source_target_pairs={{4,12},{12,20},{20,28},{5,13},{13,21},{21,29},{6,14},{14,22},{22,3... | collective-permute-start | bytes 393224 | tf_op jit(solution)/shard_map/ppermute | solution.py:286
  96.3 1.2 copy-start.5
  97.5 1.2 copy-start.8
  98.8 1.2 copy-start.11
  100.0 1.2 copy-start.14
  101.2 1.2 copy-start.17
  102.4 1.2 copy-start.20
  103.7 1.2 copy-start.23
  111.6 1.0 copy-start.2
  113.5 17.5 %collective-permute-start.13 = (bf16[512,4096]{1,0:T(8,128)(2,1)}, bf16[512,4096]{1,0:T(8,128)(2,1)}, u32[]{:S(2)}, u32[]{:S(2)}) collective-permute-start(bf16[512,4096]{1,0:T(8,128)(2,1)} %all-gather.2.cloned.1.call-done.refs_0_), channel_id=1, source_target_pairs={{0,4},{4,0},{8,12},{12,8},{16,20},{20,16},{24,28},{28,24},{1,5},{5... | collective-permute-start | bytes 12582920 | tf_op jit(solution)/shard_map/ppermute | solution.py:215
  118.0 40.9 %collective-permute-start.16 = (bf16[2,512,512]{2,1,0:T(8,128)(2,1)S(1)}, bf16[2,512,512]{2,1,0:T(8,128)(2,1)}, u32[]{:S(2)}, u32[]{:S(2)}) collective-permute-start(bf16[2,512,512]{2,1,0:T(8,128)(2,1)S(1)} %pad_maximum_fusion.1.refs_0_), channel_id=1, source_target_pairs={{8,0},{12,4},{0,8},{4,12},{24,16},{28,20},{16,24},{20,28},{9,1},{1... | collective-permute-start | bytes 3145736 | tf_op jit(solution)/shard_map/ppermute | solution.py:212
  119.4 39.4 %collective-permute-start.17 = (bf16[2,512,512]{2,1,0:T(8,128)(2,1)S(1)}, bf16[2,512,512]{2,1,0:T(8,128)(2,1)}, u32[]{:S(2)}, u32[]{:S(2)}) collective-permute-start(bf16[2,512,512]{2,1,0:T(8,128)(2,1)S(1)} %pad_maximum_fusion.1.refs_0_), channel_id=1, source_target_pairs={{16,0},{20,4},{24,8},{28,12},{0,16},{4,20},{8,24},{12,28},{17,1},{... | collective-permute-start | bytes 3145736 | tf_op jit(solution)/shard_map/ppermute | solution.py:212
  123.2 32.4 %collective-permute-start.14 = (bf16[512,512]{1,0:T(8,128)(2,1)}, bf16[512,512]{1,0:T(8,128)(2,1)}, u32[]{:S(2)}, u32[]{:S(2)}) collective-permute-start(bf16[512,512]{1,0:T(8,128)(2,1)} %slice_bitcast_fusion.3), channel_id=1, source_target_pairs={{16,0},{20,4},{24,8},{28,12},{0,16},{4,20},{8,24},{12,28},{17,1},{... | collective-permute-start | bytes 1572872 | tf_op jit(solution)/shard_map/ppermute | solution.py:212
  125.2 30.4 %collective-permute-start.15 = (bf16[512,512]{1,0:T(8,128)(2,1)}, bf16[512,512]{1,0:T(8,128)(2,1)}, u32[]{:S(2)}, u32[]{:S(2)}) collective-permute-start(bf16[512,512]{1,0:T(8,128)(2,1)} %slice_bitcast_fusion.2), channel_id=1, source_target_pairs={{8,0},{12,4},{0,8},{4,12},{24,16},{28,20},{16,24},{20,28},{9,1},{1... | collective-permute-start | bytes 1572872 | tf_op jit(solution)/shard_map/ppermute | solution.py:212
  126.1 4.8 %copy-start.6 = (bf16[2,512,512]{2,1,0:T(8,128)(2,1)S(1)}, bf16[2,512,512]{2,1,0:T(8,128)(2,1)}, u32[]{:S(2)}) copy-start(bf16[2,512,512]{2,1,0:T(8,128)(2,1)} %copy-done.4) | copy-start | bytes 3145732
  126.1 4.8 %copy-start.9 = (bf16[2,512,512]{2,1,0:T(8,128)(2,1)S(1)}, bf16[2,512,512]{2,1,0:T(8,128)(2,1)}, u32[]{:S(2)}) copy-start(bf16[2,512,512]{2,1,0:T(8,128)(2,1)} %copy-done.7) | copy-start | bytes 3145732
  126.2 4.8 %copy-start.12 = (bf16[2,512,512]{2,1,0:T(8,128)(2,1)S(1)}, bf16[2,512,512]{2,1,0:T(8,128)(2,1)}, u32[]{:S(2)}) copy-start(bf16[2,512,512]{2,1,0:T(8,128)(2,1)} %copy-done.10) | copy-start | bytes 3145732
  126.2 4.8 %copy-start.15 = (bf16[2,512,512]{2,1,0:T(8,128)(2,1)S(1)}, bf16[2,512,512]{2,1,0:T(8,128)(2,1)}, u32[]{:S(2)}) copy-start(bf16[2,512,512]{2,1,0:T(8,128)(2,1)} %copy-done.13) | copy-start | bytes 3145732
  126.2 4.9 %copy-start.18 = (bf16[2,512,512]{2,1,0:T(8,128)(2,1)S(1)}, bf16[2,512,512]{2,1,0:T(8,128)(2,1)}, u32[]{:S(2)}) copy-start(bf16[2,512,512]{2,1,0:T(8,128)(2,1)} %copy-done.16) | copy-start | bytes 3145732
  126.2 4.9 %copy-start.21 = (bf16[2,512,512]{2,1,0:T(8,128)(2,1)S(1)}, bf16[2,512,512]{2,1,0:T(8,128)(2,1)}, u32[]{:S(2)}) copy-start(bf16[2,512,512]{2,1,0:T(8,128)(2,1)} %copy-done.19) | copy-start | bytes 3145732
  126.2 4.9 %copy-start.24 = (bf16[2,512,512]{2,1,0:T(8,128)(2,1)S(1)}, bf16[2,512,512]{2,1,0:T(8,128)(2,1)}, u32[]{:S(2)}) copy-start(bf16[2,512,512]{2,1,0:T(8,128)(2,1)} %copy-done.22) | copy-start | bytes 3145732
  130.9 7.4 %copy-start.3 = (f32[512,512]{1,0:T(8,128)S(1)}, f32[512,512]{1,0:T(8,128)}, u32[]{:S(2)}) copy-start(f32[512,512]{1,0:T(8,128)} %copy-done.2) | copy-start | bytes 3145732
  162.2 5.7 %collective-permute-start.18 = (bf16[512,3072]{1,0:T(8,128)(2,1)S(1)}, bf16[512,3072]{1,0:T(8,128)(2,1)S(1)}, u32[]{:S(2)}, u32[]{:S(2)}) collective-permute-start(bf16[512,3072]{1,0:T(8,128)(2,1)S(1)} %shard_map.72), channel_id=1, source_target_pairs={{0,4},{4,0},{8,12},{12,8},{16,20},{20,16},{24,28},{28,24},{1,5},{5... | collective-permute-start | bytes 9437192 | tf_op jit(solution)/shard_map/ppermute | solution.py:215
  174.0 14.0 %collective-permute-start.19 = (bf16[512,512]{1,0:T(8,128)(2,1)S(1)}, bf16[512,512]{1,0:T(8,128)(2,1)S(1)}, u32[]{:S(2)}, u32[]{:S(2)}) collective-permute-start(bf16[512,512]{1,0:T(8,128)(2,1)S(1)} %slice_bitcast_fusion.1), channel_id=1, source_target_pairs={{16,0},{20,4},{24,8},{28,12},{0,16},{4,20},{8,24},{12,28},{17,1},{... | collective-permute-start | bytes 1572872 | tf_op jit(solution)/shard_map/ppermute | solution.py:212
  175.5 13.8 %collective-permute-start.20 = (bf16[512,512]{1,0:T(8,128)(2,1)S(1)}, bf16[512,512]{1,0:T(8,128)(2,1)S(1)}, u32[]{:S(2)}, u32[]{:S(2)}) collective-permute-start(bf16[512,512]{1,0:T(8,128)(2,1)S(1)} %slice_bitcast_fusion), channel_id=1, source_target_pairs={{8,0},{12,4},{0,8},{4,12},{24,16},{28,20},{16,24},{20,28},{9,1},{1... | collective-permute-start | bytes 1572872 | tf_op jit(solution)/shard_map/ppermute | solution.py:212
  189.9 2.7 %collective-permute-start.21 = (bf16[512,1024]{1,0:T(8,128)(2,1)S(1)}, bf16[512,1024]{1,0:T(8,128)(2,1)S(1)}, u32[]{:S(2)}, u32[]{:S(2)}) collective-permute-start(bf16[512,1024]{1,0:T(8,128)(2,1)S(1)} %shard_map.74), channel_id=1, source_target_pairs={{0,4},{4,0},{8,12},{12,8},{16,20},{20,16},{24,28},{28,24},{1,5},{5... | collective-permute-start | bytes 3145736 | tf_op jit(solution)/shard_map/ppermute | solution.py:215
  193.4 13.5 %collective-permute-start.22 = (bf16[128,1024]{1,0:T(8,128)(2,1)S(1)}, bf16[128,1024]{1,0:T(8,128)(2,1)S(1)}, u32[]{:S(2)}, u32[]{:S(2)}) collective-permute-start(bf16[128,1024]{1,0:T(8,128)(2,1)S(1)} %get-tuple-element.84), channel_id=1, source_target_pairs={{0,1},{1,2},{2,3},{4,5},{5,6},{6,7},{8,9},{9,10},{10,11},{12,13},{... | collective-permute-start | bytes 786440 | tf_op jit(solution)/shard_map/ppermute | solution.py:343
  194.7 22.8 %collective-permute-start.25 = (bf16[128,1024]{1,0:T(8,128)(2,1)S(1)}, bf16[128,1024]{1,0:T(8,128)(2,1)S(1)}, u32[]{:S(2)}, u32[]{:S(2)}) collective-permute-start(bf16[128,1024]{1,0:T(8,128)(2,1)S(1)} %get-tuple-element.82), channel_id=1, source_target_pairs={{1,0},{2,1},{3,2},{5,4},{6,5},{7,6},{9,8},{10,9},{11,10},{13,12},{... | collective-permute-start | bytes 786440 | tf_op jit(solution)/shard_map/ppermute | solution.py:344
  217.7 19.9 %collective-permute-start.26 = (bf16[128,1024]{1,0:T(8,128)(2,1)S(1)}, bf16[128,1024]{1,0:T(8,128)(2,1)S(1)}, u32[]{:S(2)}, u32[]{:S(2)}) collective-permute-start(bf16[128,1024]{1,0:T(8,128)(2,1)S(1)} %get-tuple-element.102), channel_id=1, source_target_pairs={{1,0},{2,1},{3,2},{5,4},{6,5},{7,6},{9,8},{10,9},{11,10},{13,12},{... | collective-permute-start | bytes 786440 | tf_op jit(solution)/shard_map/ppermute | solution.py:344
  219.0 20.0 %collective-permute-start.23 = (bf16[128,1024]{1,0:T(8,128)(2,1)S(1)}, bf16[128,1024]{1,0:T(8,128)(2,1)S(1)}, u32[]{:S(2)}, u32[]{:S(2)}) collective-permute-start(bf16[128,1024]{1,0:T(8,128)(2,1)S(1)} %get-tuple-element.101), channel_id=1, source_target_pairs={{0,1},{1,2},{2,3},{4,5},{5,6},{6,7},{8,9},{9,10},{10,11},{12,13},{... | collective-permute-start | bytes 786440 | tf_op jit(solution)/shard_map/ppermute | solution.py:343
  237.7 11.6 %collective-permute-start.27 = (bf16[128,1024]{1,0:T(8,128)(2,1)S(1)}, bf16[128,1024]{1,0:T(8,128)(2,1)S(1)}, u32[]{:S(2)}, u32[]{:S(2)}) collective-permute-start(bf16[128,1024]{1,0:T(8,128)(2,1)S(1)} %add_convert_fusion), channel_id=1, source_target_pairs={{1,0},{2,1},{3,2},{5,4},{6,5},{7,6},{9,8},{10,9},{11,10},{13,12},{... | collective-permute-start | bytes 786440 | tf_op jit(solution)/shard_map/ppermute | solution.py:344
  239.1 11.5 %collective-permute-start.24 = (bf16[128,1024]{1,0:T(8,128)(2,1)S(1)}, bf16[128,1024]{1,0:T(8,128)(2,1)S(1)}, u32[]{:S(2)}, u32[]{:S(2)}) collective-permute-start(bf16[128,1024]{1,0:T(8,128)(2,1)S(1)} %add_convert_fusion.1), channel_id=1, source_target_pairs={{0,1},{1,2},{2,3},{4,5},{5,6},{6,7},{8,9},{9,10},{10,11},{12,13},{... | collective-permute-start | bytes 786440 | tf_op jit(solution)/shard_map/ppermute | solution.py:343
  251.4 1.5 copy-start.27
  252.9 1.2 copy-start.26
  252.9 1.9 copy-start.28
  255.0 1.4 copy-start.31
  255.2 2.1 copy-start.1
  255.4 1.0 copy-start.29
Sparse Core Ops, SparseCore 0:
  10.2 83.4 all-gather.1
  173.1 67.9 reduce-scatter.1

commit v8 on v7

--- a/solution.py
+++ b/solution.py
@@ -10,7 +10,7 @@
 
 F32 = jnp.float32
 BF16 = jnp.bfloat16
-GRANT = 16 << 20
+GRANT = 12 << 20
 WHOLE = pl.BlockSpec(memory_space=pltpu.VMEM)
 
 
@@ -140,50 +140,50 @@
     return call(filter_kernel, at, (product, halo, taps), out, scratch)
 
 
-def terms_kernel(plan, turned, n_tp, z_ref, gated_ref, *refs):
-    count = 1 + max(which for which, _ in plan)
-    weights, refs = refs[:count], refs[count:]
-    length = gated_ref.shape[0]
-    rows = length // n_tp
-    held = gated_ref
-    if turned:
-        refs, held = refs[:-1], refs[-1]
-        for slot in range(n_tp):
-            owner = lax.rem(z_ref[0] + slot, n_tp)
-            held[slot * rows : (slot + 1) * rows] = gated_ref[
-                pl.ds(pl.multiple_of(owner * rows, rows), rows)
-            ]
-    given, outs = (refs[0], refs[1:]) if len(refs) > 1 else (None, refs)
-    wide = weights[0].shape[-1]
-    for index, (which, side) in enumerate(plan):
+def terms_kernel(plan, turned, n_tp, at_ref, *refs):
+    gates, refs, held = refs[:4], refs[4:-1], refs[-1]
+    count = sum(len(parts) for parts in plan)
+    weights, outs = refs[:count], refs[count:]
+    half = gates[0].shape[1]
+    rows = gates[0].shape[0] // n_tp
+    for slot in range(n_tp):
+        for index, gate in enumerate(gates):
+            side, whose = index % 2, index // 2
+            place = slice((2 * slot + whose) * rows, (2 * slot + whose + 1) * rows)
+            owner = lax.rem(at_ref[1] + slot, n_tp) * rows if turned else slot * rows
+            column = (at_ref[0] if side == 0 else 1 - at_ref[0]) * half
+            taken = gate[pl.ds(pl.multiple_of(owner, rows), rows)]
+            held[place, pl.ds(pl.multiple_of(column, half), half)] = taken
+    wide = weights[0].shape[1]
+    share = held.shape[0] // len(outs)
+    used = 0
+    for index, parts in enumerate(plan):
         at = slice(index * wide, (index + 1) * wide)
-        weight = weights[which]
-        total = dot(held[...], weight[...] if side is None else weight[side])
-        if given is not None:
-            total = total + given[:, at].astype(F32)
-        share = length // len(outs)
-        for slot, out in enumerate(outs):
-            out[:, at] = total[slot * share : (slot + 1) * share].astype(BF16)
-
-
-def terms(n_tp, z, gated, pairs, order, turned, given=None):
-    length, half = gated.shape
-    weights, plan = [], []
-    for pair in pairs:
-        if isinstance(pair, tuple):
-            plan += [(len(weights) + side, None) for side in order]
-            weights += pair
-        else:
-            plan += [(len(weights), side) for side in order]
-            weights.append(pair)
-    cols = len(plan) * weights[0].shape[-1]
-    slots = n_tp if turned and given is not None else 1
-    out = [jax.ShapeDtypeStruct((length // slots, cols), BF16)] * slots
-    kernel = functools.partial(terms_kernel, plan, turned, n_tp)
-    extra = () if given is None else (given,)
-    scratch = [pltpu.VMEM((length, half), BF16)] if turned else []
-    result = call(kernel, z, (gated, *weights, *extra), out, scratch)
-    return result if slots > 1 else result[0]
+        for piece in range(0, held.shape[0], share):
+            total, depth = None, 0
+            for which in range(len(parts)):
+                weight = weights[used + which]
+                low, depth = depth, depth + weight.shape[0]
+                new = dot(held[piece : piece + share, low:depth], weight[...])
+                total = new if total is None else total + new
+            outs[piece // share][:, at] = total.astype(BF16)
+        used += len(parts)
+
+
+def terms(n_tp, place, gates, blocks, turned):
+    length, half = gates[0].shape
+    weights = [part for parts in blocks for part in parts]
+    cols = len(blocks) * weights[0].shape[1]
+    slots = n_tp if turned else 1
+    out = [jax.ShapeDtypeStruct((2 * length // slots, cols), BF16)] * slots
+    kernel = functools.partial(terms_kernel, blocks_plan(blocks), turned, n_tp)
+    scratch = [pltpu.VMEM((2 * length, 2 * half), BF16)]
+    result = call(kernel, place, (*gates, *weights), out, scratch)
+    return result if turned else result[0]
+
+
+def blocks_plan(blocks):
+    return [range(len(parts)) for parts in blocks]
 
 
 def on_device(tokens, norm_gain, in_weight, filters, out_weight, keep_mask):
@@ -241,9 +241,12 @@
         found.update(rest)
         return found
 
-    def halves(array, axis, at):
-        size = array.shape[axis] // 2
-        return lax.dynamic_slice_in_dim(array, at * size, size, axis=axis)
+    def by_core(mine, other, axis):
+        return jnp.where(
+            core == 0,
+            jnp.concatenate([mine, other], axis=axis),
+            jnp.concatenate([other, mine], axis=axis),
+        )
 
     def columns(array, first, count, at):
         return lax.dynamic_slice(array, (first, 0, at * half), (count, deep, half))
@@ -258,13 +261,11 @@
     mean_sq = jnp.mean(widened * widened, axis=1, keepdims=True)
     normed = (widened * lax.rsqrt(mean_sq + 1e-06) * norm_gain).astype(BF16)
     own_rows = lax.all_gather(normed, "tp", axis=0, tiled=True)
-    in_weight_then, out_weight_then, _ = lax.optimization_barrier((in_weight, out_weight, normed))
+    in_weight_then, _ = lax.optimization_barrier((in_weight, normed))
     mine_q = columns(in_weight_then, 0, 1, core)[0]
     both_q = jnp.stack([mine_q, from_partner(columns(in_weight_then, 0, 1, 1 - core)[0])])
-    mine_o = halves(out_weight_then, 0, core)
-    both_o = jnp.stack([mine_o, from_partner(halves(out_weight_then, 0, 1 - core))])
-
-    kv_x, kv_y, both_q, both_o = lax.optimization_barrier((kv_x, kv_y, both_q, both_o))
+
+    kv_x, kv_y, both_q = lax.optimization_barrier((kv_x, kv_y, both_q))
     kv_rest = onward(kv_x, kv_y)
     q_x = {(0, dx): from_chip(both_q, 0, dx) for dx in range(1, nx)}
     q_y = {(dy, 0): from_chip(both_q, dy, 0) for dy in range(1, ny)}
@@ -309,9 +310,17 @@
         (other_rows, own_filtered, other_filtered)
     )
     other_query = project(query_kernel, at, [other_rows], [], q_early, F32)
-    both_o, q_x, q_y = lax.optimization_barrier((both_o, q_x, q_y))
-    o_x = {(0, dx): from_chip(both_o, 0, dx) for dx in range(1, nx)}
-    o_y = {(dy, 0): from_chip(both_o, dy, 0) for dy in range(1, ny)}
+    weight_then, q_x, q_y = lax.optimization_barrier((out_weight, q_x, q_y))
+    o_x = {(0, dx): from_chip(weight_then, 0, dx) for dx in range(1, nx)}
+    o_y = {(dy, 0): from_chip(weight_then, dy, 0) for dy in range(1, ny)}
+    o_rest = {
+        (dy, dx): (
+            from_chip(o_x[0, dx][:half], dy, 0),
+            from_chip(o_y[dy, 0][half:], 0, dx),
+        )
+        for dy in range(1, ny)
+        for dx in range(1, nx)
+    }
     late = [piece for pair in q_rest.values() for piece in pair]
     other_gated = project(
         gate_kernel, at[early:], [other_rows], [other_filtered, other_query], late, BF16
@@ -319,20 +328,15 @@
     own_gated = project(
         gate_kernel, at[early:], [own_rows], [own_filtered, own_query], late, BF16
     )
+    gates = (own_gated, from_partner(other_gated), other_gated, from_partner(own_gated))
 
     position = lax.axis_index("tp")
-    z = position.astype(jnp.int32).reshape(1)
+    here_at = jnp.stack([core, position]).astype(jnp.int32)
     up = [(i, i + 1) for i in range(n_tp - 1)]
     down = [(i + 1, i) for i in range(n_tp - 1)]
 
     def plus(a, b):
         return (a.astype(F32) + b.astype(F32)).astype(BF16)
-
-    def leaving_of(pairs, gates, turned):
-        return from_partner(terms(n_tp, z, gates[1], pairs, (1, 0), turned))
-
-    def terms_of(pairs, gates, turned, given):
-        return terms(n_tp, z, gates[0], pairs, (0, 1), turned, given)
 
     def chained(slots):
         rising = falling = None
@@ -345,24 +349,22 @@
         total = slots[0].astype(F32) + rising.astype(F32) + falling.astype(F32)
         return total
 
-    o_rest = crossed(o_x, o_y)
-    out_pairs = {(0, 0): both_o, **o_x, **o_y, **o_rest}
+    near = {(0, 0): (out_weight,)}
+    near.update({key: (block,) for key, block in (*o_x.items(), *o_y.items())})
+    found = terms(n_tp, here_at, gates, list(near.values()), False)
+    gates, found = lax.optimization_barrier((gates, found))
+    near_sum = lax.psum_scatter(found, "tp", scatter_dimension=0, tiled=True)
+    far_sum = chained(terms(n_tp, here_at, gates, list(o_rest.values()), True))
     result = jnp.zeros((rows, model), BF16)
-    gates = (own_gated, other_gated)
-    sets = [(0, 0), *o_x, *o_y], list(o_rest)
-    first, last = ([out_pairs[key] for key in keys] for keys in sets)
-    found = terms_of(first, gates, False, leaving_of(first, gates, False))
-    gates, found = lax.optimization_barrier((gates, found))
-    first_sum = lax.psum_scatter(found, "tp", scatter_dimension=0, tiled=True).astype(F32)
-    last_sum = chained(terms_of(last, gates, True, leaving_of(last, gates, True)))
-    for keys, mixed in zip(sets, (first_sum, last_sum)):
+    for keys, mixed in ((list(near), near_sum), (list(o_rest), far_sum)):
+        theirs = from_partner(mixed[rows:].astype(BF16)).astype(F32)
+        mine = mixed[:rows].astype(F32)
         for index, (dy, dx) in enumerate(keys):
             start = place(my_y + dy, my_x + dx, 0) * wide
-            pair = mixed[:, index * 2 * wide : (index + 1) * 2 * wide]
-            swapped = jnp.concatenate([pair[:, wide:], pair[:, :wide]], axis=1)
+            here_columns = slice(index * wide, (index + 1) * wide)
+            pair = by_core(mine[:, here_columns], theirs[:, here_columns], 1)
             kept = lax.dynamic_slice_in_dim(keep_mask, start, 2 * wide, axis=1).astype(F32)
             base = lax.dynamic_slice_in_dim(tokens, start, 2 * wide, axis=1).astype(F32)
-            pair = jnp.where(core == 0, pair, swapped)
             part = (base + kept * pair * (1.0 / 0.9)).astype(BF16)
             result = lax.dynamic_update_slice_in_dim(result, part, start, axis=1)
     return result

time: 265 us -> 254 us (0.958)
  waiting for transfers between devices: 134 us -> 122 us
  starting transfers between devices: 37 us -> 41.8 us
  local copies, waits for them, and re-layouts: 31 us -> 27.7 us
    ppermute x14, waiting for transfers between devices: 84.8 us -> 75.3 us  [from_chip(): return lax.ppermute(block, 'seq', route)]
    reduce_scatter x1, waiting for transfers between devices: 0.01 us -> 3.94 us  [on_device(): near_sum = lax.psum_scatter(found, 'tp', scatter_dimension=0, tiled=True)]
    ppermute x14, starting transfers between devices: 14.3 us -> 18.1 us  [from_chip(): return lax.ppermute(block, 'seq', route)]
    ppermute x6 -> x7, waiting for transfers between devices: 6.86 us -> 3.1 us  [from_partner(): return lax.ppermute(block, 'seq', [(s, s ^ 1) for s in range(n_seq)])]
    ppermute x6 -> x7, starting transfers between devices: 5.45 us -> 7.15 us  [from_partner(): return lax.ppermute(block, 'seq', [(s, s ^ 1) for s in range(n_seq)])]
    pallas_call x12 -> x10, Pallas kernels: 43.7 us -> 42.1 us  [call(): pl.pallas_call(kernel, out_shape=out, in_specs=[pl.BlockSpec(memory_space...]
    unnamed x66 -> x60, local copies, waits for them, and re-layouts: 18.5 us -> 18.2 us
  transfers between devices with their start and end apart: 30 -> 31, of which waited for: 19 -> 16; matrix products, arithmetic and copies ran while one was open for 4% -> 4% of each run, Pallas kernels for 13% -> 14%
where the time goes in v8:
time: 254 us
  waiting for transfers between devices  122 us (48%)
  Pallas kernels  42.1 us (17%)
  starting transfers between devices  41.8 us (16%)
  local copies, waits for them, and re-layouts  27.7 us (11%)
  between operations  14.2 us (6%)
  other arithmetic  5.56 us (2%)
    ppermute x14, waiting for transfers between devices, from_chip(): return lax.ppermute(block, 'seq', route)  75.3 us
    pallas_call x10, Pallas kernels, call(): pl.pallas_call(kernel, out_shape=out, in_specs=[pl.BlockSpec(memory_space...  42.1 us
    ppermute x3, waiting for transfers between devices, chained(): falling = lax.ppermute(send_down, 'tp', down)  26.5 us
    unnamed x60, local copies, waits for them, and re-layouts  18.2 us
    ppermute x14, starting transfers between devices, from_chip(): return lax.ppermute(block, 'seq', route)  18.1 us
    ppermute x3, starting transfers between devices, chained(): rising = lax.ppermute(send_up, 'tp', up)  11.3 us
    ppermute x3, waiting for transfers between devices, chained(): rising = lax.ppermute(send_up, 'tp', up)  9.97 us
    ppermute x7, starting transfers between devices, from_partner(): return lax.ppermute(block, 'seq', [(s, s ^ 1) for s in range(n_seq)])  7.15 us
  transfers between devices with their start and end apart: 31, of which 16 were waited for; matrix products, arithmetic and copies ran while one was open for 4% of the time, Pallas kernels for 14%

profile of v8, /device:TPU:0, one launch (start us, length us, event | category | flops | bytes accessed | tf_op | source)
XLA Modules:
  0.0 253.5 jit_solution(12234331815918577434)
XLA Ops:
  6.5 1.8 constant_dynamic-slice_fusion.2
  8.7 1.3 fusion.2
  10.6 2.6 %collective-permute-start.1 = (bf16[2,512,512]{2,1,0:T(8,128)(2,1)S(1)}, bf16[2,512,512]{2,1,0:T(8,128)(2,1)S(1)}, u32[]{:S(2)}, u32[]{:S(2)}) collective-permute-start(bf16[2,512,512]{2,1,0:T(8,128)(2,1)S(1)} %get-tuple-element.55.refs_1_.refs_0_), channel_id=1, source_target_pairs={{8,0},{12,4},{0,8},{4,12},{24,16},{28,20},{16,24},{20,28},{9,1},{1... | collective-permute-start | bytes 3145736 | tf_op jit(solution)/shard_map/ppermute | solution.py:212
  13.2 1.5 collective-permute-start.3
  14.7 1.1 collective-permute-start.2
  15.8 1.5 collective-permute-start.4
  17.3 1.3 constant_dynamic-slice_fusion.1
  18.6 1.9 collective-permute-done.5
  20.6 16.5 %collective-permute-done.1.refs_3_.refs_2_ = bf16[2,512,512]{2,1,0:T(8,128)(2,1)S(1)} collective-permute-done((bf16[2,512,512]{2,1,0:T(8,128)(2,1)S(1)}, bf16[2,512,512]{2,1,0:T(8,128)(2,1)S(1)}, u32[]{:S(2)}, u32[]{:S(2)}) %collective-permute-start.1) | collective-permute-done | bytes 1048608 | tf_op jit(solution)/shard_map/ppermute | solution.py:212
  37.2 2.0 collective-permute-done.3.refs_5_.refs_4_
  39.2 1.0 copy-done.9
  40.2 19.2 %collective-permute-done.2.refs_4_.refs_3_ = bf16[2,512,512]{2,1,0:T(8,128)(2,1)S(1)} collective-permute-done((bf16[2,512,512]{2,1,0:T(8,128)(2,1)S(1)}, bf16[2,512,512]{2,1,0:T(8,128)(2,1)S(1)}, u32[]{:S(2)}, u32[]{:S(2)}) %collective-permute-start.2) | collective-permute-done | bytes 1048608 | tf_op jit(solution)/shard_map/ppermute | solution.py:212
  59.4 1.0 copy-done.12
  60.9 1.5 collective-permute-start.6
  62.4 1.0 copy-done.6
  63.4 1.3 collective-permute-start.7
  64.6 1.0 copy-done.15
  66.9 20.1 %collective-permute-done.6.refs_7_.refs_6_ = bf16[2,512,512]{2,1,0:T(8,128)(2,1)S(1)} collective-permute-done((bf16[2,512,512]{2,1,0:T(8,128)(2,1)S(1)}, bf16[2,512,512]{2,1,0:T(8,128)(2,1)S(1)}, u32[]{:S(2)}, u32[]{:S(2)}) %collective-permute-start.6) | collective-permute-done | bytes 1048608 | tf_op jit(solution)/shard_map/ppermute | solution.py:212
  87.0 1.0 copy-done.18
  88.0 1.5 collective-permute-done.7.refs_8_.refs_7_
  89.5 1.0 copy-done.21
  90.5 3.2 %all-gather.2.cloned.1.call-done.refs_0_ = bf16[512,4096]{1,0:T(8,128)(2,1)} async-done(((bf16[128,4096]{1,0:T(8,128)(2,1)}), bf16[512,4096]{1,0:T(8,128)(2,1)}) %all-gather.2.cloned.1.call-update) | async-done | bytes 4194320 | tf_op jit(solution)/shard_map/all_gather | solution.py:263
  96.1 1.2 copy-done.4
  97.4 1.2 copy-done.7
  98.6 1.2 copy-done.10
  99.8 1.2 copy-done.13
  101.0 1.2 copy-done.16
  102.3 1.2 copy-done.19
  103.5 1.2 copy-done.22
  104.7 6.7 %shard_map.64.product_ref = f32[512,512]{1,0:T(8,128)S(1)} custom-call(s32[8]{0:T(128)S(1)} %stack.55.at_ref._, bf16[512,4096]{1,0:T(8,128)(2,1)} %all-gather.2.cloned.1.call-done.refs_0_, bf16[2,512,512]{2,1,0:T(8,128)(2,1)S(1)} %get-tuple-element.55.refs_1_.refs_0_, bf16[2,512,512]{2,1,0:T(8,128)(2,1)S(1)} %copy-done.4, ...), custom_call_target="tpu_custom_call" | custom-call | flops 1 | bytes 1 | tf_op jit(solution)/shard_map/pallas_call | solution.py:99
  111.4 1.0 copy-done.1
  112.4 5.4 %collective-permute-start.12 = (bf16[512,4096]{1,0:T(8,128)(2,1)}, bf16[512,4096]{1,0:T(8,128)(2,1)}, u32[]{:S(2)}, u32[]{:S(2)}) collective-permute-start(bf16[512,4096]{1,0:T(8,128)(2,1)} %all-gather.2.cloned.1.call-done.refs_0_), channel_id=1, source_target_pairs={{0,4},{4,0},{8,12},{12,8},{16,20},{20,16},{24,28},{28,24},{1,5},{5... | collective-permute-start | bytes 12582920 | tf_op jit(solution)/shard_map/ppermute | solution.py:215
  118.9 1.9 slice_bitcast_fusion
  120.8 1.2 collective-permute-start.14
  122.8 1.7 collective-permute-start.18
  125.0 4.4 %shard_map.65.refs_2_ = f32[512,512]{1,0:T(8,128)S(1)} custom-call(s32[8]{0:T(128)S(1)} %stack.55.at_ref._, bf16[512,4096]{1,0:T(8,128)(2,1)} %all-gather.2.cloned.1.call-done.refs_0_, bf16[2,512,512]{2,1,0:T(8,128)(2,1)S(1)} %pad_maximum_fusion.refs_1_, bf16[2,512,512]{2,1,0:T(8,128)(2,1)S(1)} %collective-permute-done.8.refs_2_, ...), custom_call_target="tpu_custom_call" | custom-call | flops 1 | bytes 1 | tf_op jit(solution)/shard_map/pallas_call | solution.py:99
  129.6 7.2 %shard_map.66 = (f32[16,512]{1,0:T(8,128)S(1)}, f32[512,512]{1,0:T(8,128)S(1)}) custom-call(s32[8]{0:T(128)S(1)} %stack.55.at_ref._, bf16[16,4096]{1,0:T(8,128)(2,1)S(1)} %broadcast_select_fusion.before_ref, bf16[512,4096]{1,0:T(8,128)(2,1)} %collective-permute-done.12.x_ref.refs_0_, bf16[2,512,512]{2,1,0:T(8,128)(2,1)S(1)} %get-tuple-element.55.refs_1_.refs_0_, ...), custom_call_target="tpu_custom_call" | custom-call | flops 1 | bytes 1 | tf_op jit(solution)/shard_map/pallas_call | solution.py:99
  136.9 2.0 shard_map.67.refs_1_
  138.9 2.0 shard_map.68.refs_1_
  141.0 4.3 %shard_map.70.refs_2_ = f32[512,512]{1,0:T(8,128)S(1)} custom-call(s32[8]{0:T(128)S(1)} %stack.55.at_ref._, bf16[512,4096]{1,0:T(8,128)(2,1)} %collective-permute-done.12.x_ref.refs_0_, bf16[2,512,512]{2,1,0:T(8,128)(2,1)S(1)} %pad_maximum_fusion.refs_1_, bf16[2,512,512]{2,1,0:T(8,128)(2,1)S(1)} %collective-permute-done.8.refs_2_, ...), custom_call_target="tpu_custom_call" | custom-call | flops 1 | bytes 1 | tf_op jit(solution)/shard_map/pallas_call | solution.py:99
  145.5 3.2 %shard_map.71.refs_2_ = bf16[512,512]{1,0:T(8,128)(2,1)S(1)} custom-call(s32[2]{0:T(128)S(1)} %pad_add_fusion.at_ref, bf16[512,4096]{1,0:T(8,128)(2,1)} %collective-permute-done.12.x_ref.refs_0_, f32[512,512]{1,0:T(8,128)S(1)} %shard_map.68.refs_1_, f32[512,512]{1,0:T(8,128)S(1)} %shard_map.70.refs_2_, bf16[512,512]{1,0:T(8,128)(2,1)} %collective-permute-done.13.refs_3_, ...), custom_call_target="tpu_custom_call" | custom-call | flops 1 | bytes 1 | tf_op jit(solution)/shard_map/pallas_call | solution.py:99
  148.7 3.2 %shard_map.69.refs_0_ = bf16[512,512]{1,0:T(8,128)(2,1)S(1)} custom-call(s32[2]{0:T(128)S(1)} %pad_add_fusion.at_ref, bf16[512,4096]{1,0:T(8,128)(2,1)} %all-gather.2.cloned.1.call-done.refs_0_, f32[512,512]{1,0:T(8,128)S(1)} %shard_map.67.refs_1_, f32[512,512]{1,0:T(8,128)S(1)} %shard_map.65.refs_2_, bf16[512,512]{1,0:T(8,128)(2,1)} %collective-permute-done.13.refs_3_, ...), custom_call_target="tpu_custom_call" | custom-call | flops 1 | bytes 1 | tf_op jit(solution)/shard_map/pallas_call | solution.py:99
  152.6 4.6 %collective-permute-done.17.refs_5_ = bf16[1024,512]{1,0:T(8,128)(2,1)} collective-permute-done((bf16[1024,512]{1,0:T(8,128)(2,1)}, bf16[1024,512]{1,0:T(8,128)(2,1)}, u32[]{:S(2)}, u32[]{:S(2)}) %collective-permute-start.17) | collective-permute-done | bytes 1048608 | tf_op jit(solution)/shard_map/ppermute | solution.py:212
  157.2 7.0 %shard_map.72 = bf16[1024,1536]{1,0:T(8,128)(2,1)} custom-call(s32[2]{0:T(128)S(1)} %pad_add_fusion.1.at_ref, bf16[512,512]{1,0:T(8,128)(2,1)S(1)} %shard_map.69.refs_0_, bf16[512,512]{1,0:T(8,128)(2,1)S(1)} %collective-permute-done.15.refs_1_, bf16[512,512]{1,0:T(8,128)(2,1)S(1)} %shard_map.71.refs_2_, ...), custom_call_target="tpu_custom_call" | custom-call | flops 1 | bytes 1 | tf_op jit(solution)/shard_map/pallas_call | solution.py:99
  164.2 1.1 slice.81
  165.3 1.8 collective-permute-start.20
  167.1 1.1 slice.82
  168.2 1.5 collective-permute-start.21
  169.7 8.3 %collective-permute-done.20.refs_4_ = bf16[512,512]{1,0:T(8,128)(2,1)S(1)} collective-permute-done((bf16[512,512]{1,0:T(8,128)(2,1)S(1)}, bf16[512,512]{1,0:T(8,128)(2,1)S(1)}, u32[]{:S(2)}, u32[]{:S(2)}) %collective-permute-start.20) | collective-permute-done | bytes 524320 | tf_op jit(solution)/shard_map/ppermute | solution.py:212
  178.0 2.6 %collective-permute-done.21.refs_5_ = bf16[512,512]{1,0:T(8,128)(2,1)S(1)} collective-permute-done((bf16[512,512]{1,0:T(8,128)(2,1)S(1)}, bf16[512,512]{1,0:T(8,128)(2,1)S(1)}, u32[]{:S(2)}, u32[]{:S(2)}) %collective-permute-start.21) | collective-permute-done | bytes 524320 | tf_op jit(solution)/shard_map/ppermute | solution.py:212
  180.6 1.9 shard_map.73
  182.6 1.3 collective-permute-start.22
  183.9 1.3 collective-permute-start.25
  185.2 10.0 %collective-permute-done.22 = bf16[256,512]{1,0:T(8,128)(2,1)S(1)} collective-permute-done((bf16[256,512]{1,0:T(8,128)(2,1)S(1)}, bf16[256,512]{1,0:T(8,128)(2,1)S(1)}, u32[]{:S(2)}, u32[]{:S(2)}) %collective-permute-start.22) | collective-permute-done | bytes 262176 | tf_op jit(solution)/shard_map/ppermute | solution.py:347
  195.1 10.8 %collective-permute-done.25 = bf16[256,512]{1,0:T(8,128)(2,1)S(1)} collective-permute-done((bf16[256,512]{1,0:T(8,128)(2,1)S(1)}, bf16[256,512]{1,0:T(8,128)(2,1)S(1)}, u32[]{:S(2)}, u32[]{:S(2)}) %collective-permute-start.25) | collective-permute-done | bytes 262176 | tf_op jit(solution)/shard_map/ppermute | solution.py:348
  206.0 1.3 collective-permute-start.26
  207.3 4.8 %collective-permute-start.23 = (bf16[256,512]{1,0:T(8,128)(2,1)S(1)}, bf16[256,512]{1,0:T(8,128)(2,1)S(1)}, u32[]{:S(2)}, u32[]{:S(2)}) collective-permute-start(bf16[256,512]{1,0:T(8,128)(2,1)S(1)} %get-tuple-element.99), channel_id=1, source_target_pairs={{0,1},{1,2},{2,3},{4,5},{5,6},{6,7},{8,9},{9,10},{10,11},{12,13},{... | collective-permute-start | bytes 786440 | tf_op jit(solution)/shard_map/ppermute | solution.py:347
  212.1 15.7 %collective-permute-done.26 = bf16[256,512]{1,0:T(8,128)(2,1)S(1)} collective-permute-done((bf16[256,512]{1,0:T(8,128)(2,1)S(1)}, bf16[256,512]{1,0:T(8,128)(2,1)S(1)}, u32[]{:S(2)}, u32[]{:S(2)}) %collective-permute-start.26) | collective-permute-done | bytes 262176 | tf_op jit(solution)/shard_map/ppermute | solution.py:348
  228.0 1.3 collective-permute-start.27
  229.3 5.2 %collective-permute-start.24 = (bf16[256,512]{1,0:T(8,128)(2,1)S(1)}, bf16[256,512]{1,0:T(8,128)(2,1)S(1)}, u32[]{:S(2)}, u32[]{:S(2)}) collective-permute-start(bf16[256,512]{1,0:T(8,128)(2,1)S(1)} %add_convert_fusion.1), channel_id=1, source_target_pairs={{0,1},{1,2},{2,3},{4,5},{5,6},{6,7},{8,9},{9,10},{10,11},{12,13},{... | collective-permute-start | bytes 786440 | tf_op jit(solution)/shard_map/ppermute | solution.py:347
  234.6 3.9 %reduce-scatter.2.cloned.1.call-done = bf16[256,1536]{1,0:T(8,128)(2,1)} async-done(((bf16[1024,1536]{1,0:T(8,128)(2,1)}), bf16[256,1536]{1,0:T(8,128)(2,1)}) %reduce-scatter.2.cloned.1.call-update) | async-done | bytes 786448 | tf_op jit(solution)/shard_map/reduce_scatter | solution.py:356
  238.5 1.9 fusion.26
  241.2 1.2 collective-permute-done.28
  244.8 1.0 copy-done.28
  (105 shorter events, 12.7 us)
Async XLA Ops:
  6.5 118.0 %copy-start = (f32[7,64]{1,0:T(8,128)S(1)}, f32[7,64]{1,0:T(8,128)}, u32[]{:S(2)}) copy-start(f32[7,64]{1,0:T(8,128)} %param.9) | copy-start | bytes 5380
  6.5 87.1 %all-gather.2.cloned.1.call-start = ((), (), s32[]{:S(2)}) async-start(), calls=%async_computation.1 | async-start | bytes 5242880 | tf_op jit(solution)/shard_map/all_gather | solution.py:263
  6.5 1.9 copy-start.24
  6.5 2.2 copy-start.29
  10.0 228.5 %reduce-scatter.2.cloned.1.call-start = ((), (), s32[]{:S(2)}) async-start(), calls=%async_computation.2 | async-start | bytes 3932160 | tf_op jit(solution)/shard_map/reduce_scatter | solution.py:356
  10.1 4.6 %collective-permute-start = (bf16[2,512,512]{2,1,0:T(8,128)(2,1)S(1)}, bf16[2,512,512]{2,1,0:T(8,128)(2,1)S(1)}, u32[]{:S(2)}, u32[]{:S(2)}) collective-permute-start(bf16[2,512,512]{2,1,0:T(8,128)(2,1)S(1)} %get-tuple-element.88), channel_id=1, source_target_pairs={{0,4},{4,0},{8,12},{12,8},{16,20},{20,16},{24,28},{28,24},{1,5},{5... | collective-permute-start | bytes 3145736 | tf_op jit(solution)/shard_map/ppermute | solution.py:215
  10.6 26.6 %collective-permute-start.1 = (bf16[2,512,512]{2,1,0:T(8,128)(2,1)S(1)}, bf16[2,512,512]{2,1,0:T(8,128)(2,1)S(1)}, u32[]{:S(2)}, u32[]{:S(2)}) collective-permute-start(bf16[2,512,512]{2,1,0:T(8,128)(2,1)S(1)} %get-tuple-element.55.refs_1_.refs_0_), channel_id=1, source_target_pairs={{8,0},{12,4},{0,8},{4,12},{24,16},{28,20},{16,24},{20,28},{9,1},{1... | collective-permute-start | bytes 3145736 | tf_op jit(solution)/shard_map/ppermute | solution.py:212
  13.2 26.0 %collective-permute-start.3 = (bf16[2,512,512]{2,1,0:T(8,128)(2,1)S(1)}, bf16[2,512,512]{2,1,0:T(8,128)(2,1)S(1)}, u32[]{:S(2)}, u32[]{:S(2)}) collective-permute-start(bf16[2,512,512]{2,1,0:T(8,128)(2,1)S(1)} %get-tuple-element.55.refs_1_.refs_0_), channel_id=1, source_target_pairs={{16,0},{20,4},{24,8},{28,12},{0,16},{4,20},{8,24},{12,28},{17,1},{... | collective-permute-start | bytes 3145736 | tf_op jit(solution)/shard_map/ppermute | solution.py:212
  14.7 5.9 %copy-start.3 = (bf16[2,512,512]{2,1,0:T(8,128)(2,1)}, bf16[2,512,512]{2,1,0:T(8,128)(2,1)S(1)}, u32[]{:S(2)}) copy-start(bf16[2,512,512]{2,1,0:T(8,128)(2,1)S(1)} %collective-permute-done.refs_2_.refs_1_) | copy-start | bytes 3145732
  14.7 44.7 %collective-permute-start.2 = (bf16[2,512,512]{2,1,0:T(8,128)(2,1)S(1)}, bf16[2,512,512]{2,1,0:T(8,128)(2,1)S(1)}, u32[]{:S(2)}, u32[]{:S(2)}) collective-permute-start(bf16[2,512,512]{2,1,0:T(8,128)(2,1)S(1)} %collective-permute-done.refs_2_.refs_1_), channel_id=1, source_target_pairs={{8,0},{12,4},{0,8},{4,12},{24,16},{28,20},{16,24},{20,28},{9,1},{1... | collective-permute-start | bytes 3145736 | tf_op jit(solution)/shard_map/ppermute | solution.py:212
  15.8 45.1 %collective-permute-start.4 = (bf16[2,512,512]{2,1,0:T(8,128)(2,1)S(1)}, bf16[2,512,512]{2,1,0:T(8,128)(2,1)S(1)}, u32[]{:S(2)}, u32[]{:S(2)}) collective-permute-start(bf16[2,512,512]{2,1,0:T(8,128)(2,1)S(1)} %collective-permute-done.refs_2_.refs_1_), channel_id=1, source_target_pairs={{16,0},{20,4},{24,8},{28,12},{0,16},{4,20},{8,24},{12,28},{17,1},{... | collective-permute-start | bytes 3145736 | tf_op jit(solution)/shard_map/ppermute | solution.py:212
  18.5 2.0 collective-permute-start.5
  39.2 1.0 copy-start.9
  59.4 1.0 copy-start.12
  60.9 26.1 %collective-permute-start.6 = (bf16[2,512,512]{2,1,0:T(8,128)(2,1)S(1)}, bf16[2,512,512]{2,1,0:T(8,128)(2,1)S(1)}, u32[]{:S(2)}, u32[]{:S(2)}) collective-permute-start(bf16[2,512,512]{2,1,0:T(8,128)(2,1)S(1)} %collective-permute-done.1.refs_3_.refs_2_), channel_id=1, source_target_pairs={{16,0},{20,4},{24,8},{28,12},{0,16},{4,20},{8,24},{12,28},{17,1},{... | collective-permute-start | bytes 3145736 | tf_op jit(solution)/shard_map/ppermute | solution.py:212
  62.4 1.0 copy-start.6
  63.4 26.1 %collective-permute-start.7 = (bf16[2,512,512]{2,1,0:T(8,128)(2,1)S(1)}, bf16[2,512,512]{2,1,0:T(8,128)(2,1)S(1)}, u32[]{:S(2)}, u32[]{:S(2)}) collective-permute-start(bf16[2,512,512]{2,1,0:T(8,128)(2,1)S(1)} %collective-permute-done.4.refs_6_.refs_5_), channel_id=1, source_target_pairs={{8,0},{12,4},{0,8},{4,12},{24,16},{28,20},{16,24},{20,28},{9,1},{1... | collective-permute-start | bytes 3145736 | tf_op jit(solution)/shard_map/ppermute | solution.py:212
  64.6 1.0 copy-start.15
  65.6 46.8 %collective-permute-start.8 = (bf16[2,512,512]{2,1,0:T(8,128)(2,1)S(1)}, bf16[2,512,512]{2,1,0:T(8,128)(2,1)S(1)}, u32[]{:S(2)}, u32[]{:S(2)}) collective-permute-start(bf16[2,512,512]{2,1,0:T(8,128)(2,1)S(1)} %pad_maximum_fusion.refs_1_), channel_id=1, source_target_pairs={{8,0},{12,4},{0,8},{4,12},{24,16},{28,20},{16,24},{20,28},{9,1},{1... | collective-permute-start | bytes 3145736 | tf_op jit(solution)/shard_map/ppermute | solution.py:212
  66.4 46.0 %collective-permute-start.9 = (bf16[2,512,512]{2,1,0:T(8,128)(2,1)S(1)}, bf16[2,512,512]{2,1,0:T(8,128)(2,1)}, u32[]{:S(2)}, u32[]{:S(2)}) collective-permute-start(bf16[2,512,512]{2,1,0:T(8,128)(2,1)S(1)} %pad_maximum_fusion.refs_1_), channel_id=1, source_target_pairs={{16,0},{20,4},{24,8},{28,12},{0,16},{4,20},{8,24},{12,28},{17,1},{... | collective-permute-start | bytes 3145736 | tf_op jit(solution)/shard_map/ppermute | solution.py:212
  87.0 1.0 copy-start.18
  89.5 1.0 copy-start.21
  94.6 17.8 %collective-permute-start.10 = (bf16[16,4096]{1,0:T(8,128)(2,1)S(1)}, bf16[16,4096]{1,0:T(8,128)(2,1)S(1)}, u32[]{:S(2)}, u32[]{:S(2)}) collective-permute-start(bf16[16,4096]{1,0:T(8,128)(2,1)S(1)} %slice.56), channel_id=1, source_target_pairs={{4,8},{12,16},{20,24},{5,9},{13,17},{21,25},{6,10},{14,18},{22,26}... | collective-permute-start | bytes 393224 | tf_op jit(solution)/shard_map/ppermute | solution.py:287
  95.2 17.1 %collective-permute-start.11 = (bf16[16,4096]{1,0:T(8,128)(2,1)S(1)}, bf16[16,4096]{1,0:T(8,128)(2,1)S(1)}, u32[]{:S(2)}, u32[]{:S(2)}) collective-permute-start(bf16[16,4096]{1,0:T(8,128)(2,1)S(1)} %slice.56), channel_id=1, source_target_pairs={{4,12},{12,20},{20,28},{5,13},{13,21},{21,29},{6,14},{14,22},{22,3... | collective-permute-start | bytes 393224 | tf_op jit(solution)/shard_map/ppermute | solution.py:287
  96.1 1.2 copy-start.4
  97.4 1.2 copy-start.7
  98.6 1.2 copy-start.10
  99.8 1.2 copy-start.13
  101.0 1.2 copy-start.16
  102.3 1.2 copy-start.19
  103.5 1.2 copy-start.22
  111.4 1.0 copy-start.1
  112.4 17.0 %collective-permute-start.12 = (bf16[512,4096]{1,0:T(8,128)(2,1)}, bf16[512,4096]{1,0:T(8,128)(2,1)}, u32[]{:S(2)}, u32[]{:S(2)}) collective-permute-start(bf16[512,4096]{1,0:T(8,128)(2,1)} %all-gather.2.cloned.1.call-done.refs_0_), channel_id=1, source_target_pairs={{0,4},{4,0},{8,12},{12,8},{16,20},{20,16},{24,28},{28,24},{1,5},{5... | collective-permute-start | bytes 12582920 | tf_op jit(solution)/shard_map/ppermute | solution.py:215
  118.6 26.8 %collective-permute-start.13 = (bf16[512,512]{1,0:T(8,128)(2,1)}, bf16[512,512]{1,0:T(8,128)(2,1)}, u32[]{:S(2)}, u32[]{:S(2)}) collective-permute-start(bf16[512,512]{1,0:T(8,128)(2,1)} %slice_bitcast_fusion.1), channel_id=1, source_target_pairs={{16,0},{20,4},{24,8},{28,12},{0,16},{4,20},{8,24},{12,28},{17,1},{... | collective-permute-start | bytes 1572872 | tf_op jit(solution)/shard_map/ppermute | solution.py:212
  120.8 24.6 %collective-permute-start.14 = (bf16[512,512]{1,0:T(8,128)(2,1)}, bf16[512,512]{1,0:T(8,128)(2,1)}, u32[]{:S(2)}, u32[]{:S(2)}) collective-permute-start(bf16[512,512]{1,0:T(8,128)(2,1)} %slice_bitcast_fusion), channel_id=1, source_target_pairs={{8,0},{12,4},{0,8},{4,12},{24,16},{28,20},{16,24},{20,28},{9,1},{1... | collective-permute-start | bytes 1572872 | tf_op jit(solution)/shard_map/ppermute | solution.py:212
  122.0 35.2 %collective-permute-start.17 = (bf16[1024,512]{1,0:T(8,128)(2,1)}, bf16[1024,512]{1,0:T(8,128)(2,1)}, u32[]{:S(2)}, u32[]{:S(2)}) collective-permute-start(bf16[1024,512]{1,0:T(8,128)(2,1)} %refs_4_.1), channel_id=1, source_target_pairs={{8,0},{12,4},{0,8},{4,12},{24,16},{28,20},{16,24},{20,28},{9,1},{1... | collective-permute-start | bytes 3145736 | tf_op jit(solution)/shard_map/ppermute | solution.py:212
  122.8 34.3 %collective-permute-start.18 = (bf16[1024,512]{1,0:T(8,128)(2,1)}, bf16[1024,512]{1,0:T(8,128)(2,1)}, u32[]{:S(2)}, u32[]{:S(2)}) collective-permute-start(bf16[1024,512]{1,0:T(8,128)(2,1)} %refs_4_.1), channel_id=1, source_target_pairs={{16,0},{20,4},{24,8},{28,12},{0,16},{4,20},{8,24},{12,28},{17,1},{... | collective-permute-start | bytes 3145736 | tf_op jit(solution)/shard_map/ppermute | solution.py:212
  124.9 4.5 %copy-start.5 = (bf16[2,512,512]{2,1,0:T(8,128)(2,1)S(1)}, bf16[2,512,512]{2,1,0:T(8,128)(2,1)}, u32[]{:S(2)}) copy-start(bf16[2,512,512]{2,1,0:T(8,128)(2,1)} %copy-done.3) | copy-start | bytes 3145732
  124.9 4.5 %copy-start.8 = (bf16[2,512,512]{2,1,0:T(8,128)(2,1)S(1)}, bf16[2,512,512]{2,1,0:T(8,128)(2,1)}, u32[]{:S(2)}) copy-start(bf16[2,512,512]{2,1,0:T(8,128)(2,1)} %copy-done.6) | copy-start | bytes 3145732
  124.9 4.5 %copy-start.11 = (bf16[2,512,512]{2,1,0:T(8,128)(2,1)S(1)}, bf16[2,512,512]{2,1,0:T(8,128)(2,1)}, u32[]{:S(2)}) copy-start(bf16[2,512,512]{2,1,0:T(8,128)(2,1)} %copy-done.9) | copy-start | bytes 3145732
  124.9 4.5 %copy-start.14 = (bf16[2,512,512]{2,1,0:T(8,128)(2,1)S(1)}, bf16[2,512,512]{2,1,0:T(8,128)(2,1)}, u32[]{:S(2)}) copy-start(bf16[2,512,512]{2,1,0:T(8,128)(2,1)} %copy-done.12) | copy-start | bytes 3145732
  124.9 4.5 %copy-start.17 = (bf16[2,512,512]{2,1,0:T(8,128)(2,1)S(1)}, bf16[2,512,512]{2,1,0:T(8,128)(2,1)}, u32[]{:S(2)}) copy-start(bf16[2,512,512]{2,1,0:T(8,128)(2,1)} %copy-done.15) | copy-start | bytes 3145732
  124.9 4.5 %copy-start.20 = (bf16[2,512,512]{2,1,0:T(8,128)(2,1)S(1)}, bf16[2,512,512]{2,1,0:T(8,128)(2,1)}, u32[]{:S(2)}) copy-start(bf16[2,512,512]{2,1,0:T(8,128)(2,1)} %copy-done.18) | copy-start | bytes 3145732
  124.9 4.7 %copy-start.23 = (bf16[2,512,512]{2,1,0:T(8,128)(2,1)S(1)}, bf16[2,512,512]{2,1,0:T(8,128)(2,1)}, u32[]{:S(2)}) copy-start(bf16[2,512,512]{2,1,0:T(8,128)(2,1)} %copy-done.21) | copy-start | bytes 3145732
  129.4 7.4 %copy-start.2 = (f32[512,512]{1,0:T(8,128)S(1)}, f32[512,512]{1,0:T(8,128)}, u32[]{:S(2)}) copy-start(f32[512,512]{1,0:T(8,128)} %copy-done.1) | copy-start | bytes 3145732
  148.7 8.5 %collective-permute-start.15 = (bf16[512,512]{1,0:T(8,128)(2,1)S(1)}, bf16[512,512]{1,0:T(8,128)(2,1)S(1)}, u32[]{:S(2)}, u32[]{:S(2)}) collective-permute-start(bf16[512,512]{1,0:T(8,128)(2,1)S(1)} %shard_map.71.refs_2_), channel_id=1, source_target_pairs={{0,4},{4,0},{8,12},{12,8},{16,20},{20,16},{24,28},{28,24},{1,5},{5... | collective-permute-start | bytes 1572872 | tf_op jit(solution)/shard_map/ppermute | solution.py:215
  152.0 5.2 %collective-permute-start.16 = (bf16[512,512]{1,0:T(8,128)(2,1)S(1)}, bf16[512,512]{1,0:T(8,128)(2,1)S(1)}, u32[]{:S(2)}, u32[]{:S(2)}) collective-permute-start(bf16[512,512]{1,0:T(8,128)(2,1)S(1)} %shard_map.69.refs_0_), channel_id=1, source_target_pairs={{0,4},{4,0},{8,12},{12,8},{16,20},{20,16},{24,28},{28,24},{1,5},{5... | collective-permute-start | bytes 1572872 | tf_op jit(solution)/shard_map/ppermute | solution.py:215
  165.3 12.7 %collective-permute-start.20 = (bf16[512,512]{1,0:T(8,128)(2,1)S(1)}, bf16[512,512]{1,0:T(8,128)(2,1)S(1)}, u32[]{:S(2)}, u32[]{:S(2)}) collective-permute-start(bf16[512,512]{1,0:T(8,128)(2,1)S(1)} %slice.81), channel_id=1, source_target_pairs={{16,0},{20,4},{24,8},{28,12},{0,16},{4,20},{8,24},{12,28},{17,1},{... | collective-permute-start | bytes 1572872 | tf_op jit(solution)/shard_map/ppermute | solution.py:212
  168.2 12.5 %collective-permute-start.21 = (bf16[512,512]{1,0:T(8,128)(2,1)S(1)}, bf16[512,512]{1,0:T(8,128)(2,1)S(1)}, u32[]{:S(2)}, u32[]{:S(2)}) collective-permute-start(bf16[512,512]{1,0:T(8,128)(2,1)S(1)} %slice.82), channel_id=1, source_target_pairs={{8,0},{12,4},{0,8},{4,12},{24,16},{28,20},{16,24},{20,28},{9,1},{1... | collective-permute-start | bytes 1572872 | tf_op jit(solution)/shard_map/ppermute | solution.py:212
  182.6 12.6 %collective-permute-start.22 = (bf16[256,512]{1,0:T(8,128)(2,1)S(1)}, bf16[256,512]{1,0:T(8,128)(2,1)S(1)}, u32[]{:S(2)}, u32[]{:S(2)}) collective-permute-start(bf16[256,512]{1,0:T(8,128)(2,1)S(1)} %get-tuple-element.84), channel_id=1, source_target_pairs={{0,1},{1,2},{2,3},{4,5},{5,6},{6,7},{8,9},{9,10},{10,11},{12,13},{... | collective-permute-start | bytes 786440 | tf_op jit(solution)/shard_map/ppermute | solution.py:347
  183.9 22.0 %collective-permute-start.25 = (bf16[256,512]{1,0:T(8,128)(2,1)S(1)}, bf16[256,512]{1,0:T(8,128)(2,1)S(1)}, u32[]{:S(2)}, u32[]{:S(2)}) collective-permute-start(bf16[256,512]{1,0:T(8,128)(2,1)S(1)} %get-tuple-element.82), channel_id=1, source_target_pairs={{1,0},{2,1},{3,2},{5,4},{6,5},{7,6},{9,8},{10,9},{11,10},{13,12},{... | collective-permute-start | bytes 786440 | tf_op jit(solution)/shard_map/ppermute | solution.py:348
  206.0 21.9 %collective-permute-start.26 = (bf16[256,512]{1,0:T(8,128)(2,1)S(1)}, bf16[256,512]{1,0:T(8,128)(2,1)S(1)}, u32[]{:S(2)}, u32[]{:S(2)}) collective-permute-start(bf16[256,512]{1,0:T(8,128)(2,1)S(1)} %get-tuple-element.100), channel_id=1, source_target_pairs={{1,0},{2,1},{3,2},{5,4},{6,5},{7,6},{9,8},{10,9},{11,10},{13,12},{... | collective-permute-start | bytes 786440 | tf_op jit(solution)/shard_map/ppermute | solution.py:348
  207.3 21.9 %collective-permute-start.23 = (bf16[256,512]{1,0:T(8,128)(2,1)S(1)}, bf16[256,512]{1,0:T(8,128)(2,1)S(1)}, u32[]{:S(2)}, u32[]{:S(2)}) collective-permute-start(bf16[256,512]{1,0:T(8,128)(2,1)S(1)} %get-tuple-element.99), channel_id=1, source_target_pairs={{0,1},{1,2},{2,3},{4,5},{5,6},{6,7},{8,9},{9,10},{10,11},{12,13},{... | collective-permute-start | bytes 786440 | tf_op jit(solution)/shard_map/ppermute | solution.py:347
  228.0 12.5 %collective-permute-start.27 = (bf16[256,512]{1,0:T(8,128)(2,1)S(1)}, bf16[256,512]{1,0:T(8,128)(2,1)S(1)}, u32[]{:S(2)}, u32[]{:S(2)}) collective-permute-start(bf16[256,512]{1,0:T(8,128)(2,1)S(1)} %add_convert_fusion), channel_id=1, source_target_pairs={{1,0},{2,1},{3,2},{5,4},{6,5},{7,6},{9,8},{10,9},{11,10},{13,12},{... | collective-permute-start | bytes 786440 | tf_op jit(solution)/shard_map/ppermute | solution.py:348
  229.3 11.1 %collective-permute-start.24 = (bf16[256,512]{1,0:T(8,128)(2,1)S(1)}, bf16[256,512]{1,0:T(8,128)(2,1)S(1)}, u32[]{:S(2)}, u32[]{:S(2)}) collective-permute-start(bf16[256,512]{1,0:T(8,128)(2,1)S(1)} %add_convert_fusion.1), channel_id=1, source_target_pairs={{0,1},{1,2},{2,3},{4,5},{5,6},{6,7},{8,9},{9,10},{10,11},{12,13},{... | collective-permute-start | bytes 786440 | tf_op jit(solution)/shard_map/ppermute | solution.py:347
  240.4 2.0 collective-permute-start.19
  240.6 2.0 copy-start.27
  240.6 1.8 collective-permute-start.28
  242.4 1.2 copy-start.25
  242.4 1.9 copy-start.26
  244.3 1.5 slice-start
  244.8 1.0 copy-start.28
Sparse Core Ops, SparseCore 0:
  10.2 83.4 all-gather.1
  164.3 74.1 reduce-scatter.1

commit v9 on v8

--- a/solution.py
+++ b/solution.py
@@ -38,37 +38,6 @@
     for at in range(0, out_ref.shape[1], tile):
         for index, x_ref in enumerate(xs):
             yield x_ref, slice(index * size, (index + 1) * size), slice(at, at + tile)
-
-
-def product_kernel(parts, at_ref, *refs):
-    xs, pieces, out_ref = refs[:parts], refs[parts:-1], refs[-1]
-    deep = pieces[0].shape[1]
-    for x_ref, rows, tile in blocks_of(xs, out_ref):
-        key = value = None
-        for index, piece in enumerate(pieces):
-            x = columns_of(x_ref, at_ref, index, deep)
-            new_key, new_value = dot(x, piece[0, :, tile]), dot(x, piece[1, :, tile])
-            key = new_key if key is None else key + new_key
-            value = new_value if value is None else value + new_value
-        out_ref[rows, tile] = key.astype(BF16).astype(F32) * value.astype(BF16).astype(F32)
-
-
-def joined_kernel(at_ref, before_ref, x_ref, *refs):
-    pieces, (rim_ref, out_ref, joined) = refs[:-3], refs[-3:]
-    pad = before_ref.shape[0]
-    joined[:pad] = before_ref[...]
-    joined[pad:] = x_ref[...]
-    deep = pieces[0].shape[1]
-    for _, _, tile in blocks_of([x_ref], out_ref):
-        key = value = None
-        for index, piece in enumerate(pieces):
-            x = columns_of(joined, at_ref, index, deep)
-            new_key, new_value = dot(x, piece[0, :, tile]), dot(x, piece[1, :, tile])
-            key = new_key if key is None else key + new_key
-            value = new_value if value is None else value + new_value
-        product = key.astype(BF16).astype(F32) * value.astype(BF16).astype(F32)
-        rim_ref[:, tile] = product[:pad]
-        out_ref[:, tile] = product[pad:]
 
 
 def query_kernel(parts, at_ref, *refs):
@@ -113,12 +82,55 @@
     return call(functools.partial(kernel, len(xs)), at, (*xs, *extra, *pieces), out)
 
 
-def project_joined(at, before, x, pieces):
-    half = pieces[0].shape[-1]
-    pad, length = before.shape[0], x.shape[0]
-    out = [jax.ShapeDtypeStruct((rows, half), F32) for rows in (pad, length)]
-    scratch = [pltpu.VMEM((pad + length, x.shape[1]), BF16)]
-    return call(joined_kernel, at, (before, x, *pieces), out, scratch)
+def product_kernel(parts, count, at_ref, *refs):
+    xs, refs = refs[:parts], refs[parts:]
+    given, refs = refs[:count], refs[count:]
+    outs, (joined, *pieces, sems) = refs[:parts], refs[parts:]
+    ends = [0]
+    for x_ref in xs:
+        ends.append(ends[-1] + x_ref.shape[0])
+    targets = [joined.at[low:high] for low, high in zip(ends, ends[1:])] + list(pieces)
+    copies = [
+        pltpu.make_async_copy(source, target, sems.at[index])
+        for index, (source, target) in enumerate(zip((*xs, *given), targets))
+    ]
+    for copy in copies:
+        copy.start()
+    for copy in copies[:parts]:
+        copy.wait()
+    deep = pieces[0].shape[1]
+    half = pieces[0].shape[2]
+    tile = math.gcd(half, 256)
+    for low in range(0, half, tile):
+        columns = slice(low, low + tile)
+        key = value = None
+        for index, piece in enumerate(pieces):
+            if low == 0:
+                copies[parts + index].wait()
+            x = columns_of(joined, at_ref, index, deep)
+            new_key, new_value = dot(x, piece[0, :, columns]), dot(x, piece[1, :, columns])
+            key = new_key if key is None else key + new_key
+            value = new_value if value is None else value + new_value
+        product = key.astype(BF16).astype(F32) * value.astype(BF16).astype(F32)
+        for out, start, end in zip(outs, ends, ends[1:]):
+            out[:, columns] = product[start:end]
+
+
+def products(at, xs, pieces):
+    half = pieces[0].shape[2]
+    held = [pltpu.VMEM((sum(x.shape[0] for x in xs), xs[0].shape[1]), BF16)]
+    held += [pltpu.VMEM(piece.shape, BF16) for piece in pieces]
+    held.append(pltpu.SemaphoreType.DMA((len(xs) + len(pieces),)))
+    return pl.pallas_call(
+        functools.partial(product_kernel, len(xs), len(pieces)),
+        out_shape=[jax.ShapeDtypeStruct((x.shape[0], half), F32) for x in xs],
+        in_specs=[pl.BlockSpec(memory_space=pltpu.SMEM)]
+        + [pl.BlockSpec(memory_space=pl.ANY)] * (len(xs) + len(pieces)),
+        out_specs=[WHOLE] * len(xs),
+        scratch_shapes=held,
+        compiler_params=pltpu.CompilerParams(vmem_limit_bytes=2 * GRANT),
+        cost_estimate=pl.CostEstimate(flops=1, bytes_accessed=1, transcendentals=0),
+    )(at, *xs, *pieces)
 
 
 def filter_kernel(_, product_ref, halo_ref, taps_ref, out_ref, held):
@@ -280,7 +292,7 @@
     ).astype(jnp.int32)
     early = 2 * (ny + nx - 1)
 
-    own_product = project(product_kernel, at, [own_rows], [], kv_pieces, F32)
+    (own_product,) = products(at, [own_rows], kv_pieces)
     reach = filters.shape[0] - 1
     pad = -(-reach // 16) * 16
     ends = [
@@ -296,7 +308,7 @@
     q_early = [q_pairs[key] for key in order if key in q_pairs]
     own_query = project(query_kernel, at, [own_rows], [], q_early, F32)
     other_rows, own_query = lax.optimization_barrier((other_rows, own_query))
-    rim, other_product = project_joined(at, before, other_rows, kv_pieces)
+    rim, other_product = products(at, [before, other_rows], kv_pieces)
     own_tail, other_tail = own_product[length - pad :], other_product[length - pad :]
     first_tail = jnp.where(core == 0, own_tail, other_tail)
     groups = filters.shape[1] // 2

time: 254 us -> 256 us (level)
    pallas_call x0 -> x2, Pallas kernels: none -> 15.9 us  [products(): pl.pallas_call(functools.partial(product_kernel, len(xs), len(pieces)), o...]
    pallas_call x10 -> x8, Pallas kernels: 42.1 us -> 28.2 us  [call(): pl.pallas_call(kernel, out_shape=out, in_specs=[pl.BlockSpec(memory_space...]
  transfers between devices with their start and end apart: 31 -> 31, of which waited for: 16 -> 16; matrix products, arithmetic and copies ran while one was open for 4% -> 4% of each run, Pallas kernels for 14% -> 15%
where the time goes in v9:
time: 256 us; the launch traced here: 255 us
  waiting for transfers between devices  121 us (47%)
  Pallas kernels  44.1 us (17%)
  starting transfers between devices  41.8 us (16%)
  local copies, waits for them, and re-layouts  27.7 us (11%)
  between operations  14 us (5%)
  other arithmetic  5.56 us (2%)
    ppermute x14, waiting for transfers between devices, from_chip(): return lax.ppermute(block, 'seq', route)  74.7 us
    pallas_call x8, Pallas kernels, call(): pl.pallas_call(kernel, out_shape=out, in_specs=[pl.BlockSpec(memory_space...  28.2 us
    ppermute x3, waiting for transfers between devices, chained(): falling = lax.ppermute(send_down, 'tp', down)  26.5 us
    unnamed x60, local copies, waits for them, and re-layouts  18.2 us
    ppermute x14, starting transfers between devices, from_chip(): return lax.ppermute(block, 'seq', route)  18.1 us
    pallas_call x2, Pallas kernels, products(): pl.pallas_call(functools.partial(product_kernel, len(xs), len(pieces)), o...  15.9 us
    ppermute x3, starting transfers between devices, chained(): rising = lax.ppermute(send_up, 'tp', up)  11.4 us
    ppermute x3, waiting for transfers between devices, chained(): rising = lax.ppermute(send_up, 'tp', up)  9.96 us
  transfers between devices with their start and end apart: 31, of which 16 were waited for; matrix products, arithmetic and copies ran while one was open for 4% of the time, Pallas kernels for 15%

profile of v9, /device:TPU:0, one launch (start us, length us, event | category | flops | bytes accessed | tf_op | source)
XLA Modules:
  0.0 254.6 jit_solution(6490131528506578746)
XLA Ops:
  6.5 1.8 constant_dynamic-slice_fusion.2
  8.7 1.3 fusion.2
  10.6 2.6 %collective-permute-start.1 = (bf16[2,512,512]{2,1,0:T(8,128)(2,1)S(1)}, bf16[2,512,512]{2,1,0:T(8,128)(2,1)S(1)}, u32[]{:S(2)}, u32[]{:S(2)}) collective-permute-start(bf16[2,512,512]{2,1,0:T(8,128)(2,1)S(1)} %get-tuple-element.55.refs_1_.refs_2_), channel_id=1, source_target_pairs={{8,0},{12,4},{0,8},{4,12},{24,16},{28,20},{16,24},{20,28},{9,1},{1... | collective-permute-start | bytes 3145736 | tf_op jit(solution)/shard_map/ppermute | solution.py:224
  13.2 1.5 collective-permute-start.3
  14.7 1.1 collective-permute-start.2
  15.8 1.5 collective-permute-start.4
  17.3 1.3 constant_dynamic-slice_fusion.1
  18.6 1.9 collective-permute-done.5
  20.6 16.5 %collective-permute-done.1.refs_3_.refs_4_ = bf16[2,512,512]{2,1,0:T(8,128)(2,1)S(1)} collective-permute-done((bf16[2,512,512]{2,1,0:T(8,128)(2,1)S(1)}, bf16[2,512,512]{2,1,0:T(8,128)(2,1)S(1)}, u32[]{:S(2)}, u32[]{:S(2)}) %collective-permute-start.1) | collective-permute-done | bytes 1048608 | tf_op jit(solution)/shard_map/ppermute | solution.py:224
  37.2 2.0 collective-permute-done.3.refs_5_.refs_6_
  39.2 1.0 copy-done.9
  40.2 19.2 %collective-permute-done.2.refs_4_.refs_5_ = bf16[2,512,512]{2,1,0:T(8,128)(2,1)S(1)} collective-permute-done((bf16[2,512,512]{2,1,0:T(8,128)(2,1)S(1)}, bf16[2,512,512]{2,1,0:T(8,128)(2,1)S(1)}, u32[]{:S(2)}, u32[]{:S(2)}) %collective-permute-start.2) | collective-permute-done | bytes 1048608 | tf_op jit(solution)/shard_map/ppermute | solution.py:224
  59.4 1.0 copy-done.12
  60.9 1.5 collective-permute-start.6
  62.4 1.0 copy-done.6
  63.4 1.3 collective-permute-start.7
  64.6 1.0 copy-done.15
  66.9 20.1 %collective-permute-done.6.refs_7_.refs_8_ = bf16[2,512,512]{2,1,0:T(8,128)(2,1)S(1)} collective-permute-done((bf16[2,512,512]{2,1,0:T(8,128)(2,1)S(1)}, bf16[2,512,512]{2,1,0:T(8,128)(2,1)S(1)}, u32[]{:S(2)}, u32[]{:S(2)}) %collective-permute-start.6) | collective-permute-done | bytes 1048608 | tf_op jit(solution)/shard_map/ppermute | solution.py:224
  87.0 1.0 copy-done.18
  88.0 1.5 collective-permute-done.7.refs_8_.refs_9_
  89.5 1.0 copy-done.21
  90.5 3.2 %all-gather.2.cloned.1.call-done.refs_0_ = bf16[512,4096]{1,0:T(8,128)(2,1)} async-done(((bf16[128,4096]{1,0:T(8,128)(2,1)}), bf16[512,4096]{1,0:T(8,128)(2,1)}) %all-gather.2.cloned.1.call-update) | async-done | bytes 4194320 | tf_op jit(solution)/shard_map/all_gather | solution.py:275
  96.1 1.2 copy-done.4
  97.4 1.2 copy-done.7
  98.6 1.2 copy-done.10
  99.8 1.2 copy-done.13
  101.0 1.2 copy-done.16
  102.3 1.2 copy-done.19
  103.5 1.2 copy-done.22
  104.7 7.8 %shard_map.64.product_ref = f32[512,512]{1,0:T(8,128)S(1)} custom-call(s32[8]{0:T(128)S(1)} %stack.55.at_ref._, bf16[512,4096]{1,0:T(8,128)(2,1)} %all-gather.2.cloned.1.call-done.refs_0_, bf16[2,512,512]{2,1,0:T(8,128)(2,1)S(1)} %get-tuple-element.55.refs_1_.refs_2_, bf16[2,512,512]{2,1,0:T(8,128)(2,1)S(1)} %copy-done.4, ...), custom_call_target="tpu_custom_call" | custom-call | flops 1 | bytes 1 | tf_op jit(solution)/shard_map/pallas_call | solution.py:124
  112.5 1.0 copy-done.1
  113.6 5.4 %collective-permute-start.12 = (bf16[512,4096]{1,0:T(8,128)(2,1)}, bf16[512,4096]{1,0:T(8,128)(2,1)}, u32[]{:S(2)}, u32[]{:S(2)}) collective-permute-start(bf16[512,4096]{1,0:T(8,128)(2,1)} %all-gather.2.cloned.1.call-done.refs_0_), channel_id=1, source_target_pairs={{0,4},{4,0},{8,12},{12,8},{16,20},{20,16},{24,28},{28,24},{1,5},{5... | collective-permute-start | bytes 12582920 | tf_op jit(solution)/shard_map/ppermute | solution.py:227
  120.0 1.9 slice_bitcast_fusion
  121.9 1.2 collective-permute-start.14
  123.9 1.7 collective-permute-start.18
  126.1 4.4 %shard_map.65.refs_2_ = f32[512,512]{1,0:T(8,128)S(1)} custom-call(s32[8]{0:T(128)S(1)} %stack.55.at_ref._, bf16[512,4096]{1,0:T(8,128)(2,1)} %all-gather.2.cloned.1.call-done.refs_0_, bf16[2,512,512]{2,1,0:T(8,128)(2,1)S(1)} %pad_maximum_fusion.refs_1_, bf16[2,512,512]{2,1,0:T(8,128)(2,1)S(1)} %collective-permute-done.8.refs_2_, ...), custom_call_target="tpu_custom_call" | custom-call | flops 1 | bytes 1 | tf_op jit(solution)/shard_map/pallas_call | solution.py:68
  130.7 8.1 %shard_map.66 = (f32[16,512]{1,0:T(8,128)S(1)}, f32[512,512]{1,0:T(8,128)S(1)}) custom-call(s32[8]{0:T(128)S(1)} %stack.55.at_ref._, bf16[16,4096]{1,0:T(8,128)(2,1)S(1)} %broadcast_select_fusion.refs_0_, bf16[512,4096]{1,0:T(8,128)(2,1)} %collective-permute-done.12.refs_1_.refs_0_, bf16[2,512,512]{2,1,0:T(8,128)(2,1)S(1)} %get-tuple-element.55.refs_1_.refs_2_, ...), custom_call_target="tpu_custom_call" | custom-call | flops 1 | bytes 1 | tf_op jit(solution)/shard_map/pallas_call | solution.py:124
  138.8 2.0 shard_map.67.refs_1_
  140.9 2.0 shard_map.68.refs_1_
  142.9 4.3 %shard_map.70.refs_2_ = f32[512,512]{1,0:T(8,128)S(1)} custom-call(s32[8]{0:T(128)S(1)} %stack.55.at_ref._, bf16[512,4096]{1,0:T(8,128)(2,1)} %collective-permute-done.12.refs_1_.refs_0_, bf16[2,512,512]{2,1,0:T(8,128)(2,1)S(1)} %pad_maximum_fusion.refs_1_, bf16[2,512,512]{2,1,0:T(8,128)(2,1)S(1)} %collective-permute-done.8.refs_2_, ...), custom_call_target="tpu_custom_call" | custom-call | flops 1 | bytes 1 | tf_op jit(solution)/shard_map/pallas_call | solution.py:68
  147.2 3.2 %shard_map.71.refs_2_ = bf16[512,512]{1,0:T(8,128)(2,1)S(1)} custom-call(s32[2]{0:T(128)S(1)} %pad_add_fusion.at_ref, bf16[512,4096]{1,0:T(8,128)(2,1)} %collective-permute-done.12.refs_1_.refs_0_, f32[512,512]{1,0:T(8,128)S(1)} %shard_map.68.refs_1_, f32[512,512]{1,0:T(8,128)S(1)} %shard_map.70.refs_2_, bf16[512,512]{1,0:T(8,128)(2,1)} %collective-permute-done.13.refs_3_, ...), custom_call_target="tpu_custom_call" | custom-call | flops 1 | bytes 1 | tf_op jit(solution)/shard_map/pallas_call | solution.py:68
  150.5 3.2 %shard_map.69.refs_0_ = bf16[512,512]{1,0:T(8,128)(2,1)S(1)} custom-call(s32[2]{0:T(128)S(1)} %pad_add_fusion.at_ref, bf16[512,4096]{1,0:T(8,128)(2,1)} %all-gather.2.cloned.1.call-done.refs_0_, f32[512,512]{1,0:T(8,128)S(1)} %shard_map.67.refs_1_, f32[512,512]{1,0:T(8,128)S(1)} %shard_map.65.refs_2_, bf16[512,512]{1,0:T(8,128)(2,1)} %collective-permute-done.13.refs_3_, ...), custom_call_target="tpu_custom_call" | custom-call | flops 1 | bytes 1 | tf_op jit(solution)/shard_map/pallas_call | solution.py:68
  154.4 3.9 %collective-permute-done.17.refs_5_ = bf16[1024,512]{1,0:T(8,128)(2,1)} collective-permute-done((bf16[1024,512]{1,0:T(8,128)(2,1)}, bf16[1024,512]{1,0:T(8,128)(2,1)}, u32[]{:S(2)}, u32[]{:S(2)}) %collective-permute-start.17) | collective-permute-done | bytes 1048608 | tf_op jit(solution)/shard_map/ppermute | solution.py:224
  158.3 7.0 %shard_map.72 = bf16[1024,1536]{1,0:T(8,128)(2,1)} custom-call(s32[2]{0:T(128)S(1)} %pad_add_fusion.1.at_ref, bf16[512,512]{1,0:T(8,128)(2,1)S(1)} %shard_map.69.refs_0_, bf16[512,512]{1,0:T(8,128)(2,1)S(1)} %collective-permute-done.15.refs_1_, bf16[512,512]{1,0:T(8,128)(2,1)S(1)} %shard_map.71.refs_2_, ...), custom_call_target="tpu_custom_call" | custom-call | flops 1 | bytes 1 | tf_op jit(solution)/shard_map/pallas_call | solution.py:68
  165.3 1.1 slice.81
  166.4 1.8 collective-permute-start.20
  168.2 1.1 slice.82
  169.3 1.5 collective-permute-start.21
  170.8 8.3 %collective-permute-done.20.refs_4_ = bf16[512,512]{1,0:T(8,128)(2,1)S(1)} collective-permute-done((bf16[512,512]{1,0:T(8,128)(2,1)S(1)}, bf16[512,512]{1,0:T(8,128)(2,1)S(1)}, u32[]{:S(2)}, u32[]{:S(2)}) %collective-permute-start.20) | collective-permute-done | bytes 524320 | tf_op jit(solution)/shard_map/ppermute | solution.py:224
  179.2 2.6 %collective-permute-done.21.refs_5_ = bf16[512,512]{1,0:T(8,128)(2,1)S(1)} collective-permute-done((bf16[512,512]{1,0:T(8,128)(2,1)S(1)}, bf16[512,512]{1,0:T(8,128)(2,1)S(1)}, u32[]{:S(2)}, u32[]{:S(2)}) %collective-permute-start.21) | collective-permute-done | bytes 524320 | tf_op jit(solution)/shard_map/ppermute | solution.py:224
  181.8 1.9 shard_map.73
  183.7 1.3 collective-permute-start.22
  185.0 1.3 collective-permute-start.25
  186.3 10.0 %collective-permute-done.22 = bf16[256,512]{1,0:T(8,128)(2,1)S(1)} collective-permute-done((bf16[256,512]{1,0:T(8,128)(2,1)S(1)}, bf16[256,512]{1,0:T(8,128)(2,1)S(1)}, u32[]{:S(2)}, u32[]{:S(2)}) %collective-permute-start.22) | collective-permute-done | bytes 262176 | tf_op jit(solution)/shard_map/ppermute | solution.py:359
  196.2 10.8 %collective-permute-done.25 = bf16[256,512]{1,0:T(8,128)(2,1)S(1)} collective-permute-done((bf16[256,512]{1,0:T(8,128)(2,1)S(1)}, bf16[256,512]{1,0:T(8,128)(2,1)S(1)}, u32[]{:S(2)}, u32[]{:S(2)}) %collective-permute-start.25) | collective-permute-done | bytes 262176 | tf_op jit(solution)/shard_map/ppermute | solution.py:360
  207.1 1.3 collective-permute-start.26
  208.4 4.8 %collective-permute-start.23 = (bf16[256,512]{1,0:T(8,128)(2,1)S(1)}, bf16[256,512]{1,0:T(8,128)(2,1)S(1)}, u32[]{:S(2)}, u32[]{:S(2)}) collective-permute-start(bf16[256,512]{1,0:T(8,128)(2,1)S(1)} %get-tuple-element.99), channel_id=1, source_target_pairs={{0,1},{1,2},{2,3},{4,5},{5,6},{6,7},{8,9},{9,10},{10,11},{12,13},{... | collective-permute-start | bytes 786440 | tf_op jit(solution)/shard_map/ppermute | solution.py:359
  213.3 15.7 %collective-permute-done.26 = bf16[256,512]{1,0:T(8,128)(2,1)S(1)} collective-permute-done((bf16[256,512]{1,0:T(8,128)(2,1)S(1)}, bf16[256,512]{1,0:T(8,128)(2,1)S(1)}, u32[]{:S(2)}, u32[]{:S(2)}) %collective-permute-start.26) | collective-permute-done | bytes 262176 | tf_op jit(solution)/shard_map/ppermute | solution.py:360
  229.1 1.3 collective-permute-start.27
  230.5 5.2 %collective-permute-start.24 = (bf16[256,512]{1,0:T(8,128)(2,1)S(1)}, bf16[256,512]{1,0:T(8,128)(2,1)S(1)}, u32[]{:S(2)}, u32[]{:S(2)}) collective-permute-start(bf16[256,512]{1,0:T(8,128)(2,1)S(1)} %add_convert_fusion.1), channel_id=1, source_target_pairs={{0,1},{1,2},{2,3},{4,5},{5,6},{6,7},{8,9},{9,10},{10,11},{12,13},{... | collective-permute-start | bytes 786440 | tf_op jit(solution)/shard_map/ppermute | solution.py:359
  235.7 3.9 %reduce-scatter.2.cloned.1.call-done = bf16[256,1536]{1,0:T(8,128)(2,1)} async-done(((bf16[1024,1536]{1,0:T(8,128)(2,1)}), bf16[256,1536]{1,0:T(8,128)(2,1)}) %reduce-scatter.2.cloned.1.call-update) | async-done | bytes 786448 | tf_op jit(solution)/shard_map/reduce_scatter | solution.py:368
  239.6 1.9 fusion.26
  242.3 1.2 collective-permute-done.28
  246.0 1.0 copy-done.28
  (105 shorter events, 12.7 us)
Async XLA Ops:
  6.5 119.1 %copy-start = (f32[7,64]{1,0:T(8,128)S(1)}, f32[7,64]{1,0:T(8,128)}, u32[]{:S(2)}) copy-start(f32[7,64]{1,0:T(8,128)} %param.9) | copy-start | bytes 5380
  6.5 87.1 %all-gather.2.cloned.1.call-start = ((), (), s32[]{:S(2)}) async-start(), calls=%async_computation.1 | async-start | bytes 5242880 | tf_op jit(solution)/shard_map/all_gather | solution.py:275
  6.5 1.9 copy-start.24
  6.5 2.2 copy-start.29
  10.0 229.6 %reduce-scatter.2.cloned.1.call-start = ((), (), s32[]{:S(2)}) async-start(), calls=%async_computation.2 | async-start | bytes 3932160 | tf_op jit(solution)/shard_map/reduce_scatter | solution.py:368
  10.1 4.6 %collective-permute-start = (bf16[2,512,512]{2,1,0:T(8,128)(2,1)S(1)}, bf16[2,512,512]{2,1,0:T(8,128)(2,1)S(1)}, u32[]{:S(2)}, u32[]{:S(2)}) collective-permute-start(bf16[2,512,512]{2,1,0:T(8,128)(2,1)S(1)} %get-tuple-element.88), channel_id=1, source_target_pairs={{0,4},{4,0},{8,12},{12,8},{16,20},{20,16},{24,28},{28,24},{1,5},{5... | collective-permute-start | bytes 3145736 | tf_op jit(solution)/shard_map/ppermute | solution.py:227
  10.6 26.6 %collective-permute-start.1 = (bf16[2,512,512]{2,1,0:T(8,128)(2,1)S(1)}, bf16[2,512,512]{2,1,0:T(8,128)(2,1)S(1)}, u32[]{:S(2)}, u32[]{:S(2)}) collective-permute-start(bf16[2,512,512]{2,1,0:T(8,128)(2,1)S(1)} %get-tuple-element.55.refs_1_.refs_2_), channel_id=1, source_target_pairs={{8,0},{12,4},{0,8},{4,12},{24,16},{28,20},{16,24},{20,28},{9,1},{1... | collective-permute-start | bytes 3145736 | tf_op jit(solution)/shard_map/ppermute | solution.py:224
  13.2 26.0 %collective-permute-start.3 = (bf16[2,512,512]{2,1,0:T(8,128)(2,1)S(1)}, bf16[2,512,512]{2,1,0:T(8,128)(2,1)S(1)}, u32[]{:S(2)}, u32[]{:S(2)}) collective-permute-start(bf16[2,512,512]{2,1,0:T(8,128)(2,1)S(1)} %get-tuple-element.55.refs_1_.refs_2_), channel_id=1, source_target_pairs={{16,0},{20,4},{24,8},{28,12},{0,16},{4,20},{8,24},{12,28},{17,1},{... | collective-permute-start | bytes 3145736 | tf_op jit(solution)/shard_map/ppermute | solution.py:224
  14.7 5.9 %copy-start.3 = (bf16[2,512,512]{2,1,0:T(8,128)(2,1)}, bf16[2,512,512]{2,1,0:T(8,128)(2,1)S(1)}, u32[]{:S(2)}) copy-start(bf16[2,512,512]{2,1,0:T(8,128)(2,1)S(1)} %collective-permute-done.refs_2_.refs_3_) | copy-start | bytes 3145732
  14.7 44.7 %collective-permute-start.2 = (bf16[2,512,512]{2,1,0:T(8,128)(2,1)S(1)}, bf16[2,512,512]{2,1,0:T(8,128)(2,1)S(1)}, u32[]{:S(2)}, u32[]{:S(2)}) collective-permute-start(bf16[2,512,512]{2,1,0:T(8,128)(2,1)S(1)} %collective-permute-done.refs_2_.refs_3_), channel_id=1, source_target_pairs={{8,0},{12,4},{0,8},{4,12},{24,16},{28,20},{16,24},{20,28},{9,1},{1... | collective-permute-start | bytes 3145736 | tf_op jit(solution)/shard_map/ppermute | solution.py:224
  15.8 45.1 %collective-permute-start.4 = (bf16[2,512,512]{2,1,0:T(8,128)(2,1)S(1)}, bf16[2,512,512]{2,1,0:T(8,128)(2,1)S(1)}, u32[]{:S(2)}, u32[]{:S(2)}) collective-permute-start(bf16[2,512,512]{2,1,0:T(8,128)(2,1)S(1)} %collective-permute-done.refs_2_.refs_3_), channel_id=1, source_target_pairs={{16,0},{20,4},{24,8},{28,12},{0,16},{4,20},{8,24},{12,28},{17,1},{... | collective-permute-start | bytes 3145736 | tf_op jit(solution)/shard_map/ppermute | solution.py:224
  18.5 2.0 collective-permute-start.5
  39.2 1.0 copy-start.9
  59.4 1.0 copy-start.12
  60.9 26.1 %collective-permute-start.6 = (bf16[2,512,512]{2,1,0:T(8,128)(2,1)S(1)}, bf16[2,512,512]{2,1,0:T(8,128)(2,1)S(1)}, u32[]{:S(2)}, u32[]{:S(2)}) collective-permute-start(bf16[2,512,512]{2,1,0:T(8,128)(2,1)S(1)} %collective-permute-done.1.refs_3_.refs_4_), channel_id=1, source_target_pairs={{16,0},{20,4},{24,8},{28,12},{0,16},{4,20},{8,24},{12,28},{17,1},{... | collective-permute-start | bytes 3145736 | tf_op jit(solution)/shard_map/ppermute | solution.py:224
  62.4 1.0 copy-start.6
  63.4 26.1 %collective-permute-start.7 = (bf16[2,512,512]{2,1,0:T(8,128)(2,1)S(1)}, bf16[2,512,512]{2,1,0:T(8,128)(2,1)S(1)}, u32[]{:S(2)}, u32[]{:S(2)}) collective-permute-start(bf16[2,512,512]{2,1,0:T(8,128)(2,1)S(1)} %collective-permute-done.4.refs_6_.refs_7_), channel_id=1, source_target_pairs={{8,0},{12,4},{0,8},{4,12},{24,16},{28,20},{16,24},{20,28},{9,1},{1... | collective-permute-start | bytes 3145736 | tf_op jit(solution)/shard_map/ppermute | solution.py:224
  64.6 1.0 copy-start.15
  65.6 47.9 %collective-permute-start.8 = (bf16[2,512,512]{2,1,0:T(8,128)(2,1)S(1)}, bf16[2,512,512]{2,1,0:T(8,128)(2,1)S(1)}, u32[]{:S(2)}, u32[]{:S(2)}) collective-permute-start(bf16[2,512,512]{2,1,0:T(8,128)(2,1)S(1)} %pad_maximum_fusion.refs_1_), channel_id=1, source_target_pairs={{8,0},{12,4},{0,8},{4,12},{24,16},{28,20},{16,24},{20,28},{9,1},{1... | collective-permute-start | bytes 3145736 | tf_op jit(solution)/shard_map/ppermute | solution.py:224
  66.4 47.2 %collective-permute-start.9 = (bf16[2,512,512]{2,1,0:T(8,128)(2,1)S(1)}, bf16[2,512,512]{2,1,0:T(8,128)(2,1)}, u32[]{:S(2)}, u32[]{:S(2)}) collective-permute-start(bf16[2,512,512]{2,1,0:T(8,128)(2,1)S(1)} %pad_maximum_fusion.refs_1_), channel_id=1, source_target_pairs={{16,0},{20,4},{24,8},{28,12},{0,16},{4,20},{8,24},{12,28},{17,1},{... | collective-permute-start | bytes 3145736 | tf_op jit(solution)/shard_map/ppermute | solution.py:224
  87.0 1.0 copy-start.18
  89.5 1.0 copy-start.21
  94.6 18.9 %collective-permute-start.10 = (bf16[16,4096]{1,0:T(8,128)(2,1)S(1)}, bf16[16,4096]{1,0:T(8,128)(2,1)S(1)}, u32[]{:S(2)}, u32[]{:S(2)}) collective-permute-start(bf16[16,4096]{1,0:T(8,128)(2,1)S(1)} %slice.56), channel_id=1, source_target_pairs={{4,8},{12,16},{20,24},{5,9},{13,17},{21,25},{6,10},{14,18},{22,26}... | collective-permute-start | bytes 393224 | tf_op jit(solution)/shard_map/ppermute | solution.py:299
  95.2 18.3 %collective-permute-start.11 = (bf16[16,4096]{1,0:T(8,128)(2,1)S(1)}, bf16[16,4096]{1,0:T(8,128)(2,1)S(1)}, u32[]{:S(2)}, u32[]{:S(2)}) collective-permute-start(bf16[16,4096]{1,0:T(8,128)(2,1)S(1)} %slice.56), channel_id=1, source_target_pairs={{4,12},{12,20},{20,28},{5,13},{13,21},{21,29},{6,14},{14,22},{22,3... | collective-permute-start | bytes 393224 | tf_op jit(solution)/shard_map/ppermute | solution.py:299
  96.1 1.2 copy-start.4
  97.4 1.2 copy-start.7
  98.6 1.2 copy-start.10
  99.8 1.2 copy-start.13
  101.0 1.2 copy-start.16
  102.3 1.2 copy-start.19
  103.5 1.2 copy-start.22
  112.5 1.0 copy-start.1
  113.6 17.0 %collective-permute-start.12 = (bf16[512,4096]{1,0:T(8,128)(2,1)}, bf16[512,4096]{1,0:T(8,128)(2,1)}, u32[]{:S(2)}, u32[]{:S(2)}) collective-permute-start(bf16[512,4096]{1,0:T(8,128)(2,1)} %all-gather.2.cloned.1.call-done.refs_0_), channel_id=1, source_target_pairs={{0,4},{4,0},{8,12},{12,8},{16,20},{20,16},{24,28},{28,24},{1,5},{5... | collective-permute-start | bytes 12582920 | tf_op jit(solution)/shard_map/ppermute | solution.py:227
  119.7 27.5 %collective-permute-start.13 = (bf16[512,512]{1,0:T(8,128)(2,1)}, bf16[512,512]{1,0:T(8,128)(2,1)}, u32[]{:S(2)}, u32[]{:S(2)}) collective-permute-start(bf16[512,512]{1,0:T(8,128)(2,1)} %slice_bitcast_fusion.1), channel_id=1, source_target_pairs={{16,0},{20,4},{24,8},{28,12},{0,16},{4,20},{8,24},{12,28},{17,1},{... | collective-permute-start | bytes 1572872 | tf_op jit(solution)/shard_map/ppermute | solution.py:224
  121.9 25.3 %collective-permute-start.14 = (bf16[512,512]{1,0:T(8,128)(2,1)}, bf16[512,512]{1,0:T(8,128)(2,1)}, u32[]{:S(2)}, u32[]{:S(2)}) collective-permute-start(bf16[512,512]{1,0:T(8,128)(2,1)} %slice_bitcast_fusion), channel_id=1, source_target_pairs={{8,0},{12,4},{0,8},{4,12},{24,16},{28,20},{16,24},{20,28},{9,1},{1... | collective-permute-start | bytes 1572872 | tf_op jit(solution)/shard_map/ppermute | solution.py:224
  123.1 35.2 %collective-permute-start.17 = (bf16[1024,512]{1,0:T(8,128)(2,1)}, bf16[1024,512]{1,0:T(8,128)(2,1)}, u32[]{:S(2)}, u32[]{:S(2)}) collective-permute-start(bf16[1024,512]{1,0:T(8,128)(2,1)} %refs_4_.1), channel_id=1, source_target_pairs={{8,0},{12,4},{0,8},{4,12},{24,16},{28,20},{16,24},{20,28},{9,1},{1... | collective-permute-start | bytes 3145736 | tf_op jit(solution)/shard_map/ppermute | solution.py:224
  123.9 34.3 %collective-permute-start.18 = (bf16[1024,512]{1,0:T(8,128)(2,1)}, bf16[1024,512]{1,0:T(8,128)(2,1)}, u32[]{:S(2)}, u32[]{:S(2)}) collective-permute-start(bf16[1024,512]{1,0:T(8,128)(2,1)} %refs_4_.1), channel_id=1, source_target_pairs={{16,0},{20,4},{24,8},{28,12},{0,16},{4,20},{8,24},{12,28},{17,1},{... | collective-permute-start | bytes 3145736 | tf_op jit(solution)/shard_map/ppermute | solution.py:224
  126.0 4.5 %copy-start.5 = (bf16[2,512,512]{2,1,0:T(8,128)(2,1)S(1)}, bf16[2,512,512]{2,1,0:T(8,128)(2,1)}, u32[]{:S(2)}) copy-start(bf16[2,512,512]{2,1,0:T(8,128)(2,1)} %copy-done.3) | copy-start | bytes 3145732
  126.0 4.5 %copy-start.8 = (bf16[2,512,512]{2,1,0:T(8,128)(2,1)S(1)}, bf16[2,512,512]{2,1,0:T(8,128)(2,1)}, u32[]{:S(2)}) copy-start(bf16[2,512,512]{2,1,0:T(8,128)(2,1)} %copy-done.6) | copy-start | bytes 3145732
  126.0 4.5 %copy-start.11 = (bf16[2,512,512]{2,1,0:T(8,128)(2,1)S(1)}, bf16[2,512,512]{2,1,0:T(8,128)(2,1)}, u32[]{:S(2)}) copy-start(bf16[2,512,512]{2,1,0:T(8,128)(2,1)} %copy-done.9) | copy-start | bytes 3145732
  126.0 4.5 %copy-start.14 = (bf16[2,512,512]{2,1,0:T(8,128)(2,1)S(1)}, bf16[2,512,512]{2,1,0:T(8,128)(2,1)}, u32[]{:S(2)}) copy-start(bf16[2,512,512]{2,1,0:T(8,128)(2,1)} %copy-done.12) | copy-start | bytes 3145732
  126.0 4.5 %copy-start.17 = (bf16[2,512,512]{2,1,0:T(8,128)(2,1)S(1)}, bf16[2,512,512]{2,1,0:T(8,128)(2,1)}, u32[]{:S(2)}) copy-start(bf16[2,512,512]{2,1,0:T(8,128)(2,1)} %copy-done.15) | copy-start | bytes 3145732
  126.1 4.5 %copy-start.20 = (bf16[2,512,512]{2,1,0:T(8,128)(2,1)S(1)}, bf16[2,512,512]{2,1,0:T(8,128)(2,1)}, u32[]{:S(2)}) copy-start(bf16[2,512,512]{2,1,0:T(8,128)(2,1)} %copy-done.18) | copy-start | bytes 3145732
  126.1 4.7 %copy-start.23 = (bf16[2,512,512]{2,1,0:T(8,128)(2,1)S(1)}, bf16[2,512,512]{2,1,0:T(8,128)(2,1)}, u32[]{:S(2)}) copy-start(bf16[2,512,512]{2,1,0:T(8,128)(2,1)} %copy-done.21) | copy-start | bytes 3145732
  130.5 8.3 %copy-start.2 = (f32[512,512]{1,0:T(8,128)S(1)}, f32[512,512]{1,0:T(8,128)}, u32[]{:S(2)}) copy-start(f32[512,512]{1,0:T(8,128)} %copy-done.1) | copy-start | bytes 3145732
  150.4 7.8 %collective-permute-start.15 = (bf16[512,512]{1,0:T(8,128)(2,1)S(1)}, bf16[512,512]{1,0:T(8,128)(2,1)S(1)}, u32[]{:S(2)}, u32[]{:S(2)}) collective-permute-start(bf16[512,512]{1,0:T(8,128)(2,1)S(1)} %shard_map.71.refs_2_), channel_id=1, source_target_pairs={{0,4},{4,0},{8,12},{12,8},{16,20},{20,16},{24,28},{28,24},{1,5},{5... | collective-permute-start | bytes 1572872 | tf_op jit(solution)/shard_map/ppermute | solution.py:227
  153.7 4.5 %collective-permute-start.16 = (bf16[512,512]{1,0:T(8,128)(2,1)S(1)}, bf16[512,512]{1,0:T(8,128)(2,1)S(1)}, u32[]{:S(2)}, u32[]{:S(2)}) collective-permute-start(bf16[512,512]{1,0:T(8,128)(2,1)S(1)} %shard_map.69.refs_0_), channel_id=1, source_target_pairs={{0,4},{4,0},{8,12},{12,8},{16,20},{20,16},{24,28},{28,24},{1,5},{5... | collective-permute-start | bytes 1572872 | tf_op jit(solution)/shard_map/ppermute | solution.py:227
  166.4 12.7 %collective-permute-start.20 = (bf16[512,512]{1,0:T(8,128)(2,1)S(1)}, bf16[512,512]{1,0:T(8,128)(2,1)S(1)}, u32[]{:S(2)}, u32[]{:S(2)}) collective-permute-start(bf16[512,512]{1,0:T(8,128)(2,1)S(1)} %slice.81), channel_id=1, source_target_pairs={{16,0},{20,4},{24,8},{28,12},{0,16},{4,20},{8,24},{12,28},{17,1},{... | collective-permute-start | bytes 1572872 | tf_op jit(solution)/shard_map/ppermute | solution.py:224
  169.3 12.5 %collective-permute-start.21 = (bf16[512,512]{1,0:T(8,128)(2,1)S(1)}, bf16[512,512]{1,0:T(8,128)(2,1)S(1)}, u32[]{:S(2)}, u32[]{:S(2)}) collective-permute-start(bf16[512,512]{1,0:T(8,128)(2,1)S(1)} %slice.82), channel_id=1, source_target_pairs={{8,0},{12,4},{0,8},{4,12},{24,16},{28,20},{16,24},{20,28},{9,1},{1... | collective-permute-start | bytes 1572872 | tf_op jit(solution)/shard_map/ppermute | solution.py:224
  183.7 12.6 %collective-permute-start.22 = (bf16[256,512]{1,0:T(8,128)(2,1)S(1)}, bf16[256,512]{1,0:T(8,128)(2,1)S(1)}, u32[]{:S(2)}, u32[]{:S(2)}) collective-permute-start(bf16[256,512]{1,0:T(8,128)(2,1)S(1)} %get-tuple-element.84), channel_id=1, source_target_pairs={{0,1},{1,2},{2,3},{4,5},{5,6},{6,7},{8,9},{9,10},{10,11},{12,13},{... | collective-permute-start | bytes 786440 | tf_op jit(solution)/shard_map/ppermute | solution.py:359
  185.0 22.0 %collective-permute-start.25 = (bf16[256,512]{1,0:T(8,128)(2,1)S(1)}, bf16[256,512]{1,0:T(8,128)(2,1)S(1)}, u32[]{:S(2)}, u32[]{:S(2)}) collective-permute-start(bf16[256,512]{1,0:T(8,128)(2,1)S(1)} %get-tuple-element.82), channel_id=1, source_target_pairs={{1,0},{2,1},{3,2},{5,4},{6,5},{7,6},{9,8},{10,9},{11,10},{13,12},{... | collective-permute-start | bytes 786440 | tf_op jit(solution)/shard_map/ppermute | solution.py:360
  207.1 21.9 %collective-permute-start.26 = (bf16[256,512]{1,0:T(8,128)(2,1)S(1)}, bf16[256,512]{1,0:T(8,128)(2,1)S(1)}, u32[]{:S(2)}, u32[]{:S(2)}) collective-permute-start(bf16[256,512]{1,0:T(8,128)(2,1)S(1)} %get-tuple-element.100), channel_id=1, source_target_pairs={{1,0},{2,1},{3,2},{5,4},{6,5},{7,6},{9,8},{10,9},{11,10},{13,12},{... | collective-permute-start | bytes 786440 | tf_op jit(solution)/shard_map/ppermute | solution.py:360
  208.4 21.9 %collective-permute-start.23 = (bf16[256,512]{1,0:T(8,128)(2,1)S(1)}, bf16[256,512]{1,0:T(8,128)(2,1)S(1)}, u32[]{:S(2)}, u32[]{:S(2)}) collective-permute-start(bf16[256,512]{1,0:T(8,128)(2,1)S(1)} %get-tuple-element.99), channel_id=1, source_target_pairs={{0,1},{1,2},{2,3},{4,5},{5,6},{6,7},{8,9},{9,10},{10,11},{12,13},{... | collective-permute-start | bytes 786440 | tf_op jit(solution)/shard_map/ppermute | solution.py:359
  229.1 12.5 %collective-permute-start.27 = (bf16[256,512]{1,0:T(8,128)(2,1)S(1)}, bf16[256,512]{1,0:T(8,128)(2,1)S(1)}, u32[]{:S(2)}, u32[]{:S(2)}) collective-permute-start(bf16[256,512]{1,0:T(8,128)(2,1)S(1)} %add_convert_fusion), channel_id=1, source_target_pairs={{1,0},{2,1},{3,2},{5,4},{6,5},{7,6},{9,8},{10,9},{11,10},{13,12},{... | collective-permute-start | bytes 786440 | tf_op jit(solution)/shard_map/ppermute | solution.py:360
  230.5 11.1 %collective-permute-start.24 = (bf16[256,512]{1,0:T(8,128)(2,1)S(1)}, bf16[256,512]{1,0:T(8,128)(2,1)S(1)}, u32[]{:S(2)}, u32[]{:S(2)}) collective-permute-start(bf16[256,512]{1,0:T(8,128)(2,1)S(1)} %add_convert_fusion.1), channel_id=1, source_target_pairs={{0,1},{1,2},{2,3},{4,5},{5,6},{6,7},{8,9},{9,10},{10,11},{12,13},{... | collective-permute-start | bytes 786440 | tf_op jit(solution)/shard_map/ppermute | solution.py:359
  241.6 2.0 collective-permute-start.19
  241.7 2.0 copy-start.27
  241.7 1.8 collective-permute-start.28
  243.5 1.2 copy-start.25
  243.5 1.9 copy-start.26
  245.4 1.5 slice-start
  246.0 1.0 copy-start.28
Sparse Core Ops, SparseCore 0:
  10.2 83.4 all-gather.1
  165.5 74.1 reduce-scatter.1

commit v10 on v9

--- a/solution.py
+++ b/solution.py
@@ -125,7 +125,7 @@
         functools.partial(product_kernel, len(xs), len(pieces)),
         out_shape=[jax.ShapeDtypeStruct((x.shape[0], half), F32) for x in xs],
         in_specs=[pl.BlockSpec(memory_space=pltpu.SMEM)]
-        + [pl.BlockSpec(memory_space=pl.ANY)] * (len(xs) + len(pieces)),
+        + [pl.BlockSpec(memory_space=pltpu.HBM)] * (len(xs) + len(pieces)),
         out_specs=[WHOLE] * len(xs),
         scratch_shapes=held,
         compiler_params=pltpu.CompilerParams(vmem_limit_bytes=2 * GRANT),

time: 256 us -> 256 us (level)
  no operation moved by 1% of the time
where the time goes in v10:
time: 256 us; the launch traced here: 255 us
  waiting for transfers between devices  121 us (47%)
  Pallas kernels  44.1 us (17%)
  starting transfers between devices  41.8 us (16%)
  local copies, waits for them, and re-layouts  27.7 us (11%)
  between operations  14 us (5%)
  other arithmetic  5.56 us (2%)
    ppermute x14, waiting for transfers between devices, from_chip(): return lax.ppermute(block, 'seq', route)  74.7 us
    pallas_call x8, Pallas kernels, call(): pl.pallas_call(kernel, out_shape=out, in_specs=[pl.BlockSpec(memory_space...  28.2 us
    ppermute x3, waiting for transfers between devices, chained(): falling = lax.ppermute(send_down, 'tp', down)  26.5 us
    unnamed x60, local copies, waits for them, and re-layouts  18.2 us
    ppermute x14, starting transfers between devices, from_chip(): return lax.ppermute(block, 'seq', route)  18.1 us
    pallas_call x2, Pallas kernels, products(): pl.pallas_call(functools.partial(product_kernel, len(xs), len(pieces)), o...  15.9 us
    ppermute x3, starting transfers between devices, chained(): rising = lax.ppermute(send_up, 'tp', up)  11.4 us
    ppermute x3, waiting for transfers between devices, chained(): rising = lax.ppermute(send_up, 'tp', up)  9.96 us
  transfers between devices with their start and end apart: 31, of which 16 were waited for; matrix products, arithmetic and copies ran while one was open for 4% of the time, Pallas kernels for 15%

profile of v10, /device:TPU:0, one launch (start us, length us, event | category | flops | bytes accessed | tf_op | source)
XLA Modules:
  0.0 254.6 jit_solution(6490131528506578746)
XLA Ops:
  6.5 1.8 constant_dynamic-slice_fusion.2
  8.7 1.3 fusion.2
  10.6 2.6 %collective-permute-start.1 = (bf16[2,512,512]{2,1,0:T(8,128)(2,1)S(1)}, bf16[2,512,512]{2,1,0:T(8,128)(2,1)S(1)}, u32[]{:S(2)}, u32[]{:S(2)}) collective-permute-start(bf16[2,512,512]{2,1,0:T(8,128)(2,1)S(1)} %get-tuple-element.55.refs_1_.refs_2_), channel_id=1, source_target_pairs={{8,0},{12,4},{0,8},{4,12},{24,16},{28,20},{16,24},{20,28},{9,1},{1... | collective-permute-start | bytes 3145736 | tf_op jit(solution)/shard_map/ppermute | solution.py:224
  13.2 1.5 collective-permute-start.3
  14.7 1.1 collective-permute-start.2
  15.8 1.5 collective-permute-start.4
  17.3 1.3 constant_dynamic-slice_fusion.1
  18.6 1.9 collective-permute-done.5
  20.6 16.5 %collective-permute-done.1.refs_3_.refs_4_ = bf16[2,512,512]{2,1,0:T(8,128)(2,1)S(1)} collective-permute-done((bf16[2,512,512]{2,1,0:T(8,128)(2,1)S(1)}, bf16[2,512,512]{2,1,0:T(8,128)(2,1)S(1)}, u32[]{:S(2)}, u32[]{:S(2)}) %collective-permute-start.1) | collective-permute-done | bytes 1048608 | tf_op jit(solution)/shard_map/ppermute | solution.py:224
  37.2 2.0 collective-permute-done.3.refs_5_.refs_6_
  39.2 1.0 copy-done.9
  40.2 19.2 %collective-permute-done.2.refs_4_.refs_5_ = bf16[2,512,512]{2,1,0:T(8,128)(2,1)S(1)} collective-permute-done((bf16[2,512,512]{2,1,0:T(8,128)(2,1)S(1)}, bf16[2,512,512]{2,1,0:T(8,128)(2,1)S(1)}, u32[]{:S(2)}, u32[]{:S(2)}) %collective-permute-start.2) | collective-permute-done | bytes 1048608 | tf_op jit(solution)/shard_map/ppermute | solution.py:224
  59.4 1.0 copy-done.12
  60.9 1.5 collective-permute-start.6
  62.4 1.0 copy-done.6
  63.4 1.3 collective-permute-start.7
  64.6 1.0 copy-done.15
  66.9 20.1 %collective-permute-done.6.refs_7_.refs_8_ = bf16[2,512,512]{2,1,0:T(8,128)(2,1)S(1)} collective-permute-done((bf16[2,512,512]{2,1,0:T(8,128)(2,1)S(1)}, bf16[2,512,512]{2,1,0:T(8,128)(2,1)S(1)}, u32[]{:S(2)}, u32[]{:S(2)}) %collective-permute-start.6) | collective-permute-done | bytes 1048608 | tf_op jit(solution)/shard_map/ppermute | solution.py:224
  87.0 1.0 copy-done.18
  88.0 1.5 collective-permute-done.7.refs_8_.refs_9_
  89.5 1.0 copy-done.21
  90.5 3.2 %all-gather.2.cloned.1.call-done.refs_0_ = bf16[512,4096]{1,0:T(8,128)(2,1)} async-done(((bf16[128,4096]{1,0:T(8,128)(2,1)}), bf16[512,4096]{1,0:T(8,128)(2,1)}) %all-gather.2.cloned.1.call-update) | async-done | bytes 4194320 | tf_op jit(solution)/shard_map/all_gather | solution.py:275
  96.1 1.2 copy-done.4
  97.4 1.2 copy-done.7
  98.6 1.2 copy-done.10
  99.8 1.2 copy-done.13
  101.0 1.2 copy-done.16
  102.3 1.2 copy-done.19
  103.5 1.2 copy-done.22
  104.7 7.8 %shard_map.64.product_ref = f32[512,512]{1,0:T(8,128)S(1)} custom-call(s32[8]{0:T(128)S(1)} %stack.55.at_ref._, bf16[512,4096]{1,0:T(8,128)(2,1)} %all-gather.2.cloned.1.call-done.refs_0_, bf16[2,512,512]{2,1,0:T(8,128)(2,1)S(1)} %get-tuple-element.55.refs_1_.refs_2_, bf16[2,512,512]{2,1,0:T(8,128)(2,1)S(1)} %copy-done.4, ...), custom_call_target="tpu_custom_call" | custom-call | flops 1 | bytes 1 | tf_op jit(solution)/shard_map/pallas_call | solution.py:124
  112.5 1.0 copy-done.1
  113.6 5.4 %collective-permute-start.12 = (bf16[512,4096]{1,0:T(8,128)(2,1)}, bf16[512,4096]{1,0:T(8,128)(2,1)}, u32[]{:S(2)}, u32[]{:S(2)}) collective-permute-start(bf16[512,4096]{1,0:T(8,128)(2,1)} %all-gather.2.cloned.1.call-done.refs_0_), channel_id=1, source_target_pairs={{0,4},{4,0},{8,12},{12,8},{16,20},{20,16},{24,28},{28,24},{1,5},{5... | collective-permute-start | bytes 12582920 | tf_op jit(solution)/shard_map/ppermute | solution.py:227
  120.0 1.9 slice_bitcast_fusion
  121.9 1.2 collective-permute-start.14
  123.9 1.7 collective-permute-start.18
  126.1 4.4 %shard_map.65.refs_2_ = f32[512,512]{1,0:T(8,128)S(1)} custom-call(s32[8]{0:T(128)S(1)} %stack.55.at_ref._, bf16[512,4096]{1,0:T(8,128)(2,1)} %all-gather.2.cloned.1.call-done.refs_0_, bf16[2,512,512]{2,1,0:T(8,128)(2,1)S(1)} %pad_maximum_fusion.refs_1_, bf16[2,512,512]{2,1,0:T(8,128)(2,1)S(1)} %collective-permute-done.8.refs_2_, ...), custom_call_target="tpu_custom_call" | custom-call | flops 1 | bytes 1 | tf_op jit(solution)/shard_map/pallas_call | solution.py:68
  130.7 8.1 %shard_map.66 = (f32[16,512]{1,0:T(8,128)S(1)}, f32[512,512]{1,0:T(8,128)S(1)}) custom-call(s32[8]{0:T(128)S(1)} %stack.55.at_ref._, bf16[16,4096]{1,0:T(8,128)(2,1)S(1)} %broadcast_select_fusion.refs_0_, bf16[512,4096]{1,0:T(8,128)(2,1)} %collective-permute-done.12.refs_1_.refs_0_, bf16[2,512,512]{2,1,0:T(8,128)(2,1)S(1)} %get-tuple-element.55.refs_1_.refs_2_, ...), custom_call_target="tpu_custom_call" | custom-call | flops 1 | bytes 1 | tf_op jit(solution)/shard_map/pallas_call | solution.py:124
  138.8 2.0 shard_map.67.refs_1_
  140.9 2.0 shard_map.68.refs_1_
  142.9 4.3 %shard_map.70.refs_2_ = f32[512,512]{1,0:T(8,128)S(1)} custom-call(s32[8]{0:T(128)S(1)} %stack.55.at_ref._, bf16[512,4096]{1,0:T(8,128)(2,1)} %collective-permute-done.12.refs_1_.refs_0_, bf16[2,512,512]{2,1,0:T(8,128)(2,1)S(1)} %pad_maximum_fusion.refs_1_, bf16[2,512,512]{2,1,0:T(8,128)(2,1)S(1)} %collective-permute-done.8.refs_2_, ...), custom_call_target="tpu_custom_call" | custom-call | flops 1 | bytes 1 | tf_op jit(solution)/shard_map/pallas_call | solution.py:68
  147.2 3.2 %shard_map.71.refs_2_ = bf16[512,512]{1,0:T(8,128)(2,1)S(1)} custom-call(s32[2]{0:T(128)S(1)} %pad_add_fusion.at_ref, bf16[512,4096]{1,0:T(8,128)(2,1)} %collective-permute-done.12.refs_1_.refs_0_, f32[512,512]{1,0:T(8,128)S(1)} %shard_map.68.refs_1_, f32[512,512]{1,0:T(8,128)S(1)} %shard_map.70.refs_2_, bf16[512,512]{1,0:T(8,128)(2,1)} %collective-permute-done.13.refs_3_, ...), custom_call_target="tpu_custom_call" | custom-call | flops 1 | bytes 1 | tf_op jit(solution)/shard_map/pallas_call | solution.py:68
  150.5 3.2 %shard_map.69.refs_0_ = bf16[512,512]{1,0:T(8,128)(2,1)S(1)} custom-call(s32[2]{0:T(128)S(1)} %pad_add_fusion.at_ref, bf16[512,4096]{1,0:T(8,128)(2,1)} %all-gather.2.cloned.1.call-done.refs_0_, f32[512,512]{1,0:T(8,128)S(1)} %shard_map.67.refs_1_, f32[512,512]{1,0:T(8,128)S(1)} %shard_map.65.refs_2_, bf16[512,512]{1,0:T(8,128)(2,1)} %collective-permute-done.13.refs_3_, ...), custom_call_target="tpu_custom_call" | custom-call | flops 1 | bytes 1 | tf_op jit(solution)/shard_map/pallas_call | solution.py:68
  154.4 3.9 %collective-permute-done.17.refs_5_ = bf16[1024,512]{1,0:T(8,128)(2,1)} collective-permute-done((bf16[1024,512]{1,0:T(8,128)(2,1)}, bf16[1024,512]{1,0:T(8,128)(2,1)}, u32[]{:S(2)}, u32[]{:S(2)}) %collective-permute-start.17) | collective-permute-done | bytes 1048608 | tf_op jit(solution)/shard_map/ppermute | solution.py:224
  158.3 7.0 %shard_map.72 = bf16[1024,1536]{1,0:T(8,128)(2,1)} custom-call(s32[2]{0:T(128)S(1)} %pad_add_fusion.1.at_ref, bf16[512,512]{1,0:T(8,128)(2,1)S(1)} %shard_map.69.refs_0_, bf16[512,512]{1,0:T(8,128)(2,1)S(1)} %collective-permute-done.15.refs_1_, bf16[512,512]{1,0:T(8,128)(2,1)S(1)} %shard_map.71.refs_2_, ...), custom_call_target="tpu_custom_call" | custom-call | flops 1 | bytes 1 | tf_op jit(solution)/shard_map/pallas_call | solution.py:68
  165.3 1.1 slice.81
  166.4 1.8 collective-permute-start.20
  168.2 1.1 slice.82
  169.3 1.5 collective-permute-start.21
  170.8 8.3 %collective-permute-done.20.refs_4_ = bf16[512,512]{1,0:T(8,128)(2,1)S(1)} collective-permute-done((bf16[512,512]{1,0:T(8,128)(2,1)S(1)}, bf16[512,512]{1,0:T(8,128)(2,1)S(1)}, u32[]{:S(2)}, u32[]{:S(2)}) %collective-permute-start.20) | collective-permute-done | bytes 524320 | tf_op jit(solution)/shard_map/ppermute | solution.py:224
  179.2 2.6 %collective-permute-done.21.refs_5_ = bf16[512,512]{1,0:T(8,128)(2,1)S(1)} collective-permute-done((bf16[512,512]{1,0:T(8,128)(2,1)S(1)}, bf16[512,512]{1,0:T(8,128)(2,1)S(1)}, u32[]{:S(2)}, u32[]{:S(2)}) %collective-permute-start.21) | collective-permute-done | bytes 524320 | tf_op jit(solution)/shard_map/ppermute | solution.py:224
  181.8 1.9 shard_map.73
  183.7 1.3 collective-permute-start.22
  185.0 1.3 collective-permute-start.25
  186.3 10.0 %collective-permute-done.22 = bf16[256,512]{1,0:T(8,128)(2,1)S(1)} collective-permute-done((bf16[256,512]{1,0:T(8,128)(2,1)S(1)}, bf16[256,512]{1,0:T(8,128)(2,1)S(1)}, u32[]{:S(2)}, u32[]{:S(2)}) %collective-permute-start.22) | collective-permute-done | bytes 262176 | tf_op jit(solution)/shard_map/ppermute | solution.py:359
  196.2 10.8 %collective-permute-done.25 = bf16[256,512]{1,0:T(8,128)(2,1)S(1)} collective-permute-done((bf16[256,512]{1,0:T(8,128)(2,1)S(1)}, bf16[256,512]{1,0:T(8,128)(2,1)S(1)}, u32[]{:S(2)}, u32[]{:S(2)}) %collective-permute-start.25) | collective-permute-done | bytes 262176 | tf_op jit(solution)/shard_map/ppermute | solution.py:360
  207.1 1.3 collective-permute-start.26
  208.4 4.8 %collective-permute-start.23 = (bf16[256,512]{1,0:T(8,128)(2,1)S(1)}, bf16[256,512]{1,0:T(8,128)(2,1)S(1)}, u32[]{:S(2)}, u32[]{:S(2)}) collective-permute-start(bf16[256,512]{1,0:T(8,128)(2,1)S(1)} %get-tuple-element.99), channel_id=1, source_target_pairs={{0,1},{1,2},{2,3},{4,5},{5,6},{6,7},{8,9},{9,10},{10,11},{12,13},{... | collective-permute-start | bytes 786440 | tf_op jit(solution)/shard_map/ppermute | solution.py:359
  213.3 15.7 %collective-permute-done.26 = bf16[256,512]{1,0:T(8,128)(2,1)S(1)} collective-permute-done((bf16[256,512]{1,0:T(8,128)(2,1)S(1)}, bf16[256,512]{1,0:T(8,128)(2,1)S(1)}, u32[]{:S(2)}, u32[]{:S(2)}) %collective-permute-start.26) | collective-permute-done | bytes 262176 | tf_op jit(solution)/shard_map/ppermute | solution.py:360
  229.1 1.3 collective-permute-start.27
  230.5 5.2 %collective-permute-start.24 = (bf16[256,512]{1,0:T(8,128)(2,1)S(1)}, bf16[256,512]{1,0:T(8,128)(2,1)S(1)}, u32[]{:S(2)}, u32[]{:S(2)}) collective-permute-start(bf16[256,512]{1,0:T(8,128)(2,1)S(1)} %add_convert_fusion.1), channel_id=1, source_target_pairs={{0,1},{1,2},{2,3},{4,5},{5,6},{6,7},{8,9},{9,10},{10,11},{12,13},{... | collective-permute-start | bytes 786440 | tf_op jit(solution)/shard_map/ppermute | solution.py:359
  235.7 3.9 %reduce-scatter.2.cloned.1.call-done = bf16[256,1536]{1,0:T(8,128)(2,1)} async-done(((bf16[1024,1536]{1,0:T(8,128)(2,1)}), bf16[256,1536]{1,0:T(8,128)(2,1)}) %reduce-scatter.2.cloned.1.call-update) | async-done | bytes 786448 | tf_op jit(solution)/shard_map/reduce_scatter | solution.py:368
  239.6 1.9 fusion.26
  242.3 1.2 collective-permute-done.28
  246.0 1.0 copy-done.28
  (105 shorter events, 12.7 us)
Async XLA Ops:
  6.5 119.1 %copy-start = (f32[7,64]{1,0:T(8,128)S(1)}, f32[7,64]{1,0:T(8,128)}, u32[]{:S(2)}) copy-start(f32[7,64]{1,0:T(8,128)} %param.9) | copy-start | bytes 5380
  6.5 87.1 %all-gather.2.cloned.1.call-start = ((), (), s32[]{:S(2)}) async-start(), calls=%async_computation.1 | async-start | bytes 5242880 | tf_op jit(solution)/shard_map/all_gather | solution.py:275
  6.5 1.9 copy-start.24
  6.5 2.2 copy-start.29
  10.0 229.6 %reduce-scatter.2.cloned.1.call-start = ((), (), s32[]{:S(2)}) async-start(), calls=%async_computation.2 | async-start | bytes 3932160 | tf_op jit(solution)/shard_map/reduce_scatter | solution.py:368
  10.1 4.6 %collective-permute-start = (bf16[2,512,512]{2,1,0:T(8,128)(2,1)S(1)}, bf16[2,512,512]{2,1,0:T(8,128)(2,1)S(1)}, u32[]{:S(2)}, u32[]{:S(2)}) collective-permute-start(bf16[2,512,512]{2,1,0:T(8,128)(2,1)S(1)} %get-tuple-element.88), channel_id=1, source_target_pairs={{0,4},{4,0},{8,12},{12,8},{16,20},{20,16},{24,28},{28,24},{1,5},{5... | collective-permute-start | bytes 3145736 | tf_op jit(solution)/shard_map/ppermute | solution.py:227
  10.6 26.6 %collective-permute-start.1 = (bf16[2,512,512]{2,1,0:T(8,128)(2,1)S(1)}, bf16[2,512,512]{2,1,0:T(8,128)(2,1)S(1)}, u32[]{:S(2)}, u32[]{:S(2)}) collective-permute-start(bf16[2,512,512]{2,1,0:T(8,128)(2,1)S(1)} %get-tuple-element.55.refs_1_.refs_2_), channel_id=1, source_target_pairs={{8,0},{12,4},{0,8},{4,12},{24,16},{28,20},{16,24},{20,28},{9,1},{1... | collective-permute-start | bytes 3145736 | tf_op jit(solution)/shard_map/ppermute | solution.py:224
  13.2 26.0 %collective-permute-start.3 = (bf16[2,512,512]{2,1,0:T(8,128)(2,1)S(1)}, bf16[2,512,512]{2,1,0:T(8,128)(2,1)S(1)}, u32[]{:S(2)}, u32[]{:S(2)}) collective-permute-start(bf16[2,512,512]{2,1,0:T(8,128)(2,1)S(1)} %get-tuple-element.55.refs_1_.refs_2_), channel_id=1, source_target_pairs={{16,0},{20,4},{24,8},{28,12},{0,16},{4,20},{8,24},{12,28},{17,1},{... | collective-permute-start | bytes 3145736 | tf_op jit(solution)/shard_map/ppermute | solution.py:224
  14.7 5.9 %copy-start.3 = (bf16[2,512,512]{2,1,0:T(8,128)(2,1)}, bf16[2,512,512]{2,1,0:T(8,128)(2,1)S(1)}, u32[]{:S(2)}) copy-start(bf16[2,512,512]{2,1,0:T(8,128)(2,1)S(1)} %collective-permute-done.refs_2_.refs_3_) | copy-start | bytes 3145732
  14.7 44.7 %collective-permute-start.2 = (bf16[2,512,512]{2,1,0:T(8,128)(2,1)S(1)}, bf16[2,512,512]{2,1,0:T(8,128)(2,1)S(1)}, u32[]{:S(2)}, u32[]{:S(2)}) collective-permute-start(bf16[2,512,512]{2,1,0:T(8,128)(2,1)S(1)} %collective-permute-done.refs_2_.refs_3_), channel_id=1, source_target_pairs={{8,0},{12,4},{0,8},{4,12},{24,16},{28,20},{16,24},{20,28},{9,1},{1... | collective-permute-start | bytes 3145736 | tf_op jit(solution)/shard_map/ppermute | solution.py:224
  15.8 45.1 %collective-permute-start.4 = (bf16[2,512,512]{2,1,0:T(8,128)(2,1)S(1)}, bf16[2,512,512]{2,1,0:T(8,128)(2,1)S(1)}, u32[]{:S(2)}, u32[]{:S(2)}) collective-permute-start(bf16[2,512,512]{2,1,0:T(8,128)(2,1)S(1)} %collective-permute-done.refs_2_.refs_3_), channel_id=1, source_target_pairs={{16,0},{20,4},{24,8},{28,12},{0,16},{4,20},{8,24},{12,28},{17,1},{... | collective-permute-start | bytes 3145736 | tf_op jit(solution)/shard_map/ppermute | solution.py:224
  18.5 2.0 collective-permute-start.5
  39.2 1.0 copy-start.9
  59.4 1.0 copy-start.12
  60.9 26.1 %collective-permute-start.6 = (bf16[2,512,512]{2,1,0:T(8,128)(2,1)S(1)}, bf16[2,512,512]{2,1,0:T(8,128)(2,1)S(1)}, u32[]{:S(2)}, u32[]{:S(2)}) collective-permute-start(bf16[2,512,512]{2,1,0:T(8,128)(2,1)S(1)} %collective-permute-done.1.refs_3_.refs_4_), channel_id=1, source_target_pairs={{16,0},{20,4},{24,8},{28,12},{0,16},{4,20},{8,24},{12,28},{17,1},{... | collective-permute-start | bytes 3145736 | tf_op jit(solution)/shard_map/ppermute | solution.py:224
  62.4 1.0 copy-start.6
  63.4 26.1 %collective-permute-start.7 = (bf16[2,512,512]{2,1,0:T(8,128)(2,1)S(1)}, bf16[2,512,512]{2,1,0:T(8,128)(2,1)S(1)}, u32[]{:S(2)}, u32[]{:S(2)}) collective-permute-start(bf16[2,512,512]{2,1,0:T(8,128)(2,1)S(1)} %collective-permute-done.4.refs_6_.refs_7_), channel_id=1, source_target_pairs={{8,0},{12,4},{0,8},{4,12},{24,16},{28,20},{16,24},{20,28},{9,1},{1... | collective-permute-start | bytes 3145736 | tf_op jit(solution)/shard_map/ppermute | solution.py:224
  64.6 1.0 copy-start.15
  65.6 47.9 %collective-permute-start.8 = (bf16[2,512,512]{2,1,0:T(8,128)(2,1)S(1)}, bf16[2,512,512]{2,1,0:T(8,128)(2,1)S(1)}, u32[]{:S(2)}, u32[]{:S(2)}) collective-permute-start(bf16[2,512,512]{2,1,0:T(8,128)(2,1)S(1)} %pad_maximum_fusion.refs_1_), channel_id=1, source_target_pairs={{8,0},{12,4},{0,8},{4,12},{24,16},{28,20},{16,24},{20,28},{9,1},{1... | collective-permute-start | bytes 3145736 | tf_op jit(solution)/shard_map/ppermute | solution.py:224
  66.4 47.2 %collective-permute-start.9 = (bf16[2,512,512]{2,1,0:T(8,128)(2,1)S(1)}, bf16[2,512,512]{2,1,0:T(8,128)(2,1)}, u32[]{:S(2)}, u32[]{:S(2)}) collective-permute-start(bf16[2,512,512]{2,1,0:T(8,128)(2,1)S(1)} %pad_maximum_fusion.refs_1_), channel_id=1, source_target_pairs={{16,0},{20,4},{24,8},{28,12},{0,16},{4,20},{8,24},{12,28},{17,1},{... | collective-permute-start | bytes 3145736 | tf_op jit(solution)/shard_map/ppermute | solution.py:224
  87.0 1.0 copy-start.18
  89.5 1.0 copy-start.21
  94.6 18.9 %collective-permute-start.10 = (bf16[16,4096]{1,0:T(8,128)(2,1)S(1)}, bf16[16,4096]{1,0:T(8,128)(2,1)S(1)}, u32[]{:S(2)}, u32[]{:S(2)}) collective-permute-start(bf16[16,4096]{1,0:T(8,128)(2,1)S(1)} %slice.56), channel_id=1, source_target_pairs={{4,8},{12,16},{20,24},{5,9},{13,17},{21,25},{6,10},{14,18},{22,26}... | collective-permute-start | bytes 393224 | tf_op jit(solution)/shard_map/ppermute | solution.py:299
  95.2 18.3 %collective-permute-start.11 = (bf16[16,4096]{1,0:T(8,128)(2,1)S(1)}, bf16[16,4096]{1,0:T(8,128)(2,1)S(1)}, u32[]{:S(2)}, u32[]{:S(2)}) collective-permute-start(bf16[16,4096]{1,0:T(8,128)(2,1)S(1)} %slice.56), channel_id=1, source_target_pairs={{4,12},{12,20},{20,28},{5,13},{13,21},{21,29},{6,14},{14,22},{22,3... | collective-permute-start | bytes 393224 | tf_op jit(solution)/shard_map/ppermute | solution.py:299
  96.1 1.2 copy-start.4
  97.4 1.2 copy-start.7
  98.6 1.2 copy-start.10
  99.8 1.2 copy-start.13
  101.0 1.2 copy-start.16
  102.3 1.2 copy-start.19
  103.5 1.2 copy-start.22
  112.5 1.0 copy-start.1
  113.6 17.0 %collective-permute-start.12 = (bf16[512,4096]{1,0:T(8,128)(2,1)}, bf16[512,4096]{1,0:T(8,128)(2,1)}, u32[]{:S(2)}, u32[]{:S(2)}) collective-permute-start(bf16[512,4096]{1,0:T(8,128)(2,1)} %all-gather.2.cloned.1.call-done.refs_0_), channel_id=1, source_target_pairs={{0,4},{4,0},{8,12},{12,8},{16,20},{20,16},{24,28},{28,24},{1,5},{5... | collective-permute-start | bytes 12582920 | tf_op jit(solution)/shard_map/ppermute | solution.py:227
  119.7 27.5 %collective-permute-start.13 = (bf16[512,512]{1,0:T(8,128)(2,1)}, bf16[512,512]{1,0:T(8,128)(2,1)}, u32[]{:S(2)}, u32[]{:S(2)}) collective-permute-start(bf16[512,512]{1,0:T(8,128)(2,1)} %slice_bitcast_fusion.1), channel_id=1, source_target_pairs={{16,0},{20,4},{24,8},{28,12},{0,16},{4,20},{8,24},{12,28},{17,1},{... | collective-permute-start | bytes 1572872 | tf_op jit(solution)/shard_map/ppermute | solution.py:224
  121.9 25.3 %collective-permute-start.14 = (bf16[512,512]{1,0:T(8,128)(2,1)}, bf16[512,512]{1,0:T(8,128)(2,1)}, u32[]{:S(2)}, u32[]{:S(2)}) collective-permute-start(bf16[512,512]{1,0:T(8,128)(2,1)} %slice_bitcast_fusion), channel_id=1, source_target_pairs={{8,0},{12,4},{0,8},{4,12},{24,16},{28,20},{16,24},{20,28},{9,1},{1... | collective-permute-start | bytes 1572872 | tf_op jit(solution)/shard_map/ppermute | solution.py:224
  123.1 35.2 %collective-permute-start.17 = (bf16[1024,512]{1,0:T(8,128)(2,1)}, bf16[1024,512]{1,0:T(8,128)(2,1)}, u32[]{:S(2)}, u32[]{:S(2)}) collective-permute-start(bf16[1024,512]{1,0:T(8,128)(2,1)} %refs_4_.1), channel_id=1, source_target_pairs={{8,0},{12,4},{0,8},{4,12},{24,16},{28,20},{16,24},{20,28},{9,1},{1... | collective-permute-start | bytes 3145736 | tf_op jit(solution)/shard_map/ppermute | solution.py:224
  123.9 34.3 %collective-permute-start.18 = (bf16[1024,512]{1,0:T(8,128)(2,1)}, bf16[1024,512]{1,0:T(8,128)(2,1)}, u32[]{:S(2)}, u32[]{:S(2)}) collective-permute-start(bf16[1024,512]{1,0:T(8,128)(2,1)} %refs_4_.1), channel_id=1, source_target_pairs={{16,0},{20,4},{24,8},{28,12},{0,16},{4,20},{8,24},{12,28},{17,1},{... | collective-permute-start | bytes 3145736 | tf_op jit(solution)/shard_map/ppermute | solution.py:224
  126.0 4.5 %copy-start.5 = (bf16[2,512,512]{2,1,0:T(8,128)(2,1)S(1)}, bf16[2,512,512]{2,1,0:T(8,128)(2,1)}, u32[]{:S(2)}) copy-start(bf16[2,512,512]{2,1,0:T(8,128)(2,1)} %copy-done.3) | copy-start | bytes 3145732
  126.0 4.5 %copy-start.8 = (bf16[2,512,512]{2,1,0:T(8,128)(2,1)S(1)}, bf16[2,512,512]{2,1,0:T(8,128)(2,1)}, u32[]{:S(2)}) copy-start(bf16[2,512,512]{2,1,0:T(8,128)(2,1)} %copy-done.6) | copy-start | bytes 3145732
  126.0 4.5 %copy-start.11 = (bf16[2,512,512]{2,1,0:T(8,128)(2,1)S(1)}, bf16[2,512,512]{2,1,0:T(8,128)(2,1)}, u32[]{:S(2)}) copy-start(bf16[2,512,512]{2,1,0:T(8,128)(2,1)} %copy-done.9) | copy-start | bytes 3145732
  126.0 4.5 %copy-start.14 = (bf16[2,512,512]{2,1,0:T(8,128)(2,1)S(1)}, bf16[2,512,512]{2,1,0:T(8,128)(2,1)}, u32[]{:S(2)}) copy-start(bf16[2,512,512]{2,1,0:T(8,128)(2,1)} %copy-done.12) | copy-start | bytes 3145732
  126.0 4.5 %copy-start.17 = (bf16[2,512,512]{2,1,0:T(8,128)(2,1)S(1)}, bf16[2,512,512]{2,1,0:T(8,128)(2,1)}, u32[]{:S(2)}) copy-start(bf16[2,512,512]{2,1,0:T(8,128)(2,1)} %copy-done.15) | copy-start | bytes 3145732
  126.1 4.5 %copy-start.20 = (bf16[2,512,512]{2,1,0:T(8,128)(2,1)S(1)}, bf16[2,512,512]{2,1,0:T(8,128)(2,1)}, u32[]{:S(2)}) copy-start(bf16[2,512,512]{2,1,0:T(8,128)(2,1)} %copy-done.18) | copy-start | bytes 3145732
  126.1 4.7 %copy-start.23 = (bf16[2,512,512]{2,1,0:T(8,128)(2,1)S(1)}, bf16[2,512,512]{2,1,0:T(8,128)(2,1)}, u32[]{:S(2)}) copy-start(bf16[2,512,512]{2,1,0:T(8,128)(2,1)} %copy-done.21) | copy-start | bytes 3145732
  130.5 8.3 %copy-start.2 = (f32[512,512]{1,0:T(8,128)S(1)}, f32[512,512]{1,0:T(8,128)}, u32[]{:S(2)}) copy-start(f32[512,512]{1,0:T(8,128)} %copy-done.1) | copy-start | bytes 3145732
  150.4 7.8 %collective-permute-start.15 = (bf16[512,512]{1,0:T(8,128)(2,1)S(1)}, bf16[512,512]{1,0:T(8,128)(2,1)S(1)}, u32[]{:S(2)}, u32[]{:S(2)}) collective-permute-start(bf16[512,512]{1,0:T(8,128)(2,1)S(1)} %shard_map.71.refs_2_), channel_id=1, source_target_pairs={{0,4},{4,0},{8,12},{12,8},{16,20},{20,16},{24,28},{28,24},{1,5},{5... | collective-permute-start | bytes 1572872 | tf_op jit(solution)/shard_map/ppermute | solution.py:227
  153.7 4.5 %collective-permute-start.16 = (bf16[512,512]{1,0:T(8,128)(2,1)S(1)}, bf16[512,512]{1,0:T(8,128)(2,1)S(1)}, u32[]{:S(2)}, u32[]{:S(2)}) collective-permute-start(bf16[512,512]{1,0:T(8,128)(2,1)S(1)} %shard_map.69.refs_0_), channel_id=1, source_target_pairs={{0,4},{4,0},{8,12},{12,8},{16,20},{20,16},{24,28},{28,24},{1,5},{5... | collective-permute-start | bytes 1572872 | tf_op jit(solution)/shard_map/ppermute | solution.py:227
  166.4 12.7 %collective-permute-start.20 = (bf16[512,512]{1,0:T(8,128)(2,1)S(1)}, bf16[512,512]{1,0:T(8,128)(2,1)S(1)}, u32[]{:S(2)}, u32[]{:S(2)}) collective-permute-start(bf16[512,512]{1,0:T(8,128)(2,1)S(1)} %slice.81), channel_id=1, source_target_pairs={{16,0},{20,4},{24,8},{28,12},{0,16},{4,20},{8,24},{12,28},{17,1},{... | collective-permute-start | bytes 1572872 | tf_op jit(solution)/shard_map/ppermute | solution.py:224
  169.3 12.5 %collective-permute-start.21 = (bf16[512,512]{1,0:T(8,128)(2,1)S(1)}, bf16[512,512]{1,0:T(8,128)(2,1)S(1)}, u32[]{:S(2)}, u32[]{:S(2)}) collective-permute-start(bf16[512,512]{1,0:T(8,128)(2,1)S(1)} %slice.82), channel_id=1, source_target_pairs={{8,0},{12,4},{0,8},{4,12},{24,16},{28,20},{16,24},{20,28},{9,1},{1... | collective-permute-start | bytes 1572872 | tf_op jit(solution)/shard_map/ppermute | solution.py:224
  183.7 12.6 %collective-permute-start.22 = (bf16[256,512]{1,0:T(8,128)(2,1)S(1)}, bf16[256,512]{1,0:T(8,128)(2,1)S(1)}, u32[]{:S(2)}, u32[]{:S(2)}) collective-permute-start(bf16[256,512]{1,0:T(8,128)(2,1)S(1)} %get-tuple-element.84), channel_id=1, source_target_pairs={{0,1},{1,2},{2,3},{4,5},{5,6},{6,7},{8,9},{9,10},{10,11},{12,13},{... | collective-permute-start | bytes 786440 | tf_op jit(solution)/shard_map/ppermute | solution.py:359
  185.0 22.0 %collective-permute-start.25 = (bf16[256,512]{1,0:T(8,128)(2,1)S(1)}, bf16[256,512]{1,0:T(8,128)(2,1)S(1)}, u32[]{:S(2)}, u32[]{:S(2)}) collective-permute-start(bf16[256,512]{1,0:T(8,128)(2,1)S(1)} %get-tuple-element.82), channel_id=1, source_target_pairs={{1,0},{2,1},{3,2},{5,4},{6,5},{7,6},{9,8},{10,9},{11,10},{13,12},{... | collective-permute-start | bytes 786440 | tf_op jit(solution)/shard_map/ppermute | solution.py:360
  207.1 21.9 %collective-permute-start.26 = (bf16[256,512]{1,0:T(8,128)(2,1)S(1)}, bf16[256,512]{1,0:T(8,128)(2,1)S(1)}, u32[]{:S(2)}, u32[]{:S(2)}) collective-permute-start(bf16[256,512]{1,0:T(8,128)(2,1)S(1)} %get-tuple-element.100), channel_id=1, source_target_pairs={{1,0},{2,1},{3,2},{5,4},{6,5},{7,6},{9,8},{10,9},{11,10},{13,12},{... | collective-permute-start | bytes 786440 | tf_op jit(solution)/shard_map/ppermute | solution.py:360
  208.4 21.9 %collective-permute-start.23 = (bf16[256,512]{1,0:T(8,128)(2,1)S(1)}, bf16[256,512]{1,0:T(8,128)(2,1)S(1)}, u32[]{:S(2)}, u32[]{:S(2)}) collective-permute-start(bf16[256,512]{1,0:T(8,128)(2,1)S(1)} %get-tuple-element.99), channel_id=1, source_target_pairs={{0,1},{1,2},{2,3},{4,5},{5,6},{6,7},{8,9},{9,10},{10,11},{12,13},{... | collective-permute-start | bytes 786440 | tf_op jit(solution)/shard_map/ppermute | solution.py:359
  229.1 12.5 %collective-permute-start.27 = (bf16[256,512]{1,0:T(8,128)(2,1)S(1)}, bf16[256,512]{1,0:T(8,128)(2,1)S(1)}, u32[]{:S(2)}, u32[]{:S(2)}) collective-permute-start(bf16[256,512]{1,0:T(8,128)(2,1)S(1)} %add_convert_fusion), channel_id=1, source_target_pairs={{1,0},{2,1},{3,2},{5,4},{6,5},{7,6},{9,8},{10,9},{11,10},{13,12},{... | collective-permute-start | bytes 786440 | tf_op jit(solution)/shard_map/ppermute | solution.py:360
  230.5 11.1 %collective-permute-start.24 = (bf16[256,512]{1,0:T(8,128)(2,1)S(1)}, bf16[256,512]{1,0:T(8,128)(2,1)S(1)}, u32[]{:S(2)}, u32[]{:S(2)}) collective-permute-start(bf16[256,512]{1,0:T(8,128)(2,1)S(1)} %add_convert_fusion.1), channel_id=1, source_target_pairs={{0,1},{1,2},{2,3},{4,5},{5,6},{6,7},{8,9},{9,10},{10,11},{12,13},{... | collective-permute-start | bytes 786440 | tf_op jit(solution)/shard_map/ppermute | solution.py:359
  241.6 2.0 collective-permute-start.19
  241.7 2.0 copy-start.27
  241.7 1.8 collective-permute-start.28
  243.5 1.2 copy-start.25
  243.5 1.9 copy-start.26
  245.4 1.5 slice-start
  246.0 1.0 copy-start.28
Sparse Core Ops, SparseCore 0:
  10.2 83.4 all-gather.1
  165.5 74.1 reduce-scatter.1

commit v11 on v9

--- a/solution.py
+++ b/solution.py
@@ -128,7 +128,7 @@
         + [pl.BlockSpec(memory_space=pl.ANY)] * (len(xs) + len(pieces)),
         out_specs=[WHOLE] * len(xs),
         scratch_shapes=held,
-        compiler_params=pltpu.CompilerParams(vmem_limit_bytes=2 * GRANT),
+        compiler_params=pltpu.CompilerParams(vmem_limit_bytes=56 << 20),
         cost_estimate=pl.CostEstimate(flops=1, bytes_accessed=1, transcendentals=0),
     )(at, *xs, *pieces)
 

time: 256 us -> 249 us (0.973)
  local copies, waits for them, and re-layouts: 27.7 us -> 12.7 us
  waiting for transfers between devices: 121 us -> 131 us
  starting transfers between devices: 41.8 us -> 37.5 us
  Pallas kernels: 44.1 us -> 46.8 us
    unnamed x60 -> x36, local copies, waits for them, and re-layouts: 18.2 us -> 3.74 us
    ppermute x14, waiting for transfers between devices: 74.7 us -> 82.4 us  [from_chip(): return lax.ppermute(block, 'seq', route)]
    ppermute x7, starting transfers between devices: 7.14 us -> 2.98 us  [from_partner(): return lax.ppermute(block, 'seq', [(s, s ^ 1) for s in range(n_seq)])]
    pallas_call x2, Pallas kernels: 15.9 us -> 19.2 us  [products(): pl.pallas_call(functools.partial(product_kernel, len(xs), len(pieces)), o...]
  transfers between devices with their start and end apart: 31 -> 31, of which waited for: 16 -> 17; matrix products, arithmetic and copies ran while one was open for 4% -> 4% of each run, Pallas kernels for 15% -> 16%
where the time goes in v11:
time: 249 us; the launch traced here: 248 us
  waiting for transfers between devices  131 us (53%)
  Pallas kernels  46.8 us (19%)
  starting transfers between devices  37.5 us (15%)
  between operations  14 us (6%)
  local copies, waits for them, and re-layouts  12.7 us (5%)
  other arithmetic  6.32 us (3%)
    ppermute x14, waiting for transfers between devices, from_chip(): return lax.ppermute(block, 'seq', route)  82.4 us
    pallas_call x8, Pallas kernels, call(): pl.pallas_call(kernel, out_shape=out, in_specs=[pl.BlockSpec(memory_space...  27.6 us
    ppermute x3, waiting for transfers between devices, chained(): falling = lax.ppermute(send_down, 'tp', down)  26 us
    pallas_call x2, Pallas kernels, products(): pl.pallas_call(functools.partial(product_kernel, len(xs), len(pieces)), o...  19.2 us
    ppermute x14, starting transfers between devices, from_chip(): return lax.ppermute(block, 'seq', route)  16.6 us
    ppermute x3, starting transfers between devices, chained(): rising = lax.ppermute(send_up, 'tp', up)  12.6 us
    ppermute x3, waiting for transfers between devices, chained(): rising = lax.ppermute(send_up, 'tp', up)  10.2 us
    all_gather x1, waiting for transfers between devices, on_device(): own_rows = lax.all_gather(normed, 'tp', axis=0, tiled=True)  5.06 us
  transfers between devices with their start and end apart: 31, of which 17 were waited for; matrix products, arithmetic and copies ran while one was open for 4% of the time, Pallas kernels for 16%

profile of v11, /device:TPU:0, one launch (start us, length us, event | category | flops | bytes accessed | tf_op | source)
XLA Modules:
  0.0 247.9 jit_solution(9675495119835693090)
XLA Ops:
  6.5 1.8 constant_dynamic-slice_fusion.2
  8.7 1.3 fusion.2
  10.6 2.6 %collective-permute-start.1 = (bf16[2,512,512]{2,1,0:T(8,128)(2,1)S(1)}, bf16[2,512,512]{2,1,0:T(8,128)(2,1)S(1)}, u32[]{:S(2)}, u32[]{:S(2)}) collective-permute-start(bf16[2,512,512]{2,1,0:T(8,128)(2,1)S(1)} %get-tuple-element.55.refs_1_.refs_2_), channel_id=1, source_target_pairs={{8,0},{12,4},{0,8},{4,12},{24,16},{28,20},{16,24},{20,28},{9,1},{1... | collective-permute-start | bytes 3145736 | tf_op jit(solution)/shard_map/ppermute | solution.py:224
  13.2 1.5 collective-permute-start.3
  14.7 1.1 collective-permute-start.2
  15.8 1.5 collective-permute-start.4
  17.3 1.3 constant_dynamic-slice_fusion.1
  18.6 1.9 collective-permute-done.5
  20.6 16.5 %collective-permute-done.1.refs_3_.refs_4_ = bf16[2,512,512]{2,1,0:T(8,128)(2,1)S(1)} collective-permute-done((bf16[2,512,512]{2,1,0:T(8,128)(2,1)S(1)}, bf16[2,512,512]{2,1,0:T(8,128)(2,1)S(1)}, u32[]{:S(2)}, u32[]{:S(2)}) %collective-permute-start.1) | collective-permute-done | bytes 1048608 | tf_op jit(solution)/shard_map/ppermute | solution.py:224
  37.2 2.0 collective-permute-done.3.refs_5_.refs_6_
  39.2 20.2 %collective-permute-done.2.refs_4_.refs_5_ = bf16[2,512,512]{2,1,0:T(8,128)(2,1)S(1)} collective-permute-done((bf16[2,512,512]{2,1,0:T(8,128)(2,1)S(1)}, bf16[2,512,512]{2,1,0:T(8,128)(2,1)S(1)}, u32[]{:S(2)}, u32[]{:S(2)}) %collective-permute-start.2) | collective-permute-done | bytes 1048608 | tf_op jit(solution)/shard_map/ppermute | solution.py:224
  59.4 1.5 collective-permute-done.4.refs_6_.refs_7_
  60.9 1.5 collective-permute-start.6
  62.4 0.5 collective-permute-start.7
  62.9 1.5 collective-permute-start.8
  64.9 22.0 %collective-permute-done.6.refs_7_.refs_8_ = bf16[2,512,512]{2,1,0:T(8,128)(2,1)S(1)} collective-permute-done((bf16[2,512,512]{2,1,0:T(8,128)(2,1)S(1)}, bf16[2,512,512]{2,1,0:T(8,128)(2,1)S(1)}, u32[]{:S(2)}, u32[]{:S(2)}) %collective-permute-start.6) | collective-permute-done | bytes 1048608 | tf_op jit(solution)/shard_map/ppermute | solution.py:224
  87.0 1.0 copy-done.13
  88.0 0.6 collective-permute-done.7.refs_8_.refs_9_
  88.6 5.1 %all-gather.2.cloned.1.call-done.refs_0_ = bf16[512,4096]{1,0:T(8,128)(2,1)} async-done(((bf16[128,4096]{1,0:T(8,128)(2,1)}), bf16[512,4096]{1,0:T(8,128)(2,1)}) %all-gather.2.cloned.1.call-update) | async-done | bytes 4194320 | tf_op jit(solution)/shard_map/all_gather | solution.py:275
  93.7 0.9 slice.56
  94.6 0.7 collective-permute-start.10
  95.2 0.7 collective-permute-start.11
  96.0 0.6 stack.55.at_ref._
  96.7 9.4 %shard_map.64.product_ref = f32[512,512]{1,0:T(8,128)} custom-call(s32[8]{0:T(128)} %stack.55.at_ref._, bf16[512,4096]{1,0:T(8,128)(2,1)} %all-gather.2.cloned.1.call-done.refs_0_, bf16[2,512,512]{2,1,0:T(8,128)(2,1)} %copy-done.7, bf16[2,512,512]{2,1,0:T(8,128)(2,1)} %copy-done.8, bf16[2,512,512]{2,1,0:T(8,128)(2,1)} %copy-done.9, ...), custom_call_target="tpu_custom_call" | custom-call | flops 1 | bytes 1 | tf_op jit(solution)/shard_map/pallas_call | solution.py:124
  106.1 0.7 broadcast_select_fusion.refs_0_
  106.8 4.2 %collective-permute-done.8.refs_2_ = bf16[2,512,512]{2,1,0:T(8,128)(2,1)S(1)} collective-permute-done((bf16[2,512,512]{2,1,0:T(8,128)(2,1)S(1)}, bf16[2,512,512]{2,1,0:T(8,128)(2,1)S(1)}, u32[]{:S(2)}, u32[]{:S(2)}) %collective-permute-start.8) | collective-permute-done | bytes 1048608 | tf_op jit(solution)/shard_map/ppermute | solution.py:224
  111.0 1.1 collective-permute-start.12
  112.1 0.8 slice_bitcast_fusion.1
  112.9 1.8 collective-permute-start.13
  114.7 0.8 slice_bitcast_fusion
  115.5 2.0 collective-permute-start.17
  118.2 4.0 %shard_map.65.refs_2_ = f32[512,512]{1,0:T(8,128)S(1)} custom-call(s32[8]{0:T(128)S(1)} %copy-done.3, bf16[512,4096]{1,0:T(8,128)(2,1)} %all-gather.2.cloned.1.call-done.refs_0_, bf16[2,512,512]{2,1,0:T(8,128)(2,1)S(1)} %pad_maximum_fusion.refs_1_, bf16[2,512,512]{2,1,0:T(8,128)(2,1)S(1)} %collective-permute-done.8.refs_2_, ...), custom_call_target="tpu_custom_call" | custom-call | flops 1 | bytes 1 | tf_op jit(solution)/shard_map/pallas_call | solution.py:68
  122.2 9.8 %shard_map.66 = (f32[16,512]{1,0:T(8,128)}, f32[512,512]{1,0:T(8,128)}) custom-call(s32[8]{0:T(128)} %stack.55.at_ref._, bf16[16,4096]{1,0:T(8,128)(2,1)} %broadcast_select_fusion.refs_0_, bf16[512,4096]{1,0:T(8,128)(2,1)} %collective-permute-done.12.refs_1_.refs_0_, bf16[2,512,512]{2,1,0:T(8,128)(2,1)} %copy-done.7, bf16[2,512,512]{2,1,0:T(8,128)(2,1)} %copy-done.8, ...), custom_call_target="tpu_custom_call" | custom-call | flops 1 | bytes 1 | tf_op jit(solution)/shard_map/pallas_call | solution.py:124
  132.0 0.9 broadcast_select_fusion.1
  132.9 2.0 shard_map.67.refs_1_
  134.9 2.0 shard_map.68.refs_1_
  137.0 4.2 %shard_map.70.refs_2_ = f32[512,512]{1,0:T(8,128)S(1)} custom-call(s32[8]{0:T(128)S(1)} %copy-done.4, bf16[512,4096]{1,0:T(8,128)(2,1)} %collective-permute-done.12.refs_1_.refs_0_, bf16[2,512,512]{2,1,0:T(8,128)(2,1)S(1)} %pad_maximum_fusion.refs_1_, bf16[2,512,512]{2,1,0:T(8,128)(2,1)S(1)} %collective-permute-done.8.refs_2_, ...), custom_call_target="tpu_custom_call" | custom-call | flops 1 | bytes 1 | tf_op jit(solution)/shard_map/pallas_call | solution.py:68
  141.2 3.2 %shard_map.71.refs_2_ = bf16[512,512]{1,0:T(8,128)(2,1)S(1)} custom-call(s32[2]{0:T(128)S(1)} %pad_add_fusion.at_ref, bf16[512,4096]{1,0:T(8,128)(2,1)} %collective-permute-done.12.refs_1_.refs_0_, f32[512,512]{1,0:T(8,128)S(1)} %shard_map.68.refs_1_, f32[512,512]{1,0:T(8,128)S(1)} %shard_map.70.refs_2_, bf16[512,512]{1,0:T(8,128)(2,1)} %collective-permute-done.13.refs_3_, ...), custom_call_target="tpu_custom_call" | custom-call | flops 1 | bytes 1 | tf_op jit(solution)/shard_map/pallas_call | solution.py:68
  144.5 3.2 %shard_map.69.refs_0_ = bf16[512,512]{1,0:T(8,128)(2,1)S(1)} custom-call(s32[2]{0:T(128)S(1)} %pad_add_fusion.at_ref, bf16[512,4096]{1,0:T(8,128)(2,1)} %all-gather.2.cloned.1.call-done.refs_0_, f32[512,512]{1,0:T(8,128)S(1)} %shard_map.67.refs_1_, f32[512,512]{1,0:T(8,128)S(1)} %shard_map.65.refs_2_, bf16[512,512]{1,0:T(8,128)(2,1)} %collective-permute-done.13.refs_3_, ...), custom_call_target="tpu_custom_call" | custom-call | flops 1 | bytes 1 | tf_op jit(solution)/shard_map/pallas_call | solution.py:68
  147.7 0.6 collective-permute-start.16
  148.3 3.5 %collective-permute-done.17.refs_5_ = bf16[1024,512]{1,0:T(8,128)(2,1)} collective-permute-done((bf16[1024,512]{1,0:T(8,128)(2,1)}, bf16[1024,512]{1,0:T(8,128)(2,1)}, u32[]{:S(2)}, u32[]{:S(2)}) %collective-permute-start.17) | collective-permute-done | bytes 1048608 | tf_op jit(solution)/shard_map/ppermute | solution.py:224
  151.9 7.0 %shard_map.72 = bf16[1024,1536]{1,0:T(8,128)(2,1)} custom-call(s32[2]{0:T(128)S(1)} %pad_add_fusion.1.at_ref, bf16[512,512]{1,0:T(8,128)(2,1)S(1)} %shard_map.69.refs_0_, bf16[512,512]{1,0:T(8,128)(2,1)S(1)} %collective-permute-done.15.refs_1_, bf16[512,512]{1,0:T(8,128)(2,1)S(1)} %shard_map.71.refs_2_, ...), custom_call_target="tpu_custom_call" | custom-call | flops 1 | bytes 1 | tf_op jit(solution)/shard_map/pallas_call | solution.py:68
  159.0 1.1 slice.81
  160.4 1.1 slice.82
  161.5 1.5 collective-permute-start.21
  163.0 9.8 %collective-permute-done.20.refs_4_ = bf16[512,512]{1,0:T(8,128)(2,1)S(1)} collective-permute-done((bf16[512,512]{1,0:T(8,128)(2,1)S(1)}, bf16[512,512]{1,0:T(8,128)(2,1)S(1)}, u32[]{:S(2)}, u32[]{:S(2)}) %collective-permute-start.20) | collective-permute-done | bytes 524320 | tf_op jit(solution)/shard_map/ppermute | solution.py:224
  172.8 2.0 collective-permute-done.21.refs_5_
  174.8 1.9 shard_map.73
  176.7 3.5 %collective-permute-start.22 = (bf16[256,512]{1,0:T(8,128)(2,1)S(1)}, bf16[256,512]{1,0:T(8,128)(2,1)S(1)}, u32[]{:S(2)}, u32[]{:S(2)}) collective-permute-start(bf16[256,512]{1,0:T(8,128)(2,1)S(1)} %get-tuple-element.84), channel_id=1, source_target_pairs={{0,1},{1,2},{2,3},{4,5},{5,6},{6,7},{8,9},{9,10},{10,11},{12,13},{... | collective-permute-start | bytes 786440 | tf_op jit(solution)/shard_map/ppermute | solution.py:359
  180.2 1.3 collective-permute-start.25
  181.5 10.2 %collective-permute-done.22 = bf16[256,512]{1,0:T(8,128)(2,1)S(1)} collective-permute-done((bf16[256,512]{1,0:T(8,128)(2,1)S(1)}, bf16[256,512]{1,0:T(8,128)(2,1)S(1)}, u32[]{:S(2)}, u32[]{:S(2)}) %collective-permute-start.22) | collective-permute-done | bytes 262176 | tf_op jit(solution)/shard_map/ppermute | solution.py:359
  191.7 10.8 %collective-permute-done.25 = bf16[256,512]{1,0:T(8,128)(2,1)S(1)} collective-permute-done((bf16[256,512]{1,0:T(8,128)(2,1)S(1)}, bf16[256,512]{1,0:T(8,128)(2,1)S(1)}, u32[]{:S(2)}, u32[]{:S(2)}) %collective-permute-start.25) | collective-permute-done | bytes 262176 | tf_op jit(solution)/shard_map/ppermute | solution.py:360
  202.6 1.3 collective-permute-start.26
  203.9 4.6 %collective-permute-start.23 = (bf16[256,512]{1,0:T(8,128)(2,1)S(1)}, bf16[256,512]{1,0:T(8,128)(2,1)S(1)}, u32[]{:S(2)}, u32[]{:S(2)}) collective-permute-start(bf16[256,512]{1,0:T(8,128)(2,1)S(1)} %get-tuple-element.99), channel_id=1, source_target_pairs={{0,1},{1,2},{2,3},{4,5},{5,6},{6,7},{8,9},{9,10},{10,11},{12,13},{... | collective-permute-start | bytes 786440 | tf_op jit(solution)/shard_map/ppermute | solution.py:359
  208.5 15.2 %collective-permute-done.26 = bf16[256,512]{1,0:T(8,128)(2,1)S(1)} collective-permute-done((bf16[256,512]{1,0:T(8,128)(2,1)S(1)}, bf16[256,512]{1,0:T(8,128)(2,1)S(1)}, u32[]{:S(2)}, u32[]{:S(2)}) %collective-permute-start.26) | collective-permute-done | bytes 262176 | tf_op jit(solution)/shard_map/ppermute | solution.py:360
  223.8 1.3 collective-permute-start.27
  225.1 4.6 %collective-permute-start.24 = (bf16[256,512]{1,0:T(8,128)(2,1)S(1)}, bf16[256,512]{1,0:T(8,128)(2,1)S(1)}, u32[]{:S(2)}, u32[]{:S(2)}) collective-permute-start(bf16[256,512]{1,0:T(8,128)(2,1)S(1)} %add_convert_fusion.1), channel_id=1, source_target_pairs={{0,1},{1,2},{2,3},{4,5},{5,6},{6,7},{8,9},{9,10},{10,11},{12,13},{... | collective-permute-start | bytes 786440 | tf_op jit(solution)/shard_map/ppermute | solution.py:359
  229.7 3.8 %reduce-scatter.2.cloned.1.call-done = bf16[256,1536]{1,0:T(8,128)(2,1)} async-done(((bf16[1024,1536]{1,0:T(8,128)(2,1)}), bf16[256,1536]{1,0:T(8,128)(2,1)}) %reduce-scatter.2.cloned.1.call-update) | async-done | bytes 786448 | tf_op jit(solution)/shard_map/reduce_scatter | solution.py:368
  233.5 1.2 fusion.26
  235.5 1.2 collective-permute-done.28
  237.0 0.9 copy-done.6
  238.0 0.7 copy-done.14
  239.2 1.0 copy-done.16
  240.2 0.9 fusion.21
  (81 shorter events, 4.6 us)
Async XLA Ops:
  6.5 111.3 %copy-start = (f32[7,64]{1,0:T(8,128)S(1)}, f32[7,64]{1,0:T(8,128)}, u32[]{:S(2)}) copy-start(f32[7,64]{1,0:T(8,128)} %param.9) | copy-start | bytes 5380
  6.5 87.1 %all-gather.2.cloned.1.call-start = ((), (), s32[]{:S(2)}) async-start(), calls=%async_computation.1 | async-start | bytes 5242880 | tf_op jit(solution)/shard_map/all_gather | solution.py:275
  6.5 1.9 copy-start.5
  6.5 2.2 copy-start.17
  8.3 4.8 %copy-start.7 = (bf16[2,512,512]{2,1,0:T(8,128)(2,1)}, bf16[2,512,512]{2,1,0:T(8,128)(2,1)S(1)}, u32[]{:S(2)}) copy-start(bf16[2,512,512]{2,1,0:T(8,128)(2,1)S(1)} %get-tuple-element.55.refs_1_.refs_2_) | copy-start | bytes 3145732
  10.0 223.5 %reduce-scatter.2.cloned.1.call-start = ((), (), s32[]{:S(2)}) async-start(), calls=%async_computation.2 | async-start | bytes 3932160 | tf_op jit(solution)/shard_map/reduce_scatter | solution.py:368
  10.1 4.6 %collective-permute-start = (bf16[2,512,512]{2,1,0:T(8,128)(2,1)S(1)}, bf16[2,512,512]{2,1,0:T(8,128)(2,1)S(1)}, u32[]{:S(2)}, u32[]{:S(2)}) collective-permute-start(bf16[2,512,512]{2,1,0:T(8,128)(2,1)S(1)} %get-tuple-element.88), channel_id=1, source_target_pairs={{0,4},{4,0},{8,12},{12,8},{16,20},{20,16},{24,28},{28,24},{1,5},{5... | collective-permute-start | bytes 3145736 | tf_op jit(solution)/shard_map/ppermute | solution.py:227
  10.6 26.6 %collective-permute-start.1 = (bf16[2,512,512]{2,1,0:T(8,128)(2,1)S(1)}, bf16[2,512,512]{2,1,0:T(8,128)(2,1)S(1)}, u32[]{:S(2)}, u32[]{:S(2)}) collective-permute-start(bf16[2,512,512]{2,1,0:T(8,128)(2,1)S(1)} %get-tuple-element.55.refs_1_.refs_2_), channel_id=1, source_target_pairs={{8,0},{12,4},{0,8},{4,12},{24,16},{28,20},{16,24},{20,28},{9,1},{1... | collective-permute-start | bytes 3145736 | tf_op jit(solution)/shard_map/ppermute | solution.py:224
  13.2 26.0 %collective-permute-start.3 = (bf16[2,512,512]{2,1,0:T(8,128)(2,1)S(1)}, bf16[2,512,512]{2,1,0:T(8,128)(2,1)S(1)}, u32[]{:S(2)}, u32[]{:S(2)}) collective-permute-start(bf16[2,512,512]{2,1,0:T(8,128)(2,1)S(1)} %get-tuple-element.55.refs_1_.refs_2_), channel_id=1, source_target_pairs={{16,0},{20,4},{24,8},{28,12},{0,16},{4,20},{8,24},{12,28},{17,1},{... | collective-permute-start | bytes 3145736 | tf_op jit(solution)/shard_map/ppermute | solution.py:224
  14.7 5.9 %copy-start.8 = (bf16[2,512,512]{2,1,0:T(8,128)(2,1)}, bf16[2,512,512]{2,1,0:T(8,128)(2,1)S(1)}, u32[]{:S(2)}) copy-start(bf16[2,512,512]{2,1,0:T(8,128)(2,1)S(1)} %collective-permute-done.refs_2_.refs_3_) | copy-start | bytes 3145732
  14.7 44.7 %collective-permute-start.2 = (bf16[2,512,512]{2,1,0:T(8,128)(2,1)S(1)}, bf16[2,512,512]{2,1,0:T(8,128)(2,1)S(1)}, u32[]{:S(2)}, u32[]{:S(2)}) collective-permute-start(bf16[2,512,512]{2,1,0:T(8,128)(2,1)S(1)} %collective-permute-done.refs_2_.refs_3_), channel_id=1, source_target_pairs={{8,0},{12,4},{0,8},{4,12},{24,16},{28,20},{16,24},{20,28},{9,1},{1... | collective-permute-start | bytes 3145736 | tf_op jit(solution)/shard_map/ppermute | solution.py:224
  15.8 45.1 %collective-permute-start.4 = (bf16[2,512,512]{2,1,0:T(8,128)(2,1)S(1)}, bf16[2,512,512]{2,1,0:T(8,128)(2,1)S(1)}, u32[]{:S(2)}, u32[]{:S(2)}) collective-permute-start(bf16[2,512,512]{2,1,0:T(8,128)(2,1)S(1)} %collective-permute-done.refs_2_.refs_3_), channel_id=1, source_target_pairs={{16,0},{20,4},{24,8},{28,12},{0,16},{4,20},{8,24},{12,28},{17,1},{... | collective-permute-start | bytes 3145736 | tf_op jit(solution)/shard_map/ppermute | solution.py:224
  18.5 2.0 collective-permute-start.5
  37.2 25.8 %copy-start.9 = (bf16[2,512,512]{2,1,0:T(8,128)(2,1)}, bf16[2,512,512]{2,1,0:T(8,128)(2,1)S(1)}, u32[]{:S(2)}) copy-start(bf16[2,512,512]{2,1,0:T(8,128)(2,1)S(1)} %collective-permute-done.1.refs_3_.refs_4_) | copy-start | bytes 3145732
  39.2 47.8 %copy-start.10 = (bf16[2,512,512]{2,1,0:T(8,128)(2,1)}, bf16[2,512,512]{2,1,0:T(8,128)(2,1)S(1)}, u32[]{:S(2)}) copy-start(bf16[2,512,512]{2,1,0:T(8,128)(2,1)S(1)} %collective-permute-done.3.refs_5_.refs_6_) | copy-start | bytes 3145732
  59.4 27.6 %copy-start.11 = (bf16[2,512,512]{2,1,0:T(8,128)(2,1)}, bf16[2,512,512]{2,1,0:T(8,128)(2,1)S(1)}, u32[]{:S(2)}) copy-start(bf16[2,512,512]{2,1,0:T(8,128)(2,1)S(1)} %collective-permute-done.2.refs_4_.refs_5_) | copy-start | bytes 3145732
  60.9 26.1 %copy-start.12 = (bf16[2,512,512]{2,1,0:T(8,128)(2,1)}, bf16[2,512,512]{2,1,0:T(8,128)(2,1)S(1)}, u32[]{:S(2)}) copy-start(bf16[2,512,512]{2,1,0:T(8,128)(2,1)S(1)} %collective-permute-done.4.refs_6_.refs_7_) | copy-start | bytes 3145732
  60.9 26.1 %collective-permute-start.6 = (bf16[2,512,512]{2,1,0:T(8,128)(2,1)S(1)}, bf16[2,512,512]{2,1,0:T(8,128)(2,1)S(1)}, u32[]{:S(2)}, u32[]{:S(2)}) collective-permute-start(bf16[2,512,512]{2,1,0:T(8,128)(2,1)S(1)} %collective-permute-done.1.refs_3_.refs_4_), channel_id=1, source_target_pairs={{16,0},{20,4},{24,8},{28,12},{0,16},{4,20},{8,24},{12,28},{17,1},{... | collective-permute-start | bytes 3145736 | tf_op jit(solution)/shard_map/ppermute | solution.py:224
  62.4 26.2 %collective-permute-start.7 = (bf16[2,512,512]{2,1,0:T(8,128)(2,1)S(1)}, bf16[2,512,512]{2,1,0:T(8,128)(2,1)}, u32[]{:S(2)}, u32[]{:S(2)}) collective-permute-start(bf16[2,512,512]{2,1,0:T(8,128)(2,1)S(1)} %collective-permute-done.4.refs_6_.refs_7_), channel_id=1, source_target_pairs={{8,0},{12,4},{0,8},{4,12},{24,16},{28,20},{16,24},{20,28},{9,1},{1... | collective-permute-start | bytes 3145736 | tf_op jit(solution)/shard_map/ppermute | solution.py:224
  62.9 48.0 %collective-permute-start.8 = (bf16[2,512,512]{2,1,0:T(8,128)(2,1)S(1)}, bf16[2,512,512]{2,1,0:T(8,128)(2,1)S(1)}, u32[]{:S(2)}, u32[]{:S(2)}) collective-permute-start(bf16[2,512,512]{2,1,0:T(8,128)(2,1)S(1)} %pad_maximum_fusion.refs_1_), channel_id=1, source_target_pairs={{8,0},{12,4},{0,8},{4,12},{24,16},{28,20},{16,24},{20,28},{9,1},{1... | collective-permute-start | bytes 3145736 | tf_op jit(solution)/shard_map/ppermute | solution.py:224
  64.4 46.5 %collective-permute-start.9 = (bf16[2,512,512]{2,1,0:T(8,128)(2,1)S(1)}, bf16[2,512,512]{2,1,0:T(8,128)(2,1)S(1)}, u32[]{:S(2)}, u32[]{:S(2)}) collective-permute-start(bf16[2,512,512]{2,1,0:T(8,128)(2,1)S(1)} %pad_maximum_fusion.refs_1_), channel_id=1, source_target_pairs={{16,0},{20,4},{24,8},{28,12},{0,16},{4,20},{8,24},{12,28},{17,1},{... | collective-permute-start | bytes 3145736 | tf_op jit(solution)/shard_map/ppermute | solution.py:224
  87.0 1.0 copy-start.13
  94.6 11.6 %collective-permute-start.10 = (bf16[16,4096]{1,0:T(8,128)(2,1)S(1)}, bf16[16,4096]{1,0:T(8,128)(2,1)S(1)}, u32[]{:S(2)}, u32[]{:S(2)}) collective-permute-start(bf16[16,4096]{1,0:T(8,128)(2,1)S(1)} %slice.56), channel_id=1, source_target_pairs={{4,8},{12,16},{20,24},{5,9},{13,17},{21,25},{6,10},{14,18},{22,26}... | collective-permute-start | bytes 393224 | tf_op jit(solution)/shard_map/ppermute | solution.py:299
  95.2 10.9 %collective-permute-start.11 = (bf16[16,4096]{1,0:T(8,128)(2,1)S(1)}, bf16[16,4096]{1,0:T(8,128)(2,1)S(1)}, u32[]{:S(2)}, u32[]{:S(2)}) collective-permute-start(bf16[16,4096]{1,0:T(8,128)(2,1)S(1)} %slice.56), channel_id=1, source_target_pairs={{4,12},{12,20},{20,28},{5,13},{13,21},{21,29},{6,14},{14,22},{22,3... | collective-permute-start | bytes 393224 | tf_op jit(solution)/shard_map/ppermute | solution.py:299
  106.1 12.1 %copy-start.3 = (s32[8]{0:T(128)S(1)}, s32[8]{0:T(128)}, u32[]{:S(2)}) copy-start(s32[8]{0:T(128)} %stack.55.at_ref._) | copy-start | bytes 100
  111.0 11.2 %collective-permute-start.12 = (bf16[512,4096]{1,0:T(8,128)(2,1)}, bf16[512,4096]{1,0:T(8,128)(2,1)}, u32[]{:S(2)}, u32[]{:S(2)}) collective-permute-start(bf16[512,4096]{1,0:T(8,128)(2,1)} %all-gather.2.cloned.1.call-done.refs_0_), channel_id=1, source_target_pairs={{0,4},{4,0},{8,12},{12,8},{16,20},{20,16},{24,28},{28,24},{1,5},{5... | collective-permute-start | bytes 12582920 | tf_op jit(solution)/shard_map/ppermute | solution.py:227
  112.9 28.2 %collective-permute-start.13 = (bf16[512,512]{1,0:T(8,128)(2,1)}, bf16[512,512]{1,0:T(8,128)(2,1)}, u32[]{:S(2)}, u32[]{:S(2)}) collective-permute-start(bf16[512,512]{1,0:T(8,128)(2,1)} %slice_bitcast_fusion.1), channel_id=1, source_target_pairs={{16,0},{20,4},{24,8},{28,12},{0,16},{4,20},{8,24},{12,28},{17,1},{... | collective-permute-start | bytes 1572872 | tf_op jit(solution)/shard_map/ppermute | solution.py:224
  115.5 25.7 %collective-permute-start.14 = (bf16[512,512]{1,0:T(8,128)(2,1)}, bf16[512,512]{1,0:T(8,128)(2,1)}, u32[]{:S(2)}, u32[]{:S(2)}) collective-permute-start(bf16[512,512]{1,0:T(8,128)(2,1)} %slice_bitcast_fusion), channel_id=1, source_target_pairs={{8,0},{12,4},{0,8},{4,12},{24,16},{28,20},{16,24},{20,28},{9,1},{1... | collective-permute-start | bytes 1572872 | tf_op jit(solution)/shard_map/ppermute | solution.py:224
  115.5 36.3 %collective-permute-start.17 = (bf16[1024,512]{1,0:T(8,128)(2,1)}, bf16[1024,512]{1,0:T(8,128)(2,1)}, u32[]{:S(2)}, u32[]{:S(2)}) collective-permute-start(bf16[1024,512]{1,0:T(8,128)(2,1)} %refs_4_.1), channel_id=1, source_target_pairs={{8,0},{12,4},{0,8},{4,12},{24,16},{28,20},{16,24},{20,28},{9,1},{1... | collective-permute-start | bytes 3145736 | tf_op jit(solution)/shard_map/ppermute | solution.py:224
  117.6 34.3 %collective-permute-start.18 = (bf16[1024,512]{1,0:T(8,128)(2,1)}, bf16[1024,512]{1,0:T(8,128)(2,1)}, u32[]{:S(2)}, u32[]{:S(2)}) collective-permute-start(bf16[1024,512]{1,0:T(8,128)(2,1)} %refs_4_.1), channel_id=1, source_target_pairs={{16,0},{20,4},{24,8},{28,12},{0,16},{4,20},{8,24},{12,28},{17,1},{... | collective-permute-start | bytes 3145736 | tf_op jit(solution)/shard_map/ppermute | solution.py:224
  122.2 9.8 %copy-start.1 = (f32[512,512]{1,0:T(8,128)S(1)}, f32[512,512]{1,0:T(8,128)}, u32[]{:S(2)}) copy-start(f32[512,512]{1,0:T(8,128)} %shard_map.64.product_ref) | copy-start | bytes 3145732
  122.2 10.7 %copy-start.4 = (s32[8]{0:T(128)S(1)}, s32[8]{0:T(128)}, u32[]{:S(2)}) copy-start(s32[8]{0:T(128)} %stack.55.at_ref._) | copy-start | bytes 100
  132.0 2.9 %copy-start.2 = (f32[512,512]{1,0:T(8,128)S(1)}, f32[512,512]{1,0:T(8,128)}, u32[]{:S(2)}) copy-start(f32[512,512]{1,0:T(8,128)} %get-tuple-element.70.product_ref) | copy-start | bytes 3145732
  144.4 7.5 %collective-permute-start.15 = (bf16[512,512]{1,0:T(8,128)(2,1)S(1)}, bf16[512,512]{1,0:T(8,128)(2,1)S(1)}, u32[]{:S(2)}, u32[]{:S(2)}) collective-permute-start(bf16[512,512]{1,0:T(8,128)(2,1)S(1)} %shard_map.71.refs_2_), channel_id=1, source_target_pairs={{0,4},{4,0},{8,12},{12,8},{16,20},{20,16},{24,28},{28,24},{1,5},{5... | collective-permute-start | bytes 1572872 | tf_op jit(solution)/shard_map/ppermute | solution.py:227
  147.7 4.2 %collective-permute-start.16 = (bf16[512,512]{1,0:T(8,128)(2,1)S(1)}, bf16[512,512]{1,0:T(8,128)(2,1)S(1)}, u32[]{:S(2)}, u32[]{:S(2)}) collective-permute-start(bf16[512,512]{1,0:T(8,128)(2,1)S(1)} %shard_map.69.refs_0_), channel_id=1, source_target_pairs={{0,4},{4,0},{8,12},{12,8},{16,20},{20,16},{24,28},{28,24},{1,5},{5... | collective-permute-start | bytes 1572872 | tf_op jit(solution)/shard_map/ppermute | solution.py:227
  160.0 12.7 %collective-permute-start.20 = (bf16[512,512]{1,0:T(8,128)(2,1)S(1)}, bf16[512,512]{1,0:T(8,128)(2,1)S(1)}, u32[]{:S(2)}, u32[]{:S(2)}) collective-permute-start(bf16[512,512]{1,0:T(8,128)(2,1)S(1)} %slice.81), channel_id=1, source_target_pairs={{16,0},{20,4},{24,8},{28,12},{0,16},{4,20},{8,24},{12,28},{17,1},{... | collective-permute-start | bytes 1572872 | tf_op jit(solution)/shard_map/ppermute | solution.py:224
  161.5 13.4 %collective-permute-start.21 = (bf16[512,512]{1,0:T(8,128)(2,1)S(1)}, bf16[512,512]{1,0:T(8,128)(2,1)S(1)}, u32[]{:S(2)}, u32[]{:S(2)}) collective-permute-start(bf16[512,512]{1,0:T(8,128)(2,1)S(1)} %slice.82), channel_id=1, source_target_pairs={{8,0},{12,4},{0,8},{4,12},{24,16},{28,20},{16,24},{20,28},{9,1},{1... | collective-permute-start | bytes 1572872 | tf_op jit(solution)/shard_map/ppermute | solution.py:224
  176.7 15.0 %collective-permute-start.22 = (bf16[256,512]{1,0:T(8,128)(2,1)S(1)}, bf16[256,512]{1,0:T(8,128)(2,1)S(1)}, u32[]{:S(2)}, u32[]{:S(2)}) collective-permute-start(bf16[256,512]{1,0:T(8,128)(2,1)S(1)} %get-tuple-element.84), channel_id=1, source_target_pairs={{0,1},{1,2},{2,3},{4,5},{5,6},{6,7},{8,9},{9,10},{10,11},{12,13},{... | collective-permute-start | bytes 786440 | tf_op jit(solution)/shard_map/ppermute | solution.py:359
  180.2 22.3 %collective-permute-start.25 = (bf16[256,512]{1,0:T(8,128)(2,1)S(1)}, bf16[256,512]{1,0:T(8,128)(2,1)S(1)}, u32[]{:S(2)}, u32[]{:S(2)}) collective-permute-start(bf16[256,512]{1,0:T(8,128)(2,1)S(1)} %get-tuple-element.82), channel_id=1, source_target_pairs={{1,0},{2,1},{3,2},{5,4},{6,5},{7,6},{9,8},{10,9},{11,10},{13,12},{... | collective-permute-start | bytes 786440 | tf_op jit(solution)/shard_map/ppermute | solution.py:360
  202.6 21.1 %collective-permute-start.26 = (bf16[256,512]{1,0:T(8,128)(2,1)S(1)}, bf16[256,512]{1,0:T(8,128)(2,1)S(1)}, u32[]{:S(2)}, u32[]{:S(2)}) collective-permute-start(bf16[256,512]{1,0:T(8,128)(2,1)S(1)} %get-tuple-element.100), channel_id=1, source_target_pairs={{1,0},{2,1},{3,2},{5,4},{6,5},{7,6},{9,8},{10,9},{11,10},{13,12},{... | collective-permute-start | bytes 786440 | tf_op jit(solution)/shard_map/ppermute | solution.py:360
  203.9 21.1 %collective-permute-start.23 = (bf16[256,512]{1,0:T(8,128)(2,1)S(1)}, bf16[256,512]{1,0:T(8,128)(2,1)S(1)}, u32[]{:S(2)}, u32[]{:S(2)}) collective-permute-start(bf16[256,512]{1,0:T(8,128)(2,1)S(1)} %get-tuple-element.99), channel_id=1, source_target_pairs={{0,1},{1,2},{2,3},{4,5},{5,6},{6,7},{8,9},{9,10},{10,11},{12,13},{... | collective-permute-start | bytes 786440 | tf_op jit(solution)/shard_map/ppermute | solution.py:359
  223.8 11.1 %collective-permute-start.27 = (bf16[256,512]{1,0:T(8,128)(2,1)S(1)}, bf16[256,512]{1,0:T(8,128)(2,1)S(1)}, u32[]{:S(2)}, u32[]{:S(2)}) collective-permute-start(bf16[256,512]{1,0:T(8,128)(2,1)S(1)} %add_convert_fusion), channel_id=1, source_target_pairs={{1,0},{2,1},{3,2},{5,4},{6,5},{7,6},{9,8},{10,9},{11,10},{13,12},{... | collective-permute-start | bytes 786440 | tf_op jit(solution)/shard_map/ppermute | solution.py:360
  225.1 9.7 %collective-permute-start.24 = (bf16[256,512]{1,0:T(8,128)(2,1)S(1)}, bf16[256,512]{1,0:T(8,128)(2,1)S(1)}, u32[]{:S(2)}, u32[]{:S(2)}) collective-permute-start(bf16[256,512]{1,0:T(8,128)(2,1)S(1)} %add_convert_fusion.1), channel_id=1, source_target_pairs={{0,1},{1,2},{2,3},{4,5},{5,6},{6,7},{8,9},{9,10},{10,11},{12,13},{... | collective-permute-start | bytes 786440 | tf_op jit(solution)/shard_map/ppermute | solution.py:359
  234.7 2.1 collective-permute-start.19
  234.9 2.0 copy-start.15
  235.0 1.7 collective-permute-start.28
  236.7 1.2 copy-start.6
  236.8 1.9 copy-start.14
  238.7 1.5 slice-start
  239.2 1.0 copy-start.16
Sparse Core Ops, SparseCore 0:
  10.2 83.4 all-gather.1
  159.1 74.4 reduce-scatter.1

commit v12 on v11

--- a/solution.py
+++ b/solution.py
@@ -198,6 +198,58 @@
     return [range(len(parts)) for parts in blocks]
 
 
+def near_kernel(n_tp, at_ref, *refs):
+    gates, refs = refs[:4], refs[4:]
+    count = (len(refs) - 4) // 2
+    given, (out_ref, held, *refs) = refs[:count], refs[count:]
+    weights, (ready, sems, out_sems) = refs[:count], refs[count:]
+    copies = [
+        pltpu.make_async_copy(source, target, sems.at[index])
+        for index, (source, target) in enumerate(zip(given, weights))
+    ]
+    for copy in copies:
+        copy.start()
+    half = gates[0].shape[1]
+    rows = gates[0].shape[0] // n_tp
+    for slot in range(n_tp):
+        for index, gate in enumerate(gates):
+            side, whose = index % 2, index // 2
+            place = slice((2 * slot + whose) * rows, (2 * slot + whose + 1) * rows)
+            column = (at_ref[0] if side == 0 else 1 - at_ref[0]) * half
+            columns = pl.ds(pl.multiple_of(column, half), half)
+            held[place, columns] = gate[slot * rows : (slot + 1) * rows]
+    wide = weights[0].shape[1]
+    leaving = []
+    for index, weight in enumerate(weights):
+        copies[index].wait()
+        at = slice(index * wide, (index + 1) * wide)
+        ready[:, at] = dot(held[...], weight[...]).astype(BF16)
+        leaving.append(pltpu.make_async_copy(ready.at[:, at], out_ref.at[:, at], out_sems.at[index]))
+        leaving[-1].start()
+    for copy in leaving:
+        copy.wait()
+
+
+def near_terms(n_tp, place, gates, weights):
+    length, half = gates[0].shape
+    shape = (2 * length, len(weights) * weights[0].shape[1])
+    anywhere = pl.BlockSpec(memory_space=pl.ANY)
+    return pl.pallas_call(
+        functools.partial(near_kernel, n_tp),
+        out_shape=jax.ShapeDtypeStruct(shape, BF16),
+        in_specs=[pl.BlockSpec(memory_space=pltpu.SMEM)]
+        + [WHOLE] * 4
+        + [anywhere] * len(weights),
+        out_specs=anywhere,
+        scratch_shapes=[pltpu.VMEM((2 * length, 2 * half), BF16)]
+        + [pltpu.VMEM(weight.shape, BF16) for weight in weights]
+        + [pltpu.VMEM(shape, BF16)]
+        + [pltpu.SemaphoreType.DMA((len(weights),))] * 2,
+        compiler_params=pltpu.CompilerParams(vmem_limit_bytes=24 << 20),
+        cost_estimate=pl.CostEstimate(flops=1, bytes_accessed=1, transcendentals=0),
+    )(place, *gates, *weights)
+
+
 def on_device(tokens, norm_gain, in_weight, filters, out_weight, keep_mask):
     n_seq, n_tp = lax.axis_size("seq"), lax.axis_size("tp")
     chips = n_seq // 2
@@ -363,7 +415,7 @@
 
     near = {(0, 0): (out_weight,)}
     near.update({key: (block,) for key, block in (*o_x.items(), *o_y.items())})
-    found = terms(n_tp, here_at, gates, list(near.values()), False)
+    found = near_terms(n_tp, here_at, gates, [block for (block,) in near.values()])
     gates, found = lax.optimization_barrier((gates, found))
     near_sum = lax.psum_scatter(found, "tp", scatter_dimension=0, tiled=True)
     far_sum = chained(terms(n_tp, here_at, gates, list(o_rest.values()), True))

time: 249 us -> 248 us (level)
    pallas_call x8 -> x7, Pallas kernels: 27.6 us -> 20.6 us  [call(): pl.pallas_call(kernel, out_shape=out, in_specs=[pl.BlockSpec(memory_space...]
    pallas_call x0 -> x1, Pallas kernels: none -> 6.62 us  [near_terms(): pl.pallas_call(functools.partial(near_kernel, n_tp), out_shape=jax.ShapeD...]
where the time goes in v12:
time: 248 us; the launch traced here: 247 us
  waiting for transfers between devices  131 us (53%)
  Pallas kernels  46.4 us (19%)
  starting transfers between devices  37.5 us (15%)
  between operations  14 us (6%)
  local copies, waits for them, and re-layouts  12.7 us (5%)
  other arithmetic  6.32 us (3%)
    ppermute x14, waiting for transfers between devices, from_chip(): return lax.ppermute(block, 'seq', route)  82.4 us
    ppermute x3, waiting for transfers between devices, chained(): falling = lax.ppermute(send_down, 'tp', down)  26 us
    pallas_call x7, Pallas kernels, call(): pl.pallas_call(kernel, out_shape=out, in_specs=[pl.BlockSpec(memory_space...  20.6 us
    pallas_call x2, Pallas kernels, products(): pl.pallas_call(functools.partial(product_kernel, len(xs), len(pieces)), o...  19.2 us
    ppermute x14, starting transfers between devices, from_chip(): return lax.ppermute(block, 'seq', route)  16.6 us
    ppermute x3, starting transfers between devices, chained(): rising = lax.ppermute(send_up, 'tp', up)  12.6 us
    ppermute x3, waiting for transfers between devices, chained(): rising = lax.ppermute(send_up, 'tp', up)  10.2 us
    pallas_call x1, Pallas kernels, near_terms(): pl.pallas_call(functools.partial(near_kernel, n_tp), out_shape=jax.ShapeD...  6.62 us
  transfers between devices with their start and end apart: 31, of which 17 were waited for; matrix products, arithmetic and copies ran while one was open for 4% of the time, Pallas kernels for 16%

profile of v12, /device:TPU:0, one launch (start us, length us, event | category | flops | bytes accessed | tf_op | source)
XLA Modules:
  0.0 247.4 jit_solution(15430680565730660211)
XLA Ops:
  6.5 1.8 constant_dynamic-slice_fusion.2
  8.7 1.3 fusion.2
  10.6 2.6 %collective-permute-start.1 = (bf16[2,512,512]{2,1,0:T(8,128)(2,1)S(1)}, bf16[2,512,512]{2,1,0:T(8,128)(2,1)S(1)}, u32[]{:S(2)}, u32[]{:S(2)}) collective-permute-start(bf16[2,512,512]{2,1,0:T(8,128)(2,1)S(1)} %get-tuple-element.55.refs_1_.refs_2_), channel_id=1, source_target_pairs={{8,0},{12,4},{0,8},{4,12},{24,16},{28,20},{16,24},{20,28},{9,1},{1... | collective-permute-start | bytes 3145736 | tf_op jit(solution)/shard_map/ppermute | solution.py:276
  13.2 1.5 collective-permute-start.3
  14.7 1.1 collective-permute-start.2
  15.8 1.5 collective-permute-start.4
  17.3 1.3 constant_dynamic-slice_fusion.1
  18.6 1.9 collective-permute-done.5
  20.6 16.5 %collective-permute-done.1.refs_3_.refs_4_ = bf16[2,512,512]{2,1,0:T(8,128)(2,1)S(1)} collective-permute-done((bf16[2,512,512]{2,1,0:T(8,128)(2,1)S(1)}, bf16[2,512,512]{2,1,0:T(8,128)(2,1)S(1)}, u32[]{:S(2)}, u32[]{:S(2)}) %collective-permute-start.1) | collective-permute-done | bytes 1048608 | tf_op jit(solution)/shard_map/ppermute | solution.py:276
  37.2 2.0 collective-permute-done.3.refs_5_.refs_6_
  39.2 20.2 %collective-permute-done.2.refs_4_.refs_5_ = bf16[2,512,512]{2,1,0:T(8,128)(2,1)S(1)} collective-permute-done((bf16[2,512,512]{2,1,0:T(8,128)(2,1)S(1)}, bf16[2,512,512]{2,1,0:T(8,128)(2,1)S(1)}, u32[]{:S(2)}, u32[]{:S(2)}) %collective-permute-start.2) | collective-permute-done | bytes 1048608 | tf_op jit(solution)/shard_map/ppermute | solution.py:276
  59.4 1.5 collective-permute-done.4.refs_6_.refs_7_
  60.9 1.5 collective-permute-start.6
  62.4 0.5 collective-permute-start.7
  62.9 1.5 collective-permute-start.8
  64.9 22.0 %collective-permute-done.6.refs_7_.refs_8_ = bf16[2,512,512]{2,1,0:T(8,128)(2,1)S(1)} collective-permute-done((bf16[2,512,512]{2,1,0:T(8,128)(2,1)S(1)}, bf16[2,512,512]{2,1,0:T(8,128)(2,1)S(1)}, u32[]{:S(2)}, u32[]{:S(2)}) %collective-permute-start.6) | collective-permute-done | bytes 1048608 | tf_op jit(solution)/shard_map/ppermute | solution.py:276
  87.0 1.0 copy-done.13
  88.0 0.6 collective-permute-done.7.refs_8_.refs_9_
  88.6 5.1 %all-gather.2.cloned.1.call-done.refs_0_ = bf16[512,4096]{1,0:T(8,128)(2,1)} async-done(((bf16[128,4096]{1,0:T(8,128)(2,1)}), bf16[512,4096]{1,0:T(8,128)(2,1)}) %all-gather.2.cloned.1.call-update) | async-done | bytes 4194320 | tf_op jit(solution)/shard_map/all_gather | solution.py:327
  93.7 0.9 slice.56
  94.6 0.7 collective-permute-start.10
  95.2 0.7 collective-permute-start.11
  96.0 0.6 stack.55.at_ref._
  96.7 9.4 %shard_map.64.product_ref = f32[512,512]{1,0:T(8,128)} custom-call(s32[8]{0:T(128)} %stack.55.at_ref._, bf16[512,4096]{1,0:T(8,128)(2,1)} %all-gather.2.cloned.1.call-done.refs_0_, bf16[2,512,512]{2,1,0:T(8,128)(2,1)} %copy-done.7, bf16[2,512,512]{2,1,0:T(8,128)(2,1)} %copy-done.8, bf16[2,512,512]{2,1,0:T(8,128)(2,1)} %copy-done.9, ...), custom_call_target="tpu_custom_call" | custom-call | flops 1 | bytes 1 | tf_op jit(solution)/shard_map/pallas_call | solution.py:124
  106.1 0.7 broadcast_select_fusion.refs_0_
  106.8 4.2 %collective-permute-done.8.refs_2_ = bf16[2,512,512]{2,1,0:T(8,128)(2,1)S(1)} collective-permute-done((bf16[2,512,512]{2,1,0:T(8,128)(2,1)S(1)}, bf16[2,512,512]{2,1,0:T(8,128)(2,1)S(1)}, u32[]{:S(2)}, u32[]{:S(2)}) %collective-permute-start.8) | collective-permute-done | bytes 1048608 | tf_op jit(solution)/shard_map/ppermute | solution.py:276
  111.0 1.1 collective-permute-start.12
  112.1 0.8 slice_bitcast_fusion.1
  112.9 1.8 collective-permute-start.13
  114.7 0.8 slice_bitcast_fusion
  115.5 2.0 collective-permute-start.17
  118.2 4.0 %shard_map.65.refs_2_ = f32[512,512]{1,0:T(8,128)S(1)} custom-call(s32[8]{0:T(128)S(1)} %copy-done.3, bf16[512,4096]{1,0:T(8,128)(2,1)} %all-gather.2.cloned.1.call-done.refs_0_, bf16[2,512,512]{2,1,0:T(8,128)(2,1)S(1)} %pad_maximum_fusion.refs_1_, bf16[2,512,512]{2,1,0:T(8,128)(2,1)S(1)} %collective-permute-done.8.refs_2_, ...), custom_call_target="tpu_custom_call" | custom-call | flops 1 | bytes 1 | tf_op jit(solution)/shard_map/pallas_call | solution.py:68
  122.2 9.8 %shard_map.66 = (f32[16,512]{1,0:T(8,128)}, f32[512,512]{1,0:T(8,128)}) custom-call(s32[8]{0:T(128)} %stack.55.at_ref._, bf16[16,4096]{1,0:T(8,128)(2,1)} %broadcast_select_fusion.refs_0_, bf16[512,4096]{1,0:T(8,128)(2,1)} %collective-permute-done.12.refs_1_.refs_0_, bf16[2,512,512]{2,1,0:T(8,128)(2,1)} %copy-done.7, bf16[2,512,512]{2,1,0:T(8,128)(2,1)} %copy-done.8, ...), custom_call_target="tpu_custom_call" | custom-call | flops 1 | bytes 1 | tf_op jit(solution)/shard_map/pallas_call | solution.py:124
  132.0 0.9 broadcast_select_fusion.1
  132.9 2.0 shard_map.67.refs_1_
  134.9 2.0 shard_map.68.refs_1_
  137.0 4.2 %shard_map.70.refs_2_ = f32[512,512]{1,0:T(8,128)S(1)} custom-call(s32[8]{0:T(128)S(1)} %copy-done.4, bf16[512,4096]{1,0:T(8,128)(2,1)} %collective-permute-done.12.refs_1_.refs_0_, bf16[2,512,512]{2,1,0:T(8,128)(2,1)S(1)} %pad_maximum_fusion.refs_1_, bf16[2,512,512]{2,1,0:T(8,128)(2,1)S(1)} %collective-permute-done.8.refs_2_, ...), custom_call_target="tpu_custom_call" | custom-call | flops 1 | bytes 1 | tf_op jit(solution)/shard_map/pallas_call | solution.py:68
  141.2 3.2 %shard_map.71.refs_2_ = bf16[512,512]{1,0:T(8,128)(2,1)S(1)} custom-call(s32[2]{0:T(128)S(1)} %pad_add_fusion.at_ref, bf16[512,4096]{1,0:T(8,128)(2,1)} %collective-permute-done.12.refs_1_.refs_0_, f32[512,512]{1,0:T(8,128)S(1)} %shard_map.68.refs_1_, f32[512,512]{1,0:T(8,128)S(1)} %shard_map.70.refs_2_, bf16[512,512]{1,0:T(8,128)(2,1)} %collective-permute-done.13.refs_3_, ...), custom_call_target="tpu_custom_call" | custom-call | flops 1 | bytes 1 | tf_op jit(solution)/shard_map/pallas_call | solution.py:68
  144.5 3.2 %shard_map.69.refs_0_ = bf16[512,512]{1,0:T(8,128)(2,1)S(1)} custom-call(s32[2]{0:T(128)S(1)} %pad_add_fusion.at_ref, bf16[512,4096]{1,0:T(8,128)(2,1)} %all-gather.2.cloned.1.call-done.refs_0_, f32[512,512]{1,0:T(8,128)S(1)} %shard_map.67.refs_1_, f32[512,512]{1,0:T(8,128)S(1)} %shard_map.65.refs_2_, bf16[512,512]{1,0:T(8,128)(2,1)} %collective-permute-done.13.refs_3_, ...), custom_call_target="tpu_custom_call" | custom-call | flops 1 | bytes 1 | tf_op jit(solution)/shard_map/pallas_call | solution.py:68
  147.7 0.6 collective-permute-start.16
  148.3 3.5 %collective-permute-done.17.refs_5_ = bf16[1024,512]{1,0:T(8,128)(2,1)} collective-permute-done((bf16[1024,512]{1,0:T(8,128)(2,1)}, bf16[1024,512]{1,0:T(8,128)(2,1)}, u32[]{:S(2)}, u32[]{:S(2)}) %collective-permute-start.17) | collective-permute-done | bytes 1048608 | tf_op jit(solution)/shard_map/ppermute | solution.py:276
  151.9 6.6 %shard_map.72 = bf16[1024,1536]{1,0:T(8,128)(2,1)} custom-call(s32[2]{0:T(128)S(1)} %pad_add_fusion.1.at_ref, bf16[512,512]{1,0:T(8,128)(2,1)S(1)} %shard_map.69.refs_0_, bf16[512,512]{1,0:T(8,128)(2,1)S(1)} %collective-permute-done.15.refs_1_, bf16[512,512]{1,0:T(8,128)(2,1)S(1)} %shard_map.71.refs_2_, ...), custom_call_target="tpu_custom_call" | custom-call | flops 1 | bytes 1 | tf_op jit(solution)/shard_map/pallas_call | solution.py:237
  158.5 1.1 slice.81
  160.0 1.1 slice.82
  161.0 1.5 collective-permute-start.21
  162.6 9.8 %collective-permute-done.20.refs_4_ = bf16[512,512]{1,0:T(8,128)(2,1)S(1)} collective-permute-done((bf16[512,512]{1,0:T(8,128)(2,1)S(1)}, bf16[512,512]{1,0:T(8,128)(2,1)S(1)}, u32[]{:S(2)}, u32[]{:S(2)}) %collective-permute-start.20) | collective-permute-done | bytes 524320 | tf_op jit(solution)/shard_map/ppermute | solution.py:276
  172.3 2.1 collective-permute-done.21.refs_5_
  174.4 1.9 shard_map.73
  176.3 3.5 %collective-permute-start.22 = (bf16[256,512]{1,0:T(8,128)(2,1)S(1)}, bf16[256,512]{1,0:T(8,128)(2,1)S(1)}, u32[]{:S(2)}, u32[]{:S(2)}) collective-permute-start(bf16[256,512]{1,0:T(8,128)(2,1)S(1)} %get-tuple-element.84), channel_id=1, source_target_pairs={{0,1},{1,2},{2,3},{4,5},{5,6},{6,7},{8,9},{9,10},{10,11},{12,13},{... | collective-permute-start | bytes 786440 | tf_op jit(solution)/shard_map/ppermute | solution.py:411
  179.8 1.3 collective-permute-start.25
  181.1 10.2 %collective-permute-done.22 = bf16[256,512]{1,0:T(8,128)(2,1)S(1)} collective-permute-done((bf16[256,512]{1,0:T(8,128)(2,1)S(1)}, bf16[256,512]{1,0:T(8,128)(2,1)S(1)}, u32[]{:S(2)}, u32[]{:S(2)}) %collective-permute-start.22) | collective-permute-done | bytes 262176 | tf_op jit(solution)/shard_map/ppermute | solution.py:411
  191.3 10.8 %collective-permute-done.25 = bf16[256,512]{1,0:T(8,128)(2,1)S(1)} collective-permute-done((bf16[256,512]{1,0:T(8,128)(2,1)S(1)}, bf16[256,512]{1,0:T(8,128)(2,1)S(1)}, u32[]{:S(2)}, u32[]{:S(2)}) %collective-permute-start.25) | collective-permute-done | bytes 262176 | tf_op jit(solution)/shard_map/ppermute | solution.py:412
  202.2 1.3 collective-permute-start.26
  203.5 4.6 %collective-permute-start.23 = (bf16[256,512]{1,0:T(8,128)(2,1)S(1)}, bf16[256,512]{1,0:T(8,128)(2,1)S(1)}, u32[]{:S(2)}, u32[]{:S(2)}) collective-permute-start(bf16[256,512]{1,0:T(8,128)(2,1)S(1)} %get-tuple-element.99), channel_id=1, source_target_pairs={{0,1},{1,2},{2,3},{4,5},{5,6},{6,7},{8,9},{9,10},{10,11},{12,13},{... | collective-permute-start | bytes 786440 | tf_op jit(solution)/shard_map/ppermute | solution.py:411
  208.1 15.2 %collective-permute-done.26 = bf16[256,512]{1,0:T(8,128)(2,1)S(1)} collective-permute-done((bf16[256,512]{1,0:T(8,128)(2,1)S(1)}, bf16[256,512]{1,0:T(8,128)(2,1)S(1)}, u32[]{:S(2)}, u32[]{:S(2)}) %collective-permute-start.26) | collective-permute-done | bytes 262176 | tf_op jit(solution)/shard_map/ppermute | solution.py:412
  223.3 1.3 collective-permute-start.27
  224.7 4.6 %collective-permute-start.24 = (bf16[256,512]{1,0:T(8,128)(2,1)S(1)}, bf16[256,512]{1,0:T(8,128)(2,1)S(1)}, u32[]{:S(2)}, u32[]{:S(2)}) collective-permute-start(bf16[256,512]{1,0:T(8,128)(2,1)S(1)} %add_convert_fusion.1), channel_id=1, source_target_pairs={{0,1},{1,2},{2,3},{4,5},{5,6},{6,7},{8,9},{9,10},{10,11},{12,13},{... | collective-permute-start | bytes 786440 | tf_op jit(solution)/shard_map/ppermute | solution.py:411
  229.3 3.8 %reduce-scatter.2.cloned.1.call-done = bf16[256,1536]{1,0:T(8,128)(2,1)} async-done(((bf16[1024,1536]{1,0:T(8,128)(2,1)}), bf16[256,1536]{1,0:T(8,128)(2,1)}) %reduce-scatter.2.cloned.1.call-update) | async-done | bytes 786448 | tf_op jit(solution)/shard_map/reduce_scatter | solution.py:420
  233.1 1.2 fusion.26
  235.1 1.2 collective-permute-done.28
  236.6 0.9 copy-done.6
  237.5 0.7 copy-done.14
  238.8 1.0 copy-done.16
  239.7 0.9 fusion.21
  (81 shorter events, 4.6 us)
Async XLA Ops:
  6.5 111.3 %copy-start = (f32[7,64]{1,0:T(8,128)S(1)}, f32[7,64]{1,0:T(8,128)}, u32[]{:S(2)}) copy-start(f32[7,64]{1,0:T(8,128)} %param.9) | copy-start | bytes 5380
  6.5 87.1 %all-gather.2.cloned.1.call-start = ((), (), s32[]{:S(2)}) async-start(), calls=%async_computation.1 | async-start | bytes 5242880 | tf_op jit(solution)/shard_map/all_gather | solution.py:327
  6.5 1.9 copy-start.5
  6.5 2.2 copy-start.17
  8.3 4.8 %copy-start.7 = (bf16[2,512,512]{2,1,0:T(8,128)(2,1)}, bf16[2,512,512]{2,1,0:T(8,128)(2,1)S(1)}, u32[]{:S(2)}) copy-start(bf16[2,512,512]{2,1,0:T(8,128)(2,1)S(1)} %get-tuple-element.55.refs_1_.refs_2_) | copy-start | bytes 3145732
  10.0 223.0 %reduce-scatter.2.cloned.1.call-start = ((), (), s32[]{:S(2)}) async-start(), calls=%async_computation.2 | async-start | bytes 3932160 | tf_op jit(solution)/shard_map/reduce_scatter | solution.py:420
  10.1 4.6 %collective-permute-start = (bf16[2,512,512]{2,1,0:T(8,128)(2,1)S(1)}, bf16[2,512,512]{2,1,0:T(8,128)(2,1)S(1)}, u32[]{:S(2)}, u32[]{:S(2)}) collective-permute-start(bf16[2,512,512]{2,1,0:T(8,128)(2,1)S(1)} %get-tuple-element.88), channel_id=1, source_target_pairs={{0,4},{4,0},{8,12},{12,8},{16,20},{20,16},{24,28},{28,24},{1,5},{5... | collective-permute-start | bytes 3145736 | tf_op jit(solution)/shard_map/ppermute | solution.py:279
  10.6 26.6 %collective-permute-start.1 = (bf16[2,512,512]{2,1,0:T(8,128)(2,1)S(1)}, bf16[2,512,512]{2,1,0:T(8,128)(2,1)S(1)}, u32[]{:S(2)}, u32[]{:S(2)}) collective-permute-start(bf16[2,512,512]{2,1,0:T(8,128)(2,1)S(1)} %get-tuple-element.55.refs_1_.refs_2_), channel_id=1, source_target_pairs={{8,0},{12,4},{0,8},{4,12},{24,16},{28,20},{16,24},{20,28},{9,1},{1... | collective-permute-start | bytes 3145736 | tf_op jit(solution)/shard_map/ppermute | solution.py:276
  13.2 26.0 %collective-permute-start.3 = (bf16[2,512,512]{2,1,0:T(8,128)(2,1)S(1)}, bf16[2,512,512]{2,1,0:T(8,128)(2,1)S(1)}, u32[]{:S(2)}, u32[]{:S(2)}) collective-permute-start(bf16[2,512,512]{2,1,0:T(8,128)(2,1)S(1)} %get-tuple-element.55.refs_1_.refs_2_), channel_id=1, source_target_pairs={{16,0},{20,4},{24,8},{28,12},{0,16},{4,20},{8,24},{12,28},{17,1},{... | collective-permute-start | bytes 3145736 | tf_op jit(solution)/shard_map/ppermute | solution.py:276
  14.7 5.9 %copy-start.8 = (bf16[2,512,512]{2,1,0:T(8,128)(2,1)}, bf16[2,512,512]{2,1,0:T(8,128)(2,1)S(1)}, u32[]{:S(2)}) copy-start(bf16[2,512,512]{2,1,0:T(8,128)(2,1)S(1)} %collective-permute-done.refs_2_.refs_3_) | copy-start | bytes 3145732
  14.7 44.7 %collective-permute-start.2 = (bf16[2,512,512]{2,1,0:T(8,128)(2,1)S(1)}, bf16[2,512,512]{2,1,0:T(8,128)(2,1)S(1)}, u32[]{:S(2)}, u32[]{:S(2)}) collective-permute-start(bf16[2,512,512]{2,1,0:T(8,128)(2,1)S(1)} %collective-permute-done.refs_2_.refs_3_), channel_id=1, source_target_pairs={{8,0},{12,4},{0,8},{4,12},{24,16},{28,20},{16,24},{20,28},{9,1},{1... | collective-permute-start | bytes 3145736 | tf_op jit(solution)/shard_map/ppermute | solution.py:276
  15.8 45.1 %collective-permute-start.4 = (bf16[2,512,512]{2,1,0:T(8,128)(2,1)S(1)}, bf16[2,512,512]{2,1,0:T(8,128)(2,1)S(1)}, u32[]{:S(2)}, u32[]{:S(2)}) collective-permute-start(bf16[2,512,512]{2,1,0:T(8,128)(2,1)S(1)} %collective-permute-done.refs_2_.refs_3_), channel_id=1, source_target_pairs={{16,0},{20,4},{24,8},{28,12},{0,16},{4,20},{8,24},{12,28},{17,1},{... | collective-permute-start | bytes 3145736 | tf_op jit(solution)/shard_map/ppermute | solution.py:276
  18.5 2.0 collective-permute-start.5
  37.2 25.8 %copy-start.9 = (bf16[2,512,512]{2,1,0:T(8,128)(2,1)}, bf16[2,512,512]{2,1,0:T(8,128)(2,1)S(1)}, u32[]{:S(2)}) copy-start(bf16[2,512,512]{2,1,0:T(8,128)(2,1)S(1)} %collective-permute-done.1.refs_3_.refs_4_) | copy-start | bytes 3145732
  39.2 47.8 %copy-start.10 = (bf16[2,512,512]{2,1,0:T(8,128)(2,1)}, bf16[2,512,512]{2,1,0:T(8,128)(2,1)S(1)}, u32[]{:S(2)}) copy-start(bf16[2,512,512]{2,1,0:T(8,128)(2,1)S(1)} %collective-permute-done.3.refs_5_.refs_6_) | copy-start | bytes 3145732
  59.4 27.6 %copy-start.11 = (bf16[2,512,512]{2,1,0:T(8,128)(2,1)}, bf16[2,512,512]{2,1,0:T(8,128)(2,1)S(1)}, u32[]{:S(2)}) copy-start(bf16[2,512,512]{2,1,0:T(8,128)(2,1)S(1)} %collective-permute-done.2.refs_4_.refs_5_) | copy-start | bytes 3145732
  60.9 26.1 %copy-start.12 = (bf16[2,512,512]{2,1,0:T(8,128)(2,1)}, bf16[2,512,512]{2,1,0:T(8,128)(2,1)S(1)}, u32[]{:S(2)}) copy-start(bf16[2,512,512]{2,1,0:T(8,128)(2,1)S(1)} %collective-permute-done.4.refs_6_.refs_7_) | copy-start | bytes 3145732
  60.9 26.1 %collective-permute-start.6 = (bf16[2,512,512]{2,1,0:T(8,128)(2,1)S(1)}, bf16[2,512,512]{2,1,0:T(8,128)(2,1)S(1)}, u32[]{:S(2)}, u32[]{:S(2)}) collective-permute-start(bf16[2,512,512]{2,1,0:T(8,128)(2,1)S(1)} %collective-permute-done.1.refs_3_.refs_4_), channel_id=1, source_target_pairs={{16,0},{20,4},{24,8},{28,12},{0,16},{4,20},{8,24},{12,28},{17,1},{... | collective-permute-start | bytes 3145736 | tf_op jit(solution)/shard_map/ppermute | solution.py:276
  62.4 26.2 %collective-permute-start.7 = (bf16[2,512,512]{2,1,0:T(8,128)(2,1)S(1)}, bf16[2,512,512]{2,1,0:T(8,128)(2,1)}, u32[]{:S(2)}, u32[]{:S(2)}) collective-permute-start(bf16[2,512,512]{2,1,0:T(8,128)(2,1)S(1)} %collective-permute-done.4.refs_6_.refs_7_), channel_id=1, source_target_pairs={{8,0},{12,4},{0,8},{4,12},{24,16},{28,20},{16,24},{20,28},{9,1},{1... | collective-permute-start | bytes 3145736 | tf_op jit(solution)/shard_map/ppermute | solution.py:276
  62.9 48.0 %collective-permute-start.8 = (bf16[2,512,512]{2,1,0:T(8,128)(2,1)S(1)}, bf16[2,512,512]{2,1,0:T(8,128)(2,1)S(1)}, u32[]{:S(2)}, u32[]{:S(2)}) collective-permute-start(bf16[2,512,512]{2,1,0:T(8,128)(2,1)S(1)} %pad_maximum_fusion.refs_1_), channel_id=1, source_target_pairs={{8,0},{12,4},{0,8},{4,12},{24,16},{28,20},{16,24},{20,28},{9,1},{1... | collective-permute-start | bytes 3145736 | tf_op jit(solution)/shard_map/ppermute | solution.py:276
  64.4 46.5 %collective-permute-start.9 = (bf16[2,512,512]{2,1,0:T(8,128)(2,1)S(1)}, bf16[2,512,512]{2,1,0:T(8,128)(2,1)S(1)}, u32[]{:S(2)}, u32[]{:S(2)}) collective-permute-start(bf16[2,512,512]{2,1,0:T(8,128)(2,1)S(1)} %pad_maximum_fusion.refs_1_), channel_id=1, source_target_pairs={{16,0},{20,4},{24,8},{28,12},{0,16},{4,20},{8,24},{12,28},{17,1},{... | collective-permute-start | bytes 3145736 | tf_op jit(solution)/shard_map/ppermute | solution.py:276
  87.0 1.0 copy-start.13
  94.6 11.6 %collective-permute-start.10 = (bf16[16,4096]{1,0:T(8,128)(2,1)S(1)}, bf16[16,4096]{1,0:T(8,128)(2,1)S(1)}, u32[]{:S(2)}, u32[]{:S(2)}) collective-permute-start(bf16[16,4096]{1,0:T(8,128)(2,1)S(1)} %slice.56), channel_id=1, source_target_pairs={{4,8},{12,16},{20,24},{5,9},{13,17},{21,25},{6,10},{14,18},{22,26}... | collective-permute-start | bytes 393224 | tf_op jit(solution)/shard_map/ppermute | solution.py:351
  95.2 10.9 %collective-permute-start.11 = (bf16[16,4096]{1,0:T(8,128)(2,1)S(1)}, bf16[16,4096]{1,0:T(8,128)(2,1)S(1)}, u32[]{:S(2)}, u32[]{:S(2)}) collective-permute-start(bf16[16,4096]{1,0:T(8,128)(2,1)S(1)} %slice.56), channel_id=1, source_target_pairs={{4,12},{12,20},{20,28},{5,13},{13,21},{21,29},{6,14},{14,22},{22,3... | collective-permute-start | bytes 393224 | tf_op jit(solution)/shard_map/ppermute | solution.py:351
  106.1 12.1 %copy-start.3 = (s32[8]{0:T(128)S(1)}, s32[8]{0:T(128)}, u32[]{:S(2)}) copy-start(s32[8]{0:T(128)} %stack.55.at_ref._) | copy-start | bytes 100
  111.0 11.2 %collective-permute-start.12 = (bf16[512,4096]{1,0:T(8,128)(2,1)}, bf16[512,4096]{1,0:T(8,128)(2,1)}, u32[]{:S(2)}, u32[]{:S(2)}) collective-permute-start(bf16[512,4096]{1,0:T(8,128)(2,1)} %all-gather.2.cloned.1.call-done.refs_0_), channel_id=1, source_target_pairs={{0,4},{4,0},{8,12},{12,8},{16,20},{20,16},{24,28},{28,24},{1,5},{5... | collective-permute-start | bytes 12582920 | tf_op jit(solution)/shard_map/ppermute | solution.py:279
  112.9 28.2 %collective-permute-start.13 = (bf16[512,512]{1,0:T(8,128)(2,1)}, bf16[512,512]{1,0:T(8,128)(2,1)}, u32[]{:S(2)}, u32[]{:S(2)}) collective-permute-start(bf16[512,512]{1,0:T(8,128)(2,1)} %slice_bitcast_fusion.1), channel_id=1, source_target_pairs={{16,0},{20,4},{24,8},{28,12},{0,16},{4,20},{8,24},{12,28},{17,1},{... | collective-permute-start | bytes 1572872 | tf_op jit(solution)/shard_map/ppermute | solution.py:276
  115.5 25.7 %collective-permute-start.14 = (bf16[512,512]{1,0:T(8,128)(2,1)}, bf16[512,512]{1,0:T(8,128)(2,1)}, u32[]{:S(2)}, u32[]{:S(2)}) collective-permute-start(bf16[512,512]{1,0:T(8,128)(2,1)} %slice_bitcast_fusion), channel_id=1, source_target_pairs={{8,0},{12,4},{0,8},{4,12},{24,16},{28,20},{16,24},{20,28},{9,1},{1... | collective-permute-start | bytes 1572872 | tf_op jit(solution)/shard_map/ppermute | solution.py:276
  115.5 36.3 %collective-permute-start.17 = (bf16[1024,512]{1,0:T(8,128)(2,1)}, bf16[1024,512]{1,0:T(8,128)(2,1)}, u32[]{:S(2)}, u32[]{:S(2)}) collective-permute-start(bf16[1024,512]{1,0:T(8,128)(2,1)} %refs_4_.1), channel_id=1, source_target_pairs={{8,0},{12,4},{0,8},{4,12},{24,16},{28,20},{16,24},{20,28},{9,1},{1... | collective-permute-start | bytes 3145736 | tf_op jit(solution)/shard_map/ppermute | solution.py:276
  117.6 34.3 %collective-permute-start.18 = (bf16[1024,512]{1,0:T(8,128)(2,1)}, bf16[1024,512]{1,0:T(8,128)(2,1)}, u32[]{:S(2)}, u32[]{:S(2)}) collective-permute-start(bf16[1024,512]{1,0:T(8,128)(2,1)} %refs_4_.1), channel_id=1, source_target_pairs={{16,0},{20,4},{24,8},{28,12},{0,16},{4,20},{8,24},{12,28},{17,1},{... | collective-permute-start | bytes 3145736 | tf_op jit(solution)/shard_map/ppermute | solution.py:276
  122.2 9.8 %copy-start.1 = (f32[512,512]{1,0:T(8,128)S(1)}, f32[512,512]{1,0:T(8,128)}, u32[]{:S(2)}) copy-start(f32[512,512]{1,0:T(8,128)} %shard_map.64.product_ref) | copy-start | bytes 3145732
  122.2 10.7 %copy-start.4 = (s32[8]{0:T(128)S(1)}, s32[8]{0:T(128)}, u32[]{:S(2)}) copy-start(s32[8]{0:T(128)} %stack.55.at_ref._) | copy-start | bytes 100
  132.0 2.9 %copy-start.2 = (f32[512,512]{1,0:T(8,128)S(1)}, f32[512,512]{1,0:T(8,128)}, u32[]{:S(2)}) copy-start(f32[512,512]{1,0:T(8,128)} %get-tuple-element.70.product_ref) | copy-start | bytes 3145732
  144.4 7.5 %collective-permute-start.15 = (bf16[512,512]{1,0:T(8,128)(2,1)S(1)}, bf16[512,512]{1,0:T(8,128)(2,1)S(1)}, u32[]{:S(2)}, u32[]{:S(2)}) collective-permute-start(bf16[512,512]{1,0:T(8,128)(2,1)S(1)} %shard_map.71.refs_2_), channel_id=1, source_target_pairs={{0,4},{4,0},{8,12},{12,8},{16,20},{20,16},{24,28},{28,24},{1,5},{5... | collective-permute-start | bytes 1572872 | tf_op jit(solution)/shard_map/ppermute | solution.py:279
  147.7 4.2 %collective-permute-start.16 = (bf16[512,512]{1,0:T(8,128)(2,1)S(1)}, bf16[512,512]{1,0:T(8,128)(2,1)S(1)}, u32[]{:S(2)}, u32[]{:S(2)}) collective-permute-start(bf16[512,512]{1,0:T(8,128)(2,1)S(1)} %shard_map.69.refs_0_), channel_id=1, source_target_pairs={{0,4},{4,0},{8,12},{12,8},{16,20},{20,16},{24,28},{28,24},{1,5},{5... | collective-permute-start | bytes 1572872 | tf_op jit(solution)/shard_map/ppermute | solution.py:279
  159.6 12.7 %collective-permute-start.20 = (bf16[512,512]{1,0:T(8,128)(2,1)S(1)}, bf16[512,512]{1,0:T(8,128)(2,1)S(1)}, u32[]{:S(2)}, u32[]{:S(2)}) collective-permute-start(bf16[512,512]{1,0:T(8,128)(2,1)S(1)} %slice.81), channel_id=1, source_target_pairs={{16,0},{20,4},{24,8},{28,12},{0,16},{4,20},{8,24},{12,28},{17,1},{... | collective-permute-start | bytes 1572872 | tf_op jit(solution)/shard_map/ppermute | solution.py:276
  161.0 13.4 %collective-permute-start.21 = (bf16[512,512]{1,0:T(8,128)(2,1)S(1)}, bf16[512,512]{1,0:T(8,128)(2,1)S(1)}, u32[]{:S(2)}, u32[]{:S(2)}) collective-permute-start(bf16[512,512]{1,0:T(8,128)(2,1)S(1)} %slice.82), channel_id=1, source_target_pairs={{8,0},{12,4},{0,8},{4,12},{24,16},{28,20},{16,24},{20,28},{9,1},{1... | collective-permute-start | bytes 1572872 | tf_op jit(solution)/shard_map/ppermute | solution.py:276
  176.3 15.0 %collective-permute-start.22 = (bf16[256,512]{1,0:T(8,128)(2,1)S(1)}, bf16[256,512]{1,0:T(8,128)(2,1)S(1)}, u32[]{:S(2)}, u32[]{:S(2)}) collective-permute-start(bf16[256,512]{1,0:T(8,128)(2,1)S(1)} %get-tuple-element.84), channel_id=1, source_target_pairs={{0,1},{1,2},{2,3},{4,5},{5,6},{6,7},{8,9},{9,10},{10,11},{12,13},{... | collective-permute-start | bytes 786440 | tf_op jit(solution)/shard_map/ppermute | solution.py:411
  179.8 22.3 %collective-permute-start.25 = (bf16[256,512]{1,0:T(8,128)(2,1)S(1)}, bf16[256,512]{1,0:T(8,128)(2,1)S(1)}, u32[]{:S(2)}, u32[]{:S(2)}) collective-permute-start(bf16[256,512]{1,0:T(8,128)(2,1)S(1)} %get-tuple-element.82), channel_id=1, source_target_pairs={{1,0},{2,1},{3,2},{5,4},{6,5},{7,6},{9,8},{10,9},{11,10},{13,12},{... | collective-permute-start | bytes 786440 | tf_op jit(solution)/shard_map/ppermute | solution.py:412
  202.2 21.1 %collective-permute-start.26 = (bf16[256,512]{1,0:T(8,128)(2,1)S(1)}, bf16[256,512]{1,0:T(8,128)(2,1)S(1)}, u32[]{:S(2)}, u32[]{:S(2)}) collective-permute-start(bf16[256,512]{1,0:T(8,128)(2,1)S(1)} %get-tuple-element.100), channel_id=1, source_target_pairs={{1,0},{2,1},{3,2},{5,4},{6,5},{7,6},{9,8},{10,9},{11,10},{13,12},{... | collective-permute-start | bytes 786440 | tf_op jit(solution)/shard_map/ppermute | solution.py:412
  203.5 21.1 %collective-permute-start.23 = (bf16[256,512]{1,0:T(8,128)(2,1)S(1)}, bf16[256,512]{1,0:T(8,128)(2,1)S(1)}, u32[]{:S(2)}, u32[]{:S(2)}) collective-permute-start(bf16[256,512]{1,0:T(8,128)(2,1)S(1)} %get-tuple-element.99), channel_id=1, source_target_pairs={{0,1},{1,2},{2,3},{4,5},{5,6},{6,7},{8,9},{9,10},{10,11},{12,13},{... | collective-permute-start | bytes 786440 | tf_op jit(solution)/shard_map/ppermute | solution.py:411
  223.3 11.0 %collective-permute-start.27 = (bf16[256,512]{1,0:T(8,128)(2,1)S(1)}, bf16[256,512]{1,0:T(8,128)(2,1)S(1)}, u32[]{:S(2)}, u32[]{:S(2)}) collective-permute-start(bf16[256,512]{1,0:T(8,128)(2,1)S(1)} %add_convert_fusion), channel_id=1, source_target_pairs={{1,0},{2,1},{3,2},{5,4},{6,5},{7,6},{9,8},{10,9},{11,10},{13,12},{... | collective-permute-start | bytes 786440 | tf_op jit(solution)/shard_map/ppermute | solution.py:412
  224.7 9.7 %collective-permute-start.24 = (bf16[256,512]{1,0:T(8,128)(2,1)S(1)}, bf16[256,512]{1,0:T(8,128)(2,1)S(1)}, u32[]{:S(2)}, u32[]{:S(2)}) collective-permute-start(bf16[256,512]{1,0:T(8,128)(2,1)S(1)} %add_convert_fusion.1), channel_id=1, source_target_pairs={{0,1},{1,2},{2,3},{4,5},{5,6},{6,7},{8,9},{9,10},{10,11},{12,13},{... | collective-permute-start | bytes 786440 | tf_op jit(solution)/shard_map/ppermute | solution.py:411
  234.3 2.1 collective-permute-start.19
  234.5 2.0 copy-start.15
  234.5 1.7 collective-permute-start.28
  236.3 1.2 copy-start.6
  236.3 1.9 copy-start.14
  238.2 1.5 slice-start
  238.7 1.0 copy-start.16
Sparse Core Ops, SparseCore 0:
  10.2 83.4 all-gather.1
  158.7 74.3 reduce-scatter.1

commit v13 on v11

--- a/solution.py
+++ b/solution.py
@@ -52,16 +52,37 @@
         out_ref[rows, tile] = query
 
 
-def gate_kernel(parts, at_ref, *refs):
-    xs, refs = refs[:parts], refs[parts:]
-    filtered_ref, partial_ref, pieces, out_ref = refs[0], refs[1], refs[2:-1], refs[-1]
+def gate_kernel(at_ref, x_ref, filtered_ref, partial_ref, *refs):
+    count = (len(refs) - 2) // 2
+    pieces, out_ref, (*held, sems) = refs[:count], refs[count], refs[count + 1 :]
     deep = pieces[0].shape[0]
-    for x_ref, rows, tile in blocks_of(xs, out_ref):
-        query = partial_ref[rows, tile]
-        for index, piece in enumerate(pieces):
-            query = query + dot(columns_of(x_ref, at_ref, index, deep), piece[:, tile])
-        gated = query.astype(BF16).astype(F32) * filtered_ref[rows, tile]
-        out_ref[rows, tile] = gated.astype(BF16)
+    copies = []
+    for index, target in enumerate(held):
+        columns = pl.ds(pl.multiple_of(at_ref[index], deep), deep)
+        copies.append(pltpu.make_async_copy(x_ref.at[:, columns], target, sems.at[index]))
+        copies[-1].start()
+    for copy in copies:
+        copy.wait()
+    for tile in tiles_of(out_ref):
+        query = partial_ref[:, tile]
+        for x, piece in zip(held, pieces):
+            query = query + dot(x[...], piece[:, tile])
+        out_ref[:, tile] = (query.astype(BF16).astype(F32) * filtered_ref[:, tile]).astype(BF16)
+
+
+def gate(at, x, filtered, partial, pieces):
+    length, deep = x.shape[0], pieces[0].shape[0]
+    return pl.pallas_call(
+        gate_kernel,
+        out_shape=jax.ShapeDtypeStruct(filtered.shape, BF16),
+        in_specs=[pl.BlockSpec(memory_space=pltpu.SMEM), pl.BlockSpec(memory_space=pl.ANY)]
+        + [WHOLE] * (2 + len(pieces)),
+        out_specs=WHOLE,
+        scratch_shapes=[pltpu.VMEM((length, deep), BF16) for _ in pieces]
+        + [pltpu.SemaphoreType.DMA((len(pieces),))],
+        compiler_params=pltpu.CompilerParams(vmem_limit_bytes=GRANT),
+        cost_estimate=pl.CostEstimate(flops=1, bytes_accessed=1, transcendentals=0),
+    )(at, x, filtered, partial, *pieces)
 
 
 def call(kernel, scalars, operands, out, scratch=()):
@@ -198,6 +219,83 @@
     return [range(len(parts)) for parts in blocks]
 
 
+def first_kernel(n_tp, at_ref, *refs):
+    gates, (weight_ref, out_ref, held, ready, sem) = refs[:4], refs[4:]
+    half = gates[0].shape[1]
+    rows = gates[0].shape[0] // n_tp
+    for slot in range(n_tp):
+        for index, taken in enumerate(gates):
+            side, whose = index % 2, index // 2
+            place = slice((2 * slot + whose) * rows, (2 * slot + whose + 1) * rows)
+            column = (at_ref[0] if side == 0 else 1 - at_ref[0]) * half
+            columns = pl.ds(pl.multiple_of(column, half), half)
+            held[place, columns] = taken[slot * rows : (slot + 1) * rows]
+    ready[...] = dot(held[...], weight_ref[...]).astype(BF16)
+    copy = pltpu.make_async_copy(ready, out_ref.at[:, : ready.shape[1]], sem)
+    copy.start()
+    copy.wait()
+
+
+def rest_kernel(held, *refs):
+    count = (len(refs) - 5) // 2
+    given, (_, out_ref), (*weights, ready, sems, out_sems) = (
+        refs[:count],
+        refs[count : count + 2],
+        refs[count + 2 :],
+    )
+    copies = [
+        pltpu.make_async_copy(source, target, sems.at[index])
+        for index, (source, target) in enumerate(zip(given, weights))
+    ]
+    for copy in copies:
+        copy.start()
+    wide = weights[0].shape[1]
+    leaving = []
+    for index, weight in enumerate(weights):
+        copies[index].wait()
+        at = slice(index * wide, (index + 1) * wide)
+        ready[:, at] = dot(held[...], weight[...]).astype(BF16)
+        to = out_ref.at[:, (index + 1) * wide : (index + 2) * wide]
+        leaving.append(pltpu.make_async_copy(ready.at[:, at], to, out_sems.at[index]))
+        leaving[-1].start()
+    for copy in leaving:
+        copy.wait()
+
+
+def first_terms(n_tp, place, gates, weight, blocks):
+    length, half = gates[0].shape
+    wide = weight.shape[1]
+    return pl.pallas_call(
+        functools.partial(first_kernel, n_tp),
+        out_shape=[
+            jax.ShapeDtypeStruct((2 * length, blocks * wide), BF16),
+            jax.ShapeDtypeStruct((2 * length, 2 * half), BF16),
+        ],
+        in_specs=[pl.BlockSpec(memory_space=pltpu.SMEM)] + [WHOLE] * 5,
+        out_specs=[pl.BlockSpec(memory_space=pl.ANY), WHOLE],
+        scratch_shapes=[pltpu.VMEM((2 * length, wide), BF16), pltpu.SemaphoreType.DMA],
+        compiler_params=pltpu.CompilerParams(vmem_limit_bytes=GRANT),
+        cost_estimate=pl.CostEstimate(flops=1, bytes_accessed=1, transcendentals=0),
+    )(place, *gates, weight)
+
+
+def rest_terms(held, found, weights):
+    anywhere = pl.BlockSpec(memory_space=pl.ANY)
+    count, wide = len(weights), weights[0].shape[1]
+    return pl.pallas_call(
+        rest_kernel,
+        out_shape=jax.ShapeDtypeStruct(found.shape, BF16),
+        in_specs=[WHOLE] + [anywhere] * (count + 1),
+        out_specs=anywhere,
+        input_output_aliases={count + 1: 0},
+        scratch_shapes=[pltpu.VMEM(weight.shape, BF16) for weight in weights]
+        + [pltpu.VMEM((found.shape[0], count * wide), BF16)]
+        + [pltpu.SemaphoreType.DMA((count,))] * 2,
+        compiler_params=pltpu.CompilerParams(vmem_limit_bytes=2 * GRANT),
+        cost_estimate=pl.CostEstimate(flops=1, bytes_accessed=1, transcendentals=0),
+    )(held, *weights, found)
+
+
 def on_device(tokens, norm_gain, in_weight, filters, out_weight, keep_mask):
     n_seq, n_tp = lax.axis_size("seq"), lax.axis_size("tp")
     chips = n_seq // 2
@@ -334,12 +432,8 @@
         for dx in range(1, nx)
     }
     late = [piece for pair in q_rest.values() for piece in pair]
-    other_gated = project(
-        gate_kernel, at[early:], [other_rows], [other_filtered, other_query], late, BF16
-    )
-    own_gated = project(
-        gate_kernel, at[early:], [own_rows], [own_filtered, own_query], late, BF16
-    )
+    other_gated = gate(at[early:], other_rows, other_filtered, other_query, late)
+    own_gated = gate(at[early:], own_rows, own_filtered, own_query, late)
     gates = (own_gated, from_partner(other_gated), other_gated, from_partner(own_gated))
 
     position = lax.axis_index("tp")
@@ -363,7 +457,8 @@
 
     near = {(0, 0): (out_weight,)}
     near.update({key: (block,) for key, block in (*o_x.items(), *o_y.items())})
-    found = terms(n_tp, here_at, gates, list(near.values()), False)
+    found, held = first_terms(n_tp, here_at, gates, out_weight, len(near))
+    found = rest_terms(held, found, [*o_x.values(), *o_y.values()])
     gates, found = lax.optimization_barrier((gates, found))
     near_sum = lax.psum_scatter(found, "tp", scatter_dimension=0, tiled=True)
     far_sum = chained(terms(n_tp, here_at, gates, list(o_rest.values()), True))

time: 249 us -> 252 us (1.012)
    pallas_call x0 -> x4, Pallas kernels: none -> 14.8 us  [the longest x2 6.3 us: gate(): pl.pallas_call(gate_kernel, out_shape=jax.ShapeDtypeStruct(filtered.shape...]
    pallas_call x8 -> x5, Pallas kernels: 27.6 us -> 14.1 us  [call(): pl.pallas_call(kernel, out_shape=out, in_specs=[pl.BlockSpec(memory_space...]
    ppermute x3, waiting for transfers between devices: 10.2 us -> 22.2 us  [chained(): rising = lax.ppermute(send_up, 'tp', up)]
    ppermute x3, waiting for transfers between devices: 26 us -> 14.9 us  [chained(): falling = lax.ppermute(send_down, 'tp', down)]
  transfers between devices with their start and end apart: 31 -> 31, of which waited for: 17 -> 20; matrix products, arithmetic and copies ran while one was open for 4% -> 4% of each run, Pallas kernels for 16% -> 17%
where the time goes in v13:
time: 252 us; the launch traced here: 251 us
  waiting for transfers between devices  130 us (52%)
  Pallas kernels  48.1 us (19%)
  starting transfers between devices  38.7 us (15%)
  between operations  14.1 us (6%)
  local copies, waits for them, and re-layouts  13.9 us (6%)
  other arithmetic  6.23 us (2%)
    ppermute x14, waiting for transfers between devices, from_chip(): return lax.ppermute(block, 'seq', route)  80.9 us
    ppermute x3, waiting for transfers between devices, chained(): rising = lax.ppermute(send_up, 'tp', up)  22.2 us
    pallas_call x2, Pallas kernels, products(): pl.pallas_call(functools.partial(product_kernel, len(xs), len(pieces)), o...  19.2 us
    ppermute x14, starting transfers between devices, from_chip(): return lax.ppermute(block, 'seq', route)  16.7 us
    ppermute x3, waiting for transfers between devices, chained(): falling = lax.ppermute(send_down, 'tp', down)  14.9 us
    ppermute x3, starting transfers between devices, chained(): rising = lax.ppermute(send_up, 'tp', up)  14.3 us
    pallas_call x5, Pallas kernels, call(): pl.pallas_call(kernel, out_shape=out, in_specs=[pl.BlockSpec(memory_space...  14.1 us
    pallas_call x2, Pallas kernels, gate(): pl.pallas_call(gate_kernel, out_shape=jax.ShapeDtypeStruct(filtered.shape...  6.3 us
  transfers between devices with their start and end apart: 31, of which 20 were waited for; matrix products, arithmetic and copies ran while one was open for 4% of the time, Pallas kernels for 17%

profile of v13, /device:TPU:0, one launch (start us, length us, event | category | flops | bytes accessed | tf_op | source)
XLA Modules:
  0.0 251.0 jit_solution(11984891666183202775)
XLA Ops:
  6.5 1.8 constant_dynamic-slice_fusion.2
  8.7 1.3 fusion.2
  10.6 2.6 %collective-permute-start.1 = (bf16[2,512,512]{2,1,0:T(8,128)(2,1)S(1)}, bf16[2,512,512]{2,1,0:T(8,128)(2,1)S(1)}, u32[]{:S(2)}, u32[]{:S(2)}) collective-permute-start(bf16[2,512,512]{2,1,0:T(8,128)(2,1)S(1)} %get-tuple-element.57.refs_1_.refs_2_), channel_id=1, source_target_pairs={{8,0},{12,4},{0,8},{4,12},{24,16},{28,20},{16,24},{20,28},{9,1},{1... | collective-permute-start | bytes 3145736 | tf_op jit(solution)/shard_map/ppermute | solution.py:322
  13.2 1.5 collective-permute-start.3
  14.7 1.1 collective-permute-start.2
  15.8 1.5 collective-permute-start.4
  17.3 1.3 constant_dynamic-slice_fusion.1
  18.6 1.9 collective-permute-done.5
  20.6 16.5 %collective-permute-done.1.refs_3_.refs_4_ = bf16[2,512,512]{2,1,0:T(8,128)(2,1)S(1)} collective-permute-done((bf16[2,512,512]{2,1,0:T(8,128)(2,1)S(1)}, bf16[2,512,512]{2,1,0:T(8,128)(2,1)S(1)}, u32[]{:S(2)}, u32[]{:S(2)}) %collective-permute-start.1) | collective-permute-done | bytes 1048608 | tf_op jit(solution)/shard_map/ppermute | solution.py:322
  37.2 2.0 collective-permute-done.3.refs_5_.refs_6_
  39.2 20.2 %collective-permute-done.2.refs_4_.refs_5_ = bf16[2,512,512]{2,1,0:T(8,128)(2,1)S(1)} collective-permute-done((bf16[2,512,512]{2,1,0:T(8,128)(2,1)S(1)}, bf16[2,512,512]{2,1,0:T(8,128)(2,1)S(1)}, u32[]{:S(2)}, u32[]{:S(2)}) %collective-permute-start.2) | collective-permute-done | bytes 1048608 | tf_op jit(solution)/shard_map/ppermute | solution.py:322
  59.4 1.5 collective-permute-done.4.refs_6_.refs_7_
  60.9 1.5 collective-permute-start.6
  62.9 1.5 collective-permute-start.8
  64.9 22.0 %collective-permute-done.6.refs_7_.refs_8_ = bf16[2,512,512]{2,1,0:T(8,128)(2,1)S(1)} collective-permute-done((bf16[2,512,512]{2,1,0:T(8,128)(2,1)S(1)}, bf16[2,512,512]{2,1,0:T(8,128)(2,1)S(1)}, u32[]{:S(2)}, u32[]{:S(2)}) %collective-permute-start.6) | collective-permute-done | bytes 1048608 | tf_op jit(solution)/shard_map/ppermute | solution.py:322
  87.0 1.0 copy-done.13
  88.6 5.1 %all-gather.2.cloned.1.call-done.refs_0_.x_ref = bf16[512,4096]{1,0:T(8,128)(2,1)} async-done(((bf16[128,4096]{1,0:T(8,128)(2,1)}), bf16[512,4096]{1,0:T(8,128)(2,1)}) %all-gather.2.cloned.1.call-update) | async-done | bytes 4194320 | tf_op jit(solution)/shard_map/all_gather | solution.py:373
  93.7 0.9 slice.56
  94.6 0.7 collective-permute-start.10
  95.2 0.7 collective-permute-start.11
  96.0 0.7 stack.55.at_ref._
  96.7 9.4 %shard_map.64.product_ref = f32[512,512]{1,0:T(8,128)} custom-call(s32[8]{0:T(128)} %stack.55.at_ref._, bf16[512,4096]{1,0:T(8,128)(2,1)} %all-gather.2.cloned.1.call-done.refs_0_.x_ref, bf16[2,512,512]{2,1,0:T(8,128)(2,1)} %copy-done.7, bf16[2,512,512]{2,1,0:T(8,128)(2,1)} %copy-done.8, bf16[2,512,512]{2,1,0:T(8,128)(2,1)} %copy-done.9, ...), custom_call_target="tpu_custom_call" | custom-call | flops 1 | bytes 1 | tf_op jit(solution)/shard_map/pallas_call | solution.py:145
  106.8 4.1 %collective-permute-done.8.refs_2_ = bf16[2,512,512]{2,1,0:T(8,128)(2,1)S(1)} collective-permute-done((bf16[2,512,512]{2,1,0:T(8,128)(2,1)S(1)}, bf16[2,512,512]{2,1,0:T(8,128)(2,1)S(1)}, u32[]{:S(2)}, u32[]{:S(2)}) %collective-permute-start.8) | collective-permute-done | bytes 1048608 | tf_op jit(solution)/shard_map/ppermute | solution.py:322
  111.0 1.2 collective-permute-start.12
  112.1 0.8 slice_bitcast_fusion.1
  113.0 1.7 collective-permute-start.13
  114.7 0.8 slice_bitcast_fusion
  115.5 2.0 collective-permute-start.17
  118.2 4.0 %shard_map.65.partial_ref = f32[512,512]{1,0:T(8,128)S(1)} custom-call(s32[8]{0:T(128)S(1)} %copy-done.3, bf16[512,4096]{1,0:T(8,128)(2,1)} %all-gather.2.cloned.1.call-done.refs_0_.x_ref, bf16[2,512,512]{2,1,0:T(8,128)(2,1)S(1)} %pad_maximum_fusion.refs_1_, bf16[2,512,512]{2,1,0:T(8,128)(2,1)S(1)} %collective-permute-done.8.refs_2_, ...), custom_call_target="tpu_custom_call" | custom-call | flops 1 | bytes 1 | tf_op jit(solution)/shard_map/pallas_call | solution.py:89
  122.3 9.8 %shard_map.66 = (f32[16,512]{1,0:T(8,128)}, f32[512,512]{1,0:T(8,128)}) custom-call(s32[8]{0:T(128)} %stack.55.at_ref._, bf16[16,4096]{1,0:T(8,128)(2,1)} %broadcast_select_fusion.refs_0_, bf16[512,4096]{1,0:T(8,128)(2,1)} %collective-permute-done.12.refs_1_.refs_0_.x_ref, bf16[2,512,512]{2,1,0:T(8,128)(2,1)} %copy-done.7, bf16[2,512,512]{2,1,0:T(8,128)(2,1)} %copy-done.8, ...), custom_call_target="tpu_custom_call" | custom-call | flops 1 | bytes 1 | tf_op jit(solution)/shard_map/pallas_call | solution.py:145
  132.0 0.8 broadcast_select_fusion.1
  132.8 1.2 copy-done.2
  134.0 2.0 shard_map.68.filtered_ref
  136.1 2.0 shard_map.67.filtered_ref
  138.1 4.2 %shard_map.70.partial_ref = f32[512,512]{1,0:T(8,128)S(1)} custom-call(s32[8]{0:T(128)S(1)} %copy-done.4, bf16[512,4096]{1,0:T(8,128)(2,1)} %collective-permute-done.12.refs_1_.refs_0_.x_ref, bf16[2,512,512]{2,1,0:T(8,128)(2,1)S(1)} %pad_maximum_fusion.refs_1_, bf16[2,512,512]{2,1,0:T(8,128)(2,1)S(1)} %collective-permute-done.8.refs_2_, ...), custom_call_target="tpu_custom_call" | custom-call | flops 1 | bytes 1 | tf_op jit(solution)/shard_map/pallas_call | solution.py:89
  142.3 3.2 %shard_map.71.refs_2_ = bf16[512,512]{1,0:T(8,128)(2,1)S(1)} custom-call(s32[2]{0:T(128)S(1)} %pad_add_fusion.at_ref, bf16[512,4096]{1,0:T(8,128)(2,1)} %collective-permute-done.12.refs_1_.refs_0_.x_ref, f32[512,512]{1,0:T(8,128)S(1)} %shard_map.68.filtered_ref, f32[512,512]{1,0:T(8,128)S(1)} %shard_map.70.partial_ref, ...), custom_call_target="tpu_custom_call" | custom-call | flops 1 | bytes 1 | tf_op jit(solution)/shard_map/pallas_call | solution.py:75
  145.6 3.2 %shard_map.69.refs_0_ = bf16[512,512]{1,0:T(8,128)(2,1)S(1)} custom-call(s32[2]{0:T(128)S(1)} %pad_add_fusion.at_ref, bf16[512,4096]{1,0:T(8,128)(2,1)} %all-gather.2.cloned.1.call-done.refs_0_.x_ref, f32[512,512]{1,0:T(8,128)S(1)} %shard_map.67.filtered_ref, f32[512,512]{1,0:T(8,128)S(1)} %shard_map.65.partial_ref, ...), custom_call_target="tpu_custom_call" | custom-call | flops 1 | bytes 1 | tf_op jit(solution)/shard_map/pallas_call | solution.py:75
  149.4 1.5 collective-permute-done.16.refs_3_
  150.8 3.7 %shard_map.72 = (bf16[1024,1536]{1,0:T(8,128)(2,1)}, bf16[1024,1024]{1,0:T(8,128)(2,1)S(1)}) custom-call(s32[2]{0:T(128)S(1)} %pad_add_fusion.1.at_ref, bf16[512,512]{1,0:T(8,128)(2,1)S(1)} %shard_map.69.refs_0_, bf16[512,512]{1,0:T(8,128)(2,1)S(1)} %collective-permute-done.15.refs_1_, bf16[512,512]{1,0:T(8,128)(2,1)S(1)} %shard_map.71.refs_2_, ...), custom_call_target="tpu_custom_call" | custom-call | flops 1 | bytes 1 | tf_op jit(solution)/shard_map/pallas_call | solution.py:268
  154.5 4.8 %shard_map.73 = bf16[1024,1536]{1,0:T(8,128)(2,1)} custom-call(bf16[1024,1024]{1,0:T(8,128)(2,1)S(1)} %get-tuple-element.77.held, bf16[1024,512]{1,0:T(8,128)(2,1)} %collective-permute-done.17.refs_0_, bf16[1024,512]{1,0:T(8,128)(2,1)} %collective-permute-done.18.refs_1_, bf16[1024,1536]{1,0:T(8,128)(2,1)} %get-tuple-element.79.refs_2_), custom_call_target="tpu_custom_call", output_to_operand_aliasing={{}: (3, {})} | custom-call | flops 1 | bytes 1 | tf_op jit(solution)/shard_map/pallas_call | solution.py:285
  159.4 1.1 slice.81
  160.4 1.8 collective-permute-start.20
  162.2 1.1 slice.82
  163.4 11.3 %collective-permute-done.20.refs_4_ = bf16[512,512]{1,0:T(8,128)(2,1)S(1)} collective-permute-done((bf16[512,512]{1,0:T(8,128)(2,1)S(1)}, bf16[512,512]{1,0:T(8,128)(2,1)S(1)}, u32[]{:S(2)}, u32[]{:S(2)}) %collective-permute-start.20) | collective-permute-done | bytes 524320 | tf_op jit(solution)/shard_map/ppermute | solution.py:322
  174.7 2.6 %collective-permute-done.21.refs_5_ = bf16[512,512]{1,0:T(8,128)(2,1)S(1)} collective-permute-done((bf16[512,512]{1,0:T(8,128)(2,1)S(1)}, bf16[512,512]{1,0:T(8,128)(2,1)S(1)}, u32[]{:S(2)}, u32[]{:S(2)}) %collective-permute-start.21) | collective-permute-done | bytes 524320 | tf_op jit(solution)/shard_map/ppermute | solution.py:322
  177.3 1.9 shard_map.74
  179.2 3.5 %collective-permute-start.22 = (bf16[256,512]{1,0:T(8,128)(2,1)S(1)}, bf16[256,512]{1,0:T(8,128)(2,1)S(1)}, u32[]{:S(2)}, u32[]{:S(2)}) collective-permute-start(bf16[256,512]{1,0:T(8,128)(2,1)S(1)} %get-tuple-element.88), channel_id=1, source_target_pairs={{0,1},{1,2},{2,3},{4,5},{5,6},{6,7},{8,9},{9,10},{10,11},{12,13},{... | collective-permute-start | bytes 786440 | tf_op jit(solution)/shard_map/ppermute | solution.py:453
  182.7 1.3 collective-permute-start.25
  184.0 10.6 %collective-permute-done.22 = bf16[256,512]{1,0:T(8,128)(2,1)S(1)} collective-permute-done((bf16[256,512]{1,0:T(8,128)(2,1)S(1)}, bf16[256,512]{1,0:T(8,128)(2,1)S(1)}, u32[]{:S(2)}, u32[]{:S(2)}) %collective-permute-start.22) | collective-permute-done | bytes 262176 | tf_op jit(solution)/shard_map/ppermute | solution.py:453
  194.6 9.8 %collective-permute-done.25 = bf16[256,512]{1,0:T(8,128)(2,1)S(1)} collective-permute-done((bf16[256,512]{1,0:T(8,128)(2,1)S(1)}, bf16[256,512]{1,0:T(8,128)(2,1)S(1)}, u32[]{:S(2)}, u32[]{:S(2)}) %collective-permute-start.25) | collective-permute-done | bytes 262176 | tf_op jit(solution)/shard_map/ppermute | solution.py:454
  204.5 2.8 %collective-permute-start.23 = (bf16[256,512]{1,0:T(8,128)(2,1)S(1)}, bf16[256,512]{1,0:T(8,128)(2,1)S(1)}, u32[]{:S(2)}, u32[]{:S(2)}) collective-permute-start(bf16[256,512]{1,0:T(8,128)(2,1)S(1)} %get-tuple-element.103), channel_id=1, source_target_pairs={{0,1},{1,2},{2,3},{4,5},{5,6},{6,7},{8,9},{9,10},{10,11},{12,13},{... | collective-permute-start | bytes 786440 | tf_op jit(solution)/shard_map/ppermute | solution.py:453
  207.3 1.3 collective-permute-start.26
  208.6 10.8 %collective-permute-done.23 = bf16[256,512]{1,0:T(8,128)(2,1)S(1)} collective-permute-done((bf16[256,512]{1,0:T(8,128)(2,1)S(1)}, bf16[256,512]{1,0:T(8,128)(2,1)S(1)}, u32[]{:S(2)}, u32[]{:S(2)}) %collective-permute-start.23) | collective-permute-done | bytes 262176 | tf_op jit(solution)/shard_map/ppermute | solution.py:453
  219.5 8.0 %collective-permute-start.24 = (bf16[256,512]{1,0:T(8,128)(2,1)S(1)}, bf16[256,512]{1,0:T(8,128)(2,1)S(1)}, u32[]{:S(2)}, u32[]{:S(2)}) collective-permute-start(bf16[256,512]{1,0:T(8,128)(2,1)S(1)} %add_convert_fusion.1), channel_id=1, source_target_pairs={{0,1},{1,2},{2,3},{4,5},{5,6},{6,7},{8,9},{9,10},{10,11},{12,13},{... | collective-permute-start | bytes 786440 | tf_op jit(solution)/shard_map/ppermute | solution.py:453
  227.9 1.3 collective-permute-start.27
  229.2 2.2 reduce-scatter.2.cloned.1.call-done
  231.4 1.2 fusion.26
  232.7 0.9 collective-permute-done.24
  233.6 4.6 %collective-permute-done.27 = bf16[256,512]{1,0:T(8,128)(2,1)S(1)} collective-permute-done((bf16[256,512]{1,0:T(8,128)(2,1)S(1)}, bf16[256,512]{1,0:T(8,128)(2,1)S(1)}, u32[]{:S(2)}, u32[]{:S(2)}) %collective-permute-start.27) | collective-permute-done | bytes 262176 | tf_op jit(solution)/shard_map/ppermute | solution.py:454
  238.5 1.3 collective-permute-done.28
  240.2 0.9 copy-done.6
  241.1 0.7 copy-done.14
  242.3 1.0 copy-done.16
  243.3 0.9 fusion.21
  (82 shorter events, 6.7 us)
Async XLA Ops:
  6.5 111.3 %copy-start = (f32[7,64]{1,0:T(8,128)S(1)}, f32[7,64]{1,0:T(8,128)}, u32[]{:S(2)}) copy-start(f32[7,64]{1,0:T(8,128)} %param.9) | copy-start | bytes 5380
  6.5 87.1 %all-gather.2.cloned.1.call-start = ((), (), s32[]{:S(2)}) async-start(), calls=%async_computation.1 | async-start | bytes 5242880 | tf_op jit(solution)/shard_map/all_gather | solution.py:373
  6.5 1.9 copy-start.5
  6.5 2.2 copy-start.17
  8.3 4.8 %copy-start.7 = (bf16[2,512,512]{2,1,0:T(8,128)(2,1)}, bf16[2,512,512]{2,1,0:T(8,128)(2,1)S(1)}, u32[]{:S(2)}) copy-start(bf16[2,512,512]{2,1,0:T(8,128)(2,1)S(1)} %get-tuple-element.57.refs_1_.refs_2_) | copy-start | bytes 3145732
  10.0 221.4 %reduce-scatter.2.cloned.1.call-start = ((), (), s32[]{:S(2)}) async-start(), calls=%async_computation.2 | async-start | bytes 3932160 | tf_op jit(solution)/shard_map/reduce_scatter | solution.py:463
  10.1 4.6 %collective-permute-start = (bf16[2,512,512]{2,1,0:T(8,128)(2,1)S(1)}, bf16[2,512,512]{2,1,0:T(8,128)(2,1)S(1)}, u32[]{:S(2)}, u32[]{:S(2)}) collective-permute-start(bf16[2,512,512]{2,1,0:T(8,128)(2,1)S(1)} %get-tuple-element.92), channel_id=1, source_target_pairs={{0,4},{4,0},{8,12},{12,8},{16,20},{20,16},{24,28},{28,24},{1,5},{5... | collective-permute-start | bytes 3145736 | tf_op jit(solution)/shard_map/ppermute | solution.py:325
  10.6 26.6 %collective-permute-start.1 = (bf16[2,512,512]{2,1,0:T(8,128)(2,1)S(1)}, bf16[2,512,512]{2,1,0:T(8,128)(2,1)S(1)}, u32[]{:S(2)}, u32[]{:S(2)}) collective-permute-start(bf16[2,512,512]{2,1,0:T(8,128)(2,1)S(1)} %get-tuple-element.57.refs_1_.refs_2_), channel_id=1, source_target_pairs={{8,0},{12,4},{0,8},{4,12},{24,16},{28,20},{16,24},{20,28},{9,1},{1... | collective-permute-start | bytes 3145736 | tf_op jit(solution)/shard_map/ppermute | solution.py:322
  13.2 26.0 %collective-permute-start.3 = (bf16[2,512,512]{2,1,0:T(8,128)(2,1)S(1)}, bf16[2,512,512]{2,1,0:T(8,128)(2,1)S(1)}, u32[]{:S(2)}, u32[]{:S(2)}) collective-permute-start(bf16[2,512,512]{2,1,0:T(8,128)(2,1)S(1)} %get-tuple-element.57.refs_1_.refs_2_), channel_id=1, source_target_pairs={{16,0},{20,4},{24,8},{28,12},{0,16},{4,20},{8,24},{12,28},{17,1},{... | collective-permute-start | bytes 3145736 | tf_op jit(solution)/shard_map/ppermute | solution.py:322
  14.7 5.9 %copy-start.8 = (bf16[2,512,512]{2,1,0:T(8,128)(2,1)}, bf16[2,512,512]{2,1,0:T(8,128)(2,1)S(1)}, u32[]{:S(2)}) copy-start(bf16[2,512,512]{2,1,0:T(8,128)(2,1)S(1)} %collective-permute-done.refs_2_.refs_3_) | copy-start | bytes 3145732
  14.7 44.7 %collective-permute-start.2 = (bf16[2,512,512]{2,1,0:T(8,128)(2,1)S(1)}, bf16[2,512,512]{2,1,0:T(8,128)(2,1)S(1)}, u32[]{:S(2)}, u32[]{:S(2)}) collective-permute-start(bf16[2,512,512]{2,1,0:T(8,128)(2,1)S(1)} %collective-permute-done.refs_2_.refs_3_), channel_id=1, source_target_pairs={{8,0},{12,4},{0,8},{4,12},{24,16},{28,20},{16,24},{20,28},{9,1},{1... | collective-permute-start | bytes 3145736 | tf_op jit(solution)/shard_map/ppermute | solution.py:322
  15.8 45.1 %collective-permute-start.4 = (bf16[2,512,512]{2,1,0:T(8,128)(2,1)S(1)}, bf16[2,512,512]{2,1,0:T(8,128)(2,1)S(1)}, u32[]{:S(2)}, u32[]{:S(2)}) collective-permute-start(bf16[2,512,512]{2,1,0:T(8,128)(2,1)S(1)} %collective-permute-done.refs_2_.refs_3_), channel_id=1, source_target_pairs={{16,0},{20,4},{24,8},{28,12},{0,16},{4,20},{8,24},{12,28},{17,1},{... | collective-permute-start | bytes 3145736 | tf_op jit(solution)/shard_map/ppermute | solution.py:322
  18.5 2.0 collective-permute-start.5
  37.2 25.8 %copy-start.9 = (bf16[2,512,512]{2,1,0:T(8,128)(2,1)}, bf16[2,512,512]{2,1,0:T(8,128)(2,1)S(1)}, u32[]{:S(2)}) copy-start(bf16[2,512,512]{2,1,0:T(8,128)(2,1)S(1)} %collective-permute-done.1.refs_3_.refs_4_) | copy-start | bytes 3145732
  39.2 47.8 %copy-start.10 = (bf16[2,512,512]{2,1,0:T(8,128)(2,1)}, bf16[2,512,512]{2,1,0:T(8,128)(2,1)S(1)}, u32[]{:S(2)}) copy-start(bf16[2,512,512]{2,1,0:T(8,128)(2,1)S(1)} %collective-permute-done.3.refs_5_.refs_6_) | copy-start | bytes 3145732
  59.4 27.6 %copy-start.11 = (bf16[2,512,512]{2,1,0:T(8,128)(2,1)}, bf16[2,512,512]{2,1,0:T(8,128)(2,1)S(1)}, u32[]{:S(2)}) copy-start(bf16[2,512,512]{2,1,0:T(8,128)(2,1)S(1)} %collective-permute-done.2.refs_4_.refs_5_) | copy-start | bytes 3145732
  60.9 26.1 %copy-start.12 = (bf16[2,512,512]{2,1,0:T(8,128)(2,1)}, bf16[2,512,512]{2,1,0:T(8,128)(2,1)S(1)}, u32[]{:S(2)}) copy-start(bf16[2,512,512]{2,1,0:T(8,128)(2,1)S(1)} %collective-permute-done.4.refs_6_.refs_7_) | copy-start | bytes 3145732
  60.9 26.1 %collective-permute-start.6 = (bf16[2,512,512]{2,1,0:T(8,128)(2,1)S(1)}, bf16[2,512,512]{2,1,0:T(8,128)(2,1)S(1)}, u32[]{:S(2)}, u32[]{:S(2)}) collective-permute-start(bf16[2,512,512]{2,1,0:T(8,128)(2,1)S(1)} %collective-permute-done.1.refs_3_.refs_4_), channel_id=1, source_target_pairs={{16,0},{20,4},{24,8},{28,12},{0,16},{4,20},{8,24},{12,28},{17,1},{... | collective-permute-start | bytes 3145736 | tf_op jit(solution)/shard_map/ppermute | solution.py:322
  62.4 26.2 %collective-permute-start.7 = (bf16[2,512,512]{2,1,0:T(8,128)(2,1)S(1)}, bf16[2,512,512]{2,1,0:T(8,128)(2,1)}, u32[]{:S(2)}, u32[]{:S(2)}) collective-permute-start(bf16[2,512,512]{2,1,0:T(8,128)(2,1)S(1)} %collective-permute-done.4.refs_6_.refs_7_), channel_id=1, source_target_pairs={{8,0},{12,4},{0,8},{4,12},{24,16},{28,20},{16,24},{20,28},{9,1},{1... | collective-permute-start | bytes 3145736 | tf_op jit(solution)/shard_map/ppermute | solution.py:322
  62.9 48.0 %collective-permute-start.8 = (bf16[2,512,512]{2,1,0:T(8,128)(2,1)S(1)}, bf16[2,512,512]{2,1,0:T(8,128)(2,1)S(1)}, u32[]{:S(2)}, u32[]{:S(2)}) collective-permute-start(bf16[2,512,512]{2,1,0:T(8,128)(2,1)S(1)} %pad_maximum_fusion.refs_1_), channel_id=1, source_target_pairs={{8,0},{12,4},{0,8},{4,12},{24,16},{28,20},{16,24},{20,28},{9,1},{1... | collective-permute-start | bytes 3145736 | tf_op jit(solution)/shard_map/ppermute | solution.py:322
  64.4 46.5 %collective-permute-start.9 = (bf16[2,512,512]{2,1,0:T(8,128)(2,1)S(1)}, bf16[2,512,512]{2,1,0:T(8,128)(2,1)S(1)}, u32[]{:S(2)}, u32[]{:S(2)}) collective-permute-start(bf16[2,512,512]{2,1,0:T(8,128)(2,1)S(1)} %pad_maximum_fusion.refs_1_), channel_id=1, source_target_pairs={{16,0},{20,4},{24,8},{28,12},{0,16},{4,20},{8,24},{12,28},{17,1},{... | collective-permute-start | bytes 3145736 | tf_op jit(solution)/shard_map/ppermute | solution.py:322
  87.0 1.0 copy-start.13
  94.6 11.6 %collective-permute-start.10 = (bf16[16,4096]{1,0:T(8,128)(2,1)S(1)}, bf16[16,4096]{1,0:T(8,128)(2,1)S(1)}, u32[]{:S(2)}, u32[]{:S(2)}) collective-permute-start(bf16[16,4096]{1,0:T(8,128)(2,1)S(1)} %slice.56), channel_id=1, source_target_pairs={{4,8},{12,16},{20,24},{5,9},{13,17},{21,25},{6,10},{14,18},{22,26}... | collective-permute-start | bytes 393224 | tf_op jit(solution)/shard_map/ppermute | solution.py:397
  95.2 10.9 %collective-permute-start.11 = (bf16[16,4096]{1,0:T(8,128)(2,1)S(1)}, bf16[16,4096]{1,0:T(8,128)(2,1)S(1)}, u32[]{:S(2)}, u32[]{:S(2)}) collective-permute-start(bf16[16,4096]{1,0:T(8,128)(2,1)S(1)} %slice.56), channel_id=1, source_target_pairs={{4,12},{12,20},{20,28},{5,13},{13,21},{21,29},{6,14},{14,22},{22,3... | collective-permute-start | bytes 393224 | tf_op jit(solution)/shard_map/ppermute | solution.py:397
  106.1 12.1 %copy-start.3 = (s32[8]{0:T(128)S(1)}, s32[8]{0:T(128)}, u32[]{:S(2)}) copy-start(s32[8]{0:T(128)} %stack.55.at_ref._) | copy-start | bytes 100
  111.0 11.3 %collective-permute-start.12 = (bf16[512,4096]{1,0:T(8,128)(2,1)}, bf16[512,4096]{1,0:T(8,128)(2,1)}, u32[]{:S(2)}, u32[]{:S(2)}) collective-permute-start(bf16[512,4096]{1,0:T(8,128)(2,1)} %all-gather.2.cloned.1.call-done.refs_0_.x_ref), channel_id=1, source_target_pairs={{0,4},{4,0},{8,12},{12,8},{16,20},{20,16},{24,28},{28,24},{1,5},{5... | collective-permute-start | bytes 12582920 | tf_op jit(solution)/shard_map/ppermute | solution.py:325
  113.0 29.3 %collective-permute-start.13 = (bf16[512,512]{1,0:T(8,128)(2,1)}, bf16[512,512]{1,0:T(8,128)(2,1)}, u32[]{:S(2)}, u32[]{:S(2)}) collective-permute-start(bf16[512,512]{1,0:T(8,128)(2,1)} %slice_bitcast_fusion.1), channel_id=1, source_target_pairs={{16,0},{20,4},{24,8},{28,12},{0,16},{4,20},{8,24},{12,28},{17,1},{... | collective-permute-start | bytes 1572872 | tf_op jit(solution)/shard_map/ppermute | solution.py:322
  115.5 26.8 %collective-permute-start.14 = (bf16[512,512]{1,0:T(8,128)(2,1)}, bf16[512,512]{1,0:T(8,128)(2,1)}, u32[]{:S(2)}, u32[]{:S(2)}) collective-permute-start(bf16[512,512]{1,0:T(8,128)(2,1)} %slice_bitcast_fusion), channel_id=1, source_target_pairs={{8,0},{12,4},{0,8},{4,12},{24,16},{28,20},{16,24},{20,28},{9,1},{1... | collective-permute-start | bytes 1572872 | tf_op jit(solution)/shard_map/ppermute | solution.py:322
  115.5 39.0 %collective-permute-start.17 = (bf16[1024,512]{1,0:T(8,128)(2,1)}, bf16[1024,512]{1,0:T(8,128)(2,1)}, u32[]{:S(2)}, u32[]{:S(2)}) collective-permute-start(bf16[1024,512]{1,0:T(8,128)(2,1)} %refs_4_.1), channel_id=1, source_target_pairs={{8,0},{12,4},{0,8},{4,12},{24,16},{28,20},{16,24},{20,28},{9,1},{1... | collective-permute-start | bytes 3145736 | tf_op jit(solution)/shard_map/ppermute | solution.py:322
  117.5 37.0 %collective-permute-start.18 = (bf16[1024,512]{1,0:T(8,128)(2,1)}, bf16[1024,512]{1,0:T(8,128)(2,1)}, u32[]{:S(2)}, u32[]{:S(2)}) collective-permute-start(bf16[1024,512]{1,0:T(8,128)(2,1)} %refs_4_.1), channel_id=1, source_target_pairs={{16,0},{20,4},{24,8},{28,12},{0,16},{4,20},{8,24},{12,28},{17,1},{... | collective-permute-start | bytes 3145736 | tf_op jit(solution)/shard_map/ppermute | solution.py:322
  122.2 9.8 %copy-start.1 = (f32[512,512]{1,0:T(8,128)S(1)}, f32[512,512]{1,0:T(8,128)}, u32[]{:S(2)}) copy-start(f32[512,512]{1,0:T(8,128)} %shard_map.64.product_ref) | copy-start | bytes 3145732
  122.2 10.6 %copy-start.4 = (s32[8]{0:T(128)S(1)}, s32[8]{0:T(128)}, u32[]{:S(2)}) copy-start(s32[8]{0:T(128)} %stack.55.at_ref._) | copy-start | bytes 100
  132.8 1.2 copy-start.2
  145.5 3.9 %collective-permute-start.15 = (bf16[512,512]{1,0:T(8,128)(2,1)S(1)}, bf16[512,512]{1,0:T(8,128)(2,1)S(1)}, u32[]{:S(2)}, u32[]{:S(2)}) collective-permute-start(bf16[512,512]{1,0:T(8,128)(2,1)S(1)} %shard_map.71.refs_2_), channel_id=1, source_target_pairs={{0,4},{4,0},{8,12},{12,8},{16,20},{20,16},{24,28},{28,24},{1,5},{5... | collective-permute-start | bytes 1572872 | tf_op jit(solution)/shard_map/ppermute | solution.py:325
  148.7 2.1 collective-permute-start.16
  160.4 14.3 %collective-permute-start.20 = (bf16[512,512]{1,0:T(8,128)(2,1)S(1)}, bf16[512,512]{1,0:T(8,128)(2,1)S(1)}, u32[]{:S(2)}, u32[]{:S(2)}) collective-permute-start(bf16[512,512]{1,0:T(8,128)(2,1)S(1)} %slice.81), channel_id=1, source_target_pairs={{16,0},{20,4},{24,8},{28,12},{0,16},{4,20},{8,24},{12,28},{17,1},{... | collective-permute-start | bytes 1572872 | tf_op jit(solution)/shard_map/ppermute | solution.py:322
  163.3 14.0 %collective-permute-start.21 = (bf16[512,512]{1,0:T(8,128)(2,1)S(1)}, bf16[512,512]{1,0:T(8,128)(2,1)S(1)}, u32[]{:S(2)}, u32[]{:S(2)}) collective-permute-start(bf16[512,512]{1,0:T(8,128)(2,1)S(1)} %slice.82), channel_id=1, source_target_pairs={{8,0},{12,4},{0,8},{4,12},{24,16},{28,20},{16,24},{20,28},{9,1},{1... | collective-permute-start | bytes 1572872 | tf_op jit(solution)/shard_map/ppermute | solution.py:322
  179.2 15.4 %collective-permute-start.22 = (bf16[256,512]{1,0:T(8,128)(2,1)S(1)}, bf16[256,512]{1,0:T(8,128)(2,1)S(1)}, u32[]{:S(2)}, u32[]{:S(2)}) collective-permute-start(bf16[256,512]{1,0:T(8,128)(2,1)S(1)} %get-tuple-element.88), channel_id=1, source_target_pairs={{0,1},{1,2},{2,3},{4,5},{5,6},{6,7},{8,9},{9,10},{10,11},{12,13},{... | collective-permute-start | bytes 786440 | tf_op jit(solution)/shard_map/ppermute | solution.py:453
  182.7 21.7 %collective-permute-start.25 = (bf16[256,512]{1,0:T(8,128)(2,1)S(1)}, bf16[256,512]{1,0:T(8,128)(2,1)S(1)}, u32[]{:S(2)}, u32[]{:S(2)}) collective-permute-start(bf16[256,512]{1,0:T(8,128)(2,1)S(1)} %get-tuple-element.86), channel_id=1, source_target_pairs={{1,0},{2,1},{3,2},{5,4},{6,5},{7,6},{9,8},{10,9},{11,10},{13,12},{... | collective-permute-start | bytes 786440 | tf_op jit(solution)/shard_map/ppermute | solution.py:454
  204.5 14.8 %collective-permute-start.23 = (bf16[256,512]{1,0:T(8,128)(2,1)S(1)}, bf16[256,512]{1,0:T(8,128)(2,1)S(1)}, u32[]{:S(2)}, u32[]{:S(2)}) collective-permute-start(bf16[256,512]{1,0:T(8,128)(2,1)S(1)} %get-tuple-element.103), channel_id=1, source_target_pairs={{0,1},{1,2},{2,3},{4,5},{5,6},{6,7},{8,9},{9,10},{10,11},{12,13},{... | collective-permute-start | bytes 786440 | tf_op jit(solution)/shard_map/ppermute | solution.py:453
  207.3 20.5 %collective-permute-start.26 = (bf16[256,512]{1,0:T(8,128)(2,1)S(1)}, bf16[256,512]{1,0:T(8,128)(2,1)S(1)}, u32[]{:S(2)}, u32[]{:S(2)}) collective-permute-start(bf16[256,512]{1,0:T(8,128)(2,1)S(1)} %get-tuple-element.104), channel_id=1, source_target_pairs={{1,0},{2,1},{3,2},{5,4},{6,5},{7,6},{9,8},{10,9},{11,10},{13,12},{... | collective-permute-start | bytes 786440 | tf_op jit(solution)/shard_map/ppermute | solution.py:454
  219.5 14.2 %collective-permute-start.24 = (bf16[256,512]{1,0:T(8,128)(2,1)S(1)}, bf16[256,512]{1,0:T(8,128)(2,1)S(1)}, u32[]{:S(2)}, u32[]{:S(2)}) collective-permute-start(bf16[256,512]{1,0:T(8,128)(2,1)S(1)} %add_convert_fusion.1), channel_id=1, source_target_pairs={{0,1},{1,2},{2,3},{4,5},{5,6},{6,7},{8,9},{9,10},{10,11},{12,13},{... | collective-permute-start | bytes 786440 | tf_op jit(solution)/shard_map/ppermute | solution.py:453
  227.9 10.3 %collective-permute-start.27 = (bf16[256,512]{1,0:T(8,128)(2,1)S(1)}, bf16[256,512]{1,0:T(8,128)(2,1)S(1)}, u32[]{:S(2)}, u32[]{:S(2)}) collective-permute-start(bf16[256,512]{1,0:T(8,128)(2,1)S(1)} %add_convert_fusion), channel_id=1, source_target_pairs={{1,0},{2,1},{3,2},{5,4},{6,5},{7,6},{9,8},{10,9},{11,10},{13,12},{... | collective-permute-start | bytes 786440 | tf_op jit(solution)/shard_map/ppermute | solution.py:454
  232.6 7.3 %collective-permute-start.19 = (bf16[128,1536]{1,0:T(8,128)(2,1)S(1)}, bf16[128,1536]{1,0:T(8,128)(2,1)S(1)}, u32[]{:S(2)}, u32[]{:S(2)}) collective-permute-start(bf16[128,1536]{1,0:T(8,128)(2,1)S(1)} %get-tuple-element.98), channel_id=1, source_target_pairs={{0,4},{4,0},{8,12},{12,8},{16,20},{20,16},{24,28},{28,24},{1,5},{5... | collective-permute-start | bytes 1179656 | tf_op jit(solution)/shard_map/ppermute | solution.py:325
  238.4 1.7 copy-start.15
  238.4 1.4 collective-permute-start.28
  239.9 1.2 copy-start.6
  239.9 1.9 copy-start.14
  241.8 1.5 slice-start
  242.3 1.0 copy-start.16
Sparse Core Ops, SparseCore 0:
  10.2 83.4 all-gather.1
  159.5 71.8 reduce-scatter.1

commit v14 on v12

--- a/solution.py
+++ b/solution.py
@@ -396,21 +396,11 @@
 
     position = lax.axis_index("tp")
     here_at = jnp.stack([core, position]).astype(jnp.int32)
-    up = [(i, i + 1) for i in range(n_tp - 1)]
-    down = [(i + 1, i) for i in range(n_tp - 1)]
-
-    def plus(a, b):
-        return (a.astype(F32) + b.astype(F32)).astype(BF16)
-
-    def chained(slots):
-        rising = falling = None
-        for step in range(n_tp - 1):
-            send_up, send_down = slots[n_tp - 1 - step], slots[step + 1]
-            if step:
-                send_up, send_down = plus(send_up, rising), plus(send_down, falling)
-            rising = lax.ppermute(send_up, "tp", up)
-            falling = lax.ppermute(send_down, "tp", down)
-        total = slots[0].astype(F32) + rising.astype(F32) + falling.astype(F32)
+    def collected(slots):
+        total = slots[0].astype(F32)
+        for away in range(1, n_tp):
+            route = [(i, (i + away) % n_tp) for i in range(n_tp)]
+            total = total + lax.ppermute(slots[away], "tp", route).astype(F32)
         return total
 
     near = {(0, 0): (out_weight,)}
@@ -418,10 +408,14 @@
     found = near_terms(n_tp, here_at, gates, [block for (block,) in near.values()])
     gates, found = lax.optimization_barrier((gates, found))
     near_sum = lax.psum_scatter(found, "tp", scatter_dimension=0, tiled=True)
-    far_sum = chained(terms(n_tp, here_at, gates, list(o_rest.values()), True))
+    far_sum = collected(terms(n_tp, here_at, gates, list(o_rest.values()), True))
     result = jnp.zeros((rows, model), BF16)
-    for keys, mixed in ((list(near), near_sum), (list(o_rest), far_sum)):
-        theirs = from_partner(mixed[rows:].astype(BF16)).astype(F32)
+    far_theirs = from_partner(far_sum[rows:].astype(BF16))
+    near_sum, far_theirs, far_sum = lax.optimization_barrier((near_sum, far_theirs, far_sum))
+    near_theirs = from_partner(near_sum[rows:].astype(BF16))
+    parts = (list(o_rest), far_sum, far_theirs), (list(near), near_sum, near_theirs)
+    for keys, mixed, theirs in parts:
+        theirs = theirs.astype(F32)
         mine = mixed[:rows].astype(F32)
         for index, (dy, dx) in enumerate(keys):
             start = place(my_y + dy, my_x + dx, 0) * wide

time: 248 us -> 252 us (1.016); the launches traced: 247 us -> 248 us
  waiting for transfers between devices: 131 us -> 144 us
  starting transfers between devices: 37.5 us -> 25.1 us
    ppermute x6 -> x3, waiting for transfers between devices: 36.2 us -> 49.8 us  [collected(): total = total + lax.ppermute(slots[away], 'tp', route).astype(F32)]
    ppermute x6 -> x3, starting transfers between devices: 16.5 us -> 4.58 us  [collected(): total = total + lax.ppermute(slots[away], 'tp', route).astype(F32)]
  transfers between devices with their start and end apart: 31 -> 28, of which waited for: 17 -> 16; matrix products, arithmetic and copies ran while one was open for 4% -> 4% of each run, Pallas kernels for 16% -> 16%
where the time goes in v14:
time: 252 us; the launch traced here: 248 us
  waiting for transfers between devices  144 us (57%)
  Pallas kernels  46.3 us (18%)
  starting transfers between devices  25.1 us (10%)
  between operations  14 us (6%)
  local copies, waits for them, and re-layouts  11.2 us (4%)
  other arithmetic  7.32 us (3%)
    ppermute x14, waiting for transfers between devices, from_chip(): return lax.ppermute(block, 'seq', route)  82.4 us
    ppermute x3, waiting for transfers between devices, collected(): total = total + lax.ppermute(slots[away], 'tp', route).astype(F32)  49.8 us
    pallas_call x7, Pallas kernels, call(): pl.pallas_call(kernel, out_shape=out, in_specs=[pl.BlockSpec(memory_space...  20.6 us
    pallas_call x2, Pallas kernels, products(): pl.pallas_call(functools.partial(product_kernel, len(xs), len(pieces)), o...  19.2 us
    ppermute x14, starting transfers between devices, from_chip(): return lax.ppermute(block, 'seq', route)  16.6 us
    pallas_call x1, Pallas kernels, near_terms(): pl.pallas_call(functools.partial(near_kernel, n_tp), out_shape=jax.ShapeD...  6.61 us
    all_gather x1, waiting for transfers between devices, on_device(): own_rows = lax.all_gather(normed, 'tp', axis=0, tiled=True)  5.06 us
  transfers between devices with their start and end apart: 28, of which 16 were waited for; matrix products, arithmetic and copies ran while one was open for 4% of the time, Pallas kernels for 16%

profile of v14, /device:TPU:0, one launch (start us, length us, event | category | flops | bytes accessed | tf_op | source)
XLA Modules:
  0.0 247.6 jit_solution(12771697141554069415)
XLA Ops:
  6.5 1.8 constant_dynamic-slice_fusion.2
  8.4 0.3 fusion
  8.7 1.3 fusion.2
  10.1 0.5 collective-permute-start
  10.6 2.6 %collective-permute-start.1 = (bf16[2,512,512]{2,1,0:T(8,128)(2,1)S(1)}, bf16[2,512,512]{2,1,0:T(8,128)(2,1)S(1)}, u32[]{:S(2)}, u32[]{:S(2)}) collective-permute-start(bf16[2,512,512]{2,1,0:T(8,128)(2,1)S(1)} %get-tuple-element.58.refs_1_.refs_2_), channel_id=1, source_target_pairs={{8,0},{12,4},{0,8},{4,12},{24,16},{28,20},{16,24},{20,28},{9,1},{1... | collective-permute-start | bytes 3145736 | tf_op jit(solution)/shard_map/ppermute | solution.py:276
  13.2 1.5 collective-permute-start.3
  14.7 1.1 collective-permute-start.2
  15.8 1.5 collective-permute-start.4
  17.3 1.3 constant_dynamic-slice_fusion.1
  18.6 1.9 collective-permute-done.5
  20.6 16.5 %collective-permute-done.1.refs_3_.refs_4_ = bf16[2,512,512]{2,1,0:T(8,128)(2,1)S(1)} collective-permute-done((bf16[2,512,512]{2,1,0:T(8,128)(2,1)S(1)}, bf16[2,512,512]{2,1,0:T(8,128)(2,1)S(1)}, u32[]{:S(2)}, u32[]{:S(2)}) %collective-permute-start.1) | collective-permute-done | bytes 1048608 | tf_op jit(solution)/shard_map/ppermute | solution.py:276
  37.2 2.0 collective-permute-done.3.refs_5_.refs_6_
  39.2 20.2 %collective-permute-done.2.refs_4_.refs_5_ = bf16[2,512,512]{2,1,0:T(8,128)(2,1)S(1)} collective-permute-done((bf16[2,512,512]{2,1,0:T(8,128)(2,1)S(1)}, bf16[2,512,512]{2,1,0:T(8,128)(2,1)S(1)}, u32[]{:S(2)}, u32[]{:S(2)}) %collective-permute-start.2) | collective-permute-done | bytes 1048608 | tf_op jit(solution)/shard_map/ppermute | solution.py:276
  59.4 1.5 collective-permute-done.4.refs_6_.refs_7_
  60.9 1.5 collective-permute-start.6
  62.4 0.5 collective-permute-start.7
  62.9 1.5 collective-permute-start.8
  64.4 0.5 collective-permute-start.9
  64.9 22.0 %collective-permute-done.6.refs_7_.refs_8_ = bf16[2,512,512]{2,1,0:T(8,128)(2,1)S(1)} collective-permute-done((bf16[2,512,512]{2,1,0:T(8,128)(2,1)S(1)}, bf16[2,512,512]{2,1,0:T(8,128)(2,1)S(1)}, u32[]{:S(2)}, u32[]{:S(2)}) %collective-permute-start.6) | collective-permute-done | bytes 1048608 | tf_op jit(solution)/shard_map/ppermute | solution.py:276
  87.0 1.0 copy-done.13
  88.0 0.6 collective-permute-done.7.refs_8_.refs_9_
  88.6 5.1 %all-gather.2.cloned.1.call-done.refs_0_ = bf16[512,4096]{1,0:T(8,128)(2,1)} async-done(((bf16[128,4096]{1,0:T(8,128)(2,1)}), bf16[512,4096]{1,0:T(8,128)(2,1)}) %all-gather.2.cloned.1.call-update) | async-done | bytes 4194320 | tf_op jit(solution)/shard_map/all_gather | solution.py:327
  93.7 0.9 slice.56
  94.6 0.7 collective-permute-start.10
  95.2 0.7 collective-permute-start.11
  96.0 0.6 stack.55.at_ref._
  96.7 9.4 %shard_map.64.product_ref = f32[512,512]{1,0:T(8,128)} custom-call(s32[8]{0:T(128)} %stack.55.at_ref._, bf16[512,4096]{1,0:T(8,128)(2,1)} %all-gather.2.cloned.1.call-done.refs_0_, bf16[2,512,512]{2,1,0:T(8,128)(2,1)} %copy-done.7, bf16[2,512,512]{2,1,0:T(8,128)(2,1)} %copy-done.8, bf16[2,512,512]{2,1,0:T(8,128)(2,1)} %copy-done.9, ...), custom_call_target="tpu_custom_call" | custom-call | flops 1 | bytes 1 | tf_op jit(solution)/shard_map/pallas_call | solution.py:124
  106.1 0.7 broadcast_select_fusion.refs_0_
  106.8 4.2 %collective-permute-done.8.refs_2_ = bf16[2,512,512]{2,1,0:T(8,128)(2,1)S(1)} collective-permute-done((bf16[2,512,512]{2,1,0:T(8,128)(2,1)S(1)}, bf16[2,512,512]{2,1,0:T(8,128)(2,1)S(1)}, u32[]{:S(2)}, u32[]{:S(2)}) %collective-permute-start.8) | collective-permute-done | bytes 1048608 | tf_op jit(solution)/shard_map/ppermute | solution.py:276
  111.0 1.1 collective-permute-start.12
  112.1 0.8 slice_bitcast_fusion.1
  112.9 1.8 collective-permute-start.13
  114.7 0.9 slice_bitcast_fusion
  115.6 2.0 collective-permute-start.17
  117.6 0.3 collective-permute-start.18
  118.2 4.0 %shard_map.65.refs_2_ = f32[512,512]{1,0:T(8,128)S(1)} custom-call(s32[8]{0:T(128)S(1)} %copy-done.3, bf16[512,4096]{1,0:T(8,128)(2,1)} %all-gather.2.cloned.1.call-done.refs_0_, bf16[2,512,512]{2,1,0:T(8,128)(2,1)S(1)} %pad_maximum_fusion.refs_1_, bf16[2,512,512]{2,1,0:T(8,128)(2,1)S(1)} %collective-permute-done.8.refs_2_, ...), custom_call_target="tpu_custom_call" | custom-call | flops 1 | bytes 1 | tf_op jit(solution)/shard_map/pallas_call | solution.py:68
  122.2 9.7 %shard_map.66 = (f32[16,512]{1,0:T(8,128)}, f32[512,512]{1,0:T(8,128)}) custom-call(s32[8]{0:T(128)} %stack.55.at_ref._, bf16[16,4096]{1,0:T(8,128)(2,1)} %broadcast_select_fusion.refs_0_, bf16[512,4096]{1,0:T(8,128)(2,1)} %collective-permute-done.12.refs_1_.refs_0_, bf16[2,512,512]{2,1,0:T(8,128)(2,1)} %copy-done.7, bf16[2,512,512]{2,1,0:T(8,128)(2,1)} %copy-done.8, ...), custom_call_target="tpu_custom_call" | custom-call | flops 1 | bytes 1 | tf_op jit(solution)/shard_map/pallas_call | solution.py:124
  132.0 0.9 broadcast_select_fusion.1
  132.9 2.0 shard_map.67.refs_1_
  134.9 2.0 shard_map.68.refs_1_
  137.0 4.2 %shard_map.70.refs_2_ = f32[512,512]{1,0:T(8,128)S(1)} custom-call(s32[8]{0:T(128)S(1)} %copy-done.4, bf16[512,4096]{1,0:T(8,128)(2,1)} %collective-permute-done.12.refs_1_.refs_0_, bf16[2,512,512]{2,1,0:T(8,128)(2,1)S(1)} %pad_maximum_fusion.refs_1_, bf16[2,512,512]{2,1,0:T(8,128)(2,1)S(1)} %collective-permute-done.8.refs_2_, ...), custom_call_target="tpu_custom_call" | custom-call | flops 1 | bytes 1 | tf_op jit(solution)/shard_map/pallas_call | solution.py:68
  141.2 3.2 %shard_map.71.refs_2_ = bf16[512,512]{1,0:T(8,128)(2,1)S(1)} custom-call(s32[2]{0:T(128)S(1)} %pad_add_fusion.at_ref, bf16[512,4096]{1,0:T(8,128)(2,1)} %collective-permute-done.12.refs_1_.refs_0_, f32[512,512]{1,0:T(8,128)S(1)} %shard_map.68.refs_1_, f32[512,512]{1,0:T(8,128)S(1)} %shard_map.70.refs_2_, bf16[512,512]{1,0:T(8,128)(2,1)} %collective-permute-done.13.refs_3_, ...), custom_call_target="tpu_custom_call" | custom-call | flops 1 | bytes 1 | tf_op jit(solution)/shard_map/pallas_call | solution.py:68
  144.5 3.2 %shard_map.69.refs_0_ = bf16[512,512]{1,0:T(8,128)(2,1)S(1)} custom-call(s32[2]{0:T(128)S(1)} %pad_add_fusion.at_ref, bf16[512,4096]{1,0:T(8,128)(2,1)} %all-gather.2.cloned.1.call-done.refs_0_, f32[512,512]{1,0:T(8,128)S(1)} %shard_map.67.refs_1_, f32[512,512]{1,0:T(8,128)S(1)} %shard_map.65.refs_2_, bf16[512,512]{1,0:T(8,128)(2,1)} %collective-permute-done.13.refs_3_, ...), custom_call_target="tpu_custom_call" | custom-call | flops 1 | bytes 1 | tf_op jit(solution)/shard_map/pallas_call | solution.py:68
  147.7 0.6 collective-permute-start.16
  148.3 3.6 %collective-permute-done.17.refs_5_ = bf16[1024,512]{1,0:T(8,128)(2,1)} collective-permute-done((bf16[1024,512]{1,0:T(8,128)(2,1)}, bf16[1024,512]{1,0:T(8,128)(2,1)}, u32[]{:S(2)}, u32[]{:S(2)}) %collective-permute-start.17) | collective-permute-done | bytes 1048608 | tf_op jit(solution)/shard_map/ppermute | solution.py:276
  151.9 6.6 %shard_map.72 = bf16[1024,1536]{1,0:T(8,128)(2,1)} custom-call(s32[2]{0:T(128)S(1)} %pad_add_fusion.1.at_ref, bf16[512,512]{1,0:T(8,128)(2,1)S(1)} %shard_map.69.refs_0_, bf16[512,512]{1,0:T(8,128)(2,1)S(1)} %collective-permute-done.15.refs_1_, bf16[512,512]{1,0:T(8,128)(2,1)S(1)} %shard_map.71.refs_2_, ...), custom_call_target="tpu_custom_call" | custom-call | flops 1 | bytes 1 | tf_op jit(solution)/shard_map/pallas_call | solution.py:237
  158.6 1.1 slice.73
  159.6 0.3 collective-permute-start.19
  160.0 1.1 slice.74
  161.1 1.5 collective-permute-start.20
  162.6 9.8 %collective-permute-done.19.refs_4_ = bf16[512,512]{1,0:T(8,128)(2,1)S(1)} collective-permute-done((bf16[512,512]{1,0:T(8,128)(2,1)S(1)}, bf16[512,512]{1,0:T(8,128)(2,1)S(1)}, u32[]{:S(2)}, u32[]{:S(2)}) %collective-permute-start.19) | collective-permute-done | bytes 524320 | tf_op jit(solution)/shard_map/ppermute | solution.py:276
  172.4 2.0 collective-permute-done.20.refs_5_
  174.4 1.9 shard_map.73
  176.3 3.7 %collective-permute-start.23 = (bf16[256,512]{1,0:T(8,128)(2,1)S(1)}, bf16[256,512]{1,0:T(8,128)(2,1)S(1)}, u32[]{:S(2)}, u32[]{:S(2)}) collective-permute-start(bf16[256,512]{1,0:T(8,128)(2,1)S(1)} %get-tuple-element.87), channel_id=1, source_target_pairs={{0,3},{1,0},{2,1},{3,2},{4,7},{5,4},{6,5},{7,6},{8,11},{9,8},{10,9... | collective-permute-start | bytes 786440 | tf_op jit(solution)/shard_map/ppermute | solution.py:403
  180.0 0.9 collective-permute-start.21
  180.9 14.1 %collective-permute-done.23 = bf16[256,512]{1,0:T(8,128)(2,1)S(1)} collective-permute-done((bf16[256,512]{1,0:T(8,128)(2,1)S(1)}, bf16[256,512]{1,0:T(8,128)(2,1)S(1)}, u32[]{:S(2)}, u32[]{:S(2)}) %collective-permute-start.23) | collective-permute-done | bytes 262176 | tf_op jit(solution)/shard_map/ppermute | solution.py:403
  194.9 35.8 %collective-permute-done.22 = bf16[256,512]{1,0:T(8,128)(2,1)S(1)} collective-permute-done((bf16[256,512]{1,0:T(8,128)(2,1)S(1)}, bf16[256,512]{1,0:T(8,128)(2,1)S(1)}, u32[]{:S(2)}, u32[]{:S(2)}) %collective-permute-start.22) | collective-permute-done | bytes 262176 | tf_op jit(solution)/shard_map/ppermute | solution.py:403
  231.0 1.3 collective-permute-done.24
  232.3 3.0 %reduce-scatter.2.cloned.1.call-done = bf16[256,1536]{1,0:T(8,128)(2,1)} async-done(((bf16[1024,1536]{1,0:T(8,128)(2,1)}), bf16[256,1536]{1,0:T(8,128)(2,1)}) %reduce-scatter.2.cloned.1.call-update) | async-done | bytes 786448 | tf_op jit(solution)/shard_map/reduce_scatter | solution.py:410
  235.3 1.2 fusion.24
  236.8 1.4 fusion.22
  238.7 0.2 fusion.20
  238.9 1.0 copy-done.15
  239.9 0.9 fusion.19
  (69 shorter events, 1.8 us)
Async XLA Ops:
  6.5 111.3 %copy-start = (f32[7,64]{1,0:T(8,128)S(1)}, f32[7,64]{1,0:T(8,128)}, u32[]{:S(2)}) copy-start(f32[7,64]{1,0:T(8,128)} %param.9) | copy-start | bytes 5380
  6.5 87.1 %all-gather.2.cloned.1.call-start = ((), (), s32[]{:S(2)}) async-start(), calls=%async_computation.1 | async-start | bytes 5242880 | tf_op jit(solution)/shard_map/all_gather | solution.py:327
  6.5 1.9 copy-start.5
  6.5 2.2 copy-start.16
  8.4 4.8 %copy-start.7 = (bf16[2,512,512]{2,1,0:T(8,128)(2,1)}, bf16[2,512,512]{2,1,0:T(8,128)(2,1)S(1)}, u32[]{:S(2)}) copy-start(bf16[2,512,512]{2,1,0:T(8,128)(2,1)S(1)} %get-tuple-element.58.refs_1_.refs_2_) | copy-start | bytes 3145732
  10.0 225.3 %reduce-scatter.2.cloned.1.call-start = ((), (), s32[]{:S(2)}) async-start(), calls=%async_computation.2 | async-start | bytes 3932160 | tf_op jit(solution)/shard_map/reduce_scatter | solution.py:410
  10.1 4.6 %collective-permute-start = (bf16[2,512,512]{2,1,0:T(8,128)(2,1)S(1)}, bf16[2,512,512]{2,1,0:T(8,128)(2,1)S(1)}, u32[]{:S(2)}, u32[]{:S(2)}) collective-permute-start(bf16[2,512,512]{2,1,0:T(8,128)(2,1)S(1)} %get-tuple-element.94), channel_id=1, source_target_pairs={{0,4},{4,0},{8,12},{12,8},{16,20},{20,16},{24,28},{28,24},{1,5},{5... | collective-permute-start | bytes 3145736 | tf_op jit(solution)/shard_map/ppermute | solution.py:279
  10.6 26.6 %collective-permute-start.1 = (bf16[2,512,512]{2,1,0:T(8,128)(2,1)S(1)}, bf16[2,512,512]{2,1,0:T(8,128)(2,1)S(1)}, u32[]{:S(2)}, u32[]{:S(2)}) collective-permute-start(bf16[2,512,512]{2,1,0:T(8,128)(2,1)S(1)} %get-tuple-element.58.refs_1_.refs_2_), channel_id=1, source_target_pairs={{8,0},{12,4},{0,8},{4,12},{24,16},{28,20},{16,24},{20,28},{9,1},{1... | collective-permute-start | bytes 3145736 | tf_op jit(solution)/shard_map/ppermute | solution.py:276
  13.2 26.0 %collective-permute-start.3 = (bf16[2,512,512]{2,1,0:T(8,128)(2,1)S(1)}, bf16[2,512,512]{2,1,0:T(8,128)(2,1)S(1)}, u32[]{:S(2)}, u32[]{:S(2)}) collective-permute-start(bf16[2,512,512]{2,1,0:T(8,128)(2,1)S(1)} %get-tuple-element.58.refs_1_.refs_2_), channel_id=1, source_target_pairs={{16,0},{20,4},{24,8},{28,12},{0,16},{4,20},{8,24},{12,28},{17,1},{... | collective-permute-start | bytes 3145736 | tf_op jit(solution)/shard_map/ppermute | solution.py:276
  14.7 5.9 %copy-start.8 = (bf16[2,512,512]{2,1,0:T(8,128)(2,1)}, bf16[2,512,512]{2,1,0:T(8,128)(2,1)S(1)}, u32[]{:S(2)}) copy-start(bf16[2,512,512]{2,1,0:T(8,128)(2,1)S(1)} %collective-permute-done.refs_2_.refs_3_) | copy-start | bytes 3145732
  14.7 44.7 %collective-permute-start.2 = (bf16[2,512,512]{2,1,0:T(8,128)(2,1)S(1)}, bf16[2,512,512]{2,1,0:T(8,128)(2,1)S(1)}, u32[]{:S(2)}, u32[]{:S(2)}) collective-permute-start(bf16[2,512,512]{2,1,0:T(8,128)(2,1)S(1)} %collective-permute-done.refs_2_.refs_3_), channel_id=1, source_target_pairs={{8,0},{12,4},{0,8},{4,12},{24,16},{28,20},{16,24},{20,28},{9,1},{1... | collective-permute-start | bytes 3145736 | tf_op jit(solution)/shard_map/ppermute | solution.py:276
  15.8 45.1 %collective-permute-start.4 = (bf16[2,512,512]{2,1,0:T(8,128)(2,1)S(1)}, bf16[2,512,512]{2,1,0:T(8,128)(2,1)S(1)}, u32[]{:S(2)}, u32[]{:S(2)}) collective-permute-start(bf16[2,512,512]{2,1,0:T(8,128)(2,1)S(1)} %collective-permute-done.refs_2_.refs_3_), channel_id=1, source_target_pairs={{16,0},{20,4},{24,8},{28,12},{0,16},{4,20},{8,24},{12,28},{17,1},{... | collective-permute-start | bytes 3145736 | tf_op jit(solution)/shard_map/ppermute | solution.py:276
  18.5 2.0 collective-permute-start.5
  37.2 25.8 %copy-start.9 = (bf16[2,512,512]{2,1,0:T(8,128)(2,1)}, bf16[2,512,512]{2,1,0:T(8,128)(2,1)S(1)}, u32[]{:S(2)}) copy-start(bf16[2,512,512]{2,1,0:T(8,128)(2,1)S(1)} %collective-permute-done.1.refs_3_.refs_4_) | copy-start | bytes 3145732
  39.2 47.8 %copy-start.10 = (bf16[2,512,512]{2,1,0:T(8,128)(2,1)}, bf16[2,512,512]{2,1,0:T(8,128)(2,1)S(1)}, u32[]{:S(2)}) copy-start(bf16[2,512,512]{2,1,0:T(8,128)(2,1)S(1)} %collective-permute-done.3.refs_5_.refs_6_) | copy-start | bytes 3145732
  59.4 27.6 %copy-start.11 = (bf16[2,512,512]{2,1,0:T(8,128)(2,1)}, bf16[2,512,512]{2,1,0:T(8,128)(2,1)S(1)}, u32[]{:S(2)}) copy-start(bf16[2,512,512]{2,1,0:T(8,128)(2,1)S(1)} %collective-permute-done.2.refs_4_.refs_5_) | copy-start | bytes 3145732
  60.9 26.1 %copy-start.12 = (bf16[2,512,512]{2,1,0:T(8,128)(2,1)}, bf16[2,512,512]{2,1,0:T(8,128)(2,1)S(1)}, u32[]{:S(2)}) copy-start(bf16[2,512,512]{2,1,0:T(8,128)(2,1)S(1)} %collective-permute-done.4.refs_6_.refs_7_) | copy-start | bytes 3145732
  60.9 26.1 %collective-permute-start.6 = (bf16[2,512,512]{2,1,0:T(8,128)(2,1)S(1)}, bf16[2,512,512]{2,1,0:T(8,128)(2,1)S(1)}, u32[]{:S(2)}, u32[]{:S(2)}) collective-permute-start(bf16[2,512,512]{2,1,0:T(8,128)(2,1)S(1)} %collective-permute-done.1.refs_3_.refs_4_), channel_id=1, source_target_pairs={{16,0},{20,4},{24,8},{28,12},{0,16},{4,20},{8,24},{12,28},{17,1},{... | collective-permute-start | bytes 3145736 | tf_op jit(solution)/shard_map/ppermute | solution.py:276
  62.4 26.2 %collective-permute-start.7 = (bf16[2,512,512]{2,1,0:T(8,128)(2,1)S(1)}, bf16[2,512,512]{2,1,0:T(8,128)(2,1)}, u32[]{:S(2)}, u32[]{:S(2)}) collective-permute-start(bf16[2,512,512]{2,1,0:T(8,128)(2,1)S(1)} %collective-permute-done.4.refs_6_.refs_7_), channel_id=1, source_target_pairs={{8,0},{12,4},{0,8},{4,12},{24,16},{28,20},{16,24},{20,28},{9,1},{1... | collective-permute-start | bytes 3145736 | tf_op jit(solution)/shard_map/ppermute | solution.py:276
  62.9 48.0 %collective-permute-start.8 = (bf16[2,512,512]{2,1,0:T(8,128)(2,1)S(1)}, bf16[2,512,512]{2,1,0:T(8,128)(2,1)S(1)}, u32[]{:S(2)}, u32[]{:S(2)}) collective-permute-start(bf16[2,512,512]{2,1,0:T(8,128)(2,1)S(1)} %pad_maximum_fusion.refs_1_), channel_id=1, source_target_pairs={{8,0},{12,4},{0,8},{4,12},{24,16},{28,20},{16,24},{20,28},{9,1},{1... | collective-permute-start | bytes 3145736 | tf_op jit(solution)/shard_map/ppermute | solution.py:276
  64.4 46.5 %collective-permute-start.9 = (bf16[2,512,512]{2,1,0:T(8,128)(2,1)S(1)}, bf16[2,512,512]{2,1,0:T(8,128)(2,1)S(1)}, u32[]{:S(2)}, u32[]{:S(2)}) collective-permute-start(bf16[2,512,512]{2,1,0:T(8,128)(2,1)S(1)} %pad_maximum_fusion.refs_1_), channel_id=1, source_target_pairs={{16,0},{20,4},{24,8},{28,12},{0,16},{4,20},{8,24},{12,28},{17,1},{... | collective-permute-start | bytes 3145736 | tf_op jit(solution)/shard_map/ppermute | solution.py:276
  87.0 1.0 copy-start.13
  94.6 11.5 %collective-permute-start.10 = (bf16[16,4096]{1,0:T(8,128)(2,1)S(1)}, bf16[16,4096]{1,0:T(8,128)(2,1)S(1)}, u32[]{:S(2)}, u32[]{:S(2)}) collective-permute-start(bf16[16,4096]{1,0:T(8,128)(2,1)S(1)} %slice.56), channel_id=1, source_target_pairs={{4,8},{12,16},{20,24},{5,9},{13,17},{21,25},{6,10},{14,18},{22,26}... | collective-permute-start | bytes 393224 | tf_op jit(solution)/shard_map/ppermute | solution.py:351
  95.2 10.9 %collective-permute-start.11 = (bf16[16,4096]{1,0:T(8,128)(2,1)S(1)}, bf16[16,4096]{1,0:T(8,128)(2,1)S(1)}, u32[]{:S(2)}, u32[]{:S(2)}) collective-permute-start(bf16[16,4096]{1,0:T(8,128)(2,1)S(1)} %slice.56), channel_id=1, source_target_pairs={{4,12},{12,20},{20,28},{5,13},{13,21},{21,29},{6,14},{14,22},{22,3... | collective-permute-start | bytes 393224 | tf_op jit(solution)/shard_map/ppermute | solution.py:351
  106.1 12.1 %copy-start.3 = (s32[8]{0:T(128)S(1)}, s32[8]{0:T(128)}, u32[]{:S(2)}) copy-start(s32[8]{0:T(128)} %stack.55.at_ref._) | copy-start | bytes 100
  111.0 11.3 %collective-permute-start.12 = (bf16[512,4096]{1,0:T(8,128)(2,1)}, bf16[512,4096]{1,0:T(8,128)(2,1)}, u32[]{:S(2)}, u32[]{:S(2)}) collective-permute-start(bf16[512,4096]{1,0:T(8,128)(2,1)} %all-gather.2.cloned.1.call-done.refs_0_), channel_id=1, source_target_pairs={{0,4},{4,0},{8,12},{12,8},{16,20},{20,16},{24,28},{28,24},{1,5},{5... | collective-permute-start | bytes 12582920 | tf_op jit(solution)/shard_map/ppermute | solution.py:279
  112.9 28.2 %collective-permute-start.13 = (bf16[512,512]{1,0:T(8,128)(2,1)}, bf16[512,512]{1,0:T(8,128)(2,1)}, u32[]{:S(2)}, u32[]{:S(2)}) collective-permute-start(bf16[512,512]{1,0:T(8,128)(2,1)} %slice_bitcast_fusion.1), channel_id=1, source_target_pairs={{16,0},{20,4},{24,8},{28,12},{0,16},{4,20},{8,24},{12,28},{17,1},{... | collective-permute-start | bytes 1572872 | tf_op jit(solution)/shard_map/ppermute | solution.py:276
  115.6 25.6 %collective-permute-start.14 = (bf16[512,512]{1,0:T(8,128)(2,1)}, bf16[512,512]{1,0:T(8,128)(2,1)}, u32[]{:S(2)}, u32[]{:S(2)}) collective-permute-start(bf16[512,512]{1,0:T(8,128)(2,1)} %slice_bitcast_fusion), channel_id=1, source_target_pairs={{8,0},{12,4},{0,8},{4,12},{24,16},{28,20},{16,24},{20,28},{9,1},{1... | collective-permute-start | bytes 1572872 | tf_op jit(solution)/shard_map/ppermute | solution.py:276
  115.6 36.3 %collective-permute-start.17 = (bf16[1024,512]{1,0:T(8,128)(2,1)}, bf16[1024,512]{1,0:T(8,128)(2,1)}, u32[]{:S(2)}, u32[]{:S(2)}) collective-permute-start(bf16[1024,512]{1,0:T(8,128)(2,1)} %refs_4_.1), channel_id=1, source_target_pairs={{8,0},{12,4},{0,8},{4,12},{24,16},{28,20},{16,24},{20,28},{9,1},{1... | collective-permute-start | bytes 3145736 | tf_op jit(solution)/shard_map/ppermute | solution.py:276
  117.6 34.3 %collective-permute-start.18 = (bf16[1024,512]{1,0:T(8,128)(2,1)}, bf16[1024,512]{1,0:T(8,128)(2,1)}, u32[]{:S(2)}, u32[]{:S(2)}) collective-permute-start(bf16[1024,512]{1,0:T(8,128)(2,1)} %refs_4_.1), channel_id=1, source_target_pairs={{16,0},{20,4},{24,8},{28,12},{0,16},{4,20},{8,24},{12,28},{17,1},{... | collective-permute-start | bytes 3145736 | tf_op jit(solution)/shard_map/ppermute | solution.py:276
  122.2 9.8 %copy-start.1 = (f32[512,512]{1,0:T(8,128)S(1)}, f32[512,512]{1,0:T(8,128)}, u32[]{:S(2)}) copy-start(f32[512,512]{1,0:T(8,128)} %shard_map.64.product_ref) | copy-start | bytes 3145732
  122.2 10.7 %copy-start.4 = (s32[8]{0:T(128)S(1)}, s32[8]{0:T(128)}, u32[]{:S(2)}) copy-start(s32[8]{0:T(128)} %stack.55.at_ref._) | copy-start | bytes 100
  132.0 2.9 %copy-start.2 = (f32[512,512]{1,0:T(8,128)S(1)}, f32[512,512]{1,0:T(8,128)}, u32[]{:S(2)}) copy-start(f32[512,512]{1,0:T(8,128)} %get-tuple-element.73.product_ref) | copy-start | bytes 3145732
  144.4 7.5 %collective-permute-start.15 = (bf16[512,512]{1,0:T(8,128)(2,1)S(1)}, bf16[512,512]{1,0:T(8,128)(2,1)S(1)}, u32[]{:S(2)}, u32[]{:S(2)}) collective-permute-start(bf16[512,512]{1,0:T(8,128)(2,1)S(1)} %shard_map.71.refs_2_), channel_id=1, source_target_pairs={{0,4},{4,0},{8,12},{12,8},{16,20},{20,16},{24,28},{28,24},{1,5},{5... | collective-permute-start | bytes 1572872 | tf_op jit(solution)/shard_map/ppermute | solution.py:279
  147.7 4.2 %collective-permute-start.16 = (bf16[512,512]{1,0:T(8,128)(2,1)S(1)}, bf16[512,512]{1,0:T(8,128)(2,1)S(1)}, u32[]{:S(2)}, u32[]{:S(2)}) collective-permute-start(bf16[512,512]{1,0:T(8,128)(2,1)S(1)} %shard_map.69.refs_0_), channel_id=1, source_target_pairs={{0,4},{4,0},{8,12},{12,8},{16,20},{20,16},{24,28},{28,24},{1,5},{5... | collective-permute-start | bytes 1572872 | tf_op jit(solution)/shard_map/ppermute | solution.py:279
  159.6 12.7 %collective-permute-start.19 = (bf16[512,512]{1,0:T(8,128)(2,1)S(1)}, bf16[512,512]{1,0:T(8,128)(2,1)S(1)}, u32[]{:S(2)}, u32[]{:S(2)}) collective-permute-start(bf16[512,512]{1,0:T(8,128)(2,1)S(1)} %slice.73), channel_id=1, source_target_pairs={{16,0},{20,4},{24,8},{28,12},{0,16},{4,20},{8,24},{12,28},{17,1},{... | collective-permute-start | bytes 1572872 | tf_op jit(solution)/shard_map/ppermute | solution.py:276
  161.1 13.3 %collective-permute-start.20 = (bf16[512,512]{1,0:T(8,128)(2,1)S(1)}, bf16[512,512]{1,0:T(8,128)(2,1)S(1)}, u32[]{:S(2)}, u32[]{:S(2)}) collective-permute-start(bf16[512,512]{1,0:T(8,128)(2,1)S(1)} %slice.74), channel_id=1, source_target_pairs={{8,0},{12,4},{0,8},{4,12},{24,16},{28,20},{16,24},{20,28},{9,1},{1... | collective-permute-start | bytes 1572872 | tf_op jit(solution)/shard_map/ppermute | solution.py:276
  176.3 18.6 %collective-permute-start.23 = (bf16[256,512]{1,0:T(8,128)(2,1)S(1)}, bf16[256,512]{1,0:T(8,128)(2,1)S(1)}, u32[]{:S(2)}, u32[]{:S(2)}) collective-permute-start(bf16[256,512]{1,0:T(8,128)(2,1)S(1)} %get-tuple-element.87), channel_id=1, source_target_pairs={{0,3},{1,0},{2,1},{3,2},{4,7},{5,4},{6,5},{7,6},{8,11},{9,8},{10,9... | collective-permute-start | bytes 786440 | tf_op jit(solution)/shard_map/ppermute | solution.py:403
  180.0 50.8 %collective-permute-start.22 = (bf16[256,512]{1,0:T(8,128)(2,1)S(1)}, bf16[256,512]{1,0:T(8,128)(2,1)S(1)}, u32[]{:S(2)}, u32[]{:S(2)}) collective-permute-start(bf16[256,512]{1,0:T(8,128)(2,1)S(1)} %get-tuple-element.86), channel_id=1, source_target_pairs={{0,2},{1,3},{2,0},{3,1},{4,6},{5,7},{6,4},{7,5},{8,10},{9,11},{10,... | collective-permute-start | bytes 786440 | tf_op jit(solution)/shard_map/ppermute | solution.py:403
  180.0 50.8 %collective-permute-start.21 = (bf16[256,512]{1,0:T(8,128)(2,1)S(1)}, bf16[256,512]{1,0:T(8,128)(2,1)S(1)}, u32[]{:S(2)}, u32[]{:S(2)}) collective-permute-start(bf16[256,512]{1,0:T(8,128)(2,1)S(1)} %get-tuple-element.85), channel_id=1, source_target_pairs={{0,1},{1,2},{2,3},{3,0},{4,5},{5,6},{6,7},{7,4},{8,9},{9,10},{10,1... | collective-permute-start | bytes 786440 | tf_op jit(solution)/shard_map/ppermute | solution.py:403
  230.9 5.9 %copy-start.6 = (bf16[128,4096]{1,0:T(8,128)(2,1)S(1)}, bf16[128,4096]{1,0:T(8,128)(2,1)}, u32[]{:S(2)}) copy-start(bf16[128,4096]{1,0:T(8,128)(2,1)} %param.6) | copy-start | bytes 3145732
  230.9 1.4 collective-permute-start.24
  236.5 1.8 collective-permute-start.25
  236.8 1.8 copy-start.14
  238.9 1.0 copy-start.15
Sparse Core Ops, SparseCore 0:
  10.2 83.4 all-gather.1
  158.7 76.5 reduce-scatter.1

commit v15 on v12

--- a/solution.py
+++ b/solution.py
@@ -420,8 +420,12 @@
     near_sum = lax.psum_scatter(found, "tp", scatter_dimension=0, tiled=True)
     far_sum = chained(terms(n_tp, here_at, gates, list(o_rest.values()), True))
     result = jnp.zeros((rows, model), BF16)
-    for keys, mixed in ((list(near), near_sum), (list(o_rest), far_sum)):
-        theirs = from_partner(mixed[rows:].astype(BF16)).astype(F32)
+    far_theirs = from_partner(far_sum[rows:].astype(BF16))
+    near_sum, far_theirs, far_sum = lax.optimization_barrier((near_sum, far_theirs, far_sum))
+    near_theirs = from_partner(near_sum[rows:].astype(BF16))
+    parts = (list(o_rest), far_sum, far_theirs), (list(near), near_sum, near_theirs)
+    for keys, mixed, theirs in parts:
+        theirs = theirs.astype(F32)
         mine = mixed[:rows].astype(F32)
         for index, (dy, dx) in enumerate(keys):
             start = place(my_y + dy, my_x + dx, 0) * wide

time: 248 us -> 248 us (level)
    ppermute x3, waiting for transfers between devices: 26 us -> 30.3 us  [chained(): falling = lax.ppermute(send_down, 'tp', down)]
    reduce_scatter x1, waiting for transfers between devices: 3.8 us -> 0.01 us  [on_device(): near_sum = lax.psum_scatter(found, 'tp', scatter_dimension=0, tiled=True)]
where the time goes in v15:
time: 248 us; the launch traced here: 247 us
  waiting for transfers between devices  131 us (53%)
  Pallas kernels  46.4 us (19%)
  starting transfers between devices  37.2 us (15%)
  between operations  14 us (6%)
  local copies, waits for them, and re-layouts  11.2 us (5%)
  other arithmetic  7.54 us (3%)
    ppermute x14, waiting for transfers between devices, from_chip(): return lax.ppermute(block, 'seq', route)  82.3 us
    ppermute x3, waiting for transfers between devices, chained(): falling = lax.ppermute(send_down, 'tp', down)  30.3 us
    pallas_call x7, Pallas kernels, call(): pl.pallas_call(kernel, out_shape=out, in_specs=[pl.BlockSpec(memory_space...  20.6 us
    pallas_call x2, Pallas kernels, products(): pl.pallas_call(functools.partial(product_kernel, len(xs), len(pieces)), o...  19.2 us
    ppermute x14, starting transfers between devices, from_chip(): return lax.ppermute(block, 'seq', route)  16.7 us
    ppermute x3, starting transfers between devices, chained(): rising = lax.ppermute(send_up, 'tp', up)  12.6 us
    ppermute x3, waiting for transfers between devices, chained(): rising = lax.ppermute(send_up, 'tp', up)  10.2 us
    pallas_call x1, Pallas kernels, near_terms(): pl.pallas_call(functools.partial(near_kernel, n_tp), out_shape=jax.ShapeD...  6.63 us
  transfers between devices with their start and end apart: 31, of which 17 were waited for; matrix products, arithmetic and copies ran while one was open for 4% of the time, Pallas kernels for 16%

profile of v15, /device:TPU:0, one launch (start us, length us, event | category | flops | bytes accessed | tf_op | source)
XLA Modules:
  0.0 247.4 jit_solution(13211509125851125870)
XLA Ops:
  6.5 1.8 constant_dynamic-slice_fusion.2
  8.7 1.3 fusion.2
  10.1 0.5 collective-permute-start
  10.6 2.6 %collective-permute-start.1 = (bf16[2,512,512]{2,1,0:T(8,128)(2,1)S(1)}, bf16[2,512,512]{2,1,0:T(8,128)(2,1)S(1)}, u32[]{:S(2)}, u32[]{:S(2)}) collective-permute-start(bf16[2,512,512]{2,1,0:T(8,128)(2,1)S(1)} %get-tuple-element.58.refs_1_.refs_2_), channel_id=1, source_target_pairs={{8,0},{12,4},{0,8},{4,12},{24,16},{28,20},{16,24},{20,28},{9,1},{1... | collective-permute-start | bytes 3145736 | tf_op jit(solution)/shard_map/ppermute | solution.py:276
  13.2 1.5 collective-permute-start.3
  14.7 1.1 collective-permute-start.2
  15.8 1.5 collective-permute-start.4
  17.3 1.3 constant_dynamic-slice_fusion.1
  18.6 1.9 collective-permute-done.5
  20.6 16.5 %collective-permute-done.1.refs_3_.refs_4_ = bf16[2,512,512]{2,1,0:T(8,128)(2,1)S(1)} collective-permute-done((bf16[2,512,512]{2,1,0:T(8,128)(2,1)S(1)}, bf16[2,512,512]{2,1,0:T(8,128)(2,1)S(1)}, u32[]{:S(2)}, u32[]{:S(2)}) %collective-permute-start.1) | collective-permute-done | bytes 1048608 | tf_op jit(solution)/shard_map/ppermute | solution.py:276
  37.2 2.0 collective-permute-done.3.refs_5_.refs_6_
  39.2 20.2 %collective-permute-done.2.refs_4_.refs_5_ = bf16[2,512,512]{2,1,0:T(8,128)(2,1)S(1)} collective-permute-done((bf16[2,512,512]{2,1,0:T(8,128)(2,1)S(1)}, bf16[2,512,512]{2,1,0:T(8,128)(2,1)S(1)}, u32[]{:S(2)}, u32[]{:S(2)}) %collective-permute-start.2) | collective-permute-done | bytes 1048608 | tf_op jit(solution)/shard_map/ppermute | solution.py:276
  59.4 1.5 collective-permute-done.4.refs_6_.refs_7_
  60.9 1.5 collective-permute-start.6
  62.4 0.5 collective-permute-start.7
  62.9 1.5 collective-permute-start.8
  64.9 22.0 %collective-permute-done.6.refs_7_.refs_8_ = bf16[2,512,512]{2,1,0:T(8,128)(2,1)S(1)} collective-permute-done((bf16[2,512,512]{2,1,0:T(8,128)(2,1)S(1)}, bf16[2,512,512]{2,1,0:T(8,128)(2,1)S(1)}, u32[]{:S(2)}, u32[]{:S(2)}) %collective-permute-start.6) | collective-permute-done | bytes 1048608 | tf_op jit(solution)/shard_map/ppermute | solution.py:276
  87.0 1.0 copy-done.13
  88.0 0.6 collective-permute-done.7.refs_8_.refs_9_
  88.6 5.1 %all-gather.2.cloned.1.call-done.refs_0_ = bf16[512,4096]{1,0:T(8,128)(2,1)} async-done(((bf16[128,4096]{1,0:T(8,128)(2,1)}), bf16[512,4096]{1,0:T(8,128)(2,1)}) %all-gather.2.cloned.1.call-update) | async-done | bytes 4194320 | tf_op jit(solution)/shard_map/all_gather | solution.py:327
  93.7 0.9 slice.56
  94.6 0.7 collective-permute-start.10
  95.2 0.7 collective-permute-start.11
  96.0 0.7 stack.55.at_ref._
  96.7 9.4 %shard_map.64.product_ref = f32[512,512]{1,0:T(8,128)} custom-call(s32[8]{0:T(128)} %stack.55.at_ref._, bf16[512,4096]{1,0:T(8,128)(2,1)} %all-gather.2.cloned.1.call-done.refs_0_, bf16[2,512,512]{2,1,0:T(8,128)(2,1)} %copy-done.7, bf16[2,512,512]{2,1,0:T(8,128)(2,1)} %copy-done.8, bf16[2,512,512]{2,1,0:T(8,128)(2,1)} %copy-done.9, ...), custom_call_target="tpu_custom_call" | custom-call | flops 1 | bytes 1 | tf_op jit(solution)/shard_map/pallas_call | solution.py:124
  106.2 0.7 broadcast_select_fusion.refs_0_
  106.9 4.1 %collective-permute-done.8.refs_2_ = bf16[2,512,512]{2,1,0:T(8,128)(2,1)S(1)} collective-permute-done((bf16[2,512,512]{2,1,0:T(8,128)(2,1)S(1)}, bf16[2,512,512]{2,1,0:T(8,128)(2,1)S(1)}, u32[]{:S(2)}, u32[]{:S(2)}) %collective-permute-start.8) | collective-permute-done | bytes 1048608 | tf_op jit(solution)/shard_map/ppermute | solution.py:276
  111.0 1.2 collective-permute-start.12
  112.2 0.8 slice_bitcast_fusion.1
  113.0 1.7 collective-permute-start.13
  114.7 0.8 slice_bitcast_fusion
  115.5 2.0 collective-permute-start.17
  118.2 4.0 %shard_map.65.refs_2_ = f32[512,512]{1,0:T(8,128)S(1)} custom-call(s32[8]{0:T(128)S(1)} %copy-done.3, bf16[512,4096]{1,0:T(8,128)(2,1)} %all-gather.2.cloned.1.call-done.refs_0_, bf16[2,512,512]{2,1,0:T(8,128)(2,1)S(1)} %pad_maximum_fusion.refs_1_, bf16[2,512,512]{2,1,0:T(8,128)(2,1)S(1)} %collective-permute-done.8.refs_2_, ...), custom_call_target="tpu_custom_call" | custom-call | flops 1 | bytes 1 | tf_op jit(solution)/shard_map/pallas_call | solution.py:68
  122.2 9.8 %shard_map.66 = (f32[16,512]{1,0:T(8,128)}, f32[512,512]{1,0:T(8,128)}) custom-call(s32[8]{0:T(128)} %stack.55.at_ref._, bf16[16,4096]{1,0:T(8,128)(2,1)} %broadcast_select_fusion.refs_0_, bf16[512,4096]{1,0:T(8,128)(2,1)} %collective-permute-done.12.refs_1_.refs_0_, bf16[2,512,512]{2,1,0:T(8,128)(2,1)} %copy-done.7, bf16[2,512,512]{2,1,0:T(8,128)(2,1)} %copy-done.8, ...), custom_call_target="tpu_custom_call" | custom-call | flops 1 | bytes 1 | tf_op jit(solution)/shard_map/pallas_call | solution.py:124
  132.0 0.9 broadcast_select_fusion.1
  132.9 2.0 shard_map.67.refs_1_
  135.0 2.0 shard_map.68.refs_1_
  137.0 4.2 %shard_map.70.refs_2_ = f32[512,512]{1,0:T(8,128)S(1)} custom-call(s32[8]{0:T(128)S(1)} %copy-done.4, bf16[512,4096]{1,0:T(8,128)(2,1)} %collective-permute-done.12.refs_1_.refs_0_, bf16[2,512,512]{2,1,0:T(8,128)(2,1)S(1)} %pad_maximum_fusion.refs_1_, bf16[2,512,512]{2,1,0:T(8,128)(2,1)S(1)} %collective-permute-done.8.refs_2_, ...), custom_call_target="tpu_custom_call" | custom-call | flops 1 | bytes 1 | tf_op jit(solution)/shard_map/pallas_call | solution.py:68
  141.2 3.2 %shard_map.71.refs_2_ = bf16[512,512]{1,0:T(8,128)(2,1)S(1)} custom-call(s32[2]{0:T(128)S(1)} %pad_add_fusion.at_ref, bf16[512,4096]{1,0:T(8,128)(2,1)} %collective-permute-done.12.refs_1_.refs_0_, f32[512,512]{1,0:T(8,128)S(1)} %shard_map.68.refs_1_, f32[512,512]{1,0:T(8,128)S(1)} %shard_map.70.refs_2_, bf16[512,512]{1,0:T(8,128)(2,1)} %collective-permute-done.13.refs_3_, ...), custom_call_target="tpu_custom_call" | custom-call | flops 1 | bytes 1 | tf_op jit(solution)/shard_map/pallas_call | solution.py:68
  144.5 3.2 %shard_map.69.refs_0_ = bf16[512,512]{1,0:T(8,128)(2,1)S(1)} custom-call(s32[2]{0:T(128)S(1)} %pad_add_fusion.at_ref, bf16[512,4096]{1,0:T(8,128)(2,1)} %all-gather.2.cloned.1.call-done.refs_0_, f32[512,512]{1,0:T(8,128)S(1)} %shard_map.67.refs_1_, f32[512,512]{1,0:T(8,128)S(1)} %shard_map.65.refs_2_, bf16[512,512]{1,0:T(8,128)(2,1)} %collective-permute-done.13.refs_3_, ...), custom_call_target="tpu_custom_call" | custom-call | flops 1 | bytes 1 | tf_op jit(solution)/shard_map/pallas_call | solution.py:68
  147.7 0.6 collective-permute-start.16
  148.3 3.5 %collective-permute-done.17.refs_5_ = bf16[1024,512]{1,0:T(8,128)(2,1)} collective-permute-done((bf16[1024,512]{1,0:T(8,128)(2,1)}, bf16[1024,512]{1,0:T(8,128)(2,1)}, u32[]{:S(2)}, u32[]{:S(2)}) %collective-permute-start.17) | collective-permute-done | bytes 1048608 | tf_op jit(solution)/shard_map/ppermute | solution.py:276
  151.9 6.6 %shard_map.72 = bf16[1024,1536]{1,0:T(8,128)(2,1)} custom-call(s32[2]{0:T(128)S(1)} %pad_add_fusion.1.at_ref, bf16[512,512]{1,0:T(8,128)(2,1)S(1)} %shard_map.69.refs_0_, bf16[512,512]{1,0:T(8,128)(2,1)S(1)} %collective-permute-done.15.refs_1_, bf16[512,512]{1,0:T(8,128)(2,1)S(1)} %shard_map.71.refs_2_, ...), custom_call_target="tpu_custom_call" | custom-call | flops 1 | bytes 1 | tf_op jit(solution)/shard_map/pallas_call | solution.py:237
  158.5 1.1 slice.73
  160.0 1.1 slice.74
  161.1 1.5 collective-permute-start.20
  162.6 9.7 %collective-permute-done.19.refs_4_ = bf16[512,512]{1,0:T(8,128)(2,1)S(1)} collective-permute-done((bf16[512,512]{1,0:T(8,128)(2,1)S(1)}, bf16[512,512]{1,0:T(8,128)(2,1)S(1)}, u32[]{:S(2)}, u32[]{:S(2)}) %collective-permute-start.19) | collective-permute-done | bytes 524320 | tf_op jit(solution)/shard_map/ppermute | solution.py:276
  172.3 2.0 collective-permute-done.20.refs_5_
  174.4 1.9 shard_map.73
  176.3 3.5 %collective-permute-start.21 = (bf16[256,512]{1,0:T(8,128)(2,1)S(1)}, bf16[256,512]{1,0:T(8,128)(2,1)S(1)}, u32[]{:S(2)}, u32[]{:S(2)}) collective-permute-start(bf16[256,512]{1,0:T(8,128)(2,1)S(1)} %get-tuple-element.87), channel_id=1, source_target_pairs={{0,1},{1,2},{2,3},{4,5},{5,6},{6,7},{8,9},{9,10},{10,11},{12,13},{... | collective-permute-start | bytes 786440 | tf_op jit(solution)/shard_map/ppermute | solution.py:411
  179.8 1.3 collective-permute-start.24
  181.1 10.2 %collective-permute-done.21 = bf16[256,512]{1,0:T(8,128)(2,1)S(1)} collective-permute-done((bf16[256,512]{1,0:T(8,128)(2,1)S(1)}, bf16[256,512]{1,0:T(8,128)(2,1)S(1)}, u32[]{:S(2)}, u32[]{:S(2)}) %collective-permute-start.21) | collective-permute-done | bytes 262176 | tf_op jit(solution)/shard_map/ppermute | solution.py:411
  191.2 10.8 %collective-permute-done.24 = bf16[256,512]{1,0:T(8,128)(2,1)S(1)} collective-permute-done((bf16[256,512]{1,0:T(8,128)(2,1)S(1)}, bf16[256,512]{1,0:T(8,128)(2,1)S(1)}, u32[]{:S(2)}, u32[]{:S(2)}) %collective-permute-start.24) | collective-permute-done | bytes 262176 | tf_op jit(solution)/shard_map/ppermute | solution.py:412
  202.2 1.3 collective-permute-start.25
  203.5 4.6 %collective-permute-start.22 = (bf16[256,512]{1,0:T(8,128)(2,1)S(1)}, bf16[256,512]{1,0:T(8,128)(2,1)S(1)}, u32[]{:S(2)}, u32[]{:S(2)}) collective-permute-start(bf16[256,512]{1,0:T(8,128)(2,1)S(1)} %get-tuple-element.105), channel_id=1, source_target_pairs={{0,1},{1,2},{2,3},{4,5},{5,6},{6,7},{8,9},{9,10},{10,11},{12,13},{... | collective-permute-start | bytes 786440 | tf_op jit(solution)/shard_map/ppermute | solution.py:411
  208.1 15.2 %collective-permute-done.25 = bf16[256,512]{1,0:T(8,128)(2,1)S(1)} collective-permute-done((bf16[256,512]{1,0:T(8,128)(2,1)S(1)}, bf16[256,512]{1,0:T(8,128)(2,1)S(1)}, u32[]{:S(2)}, u32[]{:S(2)}) %collective-permute-start.25) | collective-permute-done | bytes 262176 | tf_op jit(solution)/shard_map/ppermute | solution.py:412
  223.3 1.3 collective-permute-start.26
  224.7 4.6 %collective-permute-start.23 = (bf16[256,512]{1,0:T(8,128)(2,1)S(1)}, bf16[256,512]{1,0:T(8,128)(2,1)S(1)}, u32[]{:S(2)}, u32[]{:S(2)}) collective-permute-start(bf16[256,512]{1,0:T(8,128)(2,1)S(1)} %add_convert_fusion.1), channel_id=1, source_target_pairs={{0,1},{1,2},{2,3},{4,5},{5,6},{6,7},{8,9},{9,10},{10,11},{12,13},{... | collective-permute-start | bytes 786440 | tf_op jit(solution)/shard_map/ppermute | solution.py:411
  229.3 4.3 %collective-permute-done.26 = bf16[256,512]{1,0:T(8,128)(2,1)S(1)} collective-permute-done((bf16[256,512]{1,0:T(8,128)(2,1)S(1)}, bf16[256,512]{1,0:T(8,128)(2,1)S(1)}, u32[]{:S(2)}, u32[]{:S(2)}) %collective-permute-start.26) | collective-permute-done | bytes 262176 | tf_op jit(solution)/shard_map/ppermute | solution.py:412
  233.8 1.3 collective-permute-done.27
  235.1 1.2 fusion.26
  236.7 1.4 fusion.24
  238.8 1.0 copy-done.15
  239.7 0.9 fusion.21
  (78 shorter events, 3.9 us)
Async XLA Ops:
  6.5 111.3 %copy-start = (f32[7,64]{1,0:T(8,128)S(1)}, f32[7,64]{1,0:T(8,128)}, u32[]{:S(2)}) copy-start(f32[7,64]{1,0:T(8,128)} %param.9) | copy-start | bytes 5380
  6.5 87.1 %all-gather.2.cloned.1.call-start = ((), (), s32[]{:S(2)}) async-start(), calls=%async_computation.1 | async-start | bytes 5242880 | tf_op jit(solution)/shard_map/all_gather | solution.py:327
  6.5 1.9 copy-start.5
  6.5 2.2 copy-start.16
  8.3 4.8 %copy-start.7 = (bf16[2,512,512]{2,1,0:T(8,128)(2,1)}, bf16[2,512,512]{2,1,0:T(8,128)(2,1)S(1)}, u32[]{:S(2)}) copy-start(bf16[2,512,512]{2,1,0:T(8,128)(2,1)S(1)} %get-tuple-element.58.refs_1_.refs_2_) | copy-start | bytes 3145732
  10.0 225.1 %reduce-scatter.2.cloned.1.call-start = ((), (), s32[]{:S(2)}) async-start(), calls=%async_computation.2 | async-start | bytes 3932160 | tf_op jit(solution)/shard_map/reduce_scatter | solution.py:420
  10.1 4.6 %collective-permute-start = (bf16[2,512,512]{2,1,0:T(8,128)(2,1)S(1)}, bf16[2,512,512]{2,1,0:T(8,128)(2,1)S(1)}, u32[]{:S(2)}, u32[]{:S(2)}) collective-permute-start(bf16[2,512,512]{2,1,0:T(8,128)(2,1)S(1)} %get-tuple-element.94), channel_id=1, source_target_pairs={{0,4},{4,0},{8,12},{12,8},{16,20},{20,16},{24,28},{28,24},{1,5},{5... | collective-permute-start | bytes 3145736 | tf_op jit(solution)/shard_map/ppermute | solution.py:279
  10.6 26.6 %collective-permute-start.1 = (bf16[2,512,512]{2,1,0:T(8,128)(2,1)S(1)}, bf16[2,512,512]{2,1,0:T(8,128)(2,1)S(1)}, u32[]{:S(2)}, u32[]{:S(2)}) collective-permute-start(bf16[2,512,512]{2,1,0:T(8,128)(2,1)S(1)} %get-tuple-element.58.refs_1_.refs_2_), channel_id=1, source_target_pairs={{8,0},{12,4},{0,8},{4,12},{24,16},{28,20},{16,24},{20,28},{9,1},{1... | collective-permute-start | bytes 3145736 | tf_op jit(solution)/shard_map/ppermute | solution.py:276
  13.2 26.0 %collective-permute-start.3 = (bf16[2,512,512]{2,1,0:T(8,128)(2,1)S(1)}, bf16[2,512,512]{2,1,0:T(8,128)(2,1)S(1)}, u32[]{:S(2)}, u32[]{:S(2)}) collective-permute-start(bf16[2,512,512]{2,1,0:T(8,128)(2,1)S(1)} %get-tuple-element.58.refs_1_.refs_2_), channel_id=1, source_target_pairs={{16,0},{20,4},{24,8},{28,12},{0,16},{4,20},{8,24},{12,28},{17,1},{... | collective-permute-start | bytes 3145736 | tf_op jit(solution)/shard_map/ppermute | solution.py:276
  14.7 5.9 %copy-start.8 = (bf16[2,512,512]{2,1,0:T(8,128)(2,1)}, bf16[2,512,512]{2,1,0:T(8,128)(2,1)S(1)}, u32[]{:S(2)}) copy-start(bf16[2,512,512]{2,1,0:T(8,128)(2,1)S(1)} %collective-permute-done.refs_2_.refs_3_) | copy-start | bytes 3145732
  14.7 44.7 %collective-permute-start.2 = (bf16[2,512,512]{2,1,0:T(8,128)(2,1)S(1)}, bf16[2,512,512]{2,1,0:T(8,128)(2,1)S(1)}, u32[]{:S(2)}, u32[]{:S(2)}) collective-permute-start(bf16[2,512,512]{2,1,0:T(8,128)(2,1)S(1)} %collective-permute-done.refs_2_.refs_3_), channel_id=1, source_target_pairs={{8,0},{12,4},{0,8},{4,12},{24,16},{28,20},{16,24},{20,28},{9,1},{1... | collective-permute-start | bytes 3145736 | tf_op jit(solution)/shard_map/ppermute | solution.py:276
  15.8 45.1 %collective-permute-start.4 = (bf16[2,512,512]{2,1,0:T(8,128)(2,1)S(1)}, bf16[2,512,512]{2,1,0:T(8,128)(2,1)S(1)}, u32[]{:S(2)}, u32[]{:S(2)}) collective-permute-start(bf16[2,512,512]{2,1,0:T(8,128)(2,1)S(1)} %collective-permute-done.refs_2_.refs_3_), channel_id=1, source_target_pairs={{16,0},{20,4},{24,8},{28,12},{0,16},{4,20},{8,24},{12,28},{17,1},{... | collective-permute-start | bytes 3145736 | tf_op jit(solution)/shard_map/ppermute | solution.py:276
  18.5 2.0 collective-permute-start.5
  37.2 25.8 %copy-start.9 = (bf16[2,512,512]{2,1,0:T(8,128)(2,1)}, bf16[2,512,512]{2,1,0:T(8,128)(2,1)S(1)}, u32[]{:S(2)}) copy-start(bf16[2,512,512]{2,1,0:T(8,128)(2,1)S(1)} %collective-permute-done.1.refs_3_.refs_4_) | copy-start | bytes 3145732
  39.2 47.8 %copy-start.10 = (bf16[2,512,512]{2,1,0:T(8,128)(2,1)}, bf16[2,512,512]{2,1,0:T(8,128)(2,1)S(1)}, u32[]{:S(2)}) copy-start(bf16[2,512,512]{2,1,0:T(8,128)(2,1)S(1)} %collective-permute-done.3.refs_5_.refs_6_) | copy-start | bytes 3145732
  59.4 27.6 %copy-start.11 = (bf16[2,512,512]{2,1,0:T(8,128)(2,1)}, bf16[2,512,512]{2,1,0:T(8,128)(2,1)S(1)}, u32[]{:S(2)}) copy-start(bf16[2,512,512]{2,1,0:T(8,128)(2,1)S(1)} %collective-permute-done.2.refs_4_.refs_5_) | copy-start | bytes 3145732
  60.9 26.1 %copy-start.12 = (bf16[2,512,512]{2,1,0:T(8,128)(2,1)}, bf16[2,512,512]{2,1,0:T(8,128)(2,1)S(1)}, u32[]{:S(2)}) copy-start(bf16[2,512,512]{2,1,0:T(8,128)(2,1)S(1)} %collective-permute-done.4.refs_6_.refs_7_) | copy-start | bytes 3145732
  60.9 26.1 %collective-permute-start.6 = (bf16[2,512,512]{2,1,0:T(8,128)(2,1)S(1)}, bf16[2,512,512]{2,1,0:T(8,128)(2,1)S(1)}, u32[]{:S(2)}, u32[]{:S(2)}) collective-permute-start(bf16[2,512,512]{2,1,0:T(8,128)(2,1)S(1)} %collective-permute-done.1.refs_3_.refs_4_), channel_id=1, source_target_pairs={{16,0},{20,4},{24,8},{28,12},{0,16},{4,20},{8,24},{12,28},{17,1},{... | collective-permute-start | bytes 3145736 | tf_op jit(solution)/shard_map/ppermute | solution.py:276
  62.4 26.2 %collective-permute-start.7 = (bf16[2,512,512]{2,1,0:T(8,128)(2,1)S(1)}, bf16[2,512,512]{2,1,0:T(8,128)(2,1)}, u32[]{:S(2)}, u32[]{:S(2)}) collective-permute-start(bf16[2,512,512]{2,1,0:T(8,128)(2,1)S(1)} %collective-permute-done.4.refs_6_.refs_7_), channel_id=1, source_target_pairs={{8,0},{12,4},{0,8},{4,12},{24,16},{28,20},{16,24},{20,28},{9,1},{1... | collective-permute-start | bytes 3145736 | tf_op jit(solution)/shard_map/ppermute | solution.py:276
  62.9 48.0 %collective-permute-start.8 = (bf16[2,512,512]{2,1,0:T(8,128)(2,1)S(1)}, bf16[2,512,512]{2,1,0:T(8,128)(2,1)S(1)}, u32[]{:S(2)}, u32[]{:S(2)}) collective-permute-start(bf16[2,512,512]{2,1,0:T(8,128)(2,1)S(1)} %pad_maximum_fusion.refs_1_), channel_id=1, source_target_pairs={{8,0},{12,4},{0,8},{4,12},{24,16},{28,20},{16,24},{20,28},{9,1},{1... | collective-permute-start | bytes 3145736 | tf_op jit(solution)/shard_map/ppermute | solution.py:276
  64.4 46.5 %collective-permute-start.9 = (bf16[2,512,512]{2,1,0:T(8,128)(2,1)S(1)}, bf16[2,512,512]{2,1,0:T(8,128)(2,1)S(1)}, u32[]{:S(2)}, u32[]{:S(2)}) collective-permute-start(bf16[2,512,512]{2,1,0:T(8,128)(2,1)S(1)} %pad_maximum_fusion.refs_1_), channel_id=1, source_target_pairs={{16,0},{20,4},{24,8},{28,12},{0,16},{4,20},{8,24},{12,28},{17,1},{... | collective-permute-start | bytes 3145736 | tf_op jit(solution)/shard_map/ppermute | solution.py:276
  87.0 1.0 copy-start.13
  94.6 11.6 %collective-permute-start.10 = (bf16[16,4096]{1,0:T(8,128)(2,1)S(1)}, bf16[16,4096]{1,0:T(8,128)(2,1)S(1)}, u32[]{:S(2)}, u32[]{:S(2)}) collective-permute-start(bf16[16,4096]{1,0:T(8,128)(2,1)S(1)} %slice.56), channel_id=1, source_target_pairs={{4,8},{12,16},{20,24},{5,9},{13,17},{21,25},{6,10},{14,18},{22,26}... | collective-permute-start | bytes 393224 | tf_op jit(solution)/shard_map/ppermute | solution.py:351
  95.2 10.9 %collective-permute-start.11 = (bf16[16,4096]{1,0:T(8,128)(2,1)S(1)}, bf16[16,4096]{1,0:T(8,128)(2,1)S(1)}, u32[]{:S(2)}, u32[]{:S(2)}) collective-permute-start(bf16[16,4096]{1,0:T(8,128)(2,1)S(1)} %slice.56), channel_id=1, source_target_pairs={{4,12},{12,20},{20,28},{5,13},{13,21},{21,29},{6,14},{14,22},{22,3... | collective-permute-start | bytes 393224 | tf_op jit(solution)/shard_map/ppermute | solution.py:351
  106.1 12.1 %copy-start.3 = (s32[8]{0:T(128)S(1)}, s32[8]{0:T(128)}, u32[]{:S(2)}) copy-start(s32[8]{0:T(128)} %stack.55.at_ref._) | copy-start | bytes 100
  111.0 11.3 %collective-permute-start.12 = (bf16[512,4096]{1,0:T(8,128)(2,1)}, bf16[512,4096]{1,0:T(8,128)(2,1)}, u32[]{:S(2)}, u32[]{:S(2)}) collective-permute-start(bf16[512,4096]{1,0:T(8,128)(2,1)} %all-gather.2.cloned.1.call-done.refs_0_), channel_id=1, source_target_pairs={{0,4},{4,0},{8,12},{12,8},{16,20},{20,16},{24,28},{28,24},{1,5},{5... | collective-permute-start | bytes 12582920 | tf_op jit(solution)/shard_map/ppermute | solution.py:279
  113.0 28.2 %collective-permute-start.13 = (bf16[512,512]{1,0:T(8,128)(2,1)}, bf16[512,512]{1,0:T(8,128)(2,1)}, u32[]{:S(2)}, u32[]{:S(2)}) collective-permute-start(bf16[512,512]{1,0:T(8,128)(2,1)} %slice_bitcast_fusion.1), channel_id=1, source_target_pairs={{16,0},{20,4},{24,8},{28,12},{0,16},{4,20},{8,24},{12,28},{17,1},{... | collective-permute-start | bytes 1572872 | tf_op jit(solution)/shard_map/ppermute | solution.py:276
  115.5 25.7 %collective-permute-start.14 = (bf16[512,512]{1,0:T(8,128)(2,1)}, bf16[512,512]{1,0:T(8,128)(2,1)}, u32[]{:S(2)}, u32[]{:S(2)}) collective-permute-start(bf16[512,512]{1,0:T(8,128)(2,1)} %slice_bitcast_fusion), channel_id=1, source_target_pairs={{8,0},{12,4},{0,8},{4,12},{24,16},{28,20},{16,24},{20,28},{9,1},{1... | collective-permute-start | bytes 1572872 | tf_op jit(solution)/shard_map/ppermute | solution.py:276
  115.5 36.3 %collective-permute-start.17 = (bf16[1024,512]{1,0:T(8,128)(2,1)}, bf16[1024,512]{1,0:T(8,128)(2,1)}, u32[]{:S(2)}, u32[]{:S(2)}) collective-permute-start(bf16[1024,512]{1,0:T(8,128)(2,1)} %refs_4_.1), channel_id=1, source_target_pairs={{8,0},{12,4},{0,8},{4,12},{24,16},{28,20},{16,24},{20,28},{9,1},{1... | collective-permute-start | bytes 3145736 | tf_op jit(solution)/shard_map/ppermute | solution.py:276
  117.5 34.3 %collective-permute-start.18 = (bf16[1024,512]{1,0:T(8,128)(2,1)}, bf16[1024,512]{1,0:T(8,128)(2,1)}, u32[]{:S(2)}, u32[]{:S(2)}) collective-permute-start(bf16[1024,512]{1,0:T(8,128)(2,1)} %refs_4_.1), channel_id=1, source_target_pairs={{16,0},{20,4},{24,8},{28,12},{0,16},{4,20},{8,24},{12,28},{17,1},{... | collective-permute-start | bytes 3145736 | tf_op jit(solution)/shard_map/ppermute | solution.py:276
  122.2 9.8 %copy-start.1 = (f32[512,512]{1,0:T(8,128)S(1)}, f32[512,512]{1,0:T(8,128)}, u32[]{:S(2)}) copy-start(f32[512,512]{1,0:T(8,128)} %shard_map.64.product_ref) | copy-start | bytes 3145732
  122.2 10.7 %copy-start.4 = (s32[8]{0:T(128)S(1)}, s32[8]{0:T(128)}, u32[]{:S(2)}) copy-start(s32[8]{0:T(128)} %stack.55.at_ref._) | copy-start | bytes 100
  132.0 2.9 %copy-start.2 = (f32[512,512]{1,0:T(8,128)S(1)}, f32[512,512]{1,0:T(8,128)}, u32[]{:S(2)}) copy-start(f32[512,512]{1,0:T(8,128)} %get-tuple-element.73.product_ref) | copy-start | bytes 3145732
  144.4 7.4 %collective-permute-start.15 = (bf16[512,512]{1,0:T(8,128)(2,1)S(1)}, bf16[512,512]{1,0:T(8,128)(2,1)S(1)}, u32[]{:S(2)}, u32[]{:S(2)}) collective-permute-start(bf16[512,512]{1,0:T(8,128)(2,1)S(1)} %shard_map.71.refs_2_), channel_id=1, source_target_pairs={{0,4},{4,0},{8,12},{12,8},{16,20},{20,16},{24,28},{28,24},{1,5},{5... | collective-permute-start | bytes 1572872 | tf_op jit(solution)/shard_map/ppermute | solution.py:279
  147.7 4.2 %collective-permute-start.16 = (bf16[512,512]{1,0:T(8,128)(2,1)S(1)}, bf16[512,512]{1,0:T(8,128)(2,1)S(1)}, u32[]{:S(2)}, u32[]{:S(2)}) collective-permute-start(bf16[512,512]{1,0:T(8,128)(2,1)S(1)} %shard_map.69.refs_0_), channel_id=1, source_target_pairs={{0,4},{4,0},{8,12},{12,8},{16,20},{20,16},{24,28},{28,24},{1,5},{5... | collective-permute-start | bytes 1572872 | tf_op jit(solution)/shard_map/ppermute | solution.py:279
  159.6 12.7 %collective-permute-start.19 = (bf16[512,512]{1,0:T(8,128)(2,1)S(1)}, bf16[512,512]{1,0:T(8,128)(2,1)S(1)}, u32[]{:S(2)}, u32[]{:S(2)}) collective-permute-start(bf16[512,512]{1,0:T(8,128)(2,1)S(1)} %slice.73), channel_id=1, source_target_pairs={{16,0},{20,4},{24,8},{28,12},{0,16},{4,20},{8,24},{12,28},{17,1},{... | collective-permute-start | bytes 1572872 | tf_op jit(solution)/shard_map/ppermute | solution.py:276
  161.1 13.3 %collective-permute-start.20 = (bf16[512,512]{1,0:T(8,128)(2,1)S(1)}, bf16[512,512]{1,0:T(8,128)(2,1)S(1)}, u32[]{:S(2)}, u32[]{:S(2)}) collective-permute-start(bf16[512,512]{1,0:T(8,128)(2,1)S(1)} %slice.74), channel_id=1, source_target_pairs={{8,0},{12,4},{0,8},{4,12},{24,16},{28,20},{16,24},{20,28},{9,1},{1... | collective-permute-start | bytes 1572872 | tf_op jit(solution)/shard_map/ppermute | solution.py:276
  176.3 15.0 %collective-permute-start.21 = (bf16[256,512]{1,0:T(8,128)(2,1)S(1)}, bf16[256,512]{1,0:T(8,128)(2,1)S(1)}, u32[]{:S(2)}, u32[]{:S(2)}) collective-permute-start(bf16[256,512]{1,0:T(8,128)(2,1)S(1)} %get-tuple-element.87), channel_id=1, source_target_pairs={{0,1},{1,2},{2,3},{4,5},{5,6},{6,7},{8,9},{9,10},{10,11},{12,13},{... | collective-permute-start | bytes 786440 | tf_op jit(solution)/shard_map/ppermute | solution.py:411
  179.8 22.3 %collective-permute-start.24 = (bf16[256,512]{1,0:T(8,128)(2,1)S(1)}, bf16[256,512]{1,0:T(8,128)(2,1)S(1)}, u32[]{:S(2)}, u32[]{:S(2)}) collective-permute-start(bf16[256,512]{1,0:T(8,128)(2,1)S(1)} %get-tuple-element.85), channel_id=1, source_target_pairs={{1,0},{2,1},{3,2},{5,4},{6,5},{7,6},{9,8},{10,9},{11,10},{13,12},{... | collective-permute-start | bytes 786440 | tf_op jit(solution)/shard_map/ppermute | solution.py:412
  202.2 21.0 %collective-permute-start.25 = (bf16[256,512]{1,0:T(8,128)(2,1)S(1)}, bf16[256,512]{1,0:T(8,128)(2,1)S(1)}, u32[]{:S(2)}, u32[]{:S(2)}) collective-permute-start(bf16[256,512]{1,0:T(8,128)(2,1)S(1)} %get-tuple-element.106), channel_id=1, source_target_pairs={{1,0},{2,1},{3,2},{5,4},{6,5},{7,6},{9,8},{10,9},{11,10},{13,12},{... | collective-permute-start | bytes 786440 | tf_op jit(solution)/shard_map/ppermute | solution.py:412
  203.5 21.1 %collective-permute-start.22 = (bf16[256,512]{1,0:T(8,128)(2,1)S(1)}, bf16[256,512]{1,0:T(8,128)(2,1)S(1)}, u32[]{:S(2)}, u32[]{:S(2)}) collective-permute-start(bf16[256,512]{1,0:T(8,128)(2,1)S(1)} %get-tuple-element.105), channel_id=1, source_target_pairs={{0,1},{1,2},{2,3},{4,5},{5,6},{6,7},{8,9},{9,10},{10,11},{12,13},{... | collective-permute-start | bytes 786440 | tf_op jit(solution)/shard_map/ppermute | solution.py:411
  223.3 10.2 %collective-permute-start.26 = (bf16[256,512]{1,0:T(8,128)(2,1)S(1)}, bf16[256,512]{1,0:T(8,128)(2,1)S(1)}, u32[]{:S(2)}, u32[]{:S(2)}) collective-permute-start(bf16[256,512]{1,0:T(8,128)(2,1)S(1)} %add_convert_fusion), channel_id=1, source_target_pairs={{1,0},{2,1},{3,2},{5,4},{6,5},{7,6},{9,8},{10,9},{11,10},{13,12},{... | collective-permute-start | bytes 786440 | tf_op jit(solution)/shard_map/ppermute | solution.py:412
  224.7 8.9 %collective-permute-start.23 = (bf16[256,512]{1,0:T(8,128)(2,1)S(1)}, bf16[256,512]{1,0:T(8,128)(2,1)S(1)}, u32[]{:S(2)}, u32[]{:S(2)}) collective-permute-start(bf16[256,512]{1,0:T(8,128)(2,1)S(1)} %add_convert_fusion.1), channel_id=1, source_target_pairs={{0,1},{1,2},{2,3},{4,5},{5,6},{6,7},{8,9},{9,10},{10,11},{12,13},{... | collective-permute-start | bytes 786440 | tf_op jit(solution)/shard_map/ppermute | solution.py:411
  233.6 3.0 %copy-start.6 = (bf16[128,4096]{1,0:T(8,128)(2,1)S(1)}, bf16[128,4096]{1,0:T(8,128)(2,1)}, u32[]{:S(2)}) copy-start(bf16[128,4096]{1,0:T(8,128)(2,1)} %param.6) | copy-start | bytes 3145732
  233.7 1.4 collective-permute-start.27
  236.3 1.8 collective-permute-start.28
  236.7 1.8 copy-start.14
  238.8 1.0 copy-start.15
Sparse Core Ops, SparseCore 0:
  10.2 83.4 all-gather.1
  158.6 74.6 reduce-scatter.1

commit v16 on v15

--- a/solution.py
+++ b/solution.py
@@ -223,7 +223,11 @@
     for index, weight in enumerate(weights):
         copies[index].wait()
         at = slice(index * wide, (index + 1) * wide)
-        ready[:, at] = dot(held[...], weight[...]).astype(BF16)
+        tile = math.gcd(wide, 256)
+        for low in range(0, wide, tile):
+            total = dot(held[:, :half], weight[:half, low : low + tile])
+            total = total + dot(held[:, half:], weight[half:, low : low + tile])
+            ready[:, index * wide + low : index * wide + low + tile] = total.astype(BF16)
         leaving.append(pltpu.make_async_copy(ready.at[:, at], out_ref.at[:, at], out_sems.at[index]))
         leaving[-1].start()
     for copy in leaving:

time: 248 us -> 248 us (level)
  no operation moved by 1% of the time
where the time goes in v16:
time: 248 us; the launch traced here: 247 us
  waiting for transfers between devices  131 us (53%)
  Pallas kernels  46.4 us (19%)
  starting transfers between devices  37.2 us (15%)
  between operations  14 us (6%)
  local copies, waits for them, and re-layouts  11.2 us (5%)
  other arithmetic  7.54 us (3%)
    ppermute x14, waiting for transfers between devices, from_chip(): return lax.ppermute(block, 'seq', route)  82.3 us
    ppermute x3, waiting for transfers between devices, chained(): falling = lax.ppermute(send_down, 'tp', down)  30.3 us
    pallas_call x7, Pallas kernels, call(): pl.pallas_call(kernel, out_shape=out, in_specs=[pl.BlockSpec(memory_space...  20.6 us
    pallas_call x2, Pallas kernels, products(): pl.pallas_call(functools.partial(product_kernel, len(xs), len(pieces)), o...  19.2 us
    ppermute x14, starting transfers between devices, from_chip(): return lax.ppermute(block, 'seq', route)  16.7 us
    ppermute x3, starting transfers between devices, chained(): rising = lax.ppermute(send_up, 'tp', up)  12.6 us
    ppermute x3, waiting for transfers between devices, chained(): rising = lax.ppermute(send_up, 'tp', up)  10.2 us
    pallas_call x1, Pallas kernels, near_terms(): pl.pallas_call(functools.partial(near_kernel, n_tp), out_shape=jax.ShapeD...  6.63 us
  transfers between devices with their start and end apart: 31, of which 17 were waited for; matrix products, arithmetic and copies ran while one was open for 4% of the time, Pallas kernels for 16%

profile of v16, /device:TPU:0, one launch (start us, length us, event | category | flops | bytes accessed | tf_op | source)
XLA Modules:
  0.0 247.4 jit_solution(13471437516321672864)
XLA Ops:
  6.5 1.8 constant_dynamic-slice_fusion.2
  8.7 1.3 fusion.2
  10.1 0.5 collective-permute-start
  10.6 2.6 %collective-permute-start.1 = (bf16[2,512,512]{2,1,0:T(8,128)(2,1)S(1)}, bf16[2,512,512]{2,1,0:T(8,128)(2,1)S(1)}, u32[]{:S(2)}, u32[]{:S(2)}) collective-permute-start(bf16[2,512,512]{2,1,0:T(8,128)(2,1)S(1)} %get-tuple-element.58.refs_1_.refs_2_), channel_id=1, source_target_pairs={{8,0},{12,4},{0,8},{4,12},{24,16},{28,20},{16,24},{20,28},{9,1},{1... | collective-permute-start | bytes 3145736 | tf_op jit(solution)/shard_map/ppermute | solution.py:280
  13.2 1.5 collective-permute-start.3
  14.7 1.1 collective-permute-start.2
  15.8 1.5 collective-permute-start.4
  17.3 1.3 constant_dynamic-slice_fusion.1
  18.6 1.9 collective-permute-done.5
  20.6 16.5 %collective-permute-done.1.refs_3_.refs_4_ = bf16[2,512,512]{2,1,0:T(8,128)(2,1)S(1)} collective-permute-done((bf16[2,512,512]{2,1,0:T(8,128)(2,1)S(1)}, bf16[2,512,512]{2,1,0:T(8,128)(2,1)S(1)}, u32[]{:S(2)}, u32[]{:S(2)}) %collective-permute-start.1) | collective-permute-done | bytes 1048608 | tf_op jit(solution)/shard_map/ppermute | solution.py:280
  37.2 2.0 collective-permute-done.3.refs_5_.refs_6_
  39.2 20.2 %collective-permute-done.2.refs_4_.refs_5_ = bf16[2,512,512]{2,1,0:T(8,128)(2,1)S(1)} collective-permute-done((bf16[2,512,512]{2,1,0:T(8,128)(2,1)S(1)}, bf16[2,512,512]{2,1,0:T(8,128)(2,1)S(1)}, u32[]{:S(2)}, u32[]{:S(2)}) %collective-permute-start.2) | collective-permute-done | bytes 1048608 | tf_op jit(solution)/shard_map/ppermute | solution.py:280
  59.4 1.5 collective-permute-done.4.refs_6_.refs_7_
  60.9 1.5 collective-permute-start.6
  62.4 0.5 collective-permute-start.7
  62.9 1.5 collective-permute-start.8
  64.9 22.0 %collective-permute-done.6.refs_7_.refs_8_ = bf16[2,512,512]{2,1,0:T(8,128)(2,1)S(1)} collective-permute-done((bf16[2,512,512]{2,1,0:T(8,128)(2,1)S(1)}, bf16[2,512,512]{2,1,0:T(8,128)(2,1)S(1)}, u32[]{:S(2)}, u32[]{:S(2)}) %collective-permute-start.6) | collective-permute-done | bytes 1048608 | tf_op jit(solution)/shard_map/ppermute | solution.py:280
  87.0 1.0 copy-done.13
  88.0 0.6 collective-permute-done.7.refs_8_.refs_9_
  88.6 5.1 %all-gather.2.cloned.1.call-done.refs_0_ = bf16[512,4096]{1,0:T(8,128)(2,1)} async-done(((bf16[128,4096]{1,0:T(8,128)(2,1)}), bf16[512,4096]{1,0:T(8,128)(2,1)}) %all-gather.2.cloned.1.call-update) | async-done | bytes 4194320 | tf_op jit(solution)/shard_map/all_gather | solution.py:331
  93.7 0.9 slice.56
  94.6 0.7 collective-permute-start.10
  95.2 0.7 collective-permute-start.11
  96.0 0.7 stack.55.at_ref._
  96.7 9.4 %shard_map.64.product_ref = f32[512,512]{1,0:T(8,128)} custom-call(s32[8]{0:T(128)} %stack.55.at_ref._, bf16[512,4096]{1,0:T(8,128)(2,1)} %all-gather.2.cloned.1.call-done.refs_0_, bf16[2,512,512]{2,1,0:T(8,128)(2,1)} %copy-done.7, bf16[2,512,512]{2,1,0:T(8,128)(2,1)} %copy-done.8, bf16[2,512,512]{2,1,0:T(8,128)(2,1)} %copy-done.9, ...), custom_call_target="tpu_custom_call" | custom-call | flops 1 | bytes 1 | tf_op jit(solution)/shard_map/pallas_call | solution.py:124
  106.2 0.7 broadcast_select_fusion.refs_0_
  106.9 4.1 %collective-permute-done.8.refs_2_ = bf16[2,512,512]{2,1,0:T(8,128)(2,1)S(1)} collective-permute-done((bf16[2,512,512]{2,1,0:T(8,128)(2,1)S(1)}, bf16[2,512,512]{2,1,0:T(8,128)(2,1)S(1)}, u32[]{:S(2)}, u32[]{:S(2)}) %collective-permute-start.8) | collective-permute-done | bytes 1048608 | tf_op jit(solution)/shard_map/ppermute | solution.py:280
  111.0 1.2 collective-permute-start.12
  112.2 0.8 slice_bitcast_fusion.1
  113.0 1.7 collective-permute-start.13
  114.7 0.8 slice_bitcast_fusion
  115.5 2.0 collective-permute-start.17
  118.2 4.0 %shard_map.65.refs_2_ = f32[512,512]{1,0:T(8,128)S(1)} custom-call(s32[8]{0:T(128)S(1)} %copy-done.3, bf16[512,4096]{1,0:T(8,128)(2,1)} %all-gather.2.cloned.1.call-done.refs_0_, bf16[2,512,512]{2,1,0:T(8,128)(2,1)S(1)} %pad_maximum_fusion.refs_1_, bf16[2,512,512]{2,1,0:T(8,128)(2,1)S(1)} %collective-permute-done.8.refs_2_, ...), custom_call_target="tpu_custom_call" | custom-call | flops 1 | bytes 1 | tf_op jit(solution)/shard_map/pallas_call | solution.py:68
  122.2 9.8 %shard_map.66 = (f32[16,512]{1,0:T(8,128)}, f32[512,512]{1,0:T(8,128)}) custom-call(s32[8]{0:T(128)} %stack.55.at_ref._, bf16[16,4096]{1,0:T(8,128)(2,1)} %broadcast_select_fusion.refs_0_, bf16[512,4096]{1,0:T(8,128)(2,1)} %collective-permute-done.12.refs_1_.refs_0_, bf16[2,512,512]{2,1,0:T(8,128)(2,1)} %copy-done.7, bf16[2,512,512]{2,1,0:T(8,128)(2,1)} %copy-done.8, ...), custom_call_target="tpu_custom_call" | custom-call | flops 1 | bytes 1 | tf_op jit(solution)/shard_map/pallas_call | solution.py:124
  132.0 0.9 broadcast_select_fusion.1
  132.9 2.0 shard_map.67.refs_1_
  135.0 2.0 shard_map.68.refs_1_
  137.0 4.2 %shard_map.70.refs_2_ = f32[512,512]{1,0:T(8,128)S(1)} custom-call(s32[8]{0:T(128)S(1)} %copy-done.4, bf16[512,4096]{1,0:T(8,128)(2,1)} %collective-permute-done.12.refs_1_.refs_0_, bf16[2,512,512]{2,1,0:T(8,128)(2,1)S(1)} %pad_maximum_fusion.refs_1_, bf16[2,512,512]{2,1,0:T(8,128)(2,1)S(1)} %collective-permute-done.8.refs_2_, ...), custom_call_target="tpu_custom_call" | custom-call | flops 1 | bytes 1 | tf_op jit(solution)/shard_map/pallas_call | solution.py:68
  141.2 3.2 %shard_map.71.refs_2_ = bf16[512,512]{1,0:T(8,128)(2,1)S(1)} custom-call(s32[2]{0:T(128)S(1)} %pad_add_fusion.at_ref, bf16[512,4096]{1,0:T(8,128)(2,1)} %collective-permute-done.12.refs_1_.refs_0_, f32[512,512]{1,0:T(8,128)S(1)} %shard_map.68.refs_1_, f32[512,512]{1,0:T(8,128)S(1)} %shard_map.70.refs_2_, bf16[512,512]{1,0:T(8,128)(2,1)} %collective-permute-done.13.refs_3_, ...), custom_call_target="tpu_custom_call" | custom-call | flops 1 | bytes 1 | tf_op jit(solution)/shard_map/pallas_call | solution.py:68
  144.5 3.2 %shard_map.69.refs_0_ = bf16[512,512]{1,0:T(8,128)(2,1)S(1)} custom-call(s32[2]{0:T(128)S(1)} %pad_add_fusion.at_ref, bf16[512,4096]{1,0:T(8,128)(2,1)} %all-gather.2.cloned.1.call-done.refs_0_, f32[512,512]{1,0:T(8,128)S(1)} %shard_map.67.refs_1_, f32[512,512]{1,0:T(8,128)S(1)} %shard_map.65.refs_2_, bf16[512,512]{1,0:T(8,128)(2,1)} %collective-permute-done.13.refs_3_, ...), custom_call_target="tpu_custom_call" | custom-call | flops 1 | bytes 1 | tf_op jit(solution)/shard_map/pallas_call | solution.py:68
  147.7 0.6 collective-permute-start.16
  148.3 3.5 %collective-permute-done.17.refs_5_ = bf16[1024,512]{1,0:T(8,128)(2,1)} collective-permute-done((bf16[1024,512]{1,0:T(8,128)(2,1)}, bf16[1024,512]{1,0:T(8,128)(2,1)}, u32[]{:S(2)}, u32[]{:S(2)}) %collective-permute-start.17) | collective-permute-done | bytes 1048608 | tf_op jit(solution)/shard_map/ppermute | solution.py:280
  151.9 6.6 %shard_map.72 = bf16[1024,1536]{1,0:T(8,128)(2,1)} custom-call(s32[2]{0:T(128)S(1)} %pad_add_fusion.1.at_ref, bf16[512,512]{1,0:T(8,128)(2,1)S(1)} %shard_map.69.refs_0_, bf16[512,512]{1,0:T(8,128)(2,1)S(1)} %collective-permute-done.15.refs_1_, bf16[512,512]{1,0:T(8,128)(2,1)S(1)} %shard_map.71.refs_2_, ...), custom_call_target="tpu_custom_call" | custom-call | flops 1 | bytes 1 | tf_op jit(solution)/shard_map/pallas_call | solution.py:241
  158.5 1.1 slice.73
  160.0 1.1 slice.74
  161.1 1.5 collective-permute-start.20
  162.6 9.7 %collective-permute-done.19.refs_4_ = bf16[512,512]{1,0:T(8,128)(2,1)S(1)} collective-permute-done((bf16[512,512]{1,0:T(8,128)(2,1)S(1)}, bf16[512,512]{1,0:T(8,128)(2,1)S(1)}, u32[]{:S(2)}, u32[]{:S(2)}) %collective-permute-start.19) | collective-permute-done | bytes 524320 | tf_op jit(solution)/shard_map/ppermute | solution.py:280
  172.3 2.0 collective-permute-done.20.refs_5_
  174.4 1.9 shard_map.73
  176.3 3.5 %collective-permute-start.21 = (bf16[256,512]{1,0:T(8,128)(2,1)S(1)}, bf16[256,512]{1,0:T(8,128)(2,1)S(1)}, u32[]{:S(2)}, u32[]{:S(2)}) collective-permute-start(bf16[256,512]{1,0:T(8,128)(2,1)S(1)} %get-tuple-element.87), channel_id=1, source_target_pairs={{0,1},{1,2},{2,3},{4,5},{5,6},{6,7},{8,9},{9,10},{10,11},{12,13},{... | collective-permute-start | bytes 786440 | tf_op jit(solution)/shard_map/ppermute | solution.py:415
  179.8 1.3 collective-permute-start.24
  181.1 10.2 %collective-permute-done.21 = bf16[256,512]{1,0:T(8,128)(2,1)S(1)} collective-permute-done((bf16[256,512]{1,0:T(8,128)(2,1)S(1)}, bf16[256,512]{1,0:T(8,128)(2,1)S(1)}, u32[]{:S(2)}, u32[]{:S(2)}) %collective-permute-start.21) | collective-permute-done | bytes 262176 | tf_op jit(solution)/shard_map/ppermute | solution.py:415
  191.2 10.8 %collective-permute-done.24 = bf16[256,512]{1,0:T(8,128)(2,1)S(1)} collective-permute-done((bf16[256,512]{1,0:T(8,128)(2,1)S(1)}, bf16[256,512]{1,0:T(8,128)(2,1)S(1)}, u32[]{:S(2)}, u32[]{:S(2)}) %collective-permute-start.24) | collective-permute-done | bytes 262176 | tf_op jit(solution)/shard_map/ppermute | solution.py:416
  202.2 1.3 collective-permute-start.25
  203.5 4.6 %collective-permute-start.22 = (bf16[256,512]{1,0:T(8,128)(2,1)S(1)}, bf16[256,512]{1,0:T(8,128)(2,1)S(1)}, u32[]{:S(2)}, u32[]{:S(2)}) collective-permute-start(bf16[256,512]{1,0:T(8,128)(2,1)S(1)} %get-tuple-element.105), channel_id=1, source_target_pairs={{0,1},{1,2},{2,3},{4,5},{5,6},{6,7},{8,9},{9,10},{10,11},{12,13},{... | collective-permute-start | bytes 786440 | tf_op jit(solution)/shard_map/ppermute | solution.py:415
  208.1 15.2 %collective-permute-done.25 = bf16[256,512]{1,0:T(8,128)(2,1)S(1)} collective-permute-done((bf16[256,512]{1,0:T(8,128)(2,1)S(1)}, bf16[256,512]{1,0:T(8,128)(2,1)S(1)}, u32[]{:S(2)}, u32[]{:S(2)}) %collective-permute-start.25) | collective-permute-done | bytes 262176 | tf_op jit(solution)/shard_map/ppermute | solution.py:416
  223.3 1.3 collective-permute-start.26
  224.7 4.6 %collective-permute-start.23 = (bf16[256,512]{1,0:T(8,128)(2,1)S(1)}, bf16[256,512]{1,0:T(8,128)(2,1)S(1)}, u32[]{:S(2)}, u32[]{:S(2)}) collective-permute-start(bf16[256,512]{1,0:T(8,128)(2,1)S(1)} %add_convert_fusion.1), channel_id=1, source_target_pairs={{0,1},{1,2},{2,3},{4,5},{5,6},{6,7},{8,9},{9,10},{10,11},{12,13},{... | collective-permute-start | bytes 786440 | tf_op jit(solution)/shard_map/ppermute | solution.py:415
  229.3 4.3 %collective-permute-done.26 = bf16[256,512]{1,0:T(8,128)(2,1)S(1)} collective-permute-done((bf16[256,512]{1,0:T(8,128)(2,1)S(1)}, bf16[256,512]{1,0:T(8,128)(2,1)S(1)}, u32[]{:S(2)}, u32[]{:S(2)}) %collective-permute-start.26) | collective-permute-done | bytes 262176 | tf_op jit(solution)/shard_map/ppermute | solution.py:416
  233.8 1.3 collective-permute-done.27
  235.1 1.2 fusion.26
  236.7 1.4 fusion.24
  238.8 1.0 copy-done.15
  239.7 0.9 fusion.21
  (78 shorter events, 3.9 us)
Async XLA Ops:
  6.5 111.3 %copy-start = (f32[7,64]{1,0:T(8,128)S(1)}, f32[7,64]{1,0:T(8,128)}, u32[]{:S(2)}) copy-start(f32[7,64]{1,0:T(8,128)} %param.9) | copy-start | bytes 5380
  6.5 87.1 %all-gather.2.cloned.1.call-start = ((), (), s32[]{:S(2)}) async-start(), calls=%async_computation.1 | async-start | bytes 5242880 | tf_op jit(solution)/shard_map/all_gather | solution.py:331
  6.5 1.9 copy-start.5
  6.5 2.2 copy-start.16
  8.3 4.8 %copy-start.7 = (bf16[2,512,512]{2,1,0:T(8,128)(2,1)}, bf16[2,512,512]{2,1,0:T(8,128)(2,1)S(1)}, u32[]{:S(2)}) copy-start(bf16[2,512,512]{2,1,0:T(8,128)(2,1)S(1)} %get-tuple-element.58.refs_1_.refs_2_) | copy-start | bytes 3145732
  10.0 225.1 %reduce-scatter.2.cloned.1.call-start = ((), (), s32[]{:S(2)}) async-start(), calls=%async_computation.2 | async-start | bytes 3932160 | tf_op jit(solution)/shard_map/reduce_scatter | solution.py:424
  10.1 4.6 %collective-permute-start = (bf16[2,512,512]{2,1,0:T(8,128)(2,1)S(1)}, bf16[2,512,512]{2,1,0:T(8,128)(2,1)S(1)}, u32[]{:S(2)}, u32[]{:S(2)}) collective-permute-start(bf16[2,512,512]{2,1,0:T(8,128)(2,1)S(1)} %get-tuple-element.94), channel_id=1, source_target_pairs={{0,4},{4,0},{8,12},{12,8},{16,20},{20,16},{24,28},{28,24},{1,5},{5... | collective-permute-start | bytes 3145736 | tf_op jit(solution)/shard_map/ppermute | solution.py:283
  10.6 26.6 %collective-permute-start.1 = (bf16[2,512,512]{2,1,0:T(8,128)(2,1)S(1)}, bf16[2,512,512]{2,1,0:T(8,128)(2,1)S(1)}, u32[]{:S(2)}, u32[]{:S(2)}) collective-permute-start(bf16[2,512,512]{2,1,0:T(8,128)(2,1)S(1)} %get-tuple-element.58.refs_1_.refs_2_), channel_id=1, source_target_pairs={{8,0},{12,4},{0,8},{4,12},{24,16},{28,20},{16,24},{20,28},{9,1},{1... | collective-permute-start | bytes 3145736 | tf_op jit(solution)/shard_map/ppermute | solution.py:280
  13.2 26.0 %collective-permute-start.3 = (bf16[2,512,512]{2,1,0:T(8,128)(2,1)S(1)}, bf16[2,512,512]{2,1,0:T(8,128)(2,1)S(1)}, u32[]{:S(2)}, u32[]{:S(2)}) collective-permute-start(bf16[2,512,512]{2,1,0:T(8,128)(2,1)S(1)} %get-tuple-element.58.refs_1_.refs_2_), channel_id=1, source_target_pairs={{16,0},{20,4},{24,8},{28,12},{0,16},{4,20},{8,24},{12,28},{17,1},{... | collective-permute-start | bytes 3145736 | tf_op jit(solution)/shard_map/ppermute | solution.py:280
  14.7 5.9 %copy-start.8 = (bf16[2,512,512]{2,1,0:T(8,128)(2,1)}, bf16[2,512,512]{2,1,0:T(8,128)(2,1)S(1)}, u32[]{:S(2)}) copy-start(bf16[2,512,512]{2,1,0:T(8,128)(2,1)S(1)} %collective-permute-done.refs_2_.refs_3_) | copy-start | bytes 3145732
  14.7 44.7 %collective-permute-start.2 = (bf16[2,512,512]{2,1,0:T(8,128)(2,1)S(1)}, bf16[2,512,512]{2,1,0:T(8,128)(2,1)S(1)}, u32[]{:S(2)}, u32[]{:S(2)}) collective-permute-start(bf16[2,512,512]{2,1,0:T(8,128)(2,1)S(1)} %collective-permute-done.refs_2_.refs_3_), channel_id=1, source_target_pairs={{8,0},{12,4},{0,8},{4,12},{24,16},{28,20},{16,24},{20,28},{9,1},{1... | collective-permute-start | bytes 3145736 | tf_op jit(solution)/shard_map/ppermute | solution.py:280
  15.8 45.1 %collective-permute-start.4 = (bf16[2,512,512]{2,1,0:T(8,128)(2,1)S(1)}, bf16[2,512,512]{2,1,0:T(8,128)(2,1)S(1)}, u32[]{:S(2)}, u32[]{:S(2)}) collective-permute-start(bf16[2,512,512]{2,1,0:T(8,128)(2,1)S(1)} %collective-permute-done.refs_2_.refs_3_), channel_id=1, source_target_pairs={{16,0},{20,4},{24,8},{28,12},{0,16},{4,20},{8,24},{12,28},{17,1},{... | collective-permute-start | bytes 3145736 | tf_op jit(solution)/shard_map/ppermute | solution.py:280
  18.5 2.0 collective-permute-start.5
  37.2 25.8 %copy-start.9 = (bf16[2,512,512]{2,1,0:T(8,128)(2,1)}, bf16[2,512,512]{2,1,0:T(8,128)(2,1)S(1)}, u32[]{:S(2)}) copy-start(bf16[2,512,512]{2,1,0:T(8,128)(2,1)S(1)} %collective-permute-done.1.refs_3_.refs_4_) | copy-start | bytes 3145732
  39.2 47.8 %copy-start.10 = (bf16[2,512,512]{2,1,0:T(8,128)(2,1)}, bf16[2,512,512]{2,1,0:T(8,128)(2,1)S(1)}, u32[]{:S(2)}) copy-start(bf16[2,512,512]{2,1,0:T(8,128)(2,1)S(1)} %collective-permute-done.3.refs_5_.refs_6_) | copy-start | bytes 3145732
  59.4 27.6 %copy-start.11 = (bf16[2,512,512]{2,1,0:T(8,128)(2,1)}, bf16[2,512,512]{2,1,0:T(8,128)(2,1)S(1)}, u32[]{:S(2)}) copy-start(bf16[2,512,512]{2,1,0:T(8,128)(2,1)S(1)} %collective-permute-done.2.refs_4_.refs_5_) | copy-start | bytes 3145732
  60.9 26.1 %copy-start.12 = (bf16[2,512,512]{2,1,0:T(8,128)(2,1)}, bf16[2,512,512]{2,1,0:T(8,128)(2,1)S(1)}, u32[]{:S(2)}) copy-start(bf16[2,512,512]{2,1,0:T(8,128)(2,1)S(1)} %collective-permute-done.4.refs_6_.refs_7_) | copy-start | bytes 3145732
  60.9 26.1 %collective-permute-start.6 = (bf16[2,512,512]{2,1,0:T(8,128)(2,1)S(1)}, bf16[2,512,512]{2,1,0:T(8,128)(2,1)S(1)}, u32[]{:S(2)}, u32[]{:S(2)}) collective-permute-start(bf16[2,512,512]{2,1,0:T(8,128)(2,1)S(1)} %collective-permute-done.1.refs_3_.refs_4_), channel_id=1, source_target_pairs={{16,0},{20,4},{24,8},{28,12},{0,16},{4,20},{8,24},{12,28},{17,1},{... | collective-permute-start | bytes 3145736 | tf_op jit(solution)/shard_map/ppermute | solution.py:280
  62.4 26.2 %collective-permute-start.7 = (bf16[2,512,512]{2,1,0:T(8,128)(2,1)S(1)}, bf16[2,512,512]{2,1,0:T(8,128)(2,1)}, u32[]{:S(2)}, u32[]{:S(2)}) collective-permute-start(bf16[2,512,512]{2,1,0:T(8,128)(2,1)S(1)} %collective-permute-done.4.refs_6_.refs_7_), channel_id=1, source_target_pairs={{8,0},{12,4},{0,8},{4,12},{24,16},{28,20},{16,24},{20,28},{9,1},{1... | collective-permute-start | bytes 3145736 | tf_op jit(solution)/shard_map/ppermute | solution.py:280
  62.9 48.0 %collective-permute-start.8 = (bf16[2,512,512]{2,1,0:T(8,128)(2,1)S(1)}, bf16[2,512,512]{2,1,0:T(8,128)(2,1)S(1)}, u32[]{:S(2)}, u32[]{:S(2)}) collective-permute-start(bf16[2,512,512]{2,1,0:T(8,128)(2,1)S(1)} %pad_maximum_fusion.refs_1_), channel_id=1, source_target_pairs={{8,0},{12,4},{0,8},{4,12},{24,16},{28,20},{16,24},{20,28},{9,1},{1... | collective-permute-start | bytes 3145736 | tf_op jit(solution)/shard_map/ppermute | solution.py:280
  64.4 46.5 %collective-permute-start.9 = (bf16[2,512,512]{2,1,0:T(8,128)(2,1)S(1)}, bf16[2,512,512]{2,1,0:T(8,128)(2,1)S(1)}, u32[]{:S(2)}, u32[]{:S(2)}) collective-permute-start(bf16[2,512,512]{2,1,0:T(8,128)(2,1)S(1)} %pad_maximum_fusion.refs_1_), channel_id=1, source_target_pairs={{16,0},{20,4},{24,8},{28,12},{0,16},{4,20},{8,24},{12,28},{17,1},{... | collective-permute-start | bytes 3145736 | tf_op jit(solution)/shard_map/ppermute | solution.py:280
  87.0 1.0 copy-start.13
  94.6 11.6 %collective-permute-start.10 = (bf16[16,4096]{1,0:T(8,128)(2,1)S(1)}, bf16[16,4096]{1,0:T(8,128)(2,1)S(1)}, u32[]{:S(2)}, u32[]{:S(2)}) collective-permute-start(bf16[16,4096]{1,0:T(8,128)(2,1)S(1)} %slice.56), channel_id=1, source_target_pairs={{4,8},{12,16},{20,24},{5,9},{13,17},{21,25},{6,10},{14,18},{22,26}... | collective-permute-start | bytes 393224 | tf_op jit(solution)/shard_map/ppermute | solution.py:355
  95.2 10.9 %collective-permute-start.11 = (bf16[16,4096]{1,0:T(8,128)(2,1)S(1)}, bf16[16,4096]{1,0:T(8,128)(2,1)S(1)}, u32[]{:S(2)}, u32[]{:S(2)}) collective-permute-start(bf16[16,4096]{1,0:T(8,128)(2,1)S(1)} %slice.56), channel_id=1, source_target_pairs={{4,12},{12,20},{20,28},{5,13},{13,21},{21,29},{6,14},{14,22},{22,3... | collective-permute-start | bytes 393224 | tf_op jit(solution)/shard_map/ppermute | solution.py:355
  106.1 12.1 %copy-start.3 = (s32[8]{0:T(128)S(1)}, s32[8]{0:T(128)}, u32[]{:S(2)}) copy-start(s32[8]{0:T(128)} %stack.55.at_ref._) | copy-start | bytes 100
  111.0 11.3 %collective-permute-start.12 = (bf16[512,4096]{1,0:T(8,128)(2,1)}, bf16[512,4096]{1,0:T(8,128)(2,1)}, u32[]{:S(2)}, u32[]{:S(2)}) collective-permute-start(bf16[512,4096]{1,0:T(8,128)(2,1)} %all-gather.2.cloned.1.call-done.refs_0_), channel_id=1, source_target_pairs={{0,4},{4,0},{8,12},{12,8},{16,20},{20,16},{24,28},{28,24},{1,5},{5... | collective-permute-start | bytes 12582920 | tf_op jit(solution)/shard_map/ppermute | solution.py:283
  113.0 28.2 %collective-permute-start.13 = (bf16[512,512]{1,0:T(8,128)(2,1)}, bf16[512,512]{1,0:T(8,128)(2,1)}, u32[]{:S(2)}, u32[]{:S(2)}) collective-permute-start(bf16[512,512]{1,0:T(8,128)(2,1)} %slice_bitcast_fusion.1), channel_id=1, source_target_pairs={{16,0},{20,4},{24,8},{28,12},{0,16},{4,20},{8,24},{12,28},{17,1},{... | collective-permute-start | bytes 1572872 | tf_op jit(solution)/shard_map/ppermute | solution.py:280
  115.5 25.7 %collective-permute-start.14 = (bf16[512,512]{1,0:T(8,128)(2,1)}, bf16[512,512]{1,0:T(8,128)(2,1)}, u32[]{:S(2)}, u32[]{:S(2)}) collective-permute-start(bf16[512,512]{1,0:T(8,128)(2,1)} %slice_bitcast_fusion), channel_id=1, source_target_pairs={{8,0},{12,4},{0,8},{4,12},{24,16},{28,20},{16,24},{20,28},{9,1},{1... | collective-permute-start | bytes 1572872 | tf_op jit(solution)/shard_map/ppermute | solution.py:280
  115.5 36.3 %collective-permute-start.17 = (bf16[1024,512]{1,0:T(8,128)(2,1)}, bf16[1024,512]{1,0:T(8,128)(2,1)}, u32[]{:S(2)}, u32[]{:S(2)}) collective-permute-start(bf16[1024,512]{1,0:T(8,128)(2,1)} %refs_4_.1), channel_id=1, source_target_pairs={{8,0},{12,4},{0,8},{4,12},{24,16},{28,20},{16,24},{20,28},{9,1},{1... | collective-permute-start | bytes 3145736 | tf_op jit(solution)/shard_map/ppermute | solution.py:280
  117.5 34.3 %collective-permute-start.18 = (bf16[1024,512]{1,0:T(8,128)(2,1)}, bf16[1024,512]{1,0:T(8,128)(2,1)}, u32[]{:S(2)}, u32[]{:S(2)}) collective-permute-start(bf16[1024,512]{1,0:T(8,128)(2,1)} %refs_4_.1), channel_id=1, source_target_pairs={{16,0},{20,4},{24,8},{28,12},{0,16},{4,20},{8,24},{12,28},{17,1},{... | collective-permute-start | bytes 3145736 | tf_op jit(solution)/shard_map/ppermute | solution.py:280
  122.2 9.8 %copy-start.1 = (f32[512,512]{1,0:T(8,128)S(1)}, f32[512,512]{1,0:T(8,128)}, u32[]{:S(2)}) copy-start(f32[512,512]{1,0:T(8,128)} %shard_map.64.product_ref) | copy-start | bytes 3145732
  122.2 10.7 %copy-start.4 = (s32[8]{0:T(128)S(1)}, s32[8]{0:T(128)}, u32[]{:S(2)}) copy-start(s32[8]{0:T(128)} %stack.55.at_ref._) | copy-start | bytes 100
  132.0 2.9 %copy-start.2 = (f32[512,512]{1,0:T(8,128)S(1)}, f32[512,512]{1,0:T(8,128)}, u32[]{:S(2)}) copy-start(f32[512,512]{1,0:T(8,128)} %get-tuple-element.73.product_ref) | copy-start | bytes 3145732
  144.4 7.4 %collective-permute-start.15 = (bf16[512,512]{1,0:T(8,128)(2,1)S(1)}, bf16[512,512]{1,0:T(8,128)(2,1)S(1)}, u32[]{:S(2)}, u32[]{:S(2)}) collective-permute-start(bf16[512,512]{1,0:T(8,128)(2,1)S(1)} %shard_map.71.refs_2_), channel_id=1, source_target_pairs={{0,4},{4,0},{8,12},{12,8},{16,20},{20,16},{24,28},{28,24},{1,5},{5... | collective-permute-start | bytes 1572872 | tf_op jit(solution)/shard_map/ppermute | solution.py:283
  147.7 4.2 %collective-permute-start.16 = (bf16[512,512]{1,0:T(8,128)(2,1)S(1)}, bf16[512,512]{1,0:T(8,128)(2,1)S(1)}, u32[]{:S(2)}, u32[]{:S(2)}) collective-permute-start(bf16[512,512]{1,0:T(8,128)(2,1)S(1)} %shard_map.69.refs_0_), channel_id=1, source_target_pairs={{0,4},{4,0},{8,12},{12,8},{16,20},{20,16},{24,28},{28,24},{1,5},{5... | collective-permute-start | bytes 1572872 | tf_op jit(solution)/shard_map/ppermute | solution.py:283
  159.6 12.7 %collective-permute-start.19 = (bf16[512,512]{1,0:T(8,128)(2,1)S(1)}, bf16[512,512]{1,0:T(8,128)(2,1)S(1)}, u32[]{:S(2)}, u32[]{:S(2)}) collective-permute-start(bf16[512,512]{1,0:T(8,128)(2,1)S(1)} %slice.73), channel_id=1, source_target_pairs={{16,0},{20,4},{24,8},{28,12},{0,16},{4,20},{8,24},{12,28},{17,1},{... | collective-permute-start | bytes 1572872 | tf_op jit(solution)/shard_map/ppermute | solution.py:280
  161.1 13.3 %collective-permute-start.20 = (bf16[512,512]{1,0:T(8,128)(2,1)S(1)}, bf16[512,512]{1,0:T(8,128)(2,1)S(1)}, u32[]{:S(2)}, u32[]{:S(2)}) collective-permute-start(bf16[512,512]{1,0:T(8,128)(2,1)S(1)} %slice.74), channel_id=1, source_target_pairs={{8,0},{12,4},{0,8},{4,12},{24,16},{28,20},{16,24},{20,28},{9,1},{1... | collective-permute-start | bytes 1572872 | tf_op jit(solution)/shard_map/ppermute | solution.py:280
  176.3 15.0 %collective-permute-start.21 = (bf16[256,512]{1,0:T(8,128)(2,1)S(1)}, bf16[256,512]{1,0:T(8,128)(2,1)S(1)}, u32[]{:S(2)}, u32[]{:S(2)}) collective-permute-start(bf16[256,512]{1,0:T(8,128)(2,1)S(1)} %get-tuple-element.87), channel_id=1, source_target_pairs={{0,1},{1,2},{2,3},{4,5},{5,6},{6,7},{8,9},{9,10},{10,11},{12,13},{... | collective-permute-start | bytes 786440 | tf_op jit(solution)/shard_map/ppermute | solution.py:415
  179.8 22.3 %collective-permute-start.24 = (bf16[256,512]{1,0:T(8,128)(2,1)S(1)}, bf16[256,512]{1,0:T(8,128)(2,1)S(1)}, u32[]{:S(2)}, u32[]{:S(2)}) collective-permute-start(bf16[256,512]{1,0:T(8,128)(2,1)S(1)} %get-tuple-element.85), channel_id=1, source_target_pairs={{1,0},{2,1},{3,2},{5,4},{6,5},{7,6},{9,8},{10,9},{11,10},{13,12},{... | collective-permute-start | bytes 786440 | tf_op jit(solution)/shard_map/ppermute | solution.py:416
  202.2 21.0 %collective-permute-start.25 = (bf16[256,512]{1,0:T(8,128)(2,1)S(1)}, bf16[256,512]{1,0:T(8,128)(2,1)S(1)}, u32[]{:S(2)}, u32[]{:S(2)}) collective-permute-start(bf16[256,512]{1,0:T(8,128)(2,1)S(1)} %get-tuple-element.106), channel_id=1, source_target_pairs={{1,0},{2,1},{3,2},{5,4},{6,5},{7,6},{9,8},{10,9},{11,10},{13,12},{... | collective-permute-start | bytes 786440 | tf_op jit(solution)/shard_map/ppermute | solution.py:416
  203.5 21.1 %collective-permute-start.22 = (bf16[256,512]{1,0:T(8,128)(2,1)S(1)}, bf16[256,512]{1,0:T(8,128)(2,1)S(1)}, u32[]{:S(2)}, u32[]{:S(2)}) collective-permute-start(bf16[256,512]{1,0:T(8,128)(2,1)S(1)} %get-tuple-element.105), channel_id=1, source_target_pairs={{0,1},{1,2},{2,3},{4,5},{5,6},{6,7},{8,9},{9,10},{10,11},{12,13},{... | collective-permute-start | bytes 786440 | tf_op jit(solution)/shard_map/ppermute | solution.py:415
  223.3 10.2 %collective-permute-start.26 = (bf16[256,512]{1,0:T(8,128)(2,1)S(1)}, bf16[256,512]{1,0:T(8,128)(2,1)S(1)}, u32[]{:S(2)}, u32[]{:S(2)}) collective-permute-start(bf16[256,512]{1,0:T(8,128)(2,1)S(1)} %add_convert_fusion), channel_id=1, source_target_pairs={{1,0},{2,1},{3,2},{5,4},{6,5},{7,6},{9,8},{10,9},{11,10},{13,12},{... | collective-permute-start | bytes 786440 | tf_op jit(solution)/shard_map/ppermute | solution.py:416
  224.7 8.9 %collective-permute-start.23 = (bf16[256,512]{1,0:T(8,128)(2,1)S(1)}, bf16[256,512]{1,0:T(8,128)(2,1)S(1)}, u32[]{:S(2)}, u32[]{:S(2)}) collective-permute-start(bf16[256,512]{1,0:T(8,128)(2,1)S(1)} %add_convert_fusion.1), channel_id=1, source_target_pairs={{0,1},{1,2},{2,3},{4,5},{5,6},{6,7},{8,9},{9,10},{10,11},{12,13},{... | collective-permute-start | bytes 786440 | tf_op jit(solution)/shard_map/ppermute | solution.py:415
  233.6 3.0 %copy-start.6 = (bf16[128,4096]{1,0:T(8,128)(2,1)S(1)}, bf16[128,4096]{1,0:T(8,128)(2,1)}, u32[]{:S(2)}) copy-start(bf16[128,4096]{1,0:T(8,128)(2,1)} %param.6) | copy-start | bytes 3145732
  233.7 1.4 collective-permute-start.27
  236.3 1.8 collective-permute-start.28
  236.7 1.8 copy-start.14
  238.8 1.0 copy-start.15
Sparse Core Ops, SparseCore 0:
  10.2 83.4 all-gather.1
  158.6 74.6 reduce-scatter.1

commit v17 on v16

--- a/solution.py
+++ b/solution.py
@@ -220,13 +220,18 @@
             held[place, columns] = gate[slot * rows : (slot + 1) * rows]
     wide = weights[0].shape[1]
     leaving = []
-    for index, weight in enumerate(weights):
-        copies[index].wait()
+    tile = math.gcd(wide, 256)
+    for index in range((count + 1) // 2):
+        parts = [0] if index == 0 else [2 * index - 1, 2 * index]
+        for part in parts:
+            copies[part].wait()
         at = slice(index * wide, (index + 1) * wide)
-        tile = math.gcd(wide, 256)
         for low in range(0, wide, tile):
-            total = dot(held[:, :half], weight[:half, low : low + tile])
-            total = total + dot(held[:, half:], weight[half:, low : low + tile])
+            total, depth = None, 0
+            for part in parts:
+                size = weights[part].shape[0]
+                new = dot(held[:, depth : depth + size], weights[part][:, low : low + tile])
+                total, depth = new if total is None else total + new, depth + size
             ready[:, index * wide + low : index * wide + low + tile] = total.astype(BF16)
         leaving.append(pltpu.make_async_copy(ready.at[:, at], out_ref.at[:, at], out_sems.at[index]))
         leaving[-1].start()
@@ -236,7 +241,7 @@
 
 def near_terms(n_tp, place, gates, weights):
     length, half = gates[0].shape
-    shape = (2 * length, len(weights) * weights[0].shape[1])
+    shape = (2 * length, (len(weights) + 1) // 2 * weights[0].shape[1])
     anywhere = pl.BlockSpec(memory_space=pl.ANY)
     return pl.pallas_call(
         functools.partial(near_kernel, n_tp),
@@ -333,7 +338,8 @@
     mine_q = columns(in_weight_then, 0, 1, core)[0]
     both_q = jnp.stack([mine_q, from_partner(columns(in_weight_then, 0, 1, 1 - core)[0])])
 
-    kv_x, kv_y, both_q = lax.optimization_barrier((kv_x, kv_y, both_q))
+    halves = (out_weight[:half], out_weight[half:])
+    kv_x, kv_y, both_q, halves = lax.optimization_barrier((kv_x, kv_y, both_q, halves))
     kv_rest = onward(kv_x, kv_y)
     q_x = {(0, dx): from_chip(both_q, 0, dx) for dx in range(1, nx)}
     q_y = {(dy, 0): from_chip(both_q, dy, 0) for dy in range(1, ny)}
@@ -378,17 +384,11 @@
         (other_rows, own_filtered, other_filtered)
     )
     other_query = project(query_kernel, at, [other_rows], [], q_early, F32)
-    weight_then, q_x, q_y = lax.optimization_barrier((out_weight, q_x, q_y))
-    o_x = {(0, dx): from_chip(weight_then, 0, dx) for dx in range(1, nx)}
-    o_y = {(dy, 0): from_chip(weight_then, dy, 0) for dy in range(1, ny)}
-    o_rest = {
-        (dy, dx): (
-            from_chip(o_x[0, dx][:half], dy, 0),
-            from_chip(o_y[dy, 0][half:], 0, dx),
-        )
-        for dy in range(1, ny)
-        for dx in range(1, nx)
-    }
+    halves, q_x, q_y = lax.optimization_barrier((halves, q_x, q_y))
+    o_x, o_y = direct(*halves)
+    o_rest = onward(o_x, o_y)
+    o_x = {(0, dx): o_x[dx] for dx in range(1, nx)}
+    o_y = {(dy, 0): o_y[dy] for dy in range(1, ny)}
     late = [piece for pair in q_rest.values() for piece in pair]
     other_gated = project(
         gate_kernel, at[early:], [other_rows], [other_filtered, other_query], late, BF16
@@ -418,8 +418,8 @@
         return total
 
     near = {(0, 0): (out_weight,)}
-    near.update({key: (block,) for key, block in (*o_x.items(), *o_y.items())})
-    found = near_terms(n_tp, here_at, gates, [block for (block,) in near.values()])
+    near.update({**o_x, **o_y})
+    found = near_terms(n_tp, here_at, gates, [part for parts in near.values() for part in parts])
     gates, found = lax.optimization_barrier((gates, found))
     near_sum = lax.psum_scatter(found, "tp", scatter_dimension=0, tiled=True)
     far_sum = chained(terms(n_tp, here_at, gates, list(o_rest.values()), True))

time: 248 us -> 251 us (1.012)
  waiting for transfers between devices: 131 us -> 134 us
    ppermute x3, waiting for transfers between devices: 30.3 us -> 34.4 us  [chained(): falling = lax.ppermute(send_down, 'tp', down)]
    ppermute x14 -> x16, starting transfers between devices: 16.7 us -> 18.6 us  [from_chip(): return lax.ppermute(block, 'seq', route)]
    ppermute x14 -> x16, waiting for transfers between devices: 82.3 us -> 82.3 us  [from_chip(): return lax.ppermute(block, 'seq', route)]
  transfers between devices with their start and end apart: 31 -> 33, of which waited for: 17 -> 19; matrix products, arithmetic and copies ran while one was open for 4% -> 4% of each run, Pallas kernels for 16% -> 16%
where the time goes in v17:
time: 251 us
  waiting for transfers between devices  134 us (53%)
  Pallas kernels  45.4 us (18%)
  starting transfers between devices  39.4 us (16%)
  between operations  14 us (6%)
  local copies, waits for them, and re-layouts  10.2 us (4%)
  other arithmetic  7.53 us (3%)
    ppermute x16, waiting for transfers between devices, from_chip(): return lax.ppermute(block, 'seq', route)  82.3 us
    ppermute x3, waiting for transfers between devices, chained(): falling = lax.ppermute(send_down, 'tp', down)  34.4 us
    pallas_call x7, Pallas kernels, call(): pl.pallas_call(kernel, out_shape=out, in_specs=[pl.BlockSpec(memory_space...  20.7 us
    pallas_call x2, Pallas kernels, products(): pl.pallas_call(functools.partial(product_kernel, len(xs), len(pieces)), o...  19.1 us
    ppermute x16, starting transfers between devices, from_chip(): return lax.ppermute(block, 'seq', route)  18.6 us
    ppermute x3, starting transfers between devices, chained(): rising = lax.ppermute(send_up, 'tp', up)  12.6 us
    ppermute x3, waiting for transfers between devices, chained(): rising = lax.ppermute(send_up, 'tp', up)  9.58 us
    pallas_call x1, Pallas kernels, near_terms(): pl.pallas_call(functools.partial(near_kernel, n_tp), out_shape=jax.ShapeD...  5.61 us
  transfers between devices with their start and end apart: 33, of which 19 were waited for; matrix products, arithmetic and copies ran while one was open for 4% of the time, Pallas kernels for 16%

profile of v17, /device:TPU:0, one launch (start us, length us, event | category | flops | bytes accessed | tf_op | source)
XLA Modules:
  0.0 250.9 jit_solution(15653860628561209174)
XLA Ops:
  6.5 1.8 constant_dynamic-slice_fusion.2
  8.7 1.3 fusion.2
  10.6 2.6 %collective-permute-start.1 = (bf16[2,512,512]{2,1,0:T(8,128)(2,1)S(1)}, bf16[2,512,512]{2,1,0:T(8,128)(2,1)S(1)}, u32[]{:S(2)}, u32[]{:S(2)}) collective-permute-start(bf16[2,512,512]{2,1,0:T(8,128)(2,1)S(1)} %get-tuple-element.61.refs_1_.refs_2_), channel_id=1, source_target_pairs={{8,0},{12,4},{0,8},{4,12},{24,16},{28,20},{16,24},{20,28},{9,1},{1... | collective-permute-start | bytes 3145736 | tf_op jit(solution)/shard_map/ppermute | solution.py:285
  13.2 1.5 collective-permute-start.3
  14.7 1.1 collective-permute-start.2
  15.8 1.5 collective-permute-start.4
  17.3 1.3 constant_dynamic-slice_fusion.1
  18.6 1.1 fusion.25
  19.7 0.8 collective-permute-done.5
  20.6 16.6 %collective-permute-done.1.refs_3_.refs_4_ = bf16[2,512,512]{2,1,0:T(8,128)(2,1)S(1)} collective-permute-done((bf16[2,512,512]{2,1,0:T(8,128)(2,1)S(1)}, bf16[2,512,512]{2,1,0:T(8,128)(2,1)S(1)}, u32[]{:S(2)}, u32[]{:S(2)}) %collective-permute-start.1) | collective-permute-done | bytes 1048608 | tf_op jit(solution)/shard_map/ppermute | solution.py:285
  37.2 2.0 collective-permute-done.3.refs_5_.refs_6_
  39.2 20.2 %collective-permute-done.2.refs_4_.refs_5_ = bf16[2,512,512]{2,1,0:T(8,128)(2,1)S(1)} collective-permute-done((bf16[2,512,512]{2,1,0:T(8,128)(2,1)S(1)}, bf16[2,512,512]{2,1,0:T(8,128)(2,1)S(1)}, u32[]{:S(2)}, u32[]{:S(2)}) %collective-permute-start.2) | collective-permute-done | bytes 1048608 | tf_op jit(solution)/shard_map/ppermute | solution.py:285
  59.4 1.5 collective-permute-done.4.refs_6_.refs_7_
  60.9 1.5 collective-permute-start.6
  62.4 0.5 collective-permute-start.7
  62.9 1.5 collective-permute-start.8
  64.9 22.0 %collective-permute-done.6.refs_7_.refs_8_ = bf16[2,512,512]{2,1,0:T(8,128)(2,1)S(1)} collective-permute-done((bf16[2,512,512]{2,1,0:T(8,128)(2,1)S(1)}, bf16[2,512,512]{2,1,0:T(8,128)(2,1)S(1)}, u32[]{:S(2)}, u32[]{:S(2)}) %collective-permute-start.6) | collective-permute-done | bytes 1048608 | tf_op jit(solution)/shard_map/ppermute | solution.py:285
  87.0 1.0 copy-done.15
  88.0 0.6 collective-permute-done.7.refs_8_.refs_9_
  88.6 5.1 %all-gather.2.cloned.1.call-done.refs_0_ = bf16[512,4096]{1,0:T(8,128)(2,1)} async-done(((bf16[128,4096]{1,0:T(8,128)(2,1)}), bf16[512,4096]{1,0:T(8,128)(2,1)}) %all-gather.2.cloned.1.call-update) | async-done | bytes 4194320 | tf_op jit(solution)/shard_map/all_gather | solution.py:336
  93.7 0.9 slice.58
  94.6 0.7 collective-permute-start.10
  95.2 0.8 collective-permute-start.11
  96.2 0.7 stack.55.at_ref._
  96.9 9.4 %shard_map.64.product_ref = f32[512,512]{1,0:T(8,128)} custom-call(s32[8]{0:T(128)} %stack.55.at_ref._, bf16[512,4096]{1,0:T(8,128)(2,1)} %all-gather.2.cloned.1.call-done.refs_0_, bf16[2,512,512]{2,1,0:T(8,128)(2,1)} %copy-done.9, bf16[2,512,512]{2,1,0:T(8,128)(2,1)} %copy-done.10, bf16[2,512,512]{2,1,0:T(8,128)(2,1)} %copy-done.11, ...), custom_call_target="tpu_custom_call" | custom-call | flops 1 | bytes 1 | tf_op jit(solution)/shard_map/pallas_call | solution.py:124
  106.4 0.7 broadcast_select_fusion.refs_0_
  107.0 3.9 %collective-permute-done.8.refs_2_ = bf16[2,512,512]{2,1,0:T(8,128)(2,1)S(1)} collective-permute-done((bf16[2,512,512]{2,1,0:T(8,128)(2,1)S(1)}, bf16[2,512,512]{2,1,0:T(8,128)(2,1)S(1)}, u32[]{:S(2)}, u32[]{:S(2)}) %collective-permute-start.8) | collective-permute-done | bytes 1048608 | tf_op jit(solution)/shard_map/ppermute | solution.py:285
  111.0 1.4 collective-permute-start.12
  112.3 0.8 slice_bitcast_fusion.1
  113.2 1.5 collective-permute-start.13
  114.7 0.9 slice_bitcast_fusion
  115.6 2.0 collective-permute-start.17
  118.0 4.0 %shard_map.65.refs_2_ = f32[512,512]{1,0:T(8,128)S(1)} custom-call(s32[8]{0:T(128)S(1)} %copy-done.5, bf16[512,4096]{1,0:T(8,128)(2,1)} %all-gather.2.cloned.1.call-done.refs_0_, bf16[2,512,512]{2,1,0:T(8,128)(2,1)S(1)} %pad_maximum_fusion.refs_1_, bf16[2,512,512]{2,1,0:T(8,128)(2,1)S(1)} %collective-permute-done.8.refs_2_, ...), custom_call_target="tpu_custom_call" | custom-call | flops 1 | bytes 1 | tf_op jit(solution)/shard_map/pallas_call | solution.py:68
  122.0 0.6 collective-permute-start.19
  122.5 1.5 collective-permute-start.18
  124.0 9.7 %shard_map.66 = (f32[16,512]{1,0:T(8,128)}, f32[512,512]{1,0:T(8,128)}) custom-call(s32[8]{0:T(128)} %stack.55.at_ref._, bf16[16,4096]{1,0:T(8,128)(2,1)} %broadcast_select_fusion.refs_0_, bf16[512,4096]{1,0:T(8,128)(2,1)} %collective-permute-done.12.refs_1_.refs_0_, bf16[2,512,512]{2,1,0:T(8,128)(2,1)} %copy-done.9, bf16[2,512,512]{2,1,0:T(8,128)(2,1)} %copy-done.10, ...), custom_call_target="tpu_custom_call" | custom-call | flops 1 | bytes 1 | tf_op jit(solution)/shard_map/pallas_call | solution.py:124
  133.7 0.9 broadcast_select_fusion.1
  134.6 2.0 shard_map.67.refs_1_
  136.6 2.0 shard_map.68.refs_1_
  138.7 4.2 %shard_map.70.refs_2_ = f32[512,512]{1,0:T(8,128)S(1)} custom-call(s32[8]{0:T(128)S(1)} %copy-done.6, bf16[512,4096]{1,0:T(8,128)(2,1)} %collective-permute-done.12.refs_1_.refs_0_, bf16[2,512,512]{2,1,0:T(8,128)(2,1)S(1)} %pad_maximum_fusion.refs_1_, bf16[2,512,512]{2,1,0:T(8,128)(2,1)S(1)} %collective-permute-done.8.refs_2_, ...), custom_call_target="tpu_custom_call" | custom-call | flops 1 | bytes 1 | tf_op jit(solution)/shard_map/pallas_call | solution.py:68
  143.1 3.2 %shard_map.71.refs_2_ = bf16[512,512]{1,0:T(8,128)(2,1)S(1)} custom-call(s32[2]{0:T(128)S(1)} %pad_add_fusion.at_ref, bf16[512,4096]{1,0:T(8,128)(2,1)} %collective-permute-done.12.refs_1_.refs_0_, f32[512,512]{1,0:T(8,128)S(1)} %shard_map.68.refs_1_, f32[512,512]{1,0:T(8,128)S(1)} %shard_map.70.refs_2_, bf16[512,512]{1,0:T(8,128)(2,1)} %collective-permute-done.13.refs_3_, ...), custom_call_target="tpu_custom_call" | custom-call | flops 1 | bytes 1 | tf_op jit(solution)/shard_map/pallas_call | solution.py:68
  146.4 3.3 %shard_map.69.refs_0_ = bf16[512,512]{1,0:T(8,128)(2,1)S(1)} custom-call(s32[2]{0:T(128)S(1)} %pad_add_fusion.at_ref, bf16[512,4096]{1,0:T(8,128)(2,1)} %all-gather.2.cloned.1.call-done.refs_0_, f32[512,512]{1,0:T(8,128)S(1)} %shard_map.67.refs_1_, f32[512,512]{1,0:T(8,128)S(1)} %shard_map.65.refs_2_, bf16[512,512]{1,0:T(8,128)(2,1)} %collective-permute-done.13.refs_3_, ...), custom_call_target="tpu_custom_call" | custom-call | flops 1 | bytes 1 | tf_op jit(solution)/shard_map/pallas_call | solution.py:68
  150.2 1.7 collective-permute-done.18.refs_6_
  151.9 3.8 %collective-permute-done.20.refs_8_ = bf16[512,512]{1,0:T(8,128)(2,1)} collective-permute-done((bf16[512,512]{1,0:T(8,128)(2,1)}, bf16[512,512]{1,0:T(8,128)(2,1)}, u32[]{:S(2)}, u32[]{:S(2)}) %collective-permute-start.20) | collective-permute-done | bytes 524320 | tf_op jit(solution)/shard_map/ppermute | solution.py:285
  155.7 5.6 %shard_map.72 = bf16[1024,1536]{1,0:T(8,128)(2,1)} custom-call(s32[2]{0:T(128)S(1)} %pad_add_fusion.1.at_ref, bf16[512,512]{1,0:T(8,128)(2,1)S(1)} %shard_map.69.refs_0_, bf16[512,512]{1,0:T(8,128)(2,1)S(1)} %collective-permute-done.15.refs_1_, bf16[512,512]{1,0:T(8,128)(2,1)S(1)} %shard_map.71.refs_2_, ...), custom_call_target="tpu_custom_call" | custom-call | flops 1 | bytes 1 | tf_op jit(solution)/shard_map/pallas_call | solution.py:246
  161.8 1.7 collective-permute-start.22
  163.5 9.6 %collective-permute-done.21.refs_4_ = bf16[512,512]{1,0:T(8,128)(2,1)S(1)} collective-permute-done((bf16[512,512]{1,0:T(8,128)(2,1)}, bf16[512,512]{1,0:T(8,128)(2,1)S(1)}, u32[]{:S(2)}, u32[]{:S(2)}) %collective-permute-start.21) | collective-permute-done | bytes 524320 | tf_op jit(solution)/shard_map/ppermute | solution.py:285
  173.5 1.9 shard_map.73
  175.5 3.5 %collective-permute-start.23 = (bf16[256,512]{1,0:T(8,128)(2,1)S(1)}, bf16[256,512]{1,0:T(8,128)(2,1)S(1)}, u32[]{:S(2)}, u32[]{:S(2)}) collective-permute-start(bf16[256,512]{1,0:T(8,128)(2,1)S(1)} %get-tuple-element.93), channel_id=1, source_target_pairs={{0,1},{1,2},{2,3},{4,5},{5,6},{6,7},{8,9},{9,10},{10,11},{12,13},{... | collective-permute-start | bytes 786440 | tf_op jit(solution)/shard_map/ppermute | solution.py:415
  179.0 1.3 collective-permute-start.26
  180.3 9.6 %collective-permute-done.23 = bf16[256,512]{1,0:T(8,128)(2,1)S(1)} collective-permute-done((bf16[256,512]{1,0:T(8,128)(2,1)S(1)}, bf16[256,512]{1,0:T(8,128)(2,1)S(1)}, u32[]{:S(2)}, u32[]{:S(2)}) %collective-permute-start.23) | collective-permute-done | bytes 262176 | tf_op jit(solution)/shard_map/ppermute | solution.py:415
  189.8 11.3 %collective-permute-done.26 = bf16[256,512]{1,0:T(8,128)(2,1)S(1)} collective-permute-done((bf16[256,512]{1,0:T(8,128)(2,1)S(1)}, bf16[256,512]{1,0:T(8,128)(2,1)S(1)}, u32[]{:S(2)}, u32[]{:S(2)}) %collective-permute-start.26) | collective-permute-done | bytes 262176 | tf_op jit(solution)/shard_map/ppermute | solution.py:416
  201.2 1.3 collective-permute-start.27
  202.5 4.6 %collective-permute-start.24 = (bf16[256,512]{1,0:T(8,128)(2,1)S(1)}, bf16[256,512]{1,0:T(8,128)(2,1)S(1)}, u32[]{:S(2)}, u32[]{:S(2)}) collective-permute-start(bf16[256,512]{1,0:T(8,128)(2,1)S(1)} %get-tuple-element.113), channel_id=1, source_target_pairs={{0,1},{1,2},{2,3},{4,5},{5,6},{6,7},{8,9},{9,10},{10,11},{12,13},{... | collective-permute-start | bytes 786440 | tf_op jit(solution)/shard_map/ppermute | solution.py:415
  207.1 14.9 %collective-permute-done.27 = bf16[256,512]{1,0:T(8,128)(2,1)S(1)} collective-permute-done((bf16[256,512]{1,0:T(8,128)(2,1)S(1)}, bf16[256,512]{1,0:T(8,128)(2,1)S(1)}, u32[]{:S(2)}, u32[]{:S(2)}) %collective-permute-start.27) | collective-permute-done | bytes 262176 | tf_op jit(solution)/shard_map/ppermute | solution.py:416
  222.1 1.3 collective-permute-start.28
  223.5 4.6 %collective-permute-start.25 = (bf16[256,512]{1,0:T(8,128)(2,1)S(1)}, bf16[256,512]{1,0:T(8,128)(2,1)S(1)}, u32[]{:S(2)}, u32[]{:S(2)}) collective-permute-start(bf16[256,512]{1,0:T(8,128)(2,1)S(1)} %add_convert_fusion.1), channel_id=1, source_target_pairs={{0,1},{1,2},{2,3},{4,5},{5,6},{6,7},{8,9},{9,10},{10,11},{12,13},{... | collective-permute-start | bytes 786440 | tf_op jit(solution)/shard_map/ppermute | solution.py:415
  228.1 8.1 %collective-permute-done.28 = bf16[256,512]{1,0:T(8,128)(2,1)S(1)} collective-permute-done((bf16[256,512]{1,0:T(8,128)(2,1)S(1)}, bf16[256,512]{1,0:T(8,128)(2,1)S(1)}, u32[]{:S(2)}, u32[]{:S(2)}) %collective-permute-start.28) | collective-permute-done | bytes 262176 | tf_op jit(solution)/shard_map/ppermute | solution.py:416
  236.4 1.3 collective-permute-done.29
  237.8 0.9 reduce-scatter.2.cloned.1.call-done
  238.7 1.2 fusion.27
  240.2 1.4 fusion.24
  242.3 1.0 copy-done.17
  243.2 0.9 fusion.21
  (85 shorter events, 5.1 us)
Async XLA Ops:
  6.5 111.1 %copy-start = (f32[7,64]{1,0:T(8,128)S(1)}, f32[7,64]{1,0:T(8,128)}, u32[]{:S(2)}) copy-start(f32[7,64]{1,0:T(8,128)} %param.9) | copy-start | bytes 5380
  6.5 87.1 %all-gather.2.cloned.1.call-start = ((), (), s32[]{:S(2)}) async-start(), calls=%async_computation.1 | async-start | bytes 5242880 | tf_op jit(solution)/shard_map/all_gather | solution.py:336
  6.5 1.9 copy-start.7
  6.5 2.2 copy-start.18
  8.3 4.9 %copy-start.9 = (bf16[2,512,512]{2,1,0:T(8,128)(2,1)}, bf16[2,512,512]{2,1,0:T(8,128)(2,1)S(1)}, u32[]{:S(2)}) copy-start(bf16[2,512,512]{2,1,0:T(8,128)(2,1)S(1)} %get-tuple-element.61.refs_1_.refs_2_) | copy-start | bytes 3145732
  10.0 8.6 %copy-start.2 = (bf16[1024,512]{1,0:T(8,128)(2,1)S(1)}, bf16[1024,512]{1,0:T(8,128)(2,1)}, u32[]{:S(2)}) copy-start(bf16[1024,512]{1,0:T(8,128)(2,1)} %refs_4_.1) | copy-start | bytes 3145732
  10.0 228.6 %reduce-scatter.2.cloned.1.call-start = ((), (), s32[]{:S(2)}) async-start(), calls=%async_computation.2 | async-start | bytes 3932160 | tf_op jit(solution)/shard_map/reduce_scatter | solution.py:424
  10.1 4.6 %collective-permute-start = (bf16[2,512,512]{2,1,0:T(8,128)(2,1)S(1)}, bf16[2,512,512]{2,1,0:T(8,128)(2,1)S(1)}, u32[]{:S(2)}, u32[]{:S(2)}) collective-permute-start(bf16[2,512,512]{2,1,0:T(8,128)(2,1)S(1)} %get-tuple-element.100), channel_id=1, source_target_pairs={{0,4},{4,0},{8,12},{12,8},{16,20},{20,16},{24,28},{28,24},{1,5},{5... | collective-permute-start | bytes 3145736 | tf_op jit(solution)/shard_map/ppermute | solution.py:288
  10.6 26.6 %collective-permute-start.1 = (bf16[2,512,512]{2,1,0:T(8,128)(2,1)S(1)}, bf16[2,512,512]{2,1,0:T(8,128)(2,1)S(1)}, u32[]{:S(2)}, u32[]{:S(2)}) collective-permute-start(bf16[2,512,512]{2,1,0:T(8,128)(2,1)S(1)} %get-tuple-element.61.refs_1_.refs_2_), channel_id=1, source_target_pairs={{8,0},{12,4},{0,8},{4,12},{24,16},{28,20},{16,24},{20,28},{9,1},{1... | collective-permute-start | bytes 3145736 | tf_op jit(solution)/shard_map/ppermute | solution.py:285
  13.2 26.0 %collective-permute-start.3 = (bf16[2,512,512]{2,1,0:T(8,128)(2,1)S(1)}, bf16[2,512,512]{2,1,0:T(8,128)(2,1)S(1)}, u32[]{:S(2)}, u32[]{:S(2)}) collective-permute-start(bf16[2,512,512]{2,1,0:T(8,128)(2,1)S(1)} %get-tuple-element.61.refs_1_.refs_2_), channel_id=1, source_target_pairs={{16,0},{20,4},{24,8},{28,12},{0,16},{4,20},{8,24},{12,28},{17,1},{... | collective-permute-start | bytes 3145736 | tf_op jit(solution)/shard_map/ppermute | solution.py:285
  14.7 5.0 %copy-start.10 = (bf16[2,512,512]{2,1,0:T(8,128)(2,1)}, bf16[2,512,512]{2,1,0:T(8,128)(2,1)S(1)}, u32[]{:S(2)}) copy-start(bf16[2,512,512]{2,1,0:T(8,128)(2,1)S(1)} %collective-permute-done.refs_2_.refs_3_) | copy-start | bytes 3145732
  14.7 44.7 %collective-permute-start.2 = (bf16[2,512,512]{2,1,0:T(8,128)(2,1)S(1)}, bf16[2,512,512]{2,1,0:T(8,128)(2,1)S(1)}, u32[]{:S(2)}, u32[]{:S(2)}) collective-permute-start(bf16[2,512,512]{2,1,0:T(8,128)(2,1)S(1)} %collective-permute-done.refs_2_.refs_3_), channel_id=1, source_target_pairs={{8,0},{12,4},{0,8},{4,12},{24,16},{28,20},{16,24},{20,28},{9,1},{1... | collective-permute-start | bytes 3145736 | tf_op jit(solution)/shard_map/ppermute | solution.py:285
  15.8 45.1 %collective-permute-start.4 = (bf16[2,512,512]{2,1,0:T(8,128)(2,1)S(1)}, bf16[2,512,512]{2,1,0:T(8,128)(2,1)S(1)}, u32[]{:S(2)}, u32[]{:S(2)}) collective-permute-start(bf16[2,512,512]{2,1,0:T(8,128)(2,1)S(1)} %collective-permute-done.refs_2_.refs_3_), channel_id=1, source_target_pairs={{16,0},{20,4},{24,8},{28,12},{0,16},{4,20},{8,24},{12,28},{17,1},{... | collective-permute-start | bytes 3145736 | tf_op jit(solution)/shard_map/ppermute | solution.py:285
  18.5 2.0 collective-permute-start.5
  37.2 25.8 %copy-start.11 = (bf16[2,512,512]{2,1,0:T(8,128)(2,1)}, bf16[2,512,512]{2,1,0:T(8,128)(2,1)S(1)}, u32[]{:S(2)}) copy-start(bf16[2,512,512]{2,1,0:T(8,128)(2,1)S(1)} %collective-permute-done.1.refs_3_.refs_4_) | copy-start | bytes 3145732
  39.2 47.8 %copy-start.12 = (bf16[2,512,512]{2,1,0:T(8,128)(2,1)}, bf16[2,512,512]{2,1,0:T(8,128)(2,1)S(1)}, u32[]{:S(2)}) copy-start(bf16[2,512,512]{2,1,0:T(8,128)(2,1)S(1)} %collective-permute-done.3.refs_5_.refs_6_) | copy-start | bytes 3145732
  59.4 27.6 %copy-start.13 = (bf16[2,512,512]{2,1,0:T(8,128)(2,1)}, bf16[2,512,512]{2,1,0:T(8,128)(2,1)S(1)}, u32[]{:S(2)}) copy-start(bf16[2,512,512]{2,1,0:T(8,128)(2,1)S(1)} %collective-permute-done.2.refs_4_.refs_5_) | copy-start | bytes 3145732
  60.9 26.1 %copy-start.14 = (bf16[2,512,512]{2,1,0:T(8,128)(2,1)}, bf16[2,512,512]{2,1,0:T(8,128)(2,1)S(1)}, u32[]{:S(2)}) copy-start(bf16[2,512,512]{2,1,0:T(8,128)(2,1)S(1)} %collective-permute-done.4.refs_6_.refs_7_) | copy-start | bytes 3145732
  60.9 26.1 %collective-permute-start.6 = (bf16[2,512,512]{2,1,0:T(8,128)(2,1)S(1)}, bf16[2,512,512]{2,1,0:T(8,128)(2,1)S(1)}, u32[]{:S(2)}, u32[]{:S(2)}) collective-permute-start(bf16[2,512,512]{2,1,0:T(8,128)(2,1)S(1)} %collective-permute-done.1.refs_3_.refs_4_), channel_id=1, source_target_pairs={{16,0},{20,4},{24,8},{28,12},{0,16},{4,20},{8,24},{12,28},{17,1},{... | collective-permute-start | bytes 3145736 | tf_op jit(solution)/shard_map/ppermute | solution.py:285
  62.4 26.2 %collective-permute-start.7 = (bf16[2,512,512]{2,1,0:T(8,128)(2,1)S(1)}, bf16[2,512,512]{2,1,0:T(8,128)(2,1)}, u32[]{:S(2)}, u32[]{:S(2)}) collective-permute-start(bf16[2,512,512]{2,1,0:T(8,128)(2,1)S(1)} %collective-permute-done.4.refs_6_.refs_7_), channel_id=1, source_target_pairs={{8,0},{12,4},{0,8},{4,12},{24,16},{28,20},{16,24},{20,28},{9,1},{1... | collective-permute-start | bytes 3145736 | tf_op jit(solution)/shard_map/ppermute | solution.py:285
  62.9 48.0 %collective-permute-start.8 = (bf16[2,512,512]{2,1,0:T(8,128)(2,1)S(1)}, bf16[2,512,512]{2,1,0:T(8,128)(2,1)S(1)}, u32[]{:S(2)}, u32[]{:S(2)}) collective-permute-start(bf16[2,512,512]{2,1,0:T(8,128)(2,1)S(1)} %pad_maximum_fusion.refs_1_), channel_id=1, source_target_pairs={{8,0},{12,4},{0,8},{4,12},{24,16},{28,20},{16,24},{20,28},{9,1},{1... | collective-permute-start | bytes 3145736 | tf_op jit(solution)/shard_map/ppermute | solution.py:285
  64.4 46.5 %collective-permute-start.9 = (bf16[2,512,512]{2,1,0:T(8,128)(2,1)S(1)}, bf16[2,512,512]{2,1,0:T(8,128)(2,1)S(1)}, u32[]{:S(2)}, u32[]{:S(2)}) collective-permute-start(bf16[2,512,512]{2,1,0:T(8,128)(2,1)S(1)} %pad_maximum_fusion.refs_1_), channel_id=1, source_target_pairs={{16,0},{20,4},{24,8},{28,12},{0,16},{4,20},{8,24},{12,28},{17,1},{... | collective-permute-start | bytes 3145736 | tf_op jit(solution)/shard_map/ppermute | solution.py:285
  87.0 1.0 copy-start.15
  94.6 11.8 %collective-permute-start.10 = (bf16[16,4096]{1,0:T(8,128)(2,1)S(1)}, bf16[16,4096]{1,0:T(8,128)(2,1)S(1)}, u32[]{:S(2)}, u32[]{:S(2)}) collective-permute-start(bf16[16,4096]{1,0:T(8,128)(2,1)S(1)} %slice.58), channel_id=1, source_target_pairs={{4,8},{12,16},{20,24},{5,9},{13,17},{21,25},{6,10},{14,18},{22,26}... | collective-permute-start | bytes 393224 | tf_op jit(solution)/shard_map/ppermute | solution.py:361
  95.2 11.1 %collective-permute-start.11 = (bf16[16,4096]{1,0:T(8,128)(2,1)S(1)}, bf16[16,4096]{1,0:T(8,128)(2,1)S(1)}, u32[]{:S(2)}, u32[]{:S(2)}) collective-permute-start(bf16[16,4096]{1,0:T(8,128)(2,1)S(1)} %slice.58), channel_id=1, source_target_pairs={{4,12},{12,20},{20,28},{5,13},{13,21},{21,29},{6,14},{14,22},{22,3... | collective-permute-start | bytes 393224 | tf_op jit(solution)/shard_map/ppermute | solution.py:361
  106.3 11.6 %copy-start.5 = (s32[8]{0:T(128)S(1)}, s32[8]{0:T(128)}, u32[]{:S(2)}) copy-start(s32[8]{0:T(128)} %stack.55.at_ref._) | copy-start | bytes 100
  111.0 11.6 %collective-permute-start.12 = (bf16[512,4096]{1,0:T(8,128)(2,1)}, bf16[512,4096]{1,0:T(8,128)(2,1)}, u32[]{:S(2)}, u32[]{:S(2)}) collective-permute-start(bf16[512,4096]{1,0:T(8,128)(2,1)} %all-gather.2.cloned.1.call-done.refs_0_), channel_id=1, source_target_pairs={{0,4},{4,0},{8,12},{12,8},{16,20},{20,16},{24,28},{28,24},{1,5},{5... | collective-permute-start | bytes 12582920 | tf_op jit(solution)/shard_map/ppermute | solution.py:288
  113.2 29.7 %collective-permute-start.13 = (bf16[512,512]{1,0:T(8,128)(2,1)}, bf16[512,512]{1,0:T(8,128)(2,1)}, u32[]{:S(2)}, u32[]{:S(2)}) collective-permute-start(bf16[512,512]{1,0:T(8,128)(2,1)} %slice_bitcast_fusion.1), channel_id=1, source_target_pairs={{16,0},{20,4},{24,8},{28,12},{0,16},{4,20},{8,24},{12,28},{17,1},{... | collective-permute-start | bytes 1572872 | tf_op jit(solution)/shard_map/ppermute | solution.py:285
  115.6 27.5 %collective-permute-start.14 = (bf16[512,512]{1,0:T(8,128)(2,1)}, bf16[512,512]{1,0:T(8,128)(2,1)}, u32[]{:S(2)}, u32[]{:S(2)}) collective-permute-start(bf16[512,512]{1,0:T(8,128)(2,1)} %slice_bitcast_fusion), channel_id=1, source_target_pairs={{8,0},{12,4},{0,8},{4,12},{24,16},{28,20},{16,24},{20,28},{9,1},{1... | collective-permute-start | bytes 1572872 | tf_op jit(solution)/shard_map/ppermute | solution.py:285
  115.6 34.1 %collective-permute-start.17 = (bf16[512,512]{1,0:T(8,128)(2,1)}, bf16[512,512]{1,0:T(8,128)(2,1)}, u32[]{:S(2)}, u32[]{:S(2)}) collective-permute-start(bf16[512,512]{1,0:T(8,128)(2,1)} %get-tuple-element.83), channel_id=1, source_target_pairs={{8,0},{12,4},{0,8},{4,12},{24,16},{28,20},{16,24},{20,28},{9,1},{1... | collective-permute-start | bytes 1572872 | tf_op jit(solution)/shard_map/ppermute | solution.py:285
  121.9 11.7 %copy-start.1 = (f32[512,512]{1,0:T(8,128)S(1)}, f32[512,512]{1,0:T(8,128)}, u32[]{:S(2)}) copy-start(f32[512,512]{1,0:T(8,128)} %shard_map.64.product_ref) | copy-start | bytes 3145732
  122.0 12.6 %copy-start.6 = (s32[8]{0:T(128)S(1)}, s32[8]{0:T(128)}, u32[]{:S(2)}) copy-start(s32[8]{0:T(128)} %stack.55.at_ref._) | copy-start | bytes 100
  122.0 29.9 %collective-permute-start.19 = (bf16[512,512]{1,0:T(8,128)(2,1)}, bf16[512,512]{1,0:T(8,128)(2,1)}, u32[]{:S(2)}, u32[]{:S(2)}) collective-permute-start(bf16[512,512]{1,0:T(8,128)(2,1)} %get-tuple-element.83), channel_id=1, source_target_pairs={{16,0},{20,4},{24,8},{28,12},{0,16},{4,20},{8,24},{12,28},{17,1},{... | collective-permute-start | bytes 1572872 | tf_op jit(solution)/shard_map/ppermute | solution.py:285
  122.5 29.4 %collective-permute-start.18 = (bf16[512,512]{1,0:T(8,128)(2,1)}, bf16[512,512]{1,0:T(8,128)(2,1)}, u32[]{:S(2)}, u32[]{:S(2)}) collective-permute-start(bf16[512,512]{1,0:T(8,128)(2,1)} %get-tuple-element.84), channel_id=1, source_target_pairs={{8,0},{12,4},{0,8},{4,12},{24,16},{28,20},{16,24},{20,28},{9,1},{1... | collective-permute-start | bytes 1572872 | tf_op jit(solution)/shard_map/ppermute | solution.py:285
  133.7 2.9 %copy-start.4 = (f32[512,512]{1,0:T(8,128)S(1)}, f32[512,512]{1,0:T(8,128)}, u32[]{:S(2)}) copy-start(f32[512,512]{1,0:T(8,128)} %get-tuple-element.76.product_ref) | copy-start | bytes 3145732
  142.9 12.8 %collective-permute-start.20 = (bf16[512,512]{1,0:T(8,128)(2,1)}, bf16[512,512]{1,0:T(8,128)(2,1)}, u32[]{:S(2)}, u32[]{:S(2)}) collective-permute-start(bf16[512,512]{1,0:T(8,128)(2,1)} %get-tuple-element.84), channel_id=1, source_target_pairs={{16,0},{20,4},{24,8},{28,12},{0,16},{4,20},{8,24},{12,28},{17,1},{... | collective-permute-start | bytes 1572872 | tf_op jit(solution)/shard_map/ppermute | solution.py:285
  146.3 9.4 %copy-start.3 = (bf16[1024,512]{1,0:T(8,128)(2,1)S(1)}, bf16[1024,512]{1,0:T(8,128)(2,1)}, u32[]{:S(2)}) copy-start(bf16[1024,512]{1,0:T(8,128)(2,1)} %refs_4_.1) | copy-start | bytes 3145732
  146.3 9.4 %collective-permute-start.15 = (bf16[512,512]{1,0:T(8,128)(2,1)S(1)}, bf16[512,512]{1,0:T(8,128)(2,1)S(1)}, u32[]{:S(2)}, u32[]{:S(2)}) collective-permute-start(bf16[512,512]{1,0:T(8,128)(2,1)S(1)} %shard_map.71.refs_2_), channel_id=1, source_target_pairs={{0,4},{4,0},{8,12},{12,8},{16,20},{20,16},{24,28},{28,24},{1,5},{5... | collective-permute-start | bytes 1572872 | tf_op jit(solution)/shard_map/ppermute | solution.py:288
  149.7 6.0 %collective-permute-start.16 = (bf16[512,512]{1,0:T(8,128)(2,1)S(1)}, bf16[512,512]{1,0:T(8,128)(2,1)S(1)}, u32[]{:S(2)}, u32[]{:S(2)}) collective-permute-start(bf16[512,512]{1,0:T(8,128)(2,1)S(1)} %shard_map.69.refs_0_), channel_id=1, source_target_pairs={{0,4},{4,0},{8,12},{12,8},{16,20},{20,16},{24,28},{28,24},{1,5},{5... | collective-permute-start | bytes 1572872 | tf_op jit(solution)/shard_map/ppermute | solution.py:288
  161.4 11.8 %collective-permute-start.21 = (bf16[512,512]{1,0:T(8,128)(2,1)}, bf16[512,512]{1,0:T(8,128)(2,1)S(1)}, u32[]{:S(2)}, u32[]{:S(2)}) collective-permute-start(bf16[512,512]{1,0:T(8,128)(2,1)} %collective-permute-done.17.refs_5_), channel_id=1, source_target_pairs={{16,0},{20,4},{24,8},{28,12},{0,16},{4,20},{8,24},{12,28},{17,1},{... | collective-permute-start | bytes 1572872 | tf_op jit(solution)/shard_map/ppermute | solution.py:285
  161.8 11.7 %collective-permute-start.22 = (bf16[512,512]{1,0:T(8,128)(2,1)}, bf16[512,512]{1,0:T(8,128)(2,1)S(1)}, u32[]{:S(2)}, u32[]{:S(2)}) collective-permute-start(bf16[512,512]{1,0:T(8,128)(2,1)} %collective-permute-done.20.refs_8_), channel_id=1, source_target_pairs={{8,0},{12,4},{0,8},{4,12},{24,16},{28,20},{16,24},{20,28},{9,1},{1... | collective-permute-start | bytes 1572872 | tf_op jit(solution)/shard_map/ppermute | solution.py:285
  175.5 14.4 %collective-permute-start.23 = (bf16[256,512]{1,0:T(8,128)(2,1)S(1)}, bf16[256,512]{1,0:T(8,128)(2,1)S(1)}, u32[]{:S(2)}, u32[]{:S(2)}) collective-permute-start(bf16[256,512]{1,0:T(8,128)(2,1)S(1)} %get-tuple-element.93), channel_id=1, source_target_pairs={{0,1},{1,2},{2,3},{4,5},{5,6},{6,7},{8,9},{9,10},{10,11},{12,13},{... | collective-permute-start | bytes 786440 | tf_op jit(solution)/shard_map/ppermute | solution.py:415
  179.0 22.1 %collective-permute-start.26 = (bf16[256,512]{1,0:T(8,128)(2,1)S(1)}, bf16[256,512]{1,0:T(8,128)(2,1)S(1)}, u32[]{:S(2)}, u32[]{:S(2)}) collective-permute-start(bf16[256,512]{1,0:T(8,128)(2,1)S(1)} %get-tuple-element.91), channel_id=1, source_target_pairs={{1,0},{2,1},{3,2},{5,4},{6,5},{7,6},{9,8},{10,9},{11,10},{13,12},{... | collective-permute-start | bytes 786440 | tf_op jit(solution)/shard_map/ppermute | solution.py:416
  201.2 20.8 %collective-permute-start.27 = (bf16[256,512]{1,0:T(8,128)(2,1)S(1)}, bf16[256,512]{1,0:T(8,128)(2,1)S(1)}, u32[]{:S(2)}, u32[]{:S(2)}) collective-permute-start(bf16[256,512]{1,0:T(8,128)(2,1)S(1)} %get-tuple-element.114), channel_id=1, source_target_pairs={{1,0},{2,1},{3,2},{5,4},{6,5},{7,6},{9,8},{10,9},{11,10},{13,12},{... | collective-permute-start | bytes 786440 | tf_op jit(solution)/shard_map/ppermute | solution.py:416
  202.5 20.9 %collective-permute-start.24 = (bf16[256,512]{1,0:T(8,128)(2,1)S(1)}, bf16[256,512]{1,0:T(8,128)(2,1)S(1)}, u32[]{:S(2)}, u32[]{:S(2)}) collective-permute-start(bf16[256,512]{1,0:T(8,128)(2,1)S(1)} %get-tuple-element.113), channel_id=1, source_target_pairs={{0,1},{1,2},{2,3},{4,5},{5,6},{6,7},{8,9},{9,10},{10,11},{12,13},{... | collective-permute-start | bytes 786440 | tf_op jit(solution)/shard_map/ppermute | solution.py:415
  222.1 14.1 %collective-permute-start.28 = (bf16[256,512]{1,0:T(8,128)(2,1)S(1)}, bf16[256,512]{1,0:T(8,128)(2,1)S(1)}, u32[]{:S(2)}, u32[]{:S(2)}) collective-permute-start(bf16[256,512]{1,0:T(8,128)(2,1)S(1)} %add_convert_fusion), channel_id=1, source_target_pairs={{1,0},{2,1},{3,2},{5,4},{6,5},{7,6},{9,8},{10,9},{11,10},{13,12},{... | collective-permute-start | bytes 786440 | tf_op jit(solution)/shard_map/ppermute | solution.py:416
  223.5 12.7 %collective-permute-start.25 = (bf16[256,512]{1,0:T(8,128)(2,1)S(1)}, bf16[256,512]{1,0:T(8,128)(2,1)S(1)}, u32[]{:S(2)}, u32[]{:S(2)}) collective-permute-start(bf16[256,512]{1,0:T(8,128)(2,1)S(1)} %add_convert_fusion.1), channel_id=1, source_target_pairs={{0,1},{1,2},{2,3},{4,5},{5,6},{6,7},{8,9},{9,10},{10,11},{12,13},{... | collective-permute-start | bytes 786440 | tf_op jit(solution)/shard_map/ppermute | solution.py:415
  236.3 3.8 %copy-start.8 = (bf16[128,4096]{1,0:T(8,128)(2,1)S(1)}, bf16[128,4096]{1,0:T(8,128)(2,1)}, u32[]{:S(2)}) copy-start(bf16[128,4096]{1,0:T(8,128)(2,1)} %param.6) | copy-start | bytes 3145732
  236.4 1.4 collective-permute-start.29
  239.9 1.8 collective-permute-start.30
  240.2 1.8 copy-start.16
  242.3 1.0 copy-start.17
Sparse Core Ops, SparseCore 0:
  10.2 83.4 all-gather.1
  161.5 77.1 reduce-scatter.1

commit v18 on v15

--- a/solution.py
+++ b/solution.py
@@ -219,13 +219,20 @@
             columns = pl.ds(pl.multiple_of(column, half), half)
             held[place, columns] = gate[slot * rows : (slot + 1) * rows]
     wide = weights[0].shape[1]
+    tile = math.gcd(wide, 256)
     leaving = []
     for index, weight in enumerate(weights):
         copies[index].wait()
         at = slice(index * wide, (index + 1) * wide)
-        ready[:, at] = dot(held[...], weight[...]).astype(BF16)
-        leaving.append(pltpu.make_async_copy(ready.at[:, at], out_ref.at[:, at], out_sems.at[index]))
-        leaving[-1].start()
+        for low in range(at.start, at.stop, tile):
+            columns = slice(low, low + tile)
+            inner = slice(low - at.start, low - at.start + tile)
+            total = dot(held[:, :half], weight[:half, inner])
+            total = total + dot(held[:, half:], weight[half:, inner])
+            ready[:, columns] = total.astype(BF16)
+            sem = out_sems.at[len(leaving)]
+            leaving.append(pltpu.make_async_copy(ready.at[:, columns], out_ref.at[:, columns], sem))
+            leaving[-1].start()
     for copy in leaving:
         copy.wait()
 
@@ -244,7 +251,8 @@
         scratch_shapes=[pltpu.VMEM((2 * length, 2 * half), BF16)]
         + [pltpu.VMEM(weight.shape, BF16) for weight in weights]
         + [pltpu.VMEM(shape, BF16)]
-        + [pltpu.SemaphoreType.DMA((len(weights),))] * 2,
+        + [pltpu.SemaphoreType.DMA((len(weights),))]
+        + [pltpu.SemaphoreType.DMA((shape[1] // math.gcd(weights[0].shape[1], 256),))],
         compiler_params=pltpu.CompilerParams(vmem_limit_bytes=24 << 20),
         cost_estimate=pl.CostEstimate(flops=1, bytes_accessed=1, transcendentals=0),
     )(place, *gates, *weights)

time: 248 us -> 248 us (level)
  no operation moved by 1% of the time
where the time goes in v18:
time: 248 us
  waiting for transfers between devices  131 us (53%)
  Pallas kernels  46.5 us (19%)
  starting transfers between devices  37.2 us (15%)
  between operations  14 us (6%)
  local copies, waits for them, and re-layouts  11.2 us (5%)
  other arithmetic  7.54 us (3%)
    ppermute x14, waiting for transfers between devices, from_chip(): return lax.ppermute(block, 'seq', route)  82.3 us
    ppermute x3, waiting for transfers between devices, chained(): falling = lax.ppermute(send_down, 'tp', down)  30.3 us
    pallas_call x7, Pallas kernels, call(): pl.pallas_call(kernel, out_shape=out, in_specs=[pl.BlockSpec(memory_space...  20.6 us
    pallas_call x2, Pallas kernels, products(): pl.pallas_call(functools.partial(product_kernel, len(xs), len(pieces)), o...  19.2 us
    ppermute x14, starting transfers between devices, from_chip(): return lax.ppermute(block, 'seq', route)  16.7 us
    ppermute x3, starting transfers between devices, chained(): rising = lax.ppermute(send_up, 'tp', up)  12.6 us
    ppermute x3, waiting for transfers between devices, chained(): rising = lax.ppermute(send_up, 'tp', up)  10.2 us
    pallas_call x1, Pallas kernels, near_terms(): pl.pallas_call(functools.partial(near_kernel, n_tp), out_shape=jax.ShapeD...  6.76 us
  transfers between devices with their start and end apart: 31, of which 17 were waited for; matrix products, arithmetic and copies ran while one was open for 4% of the time, Pallas kernels for 16%

profile of v18, /device:TPU:0, one launch (start us, length us, event | category | flops | bytes accessed | tf_op | source)
XLA Modules:
  0.0 247.6 jit_solution(17599573421452657203)
XLA Ops:
  6.5 1.8 constant_dynamic-slice_fusion.2
  8.7 1.3 fusion.2
  10.1 0.5 collective-permute-start
  10.6 2.6 %collective-permute-start.1 = (bf16[2,512,512]{2,1,0:T(8,128)(2,1)S(1)}, bf16[2,512,512]{2,1,0:T(8,128)(2,1)S(1)}, u32[]{:S(2)}, u32[]{:S(2)}) collective-permute-start(bf16[2,512,512]{2,1,0:T(8,128)(2,1)S(1)} %get-tuple-element.58.refs_1_.refs_2_), channel_id=1, source_target_pairs={{8,0},{12,4},{0,8},{4,12},{24,16},{28,20},{16,24},{20,28},{9,1},{1... | collective-permute-start | bytes 3145736 | tf_op jit(solution)/shard_map/ppermute | solution.py:284
  13.2 1.5 collective-permute-start.3
  14.7 1.1 collective-permute-start.2
  15.8 1.5 collective-permute-start.4
  17.3 1.3 constant_dynamic-slice_fusion.1
  18.6 1.9 collective-permute-done.5
  20.6 16.5 %collective-permute-done.1.refs_3_.refs_4_ = bf16[2,512,512]{2,1,0:T(8,128)(2,1)S(1)} collective-permute-done((bf16[2,512,512]{2,1,0:T(8,128)(2,1)S(1)}, bf16[2,512,512]{2,1,0:T(8,128)(2,1)S(1)}, u32[]{:S(2)}, u32[]{:S(2)}) %collective-permute-start.1) | collective-permute-done | bytes 1048608 | tf_op jit(solution)/shard_map/ppermute | solution.py:284
  37.2 2.0 collective-permute-done.3.refs_5_.refs_6_
  39.2 20.2 %collective-permute-done.2.refs_4_.refs_5_ = bf16[2,512,512]{2,1,0:T(8,128)(2,1)S(1)} collective-permute-done((bf16[2,512,512]{2,1,0:T(8,128)(2,1)S(1)}, bf16[2,512,512]{2,1,0:T(8,128)(2,1)S(1)}, u32[]{:S(2)}, u32[]{:S(2)}) %collective-permute-start.2) | collective-permute-done | bytes 1048608 | tf_op jit(solution)/shard_map/ppermute | solution.py:284
  59.4 1.5 collective-permute-done.4.refs_6_.refs_7_
  60.9 1.5 collective-permute-start.6
  62.4 0.5 collective-permute-start.7
  62.9 1.5 collective-permute-start.8
  64.9 22.0 %collective-permute-done.6.refs_7_.refs_8_ = bf16[2,512,512]{2,1,0:T(8,128)(2,1)S(1)} collective-permute-done((bf16[2,512,512]{2,1,0:T(8,128)(2,1)S(1)}, bf16[2,512,512]{2,1,0:T(8,128)(2,1)S(1)}, u32[]{:S(2)}, u32[]{:S(2)}) %collective-permute-start.6) | collective-permute-done | bytes 1048608 | tf_op jit(solution)/shard_map/ppermute | solution.py:284
  87.0 1.0 copy-done.13
  88.0 0.6 collective-permute-done.7.refs_8_.refs_9_
  88.6 5.1 %all-gather.2.cloned.1.call-done.refs_0_ = bf16[512,4096]{1,0:T(8,128)(2,1)} async-done(((bf16[128,4096]{1,0:T(8,128)(2,1)}), bf16[512,4096]{1,0:T(8,128)(2,1)}) %all-gather.2.cloned.1.call-update) | async-done | bytes 4194320 | tf_op jit(solution)/shard_map/all_gather | solution.py:335
  93.7 0.9 slice.56
  94.6 0.7 collective-permute-start.10
  95.2 0.7 collective-permute-start.11
  96.0 0.7 stack.55.at_ref._
  96.7 9.4 %shard_map.64.product_ref = f32[512,512]{1,0:T(8,128)} custom-call(s32[8]{0:T(128)} %stack.55.at_ref._, bf16[512,4096]{1,0:T(8,128)(2,1)} %all-gather.2.cloned.1.call-done.refs_0_, bf16[2,512,512]{2,1,0:T(8,128)(2,1)} %copy-done.7, bf16[2,512,512]{2,1,0:T(8,128)(2,1)} %copy-done.8, bf16[2,512,512]{2,1,0:T(8,128)(2,1)} %copy-done.9, ...), custom_call_target="tpu_custom_call" | custom-call | flops 1 | bytes 1 | tf_op jit(solution)/shard_map/pallas_call | solution.py:124
  106.2 0.7 broadcast_select_fusion.refs_0_
  106.9 4.1 %collective-permute-done.8.refs_2_ = bf16[2,512,512]{2,1,0:T(8,128)(2,1)S(1)} collective-permute-done((bf16[2,512,512]{2,1,0:T(8,128)(2,1)S(1)}, bf16[2,512,512]{2,1,0:T(8,128)(2,1)S(1)}, u32[]{:S(2)}, u32[]{:S(2)}) %collective-permute-start.8) | collective-permute-done | bytes 1048608 | tf_op jit(solution)/shard_map/ppermute | solution.py:284
  111.0 1.2 collective-permute-start.12
  112.2 0.8 slice_bitcast_fusion.1
  113.0 1.7 collective-permute-start.13
  114.7 0.8 slice_bitcast_fusion
  115.5 2.0 collective-permute-start.17
  118.2 4.0 %shard_map.65.refs_2_ = f32[512,512]{1,0:T(8,128)S(1)} custom-call(s32[8]{0:T(128)S(1)} %copy-done.3, bf16[512,4096]{1,0:T(8,128)(2,1)} %all-gather.2.cloned.1.call-done.refs_0_, bf16[2,512,512]{2,1,0:T(8,128)(2,1)S(1)} %pad_maximum_fusion.refs_1_, bf16[2,512,512]{2,1,0:T(8,128)(2,1)S(1)} %collective-permute-done.8.refs_2_, ...), custom_call_target="tpu_custom_call" | custom-call | flops 1 | bytes 1 | tf_op jit(solution)/shard_map/pallas_call | solution.py:68
  122.2 9.8 %shard_map.66 = (f32[16,512]{1,0:T(8,128)}, f32[512,512]{1,0:T(8,128)}) custom-call(s32[8]{0:T(128)} %stack.55.at_ref._, bf16[16,4096]{1,0:T(8,128)(2,1)} %broadcast_select_fusion.refs_0_, bf16[512,4096]{1,0:T(8,128)(2,1)} %collective-permute-done.12.refs_1_.refs_0_, bf16[2,512,512]{2,1,0:T(8,128)(2,1)} %copy-done.7, bf16[2,512,512]{2,1,0:T(8,128)(2,1)} %copy-done.8, ...), custom_call_target="tpu_custom_call" | custom-call | flops 1 | bytes 1 | tf_op jit(solution)/shard_map/pallas_call | solution.py:124
  132.0 0.9 broadcast_select_fusion.1
  132.9 2.0 shard_map.67.refs_1_
  135.0 2.0 shard_map.68.refs_1_
  137.0 4.2 %shard_map.70.refs_2_ = f32[512,512]{1,0:T(8,128)S(1)} custom-call(s32[8]{0:T(128)S(1)} %copy-done.4, bf16[512,4096]{1,0:T(8,128)(2,1)} %collective-permute-done.12.refs_1_.refs_0_, bf16[2,512,512]{2,1,0:T(8,128)(2,1)S(1)} %pad_maximum_fusion.refs_1_, bf16[2,512,512]{2,1,0:T(8,128)(2,1)S(1)} %collective-permute-done.8.refs_2_, ...), custom_call_target="tpu_custom_call" | custom-call | flops 1 | bytes 1 | tf_op jit(solution)/shard_map/pallas_call | solution.py:68
  141.2 3.2 %shard_map.71.refs_2_ = bf16[512,512]{1,0:T(8,128)(2,1)S(1)} custom-call(s32[2]{0:T(128)S(1)} %pad_add_fusion.at_ref, bf16[512,4096]{1,0:T(8,128)(2,1)} %collective-permute-done.12.refs_1_.refs_0_, f32[512,512]{1,0:T(8,128)S(1)} %shard_map.68.refs_1_, f32[512,512]{1,0:T(8,128)S(1)} %shard_map.70.refs_2_, bf16[512,512]{1,0:T(8,128)(2,1)} %collective-permute-done.13.refs_3_, ...), custom_call_target="tpu_custom_call" | custom-call | flops 1 | bytes 1 | tf_op jit(solution)/shard_map/pallas_call | solution.py:68
  144.5 3.2 %shard_map.69.refs_0_ = bf16[512,512]{1,0:T(8,128)(2,1)S(1)} custom-call(s32[2]{0:T(128)S(1)} %pad_add_fusion.at_ref, bf16[512,4096]{1,0:T(8,128)(2,1)} %all-gather.2.cloned.1.call-done.refs_0_, f32[512,512]{1,0:T(8,128)S(1)} %shard_map.67.refs_1_, f32[512,512]{1,0:T(8,128)S(1)} %shard_map.65.refs_2_, bf16[512,512]{1,0:T(8,128)(2,1)} %collective-permute-done.13.refs_3_, ...), custom_call_target="tpu_custom_call" | custom-call | flops 1 | bytes 1 | tf_op jit(solution)/shard_map/pallas_call | solution.py:68
  147.7 0.6 collective-permute-start.16
  148.3 3.5 %collective-permute-done.17.refs_5_ = bf16[1024,512]{1,0:T(8,128)(2,1)} collective-permute-done((bf16[1024,512]{1,0:T(8,128)(2,1)}, bf16[1024,512]{1,0:T(8,128)(2,1)}, u32[]{:S(2)}, u32[]{:S(2)}) %collective-permute-start.17) | collective-permute-done | bytes 1048608 | tf_op jit(solution)/shard_map/ppermute | solution.py:284
  151.9 6.8 %shard_map.72 = bf16[1024,1536]{1,0:T(8,128)(2,1)} custom-call(s32[2]{0:T(128)S(1)} %pad_add_fusion.1.at_ref, bf16[512,512]{1,0:T(8,128)(2,1)S(1)} %shard_map.69.refs_0_, bf16[512,512]{1,0:T(8,128)(2,1)S(1)} %collective-permute-done.15.refs_1_, bf16[512,512]{1,0:T(8,128)(2,1)S(1)} %shard_map.71.refs_2_, ...), custom_call_target="tpu_custom_call" | custom-call | flops 1 | bytes 1 | tf_op jit(solution)/shard_map/pallas_call | solution.py:244
  158.7 1.1 slice.73
  160.1 1.1 slice.74
  161.2 1.5 collective-permute-start.20
  162.7 9.7 %collective-permute-done.19.refs_4_ = bf16[512,512]{1,0:T(8,128)(2,1)S(1)} collective-permute-done((bf16[512,512]{1,0:T(8,128)(2,1)S(1)}, bf16[512,512]{1,0:T(8,128)(2,1)S(1)}, u32[]{:S(2)}, u32[]{:S(2)}) %collective-permute-start.19) | collective-permute-done | bytes 524320 | tf_op jit(solution)/shard_map/ppermute | solution.py:284
  172.5 2.0 collective-permute-done.20.refs_5_
  174.5 1.9 shard_map.73
  176.4 3.5 %collective-permute-start.21 = (bf16[256,512]{1,0:T(8,128)(2,1)S(1)}, bf16[256,512]{1,0:T(8,128)(2,1)S(1)}, u32[]{:S(2)}, u32[]{:S(2)}) collective-permute-start(bf16[256,512]{1,0:T(8,128)(2,1)S(1)} %get-tuple-element.87), channel_id=1, source_target_pairs={{0,1},{1,2},{2,3},{4,5},{5,6},{6,7},{8,9},{9,10},{10,11},{12,13},{... | collective-permute-start | bytes 786440 | tf_op jit(solution)/shard_map/ppermute | solution.py:419
  179.9 1.3 collective-permute-start.24
  181.2 10.2 %collective-permute-done.21 = bf16[256,512]{1,0:T(8,128)(2,1)S(1)} collective-permute-done((bf16[256,512]{1,0:T(8,128)(2,1)S(1)}, bf16[256,512]{1,0:T(8,128)(2,1)S(1)}, u32[]{:S(2)}, u32[]{:S(2)}) %collective-permute-start.21) | collective-permute-done | bytes 262176 | tf_op jit(solution)/shard_map/ppermute | solution.py:419
  191.4 10.8 %collective-permute-done.24 = bf16[256,512]{1,0:T(8,128)(2,1)S(1)} collective-permute-done((bf16[256,512]{1,0:T(8,128)(2,1)S(1)}, bf16[256,512]{1,0:T(8,128)(2,1)S(1)}, u32[]{:S(2)}, u32[]{:S(2)}) %collective-permute-start.24) | collective-permute-done | bytes 262176 | tf_op jit(solution)/shard_map/ppermute | solution.py:420
  202.3 1.3 collective-permute-start.25
  203.6 4.6 %collective-permute-start.22 = (bf16[256,512]{1,0:T(8,128)(2,1)S(1)}, bf16[256,512]{1,0:T(8,128)(2,1)S(1)}, u32[]{:S(2)}, u32[]{:S(2)}) collective-permute-start(bf16[256,512]{1,0:T(8,128)(2,1)S(1)} %get-tuple-element.105), channel_id=1, source_target_pairs={{0,1},{1,2},{2,3},{4,5},{5,6},{6,7},{8,9},{9,10},{10,11},{12,13},{... | collective-permute-start | bytes 786440 | tf_op jit(solution)/shard_map/ppermute | solution.py:419
  208.2 15.2 %collective-permute-done.25 = bf16[256,512]{1,0:T(8,128)(2,1)S(1)} collective-permute-done((bf16[256,512]{1,0:T(8,128)(2,1)S(1)}, bf16[256,512]{1,0:T(8,128)(2,1)S(1)}, u32[]{:S(2)}, u32[]{:S(2)}) %collective-permute-start.25) | collective-permute-done | bytes 262176 | tf_op jit(solution)/shard_map/ppermute | solution.py:420
  223.4 1.3 collective-permute-start.26
  224.8 4.6 %collective-permute-start.23 = (bf16[256,512]{1,0:T(8,128)(2,1)S(1)}, bf16[256,512]{1,0:T(8,128)(2,1)S(1)}, u32[]{:S(2)}, u32[]{:S(2)}) collective-permute-start(bf16[256,512]{1,0:T(8,128)(2,1)S(1)} %add_convert_fusion.1), channel_id=1, source_target_pairs={{0,1},{1,2},{2,3},{4,5},{5,6},{6,7},{8,9},{9,10},{10,11},{12,13},{... | collective-permute-start | bytes 786440 | tf_op jit(solution)/shard_map/ppermute | solution.py:419
  229.4 4.3 %collective-permute-done.26 = bf16[256,512]{1,0:T(8,128)(2,1)S(1)} collective-permute-done((bf16[256,512]{1,0:T(8,128)(2,1)S(1)}, bf16[256,512]{1,0:T(8,128)(2,1)S(1)}, u32[]{:S(2)}, u32[]{:S(2)}) %collective-permute-start.26) | collective-permute-done | bytes 262176 | tf_op jit(solution)/shard_map/ppermute | solution.py:420
  233.9 1.3 collective-permute-done.27
  235.2 1.2 fusion.26
  236.8 1.4 fusion.24
  238.9 1.0 copy-done.15
  239.9 0.9 fusion.21
  (78 shorter events, 3.9 us)
Async XLA Ops:
  6.5 111.3 %copy-start = (f32[7,64]{1,0:T(8,128)S(1)}, f32[7,64]{1,0:T(8,128)}, u32[]{:S(2)}) copy-start(f32[7,64]{1,0:T(8,128)} %param.9) | copy-start | bytes 5380
  6.5 87.1 %all-gather.2.cloned.1.call-start = ((), (), s32[]{:S(2)}) async-start(), calls=%async_computation.1 | async-start | bytes 5242880 | tf_op jit(solution)/shard_map/all_gather | solution.py:335
  6.5 1.9 copy-start.5
  6.5 2.2 copy-start.16
  8.3 4.8 %copy-start.7 = (bf16[2,512,512]{2,1,0:T(8,128)(2,1)}, bf16[2,512,512]{2,1,0:T(8,128)(2,1)S(1)}, u32[]{:S(2)}) copy-start(bf16[2,512,512]{2,1,0:T(8,128)(2,1)S(1)} %get-tuple-element.58.refs_1_.refs_2_) | copy-start | bytes 3145732
  10.0 225.2 %reduce-scatter.2.cloned.1.call-start = ((), (), s32[]{:S(2)}) async-start(), calls=%async_computation.2 | async-start | bytes 3932160 | tf_op jit(solution)/shard_map/reduce_scatter | solution.py:428
  10.1 4.6 %collective-permute-start = (bf16[2,512,512]{2,1,0:T(8,128)(2,1)S(1)}, bf16[2,512,512]{2,1,0:T(8,128)(2,1)S(1)}, u32[]{:S(2)}, u32[]{:S(2)}) collective-permute-start(bf16[2,512,512]{2,1,0:T(8,128)(2,1)S(1)} %get-tuple-element.94), channel_id=1, source_target_pairs={{0,4},{4,0},{8,12},{12,8},{16,20},{20,16},{24,28},{28,24},{1,5},{5... | collective-permute-start | bytes 3145736 | tf_op jit(solution)/shard_map/ppermute | solution.py:287
  10.6 26.6 %collective-permute-start.1 = (bf16[2,512,512]{2,1,0:T(8,128)(2,1)S(1)}, bf16[2,512,512]{2,1,0:T(8,128)(2,1)S(1)}, u32[]{:S(2)}, u32[]{:S(2)}) collective-permute-start(bf16[2,512,512]{2,1,0:T(8,128)(2,1)S(1)} %get-tuple-element.58.refs_1_.refs_2_), channel_id=1, source_target_pairs={{8,0},{12,4},{0,8},{4,12},{24,16},{28,20},{16,24},{20,28},{9,1},{1... | collective-permute-start | bytes 3145736 | tf_op jit(solution)/shard_map/ppermute | solution.py:284
  13.2 26.0 %collective-permute-start.3 = (bf16[2,512,512]{2,1,0:T(8,128)(2,1)S(1)}, bf16[2,512,512]{2,1,0:T(8,128)(2,1)S(1)}, u32[]{:S(2)}, u32[]{:S(2)}) collective-permute-start(bf16[2,512,512]{2,1,0:T(8,128)(2,1)S(1)} %get-tuple-element.58.refs_1_.refs_2_), channel_id=1, source_target_pairs={{16,0},{20,4},{24,8},{28,12},{0,16},{4,20},{8,24},{12,28},{17,1},{... | collective-permute-start | bytes 3145736 | tf_op jit(solution)/shard_map/ppermute | solution.py:284
  14.7 5.9 %copy-start.8 = (bf16[2,512,512]{2,1,0:T(8,128)(2,1)}, bf16[2,512,512]{2,1,0:T(8,128)(2,1)S(1)}, u32[]{:S(2)}) copy-start(bf16[2,512,512]{2,1,0:T(8,128)(2,1)S(1)} %collective-permute-done.refs_2_.refs_3_) | copy-start | bytes 3145732
  14.7 44.7 %collective-permute-start.2 = (bf16[2,512,512]{2,1,0:T(8,128)(2,1)S(1)}, bf16[2,512,512]{2,1,0:T(8,128)(2,1)S(1)}, u32[]{:S(2)}, u32[]{:S(2)}) collective-permute-start(bf16[2,512,512]{2,1,0:T(8,128)(2,1)S(1)} %collective-permute-done.refs_2_.refs_3_), channel_id=1, source_target_pairs={{8,0},{12,4},{0,8},{4,12},{24,16},{28,20},{16,24},{20,28},{9,1},{1... | collective-permute-start | bytes 3145736 | tf_op jit(solution)/shard_map/ppermute | solution.py:284
  15.8 45.1 %collective-permute-start.4 = (bf16[2,512,512]{2,1,0:T(8,128)(2,1)S(1)}, bf16[2,512,512]{2,1,0:T(8,128)(2,1)S(1)}, u32[]{:S(2)}, u32[]{:S(2)}) collective-permute-start(bf16[2,512,512]{2,1,0:T(8,128)(2,1)S(1)} %collective-permute-done.refs_2_.refs_3_), channel_id=1, source_target_pairs={{16,0},{20,4},{24,8},{28,12},{0,16},{4,20},{8,24},{12,28},{17,1},{... | collective-permute-start | bytes 3145736 | tf_op jit(solution)/shard_map/ppermute | solution.py:284
  18.5 2.0 collective-permute-start.5
  37.2 25.8 %copy-start.9 = (bf16[2,512,512]{2,1,0:T(8,128)(2,1)}, bf16[2,512,512]{2,1,0:T(8,128)(2,1)S(1)}, u32[]{:S(2)}) copy-start(bf16[2,512,512]{2,1,0:T(8,128)(2,1)S(1)} %collective-permute-done.1.refs_3_.refs_4_) | copy-start | bytes 3145732
  39.2 47.8 %copy-start.10 = (bf16[2,512,512]{2,1,0:T(8,128)(2,1)}, bf16[2,512,512]{2,1,0:T(8,128)(2,1)S(1)}, u32[]{:S(2)}) copy-start(bf16[2,512,512]{2,1,0:T(8,128)(2,1)S(1)} %collective-permute-done.3.refs_5_.refs_6_) | copy-start | bytes 3145732
  59.4 27.6 %copy-start.11 = (bf16[2,512,512]{2,1,0:T(8,128)(2,1)}, bf16[2,512,512]{2,1,0:T(8,128)(2,1)S(1)}, u32[]{:S(2)}) copy-start(bf16[2,512,512]{2,1,0:T(8,128)(2,1)S(1)} %collective-permute-done.2.refs_4_.refs_5_) | copy-start | bytes 3145732
  60.9 26.1 %copy-start.12 = (bf16[2,512,512]{2,1,0:T(8,128)(2,1)}, bf16[2,512,512]{2,1,0:T(8,128)(2,1)S(1)}, u32[]{:S(2)}) copy-start(bf16[2,512,512]{2,1,0:T(8,128)(2,1)S(1)} %collective-permute-done.4.refs_6_.refs_7_) | copy-start | bytes 3145732
  60.9 26.1 %collective-permute-start.6 = (bf16[2,512,512]{2,1,0:T(8,128)(2,1)S(1)}, bf16[2,512,512]{2,1,0:T(8,128)(2,1)S(1)}, u32[]{:S(2)}, u32[]{:S(2)}) collective-permute-start(bf16[2,512,512]{2,1,0:T(8,128)(2,1)S(1)} %collective-permute-done.1.refs_3_.refs_4_), channel_id=1, source_target_pairs={{16,0},{20,4},{24,8},{28,12},{0,16},{4,20},{8,24},{12,28},{17,1},{... | collective-permute-start | bytes 3145736 | tf_op jit(solution)/shard_map/ppermute | solution.py:284
  62.4 26.2 %collective-permute-start.7 = (bf16[2,512,512]{2,1,0:T(8,128)(2,1)S(1)}, bf16[2,512,512]{2,1,0:T(8,128)(2,1)}, u32[]{:S(2)}, u32[]{:S(2)}) collective-permute-start(bf16[2,512,512]{2,1,0:T(8,128)(2,1)S(1)} %collective-permute-done.4.refs_6_.refs_7_), channel_id=1, source_target_pairs={{8,0},{12,4},{0,8},{4,12},{24,16},{28,20},{16,24},{20,28},{9,1},{1... | collective-permute-start | bytes 3145736 | tf_op jit(solution)/shard_map/ppermute | solution.py:284
  62.9 48.0 %collective-permute-start.8 = (bf16[2,512,512]{2,1,0:T(8,128)(2,1)S(1)}, bf16[2,512,512]{2,1,0:T(8,128)(2,1)S(1)}, u32[]{:S(2)}, u32[]{:S(2)}) collective-permute-start(bf16[2,512,512]{2,1,0:T(8,128)(2,1)S(1)} %pad_maximum_fusion.refs_1_), channel_id=1, source_target_pairs={{8,0},{12,4},{0,8},{4,12},{24,16},{28,20},{16,24},{20,28},{9,1},{1... | collective-permute-start | bytes 3145736 | tf_op jit(solution)/shard_map/ppermute | solution.py:284
  64.4 46.5 %collective-permute-start.9 = (bf16[2,512,512]{2,1,0:T(8,128)(2,1)S(1)}, bf16[2,512,512]{2,1,0:T(8,128)(2,1)S(1)}, u32[]{:S(2)}, u32[]{:S(2)}) collective-permute-start(bf16[2,512,512]{2,1,0:T(8,128)(2,1)S(1)} %pad_maximum_fusion.refs_1_), channel_id=1, source_target_pairs={{16,0},{20,4},{24,8},{28,12},{0,16},{4,20},{8,24},{12,28},{17,1},{... | collective-permute-start | bytes 3145736 | tf_op jit(solution)/shard_map/ppermute | solution.py:284
  87.0 1.0 copy-start.13
  94.6 11.6 %collective-permute-start.10 = (bf16[16,4096]{1,0:T(8,128)(2,1)S(1)}, bf16[16,4096]{1,0:T(8,128)(2,1)S(1)}, u32[]{:S(2)}, u32[]{:S(2)}) collective-permute-start(bf16[16,4096]{1,0:T(8,128)(2,1)S(1)} %slice.56), channel_id=1, source_target_pairs={{4,8},{12,16},{20,24},{5,9},{13,17},{21,25},{6,10},{14,18},{22,26}... | collective-permute-start | bytes 393224 | tf_op jit(solution)/shard_map/ppermute | solution.py:359
  95.2 10.9 %collective-permute-start.11 = (bf16[16,4096]{1,0:T(8,128)(2,1)S(1)}, bf16[16,4096]{1,0:T(8,128)(2,1)S(1)}, u32[]{:S(2)}, u32[]{:S(2)}) collective-permute-start(bf16[16,4096]{1,0:T(8,128)(2,1)S(1)} %slice.56), channel_id=1, source_target_pairs={{4,12},{12,20},{20,28},{5,13},{13,21},{21,29},{6,14},{14,22},{22,3... | collective-permute-start | bytes 393224 | tf_op jit(solution)/shard_map/ppermute | solution.py:359
  106.1 12.1 %copy-start.3 = (s32[8]{0:T(128)S(1)}, s32[8]{0:T(128)}, u32[]{:S(2)}) copy-start(s32[8]{0:T(128)} %stack.55.at_ref._) | copy-start | bytes 100
  111.0 11.3 %collective-permute-start.12 = (bf16[512,4096]{1,0:T(8,128)(2,1)}, bf16[512,4096]{1,0:T(8,128)(2,1)}, u32[]{:S(2)}, u32[]{:S(2)}) collective-permute-start(bf16[512,4096]{1,0:T(8,128)(2,1)} %all-gather.2.cloned.1.call-done.refs_0_), channel_id=1, source_target_pairs={{0,4},{4,0},{8,12},{12,8},{16,20},{20,16},{24,28},{28,24},{1,5},{5... | collective-permute-start | bytes 12582920 | tf_op jit(solution)/shard_map/ppermute | solution.py:287
  113.0 28.2 %collective-permute-start.13 = (bf16[512,512]{1,0:T(8,128)(2,1)}, bf16[512,512]{1,0:T(8,128)(2,1)}, u32[]{:S(2)}, u32[]{:S(2)}) collective-permute-start(bf16[512,512]{1,0:T(8,128)(2,1)} %slice_bitcast_fusion.1), channel_id=1, source_target_pairs={{16,0},{20,4},{24,8},{28,12},{0,16},{4,20},{8,24},{12,28},{17,1},{... | collective-permute-start | bytes 1572872 | tf_op jit(solution)/shard_map/ppermute | solution.py:284
  115.5 25.7 %collective-permute-start.14 = (bf16[512,512]{1,0:T(8,128)(2,1)}, bf16[512,512]{1,0:T(8,128)(2,1)}, u32[]{:S(2)}, u32[]{:S(2)}) collective-permute-start(bf16[512,512]{1,0:T(8,128)(2,1)} %slice_bitcast_fusion), channel_id=1, source_target_pairs={{8,0},{12,4},{0,8},{4,12},{24,16},{28,20},{16,24},{20,28},{9,1},{1... | collective-permute-start | bytes 1572872 | tf_op jit(solution)/shard_map/ppermute | solution.py:284
  115.5 36.3 %collective-permute-start.17 = (bf16[1024,512]{1,0:T(8,128)(2,1)}, bf16[1024,512]{1,0:T(8,128)(2,1)}, u32[]{:S(2)}, u32[]{:S(2)}) collective-permute-start(bf16[1024,512]{1,0:T(8,128)(2,1)} %refs_4_.1), channel_id=1, source_target_pairs={{8,0},{12,4},{0,8},{4,12},{24,16},{28,20},{16,24},{20,28},{9,1},{1... | collective-permute-start | bytes 3145736 | tf_op jit(solution)/shard_map/ppermute | solution.py:284
  117.5 34.3 %collective-permute-start.18 = (bf16[1024,512]{1,0:T(8,128)(2,1)}, bf16[1024,512]{1,0:T(8,128)(2,1)}, u32[]{:S(2)}, u32[]{:S(2)}) collective-permute-start(bf16[1024,512]{1,0:T(8,128)(2,1)} %refs_4_.1), channel_id=1, source_target_pairs={{16,0},{20,4},{24,8},{28,12},{0,16},{4,20},{8,24},{12,28},{17,1},{... | collective-permute-start | bytes 3145736 | tf_op jit(solution)/shard_map/ppermute | solution.py:284
  122.2 9.8 %copy-start.1 = (f32[512,512]{1,0:T(8,128)S(1)}, f32[512,512]{1,0:T(8,128)}, u32[]{:S(2)}) copy-start(f32[512,512]{1,0:T(8,128)} %shard_map.64.product_ref) | copy-start | bytes 3145732
  122.2 10.7 %copy-start.4 = (s32[8]{0:T(128)S(1)}, s32[8]{0:T(128)}, u32[]{:S(2)}) copy-start(s32[8]{0:T(128)} %stack.55.at_ref._) | copy-start | bytes 100
  132.0 2.9 %copy-start.2 = (f32[512,512]{1,0:T(8,128)S(1)}, f32[512,512]{1,0:T(8,128)}, u32[]{:S(2)}) copy-start(f32[512,512]{1,0:T(8,128)} %get-tuple-element.73.product_ref) | copy-start | bytes 3145732
  144.4 7.4 %collective-permute-start.15 = (bf16[512,512]{1,0:T(8,128)(2,1)S(1)}, bf16[512,512]{1,0:T(8,128)(2,1)S(1)}, u32[]{:S(2)}, u32[]{:S(2)}) collective-permute-start(bf16[512,512]{1,0:T(8,128)(2,1)S(1)} %shard_map.71.refs_2_), channel_id=1, source_target_pairs={{0,4},{4,0},{8,12},{12,8},{16,20},{20,16},{24,28},{28,24},{1,5},{5... | collective-permute-start | bytes 1572872 | tf_op jit(solution)/shard_map/ppermute | solution.py:287
  147.7 4.2 %collective-permute-start.16 = (bf16[512,512]{1,0:T(8,128)(2,1)S(1)}, bf16[512,512]{1,0:T(8,128)(2,1)S(1)}, u32[]{:S(2)}, u32[]{:S(2)}) collective-permute-start(bf16[512,512]{1,0:T(8,128)(2,1)S(1)} %shard_map.69.refs_0_), channel_id=1, source_target_pairs={{0,4},{4,0},{8,12},{12,8},{16,20},{20,16},{24,28},{28,24},{1,5},{5... | collective-permute-start | bytes 1572872 | tf_op jit(solution)/shard_map/ppermute | solution.py:287
  159.7 12.7 %collective-permute-start.19 = (bf16[512,512]{1,0:T(8,128)(2,1)S(1)}, bf16[512,512]{1,0:T(8,128)(2,1)S(1)}, u32[]{:S(2)}, u32[]{:S(2)}) collective-permute-start(bf16[512,512]{1,0:T(8,128)(2,1)S(1)} %slice.73), channel_id=1, source_target_pairs={{16,0},{20,4},{24,8},{28,12},{0,16},{4,20},{8,24},{12,28},{17,1},{... | collective-permute-start | bytes 1572872 | tf_op jit(solution)/shard_map/ppermute | solution.py:284
  161.2 13.3 %collective-permute-start.20 = (bf16[512,512]{1,0:T(8,128)(2,1)S(1)}, bf16[512,512]{1,0:T(8,128)(2,1)S(1)}, u32[]{:S(2)}, u32[]{:S(2)}) collective-permute-start(bf16[512,512]{1,0:T(8,128)(2,1)S(1)} %slice.74), channel_id=1, source_target_pairs={{8,0},{12,4},{0,8},{4,12},{24,16},{28,20},{16,24},{20,28},{9,1},{1... | collective-permute-start | bytes 1572872 | tf_op jit(solution)/shard_map/ppermute | solution.py:284
  176.4 15.0 %collective-permute-start.21 = (bf16[256,512]{1,0:T(8,128)(2,1)S(1)}, bf16[256,512]{1,0:T(8,128)(2,1)S(1)}, u32[]{:S(2)}, u32[]{:S(2)}) collective-permute-start(bf16[256,512]{1,0:T(8,128)(2,1)S(1)} %get-tuple-element.87), channel_id=1, source_target_pairs={{0,1},{1,2},{2,3},{4,5},{5,6},{6,7},{8,9},{9,10},{10,11},{12,13},{... | collective-permute-start | bytes 786440 | tf_op jit(solution)/shard_map/ppermute | solution.py:419
  179.9 22.3 %collective-permute-start.24 = (bf16[256,512]{1,0:T(8,128)(2,1)S(1)}, bf16[256,512]{1,0:T(8,128)(2,1)S(1)}, u32[]{:S(2)}, u32[]{:S(2)}) collective-permute-start(bf16[256,512]{1,0:T(8,128)(2,1)S(1)} %get-tuple-element.85), channel_id=1, source_target_pairs={{1,0},{2,1},{3,2},{5,4},{6,5},{7,6},{9,8},{10,9},{11,10},{13,12},{... | collective-permute-start | bytes 786440 | tf_op jit(solution)/shard_map/ppermute | solution.py:420
  202.3 21.0 %collective-permute-start.25 = (bf16[256,512]{1,0:T(8,128)(2,1)S(1)}, bf16[256,512]{1,0:T(8,128)(2,1)S(1)}, u32[]{:S(2)}, u32[]{:S(2)}) collective-permute-start(bf16[256,512]{1,0:T(8,128)(2,1)S(1)} %get-tuple-element.106), channel_id=1, source_target_pairs={{1,0},{2,1},{3,2},{5,4},{6,5},{7,6},{9,8},{10,9},{11,10},{13,12},{... | collective-permute-start | bytes 786440 | tf_op jit(solution)/shard_map/ppermute | solution.py:420
  203.6 21.1 %collective-permute-start.22 = (bf16[256,512]{1,0:T(8,128)(2,1)S(1)}, bf16[256,512]{1,0:T(8,128)(2,1)S(1)}, u32[]{:S(2)}, u32[]{:S(2)}) collective-permute-start(bf16[256,512]{1,0:T(8,128)(2,1)S(1)} %get-tuple-element.105), channel_id=1, source_target_pairs={{0,1},{1,2},{2,3},{4,5},{5,6},{6,7},{8,9},{9,10},{10,11},{12,13},{... | collective-permute-start | bytes 786440 | tf_op jit(solution)/shard_map/ppermute | solution.py:419
  223.4 10.2 %collective-permute-start.26 = (bf16[256,512]{1,0:T(8,128)(2,1)S(1)}, bf16[256,512]{1,0:T(8,128)(2,1)S(1)}, u32[]{:S(2)}, u32[]{:S(2)}) collective-permute-start(bf16[256,512]{1,0:T(8,128)(2,1)S(1)} %add_convert_fusion), channel_id=1, source_target_pairs={{1,0},{2,1},{3,2},{5,4},{6,5},{7,6},{9,8},{10,9},{11,10},{13,12},{... | collective-permute-start | bytes 786440 | tf_op jit(solution)/shard_map/ppermute | solution.py:420
  224.8 8.8 %collective-permute-start.23 = (bf16[256,512]{1,0:T(8,128)(2,1)S(1)}, bf16[256,512]{1,0:T(8,128)(2,1)S(1)}, u32[]{:S(2)}, u32[]{:S(2)}) collective-permute-start(bf16[256,512]{1,0:T(8,128)(2,1)S(1)} %add_convert_fusion.1), channel_id=1, source_target_pairs={{0,1},{1,2},{2,3},{4,5},{5,6},{6,7},{8,9},{9,10},{10,11},{12,13},{... | collective-permute-start | bytes 786440 | tf_op jit(solution)/shard_map/ppermute | solution.py:419
  233.8 3.0 %copy-start.6 = (bf16[128,4096]{1,0:T(8,128)(2,1)S(1)}, bf16[128,4096]{1,0:T(8,128)(2,1)}, u32[]{:S(2)}) copy-start(bf16[128,4096]{1,0:T(8,128)(2,1)} %param.6) | copy-start | bytes 3145732
  233.8 1.4 collective-permute-start.27
  236.4 1.8 collective-permute-start.28
  236.8 1.8 copy-start.14
  238.9 1.0 copy-start.15
Sparse Core Ops, SparseCore 0:
  10.2 83.4 all-gather.1
  158.8 74.4 reduce-scatter.1

commit v19 on v16

--- a/solution.py
+++ b/solution.py
@@ -417,17 +417,17 @@
         total = slots[0].astype(F32) + rising.astype(F32) + falling.astype(F32)
         return total
 
-    near = {(0, 0): (out_weight,)}
-    near.update({key: (block,) for key, block in (*o_x.items(), *o_y.items())})
+    near = {key: (block,) for key, block in (*o_x.items(), *o_y.items())}
+    far = {(0, 0): (out_weight,), **o_rest}
     found = near_terms(n_tp, here_at, gates, [block for (block,) in near.values()])
     gates, found = lax.optimization_barrier((gates, found))
     near_sum = lax.psum_scatter(found, "tp", scatter_dimension=0, tiled=True)
-    far_sum = chained(terms(n_tp, here_at, gates, list(o_rest.values()), True))
+    far_sum = chained(terms(n_tp, here_at, gates, list(far.values()), True))
     result = jnp.zeros((rows, model), BF16)
     far_theirs = from_partner(far_sum[rows:].astype(BF16))
     near_sum, far_theirs, far_sum = lax.optimization_barrier((near_sum, far_theirs, far_sum))
     near_theirs = from_partner(near_sum[rows:].astype(BF16))
-    parts = (list(o_rest), far_sum, far_theirs), (list(near), near_sum, near_theirs)
+    parts = (list(far), far_sum, far_theirs), (list(near), near_sum, near_theirs)
     for keys, mixed, theirs in parts:
         theirs = theirs.astype(F32)
         mine = mixed[:rows].astype(F32)

time: 248 us -> 254 us (1.024)
  waiting for transfers between devices: 131 us -> 136 us
    ppermute x3, waiting for transfers between devices: 10.2 us -> 23 us  [chained(): rising = lax.ppermute(send_up, 'tp', up)]
    ppermute x3, waiting for transfers between devices: 30.3 us -> 21.5 us  [chained(): falling = lax.ppermute(send_down, 'tp', down)]
  transfers between devices with their start and end apart: 31 -> 31, of which waited for: 17 -> 19; matrix products, arithmetic and copies ran while one was open for 4% -> 4% of each run, Pallas kernels for 16% -> 16%
where the time goes in v19:
time: 254 us; the launch traced here: 253 us
  waiting for transfers between devices  136 us (54%)
  Pallas kernels  46.9 us (18%)
  starting transfers between devices  38.2 us (15%)
  between operations  14 us (6%)
  local copies, waits for them, and re-layouts  11.2 us (4%)
  other arithmetic  6.98 us (3%)
    ppermute x14, waiting for transfers between devices, from_chip(): return lax.ppermute(block, 'seq', route)  82.3 us
    ppermute x3, waiting for transfers between devices, chained(): rising = lax.ppermute(send_up, 'tp', up)  23 us
    pallas_call x7, Pallas kernels, call(): pl.pallas_call(kernel, out_shape=out, in_specs=[pl.BlockSpec(memory_space...  22.3 us
    ppermute x3, waiting for transfers between devices, chained(): falling = lax.ppermute(send_down, 'tp', down)  21.5 us
    pallas_call x2, Pallas kernels, products(): pl.pallas_call(functools.partial(product_kernel, len(xs), len(pieces)), o...  19.2 us
    ppermute x14, starting transfers between devices, from_chip(): return lax.ppermute(block, 'seq', route)  16.7 us
    ppermute x3, starting transfers between devices, chained(): rising = lax.ppermute(send_up, 'tp', up)  13.5 us
    pallas_call x1, Pallas kernels, near_terms(): pl.pallas_call(functools.partial(near_kernel, n_tp), out_shape=jax.ShapeD...  5.37 us
  transfers between devices with their start and end apart: 31, of which 19 were waited for; matrix products, arithmetic and copies ran while one was open for 4% of the time, Pallas kernels for 16%

profile of v19, /device:TPU:0, one launch (start us, length us, event | category | flops | bytes accessed | tf_op | source)
XLA Modules:
  0.0 253.3 jit_solution(14510610488632432592)
XLA Ops:
  6.5 1.8 constant_dynamic-slice_fusion.2
  8.7 1.3 fusion.2
  10.6 2.6 %collective-permute-start.1 = (bf16[2,512,512]{2,1,0:T(8,128)(2,1)S(1)}, bf16[2,512,512]{2,1,0:T(8,128)(2,1)S(1)}, u32[]{:S(2)}, u32[]{:S(2)}) collective-permute-start(bf16[2,512,512]{2,1,0:T(8,128)(2,1)S(1)} %get-tuple-element.58.refs_1_.refs_2_), channel_id=1, source_target_pairs={{8,0},{12,4},{0,8},{4,12},{24,16},{28,20},{16,24},{20,28},{9,1},{1... | collective-permute-start | bytes 3145736 | tf_op jit(solution)/shard_map/ppermute | solution.py:280
  13.2 1.5 collective-permute-start.3
  14.7 1.1 collective-permute-start.2
  15.8 1.5 collective-permute-start.4
  17.3 1.3 constant_dynamic-slice_fusion.1
  18.6 1.9 collective-permute-done.5
  20.6 16.5 %collective-permute-done.1.refs_3_.refs_4_ = bf16[2,512,512]{2,1,0:T(8,128)(2,1)S(1)} collective-permute-done((bf16[2,512,512]{2,1,0:T(8,128)(2,1)S(1)}, bf16[2,512,512]{2,1,0:T(8,128)(2,1)S(1)}, u32[]{:S(2)}, u32[]{:S(2)}) %collective-permute-start.1) | collective-permute-done | bytes 1048608 | tf_op jit(solution)/shard_map/ppermute | solution.py:280
  37.2 2.0 collective-permute-done.3.refs_5_.refs_6_
  39.2 20.2 %collective-permute-done.2.refs_4_.refs_5_ = bf16[2,512,512]{2,1,0:T(8,128)(2,1)S(1)} collective-permute-done((bf16[2,512,512]{2,1,0:T(8,128)(2,1)S(1)}, bf16[2,512,512]{2,1,0:T(8,128)(2,1)S(1)}, u32[]{:S(2)}, u32[]{:S(2)}) %collective-permute-start.2) | collective-permute-done | bytes 1048608 | tf_op jit(solution)/shard_map/ppermute | solution.py:280
  59.4 1.5 collective-permute-done.4.refs_6_.refs_7_
  60.9 1.5 collective-permute-start.6
  62.4 0.5 collective-permute-start.7
  62.9 1.5 collective-permute-start.8
  64.9 22.0 %collective-permute-done.6.refs_7_.refs_8_ = bf16[2,512,512]{2,1,0:T(8,128)(2,1)S(1)} collective-permute-done((bf16[2,512,512]{2,1,0:T(8,128)(2,1)S(1)}, bf16[2,512,512]{2,1,0:T(8,128)(2,1)S(1)}, u32[]{:S(2)}, u32[]{:S(2)}) %collective-permute-start.6) | collective-permute-done | bytes 1048608 | tf_op jit(solution)/shard_map/ppermute | solution.py:280
  87.0 1.0 copy-done.13
  88.0 0.6 collective-permute-done.7.refs_8_.refs_9_
  88.6 5.1 %all-gather.2.cloned.1.call-done.refs_0_ = bf16[512,4096]{1,0:T(8,128)(2,1)} async-done(((bf16[128,4096]{1,0:T(8,128)(2,1)}), bf16[512,4096]{1,0:T(8,128)(2,1)}) %all-gather.2.cloned.1.call-update) | async-done | bytes 4194320 | tf_op jit(solution)/shard_map/all_gather | solution.py:331
  93.7 0.9 slice.62
  94.6 0.7 collective-permute-start.10
  95.2 0.7 collective-permute-start.11
  96.0 0.7 stack.55.at_ref._
  96.7 9.4 %shard_map.64.product_ref = f32[512,512]{1,0:T(8,128)} custom-call(s32[8]{0:T(128)} %stack.55.at_ref._, bf16[512,4096]{1,0:T(8,128)(2,1)} %all-gather.2.cloned.1.call-done.refs_0_, bf16[2,512,512]{2,1,0:T(8,128)(2,1)} %copy-done.7, bf16[2,512,512]{2,1,0:T(8,128)(2,1)} %copy-done.8, bf16[2,512,512]{2,1,0:T(8,128)(2,1)} %copy-done.9, ...), custom_call_target="tpu_custom_call" | custom-call | flops 1 | bytes 1 | tf_op jit(solution)/shard_map/pallas_call | solution.py:124
  106.2 0.7 broadcast_select_fusion.refs_0_
  106.9 4.1 %collective-permute-done.8.refs_2_ = bf16[2,512,512]{2,1,0:T(8,128)(2,1)S(1)} collective-permute-done((bf16[2,512,512]{2,1,0:T(8,128)(2,1)S(1)}, bf16[2,512,512]{2,1,0:T(8,128)(2,1)S(1)}, u32[]{:S(2)}, u32[]{:S(2)}) %collective-permute-start.8) | collective-permute-done | bytes 1048608 | tf_op jit(solution)/shard_map/ppermute | solution.py:280
  111.0 1.2 collective-permute-start.12
  112.2 0.8 slice_bitcast_fusion.1
  113.0 1.7 collective-permute-start.13
  114.7 0.8 slice_bitcast_fusion
  115.6 2.0 collective-permute-start.17
  118.3 4.0 %shard_map.65.refs_2_ = f32[512,512]{1,0:T(8,128)S(1)} custom-call(s32[8]{0:T(128)S(1)} %copy-done.3, bf16[512,4096]{1,0:T(8,128)(2,1)} %all-gather.2.cloned.1.call-done.refs_0_, bf16[2,512,512]{2,1,0:T(8,128)(2,1)S(1)} %pad_maximum_fusion.refs_1_, bf16[2,512,512]{2,1,0:T(8,128)(2,1)S(1)} %collective-permute-done.8.refs_2_, ...), custom_call_target="tpu_custom_call" | custom-call | flops 1 | bytes 1 | tf_op jit(solution)/shard_map/pallas_call | solution.py:68
  122.3 9.8 %shard_map.66 = (f32[16,512]{1,0:T(8,128)}, f32[512,512]{1,0:T(8,128)}) custom-call(s32[8]{0:T(128)} %stack.55.at_ref._, bf16[16,4096]{1,0:T(8,128)(2,1)} %broadcast_select_fusion.refs_0_, bf16[512,4096]{1,0:T(8,128)(2,1)} %collective-permute-done.12.refs_1_.refs_0_, bf16[2,512,512]{2,1,0:T(8,128)(2,1)} %copy-done.7, bf16[2,512,512]{2,1,0:T(8,128)(2,1)} %copy-done.8, ...), custom_call_target="tpu_custom_call" | custom-call | flops 1 | bytes 1 | tf_op jit(solution)/shard_map/pallas_call | solution.py:124
  132.1 0.9 broadcast_select_fusion.1
  133.0 2.0 shard_map.67.refs_1_
  135.0 2.0 shard_map.68.refs_1_
  137.1 4.2 %shard_map.70.refs_2_ = f32[512,512]{1,0:T(8,128)S(1)} custom-call(s32[8]{0:T(128)S(1)} %copy-done.4, bf16[512,4096]{1,0:T(8,128)(2,1)} %collective-permute-done.12.refs_1_.refs_0_, bf16[2,512,512]{2,1,0:T(8,128)(2,1)S(1)} %pad_maximum_fusion.refs_1_, bf16[2,512,512]{2,1,0:T(8,128)(2,1)S(1)} %collective-permute-done.8.refs_2_, ...), custom_call_target="tpu_custom_call" | custom-call | flops 1 | bytes 1 | tf_op jit(solution)/shard_map/pallas_call | solution.py:68
  141.3 3.2 %shard_map.71.refs_2_ = bf16[512,512]{1,0:T(8,128)(2,1)S(1)} custom-call(s32[2]{0:T(128)S(1)} %pad_add_fusion.at_ref, bf16[512,4096]{1,0:T(8,128)(2,1)} %collective-permute-done.12.refs_1_.refs_0_, f32[512,512]{1,0:T(8,128)S(1)} %shard_map.68.refs_1_, f32[512,512]{1,0:T(8,128)S(1)} %shard_map.70.refs_2_, bf16[512,512]{1,0:T(8,128)(2,1)} %collective-permute-done.13.refs_3_, ...), custom_call_target="tpu_custom_call" | custom-call | flops 1 | bytes 1 | tf_op jit(solution)/shard_map/pallas_call | solution.py:68
  144.6 3.2 %shard_map.69.refs_0_ = bf16[512,512]{1,0:T(8,128)(2,1)S(1)} custom-call(s32[2]{0:T(128)S(1)} %pad_add_fusion.at_ref, bf16[512,4096]{1,0:T(8,128)(2,1)} %all-gather.2.cloned.1.call-done.refs_0_, f32[512,512]{1,0:T(8,128)S(1)} %shard_map.67.refs_1_, f32[512,512]{1,0:T(8,128)S(1)} %shard_map.65.refs_2_, bf16[512,512]{1,0:T(8,128)(2,1)} %collective-permute-done.13.refs_3_, ...), custom_call_target="tpu_custom_call" | custom-call | flops 1 | bytes 1 | tf_op jit(solution)/shard_map/pallas_call | solution.py:68
  147.8 0.6 collective-permute-start.16
  148.4 3.5 %collective-permute-done.17.refs_4_ = bf16[1024,512]{1,0:T(8,128)(2,1)} collective-permute-done((bf16[1024,512]{1,0:T(8,128)(2,1)}, bf16[1024,512]{1,0:T(8,128)(2,1)}, u32[]{:S(2)}, u32[]{:S(2)}) %collective-permute-start.17) | collective-permute-done | bytes 1048608 | tf_op jit(solution)/shard_map/ppermute | solution.py:280
  151.9 5.4 %shard_map.72 = bf16[1024,1024]{1,0:T(8,128)(2,1)} custom-call(s32[2]{0:T(128)S(1)} %pad_add_fusion.1.at_ref, bf16[512,512]{1,0:T(8,128)(2,1)S(1)} %shard_map.69.refs_0_, bf16[512,512]{1,0:T(8,128)(2,1)S(1)} %collective-permute-done.15.refs_1_, bf16[512,512]{1,0:T(8,128)(2,1)S(1)} %shard_map.71.refs_2_, ...), custom_call_target="tpu_custom_call" | custom-call | flops 1 | bytes 1 | tf_op jit(solution)/shard_map/pallas_call | solution.py:241
  157.3 1.1 slice.80
  158.8 1.1 slice.81
  159.9 1.5 collective-permute-start.20
  161.4 9.7 %collective-permute-done.19.refs_5_ = bf16[512,512]{1,0:T(8,128)(2,1)S(1)} collective-permute-done((bf16[512,512]{1,0:T(8,128)(2,1)S(1)}, bf16[512,512]{1,0:T(8,128)(2,1)S(1)}, u32[]{:S(2)}, u32[]{:S(2)}) %collective-permute-start.19) | collective-permute-done | bytes 524320 | tf_op jit(solution)/shard_map/ppermute | solution.py:280
  171.1 2.1 collective-permute-done.20.refs_6_
  173.2 3.7 %shard_map.73 = (bf16[256,1024]{1,0:T(8,128)(2,1)S(1)}, bf16[256,1024]{1,0:T(8,128)(2,1)S(1)}, bf16[256,1024]{1,0:T(8,128)(2,1)S(1)}, bf16[256,1024]{1,0:T(8,128)(2,1)S(1)}) custom-call(s32[2]{0:T(128)S(1)} %pad_add_fusion.1.at_ref, bf16[512,512]{1,0:T(8,128)(2,1)S(1)} %shard_map.69.refs_0_, bf16[512,512]{1,0:T(8,128)(2,1)S(1)} %collective-permute-done.15.refs_1_, ...), custom_call_target="tpu_custom_call" | custom-call | flops 1 | bytes 1 | tf_op jit(solution)/shard_map/pallas_call | solution.py:68
  176.9 3.5 %collective-permute-start.21 = (bf16[256,1024]{1,0:T(8,128)(2,1)S(1)}, bf16[256,1024]{1,0:T(8,128)(2,1)S(1)}, u32[]{:S(2)}, u32[]{:S(2)}) collective-permute-start(bf16[256,1024]{1,0:T(8,128)(2,1)S(1)} %get-tuple-element.87), channel_id=1, source_target_pairs={{0,1},{1,2},{2,3},{4,5},{5,6},{6,7},{8,9},{9,10},{10,11},{12,13},{... | collective-permute-start | bytes 1572872 | tf_op jit(solution)/shard_map/ppermute | solution.py:415
  180.4 1.3 collective-permute-start.24
  181.7 21.6 %collective-permute-done.21 = bf16[256,1024]{1,0:T(8,128)(2,1)S(1)} collective-permute-done((bf16[256,1024]{1,0:T(8,128)(2,1)S(1)}, bf16[256,1024]{1,0:T(8,128)(2,1)S(1)}, u32[]{:S(2)}, u32[]{:S(2)}) %collective-permute-start.21) | collective-permute-done | bytes 524320 | tf_op jit(solution)/shard_map/ppermute | solution.py:415
  203.3 5.1 %collective-permute-done.24 = bf16[256,1024]{1,0:T(8,128)(2,1)S(1)} collective-permute-done((bf16[256,1024]{1,0:T(8,128)(2,1)S(1)}, bf16[256,1024]{1,0:T(8,128)(2,1)S(1)}, u32[]{:S(2)}, u32[]{:S(2)}) %collective-permute-start.24) | collective-permute-done | bytes 524320 | tf_op jit(solution)/shard_map/ppermute | solution.py:416
  208.8 1.3 collective-permute-start.25
  210.1 5.4 %collective-permute-start.22 = (bf16[256,1024]{1,0:T(8,128)(2,1)S(1)}, bf16[256,1024]{1,0:T(8,128)(2,1)S(1)}, u32[]{:S(2)}, u32[]{:S(2)}) collective-permute-start(bf16[256,1024]{1,0:T(8,128)(2,1)S(1)} %get-tuple-element.103), channel_id=1, source_target_pairs={{0,1},{1,2},{2,3},{4,5},{5,6},{6,7},{8,9},{9,10},{10,11},{12,13},{... | collective-permute-start | bytes 1572872 | tf_op jit(solution)/shard_map/ppermute | solution.py:415
  215.5 8.8 %collective-permute-done.25 = bf16[256,1024]{1,0:T(8,128)(2,1)S(1)} collective-permute-done((bf16[256,1024]{1,0:T(8,128)(2,1)S(1)}, bf16[256,1024]{1,0:T(8,128)(2,1)S(1)}, u32[]{:S(2)}, u32[]{:S(2)}) %collective-permute-start.25) | collective-permute-done | bytes 524320 | tf_op jit(solution)/shard_map/ppermute | solution.py:416
  224.5 1.3 collective-permute-start.26
  226.0 4.6 %collective-permute-start.23 = (bf16[256,1024]{1,0:T(8,128)(2,1)S(1)}, bf16[256,1024]{1,0:T(8,128)(2,1)S(1)}, u32[]{:S(2)}, u32[]{:S(2)}) collective-permute-start(bf16[256,1024]{1,0:T(8,128)(2,1)S(1)} %add_convert_fusion.1), channel_id=1, source_target_pairs={{0,1},{1,2},{2,3},{4,5},{5,6},{6,7},{8,9},{9,10},{10,11},{12,13},{... | collective-permute-start | bytes 1572872 | tf_op jit(solution)/shard_map/ppermute | solution.py:415
  230.6 7.6 %collective-permute-done.26 = bf16[256,1024]{1,0:T(8,128)(2,1)S(1)} collective-permute-done((bf16[256,1024]{1,0:T(8,128)(2,1)S(1)}, bf16[256,1024]{1,0:T(8,128)(2,1)S(1)}, u32[]{:S(2)}, u32[]{:S(2)}) %collective-permute-start.26) | collective-permute-done | bytes 524320 | tf_op jit(solution)/shard_map/ppermute | solution.py:416
  238.2 1.4 collective-permute-done.23
  240.0 1.5 collective-permute-done.27
  241.5 1.2 fusion.27
  243.6 0.7 collective-permute-done.28
  244.6 1.0 copy-done.15
  245.6 0.9 fusion.21
  (77 shorter events, 5.1 us)
Async XLA Ops:
  6.5 111.4 %copy-start = (f32[7,64]{1,0:T(8,128)S(1)}, f32[7,64]{1,0:T(8,128)}, u32[]{:S(2)}) copy-start(f32[7,64]{1,0:T(8,128)} %param.9) | copy-start | bytes 5380
  6.5 87.1 %all-gather.2.cloned.1.call-start = ((), (), s32[]{:S(2)}) async-start(), calls=%async_computation.1 | async-start | bytes 5242880 | tf_op jit(solution)/shard_map/all_gather | solution.py:331
  6.5 1.9 copy-start.5
  6.5 2.2 copy-start.16
  8.3 4.8 %copy-start.7 = (bf16[2,512,512]{2,1,0:T(8,128)(2,1)}, bf16[2,512,512]{2,1,0:T(8,128)(2,1)S(1)}, u32[]{:S(2)}) copy-start(bf16[2,512,512]{2,1,0:T(8,128)(2,1)S(1)} %get-tuple-element.58.refs_1_.refs_2_) | copy-start | bytes 3145732
  10.0 231.5 %reduce-scatter.2.cloned.1.call-start = ((), (), s32[]{:S(2)}) async-start(), calls=%async_computation.2 | async-start | bytes 2621440 | tf_op jit(solution)/shard_map/reduce_scatter | solution.py:424
  10.1 4.6 %collective-permute-start = (bf16[2,512,512]{2,1,0:T(8,128)(2,1)S(1)}, bf16[2,512,512]{2,1,0:T(8,128)(2,1)S(1)}, u32[]{:S(2)}, u32[]{:S(2)}) collective-permute-start(bf16[2,512,512]{2,1,0:T(8,128)(2,1)S(1)} %get-tuple-element.94), channel_id=1, source_target_pairs={{0,4},{4,0},{8,12},{12,8},{16,20},{20,16},{24,28},{28,24},{1,5},{5... | collective-permute-start | bytes 3145736 | tf_op jit(solution)/shard_map/ppermute | solution.py:283
  10.6 26.6 %collective-permute-start.1 = (bf16[2,512,512]{2,1,0:T(8,128)(2,1)S(1)}, bf16[2,512,512]{2,1,0:T(8,128)(2,1)S(1)}, u32[]{:S(2)}, u32[]{:S(2)}) collective-permute-start(bf16[2,512,512]{2,1,0:T(8,128)(2,1)S(1)} %get-tuple-element.58.refs_1_.refs_2_), channel_id=1, source_target_pairs={{8,0},{12,4},{0,8},{4,12},{24,16},{28,20},{16,24},{20,28},{9,1},{1... | collective-permute-start | bytes 3145736 | tf_op jit(solution)/shard_map/ppermute | solution.py:280
  13.2 26.0 %collective-permute-start.3 = (bf16[2,512,512]{2,1,0:T(8,128)(2,1)S(1)}, bf16[2,512,512]{2,1,0:T(8,128)(2,1)S(1)}, u32[]{:S(2)}, u32[]{:S(2)}) collective-permute-start(bf16[2,512,512]{2,1,0:T(8,128)(2,1)S(1)} %get-tuple-element.58.refs_1_.refs_2_), channel_id=1, source_target_pairs={{16,0},{20,4},{24,8},{28,12},{0,16},{4,20},{8,24},{12,28},{17,1},{... | collective-permute-start | bytes 3145736 | tf_op jit(solution)/shard_map/ppermute | solution.py:280
  14.7 5.9 %copy-start.8 = (bf16[2,512,512]{2,1,0:T(8,128)(2,1)}, bf16[2,512,512]{2,1,0:T(8,128)(2,1)S(1)}, u32[]{:S(2)}) copy-start(bf16[2,512,512]{2,1,0:T(8,128)(2,1)S(1)} %collective-permute-done.refs_2_.refs_3_) | copy-start | bytes 3145732
  14.7 44.7 %collective-permute-start.2 = (bf16[2,512,512]{2,1,0:T(8,128)(2,1)S(1)}, bf16[2,512,512]{2,1,0:T(8,128)(2,1)S(1)}, u32[]{:S(2)}, u32[]{:S(2)}) collective-permute-start(bf16[2,512,512]{2,1,0:T(8,128)(2,1)S(1)} %collective-permute-done.refs_2_.refs_3_), channel_id=1, source_target_pairs={{8,0},{12,4},{0,8},{4,12},{24,16},{28,20},{16,24},{20,28},{9,1},{1... | collective-permute-start | bytes 3145736 | tf_op jit(solution)/shard_map/ppermute | solution.py:280
  15.8 45.1 %collective-permute-start.4 = (bf16[2,512,512]{2,1,0:T(8,128)(2,1)S(1)}, bf16[2,512,512]{2,1,0:T(8,128)(2,1)S(1)}, u32[]{:S(2)}, u32[]{:S(2)}) collective-permute-start(bf16[2,512,512]{2,1,0:T(8,128)(2,1)S(1)} %collective-permute-done.refs_2_.refs_3_), channel_id=1, source_target_pairs={{16,0},{20,4},{24,8},{28,12},{0,16},{4,20},{8,24},{12,28},{17,1},{... | collective-permute-start | bytes 3145736 | tf_op jit(solution)/shard_map/ppermute | solution.py:280
  18.5 2.0 collective-permute-start.5
  37.2 25.8 %copy-start.9 = (bf16[2,512,512]{2,1,0:T(8,128)(2,1)}, bf16[2,512,512]{2,1,0:T(8,128)(2,1)S(1)}, u32[]{:S(2)}) copy-start(bf16[2,512,512]{2,1,0:T(8,128)(2,1)S(1)} %collective-permute-done.1.refs_3_.refs_4_) | copy-start | bytes 3145732
  39.2 47.8 %copy-start.10 = (bf16[2,512,512]{2,1,0:T(8,128)(2,1)}, bf16[2,512,512]{2,1,0:T(8,128)(2,1)S(1)}, u32[]{:S(2)}) copy-start(bf16[2,512,512]{2,1,0:T(8,128)(2,1)S(1)} %collective-permute-done.3.refs_5_.refs_6_) | copy-start | bytes 3145732
  59.4 27.6 %copy-start.11 = (bf16[2,512,512]{2,1,0:T(8,128)(2,1)}, bf16[2,512,512]{2,1,0:T(8,128)(2,1)S(1)}, u32[]{:S(2)}) copy-start(bf16[2,512,512]{2,1,0:T(8,128)(2,1)S(1)} %collective-permute-done.2.refs_4_.refs_5_) | copy-start | bytes 3145732
  60.9 26.1 %copy-start.12 = (bf16[2,512,512]{2,1,0:T(8,128)(2,1)}, bf16[2,512,512]{2,1,0:T(8,128)(2,1)S(1)}, u32[]{:S(2)}) copy-start(bf16[2,512,512]{2,1,0:T(8,128)(2,1)S(1)} %collective-permute-done.4.refs_6_.refs_7_) | copy-start | bytes 3145732
  60.9 26.1 %collective-permute-start.6 = (bf16[2,512,512]{2,1,0:T(8,128)(2,1)S(1)}, bf16[2,512,512]{2,1,0:T(8,128)(2,1)S(1)}, u32[]{:S(2)}, u32[]{:S(2)}) collective-permute-start(bf16[2,512,512]{2,1,0:T(8,128)(2,1)S(1)} %collective-permute-done.1.refs_3_.refs_4_), channel_id=1, source_target_pairs={{16,0},{20,4},{24,8},{28,12},{0,16},{4,20},{8,24},{12,28},{17,1},{... | collective-permute-start | bytes 3145736 | tf_op jit(solution)/shard_map/ppermute | solution.py:280
  62.4 26.2 %collective-permute-start.7 = (bf16[2,512,512]{2,1,0:T(8,128)(2,1)S(1)}, bf16[2,512,512]{2,1,0:T(8,128)(2,1)}, u32[]{:S(2)}, u32[]{:S(2)}) collective-permute-start(bf16[2,512,512]{2,1,0:T(8,128)(2,1)S(1)} %collective-permute-done.4.refs_6_.refs_7_), channel_id=1, source_target_pairs={{8,0},{12,4},{0,8},{4,12},{24,16},{28,20},{16,24},{20,28},{9,1},{1... | collective-permute-start | bytes 3145736 | tf_op jit(solution)/shard_map/ppermute | solution.py:280
  62.9 48.0 %collective-permute-start.8 = (bf16[2,512,512]{2,1,0:T(8,128)(2,1)S(1)}, bf16[2,512,512]{2,1,0:T(8,128)(2,1)S(1)}, u32[]{:S(2)}, u32[]{:S(2)}) collective-permute-start(bf16[2,512,512]{2,1,0:T(8,128)(2,1)S(1)} %pad_maximum_fusion.refs_1_), channel_id=1, source_target_pairs={{8,0},{12,4},{0,8},{4,12},{24,16},{28,20},{16,24},{20,28},{9,1},{1... | collective-permute-start | bytes 3145736 | tf_op jit(solution)/shard_map/ppermute | solution.py:280
  64.4 46.5 %collective-permute-start.9 = (bf16[2,512,512]{2,1,0:T(8,128)(2,1)S(1)}, bf16[2,512,512]{2,1,0:T(8,128)(2,1)S(1)}, u32[]{:S(2)}, u32[]{:S(2)}) collective-permute-start(bf16[2,512,512]{2,1,0:T(8,128)(2,1)S(1)} %pad_maximum_fusion.refs_1_), channel_id=1, source_target_pairs={{16,0},{20,4},{24,8},{28,12},{0,16},{4,20},{8,24},{12,28},{17,1},{... | collective-permute-start | bytes 3145736 | tf_op jit(solution)/shard_map/ppermute | solution.py:280
  87.0 1.0 copy-start.13
  94.6 11.6 %collective-permute-start.10 = (bf16[16,4096]{1,0:T(8,128)(2,1)S(1)}, bf16[16,4096]{1,0:T(8,128)(2,1)S(1)}, u32[]{:S(2)}, u32[]{:S(2)}) collective-permute-start(bf16[16,4096]{1,0:T(8,128)(2,1)S(1)} %slice.62), channel_id=1, source_target_pairs={{4,8},{12,16},{20,24},{5,9},{13,17},{21,25},{6,10},{14,18},{22,26}... | collective-permute-start | bytes 393224 | tf_op jit(solution)/shard_map/ppermute | solution.py:355
  95.2 10.9 %collective-permute-start.11 = (bf16[16,4096]{1,0:T(8,128)(2,1)S(1)}, bf16[16,4096]{1,0:T(8,128)(2,1)S(1)}, u32[]{:S(2)}, u32[]{:S(2)}) collective-permute-start(bf16[16,4096]{1,0:T(8,128)(2,1)S(1)} %slice.62), channel_id=1, source_target_pairs={{4,12},{12,20},{20,28},{5,13},{13,21},{21,29},{6,14},{14,22},{22,3... | collective-permute-start | bytes 393224 | tf_op jit(solution)/shard_map/ppermute | solution.py:355
  106.2 12.1 %copy-start.3 = (s32[8]{0:T(128)S(1)}, s32[8]{0:T(128)}, u32[]{:S(2)}) copy-start(s32[8]{0:T(128)} %stack.55.at_ref._) | copy-start | bytes 100
  111.0 11.3 %collective-permute-start.12 = (bf16[512,4096]{1,0:T(8,128)(2,1)}, bf16[512,4096]{1,0:T(8,128)(2,1)}, u32[]{:S(2)}, u32[]{:S(2)}) collective-permute-start(bf16[512,4096]{1,0:T(8,128)(2,1)} %all-gather.2.cloned.1.call-done.refs_0_), channel_id=1, source_target_pairs={{0,4},{4,0},{8,12},{12,8},{16,20},{20,16},{24,28},{28,24},{1,5},{5... | collective-permute-start | bytes 12582920 | tf_op jit(solution)/shard_map/ppermute | solution.py:283
  113.0 28.2 %collective-permute-start.13 = (bf16[512,512]{1,0:T(8,128)(2,1)}, bf16[512,512]{1,0:T(8,128)(2,1)}, u32[]{:S(2)}, u32[]{:S(2)}) collective-permute-start(bf16[512,512]{1,0:T(8,128)(2,1)} %slice_bitcast_fusion.1), channel_id=1, source_target_pairs={{16,0},{20,4},{24,8},{28,12},{0,16},{4,20},{8,24},{12,28},{17,1},{... | collective-permute-start | bytes 1572872 | tf_op jit(solution)/shard_map/ppermute | solution.py:280
  115.6 25.7 %collective-permute-start.14 = (bf16[512,512]{1,0:T(8,128)(2,1)}, bf16[512,512]{1,0:T(8,128)(2,1)}, u32[]{:S(2)}, u32[]{:S(2)}) collective-permute-start(bf16[512,512]{1,0:T(8,128)(2,1)} %slice_bitcast_fusion), channel_id=1, source_target_pairs={{8,0},{12,4},{0,8},{4,12},{24,16},{28,20},{16,24},{20,28},{9,1},{1... | collective-permute-start | bytes 1572872 | tf_op jit(solution)/shard_map/ppermute | solution.py:280
  115.6 36.3 %collective-permute-start.17 = (bf16[1024,512]{1,0:T(8,128)(2,1)}, bf16[1024,512]{1,0:T(8,128)(2,1)}, u32[]{:S(2)}, u32[]{:S(2)}) collective-permute-start(bf16[1024,512]{1,0:T(8,128)(2,1)} %refs_4_.1), channel_id=1, source_target_pairs={{8,0},{12,4},{0,8},{4,12},{24,16},{28,20},{16,24},{20,28},{9,1},{1... | collective-permute-start | bytes 3145736 | tf_op jit(solution)/shard_map/ppermute | solution.py:280
  117.6 34.3 %collective-permute-start.18 = (bf16[1024,512]{1,0:T(8,128)(2,1)}, bf16[1024,512]{1,0:T(8,128)(2,1)}, u32[]{:S(2)}, u32[]{:S(2)}) collective-permute-start(bf16[1024,512]{1,0:T(8,128)(2,1)} %refs_4_.1), channel_id=1, source_target_pairs={{16,0},{20,4},{24,8},{28,12},{0,16},{4,20},{8,24},{12,28},{17,1},{... | collective-permute-start | bytes 3145736 | tf_op jit(solution)/shard_map/ppermute | solution.py:280
  122.3 9.8 %copy-start.1 = (f32[512,512]{1,0:T(8,128)S(1)}, f32[512,512]{1,0:T(8,128)}, u32[]{:S(2)}) copy-start(f32[512,512]{1,0:T(8,128)} %shard_map.64.product_ref) | copy-start | bytes 3145732
  122.3 10.7 %copy-start.4 = (s32[8]{0:T(128)S(1)}, s32[8]{0:T(128)}, u32[]{:S(2)}) copy-start(s32[8]{0:T(128)} %stack.55.at_ref._) | copy-start | bytes 100
  132.1 2.9 %copy-start.2 = (f32[512,512]{1,0:T(8,128)S(1)}, f32[512,512]{1,0:T(8,128)}, u32[]{:S(2)}) copy-start(f32[512,512]{1,0:T(8,128)} %get-tuple-element.73.product_ref) | copy-start | bytes 3145732
  144.5 7.4 %collective-permute-start.15 = (bf16[512,512]{1,0:T(8,128)(2,1)S(1)}, bf16[512,512]{1,0:T(8,128)(2,1)S(1)}, u32[]{:S(2)}, u32[]{:S(2)}) collective-permute-start(bf16[512,512]{1,0:T(8,128)(2,1)S(1)} %shard_map.71.refs_2_), channel_id=1, source_target_pairs={{0,4},{4,0},{8,12},{12,8},{16,20},{20,16},{24,28},{28,24},{1,5},{5... | collective-permute-start | bytes 1572872 | tf_op jit(solution)/shard_map/ppermute | solution.py:283
  147.8 4.1 %collective-permute-start.16 = (bf16[512,512]{1,0:T(8,128)(2,1)S(1)}, bf16[512,512]{1,0:T(8,128)(2,1)S(1)}, u32[]{:S(2)}, u32[]{:S(2)}) collective-permute-start(bf16[512,512]{1,0:T(8,128)(2,1)S(1)} %shard_map.69.refs_0_), channel_id=1, source_target_pairs={{0,4},{4,0},{8,12},{12,8},{16,20},{20,16},{24,28},{28,24},{1,5},{5... | collective-permute-start | bytes 1572872 | tf_op jit(solution)/shard_map/ppermute | solution.py:283
  158.4 12.7 %collective-permute-start.19 = (bf16[512,512]{1,0:T(8,128)(2,1)S(1)}, bf16[512,512]{1,0:T(8,128)(2,1)S(1)}, u32[]{:S(2)}, u32[]{:S(2)}) collective-permute-start(bf16[512,512]{1,0:T(8,128)(2,1)S(1)} %slice.80), channel_id=1, source_target_pairs={{16,0},{20,4},{24,8},{28,12},{0,16},{4,20},{8,24},{12,28},{17,1},{... | collective-permute-start | bytes 1572872 | tf_op jit(solution)/shard_map/ppermute | solution.py:280
  159.9 13.3 %collective-permute-start.20 = (bf16[512,512]{1,0:T(8,128)(2,1)S(1)}, bf16[512,512]{1,0:T(8,128)(2,1)S(1)}, u32[]{:S(2)}, u32[]{:S(2)}) collective-permute-start(bf16[512,512]{1,0:T(8,128)(2,1)S(1)} %slice.81), channel_id=1, source_target_pairs={{8,0},{12,4},{0,8},{4,12},{24,16},{28,20},{16,24},{20,28},{9,1},{1... | collective-permute-start | bytes 1572872 | tf_op jit(solution)/shard_map/ppermute | solution.py:280
  176.9 26.4 %collective-permute-start.21 = (bf16[256,1024]{1,0:T(8,128)(2,1)S(1)}, bf16[256,1024]{1,0:T(8,128)(2,1)S(1)}, u32[]{:S(2)}, u32[]{:S(2)}) collective-permute-start(bf16[256,1024]{1,0:T(8,128)(2,1)S(1)} %get-tuple-element.87), channel_id=1, source_target_pairs={{0,1},{1,2},{2,3},{4,5},{5,6},{6,7},{8,9},{9,10},{10,11},{12,13},{... | collective-permute-start | bytes 1572872 | tf_op jit(solution)/shard_map/ppermute | solution.py:415
  180.4 28.1 %collective-permute-start.24 = (bf16[256,1024]{1,0:T(8,128)(2,1)S(1)}, bf16[256,1024]{1,0:T(8,128)(2,1)S(1)}, u32[]{:S(2)}, u32[]{:S(2)}) collective-permute-start(bf16[256,1024]{1,0:T(8,128)(2,1)S(1)} %get-tuple-element.85), channel_id=1, source_target_pairs={{1,0},{2,1},{3,2},{5,4},{6,5},{7,6},{9,8},{10,9},{11,10},{13,12},{... | collective-permute-start | bytes 1572872 | tf_op jit(solution)/shard_map/ppermute | solution.py:416
  208.8 15.5 %collective-permute-start.25 = (bf16[256,1024]{1,0:T(8,128)(2,1)S(1)}, bf16[256,1024]{1,0:T(8,128)(2,1)S(1)}, u32[]{:S(2)}, u32[]{:S(2)}) collective-permute-start(bf16[256,1024]{1,0:T(8,128)(2,1)S(1)} %get-tuple-element.104), channel_id=1, source_target_pairs={{1,0},{2,1},{3,2},{5,4},{6,5},{7,6},{9,8},{10,9},{11,10},{13,12},{... | collective-permute-start | bytes 1572872 | tf_op jit(solution)/shard_map/ppermute | solution.py:416
  210.1 15.7 %collective-permute-start.22 = (bf16[256,1024]{1,0:T(8,128)(2,1)S(1)}, bf16[256,1024]{1,0:T(8,128)(2,1)S(1)}, u32[]{:S(2)}, u32[]{:S(2)}) collective-permute-start(bf16[256,1024]{1,0:T(8,128)(2,1)S(1)} %get-tuple-element.103), channel_id=1, source_target_pairs={{0,1},{1,2},{2,3},{4,5},{5,6},{6,7},{8,9},{9,10},{10,11},{12,13},{... | collective-permute-start | bytes 1572872 | tf_op jit(solution)/shard_map/ppermute | solution.py:415
  224.5 13.7 %collective-permute-start.26 = (bf16[256,1024]{1,0:T(8,128)(2,1)S(1)}, bf16[256,1024]{1,0:T(8,128)(2,1)S(1)}, u32[]{:S(2)}, u32[]{:S(2)}) collective-permute-start(bf16[256,1024]{1,0:T(8,128)(2,1)S(1)} %add_convert_fusion), channel_id=1, source_target_pairs={{1,0},{2,1},{3,2},{5,4},{6,5},{7,6},{9,8},{10,9},{11,10},{13,12},{... | collective-permute-start | bytes 1572872 | tf_op jit(solution)/shard_map/ppermute | solution.py:416
  226.0 13.6 %collective-permute-start.23 = (bf16[256,1024]{1,0:T(8,128)(2,1)S(1)}, bf16[256,1024]{1,0:T(8,128)(2,1)S(1)}, u32[]{:S(2)}, u32[]{:S(2)}) collective-permute-start(bf16[256,1024]{1,0:T(8,128)(2,1)S(1)} %add_convert_fusion.1), channel_id=1, source_target_pairs={{0,1},{1,2},{2,3},{4,5},{5,6},{6,7},{8,9},{9,10},{10,11},{12,13},{... | collective-permute-start | bytes 1572872 | tf_op jit(solution)/shard_map/ppermute | solution.py:415
  239.9 1.6 collective-permute-start.27
  240.0 3.2 %copy-start.6 = (bf16[128,4096]{1,0:T(8,128)(2,1)S(1)}, bf16[128,4096]{1,0:T(8,128)(2,1)}, u32[]{:S(2)}) copy-start(bf16[128,4096]{1,0:T(8,128)(2,1)} %param.6) | copy-start | bytes 3145732
  241.5 1.7 copy-start.14
  242.7 1.6 collective-permute-start.28
  244.6 1.0 copy-start.15
Sparse Core Ops, SparseCore 0:
  10.2 83.4 all-gather.1
  157.4 54.3 reduce-scatter.1
